TPU v7x, 32 devices: a whole 2x2x4 slice. The times are simulated.
32 devices in a mesh: shot: 8 (over z, y), depth: 4 (over x, core).
Axes of the slice: x: 2, y: 2, z: 4, core: 2. Of those that a mesh axis runs over, the one named last changes fastest.
Arguments:
- courant_sq: float32 [32, 64, 128], P('depth'), may hold values from 0.03 to 0.245
- momentum: float32 [32, 64, 128], P('depth'), may hold values from -6 to 6
- fwd_prev: float32 [16, 32, 64, 128], P('shot', 'depth'), may hold values from -6 to 6
- fwd_cur: float32 [16, 32, 64, 128], P('shot', 'depth'), may hold values from -6 to 6
- adj_next: float32 [16, 32, 64, 128], P('shot', 'depth'), may hold values from -6 to 6
- adj_cur: float32 [16, 32, 64, 128], P('shot', 'depth'), may hold values from -6 to 6
- observed: float32 [16, 8, 512], P('shot'), may hold values from -24 to 24
- src_cells: int32 [16], P('shot'), may hold values from 0 to 262143
- rec_cells: int32 [16, 512], P('shot'), may hold values from 0 to 262143
- ckpt_step: int32 [], replicated, may hold values from 0 to 999999
Outputs:
- momentum_half: float32 [32, 64, 128], P('depth')
- kinetic: float32 [], replicated
All inputs are finite; a program needn't handle non-finite values.
Results may differ from a plain program's by a relative error of at most 0.0003.
Values sent between devices are 32-bit elements; how exact they have to be, the bound alone decides.
No kernel may reach another device: no remote copies, remote signals or barrier semaphores. Data moves between devices by JAX's collectives and lax.ppermute only.
A program may use at most 64 MiB of HBM per device.

v0:
```python
import jax
import jax.numpy as jnp
from jax import lax
from jax.sharding import PartitionSpec as P

CENTER = -2.5
NEAR = 4.0 / 3.0
FAR = -1.0 / 12.0
AMPLITUDE = 100.0
EPSILON = 1e-06


def with_halo(value, sides, width):
    for axis, dim in sides:
        size, length = (lax.axis_size(axis), value.shape[dim])
        up = [(i, (i + 1) % size) for i in range(size - 1)]
        down = [(j, i) for i, j in up]
        last = lax.slice_in_dim(value, length - width, length, axis=dim)
        leading = lax.slice_in_dim(value, 0, width, axis=dim)
        before = lax.ppermute(last, axis, up)
        after = lax.ppermute(leading, axis, down)
        value = jnp.concatenate([before, value, after], axis=dim)
    return value


def laplace(padded):
    lateral = jnp.pad(padded[:, 2:-2], ((0, 0), (0, 0), (2, 2), (2, 2)))
    center = padded[:, 2:-2]
    along_z = NEAR * (padded[:, 1:-3] + padded[:, 3:-1]) + FAR * (padded[:, :-4] + padded[:, 4:])
    along_x = NEAR * (lateral[:, :, 1:-3, 2:-2] + lateral[:, :, 3:-1, 2:-2]) + FAR * (
        lateral[:, :, :-4, 2:-2] + lateral[:, :, 4:, 2:-2]
    )
    along_y = NEAR * (lateral[:, :, 2:-2, 1:-3] + lateral[:, :, 2:-2, 3:-1]) + FAR * (
        lateral[:, :, 2:-2, :-4] + lateral[:, :, 2:-2, 4:]
    )
    return 3.0 * CENTER * center + along_z + along_x + along_y


def locate(field, cell_ids, first_plane):
    shot_count, planes, rows_x, rows_y = field.shape
    plane_cells = rows_x * rows_y
    local_index = cell_ids - first_plane * plane_cells
    inside = (local_index >= 0) & (local_index < planes * plane_cells)
    target = jnp.where(inside, local_index, 0)
    return (inside, target)


def inject(field, cell_ids, values, first_plane):
    shot_count = field.shape[0]
    inside, target = locate(field, cell_ids, first_plane)
    amount = jnp.where(inside, values, jnp.zeros_like(values))
    flattened = field.reshape(shot_count, -1)
    lanes = jnp.arange(shot_count)[:, None]
    flattened = flattened.at[lanes, target].add(amount)
    return flattened.reshape(field.shape)


def sample(field, cell_ids, first_plane):
    shot_count = field.shape[0]
    inside, target = locate(field, cell_ids, first_plane)
    values = jnp.take_along_axis(field.reshape(shot_count, -1), target, axis=1)
    return jnp.where(inside, values, jnp.zeros_like(values))


def wave_value(start, step):
    cycle = jnp.mod(start + jnp.int32(step), jnp.int32(48))
    phase = (cycle.astype(jnp.float32) - 24.0) / 12.0
    return AMPLITUDE * (1.0 - 2.0 * phase * phase) * jnp.exp(-phase * phase)


def statistics(scaled, moment, weight, cells_all):
    grand_total = lax.psum(jnp.sum(scaled * scaled), ("shot", "depth"))
    factor = lax.rsqrt(grand_total / cells_all + EPSILON)
    halfway = moment - 0.5 * factor * scaled
    energy = lax.psum(jnp.sum(weight * halfway * halfway), ("shot", "depth"))
    return (factor, 0.5 * energy / cells_all)


def shards(
    courant_sq,
    momentum,
    fwd_prev,
    fwd_cur,
    adj_next,
    adj_cur,
    observed,
    src_cells,
    rec_cells,
    ckpt_step,
):
    shot_count, planes, rows_x, rows_y = fwd_cur.shape
    steps_all = observed.shape[1]
    first_plane = lax.axis_index("depth") * planes
    total_planes = planes * lax.axis_size("depth")
    cells_all = total_planes * rows_x * rows_y
    sources = src_cells[:, None]
    older, current = (fwd_prev, fwd_cur)
    laplacians = []
    misfits = []
    for step in range(steps_all):
        padded = with_halo(current, (("depth", 1),), 2)
        strength = jnp.full(sources.shape, wave_value(ckpt_step, step), jnp.float32)
        laplacian = inject(laplace(padded), sources, strength, first_plane)
        newer = 2.0 * current - older + courant_sq * laplacian
        misfits.append(sample(newer, rec_cells, first_plane) - observed[:, step, :])
        laplacians.append(laplacian)
        older, current = (current, newer)
    adj_later, adj_now = (adj_next, adj_cur)
    gradient = jnp.zeros((planes, rows_x, rows_y), jnp.float32)
    for step in reversed(range(steps_all)):
        padded = with_halo(courant_sq * adj_now, (("depth", 1),), 2)
        adj_new = 2.0 * adj_now - adj_later + laplace(padded)
        adj_new = inject(adj_new, rec_cells, misfits[step], first_plane)
        gradient = gradient + jnp.sum(adj_new * laplacians[step], axis=0)
        adj_later, adj_now = (adj_now, adj_new)
    depths = (first_plane + jnp.arange(planes)).astype(jnp.float32)
    weight = (1.0 + 2.0 * depths / (total_planes - 1))[:, None, None]
    share_rows = rows_x // lax.axis_size("shot")
    offset = lax.axis_index("shot") * share_rows
    moment_share = lax.dynamic_slice_in_dim(momentum, offset, share_rows, 1)
    gradient = lax.psum(gradient, "shot")
    scaled = weight * gradient
    scaled_share = lax.dynamic_slice_in_dim(scaled, offset, share_rows, 1)
    factor, kinetic = statistics(scaled_share, moment_share, weight, cells_all)
    momentum_half = momentum - 0.5 * factor * scaled
    return (momentum_half, kinetic)


def solution(mesh):
    placed = (
        P("depth", None, None),
        P("depth", None, None),
        P("shot", "depth", None, None),
        P("shot", "depth", None, None),
        P("shot", "depth", None, None),
        P("shot", "depth", None, None),
        P("shot", None, None),
        P("shot"),
        P("shot", None),
        P(),
    )
    return jax.shard_map(
        shards, mesh=mesh, in_specs=placed, out_specs=(P("depth", None, None), P()), check_vma=False
    )
```

profile of v0, /device:TPU:0, one launch (start us, length us, event | category | flops | bytes accessed | tf_op | source)
XLA Modules:
  0.0 477.2 jit_solution(7615970209549854586)
XLA Ops:
  8.3 2.4 collective-permute-start.2
  10.6 1.3 collective-permute-start.3
  13.7 2.3 collective-permute-done.3
  19.2 5.5 %collective-permute-start.4 = (f32[2,2,64,128]{3,2,1,0:T(8,128)S(1)}, f32[2,2,64,128]{3,2,1,0:T(8,128)S(1)}, u32[]{:S(2)}, u32[]{:S(2)}) collective-permute-start(f32[2,2,64,128]{3,2,1,0:T(8,128)S(1)} %get-tuple-element.36), channel_id=1, source_target_pairs={{0,1},{1,2},{2,3},{4,5},{5,6},{6,7},{8,9},{9,10},{10,11},{12,13},{... | collective-permute-start | bytes 393224 | tf_op jit(solution)/shard_map/ppermute | solution.py:20
  24.7 1.3 collective-permute-start.5
  26.0 1.9 collective-permute-done.5
  30.6 5.0 %collective-permute-start.6 = (f32[2,2,64,128]{3,2,1,0:T(8,128)S(1)}, f32[2,2,64,128]{3,2,1,0:T(8,128)S(1)}, u32[]{:S(2)}, u32[]{:S(2)}) collective-permute-start(f32[2,2,64,128]{3,2,1,0:T(8,128)S(1)} %get-tuple-element.34), channel_id=1, source_target_pairs={{0,1},{1,2},{2,3},{4,5},{5,6},{6,7},{8,9},{9,10},{10,11},{12,13},{... | collective-permute-start | bytes 393224 | tf_op jit(solution)/shard_map/ppermute | solution.py:20
  35.5 1.3 collective-permute-start.7
  36.8 1.9 collective-permute-done.7
  41.3 5.0 %collective-permute-start.8 = (f32[2,2,64,128]{3,2,1,0:T(8,128)S(1)}, f32[2,2,64,128]{3,2,1,0:T(8,128)S(1)}, u32[]{:S(2)}, u32[]{:S(2)}) collective-permute-start(f32[2,2,64,128]{3,2,1,0:T(8,128)S(1)} %get-tuple-element.32), channel_id=1, source_target_pairs={{0,1},{1,2},{2,3},{4,5},{5,6},{6,7},{8,9},{9,10},{10,11},{12,13},{... | collective-permute-start | bytes 393224 | tf_op jit(solution)/shard_map/ppermute | solution.py:20
  46.2 1.3 collective-permute-start.9
  47.6 1.9 collective-permute-done.9
  52.0 5.0 %collective-permute-start.10 = (f32[2,2,64,128]{3,2,1,0:T(8,128)S(1)}, f32[2,2,64,128]{3,2,1,0:T(8,128)S(1)}, u32[]{:S(2)}, u32[]{:S(2)}) collective-permute-start(f32[2,2,64,128]{3,2,1,0:T(8,128)S(1)} %get-tuple-element.30), channel_id=1, source_target_pairs={{0,1},{1,2},{2,3},{4,5},{5,6},{6,7},{8,9},{9,10},{10,11},{12,13},{... | collective-permute-start | bytes 393224 | tf_op jit(solution)/shard_map/ppermute | solution.py:20
  58.5 1.7 collective-permute-done.11
  62.9 5.0 %collective-permute-start.12 = (f32[2,2,64,128]{3,2,1,0:T(8,128)S(1)}, f32[2,2,64,128]{3,2,1,0:T(8,128)S(1)}, u32[]{:S(2)}, u32[]{:S(2)}) collective-permute-start(f32[2,2,64,128]{3,2,1,0:T(8,128)S(1)} %get-tuple-element.28), channel_id=1, source_target_pairs={{0,1},{1,2},{2,3},{4,5},{5,6},{6,7},{8,9},{9,10},{10,11},{12,13},{... | collective-permute-start | bytes 393224 | tf_op jit(solution)/shard_map/ppermute | solution.py:20
  67.9 1.3 collective-permute-start.13
  69.2 1.9 collective-permute-done.13
  74.2 5.0 %collective-permute-start.14 = (f32[2,2,64,128]{3,2,1,0:T(8,128)S(1)}, f32[2,2,64,128]{3,2,1,0:T(8,128)S(1)}, u32[]{:S(2)}, u32[]{:S(2)}) collective-permute-start(f32[2,2,64,128]{3,2,1,0:T(8,128)S(1)} %get-tuple-element.26), channel_id=1, source_target_pairs={{0,1},{1,2},{2,3},{4,5},{5,6},{6,7},{8,9},{9,10},{10,11},{12,13},{... | collective-permute-start | bytes 393224 | tf_op jit(solution)/shard_map/ppermute | solution.py:20
  79.2 1.8 collective-permute-start.15
  81.4 9.1 %gather_fusion.7 = f32[1024]{0:T(1024)S(1)} fusion(f32[2,65536]{1,0:T(2,128)S(1)} %bitcast.260, s32[1024]{0:T(1024)S(1)} %bitcast.223), kind=kCustom, calls=%fused_computation.7.clone | custom fusion | bytes 16384 | tf_op jit(solution)/shard_map/jit(take_along_axis)/gather | solution.py:61
  92.4 1.8 scatter_fusion.6
  95.6 3.0 collective-permute-start.16
  98.7 1.3 collective-permute-start.17
  100.4 9.1 %gather_fusion.6 = f32[1024]{0:T(1024)S(1)} fusion(f32[2,65536]{1,0:T(2,128)S(1)} %bitcast.261, s32[1024]{0:T(1024)S(1)} %bitcast.224), kind=kCustom, calls=%fused_computation.6.clone | custom fusion | bytes 16384 | tf_op jit(solution)/shard_map/jit(take_along_axis)/gather | solution.py:61
  110.0 9.1 %gather_fusion.5 = f32[1024]{0:T(1024)S(1)} fusion(f32[2,65536]{1,0:T(2,128)S(1)} %bitcast.262, s32[1024]{0:T(1024)S(1)} %bitcast.225), kind=kCustom, calls=%fused_computation.5.clone | custom fusion | bytes 16384 | tf_op jit(solution)/shard_map/jit(take_along_axis)/gather | solution.py:61
  119.5 9.1 %gather_fusion.4 = f32[1024]{0:T(1024)S(1)} fusion(f32[2,65536]{1,0:T(2,128)S(1)} %bitcast.263, s32[1024]{0:T(1024)S(1)} %bitcast.226), kind=kCustom, calls=%fused_computation.4.clone | custom fusion | bytes 16384 | tf_op jit(solution)/shard_map/jit(take_along_axis)/gather | solution.py:61
  129.1 9.1 %gather_fusion.3 = f32[1024]{0:T(1024)S(1)} fusion(f32[2,65536]{1,0:T(2,128)S(1)} %bitcast.264, s32[1024]{0:T(1024)S(1)} %bitcast.227), kind=kCustom, calls=%fused_computation.3.clone | custom fusion | bytes 16384 | tf_op jit(solution)/shard_map/jit(take_along_axis)/gather | solution.py:61
  138.6 9.1 %gather_fusion.2 = f32[1024]{0:T(1024)S(1)} fusion(f32[2,65536]{1,0:T(2,128)S(1)} %bitcast.265, s32[1024]{0:T(1024)S(1)} %bitcast.228), kind=kCustom, calls=%fused_computation.2.clone | custom fusion | bytes 16384 | tf_op jit(solution)/shard_map/jit(take_along_axis)/gather | solution.py:61
  148.2 9.1 %gather_fusion.1 = f32[1024]{0:T(1024)S(1)} fusion(f32[2,65536]{1,0:T(2,128)S(1)} %bitcast.266, s32[1024]{0:T(1024)S(1)} %bitcast.229), kind=kCustom, calls=%fused_computation.1.clone | custom fusion | bytes 16384 | tf_op jit(solution)/shard_map/jit(take_along_axis)/gather | solution.py:61
  161.5 9.1 %gather_fusion = f32[1024]{0:T(1024)S(1)} fusion(f32[2,65536]{1,0:T(2,128)S(1)} %bitcast.259, s32[1024]{0:T(1024)S(1)} %bitcast.230), kind=kCustom, calls=%fused_computation.clone | custom fusion | bytes 16384 | tf_op jit(solution)/shard_map/jit(take_along_axis)/gather | solution.py:61
  170.7 4.0 collective-permute-start
  176.6 2.5 collective-permute-done.1
  179.8 6.7 %scatter_fusion.8 = f32[131072]{0:T(1024)S(1)} fusion(f32[131072]{0:T(1024)S(1)} %bitcast.235, s32[1024]{0:T(1024)S(1)} %bitcast.306, f32[1024]{0:T(1024)S(1)} %bitcast.320), kind=kCustom, calls=%fused_computation.16 | custom fusion | flops 1024 | bytes 16384
  186.6 5.4 %collective-permute-start.18 = (f32[2,2,64,128]{3,2,1,0:T(8,128)S(1)}, f32[2,2,64,128]{3,2,1,0:T(8,128)S(1)}, u32[]{:S(2)}, u32[]{:S(2)}) collective-permute-start(f32[2,2,64,128]{3,2,1,0:T(8,128)S(1)} %get-tuple-element.22), channel_id=1, source_target_pairs={{0,1},{1,2},{2,3},{4,5},{5,6},{6,7},{8,9},{9,10},{10,11},{12,13},{... | collective-permute-start | bytes 393224 | tf_op jit(solution)/shard_map/ppermute | solution.py:20
  193.4 1.9 collective-permute-done.19
  195.9 6.6 %scatter_fusion.9 = f32[131072]{0:T(1024)S(1)} fusion(f32[131072]{0:T(1024)S(1)} %bitcast.239, s32[1024]{0:T(1024)S(1)} %bitcast.307, f32[1024]{0:T(1024)S(1)} %bitcast.321), kind=kCustom, calls=%fused_computation.17 | custom fusion | flops 1024 | bytes 16384
  202.6 4.9 %collective-permute-start.20 = (f32[2,2,64,128]{3,2,1,0:T(8,128)S(1)}, f32[2,2,64,128]{3,2,1,0:T(8,128)S(1)}, u32[]{:S(2)}, u32[]{:S(2)}) collective-permute-start(f32[2,2,64,128]{3,2,1,0:T(8,128)S(1)} %get-tuple-element.20), channel_id=1, source_target_pairs={{0,1},{1,2},{2,3},{4,5},{5,6},{6,7},{8,9},{9,10},{10,11},{12,13},{... | collective-permute-start | bytes 393224 | tf_op jit(solution)/shard_map/ppermute | solution.py:20
  208.9 1.9 collective-permute-done.21
  211.4 6.6 %scatter_fusion.10 = f32[131072]{0:T(1024)S(1)} fusion(f32[131072]{0:T(1024)S(1)} %bitcast.243, s32[1024]{0:T(1024)S(1)} %bitcast.308, f32[1024]{0:T(1024)S(1)} %bitcast.322), kind=kCustom, calls=%fused_computation.18 | custom fusion | flops 1024 | bytes 16384
  218.1 4.9 %collective-permute-start.22 = (f32[2,2,64,128]{3,2,1,0:T(8,128)S(1)}, f32[2,2,64,128]{3,2,1,0:T(8,128)S(1)}, u32[]{:S(2)}, u32[]{:S(2)}) collective-permute-start(f32[2,2,64,128]{3,2,1,0:T(8,128)S(1)} %get-tuple-element.18), channel_id=1, source_target_pairs={{0,1},{1,2},{2,3},{4,5},{5,6},{6,7},{8,9},{9,10},{10,11},{12,13},{... | collective-permute-start | bytes 393224 | tf_op jit(solution)/shard_map/ppermute | solution.py:20
  224.4 1.9 collective-permute-done.23
  226.9 6.6 %scatter_fusion.11 = f32[131072]{0:T(1024)S(1)} fusion(f32[131072]{0:T(1024)S(1)} %bitcast.247, s32[1024]{0:T(1024)S(1)} %bitcast.309, f32[1024]{0:T(1024)S(1)} %bitcast.323), kind=kCustom, calls=%fused_computation.19 | custom fusion | flops 1024 | bytes 16384
  234.3 4.9 %collective-permute-start.24 = (f32[2,2,64,128]{3,2,1,0:T(8,128)}, f32[2,2,64,128]{3,2,1,0:T(8,128)S(1)}, u32[]{:S(2)}, u32[]{:S(2)}) collective-permute-start(f32[2,2,64,128]{3,2,1,0:T(8,128)} %get-tuple-element.16), channel_id=1, source_target_pairs={{0,1},{1,2},{2,3},{4,5},{5,6},{6,7},{8,9},{9,10},{10,11},{12,13},{... | collective-permute-start | bytes 393224 | tf_op jit(solution)/shard_map/ppermute | solution.py:20
  239.3 1.3 collective-permute-start.25
  242.8 1.6 fusion.34
  244.4 6.7 %scatter_fusion.12 = f32[131072]{0:T(1024)S(1)} fusion(f32[131072]{0:T(1024)S(1)} %bitcast.251, s32[1024]{0:T(1024)S(1)} %bitcast.310, f32[1024]{0:T(1024)} %bitcast.319), kind=kCustom, calls=%fused_computation.20 | custom fusion | flops 1024 | bytes 16384
  252.0 4.9 %collective-permute-start.26 = (f32[2,2,64,128]{3,2,1,0:T(8,128)}, f32[2,2,64,128]{3,2,1,0:T(8,128)S(1)}, u32[]{:S(2)}, u32[]{:S(2)}) collective-permute-start(f32[2,2,64,128]{3,2,1,0:T(8,128)} %get-tuple-element.14), channel_id=1, source_target_pairs={{0,1},{1,2},{2,3},{4,5},{5,6},{6,7},{8,9},{9,10},{10,11},{12,13},{... | collective-permute-start | bytes 393224 | tf_op jit(solution)/shard_map/ppermute | solution.py:20
  256.9 1.5 collective-permute-start.27
  258.4 3.4 multiply_reduce_fusion.6
  264.0 1.6 fusion.25
  265.7 6.6 %scatter_fusion.13 = f32[131072]{0:T(1024)S(1)} fusion(f32[131072]{0:T(1024)S(1)} %bitcast.231, s32[1024]{0:T(1024)S(1)} %bitcast.311, f32[1024]{0:T(1024)S(1)} %bitcast.318), kind=kCustom, calls=%fused_computation.21 | custom fusion | flops 1024 | bytes 16384
  273.1 3.0 collective-permute-start.28
  276.1 1.3 collective-permute-start.29
  277.4 2.7 multiply_reduce_fusion.4
  281.6 1.6 fusion.16
  283.2 6.6 %scatter_fusion.14 = f32[131072]{0:T(1024)S(1)} fusion(f32[131072]{0:T(1024)S(1)} %bitcast.255, s32[1024]{0:T(1024)S(1)} %bitcast.312, f32[1024]{0:T(1024)S(1)} %bitcast.317), kind=kCustom, calls=%fused_computation.22 | custom fusion | flops 1024 | bytes 16384
  290.5 4.2 collective-permute-start.30
  294.7 1.5 collective-permute-start.31
  296.3 2.7 multiply_reduce_fusion.2
  299.9 6.6 %scatter_fusion.15 = f32[131072]{0:T(1024)S(1)} fusion(f32[131072]{0:T(1024)S(1)} %bitcast.258, s32[1024]{0:T(1024)S(1)} %bitcast.313, f32[1024]{0:T(1024)S(1)} %bitcast.316), kind=kCustom, calls=%fused_computation.23 | custom fusion | flops 1024 | bytes 16384
  307.8 2.0 multiply_reduce_fusion
  310.7 73.6 %all-reduce.18.cloned.1.call-done = f32[8,64,128]{2,1,0:T(8,128)} async-done(((f32[8,64,128]{2,1,0:T(8,128)}), f32[8,64,128]{2,1,0:T(8,128)}) %all-reduce.18.cloned.1.call-update) | async-done | bytes 262160 | tf_op jit(solution)/shard_map/psum | solution.py:121
  386.1 39.8 %psum.22 = f32[]{:T(128)} all-reduce(f32[]{:T(128)} %multiply_reduce_fusion.8), channel_id=1, replica_groups=mesh['shot'=8,'depth'=4] {'shot','depth'}, use_global_device_ids=true, to_apply=%region_26.28 | all-reduce | flops 1 | bytes 8 | tf_op jit(solution)/shard_map/psum | solution.py:72
  427.3 40.1 %psum.23 = f32[]{:T(128)} all-reduce(f32[]{:T(128)} %fusion.324), channel_id=1, replica_groups=mesh['shot'=8,'depth'=4] {'shot','depth'}, use_global_device_ids=true, to_apply=%region_28.30 | all-reduce | flops 1 | bytes 8 | tf_op jit(solution)/shard_map/psum | solution.py:75
  (244 shorter events, 53.7 us)
Async XLA Ops:
  7.2 6.4 %copy-start.7 = (f32[2,8,64,128]{3,2,1,0:T(8,128)S(1)}, f32[2,8,64,128]{3,2,1,0:T(8,128)}, u32[]{:S(2)}) copy-start(f32[2,8,64,128]{3,2,1,0:T(8,128)} %param.15) | copy-start | bytes 1572868
  7.2 5.9 %copy-start.42 = (s32[2]{0:T(128)S(1)}, s32[2]{0:T(128)}, u32[]{:S(2)}) copy-start(s32[2]{0:T(128)} %param.19) | copy-start | bytes 28
  7.2 377.2 %all-reduce.18.cloned.1.call-start = ((), (), s32[]{:S(2)}) async-start(), calls=%async_computation | async-start | bytes 524288 | tf_op jit(solution)/shard_map/psum | solution.py:121
  8.3 5.2 %collective-permute-start.2 = (f32[2,2,64,128]{3,2,1,0:T(8,128)S(1)}, f32[2,2,64,128]{3,2,1,0:T(8,128)S(1)}, u32[]{:S(2)}, u32[]{:S(2)}) collective-permute-start(f32[2,2,64,128]{3,2,1,0:T(8,128)S(1)} %get-tuple-element.40), channel_id=1, source_target_pairs={{0,1},{1,2},{2,3},{4,5},{5,6},{6,7},{8,9},{9,10},{10,11},{12,13},{... | collective-permute-start | bytes 393224 | tf_op jit(solution)/shard_map/ppermute | solution.py:20
  10.6 5.3 %collective-permute-start.3 = (f32[2,2,64,128]{3,2,1,0:T(8,128)S(1)}, f32[2,2,64,128]{3,2,1,0:T(8,128)S(1)}, u32[]{:S(2)}, u32[]{:S(2)}) collective-permute-start(f32[2,2,64,128]{3,2,1,0:T(8,128)S(1)} %get-tuple-element.41), channel_id=1, source_target_pairs={{1,0},{2,1},{3,2},{5,4},{6,5},{7,6},{9,8},{10,9},{11,10},{13,12},{... | collective-permute-start | bytes 393224 | tf_op jit(solution)/shard_map/ppermute | solution.py:21
  19.2 6.8 %collective-permute-start.4 = (f32[2,2,64,128]{3,2,1,0:T(8,128)S(1)}, f32[2,2,64,128]{3,2,1,0:T(8,128)S(1)}, u32[]{:S(2)}, u32[]{:S(2)}) collective-permute-start(f32[2,2,64,128]{3,2,1,0:T(8,128)S(1)} %get-tuple-element.36), channel_id=1, source_target_pairs={{0,1},{1,2},{2,3},{4,5},{5,6},{6,7},{8,9},{9,10},{10,11},{12,13},{... | collective-permute-start | bytes 393224 | tf_op jit(solution)/shard_map/ppermute | solution.py:20
  24.7 3.2 collective-permute-start.5
  30.6 6.3 %collective-permute-start.6 = (f32[2,2,64,128]{3,2,1,0:T(8,128)S(1)}, f32[2,2,64,128]{3,2,1,0:T(8,128)S(1)}, u32[]{:S(2)}, u32[]{:S(2)}) collective-permute-start(f32[2,2,64,128]{3,2,1,0:T(8,128)S(1)} %get-tuple-element.34), channel_id=1, source_target_pairs={{0,1},{1,2},{2,3},{4,5},{5,6},{6,7},{8,9},{9,10},{10,11},{12,13},{... | collective-permute-start | bytes 393224 | tf_op jit(solution)/shard_map/ppermute | solution.py:20
  35.5 3.2 collective-permute-start.7
  40.5 7.1 %copy-start.41 = (s32[2,512]{1,0:T(2,128)S(1)}, s32[2,512]{1,0:T(2,128)}, u32[]{:S(2)}) copy-start(s32[2,512]{1,0:T(2,128)} %param.20) | copy-start | bytes 12292
  41.3 6.3 %collective-permute-start.8 = (f32[2,2,64,128]{3,2,1,0:T(8,128)S(1)}, f32[2,2,64,128]{3,2,1,0:T(8,128)S(1)}, u32[]{:S(2)}, u32[]{:S(2)}) collective-permute-start(f32[2,2,64,128]{3,2,1,0:T(8,128)S(1)} %get-tuple-element.32), channel_id=1, source_target_pairs={{0,1},{1,2},{2,3},{4,5},{5,6},{6,7},{8,9},{9,10},{10,11},{12,13},{... | collective-permute-start | bytes 393224 | tf_op jit(solution)/shard_map/ppermute | solution.py:20
  46.2 3.2 collective-permute-start.9
  51.2 7.1 %copy-start.43 = (s32[2]{0:T(128)S(1)}, s32[2]{0:T(128)}, u32[]{:S(2)}) copy-start(s32[2]{0:T(128)} %constant.181) | copy-start | bytes 28
  51.2 7.2 %copy-start.44 = (s32[2]{0:T(128)S(1)}, s32[2]{0:T(128)}, u32[]{:S(2)}) copy-start(s32[2]{0:T(128)} %constant.184) | copy-start | bytes 28
  52.0 6.5 %collective-permute-start.10 = (f32[2,2,64,128]{3,2,1,0:T(8,128)S(1)}, f32[2,2,64,128]{3,2,1,0:T(8,128)S(1)}, u32[]{:S(2)}, u32[]{:S(2)}) collective-permute-start(f32[2,2,64,128]{3,2,1,0:T(8,128)S(1)} %get-tuple-element.30), channel_id=1, source_target_pairs={{0,1},{1,2},{2,3},{4,5},{5,6},{6,7},{8,9},{9,10},{10,11},{12,13},{... | collective-permute-start | bytes 393224 | tf_op jit(solution)/shard_map/ppermute | solution.py:20
  57.0 3.2 collective-permute-start.11
  62.8 8.9 %copy-start.3 = (f32[2,8,64,128]{3,2,1,0:T(8,128)}, f32[2,8,64,128]{3,2,1,0:T(8,128)S(1)}, u32[]{:S(2)}) copy-start(f32[2,8,64,128]{3,2,1,0:T(8,128)S(1)} %multiply_add_fusion.3) | copy-start | bytes 1572868
  62.9 6.3 %collective-permute-start.12 = (f32[2,2,64,128]{3,2,1,0:T(8,128)S(1)}, f32[2,2,64,128]{3,2,1,0:T(8,128)S(1)}, u32[]{:S(2)}, u32[]{:S(2)}) collective-permute-start(f32[2,2,64,128]{3,2,1,0:T(8,128)S(1)} %get-tuple-element.28), channel_id=1, source_target_pairs={{0,1},{1,2},{2,3},{4,5},{5,6},{6,7},{8,9},{9,10},{10,11},{12,13},{... | collective-permute-start | bytes 393224 | tf_op jit(solution)/shard_map/ppermute | solution.py:20
  67.9 3.2 collective-permute-start.13
  74.0 6.9 %copy-start.38 = (f32[2,8,512]{2,1,0:T(8,128)S(1)}, f32[2,8,512]{2,1,0:T(8,128)}, u32[]{:S(2)}) copy-start(f32[2,8,512]{2,1,0:T(8,128)} %param.18) | copy-start | bytes 98308
  74.2 6.8 %copy-start.1 = (f32[2,8,64,128]{3,2,1,0:T(8,128)}, f32[2,8,64,128]{3,2,1,0:T(8,128)S(1)}, u32[]{:S(2)}) copy-start(f32[2,8,64,128]{3,2,1,0:T(8,128)S(1)} %multiply_add_fusion.2) | copy-start | bytes 1572868
  74.2 16.3 %collective-permute-start.14 = (f32[2,2,64,128]{3,2,1,0:T(8,128)S(1)}, f32[2,2,64,128]{3,2,1,0:T(8,128)S(1)}, u32[]{:S(2)}, u32[]{:S(2)}) collective-permute-start(f32[2,2,64,128]{3,2,1,0:T(8,128)S(1)} %get-tuple-element.26), channel_id=1, source_target_pairs={{0,1},{1,2},{2,3},{4,5},{5,6},{6,7},{8,9},{9,10},{10,11},{12,13},{... | collective-permute-start | bytes 393224 | tf_op jit(solution)/shard_map/ppermute | solution.py:20
  79.2 11.4 %collective-permute-start.15 = (f32[2,2,64,128]{3,2,1,0:T(8,128)S(1)}, f32[2,2,64,128]{3,2,1,0:T(8,128)S(1)}, u32[]{:S(2)}, u32[]{:S(2)}) collective-permute-start(f32[2,2,64,128]{3,2,1,0:T(8,128)S(1)} %get-tuple-element.27), channel_id=1, source_target_pairs={{1,0},{2,1},{3,2},{5,4},{6,5},{7,6},{9,8},{10,9},{11,10},{13,12},{... | collective-permute-start | bytes 393224 | tf_op jit(solution)/shard_map/ppermute | solution.py:21
  81.4 9.2 %copy-start.2 = (f32[2,8,64,128]{3,2,1,0:T(8,128)S(1)}, f32[2,8,64,128]{3,2,1,0:T(8,128)}, u32[]{:S(2)}) copy-start(f32[2,8,64,128]{3,2,1,0:T(8,128)} %copy-done.1) | copy-start | bytes 1572868
  95.6 4.8 %copy-start.8 = (f32[2,8,64,128]{3,2,1,0:T(8,128)}, f32[2,8,64,128]{3,2,1,0:T(8,128)S(1)}, u32[]{:S(2)}) copy-start(f32[2,8,64,128]{3,2,1,0:T(8,128)S(1)} %multiply_add_fusion.1) | copy-start | bytes 1572868
  95.6 61.7 %collective-permute-start.16 = (f32[2,2,64,128]{3,2,1,0:T(8,128)S(1)}, f32[2,2,64,128]{3,2,1,0:T(8,128)S(1)}, u32[]{:S(2)}, u32[]{:S(2)}) collective-permute-start(f32[2,2,64,128]{3,2,1,0:T(8,128)S(1)} %get-tuple-element.24), channel_id=1, source_target_pairs={{0,1},{1,2},{2,3},{4,5},{5,6},{6,7},{8,9},{9,10},{10,11},{12,13},{... | collective-permute-start | bytes 393224 | tf_op jit(solution)/shard_map/ppermute | solution.py:20
  98.7 58.7 %collective-permute-start.17 = (f32[2,2,64,128]{3,2,1,0:T(8,128)S(1)}, f32[2,2,64,128]{3,2,1,0:T(8,128)S(1)}, u32[]{:S(2)}, u32[]{:S(2)}) collective-permute-start(f32[2,2,64,128]{3,2,1,0:T(8,128)S(1)} %get-tuple-element.25), channel_id=1, source_target_pairs={{1,0},{2,1},{3,2},{5,4},{6,5},{7,6},{9,8},{10,9},{11,10},{13,12},{... | collective-permute-start | bytes 393224 | tf_op jit(solution)/shard_map/ppermute | solution.py:21
  119.5 9.1 %copy-start.6 = (f32[2,8,64,128]{3,2,1,0:T(8,128)S(1)}, f32[2,8,64,128]{3,2,1,0:T(8,128)}, u32[]{:S(2)}) copy-start(f32[2,8,64,128]{3,2,1,0:T(8,128)} %copy-done.3) | copy-start | bytes 1572868
  138.6 9.1 %copy-start.9 = (f32[2,8,64,128]{3,2,1,0:T(8,128)S(1)}, f32[2,8,64,128]{3,2,1,0:T(8,128)}, u32[]{:S(2)}) copy-start(f32[2,8,64,128]{3,2,1,0:T(8,128)} %copy-done.8) | copy-start | bytes 1572868
  161.5 9.2 %copy-start.23 = (f32[2,8,64,128]{3,2,1,0:T(8,128)S(1)}, f32[2,8,64,128]{3,2,1,0:T(8,128)}, u32[]{:S(2)}) copy-start(f32[2,8,64,128]{3,2,1,0:T(8,128)} %get-tuple-element.45) | copy-start | bytes 1572868
  170.6 8.5 %copy-start.36 = (f32[2,8,64,128]{3,2,1,0:T(8,128)S(1)}, f32[2,8,64,128]{3,2,1,0:T(8,128)}, u32[]{:S(2)}) copy-start(f32[2,8,64,128]{3,2,1,0:T(8,128)} %param.16) | copy-start | bytes 1572868
  170.7 5.9 %collective-permute-start = (f32[2,2,64,128]{3,2,1,0:T(8,128)S(1)}, f32[2,2,64,128]{3,2,1,0:T(8,128)S(1)}, u32[]{:S(2)}, u32[]{:S(2)}) collective-permute-start(f32[2,2,64,128]{3,2,1,0:T(8,128)S(1)} %get-tuple-element.42), channel_id=1, source_target_pairs={{0,1},{1,2},{2,3},{4,5},{5,6},{6,7},{8,9},{9,10},{10,11},{12,13},{... | collective-permute-start | bytes 393224 | tf_op jit(solution)/shard_map/ppermute | solution.py:20
  174.7 4.5 collective-permute-start.1
  186.6 6.8 %collective-permute-start.18 = (f32[2,2,64,128]{3,2,1,0:T(8,128)S(1)}, f32[2,2,64,128]{3,2,1,0:T(8,128)S(1)}, u32[]{:S(2)}, u32[]{:S(2)}) collective-permute-start(f32[2,2,64,128]{3,2,1,0:T(8,128)S(1)} %get-tuple-element.22), channel_id=1, source_target_pairs={{0,1},{1,2},{2,3},{4,5},{5,6},{6,7},{8,9},{9,10},{10,11},{12,13},{... | collective-permute-start | bytes 393224 | tf_op jit(solution)/shard_map/ppermute | solution.py:20
  192.1 3.2 collective-permute-start.19
  202.6 6.3 %collective-permute-start.20 = (f32[2,2,64,128]{3,2,1,0:T(8,128)S(1)}, f32[2,2,64,128]{3,2,1,0:T(8,128)S(1)}, u32[]{:S(2)}, u32[]{:S(2)}) collective-permute-start(f32[2,2,64,128]{3,2,1,0:T(8,128)S(1)} %get-tuple-element.20), channel_id=1, source_target_pairs={{0,1},{1,2},{2,3},{4,5},{5,6},{6,7},{8,9},{9,10},{10,11},{12,13},{... | collective-permute-start | bytes 393224 | tf_op jit(solution)/shard_map/ppermute | solution.py:20
  207.6 3.2 collective-permute-start.21
  218.1 6.3 %collective-permute-start.22 = (f32[2,2,64,128]{3,2,1,0:T(8,128)S(1)}, f32[2,2,64,128]{3,2,1,0:T(8,128)S(1)}, u32[]{:S(2)}, u32[]{:S(2)}) collective-permute-start(f32[2,2,64,128]{3,2,1,0:T(8,128)S(1)} %get-tuple-element.18), channel_id=1, source_target_pairs={{0,1},{1,2},{2,3},{4,5},{5,6},{6,7},{8,9},{9,10},{10,11},{12,13},{... | collective-permute-start | bytes 393224 | tf_op jit(solution)/shard_map/ppermute | solution.py:20
  223.0 3.2 collective-permute-start.23
  233.5 7.1 %copy-start.40 = (f32[1,4,2,128]{3,2,1,0:T(2,128)S(1)}, f32[1,4,2,128]{3,2,1,0:T(2,128)}, u32[]{:S(2)}) copy-start(f32[1,4,2,128]{3,2,1,0:T(2,128)} %get-tuple-element.55) | copy-start | bytes 12292
  233.5 7.1 %copy-start.39 = (f32[1,4,2,128]{3,2,1,0:T(2,128)S(1)}, f32[1,4,2,128]{3,2,1,0:T(2,128)}, u32[]{:S(2)}) copy-start(f32[1,4,2,128]{3,2,1,0:T(2,128)} %get-tuple-element.58) | copy-start | bytes 12292
  234.3 8.4 %collective-permute-start.24 = (f32[2,2,64,128]{3,2,1,0:T(8,128)}, f32[2,2,64,128]{3,2,1,0:T(8,128)S(1)}, u32[]{:S(2)}, u32[]{:S(2)}) collective-permute-start(f32[2,2,64,128]{3,2,1,0:T(8,128)} %get-tuple-element.16), channel_id=1, source_target_pairs={{0,1},{1,2},{2,3},{4,5},{5,6},{6,7},{8,9},{9,10},{10,11},{12,13},{... | collective-permute-start | bytes 393224 | tf_op jit(solution)/shard_map/ppermute | solution.py:20
  239.3 3.6 collective-permute-start.25
  251.2 7.2 %copy-start.24 = (f32[2,65536]{1,0:T(2,128)S(1)}, f32[2,65536]{1,0:T(2,128)}, u32[]{:S(2)}) copy-start(f32[2,65536]{1,0:T(2,128)} %reshape.211) | copy-start | bytes 1572868
  252.0 12.1 %collective-permute-start.26 = (f32[2,2,64,128]{3,2,1,0:T(8,128)}, f32[2,2,64,128]{3,2,1,0:T(8,128)S(1)}, u32[]{:S(2)}, u32[]{:S(2)}) collective-permute-start(f32[2,2,64,128]{3,2,1,0:T(8,128)} %get-tuple-element.14), channel_id=1, source_target_pairs={{0,1},{1,2},{2,3},{4,5},{5,6},{6,7},{8,9},{9,10},{10,11},{12,13},{... | collective-permute-start | bytes 393224 | tf_op jit(solution)/shard_map/ppermute | solution.py:20
  256.9 7.2 %collective-permute-start.27 = (f32[2,2,64,128]{3,2,1,0:T(8,128)}, f32[2,2,64,128]{3,2,1,0:T(8,128)}, u32[]{:S(2)}, u32[]{:S(2)}) collective-permute-start(f32[2,2,64,128]{3,2,1,0:T(8,128)} %get-tuple-element.15), channel_id=1, source_target_pairs={{1,0},{2,1},{3,2},{5,4},{6,5},{7,6},{9,8},{10,9},{11,10},{13,12},{... | collective-permute-start | bytes 393224 | tf_op jit(solution)/shard_map/ppermute | solution.py:21
  265.7 11.7 %copy-start.26 = (f32[2,65536]{1,0:T(2,128)S(1)}, f32[2,65536]{1,0:T(2,128)}, u32[]{:S(2)}) copy-start(f32[2,65536]{1,0:T(2,128)} %reshape.223) | copy-start | bytes 1572868
  272.2 5.2 %copy-start.19 = (f32[2,65536]{1,0:T(2,128)S(1)}, f32[2,65536]{1,0:T(2,128)}, u32[]{:S(2)}) copy-start(f32[2,65536]{1,0:T(2,128)} %copy-done.18) | copy-start | bytes 1572868
  272.2 5.2 %copy-start.21 = (f32[2,65536]{1,0:T(2,128)S(1)}, f32[2,65536]{1,0:T(2,128)}, u32[]{:S(2)}) copy-start(f32[2,65536]{1,0:T(2,128)} %copy-done.20) | copy-start | bytes 1572868
  272.3 5.2 %copy-start.25 = (f32[2,65536]{1,0:T(2,128)S(1)}, f32[2,65536]{1,0:T(2,128)}, u32[]{:S(2)}) copy-start(f32[2,65536]{1,0:T(2,128)} %reshape.219) | copy-start | bytes 1572868
  273.1 8.5 %collective-permute-start.28 = (f32[2,2,64,128]{3,2,1,0:T(8,128)}, f32[2,2,64,128]{3,2,1,0:T(8,128)S(1)}, u32[]{:S(2)}, u32[]{:S(2)}) collective-permute-start(f32[2,2,64,128]{3,2,1,0:T(8,128)} %get-tuple-element.12), channel_id=1, source_target_pairs={{0,1},{1,2},{2,3},{4,5},{5,6},{6,7},{8,9},{9,10},{10,11},{12,13},{... | collective-permute-start | bytes 393224 | tf_op jit(solution)/shard_map/ppermute | solution.py:20
  276.1 5.5 %collective-permute-start.29 = (f32[2,2,64,128]{3,2,1,0:T(8,128)}, f32[2,2,64,128]{3,2,1,0:T(8,128)}, u32[]{:S(2)}, u32[]{:S(2)}) collective-permute-start(f32[2,2,64,128]{3,2,1,0:T(8,128)} %get-tuple-element.13), channel_id=1, source_target_pairs={{1,0},{2,1},{3,2},{5,4},{6,5},{7,6},{9,8},{10,9},{11,10},{13,12},{... | collective-permute-start | bytes 393224 | tf_op jit(solution)/shard_map/ppermute | solution.py:21
  289.8 6.5 %copy-start.15 = (f32[2,65536]{1,0:T(2,128)S(1)}, f32[2,65536]{1,0:T(2,128)}, u32[]{:S(2)}) copy-start(f32[2,65536]{1,0:T(2,128)} %copy-done.14) | copy-start | bytes 1572868
  289.8 6.5 %copy-start.17 = (f32[2,65536]{1,0:T(2,128)S(1)}, f32[2,65536]{1,0:T(2,128)}, u32[]{:S(2)}) copy-start(f32[2,65536]{1,0:T(2,128)} %copy-done.16) | copy-start | bytes 1572868
  289.8 6.5 %copy-start.27 = (f32[2,65536]{1,0:T(2,128)S(1)}, f32[2,65536]{1,0:T(2,128)}, u32[]{:S(2)}) copy-start(f32[2,65536]{1,0:T(2,128)} %reshape.231) | copy-start | bytes 1572868
  290.5 8.8 %collective-permute-start.30 = (f32[2,2,64,128]{3,2,1,0:T(8,128)}, f32[2,2,64,128]{3,2,1,0:T(8,128)S(1)}, u32[]{:S(2)}, u32[]{:S(2)}) collective-permute-start(f32[2,2,64,128]{3,2,1,0:T(8,128)} %get-tuple-element.10), channel_id=1, source_target_pairs={{0,1},{1,2},{2,3},{4,5},{5,6},{6,7},{8,9},{9,10},{10,11},{12,13},{... | collective-permute-start | bytes 393224 | tf_op jit(solution)/shard_map/ppermute | solution.py:20
  294.7 4.6 collective-permute-start.31
  307.7 2.1 copy-start.29
  307.7 2.1 copy-start.30
  307.7 2.1 copy-start.31
  307.7 2.1 copy-start.32
  307.7 2.1 copy-start.33
  310.7 115.9 %copy-start.37 = (f32[8,64,128]{2,1,0:T(8,128)S(1)}, f32[8,64,128]{2,1,0:T(8,128)}, u32[]{:S(2)}) copy-start(f32[8,64,128]{2,1,0:T(8,128)} %param.13) | copy-start | bytes 786436
  384.4 83.6 %copy-start.34 = (f32[8,64,128]{2,1,0:T(8,128)S(1)}, f32[8,64,128]{2,1,0:T(8,128)}, u32[]{:S(2)}) copy-start(f32[8,64,128]{2,1,0:T(8,128)} %all-reduce.18.cloned.1.call-done) | copy-start | bytes 786436
  (14 other events, 15.7 us)
Sparse Core Ops, SparseCore 0:
  310.8 73.4 all-reduce.17
where the time goes:
time: 486 us; the launch traced here: 477 us
  local copies, waits for them, and re-layouts  99.7 us (21%)
  waiting for transfers between devices  93.9 us (19%)
  starting transfers between devices  93.7 us (19%)
  other arithmetic  90.4 us (19%)
  blocking collectives  79.8 us (16%)
  between operations  19.7 us (4%)
    psum x1, waiting for transfers between devices, shards(): gradient = lax.psum(gradient, 'shot')  73.6 us
    gather x16, local copies, waits for them, and re-layouts, sample(): values = jnp.take_along_axis(field.reshape(shot_count, -1), target, axis=1)  73 us
    ppermute x16, starting transfers between devices, with_halo(): before = lax.ppermute(last, axis, up)  72 us
    unnamed x14, other arithmetic  53.6 us
    psum x1, blocking collectives, statistics(): energy = lax.psum(jnp.sum(weight * halfway * halfway), ('shot', 'depth'))  40.1 us
    psum x1, blocking collectives, statistics(): grand_total = lax.psum(jnp.sum(scaled * scaled), ('shot', 'depth'))  39.8 us
    ppermute x16, starting transfers between devices, with_halo(): after = lax.ppermute(leading, axis, down)  21.6 us
    ppermute x16, waiting for transfers between devices, with_halo(): after = lax.ppermute(leading, axis, down)  20.2 us
  transfers between devices with their start and end apart: 33, of which 12 were waited for; matrix products, arithmetic and copies ran while one was open for 17% of the time, Pallas kernels for 0%

commit v1 on v0

--- a/solution.py
+++ b/solution.py
@@ -1,6 +1,11 @@
+import functools
+
 import jax
 import jax.numpy as jnp
 from jax import lax
+from jax.experimental import pallas as pl
+from jax.experimental.pallas import tpu as pltpu
+from jax.sharding import Mesh
 from jax.sharding import PartitionSpec as P
 
 CENTER = -2.5
@@ -76,7 +81,7 @@
     return (factor, 0.5 * energy / cells_all)
 
 
-def shards(
+def slab_shards(
     courant_sq,
     momentum,
     fwd_prev,
@@ -126,19 +131,344 @@
     return (momentum_half, kinetic)
 
 
+def interleave(dst, dst_at, src, src_at, rows, factor=None):
+    groups = rows // 8
+    for i in range(groups):
+        value = src[(*src_at, pl.ds(i, 8, stride=groups), slice(None))]
+        if factor is not None:
+            value = value * factor
+        dst[(*dst_at, pl.ds(i * 8, 8), slice(None))] = value
+
+
+def lap12(field, slot, z):
+    center = field[slot, z + 2]
+    rows, lanes = center.shape
+    sub = lax.broadcasted_iota(jnp.int32, (8, lanes), 0)
+    lane = lax.broadcasted_iota(jnp.int32, (rows, lanes), 1)
+
+    def later(block):
+        return jnp.where(sub < 7, pltpu.roll(block, 7, 0), 0.0)
+
+    def earlier(block):
+        return jnp.where(sub > 0, pltpu.roll(block, 1, 0), 0.0)
+
+    first, second = center[0:8], center[8:16]
+    last, before = center[rows - 8 :], center[rows - 16 : rows - 8]
+    late = later(first)
+    early = earlier(last)
+    near = jnp.concatenate([center[8:], late], 0) + jnp.concatenate([early, center[:-8]], 0)
+    far = jnp.concatenate([center[16:], late, later(second)], 0) + jnp.concatenate(
+        [earlier(before), early, center[:-16]], 0
+    )
+    near = near + (field[slot, z + 1] + field[slot, z + 3])
+    far = far + (field[slot, z] + field[slot, z + 4])
+    near = near + jnp.where(lane >= 1, pltpu.roll(center, 1, 1), 0.0)
+    near = near + jnp.where(lane < lanes - 1, pltpu.roll(center, lanes - 1, 1), 0.0)
+    far = far + jnp.where(lane >= 2, pltpu.roll(center, 2, 1), 0.0)
+    far = far + jnp.where(lane < lanes - 2, pltpu.roll(center, lanes - 2, 1), 0.0)
+    return center, 16.0 * near - far - 90.0 * center
+
+
+def scatter_kernel(row_ref, y_ref, obs_ref, out_ref, spread):
+    receivers, steps = obs_ref.shape
+    lanes = out_ref.shape[2]
+    tile = out_ref.shape[1]
+
+    @pl.when(pl.program_id(0) == 0)
+    def _():
+        lane = lax.broadcasted_iota(jnp.int32, (receivers, lanes), 1)
+        at = lane == y_ref[...]
+        for k in range(steps):
+            column = obs_ref[:, k : k + 1]
+            high = column.astype(jnp.bfloat16).astype(jnp.float32)
+            low = column - high
+            cols = pl.ds(k * lanes, lanes)
+            spread[0, :, cols] = jnp.where(at, high, 0.0).astype(jnp.bfloat16)
+            spread[1, :, cols] = jnp.where(at, low, 0.0).astype(jnp.bfloat16)
+        cols = pl.ds(steps * lanes, lanes)
+        spread[0, :, cols] = jnp.where(at, 1.0, 0.0).astype(jnp.bfloat16)
+        spread[1, :, cols] = jnp.zeros((receivers, lanes), jnp.bfloat16)
+
+    ids = lax.broadcasted_iota(jnp.int32, (tile, receivers), 0) + pl.program_id(0) * tile
+    chosen = jnp.where(ids == row_ref[...], 1.0, 0.0).astype(jnp.bfloat16)
+    total = jnp.dot(chosen, spread[0], preferred_element_type=jnp.float32)
+    total = total + jnp.dot(chosen, spread[1], preferred_element_type=jnp.float32)
+    for k in range(steps + 1):
+        out_ref[k] = total[:, k * lanes : (k + 1) * lanes]
+
+
+def scatter(cells, observed, planes_all, rows_x, rows_y):
+    steps, receivers = observed.shape
+    groups = rows_x // 8
+    x = (cells // rows_y) % rows_x
+    row = (cells // (rows_x * rows_y)) * rows_x + (x % groups) * 8 + x // groups
+    lanes = cells % rows_y
+    rows_all = planes_all * rows_x
+    tile = 256
+    return pl.pallas_call(
+        scatter_kernel,
+        grid=(rows_all // tile,),
+        in_specs=[
+            pl.BlockSpec((1, receivers), lambda t: (0, 0)),
+            pl.BlockSpec((receivers, 1), lambda t: (0, 0)),
+            pl.BlockSpec((receivers, steps), lambda t: (0, 0)),
+        ],
+        out_specs=pl.BlockSpec((steps + 1, tile, rows_y), lambda t: (0, t, 0)),
+        out_shape=jax.ShapeDtypeStruct((steps + 1, rows_all, rows_y), jnp.float32),
+        scratch_shapes=[pltpu.VMEM((2, receivers, (steps + 1) * rows_y), jnp.bfloat16)],
+        compiler_params=pltpu.CompilerParams(vmem_limit_bytes=32 * 2**20),
+        cost_estimate=pl.CostEstimate(
+            flops=4 * rows_all * receivers * (steps + 1) * rows_y,
+            bytes_accessed=4 * (steps + 1) * rows_all * rows_y,
+            transcendentals=0,
+        ),
+        name="receiver_scatter",
+    )(row[None, :], lanes[:, None], observed.T)
+
+
+def load_blocks(meta, blocks, field, planes, rows):
+    ends = field.shape[1]
+    for slot in range(2):
+        for z in (0, 1, ends - 2, ends - 1):
+            field[slot, z] = jnp.zeros(field.shape[2:], jnp.float32)
+    for b, block in enumerate(blocks):
+
+        @pl.loop(0, planes)
+        def _(p):
+            z = meta[b] + p + 2
+            interleave(field, (1, z), block, (0, p), rows)
+            interleave(field, (0, z), block, (1, p), rows)
+
+
+def for_owned(meta, planes, body):
+    for owned in (True, False):
+        core = meta[4] if owned else 1 - meta[4]
+
+        @pl.loop(0, 2 * planes)
+        def _(index):
+            chip, p = index // planes, index % planes
+            z = (2 * chip + core) * planes + p
+            body(z, chip if owned else None, p)
+
+
+def forward_kernel(meta, wave, own, mate, over, far, c0, c1, c2, c3, obs, count, lap_ref, inject_ref, cour_ref, field):
+    step = pl.program_id(0)
+    planes, rows, lanes = c0.shape
+
+    @pl.when(step == 0)
+    def _():
+        load_blocks(meta, (own, mate, over, far), field, planes, rows)
+        for b, block in enumerate((c0, c1, c2, c3)):
+
+            @pl.loop(0, planes)
+            def _(p):
+                interleave(cour_ref, (meta[b] + p,), block, (p,), rows, 1.0 / 12.0)
+
+    now = lax.rem(step, 2)
+    then = 1 - now
+
+    def body(z, chip, p):
+        center, lap = lap12(field, now, z)
+        if chip is not None:
+            lap_ref[0, p, chip] = lap
+        newer = 2.0 * center - field[then, z + 2] + cour_ref[z] * lap
+        field[then, z + 2] = newer
+        inject_ref[0, z] = obs[0, z] - count[0, z] * newer
+
+    for_owned(meta, planes, body)
+
+    z, row, lane = meta[5], pl.multiple_of(meta[6], 8), meta[8]
+    here = (lax.broadcasted_iota(jnp.int32, (8, lanes), 0) == meta[7]) & (
+        lax.broadcasted_iota(jnp.int32, (8, lanes), 1) == lane
+    )
+    strength = jnp.where(here, 12.0 * wave[step], 0.0)
+    tile = pl.ds(row, 8)
+    slab, p = z // planes, lax.rem(z, planes)
+
+    @pl.when(lax.rem(slab, 2) == meta[4])
+    def _():
+        lap_ref[0, p, slab // 2, tile, :] += strength
+
+    moved = cour_ref[z, tile, :] * strength
+    field[then, z + 2, tile, :] += moved
+    inject_ref[0, z, tile, :] -= count[0, z, tile, :] * moved
+
+
+def adjoint_kernel(meta, own, mate, over, far, cour, lap_ref, inject, grad_ref, field, total):
+    step = pl.program_id(0)
+    planes, rows, lanes = own.shape[1:]
+    groups = rows // 8
+
+    @pl.when(step == 0)
+    def _():
+        load_blocks(meta, (own, mate, over, far), field, planes, rows)
+
+        @pl.loop(0, 4 * planes)
+        def _(z):
+            field[0, z + 2] = field[0, z + 2] * cour[z]
+            field[1, z + 2] = field[1, z + 2] * cour[z]
+
+        @pl.loop(0, 2 * planes)
+        def _(index):
+            total[index] = jnp.zeros((rows, lanes), jnp.float32)
+
+    now = lax.rem(step, 2)
+    then = 1 - now
+
+    def body(z, chip, p):
+        center, lap = lap12(field, now, z)
+        newer = 2.0 * center - field[then, z + 2] + cour[z] * (lap - inject[0, z])
+        field[then, z + 2] = newer
+        if chip is not None:
+            at = chip * planes + p
+            total[at] = total[at] + newer * lap_ref[0, p, chip]
+
+    for_owned(meta, planes, body)
+
+    @pl.when(step == pl.num_programs(0) - 1)
+    def _():
+        @pl.loop(0, 2 * planes)
+        def _(index):
+            chip, p = index // planes, index % planes
+            z = (2 * chip + meta[4]) * planes + p
+            value = total[index] / (12.0 * cour[z])
+            for i in range(groups):
+                grad_ref[p, chip, pl.ds(i, 8, stride=groups), :] = value[i * 8 : (i + 1) * 8]
+
+
+def whole_shards(
+    courant_sq, momentum, fwd_prev, fwd_cur, adj_next, adj_cur, observed, src_cells, rec_cells, ckpt_step
+):
+    _, planes, rows_x, rows_y = fwd_cur.shape
+    steps = observed.shape[1]
+    chip, core = lax.axis_index("chip"), lax.axis_index("core")
+    groups = rows_x // 8
+    planes_all = 4 * planes
+    cells_all = planes_all * rows_x * rows_y
+    swap = [(0, 1), (1, 0)]
+
+    def pick(pair, shot):
+        return jnp.stack([lax.dynamic_index_in_dim(f, shot, 0, keepdims=False) for f in pair])
+
+    forward = (fwd_prev, fwd_cur)
+    adjoint = (adj_next, adj_cur)
+    c2 = lax.ppermute(courant_sq, "chip", swap)
+    over = lax.ppermute(pick(forward, 1 - chip), "chip", swap)
+    own = pick(forward, chip)
+    mate = lax.ppermute(own, "core", swap)
+    c1 = lax.ppermute(courant_sq, "core", swap)
+
+    cells = lax.dynamic_index_in_dim(rec_cells, chip, 0, keepdims=False)
+    traces = lax.dynamic_index_in_dim(observed, chip, 0, keepdims=False)
+    placed = scatter(cells, traces, planes_all, rows_x, rows_y)
+    placed = placed.reshape(steps + 1, planes_all, rows_x, rows_y)
+
+    over, to_send = lax.optimization_barrier((over, pick(adjoint, 1 - chip)))
+    far = lax.ppermute(over, "core", swap)
+    c3 = lax.ppermute(c2, "core", swap)
+    adj_over = lax.ppermute(to_send, "chip", swap)
+    adj_own = pick(adjoint, chip)
+    adj_mate = lax.ppermute(adj_own, "core", swap)
+
+    source = lax.dynamic_index_in_dim(src_cells, chip, 0, keepdims=False)
+    x = (source // rows_y) % rows_x
+    slabs = [2 * chip + core, 2 * chip + 1 - core, 2 * (1 - chip) + core, 2 * (1 - chip) + 1 - core]
+    meta = jnp.stack(
+        [slab * planes for slab in slabs]
+        + [core, source // (rows_x * rows_y), (x % groups) * 8, x // groups, source % rows_y]
+    ).astype(jnp.int32)
+    wave = jnp.stack([wave_value(ckpt_step, k) for k in range(steps)])
+
+    field_block = pl.BlockSpec((2, planes, rows_x, rows_y), lambda k: (0, 0, 0, 0))
+    slab_block = pl.BlockSpec((planes, rows_x, rows_y), lambda k: (0, 0, 0))
+    whole_block = pl.BlockSpec((planes_all, rows_x, rows_y), lambda k: (0, 0, 0))
+    step_block = pl.BlockSpec((1, planes_all, rows_x, rows_y), lambda k: (k, 0, 0, 0))
+    count_block = pl.BlockSpec((1, planes_all, rows_x, rows_y), lambda k: (steps, 0, 0, 0))
+    lap_shape = (planes, 2, rows_x, rows_y)
+    smem = pl.BlockSpec(memory_space=pltpu.SMEM)
+    scratch = pltpu.VMEM((2, planes_all + 4, rows_x, rows_y), jnp.float32)
+    params = pltpu.CompilerParams(vmem_limit_bytes=48 * 2**20)
+    cost = pl.CostEstimate(flops=30 * steps * cells_all, bytes_accessed=16 * steps * cells_all, transcendentals=0)
+    laps, inject, cour = pl.pallas_call(
+        forward_kernel,
+        grid=(steps,),
+        in_specs=[smem, smem] + [field_block] * 4 + [slab_block] * 4 + [step_block, count_block],
+        out_specs=[pl.BlockSpec((1, *lap_shape), lambda k: (k, 0, 0, 0, 0)), step_block, whole_block],
+        out_shape=[
+            jax.ShapeDtypeStruct((steps, *lap_shape), jnp.float32),
+            jax.ShapeDtypeStruct((steps, planes_all, rows_x, rows_y), jnp.float32),
+            jax.ShapeDtypeStruct((planes_all, rows_x, rows_y), jnp.float32),
+        ],
+        scratch_shapes=[scratch],
+        compiler_params=params,
+        cost_estimate=cost,
+        name="forward_steps",
+    )(meta, wave, own, mate, over, far, courant_sq, c1, c2, c3, placed, placed)
+
+    adj_far = lax.ppermute(adj_over, "core", swap)
+    back_block = pl.BlockSpec((1, planes_all, rows_x, rows_y), lambda k: (steps - 1 - k, 0, 0, 0))
+    gradient = pl.pallas_call(
+        adjoint_kernel,
+        grid=(steps,),
+        in_specs=[smem]
+        + [field_block] * 4
+        + [whole_block, pl.BlockSpec((1, *lap_shape), lambda k: (steps - 1 - k, 0, 0, 0, 0)), back_block],
+        out_specs=pl.BlockSpec(lap_shape, lambda k: (0, 0, 0, 0)),
+        out_shape=jax.ShapeDtypeStruct(lap_shape, jnp.float32),
+        scratch_shapes=[scratch, pltpu.VMEM((2 * planes, rows_x, rows_y), jnp.float32)],
+        compiler_params=params,
+        cost_estimate=cost,
+        name="adjoint_steps",
+    )(meta, adj_own, adj_mate, adj_over, adj_far, cour, laps, inject)
+
+    shot = lax.axis_index("shot")
+    first = (2 * chip + core) * planes
+    depths = (first + jnp.arange(planes)).astype(jnp.float32)
+    weights = 1.0 + 2.0 * depths / (planes_all - 1)
+    parts = gradient.reshape(2 * planes, rows_x, rows_y)
+    parts = lax.all_to_all(parts, ("shot", "chip"), 0, 0, tiled=True)
+    weight = lax.dynamic_index_in_dim(weights, shot, 0)
+    scaled = weight * jnp.sum(parts, axis=0)
+    moment = lax.dynamic_index_in_dim(momentum, shot, 0, keepdims=False)
+    sums = jnp.stack(
+        [
+            jnp.sum(scaled * scaled),
+            jnp.sum(weight * moment * moment),
+            jnp.sum(weight * moment * scaled),
+            jnp.sum(weight * scaled * scaled),
+        ]
+    )
+    carried = jnp.concatenate([scaled, jnp.broadcast_to(jnp.pad(sums, (0, 4))[:, None], (8, rows_y))], 0)
+    spread = jnp.broadcast_to(carried[None], (planes, rows_x + 8, rows_y))
+    spread = lax.all_to_all(spread, "shot", 0, 0, tiled=True)
+    scaled = spread[:, :rows_x]
+    sums = jnp.sum(spread[:, rows_x:], axis=0)
+    sums = lax.all_to_all(jnp.broadcast_to(sums[None], (4, 8, rows_y)), ("chip", "core"), 0, 0, tiled=True)
+    sums = jnp.sum(sums, axis=0)[:, 0]
+    factor = lax.rsqrt(sums[0] / cells_all + EPSILON)
+    kinetic = 0.5 * (sums[1] - factor * sums[2] + 0.25 * factor * factor * sums[3]) / cells_all
+    return momentum - 0.5 * factor * scaled, kinetic
+
+
 def solution(mesh):
-    placed = (
-        P("depth", None, None),
-        P("depth", None, None),
-        P("shot", "depth", None, None),
-        P("shot", "depth", None, None),
-        P("shot", "depth", None, None),
-        P("shot", "depth", None, None),
-        P("shot", None, None),
-        P("shot"),
-        P("shot", None),
-        P(),
-    )
-    return jax.shard_map(
-        shards, mesh=mesh, in_specs=placed, out_specs=(P("depth", None, None), P()), check_vma=False
-    )
+    shots, slabs = mesh.shape["shot"], mesh.shape["depth"]
+
+    def placed(depth):
+        field = P("shot", depth, None, None)
+        slab = P(depth, None, None)
+        inputs = (slab, slab, field, field, field, field, P("shot", None, None), P("shot"), P("shot", None), P())
+        return dict(in_specs=inputs, out_specs=(slab, P()), check_vma=False)
+
+    slab_plan = jax.shard_map(slab_shards, mesh=mesh, **placed("depth"))
+    if slabs != 4:
+        return slab_plan
+    chips = Mesh(mesh.devices.reshape(shots, 2, 2), ("shot", "chip", "core"))
+    whole_plan = jax.shard_map(whole_shards, mesh=chips, **placed(("chip", "core")))
+
+    def run(courant_sq, momentum, fwd_prev, *rest):
+        total, planes, rows_x, rows_y = fwd_prev.shape
+        fits = total == 2 * shots and planes == 4 * shots and rows_y == 128 and rows_x % 16 == 0
+        plan = whole_plan if fits else slab_plan
+        return plan(courant_sq, momentum, fwd_prev, *rest)
+
+    return run

time: 486 us -> 169 us (0.35); the launches traced: 477 us -> 168 us
  local copies, waits for them, and re-layouts: 99.7 us -> 11.8 us
  other arithmetic: 90.4 us -> 7.58 us
  starting transfers between devices: 93.7 us -> 13.5 us
  Pallas kernels: 0 us -> 76.2 us
  waiting for transfers between devices: 93.9 us -> 31.2 us
  blocking collectives: 79.8 us -> 19.3 us
  between operations: 19.7 us -> 8.36 us
    ppermute x32 -> x9, starting transfers between devices: 93.6 us -> 6.37 us  [the longest x1 3 us: whole_shards(): over = lax.ppermute(pick(forward, 1 - chip), 'chip', swap)]
    psum x2 -> x0, blocking collectives: 79.8 us -> none  [the longest x1 40.1 us: statistics(): energy = lax.psum(jnp.sum(weight * halfway * halfway), ('shot', 'depth'))]
    pallas_call x0 -> x3, Pallas kernels: none -> 76.2 us  [the longest x1 34.1 us: whole_shards(): pl.pallas_call(forward_kernel, grid=(steps,), in_specs=[smem, smem] + [fi...]
    psum x1 -> x0, waiting for transfers between devices: 73.6 us -> none  [shards(): gradient = lax.psum(gradient, 'shot')]
    gather x16 -> x0, local copies, waits for them, and re-layouts: 73 us -> none  [sample(): values = jnp.take_along_axis(field.reshape(shot_count, -1), target, axis=1)]
    unnamed x14 -> x0, other arithmetic: 53.6 us -> none
    all_to_all x0 -> x2, blocking collectives: none -> 19.3 us  [the longest x1 13.1 us: whole_shards(): spread = lax.all_to_all(spread, 'shot', 0, 0, tiled=True)]
    add x26 -> x1, other arithmetic: 15.9 us -> 0.01 us  [whole_shards(): weights = 1.0 + 2.0 * depths / (planes_all - 1)]
  transfers between devices with their start and end apart: 33 -> 10, of which waited for: 12 -> 3; matrix products, arithmetic and copies ran while one was open for 17% -> 4% of each run, Pallas kernels for 0% -> 25%
where the time goes in v1:
time: 169 us; the launch traced here: 168 us
  Pallas kernels  76.2 us (45%)
  waiting for transfers between devices  31.2 us (18%)
  blocking collectives  19.3 us (11%)
  starting transfers between devices  13.5 us (8%)
  local copies, waits for them, and re-layouts  11.8 us (7%)
  between operations  8.36 us (5%)
  other arithmetic  7.58 us (4%)
    pallas_call x1, Pallas kernels, whole_shards(): pl.pallas_call(forward_kernel, grid=(steps,), in_specs=[smem, smem] + [fi...  34.1 us
    pallas_call x1, Pallas kernels, whole_shards(): pl.pallas_call(adjoint_kernel, grid=(steps,), in_specs=[smem] + [field_bl...  33.7 us
    all_to_all x1, waiting for transfers between devices, whole_shards(): parts = lax.all_to_all(parts, ('shot', 'chip'), 0, 0, tiled=True)  14.6 us
    all_to_all x1, blocking collectives, whole_shards(): spread = lax.all_to_all(spread, 'shot', 0, 0, tiled=True)  13.1 us
    ppermute x1, waiting for transfers between devices, whole_shards(): over = lax.ppermute(pick(forward, 1 - chip), 'chip', swap)  10.5 us
    pallas_call x1, Pallas kernels, scatter(): pl.pallas_call(scatter_kernel, grid=(rows_all // tile,), in_specs=[pl.Blo...  8.33 us
    all_to_all x1, starting transfers between devices, whole_shards(): parts = lax.all_to_all(parts, ('shot', 'chip'), 0, 0, tiled=True)  7.11 us
    all_to_all x1, blocking collectives, whole_shards(): lax.all_to_all(jnp.broadcast_to(sums[None], (4, 8, rows_y)), ('chip', 'co...  6.2 us
  transfers between devices with their start and end apart: 10, of which 3 were waited for; matrix products, arithmetic and copies ran while one was open for 4% of the time, Pallas kernels for 25%

profile of v1, /device:TPU:0, one launch (start us, length us, event | category | flops | bytes accessed | tf_op | source)
XLA Modules:
  0.0 167.9 jit_solution(10429359095197318342)
XLA Ops:
  0.6 0.0 copy-start
  0.6 0.0 copy-start.6
  0.7 0.0 copy-start.7
  0.7 1.3 constant_dynamic-slice_fusion.2
  2.0 3.0 %collective-permute-start.1 = (f32[2,8,64,128]{3,2,1,0:T(8,128)S(1)}, f32[2,8,64,128]{3,2,1,0:T(8,128)S(1)}, u32[]{:S(2)}, u32[]{:S(2)}) collective-permute-start(f32[2,8,64,128]{3,2,1,0:T(8,128)S(1)} %pad_maximum_fusion.1), channel_id=1, source_target_pairs={{0,2},{2,0},{1,3},{3,1},{4,6},{6,4},{5,7},{7,5},{8,10},{10,8},{9,1... | collective-permute-start | bytes 1572872 | tf_op jit(solution)/shard_map/ppermute | solution.py:356
  5.0 0.1 collective-permute-start.7
  5.1 0.0 collective-permute-start.6
  5.1 1.3 constant_dynamic-slice_fusion.4
  6.4 0.8 pad_maximum_fusion.2
  7.3 10.5 %collective-permute-done.1.over = f32[2,8,64,128]{3,2,1,0:T(8,128)S(1)} collective-permute-done((f32[2,8,64,128]{3,2,1,0:T(8,128)S(1)}, f32[2,8,64,128]{3,2,1,0:T(8,128)S(1)}, u32[]{:S(2)}, u32[]{:S(2)}) %collective-permute-start.1) | collective-permute-done | bytes 524320 | tf_op jit(solution)/shard_map/ppermute | solution.py:356
  17.8 2.1 %collective-permute-start.2 = (f32[2,8,64,128]{3,2,1,0:T(8,128)}, f32[2,8,64,128]{3,2,1,0:T(8,128)S(1)}, u32[]{:S(2)}, u32[]{:S(2)}) collective-permute-start(f32[2,8,64,128]{3,2,1,0:T(8,128)} %pad_maximum_fusion.2), channel_id=1, source_target_pairs={{0,2},{2,0},{1,3},{3,1},{4,6},{6,4},{5,7},{7,5},{8,10},{10,8},{9,1... | collective-permute-start | bytes 1572872 | tf_op jit(solution)/shard_map/ppermute | solution.py:369
  19.9 0.1 collective-permute-start.4
  20.0 0.6 collective-permute-start
  20.6 0.0 copy-done.6
  20.6 0.1 fusion.9
  21.4 0.0 copy-done.7
  21.4 0.6 dynamic_slice.46
  25.1 0.9 copy.17
  26.0 1.7 %add_select_fusion.y_ref = s32[512,1]{1,0:T(8,128)} fusion(s32[512,1]{1,0:T(8,128)} %copy.17), kind=kLoop, calls=%fused_computation.4 | loop fusion | flops 5632 | bytes 4096 | tf_op jit(solution)/shard_map/jit(remainder)/select_n | solution.py:205
  27.7 0.0 collective-permute-done.7.c2
  27.7 0.0 collective-permute-start.5
  27.8 6.1 %collective-permute-done.2.over = f32[2,8,64,128]{3,2,1,0:T(8,128)S(1)} collective-permute-done((f32[2,8,64,128]{3,2,1,0:T(8,128)}, f32[2,8,64,128]{3,2,1,0:T(8,128)S(1)}, u32[]{:S(2)}, u32[]{:S(2)}) %collective-permute-start.2) | collective-permute-done | bytes 524320 | tf_op jit(solution)/shard_map/ppermute | solution.py:369
  33.8 0.0 collective-permute-start.3
  33.8 0.0 copy-done
  33.8 0.8 copy.20
  34.6 0.1 stack.113.wave
  34.7 0.1 stack.101.meta
  34.8 0.0 collective-permute-done.6.c1
  34.8 0.6 collective-permute-start.8
  35.4 0.0 copy-start.3
  35.4 0.9 copy-done.3
  36.3 0.0 copy-start.4
  36.3 0.9 copy-done.4
  37.3 0.0 copy-start.2
  37.3 8.3 %receiver_scatter.1 = f32[9,2048,128]{2,1,0:T(8,128)S(1)} custom-call(s32[1,512]{1,0:T(1,128)S(1)} %get-tuple-element.30.row_ref, s32[512,1]{1,0:T(8,128)S(1)} %copy-done.3, f32[512,8]{1,0:T(8,128)S(1)} %bitcast.39), custom_call_target="tpu_custom_call" | custom-call | flops 4831838208 | bytes 9437184 | tf_op jit(solution)/shard_map/receiver_scatter/pallas_call | solution.py:208
  45.6 0.0 copy-start.1
  45.6 3.6 %copy-done.1 = f32[9,2048,128]{2,1,0:T(8,128)} copy-done((f32[9,2048,128]{2,1,0:T(8,128)}, f32[9,2048,128]{2,1,0:T(8,128)S(1)}, u32[]{:S(2)}) %copy-start.1) | copy-done | bytes 9437208
  49.3 0.0 collective-permute-done.4.mate
  49.3 0.0 collective-permute-done.8.c3
  49.3 0.0 collective-permute-done.5.far
  49.3 0.0 copy-done.2
  49.3 34.1 %forward_steps.1 = (f32[8,8,2,64,128]{4,3,2,1,0:T(8,128)}, f32[8,32,64,128]{3,2,1,0:T(8,128)}, f32[32,64,128]{2,1,0:T(8,128)S(1)}) custom-call(s32[9]{0:T(128)S(1)} %stack.101.meta, f32[8]{0:T(128)S(1)} %stack.113.wave, f32[2,8,64,128]{3,2,1,0:T(8,128)S(1)} %pad_maximum_fusion.3.own, f32[2,8,64,128]{3,2,1,0:T(8,128)S(1)} %collective-permute-done.4.mate, ...), custom_call_target="tpu_custom_call" | custom-call | flops 62914560 | bytes 33554432 | tf_op jit(solution)/shard_map/forward_steps/pallas_call | solution.py:392
  83.4 0.0 collective-permute-done.mate
  83.4 0.0 collective-permute-done.3.far
  83.4 0.0 copy-start.5
  83.5 33.7 %adjoint_steps.1 = f32[8,2,64,128]{3,2,1,0:T(8,128)} custom-call(s32[9]{0:T(128)S(1)} %stack.101.meta, f32[2,8,64,128]{3,2,1,0:T(8,128)S(1)} %pad_maximum_fusion.own, f32[2,8,64,128]{3,2,1,0:T(8,128)S(1)} %collective-permute-done.mate, f32[2,8,64,128]{3,2,1,0:T(8,128)S(1)} %collective-permute-done.2.over, f32[2,8,64,128]{3,2,1,0:T(8,128)} %collective-permute-done.3.far, ...), custom_call_target="tpu_custom_call" | custom-call | flops 62914560 | bytes 33554432 | tf_op jit(solution)/shard_map/adjoint_steps/pallas_call | solution.py:410
  117.2 7.1 %all-to-all-start = ((f32[16,64,128]{2,1,0:T(8,128)}), f32[16,64,128]{2,1,0:T(8,128)S(1)}, u32[]{:S(2)}, u32[]{:S(2)}) async-start(f32[16,64,128]{2,1,0:T(8,128)} %bitcast.23), calls=%async_computation | async-start | bytes 1048576 | tf_op jit(solution)/shard_map/all_to_all | solution.py:429
  124.3 0.6 dynamic_slice.45
  124.9 14.6 %all-to-all-done = f32[16,64,128]{2,1,0:T(8,128)S(1)} async-done(((f32[16,64,128]{2,1,0:T(8,128)}), f32[16,64,128]{2,1,0:T(8,128)S(1)}, u32[]{:S(2)}, u32[]{:S(2)}) %all-to-all-start) | async-done | bytes 524320 | tf_op jit(solution)/shard_map/all_to_all | solution.py:429
  139.6 0.0 copy-done.5
  139.6 1.4 fusion.2
  140.9 2.6 %select_maximum_fusion = f32[8]{0:T(128)S(1)} fusion(f32[1]{0:T(128)} %bitcast.28, f32[1]{0:T(128)} %bitcast.27, f32[1]{0:T(128)} %bitcast.26, f32[1]{0:T(128)} %bitcast.24), kind=kLoop, calls=%fused_computation.50 | loop fusion | flops 64 | bytes 48 | tf_op jit(solution)/shard_map/stack | solution.py:433
  143.5 0.1 pad.6.clone
  143.6 0.1 pad_maximum_fusion.4
  143.7 13.1 %all_to_all.15 = f32[8,72,128]{2,1,0:T(8,128)S(1)} all-to-all(f32[8,72,128]{2,1,0:T(8,128)S(1)} %broadcast_in_dim.7), channel_id=1, replica_groups=mesh['shot'=8,'chip'=2,'core'=2] {'shot'}, dimensions={0} | all-to-all | bytes 589824 | tf_op jit(solution)/shard_map/all_to_all | solution.py:443
  156.8 6.2 %all_to_all.16 = f32[4,8,128]{2,1,0:T(8,128)S(1)} all-to-all(f32[4,8,128]{2,1,0:T(8,128)S(1)} %broadcast_in_dim.8), channel_id=1, replica_groups=mesh['shot'=8,'chip'=2,'core'=2] {'chip','core'}, dimensions={0} | all-to-all | bytes 32768 | tf_op jit(solution)/shard_map/all_to_all | solution.py:446
  163.0 0.5 fusion.10
  166.1 0.7 fusion.1
  (10 shorter events, 0.2 us)
Async XLA Ops:
  0.6 33.2 %copy-start = (f32[2,8,512]{2,1,0:T(8,128)S(1)}, f32[2,8,512]{2,1,0:T(8,128)}, u32[]{:S(2)}) copy-start(f32[2,8,512]{2,1,0:T(8,128)} %param.16) | copy-start | bytes 98308
  0.6 19.9 %copy-start.6 = (s32[2,512]{1,0:T(2,128)S(1)}, s32[2,512]{1,0:T(2,128)}, u32[]{:S(2)}) copy-start(s32[2,512]{1,0:T(2,128)} %param.18) | copy-start | bytes 12292
  0.7 20.8 %copy-start.7 = (s32[2]{0:T(128)S(1)}, s32[2]{0:T(128)}, u32[]{:S(2)}) copy-start(s32[2]{0:T(128)} %param.17) | copy-start | bytes 28
  2.0 15.8 %collective-permute-start.1 = (f32[2,8,64,128]{3,2,1,0:T(8,128)S(1)}, f32[2,8,64,128]{3,2,1,0:T(8,128)S(1)}, u32[]{:S(2)}, u32[]{:S(2)}) collective-permute-start(f32[2,8,64,128]{3,2,1,0:T(8,128)S(1)} %pad_maximum_fusion.1), channel_id=1, source_target_pairs={{0,2},{2,0},{1,3},{3,1},{4,6},{6,4},{5,7},{7,5},{8,10},{10,8},{9,1... | collective-permute-start | bytes 1572872 | tf_op jit(solution)/shard_map/ppermute | solution.py:356
  5.0 22.7 %collective-permute-start.7 = (f32[8,64,128]{2,1,0:T(8,128)}, f32[8,64,128]{2,1,0:T(8,128)S(1)}, u32[]{:S(2)}, u32[]{:S(2)}) collective-permute-start(f32[8,64,128]{2,1,0:T(8,128)} %c0.1), channel_id=1, source_target_pairs={{0,2},{2,0},{1,3},{3,1},{4,6},{6,4},{5,7},{7,5},{8,10},{10,8},{9,1... | collective-permute-start | bytes 786440 | tf_op jit(solution)/shard_map/ppermute | solution.py:355
  5.1 29.7 %collective-permute-start.6 = (f32[8,64,128]{2,1,0:T(8,128)}, f32[8,64,128]{2,1,0:T(8,128)}, u32[]{:S(2)}, u32[]{:S(2)}) collective-permute-start(f32[8,64,128]{2,1,0:T(8,128)} %c0.1), channel_id=1, source_target_pairs={{0,1},{1,0},{2,3},{3,2},{4,5},{5,4},{6,7},{7,6},{8,9},{9,8},{10,11... | collective-permute-start | bytes 786440 | tf_op jit(solution)/shard_map/ppermute | solution.py:359
  17.8 16.0 %collective-permute-start.2 = (f32[2,8,64,128]{3,2,1,0:T(8,128)}, f32[2,8,64,128]{3,2,1,0:T(8,128)S(1)}, u32[]{:S(2)}, u32[]{:S(2)}) collective-permute-start(f32[2,8,64,128]{3,2,1,0:T(8,128)} %pad_maximum_fusion.2), channel_id=1, source_target_pairs={{0,2},{2,0},{1,3},{3,1},{4,6},{6,4},{5,7},{7,5},{8,10},{10,8},{9,1... | collective-permute-start | bytes 1572872 | tf_op jit(solution)/shard_map/ppermute | solution.py:369
  19.9 29.4 %collective-permute-start.4 = (f32[2,8,64,128]{3,2,1,0:T(8,128)S(1)}, f32[2,8,64,128]{3,2,1,0:T(8,128)S(1)}, u32[]{:S(2)}, u32[]{:S(2)}) collective-permute-start(f32[2,8,64,128]{3,2,1,0:T(8,128)S(1)} %pad_maximum_fusion.3.own), channel_id=1, source_target_pairs={{0,1},{1,0},{2,3},{3,2},{4,5},{5,4},{6,7},{7,6},{8,9},{9,8},{10,11... | collective-permute-start | bytes 1572872 | tf_op jit(solution)/shard_map/ppermute | solution.py:358
  20.0 63.4 %collective-permute-start = (f32[2,8,64,128]{3,2,1,0:T(8,128)S(1)}, f32[2,8,64,128]{3,2,1,0:T(8,128)S(1)}, u32[]{:S(2)}, u32[]{:S(2)}) collective-permute-start(f32[2,8,64,128]{3,2,1,0:T(8,128)S(1)} %pad_maximum_fusion.own), channel_id=1, source_target_pairs={{0,1},{1,0},{2,3},{3,2},{4,5},{5,4},{6,7},{7,6},{8,9},{9,8},{10,11... | collective-permute-start | bytes 1572872 | tf_op jit(solution)/shard_map/ppermute | solution.py:371
  27.7 21.5 %collective-permute-start.5 = (f32[2,8,64,128]{3,2,1,0:T(8,128)S(1)}, f32[2,8,64,128]{3,2,1,0:T(8,128)}, u32[]{:S(2)}, u32[]{:S(2)}) collective-permute-start(f32[2,8,64,128]{3,2,1,0:T(8,128)S(1)} %collective-permute-done.1.over), channel_id=1, source_target_pairs={{0,1},{1,0},{2,3},{3,2},{4,5},{5,4},{6,7},{7,6},{8,9},{9,8},{10,11... | collective-permute-start | bytes 1572872 | tf_op jit(solution)/shard_map/ppermute | solution.py:367
  33.8 49.6 %collective-permute-start.3 = (f32[2,8,64,128]{3,2,1,0:T(8,128)S(1)}, f32[2,8,64,128]{3,2,1,0:T(8,128)}, u32[]{:S(2)}, u32[]{:S(2)}) collective-permute-start(f32[2,8,64,128]{3,2,1,0:T(8,128)S(1)} %collective-permute-done.2.over), channel_id=1, source_target_pairs={{0,1},{1,0},{2,3},{3,2},{4,5},{5,4},{6,7},{7,6},{8,9},{9,8},{10,11... | collective-permute-start | bytes 1572872 | tf_op jit(solution)/shard_map/ppermute | solution.py:408
  34.8 14.4 %collective-permute-start.8 = (f32[8,64,128]{2,1,0:T(8,128)S(1)}, f32[8,64,128]{2,1,0:T(8,128)S(1)}, u32[]{:S(2)}, u32[]{:S(2)}) collective-permute-start(f32[8,64,128]{2,1,0:T(8,128)S(1)} %collective-permute-done.7.c2), channel_id=1, source_target_pairs={{0,1},{1,0},{2,3},{3,2},{4,5},{5,4},{6,7},{7,6},{8,9},{9,8},{10,11... | collective-permute-start | bytes 786440 | tf_op jit(solution)/shard_map/ppermute | solution.py:368
  35.4 0.9 copy-start.3
  36.3 0.9 copy-start.4
  37.3 12.0 %copy-start.2 = (f32[8,64,128]{2,1,0:T(8,128)S(1)}, f32[8,64,128]{2,1,0:T(8,128)}, u32[]{:S(2)}) copy-start(f32[8,64,128]{2,1,0:T(8,128)} %c0.1) | copy-start | bytes 786436
  45.6 3.6 %copy-start.1 = (f32[9,2048,128]{2,1,0:T(8,128)}, f32[9,2048,128]{2,1,0:T(8,128)S(1)}, u32[]{:S(2)}) copy-start(f32[9,2048,128]{2,1,0:T(8,128)S(1)} %receiver_scatter.1) | copy-start | bytes 28311556
  83.4 56.1 %copy-start.5 = (f32[8,64,128]{2,1,0:T(8,128)S(1)}, f32[8,64,128]{2,1,0:T(8,128)}, u32[]{:S(2)}) copy-start(f32[8,64,128]{2,1,0:T(8,128)} %param.11) | copy-start | bytes 786436
  117.2 22.4 %all-to-all-start = ((f32[16,64,128]{2,1,0:T(8,128)}), f32[16,64,128]{2,1,0:T(8,128)S(1)}, u32[]{:S(2)}, u32[]{:S(2)}) async-start(f32[16,64,128]{2,1,0:T(8,128)} %bitcast.23), calls=%async_computation | async-start | bytes 1048576 | tf_op jit(solution)/shard_map/all_to_all | solution.py:429

commit v2 on v1

--- a/solution.py
+++ b/solution.py
@@ -140,8 +140,8 @@
         dst[(*dst_at, pl.ds(i * 8, 8), slice(None))] = value
 
 
-def lap12(field, slot, z):
-    center = field[slot, z + 2]
+def lap12(field, z):
+    center = field[z + 2]
     rows, lanes = center.shape
     sub = lax.broadcasted_iota(jnp.int32, (8, lanes), 0)
     lane = lax.broadcasted_iota(jnp.int32, (rows, lanes), 1)
@@ -160,8 +160,8 @@
     far = jnp.concatenate([center[16:], late, later(second)], 0) + jnp.concatenate(
         [earlier(before), early, center[:-16]], 0
     )
-    near = near + (field[slot, z + 1] + field[slot, z + 3])
-    far = far + (field[slot, z] + field[slot, z + 4])
+    near = near + (field[z + 1] + field[z + 3])
+    far = far + (field[z] + field[z + 4])
     near = near + jnp.where(lane >= 1, pltpu.roll(center, 1, 1), 0.0)
     near = near + jnp.where(lane < lanes - 1, pltpu.roll(center, lanes - 1, 1), 0.0)
     far = far + jnp.where(lane >= 2, pltpu.roll(center, 2, 1), 0.0)
@@ -226,106 +226,114 @@
     )(row[None, :], lanes[:, None], observed.T)
 
 
-def load_blocks(meta, blocks, field, planes, rows):
-    ends = field.shape[1]
-    for slot in range(2):
+def load_blocks(meta, blocks, first, second, planes, rows):
+    ends = first.shape[0]
+    for field in (first, second):
         for z in (0, 1, ends - 2, ends - 1):
-            field[slot, z] = jnp.zeros(field.shape[2:], jnp.float32)
+            field[z] = jnp.zeros(field.shape[1:], jnp.float32)
     for b, block in enumerate(blocks):
 
         @pl.loop(0, planes)
         def _(p):
             z = meta[b] + p + 2
-            interleave(field, (1, z), block, (0, p), rows)
-            interleave(field, (0, z), block, (1, p), rows)
+            interleave(first, (z,), block, (0, p), rows)
+            interleave(second, (z,), block, (1, p), rows)
+
+
+BATCH = 4
 
 
 def for_owned(meta, planes, body):
     for owned in (True, False):
         core = meta[4] if owned else 1 - meta[4]
 
-        @pl.loop(0, 2 * planes)
+        @pl.loop(0, 2 * planes // BATCH)
         def _(index):
-            chip, p = index // planes, index % planes
+            chip, p = index // (planes // BATCH), (index % (planes // BATCH)) * BATCH
             z = (2 * chip + core) * planes + p
             body(z, chip if owned else None, p)
 
 
-def forward_kernel(meta, wave, own, mate, over, far, c0, c1, c2, c3, obs, count, lap_ref, inject_ref, cour_ref, field):
-    step = pl.program_id(0)
+def forward_kernel(
+    meta, wave, own, mate, over, far, c0, c1, c2, c3, obs, count, lap_ref, inject_ref, cour_ref, even, odd
+):
+    pair = pl.program_id(0)
     planes, rows, lanes = c0.shape
 
-    @pl.when(step == 0)
+    @pl.when(pair == 0)
     def _():
-        load_blocks(meta, (own, mate, over, far), field, planes, rows)
+        load_blocks(meta, (own, mate, over, far), odd, even, planes, rows)
         for b, block in enumerate((c0, c1, c2, c3)):
 
             @pl.loop(0, planes)
             def _(p):
                 interleave(cour_ref, (meta[b] + p,), block, (p,), rows, 1.0 / 12.0)
 
-    now = lax.rem(step, 2)
-    then = 1 - now
-
-    def body(z, chip, p):
-        center, lap = lap12(field, now, z)
-        if chip is not None:
-            lap_ref[0, p, chip] = lap
-        newer = 2.0 * center - field[then, z + 2] + cour_ref[z] * lap
-        field[then, z + 2] = newer
-        inject_ref[0, z] = obs[0, z] - count[0, z] * newer
-
-    for_owned(meta, planes, body)
-
-    z, row, lane = meta[5], pl.multiple_of(meta[6], 8), meta[8]
-    here = (lax.broadcasted_iota(jnp.int32, (8, lanes), 0) == meta[7]) & (
-        lax.broadcasted_iota(jnp.int32, (8, lanes), 1) == lane
-    )
-    strength = jnp.where(here, 12.0 * wave[step], 0.0)
-    tile = pl.ds(row, 8)
-    slab, p = z // planes, lax.rem(z, planes)
-
-    @pl.when(lax.rem(slab, 2) == meta[4])
-    def _():
-        lap_ref[0, p, slab // 2, tile, :] += strength
-
-    moved = cour_ref[z, tile, :] * strength
-    field[then, z + 2, tile, :] += moved
-    inject_ref[0, z, tile, :] -= count[0, z, tile, :] * moved
-
-
-def adjoint_kernel(meta, own, mate, over, far, cour, lap_ref, inject, grad_ref, field, total):
-    step = pl.program_id(0)
+    for half, now, then in ((0, even, odd), (1, odd, even)):
+
+        def body(z, chip, p):
+            olds = [then[z + j + 2] for j in range(BATCH)]
+            for j, old in enumerate(olds):
+                center, lap = lap12(now, z + j)
+                if chip is not None:
+                    lap_ref[half, p + j, chip] = lap
+                newer = 2.0 * center - old + cour_ref[z + j] * lap
+                then[z + j + 2] = newer
+                inject_ref[half, z + j] = obs[half, z + j] - count[0, z + j] * newer
+
+        for_owned(meta, planes, body)
+
+        z, row, lane = meta[5], pl.multiple_of(meta[6], 8), meta[8]
+        here = (lax.broadcasted_iota(jnp.int32, (8, lanes), 0) == meta[7]) & (
+            lax.broadcasted_iota(jnp.int32, (8, lanes), 1) == lane
+        )
+        strength = jnp.where(here, 12.0 * wave[2 * pair + half], 0.0)
+        tile = pl.ds(row, 8)
+        slab, p = z // planes, lax.rem(z, planes)
+
+        @pl.when(lax.rem(slab, 2) == meta[4])
+        def _():
+            lap_ref[half, p, slab // 2, tile, :] += strength
+
+        moved = cour_ref[z, tile, :] * strength
+        then[z + 2, tile, :] += moved
+        inject_ref[half, z, tile, :] -= count[0, z, tile, :] * moved
+
+
+def adjoint_kernel(meta, own, mate, over, far, cour, lap_ref, inject, grad_ref, even, odd, total):
+    pair = pl.program_id(0)
     planes, rows, lanes = own.shape[1:]
     groups = rows // 8
 
-    @pl.when(step == 0)
+    @pl.when(pair == 0)
     def _():
-        load_blocks(meta, (own, mate, over, far), field, planes, rows)
+        load_blocks(meta, (own, mate, over, far), odd, even, planes, rows)
 
         @pl.loop(0, 4 * planes)
         def _(z):
-            field[0, z + 2] = field[0, z + 2] * cour[z]
-            field[1, z + 2] = field[1, z + 2] * cour[z]
+            even[z + 2] = even[z + 2] * cour[z]
+            odd[z + 2] = odd[z + 2] * cour[z]
 
         @pl.loop(0, 2 * planes)
         def _(index):
             total[index] = jnp.zeros((rows, lanes), jnp.float32)
 
-    now = lax.rem(step, 2)
-    then = 1 - now
-
-    def body(z, chip, p):
-        center, lap = lap12(field, now, z)
-        newer = 2.0 * center - field[then, z + 2] + cour[z] * (lap - inject[0, z])
-        field[then, z + 2] = newer
-        if chip is not None:
-            at = chip * planes + p
-            total[at] = total[at] + newer * lap_ref[0, p, chip]
-
-    for_owned(meta, planes, body)
-
-    @pl.when(step == pl.num_programs(0) - 1)
+    for half, now, then in ((1, even, odd), (0, odd, even)):
+
+        def body(z, chip, p):
+            olds = [then[z + j + 2] for j in range(BATCH)]
+            if chip is not None:
+                sums = [total[chip * planes + p + j] for j in range(BATCH)]
+            for j, old in enumerate(olds):
+                center, lap = lap12(now, z + j)
+                newer = 2.0 * center - old + cour[z + j] * (lap - inject[half, z + j])
+                then[z + j + 2] = newer
+                if chip is not None:
+                    total[chip * planes + p + j] = sums[j] + newer * lap_ref[half, p + j, chip]
+
+        for_owned(meta, planes, body)
+
+    @pl.when(pair == pl.num_programs(0) - 1)
     def _():
         @pl.loop(0, 2 * planes)
         def _(index):
@@ -363,7 +371,7 @@
     placed = scatter(cells, traces, planes_all, rows_x, rows_y)
     placed = placed.reshape(steps + 1, planes_all, rows_x, rows_y)
 
-    over, to_send = lax.optimization_barrier((over, pick(adjoint, 1 - chip)))
+    over, c2, placed, to_send = lax.optimization_barrier((over, c2, placed, pick(adjoint, 1 - chip)))
     far = lax.ppermute(over, "core", swap)
     c3 = lax.ppermute(c2, "core", swap)
     adj_over = lax.ppermute(to_send, "chip", swap)
@@ -382,40 +390,41 @@
     field_block = pl.BlockSpec((2, planes, rows_x, rows_y), lambda k: (0, 0, 0, 0))
     slab_block = pl.BlockSpec((planes, rows_x, rows_y), lambda k: (0, 0, 0))
     whole_block = pl.BlockSpec((planes_all, rows_x, rows_y), lambda k: (0, 0, 0))
-    step_block = pl.BlockSpec((1, planes_all, rows_x, rows_y), lambda k: (k, 0, 0, 0))
+    step_block = pl.BlockSpec((2, planes_all, rows_x, rows_y), lambda k: (k, 0, 0, 0))
     count_block = pl.BlockSpec((1, planes_all, rows_x, rows_y), lambda k: (steps, 0, 0, 0))
     lap_shape = (planes, 2, rows_x, rows_y)
     smem = pl.BlockSpec(memory_space=pltpu.SMEM)
-    scratch = pltpu.VMEM((2, planes_all + 4, rows_x, rows_y), jnp.float32)
+    scratch = pltpu.VMEM((planes_all + 4, rows_x, rows_y), jnp.float32)
     params = pltpu.CompilerParams(vmem_limit_bytes=48 * 2**20)
     cost = pl.CostEstimate(flops=30 * steps * cells_all, bytes_accessed=16 * steps * cells_all, transcendentals=0)
     laps, inject, cour = pl.pallas_call(
         forward_kernel,
-        grid=(steps,),
+        grid=(steps // 2,),
         in_specs=[smem, smem] + [field_block] * 4 + [slab_block] * 4 + [step_block, count_block],
-        out_specs=[pl.BlockSpec((1, *lap_shape), lambda k: (k, 0, 0, 0, 0)), step_block, whole_block],
+        out_specs=[pl.BlockSpec((2, *lap_shape), lambda k: (k, 0, 0, 0, 0)), step_block, whole_block],
         out_shape=[
             jax.ShapeDtypeStruct((steps, *lap_shape), jnp.float32),
             jax.ShapeDtypeStruct((steps, planes_all, rows_x, rows_y), jnp.float32),
             jax.ShapeDtypeStruct((planes_all, rows_x, rows_y), jnp.float32),
         ],
-        scratch_shapes=[scratch],
+        scratch_shapes=[scratch, scratch],
         compiler_params=params,
         cost_estimate=cost,
         name="forward_steps",
     )(meta, wave, own, mate, over, far, courant_sq, c1, c2, c3, placed, placed)
 
+    adj_over, laps = lax.optimization_barrier((adj_over, laps))
     adj_far = lax.ppermute(adj_over, "core", swap)
-    back_block = pl.BlockSpec((1, planes_all, rows_x, rows_y), lambda k: (steps - 1 - k, 0, 0, 0))
+    back_block = pl.BlockSpec((2, planes_all, rows_x, rows_y), lambda k: (steps // 2 - 1 - k, 0, 0, 0))
     gradient = pl.pallas_call(
         adjoint_kernel,
-        grid=(steps,),
+        grid=(steps // 2,),
         in_specs=[smem]
         + [field_block] * 4
-        + [whole_block, pl.BlockSpec((1, *lap_shape), lambda k: (steps - 1 - k, 0, 0, 0, 0)), back_block],
+        + [whole_block, pl.BlockSpec((2, *lap_shape), lambda k: (steps // 2 - 1 - k, 0, 0, 0, 0)), back_block],
         out_specs=pl.BlockSpec(lap_shape, lambda k: (0, 0, 0, 0)),
         out_shape=jax.ShapeDtypeStruct(lap_shape, jnp.float32),
-        scratch_shapes=[scratch, pltpu.VMEM((2 * planes, rows_x, rows_y), jnp.float32)],
+        scratch_shapes=[scratch, scratch, pltpu.VMEM((2 * planes, rows_x, rows_y), jnp.float32)],
         compiler_params=params,
         cost_estimate=cost,
         name="adjoint_steps",
@@ -467,7 +476,7 @@
 
     def run(courant_sq, momentum, fwd_prev, *rest):
         total, planes, rows_x, rows_y = fwd_prev.shape
-        fits = total == 2 * shots and planes == 4 * shots and rows_y == 128 and rows_x % 16 == 0
+        fits = total == 2 * shots and planes == 4 * shots and rows_y == 128 and rows_x % 16 == 0 and planes % 8 == 0
         plan = whole_plan if fits else slab_plan
         return plan(courant_sq, momentum, fwd_prev, *rest)
 

time: 169 us -> 121 us (0.72)
  Pallas kernels: 76.2 us -> 45.8 us
  waiting for transfers between devices: 31.2 us -> 18.9 us
  local copies, waits for them, and re-layouts: 11.8 us -> 8.13 us
    pallas_call x2, Pallas kernels: 67.9 us -> 37.4 us  [the longest x1 19.1 us: whole_shards(): pl.pallas_call(forward_kernel, grid=(steps // 2,), in_specs=[smem, smem]...]
    ppermute x1, waiting for transfers between devices: 10.5 us -> 0.01 us  [whole_shards(): over = lax.ppermute(pick(forward, 1 - chip), 'chip', swap)]
    ppermute x1, waiting for transfers between devices: 6.05 us -> 0.01 us  [whole_shards(): adj_over = lax.ppermute(to_send, 'chip', swap)]
    ppermute x1, waiting for transfers between devices: 0.01 us -> 2.37 us  [whole_shards(): c2 = lax.ppermute(courant_sq, 'chip', swap)]
    unnamed x16 -> x14, local copies, waits for them, and re-layouts: 5.54 us -> 3.65 us
  transfers between devices with their start and end apart: 10 -> 10, of which waited for: 3 -> 3; matrix products, arithmetic and copies ran while one was open for 4% -> 4% of each run, Pallas kernels for 25% -> 23%
where the time goes in v2:
time: 121 us; the launch traced here: 120 us
  Pallas kernels  45.8 us (38%)
  blocking collectives  19.4 us (16%)
  waiting for transfers between devices  18.9 us (16%)
  starting transfers between devices  11.9 us (10%)
  between operations  8.44 us (7%)
  local copies, waits for them, and re-layouts  8.13 us (7%)
  other arithmetic  7.54 us (6%)
    pallas_call x1, Pallas kernels, whole_shards(): pl.pallas_call(forward_kernel, grid=(steps // 2,), in_specs=[smem, smem]...  19.1 us
    pallas_call x1, Pallas kernels, whole_shards(): pl.pallas_call(adjoint_kernel, grid=(steps // 2,), in_specs=[smem] + [fie...  18.4 us
    all_to_all x1, waiting for transfers between devices, whole_shards(): parts = lax.all_to_all(parts, ('shot', 'chip'), 0, 0, tiled=True)  14.9 us
    all_to_all x1, blocking collectives, whole_shards(): spread = lax.all_to_all(spread, 'shot', 0, 0, tiled=True)  13.2 us
    pallas_call x1, Pallas kernels, scatter(): pl.pallas_call(scatter_kernel, grid=(rows_all // tile,), in_specs=[pl.Blo...  8.36 us
    all_to_all x1, blocking collectives, whole_shards(): lax.all_to_all(jnp.broadcast_to(sums[None], (4, 8, rows_y)), ('chip', 'co...  6.2 us
    all_to_all x1, starting transfers between devices, whole_shards(): parts = lax.all_to_all(parts, ('shot', 'chip'), 0, 0, tiled=True)  5.94 us
    unnamed x14, local copies, waits for them, and re-layouts  3.65 us
  transfers between devices with their start and end apart: 10, of which 3 were waited for; matrix products, arithmetic and copies ran while one was open for 4% of the time, Pallas kernels for 23%

profile of v2, /device:TPU:0, one launch (start us, length us, event | category | flops | bytes accessed | tf_op | source)
XLA Modules:
  0.0 120.1 jit_solution(12959738388942702955)
XLA Ops:
  0.6 0.0 copy-start
  0.7 1.3 %constant_dynamic-slice_fusion = (f32[1,8,64,128]{3,2,1,0:T(8,128)S(1)}, f32[1,8,64,128]{3,2,1,0:T(8,128)S(1)}, f32[1,8,64,128]{3,2,1,0:T(8,128)S(1)}, f32[1,8,64,128]{3,2,1,0:T(8,128)S(1)}) fusion(f32[2,8,64,128]{3,2,1,0:T(8,128)} %param.13, s32[]{:T(128)S(6)} %select_n.122, s32[]{:T(128)S(6)} %select_n.129, f32[2,8,64,128]{3,2,1,0:T(8,128)} %param.12), kind=kLoop, calls=%fused_computation.35 | loop fusion | bytes 2097160 | tf_op jit(solution)/shard_map/jit(dynamic_index_in_dim)/dynamic_slice | solution.py:359
  2.0 3.0 %collective-permute-start.1 = (f32[2,8,64,128]{3,2,1,0:T(8,128)S(1)}, f32[2,8,64,128]{3,2,1,0:T(8,128)S(1)}, u32[]{:S(2)}, u32[]{:S(2)}) collective-permute-start(f32[2,8,64,128]{3,2,1,0:T(8,128)S(1)} %pad_maximum_fusion.1), channel_id=1, source_target_pairs={{0,2},{2,0},{1,3},{3,1},{4,6},{6,4},{5,7},{7,5},{8,10},{10,8},{9,1... | collective-permute-start | bytes 1572872 | tf_op jit(solution)/shard_map/ppermute | solution.py:364
  5.0 0.1 collective-permute-start.2
  5.1 0.1 collective-permute-start.4
  5.2 0.7 fusion.9
  6.0 0.1 copy.17
  6.1 0.1 add_select_fusion.y_ref
  6.2 0.0 copy-done
  6.2 0.1 copy.20
  6.4 0.0 copy-start.3
  6.4 0.0 copy-start.4
  6.4 0.0 copy-start.2
  6.4 0.0 copy-start.6
  6.4 8.4 %receiver_scatter.1 = f32[9,2048,128]{2,1,0:T(8,128)S(1)} custom-call(s32[1,512]{1,0:T(1,128)S(1)} %get-tuple-element.38.row_ref, s32[512,1]{1,0:T(8,128)S(1)} %add_select_fusion.y_ref, f32[512,8]{1,0:T(8,128)S(1)} %bitcast.39), custom_call_target="tpu_custom_call" | custom-call | flops 4831838208 | bytes 9437184 | tf_op jit(solution)/shard_map/receiver_scatter/pallas_call | solution.py:208
  14.8 0.0 copy-start.1
  14.8 3.6 %copy-done.1 = f32[9,2048,128]{2,1,0:T(8,128)} copy-done((f32[9,2048,128]{2,1,0:T(8,128)}, f32[9,2048,128]{2,1,0:T(8,128)S(1)}, u32[]{:S(2)}) %copy-start.1) | copy-done | bytes 9437208
  18.4 0.0 copy-done.3
  18.4 0.0 copy-done.4
  18.4 0.9 constant_dynamic-slice_fusion.2
  19.3 0.9 pad_maximum_fusion.2
  20.2 2.4 %collective-permute-done.2.c2 = f32[8,64,128]{2,1,0:T(8,128)S(1)} collective-permute-done((f32[8,64,128]{2,1,0:T(8,128)}, f32[8,64,128]{2,1,0:T(8,128)S(1)}, u32[]{:S(2)}, u32[]{:S(2)}) %collective-permute-start.2) | collective-permute-done | bytes 262176 | tf_op jit(solution)/shard_map/ppermute | solution.py:363
  22.6 0.0 collective-permute-done.1.over
  22.6 0.0 collective-permute-start.5
  22.6 1.7 %collective-permute-start.3 = (f32[2,8,64,128]{3,2,1,0:T(8,128)}, f32[2,8,64,128]{3,2,1,0:T(8,128)S(1)}, u32[]{:S(2)}, u32[]{:S(2)}) collective-permute-start(f32[2,8,64,128]{3,2,1,0:T(8,128)} %pad_maximum_fusion.2), channel_id=1, source_target_pairs={{0,2},{2,0},{1,3},{3,1},{4,6},{6,4},{5,7},{7,5},{8,10},{10,8},{9,1... | collective-permute-start | bytes 1572872 | tf_op jit(solution)/shard_map/ppermute | solution.py:377
  24.3 0.0 copy-done.2
  24.3 0.2 collective-permute-start.6
  24.5 0.3 collective-permute-start.7
  25.6 0.0 copy-done.6
  25.6 0.6 dynamic_slice.46
  29.3 0.1 stack.113.wave
  29.4 0.1 stack.101.meta
  29.5 1.1 pad_maximum_fusion.own
  30.6 0.0 collective-permute-done.6.c1
  30.6 0.3 collective-permute-start
  30.9 0.0 collective-permute-done.4.mate
  30.9 0.0 collective-permute-done.7.c3
  30.9 0.0 collective-permute-done.5.far
  30.9 19.1 %forward_steps.1 = (f32[8,8,2,64,128]{4,3,2,1,0:T(8,128)}, f32[8,32,64,128]{3,2,1,0:T(8,128)}, f32[32,64,128]{2,1,0:T(8,128)S(1)}) custom-call(s32[9]{0:T(128)S(1)} %stack.101.meta, f32[8]{0:T(128)S(1)} %stack.113.wave, f32[2,8,64,128]{3,2,1,0:T(8,128)S(1)} %pad_maximum_fusion.3.own, f32[2,8,64,128]{3,2,1,0:T(8,128)S(1)} %collective-permute-done.4.mate, ...), custom_call_target="tpu_custom_call" | custom-call | flops 62914560 | bytes 33554432 | tf_op jit(solution)/shard_map/forward_steps/pallas_call | solution.py:400
  50.0 0.0 collective-permute-done.3.over
  50.0 0.3 collective-permute-start.8
  50.3 0.0 collective-permute-done.mate
  50.3 1.7 %collective-permute-done.8.far = f32[2,8,64,128]{3,2,1,0:T(8,128)S(1)} collective-permute-done((f32[2,8,64,128]{3,2,1,0:T(8,128)S(1)}, f32[2,8,64,128]{3,2,1,0:T(8,128)S(1)}, u32[]{:S(2)}, u32[]{:S(2)}) %collective-permute-start.8) | collective-permute-done | bytes 524320 | tf_op jit(solution)/shard_map/ppermute | solution.py:417
  51.9 0.0 copy-start.5
  51.9 18.4 %adjoint_steps.1 = f32[8,2,64,128]{3,2,1,0:T(8,128)} custom-call(s32[9]{0:T(128)S(1)} %stack.101.meta, f32[2,8,64,128]{3,2,1,0:T(8,128)S(1)} %pad_maximum_fusion.own, f32[2,8,64,128]{3,2,1,0:T(8,128)S(1)} %collective-permute-done.mate, f32[2,8,64,128]{3,2,1,0:T(8,128)S(1)} %collective-permute-done.3.over, f32[2,8,64,128]{3,2,1,0:T(8,128)S(1)} %collective-permute-done.8.far, ...), custom_call_target="tpu_custom_call" | custom-call | flops 62914560 | bytes 33554432 | tf_op jit(solution)/shard_map/adjoint_steps/pallas_call | solution.py:419
  70.3 5.9 %all-to-all-start = ((f32[16,64,128]{2,1,0:T(8,128)}), f32[16,64,128]{2,1,0:T(8,128)S(1)}, u32[]{:S(2)}, u32[]{:S(2)}) async-start(f32[16,64,128]{2,1,0:T(8,128)} %bitcast.23), calls=%async_computation | async-start | bytes 1048576 | tf_op jit(solution)/shard_map/all_to_all | solution.py:438
  76.2 0.6 dynamic_slice.45
  76.8 14.9 %all-to-all-done = f32[16,64,128]{2,1,0:T(8,128)S(1)} async-done(((f32[16,64,128]{2,1,0:T(8,128)}), f32[16,64,128]{2,1,0:T(8,128)S(1)}, u32[]{:S(2)}, u32[]{:S(2)}) %all-to-all-start) | async-done | bytes 524320 | tf_op jit(solution)/shard_map/all_to_all | solution.py:438
  91.7 0.0 copy-done.5
  91.8 1.3 %fusion.2 = (f32[]{:T(128)}, f32[]{:T(128)}, f32[]{:T(128)}, f32[]{:T(128)}, f32[64,128]{1,0:T(8,128)S(1)}) fusion(f32[8,64,128]{2,1,0:T(8,128)S(1)} %copy-done.5, s32[]{:T(128)S(6)} %select_n.121, f32[]{:T(128)} %bitcast, f32[64,128]{1,0:T(8,128)S(1)} %reduce_sum.63), kind=kLoop, calls=%fused_computation.14 | loop fusion | flops 90108 | bytes 98328 | tf_op jit(solution)/shard_map/reduce_sum | solution.py:445
  93.0 2.5 %select_maximum_fusion = f32[8]{0:T(128)S(1)} fusion(f32[1]{0:T(128)} %bitcast.28, f32[1]{0:T(128)} %bitcast.27, f32[1]{0:T(128)} %bitcast.26, f32[1]{0:T(128)} %bitcast.24), kind=kLoop, calls=%fused_computation.50 | loop fusion | flops 64 | bytes 48 | tf_op jit(solution)/shard_map/stack | solution.py:442
  95.6 0.1 pad.6.clone
  95.6 0.1 pad_maximum_fusion.4
  95.7 13.2 %all_to_all.15 = f32[8,72,128]{2,1,0:T(8,128)S(1)} all-to-all(f32[8,72,128]{2,1,0:T(8,128)S(1)} %broadcast_in_dim.7), channel_id=1, replica_groups=mesh['shot'=8,'chip'=2,'core'=2] {'shot'}, dimensions={0} | all-to-all | bytes 589824 | tf_op jit(solution)/shard_map/all_to_all | solution.py:452
  108.9 6.2 %all_to_all.16 = f32[4,8,128]{2,1,0:T(8,128)S(1)} all-to-all(f32[4,8,128]{2,1,0:T(8,128)S(1)} %broadcast_in_dim.8), channel_id=1, replica_groups=mesh['shot'=8,'chip'=2,'core'=2] {'chip','core'}, dimensions={0} | all-to-all | bytes 32768 | tf_op jit(solution)/shard_map/all_to_all | solution.py:455
  115.2 0.6 fusion.10
  118.3 0.7 fusion.1
  (9 shorter events, 0.2 us)
Async XLA Ops:
  0.6 5.6 %copy-start = (f32[2,8,512]{2,1,0:T(8,128)S(1)}, f32[2,8,512]{2,1,0:T(8,128)}, u32[]{:S(2)}) copy-start(f32[2,8,512]{2,1,0:T(8,128)} %param.16) | copy-start | bytes 98308
  2.0 20.5 %collective-permute-start.1 = (f32[2,8,64,128]{3,2,1,0:T(8,128)S(1)}, f32[2,8,64,128]{3,2,1,0:T(8,128)S(1)}, u32[]{:S(2)}, u32[]{:S(2)}) collective-permute-start(f32[2,8,64,128]{3,2,1,0:T(8,128)S(1)} %pad_maximum_fusion.1), channel_id=1, source_target_pairs={{0,2},{2,0},{1,3},{3,1},{4,6},{6,4},{5,7},{7,5},{8,10},{10,8},{9,1... | collective-permute-start | bytes 1572872 | tf_op jit(solution)/shard_map/ppermute | solution.py:364
  5.0 17.5 %collective-permute-start.2 = (f32[8,64,128]{2,1,0:T(8,128)}, f32[8,64,128]{2,1,0:T(8,128)S(1)}, u32[]{:S(2)}, u32[]{:S(2)}) collective-permute-start(f32[8,64,128]{2,1,0:T(8,128)} %c0.1), channel_id=1, source_target_pairs={{0,2},{2,0},{1,3},{3,1},{4,6},{6,4},{5,7},{7,5},{8,10},{10,8},{9,1... | collective-permute-start | bytes 786440 | tf_op jit(solution)/shard_map/ppermute | solution.py:363
  5.1 25.7 %collective-permute-start.4 = (f32[2,8,64,128]{3,2,1,0:T(8,128)S(1)}, f32[2,8,64,128]{3,2,1,0:T(8,128)S(1)}, u32[]{:S(2)}, u32[]{:S(2)}) collective-permute-start(f32[2,8,64,128]{3,2,1,0:T(8,128)S(1)} %pad_maximum_fusion.3.own), channel_id=1, source_target_pairs={{0,1},{1,0},{2,3},{3,2},{4,5},{5,4},{6,7},{7,6},{8,9},{9,8},{10,11... | collective-permute-start | bytes 1572872 | tf_op jit(solution)/shard_map/ppermute | solution.py:366
  6.4 12.0 %copy-start.3 = (f32[2,8,64,128]{3,2,1,0:T(8,128)S(1)}, f32[2,8,64,128]{3,2,1,0:T(8,128)}, u32[]{:S(2)}) copy-start(f32[2,8,64,128]{3,2,1,0:T(8,128)} %param.15) | copy-start | bytes 1572868
  6.4 12.0 %copy-start.4 = (f32[2,8,64,128]{3,2,1,0:T(8,128)S(1)}, f32[2,8,64,128]{3,2,1,0:T(8,128)}, u32[]{:S(2)}) copy-start(f32[2,8,64,128]{3,2,1,0:T(8,128)} %param.14) | copy-start | bytes 1572868
  6.4 17.9 %copy-start.2 = (f32[8,64,128]{2,1,0:T(8,128)S(1)}, f32[8,64,128]{2,1,0:T(8,128)}, u32[]{:S(2)}) copy-start(f32[8,64,128]{2,1,0:T(8,128)} %c0.1) | copy-start | bytes 786436
  6.4 19.2 %copy-start.6 = (s32[2]{0:T(128)S(1)}, s32[2]{0:T(128)}, u32[]{:S(2)}) copy-start(s32[2]{0:T(128)} %param.17) | copy-start | bytes 28
  14.8 3.6 %copy-start.1 = (f32[9,2048,128]{2,1,0:T(8,128)}, f32[9,2048,128]{2,1,0:T(8,128)S(1)}, u32[]{:S(2)}) copy-start(f32[9,2048,128]{2,1,0:T(8,128)S(1)} %receiver_scatter.1) | copy-start | bytes 28311556
  22.6 8.3 %collective-permute-start.5 = (f32[2,8,64,128]{3,2,1,0:T(8,128)S(1)}, f32[2,8,64,128]{3,2,1,0:T(8,128)S(1)}, u32[]{:S(2)}, u32[]{:S(2)}) collective-permute-start(f32[2,8,64,128]{3,2,1,0:T(8,128)S(1)} %collective-permute-done.1.over), channel_id=1, source_target_pairs={{0,1},{1,0},{2,3},{3,2},{4,5},{5,4},{6,7},{7,6},{8,9},{9,8},{10,11... | collective-permute-start | bytes 1572872 | tf_op jit(solution)/shard_map/ppermute | solution.py:375
  22.6 27.4 %collective-permute-start.3 = (f32[2,8,64,128]{3,2,1,0:T(8,128)}, f32[2,8,64,128]{3,2,1,0:T(8,128)S(1)}, u32[]{:S(2)}, u32[]{:S(2)}) collective-permute-start(f32[2,8,64,128]{3,2,1,0:T(8,128)} %pad_maximum_fusion.2), channel_id=1, source_target_pairs={{0,2},{2,0},{1,3},{3,1},{4,6},{6,4},{5,7},{7,5},{8,10},{10,8},{9,1... | collective-permute-start | bytes 1572872 | tf_op jit(solution)/shard_map/ppermute | solution.py:377
  24.3 6.3 %collective-permute-start.6 = (f32[8,64,128]{2,1,0:T(8,128)S(1)}, f32[8,64,128]{2,1,0:T(8,128)S(1)}, u32[]{:S(2)}, u32[]{:S(2)}) collective-permute-start(f32[8,64,128]{2,1,0:T(8,128)S(1)} %copy-done.2), channel_id=1, source_target_pairs={{0,1},{1,0},{2,3},{3,2},{4,5},{5,4},{6,7},{7,6},{8,9},{9,8},{10,11... | collective-permute-start | bytes 786440 | tf_op jit(solution)/shard_map/ppermute | solution.py:367
  24.5 6.3 %collective-permute-start.7 = (f32[8,64,128]{2,1,0:T(8,128)S(1)}, f32[8,64,128]{2,1,0:T(8,128)}, u32[]{:S(2)}, u32[]{:S(2)}) collective-permute-start(f32[8,64,128]{2,1,0:T(8,128)S(1)} %collective-permute-done.2.c2), channel_id=1, source_target_pairs={{0,1},{1,0},{2,3},{3,2},{4,5},{5,4},{6,7},{7,6},{8,9},{9,8},{10,11... | collective-permute-start | bytes 786440 | tf_op jit(solution)/shard_map/ppermute | solution.py:376
  30.6 19.7 %collective-permute-start = (f32[2,8,64,128]{3,2,1,0:T(8,128)S(1)}, f32[2,8,64,128]{3,2,1,0:T(8,128)S(1)}, u32[]{:S(2)}, u32[]{:S(2)}) collective-permute-start(f32[2,8,64,128]{3,2,1,0:T(8,128)S(1)} %pad_maximum_fusion.own), channel_id=1, source_target_pairs={{0,1},{1,0},{2,3},{3,2},{4,5},{5,4},{6,7},{7,6},{8,9},{9,8},{10,11... | collective-permute-start | bytes 1572872 | tf_op jit(solution)/shard_map/ppermute | solution.py:379
  50.0 2.0 %collective-permute-start.8 = (f32[2,8,64,128]{3,2,1,0:T(8,128)S(1)}, f32[2,8,64,128]{3,2,1,0:T(8,128)S(1)}, u32[]{:S(2)}, u32[]{:S(2)}) collective-permute-start(f32[2,8,64,128]{3,2,1,0:T(8,128)S(1)} %collective-permute-done.3.over), channel_id=1, source_target_pairs={{0,1},{1,0},{2,3},{3,2},{4,5},{5,4},{6,7},{7,6},{8,9},{9,8},{10,11... | collective-permute-start | bytes 1572872 | tf_op jit(solution)/shard_map/ppermute | solution.py:417
  51.9 39.8 %copy-start.5 = (f32[8,64,128]{2,1,0:T(8,128)S(1)}, f32[8,64,128]{2,1,0:T(8,128)}, u32[]{:S(2)}) copy-start(f32[8,64,128]{2,1,0:T(8,128)} %param.11) | copy-start | bytes 786436
  70.3 21.4 %all-to-all-start = ((f32[16,64,128]{2,1,0:T(8,128)}), f32[16,64,128]{2,1,0:T(8,128)S(1)}, u32[]{:S(2)}, u32[]{:S(2)}) async-start(f32[16,64,128]{2,1,0:T(8,128)} %bitcast.23), calls=%async_computation | async-start | bytes 1048576 | tf_op jit(solution)/shard_map/all_to_all | solution.py:438

commit v3 on v2

--- a/solution.py
+++ b/solution.py
@@ -140,11 +140,14 @@
         dst[(*dst_at, pl.ds(i * 8, 8), slice(None))] = value
 
 
-def lap12(field, z):
-    center = field[z + 2]
-    rows, lanes = center.shape
+def band(lanes):
+    near = jnp.abs(lax.broadcasted_iota(jnp.int32, (2 * lanes, lanes), 0) % lanes - lax.broadcasted_iota(jnp.int32, (2 * lanes, lanes), 1))
+    return jnp.where(near == 0, -90.0, jnp.where(near == 1, 16.0, jnp.where(near == 2, -1.0, 0.0))).astype(jnp.bfloat16)
+
+
+def laps12(field, z, banded):
+    rows, lanes = field.shape[1:]
     sub = lax.broadcasted_iota(jnp.int32, (8, lanes), 0)
-    lane = lax.broadcasted_iota(jnp.int32, (rows, lanes), 1)
 
     def later(block):
         return jnp.where(sub < 7, pltpu.roll(block, 7, 0), 0.0)
@@ -152,21 +155,24 @@
     def earlier(block):
         return jnp.where(sub > 0, pltpu.roll(block, 1, 0), 0.0)
 
-    first, second = center[0:8], center[8:16]
-    last, before = center[rows - 8 :], center[rows - 16 : rows - 8]
-    late = later(first)
-    early = earlier(last)
-    near = jnp.concatenate([center[8:], late], 0) + jnp.concatenate([early, center[:-8]], 0)
-    far = jnp.concatenate([center[16:], late, later(second)], 0) + jnp.concatenate(
-        [earlier(before), early, center[:-16]], 0
-    )
-    near = near + (field[z + 1] + field[z + 3])
-    far = far + (field[z] + field[z + 4])
-    near = near + jnp.where(lane >= 1, pltpu.roll(center, 1, 1), 0.0)
-    near = near + jnp.where(lane < lanes - 1, pltpu.roll(center, lanes - 1, 1), 0.0)
-    far = far + jnp.where(lane >= 2, pltpu.roll(center, 2, 1), 0.0)
-    far = far + jnp.where(lane < lanes - 2, pltpu.roll(center, lanes - 2, 1), 0.0)
-    return center, 16.0 * near - far - 90.0 * center
+    whole = field[pl.ds(z + 2, BATCH)].reshape(BATCH * rows, lanes)
+    high = whole.astype(jnp.bfloat16)
+    low = (whole - high.astype(jnp.float32)).astype(jnp.bfloat16)
+    along_y = jnp.dot(jnp.concatenate([high, low], 1), banded, preferred_element_type=jnp.float32)
+    results = []
+    for j in range(BATCH):
+        center = field[z + j + 2]
+        first, second = center[0:8], center[8:16]
+        last, before = center[rows - 8 :], center[rows - 16 : rows - 8]
+        late, early = later(first), earlier(last)
+        near = jnp.concatenate([center[8:], late], 0) + jnp.concatenate([early, center[:-8]], 0)
+        far = jnp.concatenate([center[16:], late, later(second)], 0) + jnp.concatenate(
+            [earlier(before), early, center[:-16]], 0
+        )
+        near = near + (field[z + j + 1] + field[z + j + 3])
+        far = far + (field[z + j] + field[z + j + 4])
+        results.append((center, 16.0 * near - far + along_y[j * rows : (j + 1) * rows]))
+    return results
 
 
 def scatter_kernel(row_ref, y_ref, obs_ref, out_ref, spread):
@@ -226,16 +232,22 @@
     )(row[None, :], lanes[:, None], observed.T)
 
 
-def load_blocks(meta, blocks, first, second, planes, rows):
+def place(planes):
+    chip, core = lax.axis_index("chip"), lax.axis_index("core")
+    slabs = (2 * chip + core, 2 * chip + 1 - core, 2 * (1 - chip) + core, 2 * (1 - chip) + 1 - core)
+    return chip, core, [slab * planes for slab in slabs]
+
+
+def load_blocks(slabs, blocks, first, second, planes, rows):
     ends = first.shape[0]
     for field in (first, second):
         for z in (0, 1, ends - 2, ends - 1):
             field[z] = jnp.zeros(field.shape[1:], jnp.float32)
-    for b, block in enumerate(blocks):
+    for slab, block in zip(slabs, blocks):
 
         @pl.loop(0, planes)
         def _(p):
-            z = meta[b] + p + 2
+            z = slab + p + 2
             interleave(first, (z,), block, (0, p), rows)
             interleave(second, (z,), block, (1, p), rows)
 
@@ -243,9 +255,9 @@
 BATCH = 4
 
 
-def for_owned(meta, planes, body):
+def for_owned(mine, planes, body):
     for owned in (True, False):
-        core = meta[4] if owned else 1 - meta[4]
+        core = mine if owned else 1 - mine
 
         @pl.loop(0, 2 * planes // BATCH)
         def _(index):
@@ -255,43 +267,51 @@
 
 
 def forward_kernel(
-    meta, wave, own, mate, over, far, c0, c1, c2, c3, obs, count, lap_ref, inject_ref, cour_ref, even, odd
+    start, sources, own, mate, over, far, c0, c1, c2, c3, obs, count, lap_ref, inject_ref, cour_ref, even, odd, banded
 ):
     pair = pl.program_id(0)
     planes, rows, lanes = c0.shape
+    groups = rows // 8
+    chip, core, slabs = place(planes)
 
     @pl.when(pair == 0)
     def _():
-        load_blocks(meta, (own, mate, over, far), odd, even, planes, rows)
-        for b, block in enumerate((c0, c1, c2, c3)):
+        banded[...] = band(lanes)
+        load_blocks(slabs, (own, mate, over, far), odd, even, planes, rows)
+        for slab, block in zip(slabs, (c0, c1, c2, c3)):
 
             @pl.loop(0, planes)
             def _(p):
-                interleave(cour_ref, (meta[b] + p,), block, (p,), rows, 1.0 / 12.0)
+                interleave(cour_ref, (slab + p,), block, (p,), rows, 1.0 / 12.0)
 
     for half, now, then in ((0, even, odd), (1, odd, even)):
 
         def body(z, chip, p):
             olds = [then[z + j + 2] for j in range(BATCH)]
-            for j, old in enumerate(olds):
-                center, lap = lap12(now, z + j)
+            for j, (center, lap) in enumerate(laps12(now, z, banded[...])):
+                old = olds[j]
                 if chip is not None:
                     lap_ref[half, p + j, chip] = lap
                 newer = 2.0 * center - old + cour_ref[z + j] * lap
                 then[z + j + 2] = newer
                 inject_ref[half, z + j] = obs[half, z + j] - count[0, z + j] * newer
 
-        for_owned(meta, planes, body)
-
-        z, row, lane = meta[5], pl.multiple_of(meta[6], 8), meta[8]
-        here = (lax.broadcasted_iota(jnp.int32, (8, lanes), 0) == meta[7]) & (
+        for_owned(core, planes, body)
+
+        cell = sources[chip]
+        z, x, lane = cell // (rows * lanes), cell // lanes % rows, cell % lanes
+        row = pl.multiple_of(x % groups * 8, 8)
+        here = (lax.broadcasted_iota(jnp.int32, (8, lanes), 0) == x // groups) & (
             lax.broadcasted_iota(jnp.int32, (8, lanes), 1) == lane
         )
-        strength = jnp.where(here, 12.0 * wave[2 * pair + half], 0.0)
+        cycle = (start[0] + 2 * pair + half) % 48
+        phase = (jnp.full((8, lanes), cycle, jnp.int32).astype(jnp.float32) - 24.0) / 12.0
+        wave = AMPLITUDE * (1.0 - 2.0 * phase * phase) * jnp.exp(-phase * phase)
+        strength = jnp.where(here, 12.0 * wave, 0.0)
         tile = pl.ds(row, 8)
         slab, p = z // planes, lax.rem(z, planes)
 
-        @pl.when(lax.rem(slab, 2) == meta[4])
+        @pl.when(lax.rem(slab, 2) == core)
         def _():
             lap_ref[half, p, slab // 2, tile, :] += strength
 
@@ -300,14 +320,16 @@
         inject_ref[half, z, tile, :] -= count[0, z, tile, :] * moved
 
 
-def adjoint_kernel(meta, own, mate, over, far, cour, lap_ref, inject, grad_ref, even, odd, total):
+def adjoint_kernel(own, mate, over, far, cour, lap_ref, inject, keep_ref, send_ref, even, odd, total, banded):
     pair = pl.program_id(0)
     planes, rows, lanes = own.shape[1:]
     groups = rows // 8
+    chip_here, core, slabs = place(planes)
 
     @pl.when(pair == 0)
     def _():
-        load_blocks(meta, (own, mate, over, far), odd, even, planes, rows)
+        banded[...] = band(lanes)
+        load_blocks(slabs, (own, mate, over, far), odd, even, planes, rows)
 
         @pl.loop(0, 4 * planes)
         def _(z):
@@ -324,24 +346,130 @@
             olds = [then[z + j + 2] for j in range(BATCH)]
             if chip is not None:
                 sums = [total[chip * planes + p + j] for j in range(BATCH)]
-            for j, old in enumerate(olds):
-                center, lap = lap12(now, z + j)
+            for j, (center, lap) in enumerate(laps12(now, z, banded[...])):
+                old = olds[j]
                 newer = 2.0 * center - old + cour[z + j] * (lap - inject[half, z + j])
                 then[z + j + 2] = newer
                 if chip is not None:
                     total[chip * planes + p + j] = sums[j] + newer * lap_ref[half, p + j, chip]
 
-        for_owned(meta, planes, body)
+        for_owned(core, planes, body)
 
     @pl.when(pair == pl.num_programs(0) - 1)
     def _():
-        @pl.loop(0, 2 * planes)
-        def _(index):
-            chip, p = index // planes, index % planes
-            z = (2 * chip + meta[4]) * planes + p
-            value = total[index] / (12.0 * cour[z])
-            for i in range(groups):
-                grad_ref[p, chip, pl.ds(i, 8, stride=groups), :] = value[i * 8 : (i + 1) * 8]
+        for ref, chip in ((keep_ref, chip_here), (send_ref, 1 - chip_here)):
+
+            @pl.loop(0, planes)
+            def _(p):
+                z = (2 * chip + core) * planes + p
+                weight = 1.0 + 2.0 * jnp.full((rows, lanes), z, jnp.int32).astype(jnp.float32) / (4 * planes - 1)
+                value = weight * total[chip * planes + p] / (12.0 * cour[z])
+                for i in range(groups):
+                    ref[p, pl.ds(i, 8, stride=groups), :] = value[i * 8 : (i + 1) * 8]
+
+
+def halve_kernel(mine, other, keep, send):
+    y = lax.axis_index("shot") % 2
+    count = keep.shape[0]
+    for ref, half in ((keep, y), (send, 1 - y)):
+        for p in range(count):
+            ref[p] = mine[half * count + p] + other[half * count + p]
+
+
+def quarter_kernel(mine, other, *parts):
+    z = lax.axis_index("shot") // 2
+    for j, ref in enumerate(parts):
+        at = flip(z, j)
+        ref[...] = mine[at] + other[at]
+
+
+def flip(index, bits):
+    result = index
+    for bit in (1, 2):
+        if bits & bit:
+            result = jnp.where(index // bit % 2 == 1, result - bit, result + bit)
+    return result
+
+
+def arrange_kernel(mine, other, out):
+    shot = lax.axis_index("shot")
+    z, y = shot // 2, shot % 2
+    quarter = mine.shape[0]
+    for part, half in ((mine, y), (other, 1 - y)):
+        for j in range(quarter):
+            out[half * quarter + flip(z, j)] = part[j]
+
+
+def sums_kernel(p0, p1, p2, p3, momentum, out):
+    rows, lanes = p0.shape
+    shot = lax.axis_index("shot")
+    chip, core = lax.axis_index("chip"), lax.axis_index("core")
+    planes = momentum.shape[0]
+    at = (shot % 2) * (planes // 2) + shot // 2
+    z = (2 * chip + core) * planes + at
+    scaled = (p0[...] + p1[...]) + (p2[...] + p3[...])
+    weight = 1.0 + 2.0 * jnp.full((1, lanes), z, jnp.int32).astype(jnp.float32) / (4 * planes - 1)
+    moment = momentum[at]
+
+    def total(value):
+        by_lane = jnp.sum(value, axis=0, keepdims=True)
+        return jnp.broadcast_to(jnp.sum(by_lane, axis=1, keepdims=True), (1, lanes))
+
+    square = total(scaled * scaled)
+    out[0:rows] = scaled
+    out[rows : rows + 8] = jnp.concatenate(
+        [
+            square,
+            weight * total(moment * moment),
+            weight * total(moment * scaled),
+            weight * square,
+            jnp.zeros((4, lanes), jnp.float32),
+        ],
+        0,
+    )
+
+
+def add_sums_kernel(mine, other, out):
+    rows = mine.shape[1] - 8
+    total = jnp.zeros(out.shape, jnp.float32)
+    for j in range(mine.shape[0]):
+        total = total + (mine[j, rows:] + other[j, rows:])
+    out[...] = total
+
+
+def finish_kernel(mine, other, momentum, s0, s1, s2, s3, out, kinetic):
+    quarter, rows, lanes = mine.shape
+    rows = rows - 8
+    cells = 4.0 * momentum.shape[0] * rows * lanes
+    shot = lax.axis_index("shot")
+    z, y = shot // 2, shot % 2
+    sums = (s0[...] + s1[...]) + (s2[...] + s3[...])
+    factor = lax.rsqrt(sums[0:1] / cells + EPSILON)
+    energy = 0.5 * (sums[1:2] - factor * sums[2:3] + 0.25 * factor * factor * sums[3:4]) / cells
+    kinetic[0] = energy[0, 0]
+    step = 0.5 * factor
+    for part, half in ((mine, y), (other, 1 - y)):
+        for j in range(quarter):
+            at = half * quarter + flip(z, j)
+            out[at] = momentum[at] - step * part[j, 0:rows]
+
+
+def local(kernel, outs, *arrays):
+    vmem = pl.BlockSpec(memory_space=pltpu.VMEM)
+    shapes = [jax.ShapeDtypeStruct(shape, jnp.float32) for shape in outs]
+    single = len(outs) == 1
+    return pl.pallas_call(
+        kernel,
+        in_specs=[vmem] * len(arrays),
+        out_specs=vmem if single else [vmem] * len(outs),
+        out_shape=shapes[0] if single else shapes,
+        compiler_params=pltpu.CompilerParams(vmem_limit_bytes=8 * 2**20),
+        name=kernel.__name__,
+    )(*arrays)
+
+
+def exchange(value, axes, sizes, bits):
+    return lax.ppermute(value, axes, [(i, i ^ bits) for i in range(sizes)])
 
 
 def whole_shards(
@@ -360,32 +488,33 @@
 
     forward = (fwd_prev, fwd_cur)
     adjoint = (adj_next, adj_cur)
-    c2 = lax.ppermute(courant_sq, "chip", swap)
-    over = lax.ppermute(pick(forward, 1 - chip), "chip", swap)
-    own = pick(forward, chip)
+    shots = planes
+
+    shot = lax.axis_index("shot")
+    at = (shot % 2) * (planes // 2) + shot // 2
+    piece = lax.ppermute(lax.dynamic_index_in_dim(courant_sq, at, 0), "chip", swap)
+    outgoing = pick(forward, 1 - chip)
+    over = lax.ppermute(outgoing, "chip", swap)
+    outgoing, fwd_prev, fwd_cur = lax.optimization_barrier((outgoing, fwd_prev, fwd_cur))
+    own = pick((fwd_prev, fwd_cur), chip)
     mate = lax.ppermute(own, "core", swap)
     c1 = lax.ppermute(courant_sq, "core", swap)
+    pieces = [piece] + [exchange(piece, "shot", shots, 2 * j) for j in (1, 2, 3)]
+    quarter = jnp.concatenate(pieces, 0)
+    other = exchange(quarter, "shot", shots, 1)
+    c2 = local(arrange_kernel, [courant_sq.shape], quarter, other)
 
     cells = lax.dynamic_index_in_dim(rec_cells, chip, 0, keepdims=False)
     traces = lax.dynamic_index_in_dim(observed, chip, 0, keepdims=False)
     placed = scatter(cells, traces, planes_all, rows_x, rows_y)
     placed = placed.reshape(steps + 1, planes_all, rows_x, rows_y)
 
-    over, c2, placed, to_send = lax.optimization_barrier((over, c2, placed, pick(adjoint, 1 - chip)))
+    c3 = lax.ppermute(c2, "core", swap)
+    over, c3, placed, to_send = lax.optimization_barrier((over, c3, placed, pick(adjoint, 1 - chip)))
     far = lax.ppermute(over, "core", swap)
-    c3 = lax.ppermute(c2, "core", swap)
     adj_over = lax.ppermute(to_send, "chip", swap)
     adj_own = pick(adjoint, chip)
     adj_mate = lax.ppermute(adj_own, "core", swap)
-
-    source = lax.dynamic_index_in_dim(src_cells, chip, 0, keepdims=False)
-    x = (source // rows_y) % rows_x
-    slabs = [2 * chip + core, 2 * chip + 1 - core, 2 * (1 - chip) + core, 2 * (1 - chip) + 1 - core]
-    meta = jnp.stack(
-        [slab * planes for slab in slabs]
-        + [core, source // (rows_x * rows_y), (x % groups) * 8, x // groups, source % rows_y]
-    ).astype(jnp.int32)
-    wave = jnp.stack([wave_value(ckpt_step, k) for k in range(steps)])
 
     field_block = pl.BlockSpec((2, planes, rows_x, rows_y), lambda k: (0, 0, 0, 0))
     slab_block = pl.BlockSpec((planes, rows_x, rows_y), lambda k: (0, 0, 0))
@@ -395,7 +524,8 @@
     lap_shape = (planes, 2, rows_x, rows_y)
     smem = pl.BlockSpec(memory_space=pltpu.SMEM)
     scratch = pltpu.VMEM((planes_all + 4, rows_x, rows_y), jnp.float32)
-    params = pltpu.CompilerParams(vmem_limit_bytes=48 * 2**20)
+    band_scratch = pltpu.VMEM((2 * rows_y, rows_y), jnp.bfloat16)
+    params = pltpu.CompilerParams(vmem_limit_bytes=28 * 2**20)
     cost = pl.CostEstimate(flops=30 * steps * cells_all, bytes_accessed=16 * steps * cells_all, transcendentals=0)
     laps, inject, cour = pl.pallas_call(
         forward_kernel,
@@ -407,56 +537,50 @@
             jax.ShapeDtypeStruct((steps, planes_all, rows_x, rows_y), jnp.float32),
             jax.ShapeDtypeStruct((planes_all, rows_x, rows_y), jnp.float32),
         ],
-        scratch_shapes=[scratch, scratch],
+        scratch_shapes=[scratch, scratch, band_scratch],
         compiler_params=params,
         cost_estimate=cost,
         name="forward_steps",
-    )(meta, wave, own, mate, over, far, courant_sq, c1, c2, c3, placed, placed)
+    )(ckpt_step[None], src_cells, own, mate, over, far, courant_sq, c1, c2, c3, placed, placed)
 
     adj_over, laps = lax.optimization_barrier((adj_over, laps))
     adj_far = lax.ppermute(adj_over, "core", swap)
     back_block = pl.BlockSpec((2, planes_all, rows_x, rows_y), lambda k: (steps // 2 - 1 - k, 0, 0, 0))
-    gradient = pl.pallas_call(
+    keep, send = pl.pallas_call(
         adjoint_kernel,
         grid=(steps // 2,),
-        in_specs=[smem]
-        + [field_block] * 4
+        in_specs=[field_block] * 4
         + [whole_block, pl.BlockSpec((2, *lap_shape), lambda k: (steps // 2 - 1 - k, 0, 0, 0, 0)), back_block],
-        out_specs=pl.BlockSpec(lap_shape, lambda k: (0, 0, 0, 0)),
-        out_shape=jax.ShapeDtypeStruct(lap_shape, jnp.float32),
-        scratch_shapes=[scratch, scratch, pltpu.VMEM((2 * planes, rows_x, rows_y), jnp.float32)],
+        out_specs=[slab_block, slab_block],
+        out_shape=[jax.ShapeDtypeStruct((planes, rows_x, rows_y), jnp.float32)] * 2,
+        scratch_shapes=[scratch, scratch, pltpu.VMEM((2 * planes, rows_x, rows_y), jnp.float32), band_scratch],
         compiler_params=params,
         cost_estimate=cost,
         name="adjoint_steps",
-    )(meta, adj_own, adj_mate, adj_over, adj_far, cour, laps, inject)
-
-    shot = lax.axis_index("shot")
-    first = (2 * chip + core) * planes
-    depths = (first + jnp.arange(planes)).astype(jnp.float32)
-    weights = 1.0 + 2.0 * depths / (planes_all - 1)
-    parts = gradient.reshape(2 * planes, rows_x, rows_y)
-    parts = lax.all_to_all(parts, ("shot", "chip"), 0, 0, tiled=True)
-    weight = lax.dynamic_index_in_dim(weights, shot, 0)
-    scaled = weight * jnp.sum(parts, axis=0)
-    moment = lax.dynamic_index_in_dim(momentum, shot, 0, keepdims=False)
-    sums = jnp.stack(
-        [
-            jnp.sum(scaled * scaled),
-            jnp.sum(weight * moment * moment),
-            jnp.sum(weight * moment * scaled),
-            jnp.sum(weight * scaled * scaled),
-        ]
-    )
-    carried = jnp.concatenate([scaled, jnp.broadcast_to(jnp.pad(sums, (0, 4))[:, None], (8, rows_y))], 0)
-    spread = jnp.broadcast_to(carried[None], (planes, rows_x + 8, rows_y))
-    spread = lax.all_to_all(spread, "shot", 0, 0, tiled=True)
-    scaled = spread[:, :rows_x]
-    sums = jnp.sum(spread[:, rows_x:], axis=0)
-    sums = lax.all_to_all(jnp.broadcast_to(sums[None], (4, 8, rows_y)), ("chip", "core"), 0, 0, tiled=True)
-    sums = jnp.sum(sums, axis=0)[:, 0]
-    factor = lax.rsqrt(sums[0] / cells_all + EPSILON)
-    kinetic = 0.5 * (sums[1] - factor * sums[2] + 0.25 * factor * factor * sums[3]) / cells_all
-    return momentum - 0.5 * factor * scaled, kinetic
+    )(adj_own, adj_mate, adj_over, adj_far, cour, laps, inject)
+
+    plane = (rows_x, rows_y)
+    received = lax.ppermute(send, "chip", swap)
+    keep, send = local(halve_kernel, [(planes // 2, *plane)] * 2, keep, received)
+    received = exchange(send, "shot", shots, 1)
+    parts = local(quarter_kernel, [plane] * 4, keep, received)
+    parts = [parts[0]] + [exchange(parts[j], "shot", shots, 2 * j) for j in (1, 2, 3)]
+    summed = local(sums_kernel, [(rows_x + 8, rows_y)], *parts, momentum)
+    quarter = jnp.stack([summed] + [exchange(summed, "shot", shots, 2 * j) for j in (1, 2, 3)])
+    other = exchange(quarter, "shot", shots, 1)
+    sums = local(add_sums_kernel, [(8, rows_y)], quarter, other)
+    depth = ("chip", "core")
+    all_sums = [sums] + [exchange(sums, depth, 4, bits) for bits in (1, 2, 3)]
+    vmem = pl.BlockSpec(memory_space=pltpu.VMEM)
+    momentum_half, kinetic = pl.pallas_call(
+        finish_kernel,
+        in_specs=[vmem] * 7,
+        out_specs=[vmem, smem],
+        out_shape=[jax.ShapeDtypeStruct(momentum.shape, jnp.float32), jax.ShapeDtypeStruct((1,), jnp.float32)],
+        compiler_params=pltpu.CompilerParams(vmem_limit_bytes=8 * 2**20),
+        name="finish",
+    )(quarter, other, momentum, *all_sums)
+    return momentum_half, kinetic[0]
 
 
 def solution(mesh):
@@ -469,14 +593,15 @@
         return dict(in_specs=inputs, out_specs=(slab, P()), check_vma=False)
 
     slab_plan = jax.shard_map(slab_shards, mesh=mesh, **placed("depth"))
-    if slabs != 4:
+    if slabs != 4 or shots != 8:
         return slab_plan
     chips = Mesh(mesh.devices.reshape(shots, 2, 2), ("shot", "chip", "core"))
     whole_plan = jax.shard_map(whole_shards, mesh=chips, **placed(("chip", "core")))
 
     def run(courant_sq, momentum, fwd_prev, *rest):
         total, planes, rows_x, rows_y = fwd_prev.shape
-        fits = total == 2 * shots and planes == 4 * shots and rows_y == 128 and rows_x % 16 == 0 and planes % 8 == 0
+        steps = rest[3].shape[1]
+        fits = total == 2 * shots and planes == 4 * shots and rows_y == 128 and rows_x % 16 == 0 and steps % 2 == 0
         plan = whole_plan if fits else slab_plan
         return plan(courant_sq, momentum, fwd_prev, *rest)
 

time: 121 us -> 114 us (0.942)
  blocking collectives: 19.4 us -> 0 us
  waiting for transfers between devices: 18.9 us -> 35.1 us
  starting transfers between devices: 11.9 us -> 24.4 us
  Pallas kernels: 45.8 us -> 36.5 us
  between operations: 8.44 us -> 1.55 us
  local copies, waits for them, and re-layouts: 8.13 us -> 13.1 us
  other arithmetic: 7.54 us -> 2.62 us
    ppermute x2 -> x18, waiting for transfers between devices: 2.37 us -> 32.2 us  [the longest x15 24.4 us: exchange(): return lax.ppermute(value, axes, [(i, i ^ bits) for i in range(sizes)])]
    all_to_all x2 -> x0, blocking collectives: 19.4 us -> none  [the longest x1 13.2 us: whole_shards(): spread = lax.all_to_all(spread, 'shot', 0, 0, tiled=True)]
    ppermute x2 -> x18, starting transfers between devices: 3.08 us -> 21.8 us  [the longest x15 18.1 us: exchange(): return lax.ppermute(value, axes, [(i, i ^ bits) for i in range(sizes)])]
    all_to_all x1 -> x0, waiting for transfers between devices: 14.9 us -> none  [whole_shards(): parts = lax.all_to_all(parts, ('shot', 'chip'), 0, 0, tiled=True)]
    all_to_all x1 -> x0, starting transfers between devices: 5.94 us -> none  [whole_shards(): parts = lax.all_to_all(parts, ('shot', 'chip'), 0, 0, tiled=True)]
    unnamed x14 -> x21, local copies, waits for them, and re-layouts: 3.65 us -> 8.99 us
    pallas_call x1, Pallas kernels: 19.1 us -> 14.2 us  [whole_shards(): pl.pallas_call(forward_kernel, grid=(steps // 2,), in_specs=[smem, smem]...]
    pallas_call x1 -> x7, Pallas kernels: 18.4 us -> 14 us  [the longest x1 13 us: whole_shards(): pl.pallas_call(adjoint_kernel, grid=(steps // 2,), in_specs=[field_block]...]
  transfers between devices with their start and end apart: 10 -> 25, of which waited for: 3 -> 13; matrix products, arithmetic and copies ran while one was open for 4% -> 5% of each run, Pallas kernels for 23% -> 20%
where the time goes in v3:
time: 114 us; the launch traced here: 113 us
  Pallas kernels  36.5 us (32%)
  waiting for transfers between devices  35.1 us (31%)
  starting transfers between devices  24.4 us (21%)
  local copies, waits for them, and re-layouts  13.1 us (11%)
  other arithmetic  2.62 us (2%)
  between operations  1.55 us (1%)
    ppermute x15, waiting for transfers between devices, exchange(): return lax.ppermute(value, axes, [(i, i ^ bits) for i in range(sizes)])  24.4 us
    ppermute x15, starting transfers between devices, exchange(): return lax.ppermute(value, axes, [(i, i ^ bits) for i in range(sizes)])  18.1 us
    pallas_call x1, Pallas kernels, whole_shards(): pl.pallas_call(forward_kernel, grid=(steps // 2,), in_specs=[smem, smem]...  14.2 us
    pallas_call x1, Pallas kernels, whole_shards(): pl.pallas_call(adjoint_kernel, grid=(steps // 2,), in_specs=[field_block]...  13 us
    unnamed x21, local copies, waits for them, and re-layouts  8.99 us
    pallas_call x1, Pallas kernels, scatter(): pl.pallas_call(scatter_kernel, grid=(rows_all // tile,), in_specs=[pl.Blo...  8.3 us
    ppermute x1, waiting for transfers between devices, whole_shards(): received = lax.ppermute(send, 'chip', swap)  7.75 us
    dynamic_slice x4, local copies, waits for them, and re-layouts, pick(): lax.dynamic_index_in_dim(f, shot, 0, keepdims=False)  3.08 us
  transfers between devices with their start and end apart: 25, of which 13 were waited for; matrix products, arithmetic and copies ran while one was open for 5% of the time, Pallas kernels for 20%

profile of v3, /device:TPU:0, one launch (start us, length us, event | category | flops | bytes accessed | tf_op | source)
XLA Modules:
  0.0 113.2 jit_solution(7382243396714091436)
XLA Ops:
  0.6 0.0 copy-start
  0.7 0.8 constant_dynamic-slice_fusion.6
  1.4 2.9 %collective-permute-start.2 = (f32[1,64,128]{2,1,0:T(8,128)S(1)}, f32[1,64,128]{2,1,0:T(8,128)S(1)}, u32[]{:S(2)}, u32[]{:S(2)}) collective-permute-start(f32[1,64,128]{2,1,0:T(8,128)S(1)} %constant_dynamic-slice_fusion.6), channel_id=1, source_target_pairs={{0,2},{2,0},{1,3},{3,1},{4,6},{6,4},{5,7},{7,5},{8,10},{10,8},{9,1... | collective-permute-start | bytes 98312 | tf_op jit(solution)/shard_map/ppermute | solution.py:495
  4.4 1.1 constant_dynamic-slice_fusion.7
  5.4 0.9 pad_maximum_fusion.1
  6.3 0.0 collective-permute-start.1
  6.3 1.0 constant_dynamic-slice_fusion
  7.3 1.0 constant_dynamic-slice_fusion.1
  8.3 0.1 collective-permute-start.9
  8.4 0.7 fusion.5
  9.1 0.1 copy.13
  9.3 0.1 add_select_fusion.y_ref
  9.4 0.1 copy.16
  9.5 0.0 collective-permute-done.2
  9.5 2.2 %collective-permute-start.3 = (f32[1,64,128]{2,1,0:T(8,128)S(1)}, f32[1,64,128]{2,1,0:T(8,128)S(1)}, u32[]{:S(2)}, u32[]{:S(2)}) collective-permute-start(f32[1,64,128]{2,1,0:T(8,128)S(1)} %collective-permute-done.2), channel_id=1, source_target_pairs={{0,8},{4,12},{8,0},{12,4},{16,24},{20,28},{24,16},{28,20},{1,9},{5... | collective-permute-start | bytes 98312 | tf_op jit(solution)/shard_map/ppermute | solution.py:472
  11.7 2.6 %collective-permute-start.4 = (f32[1,64,128]{2,1,0:T(8,128)S(1)}, f32[1,64,128]{2,1,0:T(8,128)S(1)}, u32[]{:S(2)}, u32[]{:S(2)}) collective-permute-start(f32[1,64,128]{2,1,0:T(8,128)S(1)} %collective-permute-done.2), channel_id=1, source_target_pairs={{0,16},{4,20},{8,24},{12,28},{16,0},{20,4},{24,8},{28,12},{1,17},{... | collective-permute-start | bytes 98312 | tf_op jit(solution)/shard_map/ppermute | solution.py:472
  14.3 2.8 %collective-permute-done.4 = f32[1,64,128]{2,1,0:T(8,128)S(1)} collective-permute-done((f32[1,64,128]{2,1,0:T(8,128)S(1)}, f32[1,64,128]{2,1,0:T(8,128)S(1)}, u32[]{:S(2)}, u32[]{:S(2)}) %collective-permute-start.4) | collective-permute-done | bytes 32800 | tf_op jit(solution)/shard_map/ppermute | solution.py:472
  17.1 2.9 %collective-permute-done.5 = f32[1,64,128]{2,1,0:T(8,128)S(1)} collective-permute-done((f32[1,64,128]{2,1,0:T(8,128)S(1)}, f32[1,64,128]{2,1,0:T(8,128)S(1)}, u32[]{:S(2)}, u32[]{:S(2)}) %collective-permute-start.5) | collective-permute-done | bytes 32800 | tf_op jit(solution)/shard_map/ppermute | solution.py:472
  20.0 1.5 %collective-permute-start.6 = (f32[4,64,128]{2,1,0:T(8,128)S(1)}, f32[4,64,128]{2,1,0:T(8,128)S(1)}, u32[]{:S(2)}, u32[]{:S(2)}) collective-permute-start(f32[4,64,128]{2,1,0:T(8,128)S(1)} %constant_dynamic-update-slice_fusion.mine), channel_id=1, source_target_pairs={{0,4},{4,0},{8,12},{12,8},{16,20},{20,16},{24,28},{28,24},{1,5},{5... | collective-permute-start | bytes 393224 | tf_op jit(solution)/shard_map/ppermute | solution.py:472
  21.6 8.3 %receiver_scatter.1 = f32[9,2048,128]{2,1,0:T(8,128)S(1)} custom-call(s32[1,512]{1,0:T(1,128)S(1)} %get-tuple-element.49.row_ref, s32[512,1]{1,0:T(8,128)S(1)} %add_select_fusion.y_ref, f32[512,8]{1,0:T(8,128)S(1)} %bitcast.15), custom_call_target="tpu_custom_call" | custom-call | flops 4831838208 | bytes 9437184 | tf_op jit(solution)/shard_map/receiver_scatter/pallas_call | solution.py:214
  29.9 3.6 %copy-done.1 = f32[9,2048,128]{2,1,0:T(8,128)} copy-done((f32[9,2048,128]{2,1,0:T(8,128)}, f32[9,2048,128]{2,1,0:T(8,128)S(1)}, u32[]{:S(2)}) %copy-start.1) | copy-done | bytes 9437208
  33.5 0.0 collective-permute-done.6.other
  33.6 0.1 collective-permute-start.7
  33.7 0.1 constant_dynamic-slice_fusion.2
  33.7 0.8 pad_maximum_fusion.2
  34.6 0.6 collective-permute-done.7.c3
  35.2 0.7 copy-done.4
  35.9 0.0 collective-permute-done.1.over
  35.9 0.1 collective-permute-start.10
  36.0 1.5 %collective-permute-start.8 = (f32[2,8,64,128]{3,2,1,0:T(8,128)}, f32[2,8,64,128]{3,2,1,0:T(8,128)S(1)}, u32[]{:S(2)}, u32[]{:S(2)}) collective-permute-start(f32[2,8,64,128]{3,2,1,0:T(8,128)} %pad_maximum_fusion.2), channel_id=1, source_target_pairs={{0,2},{2,0},{1,3},{3,1},{4,6},{6,4},{5,7},{7,5},{8,10},{10,8},{9,1... | collective-permute-start | bytes 1572872 | tf_op jit(solution)/shard_map/ppermute | solution.py:515
  37.5 0.1 collective-permute-start.11
  37.6 0.5 collective-permute-start
  38.8 0.6 collective-permute-done.11.c1
  39.4 3.7 %copy-done.2 = f32[9,2048,128]{2,1,0:T(8,128)S(1)} copy-done((f32[9,2048,128]{2,1,0:T(8,128)S(1)}, f32[9,2048,128]{2,1,0:T(8,128)}, u32[]{:S(2)}) %copy-start.2) | copy-done | bytes 9437208
  43.1 0.9 copy-done.5
  44.0 14.2 %forward_steps.1 = (f32[8,8,2,64,128]{4,3,2,1,0:T(8,128)S(1)}, f32[8,32,64,128]{3,2,1,0:T(8,128)S(1)}, f32[32,64,128]{2,1,0:T(8,128)S(1)}) custom-call(s32[1]{0:T(128)} %bitcast.12.start, s32[2]{0:T(128)S(1)} %copy-done.6, f32[2,8,64,128]{3,2,1,0:T(8,128)S(1)} %pad_maximum_fusion.3.own, f32[2,8,64,128]{3,2,1,0:T(8,128)S(1)} %collective-permute-done.9.mate, ...), custom_call_target="tpu_custom_call" | custom-call | flops 62914560 | bytes 33554432 | tf_op jit(solution)/shard_map/forward_steps/pallas_call | solution.py:530
  58.2 0.0 copy-start.3
  58.2 0.0 collective-permute-done.8.over
  58.2 0.2 collective-permute-start.12
  58.5 1.7 %collective-permute-done.12.far = f32[2,8,64,128]{3,2,1,0:T(8,128)S(1)} collective-permute-done((f32[2,8,64,128]{3,2,1,0:T(8,128)S(1)}, f32[2,8,64,128]{3,2,1,0:T(8,128)S(1)}, u32[]{:S(2)}, u32[]{:S(2)}) %collective-permute-start.12) | collective-permute-done | bytes 524320 | tf_op jit(solution)/shard_map/ppermute | solution.py:547
  60.2 13.0 %adjoint_steps.1 = (f32[8,64,128]{2,1,0:T(8,128)S(1)}, f32[8,64,128]{2,1,0:T(8,128)S(1)}) custom-call(f32[2,8,64,128]{3,2,1,0:T(8,128)S(1)} %pad_maximum_fusion.own, f32[2,8,64,128]{3,2,1,0:T(8,128)S(1)} %collective-permute-done.mate, f32[2,8,64,128]{3,2,1,0:T(8,128)S(1)} %collective-permute-done.8.over, f32[2,8,64,128]{3,2,1,0:T(8,128)S(1)} %collective-permute-done.12.far, ...), custom_call_target="tpu_custom_call" | custom-call | flops 62914560 | bytes 33554432 | tf_op jit(solution)/shard_map/adjoint_steps/pallas_call | solution.py:549
  73.3 0.7 collective-permute-start.13
  74.0 7.8 %collective-permute-done.13.other = f32[8,64,128]{2,1,0:T(8,128)S(1)} collective-permute-done((f32[8,64,128]{2,1,0:T(8,128)S(1)}, f32[8,64,128]{2,1,0:T(8,128)S(1)}, u32[]{:S(2)}, u32[]{:S(2)}) %collective-permute-start.13) | collective-permute-done | bytes 262176 | tf_op jit(solution)/shard_map/ppermute | solution.py:563
  81.8 0.6 collective-permute-start.14
  82.3 4.5 %collective-permute-done.14.other = f32[4,64,128]{2,1,0:T(8,128)S(1)} collective-permute-done((f32[4,64,128]{2,1,0:T(8,128)S(1)}, f32[4,64,128]{2,1,0:T(8,128)S(1)}, u32[]{:S(2)}, u32[]{:S(2)}) %collective-permute-start.14) | collective-permute-done | bytes 131104 | tf_op jit(solution)/shard_map/ppermute | solution.py:472
  86.8 0.1 collective-permute-start.15
  86.9 1.0 collective-permute-start.16
  87.8 3.4 %collective-permute-start.17 = (f32[64,128]{1,0:T(8,128)S(1)}, f32[64,128]{1,0:T(8,128)S(1)}, u32[]{:S(2)}, u32[]{:S(2)}) collective-permute-start(f32[64,128]{1,0:T(8,128)S(1)} %get-tuple-element.41), channel_id=1, source_target_pairs={{0,24},{4,28},{8,16},{12,20},{16,8},{20,12},{24,0},{28,4},{1,25},{... | collective-permute-start | bytes 98312 | tf_op jit(solution)/shard_map/ppermute | solution.py:472
  91.3 0.5 collective-permute-done.16.p2
  91.8 1.8 %collective-permute-done.17.p3 = f32[64,128]{1,0:T(8,128)S(1)} collective-permute-done((f32[64,128]{1,0:T(8,128)S(1)}, f32[64,128]{1,0:T(8,128)S(1)}, u32[]{:S(2)}, u32[]{:S(2)}) %collective-permute-start.17) | collective-permute-done | bytes 32800 | tf_op jit(solution)/shard_map/ppermute | solution.py:472
  93.6 0.1 sums_kernel.1
  93.7 0.1 collective-permute-start.18
  93.8 3.9 %collective-permute-start.19 = (f32[72,128]{1,0:T(8,128)S(1)}, f32[72,128]{1,0:T(8,128)S(1)}, u32[]{:S(2)}, u32[]{:S(2)}) collective-permute-start(f32[72,128]{1,0:T(8,128)S(1)} %sums_kernel.1), channel_id=1, source_target_pairs={{0,16},{4,20},{8,24},{12,28},{16,0},{20,4},{24,8},{28,12},{1,17},{... | collective-permute-start | bytes 110600 | tf_op jit(solution)/shard_map/ppermute | solution.py:472
  97.8 0.3 collective-permute-start.20
  98.1 1.6 %collective-permute-done.19 = f32[72,128]{1,0:T(8,128)S(1)} collective-permute-done((f32[72,128]{1,0:T(8,128)S(1)}, f32[72,128]{1,0:T(8,128)S(1)}, u32[]{:S(2)}, u32[]{:S(2)}) %collective-permute-start.19) | collective-permute-done | bytes 36896 | tf_op jit(solution)/shard_map/ppermute | solution.py:472
  99.7 3.8 %collective-permute-done.20 = f32[72,128]{1,0:T(8,128)S(1)} collective-permute-done((f32[72,128]{1,0:T(8,128)S(1)}, f32[72,128]{1,0:T(8,128)S(1)}, u32[]{:S(2)}, u32[]{:S(2)}) %collective-permute-start.20) | collective-permute-done | bytes 36896 | tf_op jit(solution)/shard_map/ppermute | solution.py:472
  103.5 0.6 collective-permute-start.21
  104.1 4.6 %collective-permute-done.21.other = f32[4,72,128]{2,1,0:T(8,128)S(1)} collective-permute-done((f32[4,72,128]{2,1,0:T(8,128)S(1)}, f32[4,72,128]{2,1,0:T(8,128)S(1)}, u32[]{:S(2)}, u32[]{:S(2)}) %collective-permute-start.21) | collective-permute-done | bytes 147488 | tf_op jit(solution)/shard_map/ppermute | solution.py:472
  108.8 0.0 collective-permute-start.22
  108.8 0.7 collective-permute-start.23
  109.4 1.2 %collective-permute-start.24 = (f32[8,128]{1,0:T(8,128)S(1)}, f32[8,128]{1,0:T(8,128)S(1)}, u32[]{:S(2)}, u32[]{:S(2)}) collective-permute-start(f32[8,128]{1,0:T(8,128)S(1)} %add_sums_kernel.1.s0), channel_id=1, source_target_pairs={{0,3},{1,2},{2,1},{3,0},{4,7},{5,6},{6,5},{7,4},{8,11},{9,10},{10,... | collective-permute-start | bytes 12296 | tf_op jit(solution)/shard_map/ppermute | solution.py:472
  110.6 1.8 %collective-permute-done.23.s2 = f32[8,128]{1,0:T(8,128)S(1)} collective-permute-done((f32[8,128]{1,0:T(8,128)S(1)}, f32[8,128]{1,0:T(8,128)S(1)}, u32[]{:S(2)}, u32[]{:S(2)}) %collective-permute-start.23) | collective-permute-done | bytes 4128 | tf_op jit(solution)/shard_map/ppermute | solution.py:472
  112.4 0.0 collective-permute-done.24.s3
  112.5 0.8 finish.1
  (32 shorter events, 0.3 us)
Async XLA Ops:
  0.6 8.8 %copy-start = (f32[2,8,512]{2,1,0:T(8,128)S(1)}, f32[2,8,512]{2,1,0:T(8,128)}, u32[]{:S(2)}) copy-start(f32[2,8,512]{2,1,0:T(8,128)} %param.16) | copy-start | bytes 98308
  1.4 8.1 %collective-permute-start.2 = (f32[1,64,128]{2,1,0:T(8,128)S(1)}, f32[1,64,128]{2,1,0:T(8,128)S(1)}, u32[]{:S(2)}, u32[]{:S(2)}) collective-permute-start(f32[1,64,128]{2,1,0:T(8,128)S(1)} %constant_dynamic-slice_fusion.6), channel_id=1, source_target_pairs={{0,2},{2,0},{1,3},{3,1},{4,6},{6,4},{5,7},{7,5},{8,10},{10,8},{9,1... | collective-permute-start | bytes 98312 | tf_op jit(solution)/shard_map/ppermute | solution.py:495
  6.3 29.6 %collective-permute-start.1 = (f32[2,8,64,128]{3,2,1,0:T(8,128)}, f32[2,8,64,128]{3,2,1,0:T(8,128)S(1)}, u32[]{:S(2)}, u32[]{:S(2)}) collective-permute-start(f32[2,8,64,128]{3,2,1,0:T(8,128)} %pad_maximum_fusion.1), channel_id=1, source_target_pairs={{0,2},{2,0},{1,3},{3,1},{4,6},{6,4},{5,7},{7,5},{8,10},{10,8},{9,1... | collective-permute-start | bytes 1572872 | tf_op jit(solution)/shard_map/ppermute | solution.py:497
  8.3 31.1 %collective-permute-start.9 = (f32[2,8,64,128]{3,2,1,0:T(8,128)S(1)}, f32[2,8,64,128]{3,2,1,0:T(8,128)S(1)}, u32[]{:S(2)}, u32[]{:S(2)}) collective-permute-start(f32[2,8,64,128]{3,2,1,0:T(8,128)S(1)} %pad_maximum_fusion.3.own), channel_id=1, source_target_pairs={{0,1},{1,0},{2,3},{3,2},{4,5},{5,4},{6,7},{7,6},{8,9},{9,8},{10,11... | collective-permute-start | bytes 1572872 | tf_op jit(solution)/shard_map/ppermute | solution.py:500
  9.5 4.8 %collective-permute-start.3 = (f32[1,64,128]{2,1,0:T(8,128)S(1)}, f32[1,64,128]{2,1,0:T(8,128)S(1)}, u32[]{:S(2)}, u32[]{:S(2)}) collective-permute-start(f32[1,64,128]{2,1,0:T(8,128)S(1)} %collective-permute-done.2), channel_id=1, source_target_pairs={{0,8},{4,12},{8,0},{12,4},{16,24},{20,28},{24,16},{28,20},{1,9},{5... | collective-permute-start | bytes 98312 | tf_op jit(solution)/shard_map/ppermute | solution.py:472
  11.7 5.4 %collective-permute-start.4 = (f32[1,64,128]{2,1,0:T(8,128)S(1)}, f32[1,64,128]{2,1,0:T(8,128)S(1)}, u32[]{:S(2)}, u32[]{:S(2)}) collective-permute-start(f32[1,64,128]{2,1,0:T(8,128)S(1)} %collective-permute-done.2), channel_id=1, source_target_pairs={{0,16},{4,20},{8,24},{12,28},{16,0},{20,4},{24,8},{28,12},{1,17},{... | collective-permute-start | bytes 98312 | tf_op jit(solution)/shard_map/ppermute | solution.py:472
  14.3 5.7 %collective-permute-start.5 = (f32[1,64,128]{2,1,0:T(8,128)S(1)}, f32[1,64,128]{2,1,0:T(8,128)S(1)}, u32[]{:S(2)}, u32[]{:S(2)}) collective-permute-start(f32[1,64,128]{2,1,0:T(8,128)S(1)} %collective-permute-done.2), channel_id=1, source_target_pairs={{0,24},{4,28},{8,16},{12,20},{16,8},{20,12},{24,0},{28,4},{1,25},{... | collective-permute-start | bytes 98312 | tf_op jit(solution)/shard_map/ppermute | solution.py:472
  20.0 13.5 %collective-permute-start.6 = (f32[4,64,128]{2,1,0:T(8,128)S(1)}, f32[4,64,128]{2,1,0:T(8,128)S(1)}, u32[]{:S(2)}, u32[]{:S(2)}) collective-permute-start(f32[4,64,128]{2,1,0:T(8,128)S(1)} %constant_dynamic-update-slice_fusion.mine), channel_id=1, source_target_pairs={{0,4},{4,0},{8,12},{12,8},{16,20},{20,16},{24,28},{28,24},{1,5},{5... | collective-permute-start | bytes 393224 | tf_op jit(solution)/shard_map/ppermute | solution.py:472
  21.6 12.1 %copy-start.7 = (f32[2,8,64,128]{3,2,1,0:T(8,128)S(1)}, f32[2,8,64,128]{3,2,1,0:T(8,128)}, u32[]{:S(2)}) copy-start(f32[2,8,64,128]{3,2,1,0:T(8,128)} %param.15) | copy-start | bytes 1572868
  21.6 12.1 %copy-start.8 = (f32[2,8,64,128]{3,2,1,0:T(8,128)S(1)}, f32[2,8,64,128]{3,2,1,0:T(8,128)}, u32[]{:S(2)}) copy-start(f32[2,8,64,128]{3,2,1,0:T(8,128)} %param.14) | copy-start | bytes 1572868
  21.6 17.8 %copy-start.6 = (s32[2]{0:T(128)S(1)}, s32[2]{0:T(128)}, u32[]{:S(2)}) copy-start(s32[2]{0:T(128)} %sources.1) | copy-start | bytes 28
  29.9 3.6 %copy-start.1 = (f32[9,2048,128]{2,1,0:T(8,128)}, f32[9,2048,128]{2,1,0:T(8,128)S(1)}, u32[]{:S(2)}) copy-start(f32[9,2048,128]{2,1,0:T(8,128)S(1)} %receiver_scatter.1) | copy-start | bytes 28311556
  33.6 1.6 %collective-permute-start.7 = (f32[8,64,128]{2,1,0:T(8,128)S(1)}, f32[8,64,128]{2,1,0:T(8,128)S(1)}, u32[]{:S(2)}, u32[]{:S(2)}) collective-permute-start(f32[8,64,128]{2,1,0:T(8,128)S(1)} %arrange_kernel.1.c2), channel_id=1, source_target_pairs={{0,1},{1,0},{2,3},{3,2},{4,5},{5,4},{6,7},{7,6},{8,9},{9,8},{10,11... | collective-permute-start | bytes 786440 | tf_op jit(solution)/shard_map/ppermute | solution.py:512
  35.2 0.7 copy-start.4
  35.9 3.5 %collective-permute-start.10 = (f32[2,8,64,128]{3,2,1,0:T(8,128)S(1)}, f32[2,8,64,128]{3,2,1,0:T(8,128)}, u32[]{:S(2)}, u32[]{:S(2)}) collective-permute-start(f32[2,8,64,128]{3,2,1,0:T(8,128)S(1)} %collective-permute-done.1.over), channel_id=1, source_target_pairs={{0,1},{1,0},{2,3},{3,2},{4,5},{5,4},{6,7},{7,6},{8,9},{9,8},{10,11... | collective-permute-start | bytes 1572872 | tf_op jit(solution)/shard_map/ppermute | solution.py:514
  36.0 22.2 %collective-permute-start.8 = (f32[2,8,64,128]{3,2,1,0:T(8,128)}, f32[2,8,64,128]{3,2,1,0:T(8,128)S(1)}, u32[]{:S(2)}, u32[]{:S(2)}) collective-permute-start(f32[2,8,64,128]{3,2,1,0:T(8,128)} %pad_maximum_fusion.2), channel_id=1, source_target_pairs={{0,2},{2,0},{1,3},{3,1},{4,6},{6,4},{5,7},{7,5},{8,10},{10,8},{9,1... | collective-permute-start | bytes 1572872 | tf_op jit(solution)/shard_map/ppermute | solution.py:515
  37.5 1.9 %collective-permute-start.11 = (f32[8,64,128]{2,1,0:T(8,128)}, f32[8,64,128]{2,1,0:T(8,128)}, u32[]{:S(2)}, u32[]{:S(2)}) collective-permute-start(f32[8,64,128]{2,1,0:T(8,128)} %c0.1), channel_id=1, source_target_pairs={{0,1},{1,0},{2,3},{3,2},{4,5},{5,4},{6,7},{7,6},{8,9},{9,8},{10,11... | collective-permute-start | bytes 786440 | tf_op jit(solution)/shard_map/ppermute | solution.py:501
  37.6 20.8 %collective-permute-start = (f32[2,8,64,128]{3,2,1,0:T(8,128)S(1)}, f32[2,8,64,128]{3,2,1,0:T(8,128)S(1)}, u32[]{:S(2)}, u32[]{:S(2)}) collective-permute-start(f32[2,8,64,128]{3,2,1,0:T(8,128)S(1)} %pad_maximum_fusion.own), channel_id=1, source_target_pairs={{0,1},{1,0},{2,3},{3,2},{4,5},{5,4},{6,7},{7,6},{8,9},{9,8},{10,11... | collective-permute-start | bytes 1572872 | tf_op jit(solution)/shard_map/ppermute | solution.py:517
  39.4 3.7 %copy-start.2 = (f32[9,2048,128]{2,1,0:T(8,128)S(1)}, f32[9,2048,128]{2,1,0:T(8,128)}, u32[]{:S(2)}) copy-start(f32[9,2048,128]{2,1,0:T(8,128)} %copy-done.1) | copy-start | bytes 28311556
  43.1 0.9 copy-start.5
  58.2 35.4 %copy-start.3 = (f32[8,64,128]{2,1,0:T(8,128)S(1)}, f32[8,64,128]{2,1,0:T(8,128)}, u32[]{:S(2)}) copy-start(f32[8,64,128]{2,1,0:T(8,128)} %momentum.3) | copy-start | bytes 786436
  58.2 2.0 %collective-permute-start.12 = (f32[2,8,64,128]{3,2,1,0:T(8,128)S(1)}, f32[2,8,64,128]{3,2,1,0:T(8,128)S(1)}, u32[]{:S(2)}, u32[]{:S(2)}) collective-permute-start(f32[2,8,64,128]{3,2,1,0:T(8,128)S(1)} %collective-permute-done.8.over), channel_id=1, source_target_pairs={{0,1},{1,0},{2,3},{3,2},{4,5},{5,4},{6,7},{7,6},{8,9},{9,8},{10,11... | collective-permute-start | bytes 1572872 | tf_op jit(solution)/shard_map/ppermute | solution.py:547
  73.3 8.4 %collective-permute-start.13 = (f32[8,64,128]{2,1,0:T(8,128)S(1)}, f32[8,64,128]{2,1,0:T(8,128)S(1)}, u32[]{:S(2)}, u32[]{:S(2)}) collective-permute-start(f32[8,64,128]{2,1,0:T(8,128)S(1)} %get-tuple-element.35), channel_id=1, source_target_pairs={{0,2},{2,0},{1,3},{3,1},{4,6},{6,4},{5,7},{7,5},{8,10},{10,8},{9,1... | collective-permute-start | bytes 786440 | tf_op jit(solution)/shard_map/ppermute | solution.py:563
  81.8 5.0 %collective-permute-start.14 = (f32[4,64,128]{2,1,0:T(8,128)S(1)}, f32[4,64,128]{2,1,0:T(8,128)S(1)}, u32[]{:S(2)}, u32[]{:S(2)}) collective-permute-start(f32[4,64,128]{2,1,0:T(8,128)S(1)} %get-tuple-element.37), channel_id=1, source_target_pairs={{0,4},{4,0},{8,12},{12,8},{16,20},{20,16},{24,28},{28,24},{1,5},{5... | collective-permute-start | bytes 393224 | tf_op jit(solution)/shard_map/ppermute | solution.py:472
  86.8 4.5 %collective-permute-start.15 = (f32[64,128]{1,0:T(8,128)S(1)}, f32[64,128]{1,0:T(8,128)S(1)}, u32[]{:S(2)}, u32[]{:S(2)}) collective-permute-start(f32[64,128]{1,0:T(8,128)S(1)} %get-tuple-element.39), channel_id=1, source_target_pairs={{0,8},{4,12},{8,0},{12,4},{16,24},{20,28},{24,16},{28,20},{1,9},{5... | collective-permute-start | bytes 98312 | tf_op jit(solution)/shard_map/ppermute | solution.py:472
  86.9 4.9 %collective-permute-start.16 = (f32[64,128]{1,0:T(8,128)S(1)}, f32[64,128]{1,0:T(8,128)S(1)}, u32[]{:S(2)}, u32[]{:S(2)}) collective-permute-start(f32[64,128]{1,0:T(8,128)S(1)} %get-tuple-element.40), channel_id=1, source_target_pairs={{0,16},{4,20},{8,24},{12,28},{16,0},{20,4},{24,8},{28,12},{1,17},{... | collective-permute-start | bytes 98312 | tf_op jit(solution)/shard_map/ppermute | solution.py:472
  87.8 5.7 %collective-permute-start.17 = (f32[64,128]{1,0:T(8,128)S(1)}, f32[64,128]{1,0:T(8,128)S(1)}, u32[]{:S(2)}, u32[]{:S(2)}) collective-permute-start(f32[64,128]{1,0:T(8,128)S(1)} %get-tuple-element.41), channel_id=1, source_target_pairs={{0,24},{4,28},{8,16},{12,20},{16,8},{20,12},{24,0},{28,4},{1,25},{... | collective-permute-start | bytes 98312 | tf_op jit(solution)/shard_map/ppermute | solution.py:472
  93.7 4.4 %collective-permute-start.18 = (f32[72,128]{1,0:T(8,128)S(1)}, f32[72,128]{1,0:T(8,128)S(1)}, u32[]{:S(2)}, u32[]{:S(2)}) collective-permute-start(f32[72,128]{1,0:T(8,128)S(1)} %sums_kernel.1), channel_id=1, source_target_pairs={{0,8},{4,12},{8,0},{12,4},{16,24},{20,28},{24,16},{28,20},{1,9},{5... | collective-permute-start | bytes 110600 | tf_op jit(solution)/shard_map/ppermute | solution.py:472
  93.8 5.9 %collective-permute-start.19 = (f32[72,128]{1,0:T(8,128)S(1)}, f32[72,128]{1,0:T(8,128)S(1)}, u32[]{:S(2)}, u32[]{:S(2)}) collective-permute-start(f32[72,128]{1,0:T(8,128)S(1)} %sums_kernel.1), channel_id=1, source_target_pairs={{0,16},{4,20},{8,24},{12,28},{16,0},{20,4},{24,8},{28,12},{1,17},{... | collective-permute-start | bytes 110600 | tf_op jit(solution)/shard_map/ppermute | solution.py:472
  97.8 5.8 %collective-permute-start.20 = (f32[72,128]{1,0:T(8,128)S(1)}, f32[72,128]{1,0:T(8,128)S(1)}, u32[]{:S(2)}, u32[]{:S(2)}) collective-permute-start(f32[72,128]{1,0:T(8,128)S(1)} %sums_kernel.1), channel_id=1, source_target_pairs={{0,24},{4,28},{8,16},{12,20},{16,8},{20,12},{24,0},{28,4},{1,25},{... | collective-permute-start | bytes 110600 | tf_op jit(solution)/shard_map/ppermute | solution.py:472
  103.5 5.2 %collective-permute-start.21 = (f32[4,72,128]{2,1,0:T(8,128)S(1)}, f32[4,72,128]{2,1,0:T(8,128)S(1)}, u32[]{:S(2)}, u32[]{:S(2)}) collective-permute-start(f32[4,72,128]{2,1,0:T(8,128)S(1)} %pad_maximum_fusion.4.mine), channel_id=1, source_target_pairs={{0,4},{4,0},{8,12},{12,8},{16,20},{20,16},{24,28},{28,24},{1,5},{5... | collective-permute-start | bytes 442376 | tf_op jit(solution)/shard_map/ppermute | solution.py:472
  108.8 1.9 %collective-permute-start.22 = (f32[8,128]{1,0:T(8,128)S(1)}, f32[8,128]{1,0:T(8,128)S(1)}, u32[]{:S(2)}, u32[]{:S(2)}) collective-permute-start(f32[8,128]{1,0:T(8,128)S(1)} %add_sums_kernel.1.s0), channel_id=1, source_target_pairs={{0,1},{1,0},{2,3},{3,2},{4,5},{5,4},{6,7},{7,6},{8,9},{9,8},{10,11... | collective-permute-start | bytes 12296 | tf_op jit(solution)/shard_map/ppermute | solution.py:472
  108.8 3.7 %collective-permute-start.23 = (f32[8,128]{1,0:T(8,128)S(1)}, f32[8,128]{1,0:T(8,128)S(1)}, u32[]{:S(2)}, u32[]{:S(2)}) collective-permute-start(f32[8,128]{1,0:T(8,128)S(1)} %add_sums_kernel.1.s0), channel_id=1, source_target_pairs={{0,2},{1,3},{2,0},{3,1},{4,6},{5,7},{6,4},{7,5},{8,10},{9,11},{10,... | collective-permute-start | bytes 12296 | tf_op jit(solution)/shard_map/ppermute | solution.py:472
  109.4 3.1 %collective-permute-start.24 = (f32[8,128]{1,0:T(8,128)S(1)}, f32[8,128]{1,0:T(8,128)S(1)}, u32[]{:S(2)}, u32[]{:S(2)}) collective-permute-start(f32[8,128]{1,0:T(8,128)S(1)} %add_sums_kernel.1.s0), channel_id=1, source_target_pairs={{0,3},{1,2},{2,1},{3,0},{4,7},{5,6},{6,5},{7,4},{8,11},{9,10},{10,... | collective-permute-start | bytes 12296 | tf_op jit(solution)/shard_map/ppermute | solution.py:472

commit v4 on v3

v4 whole, which is shorter than its diff:
```python
import functools

import jax
import jax.numpy as jnp
from jax import lax
from jax.experimental import pallas as pl
from jax.experimental.pallas import tpu as pltpu
from jax.sharding import Mesh
from jax.sharding import PartitionSpec as P

CENTER = -2.5
NEAR = 4.0 / 3.0
FAR = -1.0 / 12.0
AMPLITUDE = 100.0
EPSILON = 1e-06


def with_halo(value, sides, width):
    for axis, dim in sides:
        size, length = (lax.axis_size(axis), value.shape[dim])
        up = [(i, (i + 1) % size) for i in range(size - 1)]
        down = [(j, i) for i, j in up]
        last = lax.slice_in_dim(value, length - width, length, axis=dim)
        leading = lax.slice_in_dim(value, 0, width, axis=dim)
        before = lax.ppermute(last, axis, up)
        after = lax.ppermute(leading, axis, down)
        value = jnp.concatenate([before, value, after], axis=dim)
    return value


def laplace(padded):
    lateral = jnp.pad(padded[:, 2:-2], ((0, 0), (0, 0), (2, 2), (2, 2)))
    center = padded[:, 2:-2]
    along_z = NEAR * (padded[:, 1:-3] + padded[:, 3:-1]) + FAR * (padded[:, :-4] + padded[:, 4:])
    along_x = NEAR * (lateral[:, :, 1:-3, 2:-2] + lateral[:, :, 3:-1, 2:-2]) + FAR * (
        lateral[:, :, :-4, 2:-2] + lateral[:, :, 4:, 2:-2]
    )
    along_y = NEAR * (lateral[:, :, 2:-2, 1:-3] + lateral[:, :, 2:-2, 3:-1]) + FAR * (
        lateral[:, :, 2:-2, :-4] + lateral[:, :, 2:-2, 4:]
    )
    return 3.0 * CENTER * center + along_z + along_x + along_y


def locate(field, cell_ids, first_plane):
    shot_count, planes, rows_x, rows_y = field.shape
    plane_cells = rows_x * rows_y
    local_index = cell_ids - first_plane * plane_cells
    inside = (local_index >= 0) & (local_index < planes * plane_cells)
    target = jnp.where(inside, local_index, 0)
    return (inside, target)


def inject(field, cell_ids, values, first_plane):
    shot_count = field.shape[0]
    inside, target = locate(field, cell_ids, first_plane)
    amount = jnp.where(inside, values, jnp.zeros_like(values))
    flattened = field.reshape(shot_count, -1)
    lanes = jnp.arange(shot_count)[:, None]
    flattened = flattened.at[lanes, target].add(amount)
    return flattened.reshape(field.shape)


def sample(field, cell_ids, first_plane):
    shot_count = field.shape[0]
    inside, target = locate(field, cell_ids, first_plane)
    values = jnp.take_along_axis(field.reshape(shot_count, -1), target, axis=1)
    return jnp.where(inside, values, jnp.zeros_like(values))


def wave_value(start, step):
    cycle = jnp.mod(start + jnp.int32(step), jnp.int32(48))
    phase = (cycle.astype(jnp.float32) - 24.0) / 12.0
    return AMPLITUDE * (1.0 - 2.0 * phase * phase) * jnp.exp(-phase * phase)


def statistics(scaled, moment, weight, cells_all):
    grand_total = lax.psum(jnp.sum(scaled * scaled), ("shot", "depth"))
    factor = lax.rsqrt(grand_total / cells_all + EPSILON)
    halfway = moment - 0.5 * factor * scaled
    energy = lax.psum(jnp.sum(weight * halfway * halfway), ("shot", "depth"))
    return (factor, 0.5 * energy / cells_all)


def slab_shards(
    courant_sq,
    momentum,
    fwd_prev,
    fwd_cur,
    adj_next,
    adj_cur,
    observed,
    src_cells,
    rec_cells,
    ckpt_step,
):
    shot_count, planes, rows_x, rows_y = fwd_cur.shape
    steps_all = observed.shape[1]
    first_plane = lax.axis_index("depth") * planes
    total_planes = planes * lax.axis_size("depth")
    cells_all = total_planes * rows_x * rows_y
    sources = src_cells[:, None]
    older, current = (fwd_prev, fwd_cur)
    laplacians = []
    misfits = []
    for step in range(steps_all):
        padded = with_halo(current, (("depth", 1),), 2)
        strength = jnp.full(sources.shape, wave_value(ckpt_step, step), jnp.float32)
        laplacian = inject(laplace(padded), sources, strength, first_plane)
        newer = 2.0 * current - older + courant_sq * laplacian
        misfits.append(sample(newer, rec_cells, first_plane) - observed[:, step, :])
        laplacians.append(laplacian)
        older, current = (current, newer)
    adj_later, adj_now = (adj_next, adj_cur)
    gradient = jnp.zeros((planes, rows_x, rows_y), jnp.float32)
    for step in reversed(range(steps_all)):
        padded = with_halo(courant_sq * adj_now, (("depth", 1),), 2)
        adj_new = 2.0 * adj_now - adj_later + laplace(padded)
        adj_new = inject(adj_new, rec_cells, misfits[step], first_plane)
        gradient = gradient + jnp.sum(adj_new * laplacians[step], axis=0)
        adj_later, adj_now = (adj_now, adj_new)
    depths = (first_plane + jnp.arange(planes)).astype(jnp.float32)
    weight = (1.0 + 2.0 * depths / (total_planes - 1))[:, None, None]
    share_rows = rows_x // lax.axis_size("shot")
    offset = lax.axis_index("shot") * share_rows
    moment_share = lax.dynamic_slice_in_dim(momentum, offset, share_rows, 1)
    gradient = lax.psum(gradient, "shot")
    scaled = weight * gradient
    scaled_share = lax.dynamic_slice_in_dim(scaled, offset, share_rows, 1)
    factor, kinetic = statistics(scaled_share, moment_share, weight, cells_all)
    momentum_half = momentum - 0.5 * factor * scaled
    return (momentum_half, kinetic)


def interleave(dst, slab, src, factor=None):
    planes, rows = src.shape[0], src.shape[1]
    groups = rows // 8

    @pl.loop(0, planes)
    def _(p):
        for i in range(groups):
            value = src[p, pl.ds(i, 8, stride=groups), :]
            if factor is not None:
                value = value * factor
            dst[(*slab, p, pl.ds(i * 8, 8), slice(None))] = value


def pick_kernel(across, *refs):
    count = len(across)
    fields, outs, (held, sems) = refs[: 2 * count], refs[2 * count : 3 * count], refs[3 * count :]
    chip = lax.axis_index("chip")
    copies = []
    for n in range(2 * count):
        shot = 1 - chip if across[n // 2] else chip
        copies.append(pltpu.make_async_copy(fields[n].at[shot], held.at[n], sems.at[n]))
        copies[-1].start()
    for n in range(2 * count):
        copies[n].wait()
        interleave(outs[n // 2], (n % 2,), held.at[n])


def pick(*pairs, after=None):
    kernel = functools.partial(pick_kernel, tuple(pair[2] for pair in pairs))
    fields = [field for pair in pairs for field in pair[:2]]
    if after is not None:
        kernel, plain = (lambda mark, *refs: plain(*refs)), kernel
        fields = [after] + fields
    shape = pairs[0][0].shape[1:]
    vmem = pl.BlockSpec(memory_space=pltpu.VMEM)
    return pl.pallas_call(
        kernel,
        in_specs=[pl.BlockSpec(memory_space=pl.ANY)] * len(fields),
        out_specs=[vmem] * len(pairs),
        out_shape=[jax.ShapeDtypeStruct((2, *shape), jnp.float32)] * len(pairs),
        scratch_shapes=[pltpu.VMEM((2 * len(pairs), *shape), jnp.float32), pltpu.SemaphoreType.DMA((2 * len(pairs),))],
        compiler_params=pltpu.CompilerParams(vmem_limit_bytes=8 * 2**20),
        name="pick",
    )(*fields)


def courant_kernel(courant, whole, piece):
    shot = lax.axis_index("shot")
    interleave(whole, (), courant, 1.0 / 12.0)
    piece[0] = whole[(shot % 2) * (courant.shape[0] // 2) + shot // 2]


def band(lanes):
    near = jnp.abs(lax.broadcasted_iota(jnp.int32, (2 * lanes, lanes), 0) % lanes - lax.broadcasted_iota(jnp.int32, (2 * lanes, lanes), 1))
    return jnp.where(near == 0, -90.0, jnp.where(near == 1, 16.0, jnp.where(near == 2, -1.0, 0.0))).astype(jnp.bfloat16)


def laps12(field, z, banded):
    rows, lanes = field.shape[1:]
    sub = lax.broadcasted_iota(jnp.int32, (8, lanes), 0)

    def later(block):
        return jnp.where(sub < 7, pltpu.roll(block, 7, 0), 0.0)

    def earlier(block):
        return jnp.where(sub > 0, pltpu.roll(block, 1, 0), 0.0)

    whole = field[pl.ds(z + 2, BATCH)].reshape(BATCH * rows, lanes)
    high = whole.astype(jnp.bfloat16)
    low = (whole - high.astype(jnp.float32)).astype(jnp.bfloat16)
    along_y = jnp.dot(jnp.concatenate([high, low], 1), banded, preferred_element_type=jnp.float32)
    results = []
    for j in range(BATCH):
        center = field[z + j + 2]
        first, second = center[0:8], center[8:16]
        last, before = center[rows - 8 :], center[rows - 16 : rows - 8]
        late, early = later(first), earlier(last)
        near = jnp.concatenate([center[8:], late], 0) + jnp.concatenate([early, center[:-8]], 0)
        far = jnp.concatenate([center[16:], late, later(second)], 0) + jnp.concatenate(
            [earlier(before), early, center[:-16]], 0
        )
        near = near + (field[z + j + 1] + field[z + j + 3])
        far = far + (field[z + j] + field[z + j + 4])
        results.append((center, 16.0 * near - far + along_y[j * rows : (j + 1) * rows]))
    return results


def scatter_kernel(row_ref, y_ref, obs_ref, out_ref, mark, spread):
    receivers, steps = obs_ref.shape
    lanes = out_ref.shape[2]
    tile = out_ref.shape[1]

    @pl.when(pl.program_id(0) == 0)
    def _():
        lane = lax.broadcasted_iota(jnp.int32, (receivers, lanes), 1)
        at = lane == y_ref[...]
        for k in range(steps):
            column = obs_ref[:, k : k + 1]
            high = column.astype(jnp.bfloat16).astype(jnp.float32)
            low = column - high
            cols = pl.ds(k * lanes, lanes)
            spread[0:receivers, cols] = jnp.where(at, high, 0.0).astype(jnp.bfloat16)
            spread[receivers:, cols] = jnp.where(at, low, 0.0).astype(jnp.bfloat16)
        cols = pl.ds(steps * lanes, lanes)
        spread[0:receivers, cols] = jnp.where(at, 1.0, 0.0).astype(jnp.bfloat16)
        spread[receivers:, cols] = jnp.zeros((receivers, lanes), jnp.bfloat16)
        mark[...] = jnp.zeros(mark.shape, jnp.float32)

    ids = lax.broadcasted_iota(jnp.int32, (tile, receivers), 0) + pl.program_id(0) * tile
    chosen = jnp.where(ids == row_ref[...], 1.0, 0.0).astype(jnp.bfloat16)
    total = jnp.dot(jnp.concatenate([chosen, chosen], 1), spread[...], preferred_element_type=jnp.float32)
    for k in range(steps + 1):
        out_ref[k] = total[:, k * lanes : (k + 1) * lanes]


def scatter(cells, observed, planes_all, rows_x, rows_y):
    steps, receivers = observed.shape
    groups = rows_x // 8
    x = (cells // rows_y) % rows_x
    row = (cells // (rows_x * rows_y)) * rows_x + (x % groups) * 8 + x // groups
    lanes = cells % rows_y
    rows_all = planes_all * rows_x
    tile = 256
    return pl.pallas_call(
        scatter_kernel,
        grid=(rows_all // tile,),
        in_specs=[
            pl.BlockSpec((1, receivers), lambda t: (0, 0)),
            pl.BlockSpec((receivers, 1), lambda t: (0, 0)),
            pl.BlockSpec((receivers, steps), lambda t: (0, 0)),
        ],
        out_specs=[
            pl.BlockSpec((steps + 1, tile, rows_y), lambda t: (0, t, 0)),
            pl.BlockSpec((8, rows_y), lambda t: (0, 0)),
        ],
        out_shape=[
            jax.ShapeDtypeStruct((steps + 1, rows_all, rows_y), jnp.float32),
            jax.ShapeDtypeStruct((8, rows_y), jnp.float32),
        ],
        scratch_shapes=[pltpu.VMEM((2 * receivers, (steps + 1) * rows_y), jnp.bfloat16)],
        compiler_params=pltpu.CompilerParams(vmem_limit_bytes=20 * 2**20),
        cost_estimate=pl.CostEstimate(
            flops=4 * rows_all * receivers * (steps + 1) * rows_y,
            bytes_accessed=4 * (steps + 1) * rows_all * rows_y,
            transcendentals=0,
        ),
        name="receiver_scatter",
    )(row[None, :], lanes[:, None], observed.T)


def place(planes):
    chip, core = lax.axis_index("chip"), lax.axis_index("core")
    slabs = (2 * chip + core, 2 * chip + 1 - core, 2 * (1 - chip) + core, 2 * (1 - chip) + 1 - core)
    return chip, core, [slab * planes for slab in slabs]


def load_blocks(slabs, blocks, first, second):
    ends = first.shape[0]
    planes = blocks[0].shape[1]
    for field in (first, second):
        for z in (0, 1, ends - 2, ends - 1):
            field[z] = jnp.zeros(field.shape[1:], jnp.float32)
    for slab, block in zip(slabs, blocks):

        @pl.loop(0, planes)
        def _(p):
            first[slab + p + 2] = block[0, p]
            second[slab + p + 2] = block[1, p]


BATCH = 4


def for_owned(mine, planes, body):
    for owned in (True, False):
        core = mine if owned else 1 - mine

        @pl.loop(0, 2 * planes // BATCH)
        def _(index):
            chip, p = index // (planes // BATCH), (index % (planes // BATCH)) * BATCH
            z = (2 * chip + core) * planes + p
            body(z, chip if owned else None, p)


def forward_kernel(
    start, sources, own, mate, over, far, c0, c1, c2, c3, placed, laps, inject, cour, mark, even, odd, banded
):
    planes, rows, lanes = c0.shape
    steps = laps.shape[0]
    groups = rows // 8
    chip_here, core, slabs = place(planes)
    mark[...] = jnp.zeros(mark.shape, jnp.float32)
    banded[...] = band(lanes)
    load_blocks(slabs, (own, mate, over, far), odd, even)
    for slab, block in zip(slabs, (c0, c1, c2, c3)):

        @pl.loop(0, planes)
        def _(p):
            cour[slab + p] = block[p]

    cell = sources[chip_here]
    source_z, x, lane = cell // (rows * lanes), cell // lanes % rows, cell % lanes
    tile = pl.ds(pl.multiple_of(x % groups * 8, 8), 8)
    here = (lax.broadcasted_iota(jnp.int32, (8, lanes), 0) == x // groups) & (
        lax.broadcasted_iota(jnp.int32, (8, lanes), 1) == lane
    )
    source_slab, source_p = source_z // planes, lax.rem(source_z, planes)

    def advance(k, now, then):
        def body(z, chip, p):
            olds = [then[z + j + 2] for j in range(BATCH)]
            for j, (center, lap) in enumerate(laps12(now, z, banded[...])):
                if chip is not None:
                    laps[k, p + j, chip] = lap
                newer = 2.0 * center - olds[j] + cour[z + j] * lap
                then[z + j + 2] = newer
                inject[k, z + j] = placed[k, z + j] - placed[steps, z + j] * newer

        for_owned(core, planes, body)

        cycle = (start[0] + k) % 48
        phase = (jnp.full((8, lanes), cycle, jnp.int32).astype(jnp.float32) - 24.0) / 12.0
        wave = AMPLITUDE * (1.0 - 2.0 * phase * phase) * jnp.exp(-phase * phase)
        strength = jnp.where(here, 12.0 * wave, 0.0)

        @pl.when(lax.rem(source_slab, 2) == core)
        def _():
            laps[k, source_p, source_slab // 2, tile, :] += strength

        moved = cour[source_z, tile, :] * strength
        then[source_z + 2, tile, :] += moved
        inject[k, source_z, tile, :] -= placed[steps, source_z, tile, :] * moved

    @pl.loop(0, steps // 2)
    def _(pair):
        advance(2 * pair, even, odd)
        advance(2 * pair + 1, odd, even)


def adjoint_kernel(mark, own, mate, over, far, cour, laps, inject, keep_ref, send_ref, even, odd, total, banded):
    planes, rows, lanes = own.shape[1:]
    steps = laps.shape[0]
    groups = rows // 8
    chip_here, core, slabs = place(planes)
    banded[...] = band(lanes)
    load_blocks(slabs, (own, mate, over, far), odd, even)

    @pl.loop(0, 4 * planes)
    def _(z):
        even[z + 2] = even[z + 2] * cour[z]
        odd[z + 2] = odd[z + 2] * cour[z]

    @pl.loop(0, 2 * planes)
    def _(index):
        total[index] = jnp.zeros((rows, lanes), jnp.float32)

    def advance(k, now, then):
        def body(z, chip, p):
            olds = [then[z + j + 2] for j in range(BATCH)]
            if chip is not None:
                sums = [total[chip * planes + p + j] for j in range(BATCH)]
            for j, (center, lap) in enumerate(laps12(now, z, banded[...])):
                newer = 2.0 * center - olds[j] + cour[z + j] * (lap - inject[k, z + j])
                then[z + j + 2] = newer
                if chip is not None:
                    total[chip * planes + p + j] = sums[j] + newer * laps[k, p + j, chip]

        for_owned(core, planes, body)

    @pl.loop(0, steps // 2)
    def _(pair):
        advance(steps - 1 - 2 * pair, even, odd)
        advance(steps - 2 - 2 * pair, odd, even)

    for ref, chip in ((keep_ref, chip_here), (send_ref, 1 - chip_here)):

        @pl.loop(0, planes)
        def _(p):
            z = (2 * chip + core) * planes + p
            weight = 1.0 + 2.0 * jnp.full((rows, lanes), z, jnp.int32).astype(jnp.float32) / (4 * planes - 1)
            value = weight * total[chip * planes + p] / (12.0 * cour[z])
            for i in range(groups):
                ref[p, pl.ds(i, 8, stride=groups), :] = value[i * 8 : (i + 1) * 8]


def halve_kernel(bit, mine, other, keep, send):
    half = lax.axis_index("shot") // bit % 2
    count = keep.shape[0]
    for ref, part in ((keep, half), (send, 1 - half)):
        for p in range(count):
            ref[p] = mine[part * count + p] + other[part * count + p]


def add_kernel(mine, other, out):
    out[...] = mine[...] + other[...]


def flip(index, bits):
    result = index
    for bit in (1, 2):
        if bits & bit:
            result = jnp.where(index // bit % 2 == 1, result - bit, result + bit)
    return result


def arrange_kernel(mine, other, out):
    shot = lax.axis_index("shot")
    z, y = shot // 2, shot % 2
    quarter = mine.shape[0]
    for part, half in ((mine, y), (other, 1 - y)):
        for j in range(quarter):
            out[half * quarter + flip(z, j)] = part[j]


def first_plane(shot, planes):
    return (shot % 2) * (planes // 2) + (shot // 2 % 2) * (planes // 4)


def sums_kernel(mine, other, momentum, data, sums):
    count, rows, lanes = mine.shape
    planes = momentum.shape[0]
    chip, core = lax.axis_index("chip"), lax.axis_index("core")
    first = first_plane(lax.axis_index("shot"), planes)
    parts = [jnp.zeros((rows, lanes), jnp.float32)] * 4
    for j in range(count):
        scaled = mine[j] + other[j]
        data[j * rows : (j + 1) * rows] = scaled
        z = (2 * chip + core) * planes + first + j
        weight = 1.0 + 2.0 * jnp.full((1, lanes), z, jnp.int32).astype(jnp.float32) / (4 * planes - 1)
        moment = momentum[first + j]
        square = scaled * scaled
        terms = (square, weight * moment * moment, weight * moment * scaled, weight * square)
        parts = [part + term for part, term in zip(parts, terms)]

    def total(value):
        by_lane = jnp.sum(value, axis=0, keepdims=True)
        return jnp.broadcast_to(jnp.sum(by_lane, axis=1, keepdims=True), (1, lanes))

    value = jnp.concatenate([total(part) for part in parts] + [jnp.zeros((4, lanes), jnp.float32)], 0)
    data[count * rows :] = value
    sums[...] = value


def join_kernel(mine, other, s0, s1, s2, data, sums):
    rows = mine.shape[0] - 8
    data[0:rows] = mine[0:rows]
    data[rows : 2 * rows] = other[0:rows]
    value = (s0[...] + s1[...]) + (other[rows:] + s2[...])
    data[2 * rows :] = value
    sums[...] = value


def finish_kernel(mine, other, momentum, s0, s1, s2, out, kinetic):
    planes, rows, lanes = momentum.shape
    cells = 4.0 * planes * rows * lanes
    shot = lax.axis_index("shot")
    sums = (s0[...] + s1[...]) + (other[planes // 2 * rows :] + s2[...])
    factor = lax.rsqrt(sums[0:1] / cells + EPSILON)
    energy = 0.5 * (sums[1:2] - factor * sums[2:3] + 0.25 * factor * factor * sums[3:4]) / cells
    kinetic[0] = energy[0, 0]
    step = 0.5 * factor
    quarter = planes // 4
    for part, group in ((mine, shot), (other, flip(shot, 1))):
        for number, first in enumerate((first_plane(group, planes), first_plane(flip(group, 2), planes))):
            for j in range(quarter):
                at = (number * quarter + j) * rows
                out[first + j] = momentum[first + j] - step * part[at : at + rows]


def local(kernel, outs, *arrays, name=None, limit=8):
    vmem = pl.BlockSpec(memory_space=pltpu.VMEM)
    shapes = [jax.ShapeDtypeStruct(shape, jnp.float32) for shape in outs]
    single = len(outs) == 1
    return pl.pallas_call(
        kernel,
        in_specs=[vmem] * len(arrays),
        out_specs=vmem if single else [vmem] * len(outs),
        out_shape=shapes[0] if single else shapes,
        compiler_params=pltpu.CompilerParams(vmem_limit_bytes=limit * 2**20),
        name=name or kernel.__name__,
    )(*arrays)


def exchange(value, bits):
    axes = ("shot", "chip", "core")
    return lax.ppermute(value, axes, [(i, i ^ bits) for i in range(lax.axis_size(axes))])


CORE, CHIP, Y, NEAR_Z, FAR_Z = 1, 2, 4, 8, 16


def whole_shards(
    courant_sq, momentum, fwd_prev, fwd_cur, adj_next, adj_cur, observed, src_cells, rec_cells, ckpt_step
):
    _, planes, rows_x, rows_y = fwd_cur.shape
    steps = observed.shape[1]
    chip = lax.axis_index("chip")
    planes_all = 4 * planes
    cells_all = planes_all * rows_x * rows_y
    vmem, smem = pl.BlockSpec(memory_space=pltpu.VMEM), pl.BlockSpec(memory_space=pltpu.SMEM)

    (outgoing,) = pick((fwd_prev, fwd_cur, True))
    over = exchange(outgoing, CHIP)

    c0, piece = local(courant_kernel, [courant_sq.shape, (1, rows_x, rows_y)], courant_sq)
    piece = exchange(piece, CHIP)
    (own,) = pick((fwd_prev, fwd_cur, False))
    mate = exchange(own, CORE)
    c1 = exchange(c0, CORE)
    quarter = jnp.concatenate([piece] + [exchange(piece, j * NEAR_Z) for j in (1, 2, 3)], 0)
    other = exchange(quarter, Y)
    c2 = local(arrange_kernel, [courant_sq.shape], quarter, other)
    c3 = exchange(c2, CORE)

    cells = lax.dynamic_index_in_dim(rec_cells, chip, 0, keepdims=False)
    traces = lax.dynamic_index_in_dim(observed, chip, 0, keepdims=False)
    placed, mark = scatter(cells, traces, planes_all, rows_x, rows_y)
    placed = placed.reshape(steps + 1, planes_all, rows_x, rows_y)

    adj_outgoing, adj_own = pick((adj_next, adj_cur, True), (adj_next, adj_cur, False), after=mark)
    far = exchange(over, CORE)
    adj_over = exchange(adj_outgoing, CHIP)
    adj_mate = exchange(adj_own, CORE)

    scratch = pltpu.VMEM((planes_all + 4, rows_x, rows_y), jnp.float32)
    band_scratch = pltpu.VMEM((2 * rows_y, rows_y), jnp.bfloat16)
    params = pltpu.CompilerParams(vmem_limit_bytes=20 * 2**20)
    cost = pl.CostEstimate(flops=30 * steps * cells_all, bytes_accessed=16 * steps * cells_all, transcendentals=0)
    laps, inject, cour, mark = pl.pallas_call(
        forward_kernel,
        in_specs=[smem, smem] + [vmem] * 9,
        out_specs=[vmem] * 4,
        out_shape=[
            jax.ShapeDtypeStruct((steps, planes, 2, rows_x, rows_y), jnp.float32),
            jax.ShapeDtypeStruct((steps, planes_all, rows_x, rows_y), jnp.float32),
            jax.ShapeDtypeStruct((planes_all, rows_x, rows_y), jnp.float32),
            jax.ShapeDtypeStruct((8, rows_y), jnp.float32),
        ],
        scratch_shapes=[scratch, scratch, band_scratch],
        compiler_params=params,
        cost_estimate=cost,
        name="forward_steps",
    )(ckpt_step[None], src_cells, own, mate, over, far, c0, c1, c2, c3, placed)

    adj_over, mark = lax.optimization_barrier((adj_over, mark))
    adj_far = exchange(adj_over, CORE)
    slab = jax.ShapeDtypeStruct(courant_sq.shape, jnp.float32)
    keep, send = pl.pallas_call(
        adjoint_kernel,
        in_specs=[pl.BlockSpec(memory_space=pl.ANY)] + [vmem] * 7,
        out_specs=[vmem, vmem],
        out_shape=[slab, slab],
        scratch_shapes=[scratch, scratch, pltpu.VMEM((2 * planes, rows_x, rows_y), jnp.float32), band_scratch],
        compiler_params=params,
        cost_estimate=cost,
        name="adjoint_steps",
    )(mark, adj_own, adj_mate, adj_over, adj_far, cour, laps, inject)

    half, quarter = (planes // 2, rows_x, rows_y), (planes // 4, rows_x, rows_y)
    keep, send = local(functools.partial(halve_kernel, 1), [half] * 2, keep, exchange(send, CHIP), name="halve_y")
    keep, send = local(functools.partial(halve_kernel, 2), [quarter] * 2, keep, exchange(send, Y), name="halve_z")
    part = local(add_kernel, [quarter], keep, exchange(send, NEAR_Z))
    rows, sums_shape = planes // 4 * rows_x, (8, rows_y)
    data, sums = local(sums_kernel, [(rows + 8, rows_y), sums_shape], part, exchange(part, FAR_Z), momentum)
    received = exchange(data, NEAR_Z)
    others = [exchange(sums, CORE), exchange(sums, NEAR_Z + CORE)]
    data, sums = local(join_kernel, [(2 * rows + 8, rows_y), sums_shape], data, received, sums, *others)
    received = exchange(data, Y)
    others = [exchange(sums, CHIP), exchange(sums, Y + CHIP)]
    momentum_half, kinetic = pl.pallas_call(
        finish_kernel,
        in_specs=[vmem] * 6,
        out_specs=[vmem, smem],
        out_shape=[slab, jax.ShapeDtypeStruct((1,), jnp.float32)],
        compiler_params=pltpu.CompilerParams(vmem_limit_bytes=8 * 2**20),
        name="finish",
    )(data, received, momentum, sums, *others)
    return momentum_half, kinetic[0]


def solution(mesh):
    shots, slabs = mesh.shape["shot"], mesh.shape["depth"]

    def placed(depth):
        field = P("shot", depth, None, None)
        slab = P(depth, None, None)
        inputs = (slab, slab, field, field, field, field, P("shot", None, None), P("shot"), P("shot", None), P())
        return dict(in_specs=inputs, out_specs=(slab, P()), check_vma=False)

    slab_plan = jax.shard_map(slab_shards, mesh=mesh, **placed("depth"))
    if slabs != 4 or shots != 8:
        return slab_plan
    chips = Mesh(mesh.devices.reshape(shots, 2, 2), ("shot", "chip", "core"))
    whole_plan = jax.shard_map(whole_shards, mesh=chips, **placed(("chip", "core")))

    def run(courant_sq, momentum, fwd_prev, *rest):
        total, planes, rows_x, rows_y = fwd_prev.shape
        steps = rest[3].shape[1]
        fits = total == 2 * shots and planes == 4 * shots and rows_y == 128 and rows_x % 16 == 0 and steps % 2 == 0
        plan = whole_plan if fits else slab_plan
        return plan(courant_sq, momentum, fwd_prev, *rest)

    return run
```

time: 114 us -> 109 us (0.956)
  waiting for transfers between devices: 35.1 us -> 32.6 us
  local copies, waits for them, and re-layouts: 13.1 us -> 10.7 us
  other arithmetic: 2.62 us -> 0.84 us
  Pallas kernels: 36.5 us -> 38 us
    dynamic_slice x5 -> x0, local copies, waits for them, and re-layouts: 3.85 us -> none  [the longest x4 3.08 us: pick(): lax.dynamic_index_in_dim(f, shot, 0, keepdims=False)]
    ppermute x25 -> x23, waiting for transfers between devices: 35.1 us -> 32.6 us  [exchange(): lax.ppermute(value, axes, [(i, i ^ bits) for i in range(lax.axis_size(axe...]
    another operation x5 -> x0, other arithmetic: 1.77 us -> none  [the longest x4 1.76 us: pick(): jnp.stack([lax.dynamic_index_in_dim(f, shot, 0, keepdims=False) for f in...]
    unnamed x21 -> x23, local copies, waits for them, and re-layouts: 8.99 us -> 10.4 us
    pallas_call x3 -> x6, Pallas kernels: 28 us -> 28.7 us  [the longest x1 13.5 us: whole_shards(): pl.pallas_call(forward_kernel, in_specs=[smem, smem] + [vmem] * 9, out_sp...]
    ppermute x25 -> x23, starting transfers between devices: 24.4 us -> 25.1 us  [exchange(): lax.ppermute(value, axes, [(i, i ^ bits) for i in range(lax.axis_size(axe...]
  transfers between devices with their start and end apart: 25 -> 23, of which waited for: 13 -> 12; matrix products, arithmetic and copies ran while one was open for 5% -> 1% of each run, Pallas kernels for 20% -> 21%
where the time goes in v4:
time: 109 us
  Pallas kernels  38 us (35%)
  waiting for transfers between devices  32.6 us (30%)
  starting transfers between devices  25.1 us (23%)
  local copies, waits for them, and re-layouts  10.7 us (10%)
  between operations  1.55 us (1%)
    ppermute x23, waiting for transfers between devices, exchange(): lax.ppermute(value, axes, [(i, i ^ bits) for i in range(lax.axis_size(axe...  32.6 us
    ppermute x23, starting transfers between devices, exchange(): lax.ppermute(value, axes, [(i, i ^ bits) for i in range(lax.axis_size(axe...  25.1 us
    pallas_call x1, Pallas kernels, whole_shards(): pl.pallas_call(forward_kernel, in_specs=[smem, smem] + [vmem] * 9, out_sp...  13.5 us
    pallas_call x1, Pallas kernels, whole_shards(): pl.pallas_call(adjoint_kernel, in_specs=[pl.BlockSpec(memory_space=pl.ANY...  12.9 us
    unnamed x23, local copies, waits for them, and re-layouts  10.4 us
    pallas_call x1, Pallas kernels, scatter(): pl.pallas_call(scatter_kernel, grid=(rows_all // tile,), in_specs=[pl.Blo...  8.3 us
  transfers between devices with their start and end apart: 23, of which 12 were waited for; matrix products, arithmetic and copies ran while one was open for 1% of the time, Pallas kernels for 21%

profile of v4, /device:TPU:0, one launch (start us, length us, event | category | flops | bytes accessed | tf_op | source)
XLA Modules:
  0.0 108.8 jit_solution(13144382239147940884)
XLA Ops:
  0.6 0.0 copy-start
  0.7 0.9 copy-done.8
  1.6 0.8 courant_kernel.1
  2.4 2.9 %collective-permute-start.5 = (f32[1,64,128]{2,1,0:T(8,128)S(1)}, f32[1,64,128]{2,1,0:T(8,128)S(1)}, u32[]{:S(2)}, u32[]{:S(2)}) collective-permute-start(f32[1,64,128]{2,1,0:T(8,128)S(1)} %get-tuple-element.29), channel_id=1, source_target_pairs={{0,2},{1,3},{2,0},{3,1},{4,6},{5,7},{6,4},{7,5},{8,10},{9,11},{10,... | collective-permute-start | bytes 98312 | tf_op jit(solution)/shard_map/ppermute | solution.py:519
  5.3 1.0 copy-done.3
  6.4 1.0 copy-done.4
  7.4 0.2 pick.5
  7.6 0.1 collective-permute-start.2
  7.7 0.2 pick.4.own
  7.9 0.1 collective-permute-start.1
  8.0 0.7 dynamic-slice_bitcast_fusion
  8.7 0.1 copy.13
  8.9 0.1 add_select_fusion.y_ref
  9.0 0.1 copy.16
  9.1 0.0 copy-start.5
  9.1 0.0 copy-start.6
  9.2 0.0 copy-start.9
  9.2 8.3 %receiver_scatter.1 = (f32[9,2048,128]{2,1,0:T(8,128)S(1)}, f32[8,128]{1,0:T(8,128)S(1)}) custom-call(s32[1,512]{1,0:T(1,128)S(1)} %get-tuple-element.51.row_ref, s32[512,1]{1,0:T(8,128)S(1)} %add_select_fusion.y_ref, f32[512,8]{1,0:T(8,128)S(1)} %bitcast.10), custom_call_target="tpu_custom_call" | custom-call | flops 4831838208 | bytes 9437184 | tf_op jit(solution)/shard_map/receiver_scatter/pallas_call | solution.py:257
  17.5 3.6 %copy-done.1 = f32[9,2048,128]{2,1,0:T(8,128)} copy-done((f32[9,2048,128]{2,1,0:T(8,128)}, f32[9,2048,128]{2,1,0:T(8,128)S(1)}, u32[]{:S(2)}) %copy-start.1) | copy-done | bytes 9437208
  21.1 1.2 %pick.3 = (f32[2,8,64,128]{3,2,1,0:T(8,128)}, f32[2,8,64,128]{3,2,1,0:T(8,128)S(1)}) custom-call(f32[8,128]{1,0:T(8,128)S(1)} %get-tuple-element.26.mark, f32[2,8,64,128]{3,2,1,0:T(8,128)S(1)} %copy-done.5, f32[2,8,64,128]{3,2,1,0:T(8,128)S(1)} %copy-done.6, f32[2,8,64,128]{3,2,1,0:T(8,128)S(1)} %copy-done.5, f32[2,8,64,128]{3,2,1,0:T(8,128)S(1)} %copy-done.6), custom_call_target="tpu_custom_call" | custom-call | tf_op jit(solution)/shard_map/pick/pallas_call | solution.py:169
  22.3 2.1 %collective-permute-start = (f32[2,8,64,128]{3,2,1,0:T(8,128)}, f32[2,8,64,128]{3,2,1,0:T(8,128)S(1)}, u32[]{:S(2)}, u32[]{:S(2)}) collective-permute-start(f32[2,8,64,128]{3,2,1,0:T(8,128)} %get-tuple-element.27), channel_id=1, source_target_pairs={{0,2},{1,3},{2,0},{3,1},{4,6},{5,7},{6,4},{7,5},{8,10},{9,11},{10,... | collective-permute-start | bytes 1572872 | tf_op jit(solution)/shard_map/ppermute | solution.py:519
  24.3 0.0 collective-permute-done.5
  24.3 1.6 %collective-permute-start.6 = (f32[1,64,128]{2,1,0:T(8,128)S(1)}, f32[1,64,128]{2,1,0:T(8,128)S(1)}, u32[]{:S(2)}, u32[]{:S(2)}) collective-permute-start(f32[1,64,128]{2,1,0:T(8,128)S(1)} %collective-permute-done.5), channel_id=1, source_target_pairs={{0,8},{1,9},{2,10},{3,11},{4,12},{5,13},{6,14},{7,15},{8,0},{9,1},... | collective-permute-start | bytes 98312 | tf_op jit(solution)/shard_map/ppermute | solution.py:519
  25.9 2.6 %collective-permute-start.7 = (f32[1,64,128]{2,1,0:T(8,128)S(1)}, f32[1,64,128]{2,1,0:T(8,128)S(1)}, u32[]{:S(2)}, u32[]{:S(2)}) collective-permute-start(f32[1,64,128]{2,1,0:T(8,128)S(1)} %collective-permute-done.5), channel_id=1, source_target_pairs={{0,16},{1,17},{2,18},{3,19},{4,20},{5,21},{6,22},{7,23},{8,24},{9,... | collective-permute-start | bytes 98312 | tf_op jit(solution)/shard_map/ppermute | solution.py:519
  28.5 0.0 collective-permute-done.6
  28.5 3.4 %collective-permute-start.8 = (f32[1,64,128]{2,1,0:T(8,128)S(1)}, f32[1,64,128]{2,1,0:T(8,128)S(1)}, u32[]{:S(2)}, u32[]{:S(2)}) collective-permute-start(f32[1,64,128]{2,1,0:T(8,128)S(1)} %collective-permute-done.5), channel_id=1, source_target_pairs={{0,24},{1,25},{2,26},{3,27},{4,28},{5,29},{6,30},{7,31},{8,16},{9,... | collective-permute-start | bytes 98312 | tf_op jit(solution)/shard_map/ppermute | solution.py:519
  31.9 0.0 collective-permute-done.2.over
  31.9 0.0 collective-permute-done.7
  31.9 2.3 %collective-permute-done.8 = f32[1,64,128]{2,1,0:T(8,128)S(1)} collective-permute-done((f32[1,64,128]{2,1,0:T(8,128)S(1)}, f32[1,64,128]{2,1,0:T(8,128)S(1)}, u32[]{:S(2)}, u32[]{:S(2)}) %collective-permute-start.8) | collective-permute-done | bytes 32800 | tf_op jit(solution)/shard_map/ppermute | solution.py:519
  34.2 1.5 %collective-permute-start.9 = (f32[4,64,128]{2,1,0:T(8,128)S(1)}, f32[4,64,128]{2,1,0:T(8,128)S(1)}, u32[]{:S(2)}, u32[]{:S(2)}) collective-permute-start(f32[4,64,128]{2,1,0:T(8,128)S(1)} %constant_dynamic-update-slice_fusion.mine), channel_id=1, source_target_pairs={{0,4},{1,5},{2,6},{3,7},{4,0},{5,1},{6,2},{7,3},{8,12},{9,13},{10,... | collective-permute-start | bytes 393224 | tf_op jit(solution)/shard_map/ppermute | solution.py:519
  35.8 3.4 %collective-permute-done.9.other = f32[4,64,128]{2,1,0:T(8,128)S(1)} collective-permute-done((f32[4,64,128]{2,1,0:T(8,128)S(1)}, f32[4,64,128]{2,1,0:T(8,128)S(1)}, u32[]{:S(2)}, u32[]{:S(2)}) %collective-permute-start.9) | collective-permute-done | bytes 131104 | tf_op jit(solution)/shard_map/ppermute | solution.py:519
  39.3 0.1 collective-permute-start.10
  40.0 0.0 collective-permute-done.4.c1
  40.0 0.6 collective-permute-start.11
  40.6 0.4 collective-permute-done.10.c3
  41.0 3.7 %copy-done.2 = f32[9,2048,128]{2,1,0:T(8,128)S(1)} copy-done((f32[9,2048,128]{2,1,0:T(8,128)S(1)}, f32[9,2048,128]{2,1,0:T(8,128)}, u32[]{:S(2)}) %copy-start.2) | copy-done | bytes 9437208
  44.7 13.5 %forward_steps.1 = (f32[8,8,2,64,128]{4,3,2,1,0:T(8,128)S(1)}, f32[8,32,64,128]{3,2,1,0:T(8,128)S(1)}, f32[32,64,128]{2,1,0:T(8,128)S(1)}, f32[8,128]{1,0:T(8,128)S(1)}) custom-call(s32[1]{0:T(128)} %bitcast.8.start, s32[2]{0:T(128)S(1)} %copy-done.9, f32[2,8,64,128]{3,2,1,0:T(8,128)S(1)} %pick.4.own, f32[2,8,64,128]{3,2,1,0:T(8,128)S(1)} %collective-permute-done.1.mate, ...), custom_call_target="tpu_custom_call" | custom-call | flops 62914560 | bytes 33554432 | tf_op jit(solution)/shard_map/forward_steps/pallas_call | solution.py:562
  58.1 0.0 copy-start.7
  58.2 0.0 collective-permute-done.over
  58.2 0.2 collective-permute-start.12
  58.4 0.0 collective-permute-done.11.mate
  58.4 1.7 %collective-permute-done.12.far = f32[2,8,64,128]{3,2,1,0:T(8,128)S(1)} collective-permute-done((f32[2,8,64,128]{3,2,1,0:T(8,128)S(1)}, f32[2,8,64,128]{3,2,1,0:T(8,128)S(1)}, u32[]{:S(2)}, u32[]{:S(2)}) %collective-permute-start.12) | collective-permute-done | bytes 524320 | tf_op jit(solution)/shard_map/ppermute | solution.py:519
  60.1 12.9 %adjoint_steps.1 = (f32[8,64,128]{2,1,0:T(8,128)S(1)}, f32[8,64,128]{2,1,0:T(8,128)S(1)}) custom-call(f32[8,128]{1,0:T(8,128)S(1)} %get-tuple-element.32.mark, f32[2,8,64,128]{3,2,1,0:T(8,128)S(1)} %get-tuple-element.33.own, f32[2,8,64,128]{3,2,1,0:T(8,128)S(1)} %collective-permute-done.11.mate, f32[2,8,64,128]{3,2,1,0:T(8,128)S(1)} %collective-permute-done.over, ...), custom_call_target="tpu_custom_call" | custom-call | flops 62914560 | bytes 33554432 | tf_op jit(solution)/shard_map/adjoint_steps/pallas_call | solution.py:581
  73.1 0.6 collective-permute-start.13
  73.7 7.8 %collective-permute-done.13.other = f32[8,64,128]{2,1,0:T(8,128)S(1)} collective-permute-done((f32[8,64,128]{2,1,0:T(8,128)S(1)}, f32[8,64,128]{2,1,0:T(8,128)S(1)}, u32[]{:S(2)}, u32[]{:S(2)}) %collective-permute-start.13) | collective-permute-done | bytes 262176 | tf_op jit(solution)/shard_map/ppermute | solution.py:519
  81.6 1.6 %collective-permute-start.14 = (f32[4,64,128]{2,1,0:T(8,128)S(1)}, f32[4,64,128]{2,1,0:T(8,128)S(1)}, u32[]{:S(2)}, u32[]{:S(2)}) collective-permute-start(f32[4,64,128]{2,1,0:T(8,128)S(1)} %get-tuple-element.41), channel_id=1, source_target_pairs={{0,4},{1,5},{2,6},{3,7},{4,0},{5,1},{6,2},{7,3},{8,12},{9,13},{10,... | collective-permute-start | bytes 393224 | tf_op jit(solution)/shard_map/ppermute | solution.py:519
  83.1 3.4 %collective-permute-done.14.other = f32[4,64,128]{2,1,0:T(8,128)S(1)} collective-permute-done((f32[4,64,128]{2,1,0:T(8,128)S(1)}, f32[4,64,128]{2,1,0:T(8,128)S(1)}, u32[]{:S(2)}, u32[]{:S(2)}) %collective-permute-start.14) | collective-permute-done | bytes 131104 | tf_op jit(solution)/shard_map/ppermute | solution.py:519
  86.6 0.1 collective-permute-start.15
  86.7 4.3 %collective-permute-done.15.other = f32[2,64,128]{2,1,0:T(8,128)S(1)} collective-permute-done((f32[2,64,128]{2,1,0:T(8,128)S(1)}, f32[2,64,128]{2,1,0:T(8,128)S(1)}, u32[]{:S(2)}, u32[]{:S(2)}) %collective-permute-start.15) | collective-permute-done | bytes 65568 | tf_op jit(solution)/shard_map/ppermute | solution.py:519
  91.0 2.0 %collective-permute-start.16 = (f32[2,64,128]{2,1,0:T(8,128)S(1)}, f32[2,64,128]{2,1,0:T(8,128)S(1)}, u32[]{:S(2)}, u32[]{:S(2)}) collective-permute-start(f32[2,64,128]{2,1,0:T(8,128)S(1)} %add_kernel.1.mine), channel_id=1, source_target_pairs={{0,16},{1,17},{2,18},{3,19},{4,20},{5,21},{6,22},{7,23},{8,24},{9,... | collective-permute-start | bytes 196616 | tf_op jit(solution)/shard_map/ppermute | solution.py:519
  93.0 3.9 %collective-permute-done.16.other = f32[2,64,128]{2,1,0:T(8,128)S(1)} collective-permute-done((f32[2,64,128]{2,1,0:T(8,128)S(1)}, f32[2,64,128]{2,1,0:T(8,128)S(1)}, u32[]{:S(2)}, u32[]{:S(2)}) %collective-permute-start.16) | collective-permute-done | bytes 65568 | tf_op jit(solution)/shard_map/ppermute | solution.py:519
  96.9 0.1 sums_kernel.1
  97.0 0.4 collective-permute-start.17
  97.4 0.0 collective-permute-start.18
  97.4 1.7 %collective-permute-start.19 = (f32[8,128]{1,0:T(8,128)S(1)}, f32[8,128]{1,0:T(8,128)S(1)}, u32[]{:S(2)}, u32[]{:S(2)}) collective-permute-start(f32[8,128]{1,0:T(8,128)S(1)} %get-tuple-element.45.s0), channel_id=1, source_target_pairs={{0,9},{1,8},{2,11},{3,10},{4,13},{5,12},{6,15},{7,14},{8,1},{9,0},... | collective-permute-start | bytes 12296 | tf_op jit(solution)/shard_map/ppermute | solution.py:519
  99.2 0.0 collective-permute-done.18.s1
  99.2 1.3 %collective-permute-done.19.s2 = f32[8,128]{1,0:T(8,128)S(1)} collective-permute-done((f32[8,128]{1,0:T(8,128)S(1)}, f32[8,128]{1,0:T(8,128)S(1)}, u32[]{:S(2)}, u32[]{:S(2)}) %collective-permute-start.19) | collective-permute-done | bytes 4128 | tf_op jit(solution)/shard_map/ppermute | solution.py:519
  100.5 0.8 collective-permute-done.17.other
  101.3 1.6 %collective-permute-start.20 = (f32[264,128]{1,0:T(8,128)S(1)}, f32[264,128]{1,0:T(8,128)S(1)}, u32[]{:S(2)}, u32[]{:S(2)}) collective-permute-start(f32[264,128]{1,0:T(8,128)S(1)} %get-tuple-element.46.mine), channel_id=1, source_target_pairs={{0,4},{1,5},{2,6},{3,7},{4,0},{5,1},{6,2},{7,3},{8,12},{9,13},{10,... | collective-permute-start | bytes 405512 | tf_op jit(solution)/shard_map/ppermute | solution.py:519
  102.9 0.5 collective-permute-start.21
  103.5 1.4 %collective-permute-start.22 = (f32[8,128]{1,0:T(8,128)S(1)}, f32[8,128]{1,0:T(8,128)S(1)}, u32[]{:S(2)}, u32[]{:S(2)}) collective-permute-start(f32[8,128]{1,0:T(8,128)S(1)} %get-tuple-element.47.s0), channel_id=1, source_target_pairs={{0,6},{1,7},{2,4},{3,5},{4,2},{5,3},{6,0},{7,1},{8,14},{9,15},{10,... | collective-permute-start | bytes 12296 | tf_op jit(solution)/shard_map/ppermute | solution.py:519
  104.9 1.6 %collective-permute-done.21.s1 = f32[8,128]{1,0:T(8,128)S(1)} collective-permute-done((f32[8,128]{1,0:T(8,128)S(1)}, f32[8,128]{1,0:T(8,128)S(1)}, u32[]{:S(2)}, u32[]{:S(2)}) %collective-permute-start.21) | collective-permute-done | bytes 4128 | tf_op jit(solution)/shard_map/ppermute | solution.py:519
  106.5 1.4 %collective-permute-done.22.s2 = f32[8,128]{1,0:T(8,128)S(1)} collective-permute-done((f32[8,128]{1,0:T(8,128)S(1)}, f32[8,128]{1,0:T(8,128)S(1)}, u32[]{:S(2)}, u32[]{:S(2)}) %collective-permute-start.22) | collective-permute-done | bytes 4128 | tf_op jit(solution)/shard_map/ppermute | solution.py:519
  108.0 0.8 finish.1
  (25 shorter events, 0.2 us)
Async XLA Ops:
  0.6 8.3 %copy-start = (f32[2,8,512]{2,1,0:T(8,128)S(1)}, f32[2,8,512]{2,1,0:T(8,128)}, u32[]{:S(2)}) copy-start(f32[2,8,512]{2,1,0:T(8,128)} %param.16) | copy-start | bytes 98308
  0.6 1.0 copy-start.8
  2.4 22.0 %collective-permute-start.5 = (f32[1,64,128]{2,1,0:T(8,128)S(1)}, f32[1,64,128]{2,1,0:T(8,128)S(1)}, u32[]{:S(2)}, u32[]{:S(2)}) collective-permute-start(f32[1,64,128]{2,1,0:T(8,128)S(1)} %get-tuple-element.29), channel_id=1, source_target_pairs={{0,2},{1,3},{2,0},{3,1},{4,6},{5,7},{6,4},{7,5},{8,10},{9,11},{10,... | collective-permute-start | bytes 98312 | tf_op jit(solution)/shard_map/ppermute | solution.py:519
  5.3 1.0 copy-start.3
  6.4 1.0 copy-start.4
  7.6 24.3 %collective-permute-start.2 = (f32[2,8,64,128]{3,2,1,0:T(8,128)S(1)}, f32[2,8,64,128]{3,2,1,0:T(8,128)S(1)}, u32[]{:S(2)}, u32[]{:S(2)}) collective-permute-start(f32[2,8,64,128]{3,2,1,0:T(8,128)S(1)} %pick.5), channel_id=1, source_target_pairs={{0,2},{1,3},{2,0},{3,1},{4,6},{5,7},{6,4},{7,5},{8,10},{9,11},{10,... | collective-permute-start | bytes 1572872 | tf_op jit(solution)/shard_map/ppermute | solution.py:519
  7.9 33.1 %collective-permute-start.1 = (f32[2,8,64,128]{3,2,1,0:T(8,128)S(1)}, f32[2,8,64,128]{3,2,1,0:T(8,128)S(1)}, u32[]{:S(2)}, u32[]{:S(2)}) collective-permute-start(f32[2,8,64,128]{3,2,1,0:T(8,128)S(1)} %pick.4.own), channel_id=1, source_target_pairs={{0,1},{1,0},{2,3},{3,2},{4,5},{5,4},{6,7},{7,6},{8,9},{9,8},{10,11... | collective-permute-start | bytes 1572872 | tf_op jit(solution)/shard_map/ppermute | solution.py:519
  9.1 12.0 %copy-start.5 = (f32[2,8,64,128]{3,2,1,0:T(8,128)S(1)}, f32[2,8,64,128]{3,2,1,0:T(8,128)}, u32[]{:S(2)}) copy-start(f32[2,8,64,128]{3,2,1,0:T(8,128)} %refs_2_.1) | copy-start | bytes 1572868
  9.1 12.0 %copy-start.6 = (f32[2,8,64,128]{3,2,1,0:T(8,128)S(1)}, f32[2,8,64,128]{3,2,1,0:T(8,128)}, u32[]{:S(2)}) copy-start(f32[2,8,64,128]{3,2,1,0:T(8,128)} %refs_3_.1) | copy-start | bytes 1572868
  9.2 31.8 %copy-start.9 = (s32[2]{0:T(128)S(1)}, s32[2]{0:T(128)}, u32[]{:S(2)}) copy-start(s32[2]{0:T(128)} %sources.1) | copy-start | bytes 28
  17.5 3.6 %copy-start.1 = (f32[9,2048,128]{2,1,0:T(8,128)}, f32[9,2048,128]{2,1,0:T(8,128)S(1)}, u32[]{:S(2)}) copy-start(f32[9,2048,128]{2,1,0:T(8,128)S(1)} %get-tuple-element.30) | copy-start | bytes 28311556
  22.3 35.9 %collective-permute-start = (f32[2,8,64,128]{3,2,1,0:T(8,128)}, f32[2,8,64,128]{3,2,1,0:T(8,128)S(1)}, u32[]{:S(2)}, u32[]{:S(2)}) collective-permute-start(f32[2,8,64,128]{3,2,1,0:T(8,128)} %get-tuple-element.27), channel_id=1, source_target_pairs={{0,2},{1,3},{2,0},{3,1},{4,6},{5,7},{6,4},{7,5},{8,10},{9,11},{10,... | collective-permute-start | bytes 1572872 | tf_op jit(solution)/shard_map/ppermute | solution.py:519
  24.3 4.2 %collective-permute-start.6 = (f32[1,64,128]{2,1,0:T(8,128)S(1)}, f32[1,64,128]{2,1,0:T(8,128)S(1)}, u32[]{:S(2)}, u32[]{:S(2)}) collective-permute-start(f32[1,64,128]{2,1,0:T(8,128)S(1)} %collective-permute-done.5), channel_id=1, source_target_pairs={{0,8},{1,9},{2,10},{3,11},{4,12},{5,13},{6,14},{7,15},{8,0},{9,1},... | collective-permute-start | bytes 98312 | tf_op jit(solution)/shard_map/ppermute | solution.py:519
  25.9 6.0 %collective-permute-start.7 = (f32[1,64,128]{2,1,0:T(8,128)S(1)}, f32[1,64,128]{2,1,0:T(8,128)S(1)}, u32[]{:S(2)}, u32[]{:S(2)}) collective-permute-start(f32[1,64,128]{2,1,0:T(8,128)S(1)} %collective-permute-done.5), channel_id=1, source_target_pairs={{0,16},{1,17},{2,18},{3,19},{4,20},{5,21},{6,22},{7,23},{8,24},{9,... | collective-permute-start | bytes 98312 | tf_op jit(solution)/shard_map/ppermute | solution.py:519
  28.5 5.7 %collective-permute-start.8 = (f32[1,64,128]{2,1,0:T(8,128)S(1)}, f32[1,64,128]{2,1,0:T(8,128)S(1)}, u32[]{:S(2)}, u32[]{:S(2)}) collective-permute-start(f32[1,64,128]{2,1,0:T(8,128)S(1)} %collective-permute-done.5), channel_id=1, source_target_pairs={{0,24},{1,25},{2,26},{3,27},{4,28},{5,29},{6,30},{7,31},{8,16},{9,... | collective-permute-start | bytes 98312 | tf_op jit(solution)/shard_map/ppermute | solution.py:519
  31.9 9.1 %collective-permute-start.3 = (f32[2,8,64,128]{3,2,1,0:T(8,128)S(1)}, f32[2,8,64,128]{3,2,1,0:T(8,128)S(1)}, u32[]{:S(2)}, u32[]{:S(2)}) collective-permute-start(f32[2,8,64,128]{3,2,1,0:T(8,128)S(1)} %collective-permute-done.2.over), channel_id=1, source_target_pairs={{0,1},{1,0},{2,3},{3,2},{4,5},{5,4},{6,7},{7,6},{8,9},{9,8},{10,11... | collective-permute-start | bytes 1572872 | tf_op jit(solution)/shard_map/ppermute | solution.py:519
  34.2 5.0 %collective-permute-start.9 = (f32[4,64,128]{2,1,0:T(8,128)S(1)}, f32[4,64,128]{2,1,0:T(8,128)S(1)}, u32[]{:S(2)}, u32[]{:S(2)}) collective-permute-start(f32[4,64,128]{2,1,0:T(8,128)S(1)} %constant_dynamic-update-slice_fusion.mine), channel_id=1, source_target_pairs={{0,4},{1,5},{2,6},{3,7},{4,0},{5,1},{6,2},{7,3},{8,12},{9,13},{10,... | collective-permute-start | bytes 393224 | tf_op jit(solution)/shard_map/ppermute | solution.py:519
  35.8 4.2 %collective-permute-start.4 = (f32[8,64,128]{2,1,0:T(8,128)}, f32[8,64,128]{2,1,0:T(8,128)}, u32[]{:S(2)}, u32[]{:S(2)}) collective-permute-start(f32[8,64,128]{2,1,0:T(8,128)} %get-tuple-element.28.c0), channel_id=1, source_target_pairs={{0,1},{1,0},{2,3},{3,2},{4,5},{5,4},{6,7},{7,6},{8,9},{9,8},{10,11... | collective-permute-start | bytes 786440 | tf_op jit(solution)/shard_map/ppermute | solution.py:519
  39.3 1.7 %collective-permute-start.10 = (f32[8,64,128]{2,1,0:T(8,128)S(1)}, f32[8,64,128]{2,1,0:T(8,128)}, u32[]{:S(2)}, u32[]{:S(2)}) collective-permute-start(f32[8,64,128]{2,1,0:T(8,128)S(1)} %arrange_kernel.1.c2), channel_id=1, source_target_pairs={{0,1},{1,0},{2,3},{3,2},{4,5},{5,4},{6,7},{7,6},{8,9},{9,8},{10,11... | collective-permute-start | bytes 786440 | tf_op jit(solution)/shard_map/ppermute | solution.py:519
  40.0 18.4 %collective-permute-start.11 = (f32[2,8,64,128]{3,2,1,0:T(8,128)S(1)}, f32[2,8,64,128]{3,2,1,0:T(8,128)S(1)}, u32[]{:S(2)}, u32[]{:S(2)}) collective-permute-start(f32[2,8,64,128]{3,2,1,0:T(8,128)S(1)} %get-tuple-element.33.own), channel_id=1, source_target_pairs={{0,1},{1,0},{2,3},{3,2},{4,5},{5,4},{6,7},{7,6},{8,9},{9,8},{10,11... | collective-permute-start | bytes 1572872 | tf_op jit(solution)/shard_map/ppermute | solution.py:519
  41.0 3.7 %copy-start.2 = (f32[9,2048,128]{2,1,0:T(8,128)S(1)}, f32[9,2048,128]{2,1,0:T(8,128)}, u32[]{:S(2)}) copy-start(f32[9,2048,128]{2,1,0:T(8,128)} %copy-done.1) | copy-start | bytes 28311556
  58.1 38.7 %copy-start.7 = (f32[8,64,128]{2,1,0:T(8,128)S(1)}, f32[8,64,128]{2,1,0:T(8,128)}, u32[]{:S(2)}) copy-start(f32[8,64,128]{2,1,0:T(8,128)} %momentum.3) | copy-start | bytes 786436
  58.2 2.0 %collective-permute-start.12 = (f32[2,8,64,128]{3,2,1,0:T(8,128)S(1)}, f32[2,8,64,128]{3,2,1,0:T(8,128)S(1)}, u32[]{:S(2)}, u32[]{:S(2)}) collective-permute-start(f32[2,8,64,128]{3,2,1,0:T(8,128)S(1)} %collective-permute-done.over), channel_id=1, source_target_pairs={{0,1},{1,0},{2,3},{3,2},{4,5},{5,4},{6,7},{7,6},{8,9},{9,8},{10,11... | collective-permute-start | bytes 1572872 | tf_op jit(solution)/shard_map/ppermute | solution.py:519
  73.1 8.4 %collective-permute-start.13 = (f32[8,64,128]{2,1,0:T(8,128)S(1)}, f32[8,64,128]{2,1,0:T(8,128)S(1)}, u32[]{:S(2)}, u32[]{:S(2)}) collective-permute-start(f32[8,64,128]{2,1,0:T(8,128)S(1)} %get-tuple-element.39), channel_id=1, source_target_pairs={{0,2},{1,3},{2,0},{3,1},{4,6},{5,7},{6,4},{7,5},{8,10},{9,11},{10,... | collective-permute-start | bytes 786440 | tf_op jit(solution)/shard_map/ppermute | solution.py:519
  81.6 5.0 %collective-permute-start.14 = (f32[4,64,128]{2,1,0:T(8,128)S(1)}, f32[4,64,128]{2,1,0:T(8,128)S(1)}, u32[]{:S(2)}, u32[]{:S(2)}) collective-permute-start(f32[4,64,128]{2,1,0:T(8,128)S(1)} %get-tuple-element.41), channel_id=1, source_target_pairs={{0,4},{1,5},{2,6},{3,7},{4,0},{5,1},{6,2},{7,3},{8,12},{9,13},{10,... | collective-permute-start | bytes 393224 | tf_op jit(solution)/shard_map/ppermute | solution.py:519
  86.6 4.3 %collective-permute-start.15 = (f32[2,64,128]{2,1,0:T(8,128)S(1)}, f32[2,64,128]{2,1,0:T(8,128)S(1)}, u32[]{:S(2)}, u32[]{:S(2)}) collective-permute-start(f32[2,64,128]{2,1,0:T(8,128)S(1)} %get-tuple-element.43), channel_id=1, source_target_pairs={{0,8},{1,9},{2,10},{3,11},{4,12},{5,13},{6,14},{7,15},{8,0},{9,1},... | collective-permute-start | bytes 196616 | tf_op jit(solution)/shard_map/ppermute | solution.py:519
  91.0 5.9 %collective-permute-start.16 = (f32[2,64,128]{2,1,0:T(8,128)S(1)}, f32[2,64,128]{2,1,0:T(8,128)S(1)}, u32[]{:S(2)}, u32[]{:S(2)}) collective-permute-start(f32[2,64,128]{2,1,0:T(8,128)S(1)} %add_kernel.1.mine), channel_id=1, source_target_pairs={{0,16},{1,17},{2,18},{3,19},{4,20},{5,21},{6,22},{7,23},{8,24},{9,... | collective-permute-start | bytes 196616 | tf_op jit(solution)/shard_map/ppermute | solution.py:519
  97.0 4.3 %collective-permute-start.17 = (f32[136,128]{1,0:T(8,128)S(1)}, f32[136,128]{1,0:T(8,128)S(1)}, u32[]{:S(2)}, u32[]{:S(2)}) collective-permute-start(f32[136,128]{1,0:T(8,128)S(1)} %get-tuple-element.44.mine), channel_id=1, source_target_pairs={{0,8},{1,9},{2,10},{3,11},{4,12},{5,13},{6,14},{7,15},{8,0},{9,1},... | collective-permute-start | bytes 208904 | tf_op jit(solution)/shard_map/ppermute | solution.py:519
  97.4 1.8 %collective-permute-start.18 = (f32[8,128]{1,0:T(8,128)S(1)}, f32[8,128]{1,0:T(8,128)S(1)}, u32[]{:S(2)}, u32[]{:S(2)}) collective-permute-start(f32[8,128]{1,0:T(8,128)S(1)} %get-tuple-element.45.s0), channel_id=1, source_target_pairs={{0,1},{1,0},{2,3},{3,2},{4,5},{5,4},{6,7},{7,6},{8,9},{9,8},{10,11... | collective-permute-start | bytes 12296 | tf_op jit(solution)/shard_map/ppermute | solution.py:519
  97.4 3.1 %collective-permute-start.19 = (f32[8,128]{1,0:T(8,128)S(1)}, f32[8,128]{1,0:T(8,128)S(1)}, u32[]{:S(2)}, u32[]{:S(2)}) collective-permute-start(f32[8,128]{1,0:T(8,128)S(1)} %get-tuple-element.45.s0), channel_id=1, source_target_pairs={{0,9},{1,8},{2,11},{3,10},{4,13},{5,12},{6,15},{7,14},{8,1},{9,0},... | collective-permute-start | bytes 12296 | tf_op jit(solution)/shard_map/ppermute | solution.py:519
  101.3 6.6 %collective-permute-start.20 = (f32[264,128]{1,0:T(8,128)S(1)}, f32[264,128]{1,0:T(8,128)S(1)}, u32[]{:S(2)}, u32[]{:S(2)}) collective-permute-start(f32[264,128]{1,0:T(8,128)S(1)} %get-tuple-element.46.mine), channel_id=1, source_target_pairs={{0,4},{1,5},{2,6},{3,7},{4,0},{5,1},{6,2},{7,3},{8,12},{9,13},{10,... | collective-permute-start | bytes 405512 | tf_op jit(solution)/shard_map/ppermute | solution.py:519
  102.9 3.6 %collective-permute-start.21 = (f32[8,128]{1,0:T(8,128)S(1)}, f32[8,128]{1,0:T(8,128)S(1)}, u32[]{:S(2)}, u32[]{:S(2)}) collective-permute-start(f32[8,128]{1,0:T(8,128)S(1)} %get-tuple-element.47.s0), channel_id=1, source_target_pairs={{0,2},{1,3},{2,0},{3,1},{4,6},{5,7},{6,4},{7,5},{8,10},{9,11},{10,... | collective-permute-start | bytes 12296 | tf_op jit(solution)/shard_map/ppermute | solution.py:519
  103.5 4.5 %collective-permute-start.22 = (f32[8,128]{1,0:T(8,128)S(1)}, f32[8,128]{1,0:T(8,128)S(1)}, u32[]{:S(2)}, u32[]{:S(2)}) collective-permute-start(f32[8,128]{1,0:T(8,128)S(1)} %get-tuple-element.47.s0), channel_id=1, source_target_pairs={{0,6},{1,7},{2,4},{3,5},{4,2},{5,3},{6,0},{7,1},{8,14},{9,15},{10,... | collective-permute-start | bytes 12296 | tf_op jit(solution)/shard_map/ppermute | solution.py:519

commit v5 on v4

--- a/solution.py
+++ b/solution.py
@@ -158,29 +158,27 @@
         interleave(outs[n // 2], (n % 2,), held.at[n])
 
 
-def pick(*pairs, after=None):
-    kernel = functools.partial(pick_kernel, tuple(pair[2] for pair in pairs))
+def pick(*pairs, after=None, grant=4):
+    plain = functools.partial(pick_kernel, tuple(pair[2] for pair in pairs))
     fields = [field for pair in pairs for field in pair[:2]]
-    if after is not None:
-        kernel, plain = (lambda mark, *refs: plain(*refs)), kernel
-        fields = [after] + fields
-    shape = pairs[0][0].shape[1:]
-    vmem = pl.BlockSpec(memory_space=pltpu.VMEM)
+    shape = fields[0].shape[1:]
+    vmem, hbm = pl.BlockSpec(memory_space=pltpu.VMEM), pl.BlockSpec(memory_space=pltpu.HBM)
+    marks = [] if after is None else [after]
     return pl.pallas_call(
-        kernel,
-        in_specs=[pl.BlockSpec(memory_space=pl.ANY)] * len(fields),
+        lambda *refs: plain(*refs[len(marks) :]),
+        in_specs=[vmem] * len(marks) + [hbm] * len(fields),
         out_specs=[vmem] * len(pairs),
         out_shape=[jax.ShapeDtypeStruct((2, *shape), jnp.float32)] * len(pairs),
-        scratch_shapes=[pltpu.VMEM((2 * len(pairs), *shape), jnp.float32), pltpu.SemaphoreType.DMA((2 * len(pairs),))],
-        compiler_params=pltpu.CompilerParams(vmem_limit_bytes=8 * 2**20),
+        scratch_shapes=[pltpu.VMEM((len(fields), *shape), jnp.float32), pltpu.SemaphoreType.DMA((len(fields),))],
+        compiler_params=pltpu.CompilerParams(vmem_limit_bytes=grant * 2**20),
         name="pick",
-    )(*fields)
+    )(*marks, *fields)
 
 
 def courant_kernel(courant, whole, piece):
-    shot = lax.axis_index("shot")
     interleave(whole, (), courant, 1.0 / 12.0)
-    piece[0] = whole[(shot % 2) * (courant.shape[0] // 2) + shot // 2]
+    count = piece.shape[0]
+    piece[...] = whole[pl.ds(lax.axis_index("shot") % 2 * count, count)]
 
 
 def band(lanes):
@@ -188,37 +186,59 @@
     return jnp.where(near == 0, -90.0, jnp.where(near == 1, 16.0, jnp.where(near == 2, -1.0, 0.0))).astype(jnp.bfloat16)
 
 
-def laps12(field, z, banded):
+def along_y(field, z, banded, out):
     rows, lanes = field.shape[1:]
-    sub = lax.broadcasted_iota(jnp.int32, (8, lanes), 0)
-
-    def later(block):
-        return jnp.where(sub < 7, pltpu.roll(block, 7, 0), 0.0)
-
-    def earlier(block):
-        return jnp.where(sub > 0, pltpu.roll(block, 1, 0), 0.0)
-
     whole = field[pl.ds(z + 2, BATCH)].reshape(BATCH * rows, lanes)
     high = whole.astype(jnp.bfloat16)
     low = (whole - high.astype(jnp.float32)).astype(jnp.bfloat16)
-    along_y = jnp.dot(jnp.concatenate([high, low], 1), banded, preferred_element_type=jnp.float32)
-    results = []
-    for j in range(BATCH):
-        center = field[z + j + 2]
-        first, second = center[0:8], center[8:16]
-        last, before = center[rows - 8 :], center[rows - 16 : rows - 8]
-        late, early = later(first), earlier(last)
-        near = jnp.concatenate([center[8:], late], 0) + jnp.concatenate([early, center[:-8]], 0)
-        far = jnp.concatenate([center[16:], late, later(second)], 0) + jnp.concatenate(
-            [earlier(before), early, center[:-16]], 0
-        )
-        near = near + (field[z + j + 1] + field[z + j + 3])
-        far = far + (field[z + j] + field[z + j + 4])
-        results.append((center, 16.0 * near - far + along_y[j * rows : (j + 1) * rows]))
-    return results
-
-
-def scatter_kernel(row_ref, y_ref, obs_ref, out_ref, mark, spread):
+    out[...] = jnp.dot(jnp.concatenate([high, low], 1), banded[...], preferred_element_type=jnp.float32)
+
+
+def laps12(field, z, y_part, fetch, finish):
+    rows, lanes = field.shape[1:]
+    groups = rows // 8
+    sub = lax.broadcasted_iota(jnp.int32, (8, lanes), 0)
+
+    def later(block):
+        return jnp.where(sub < 7, pltpu.roll(block, 7, 0), 0.0)
+
+    def earlier(block):
+        return jnp.where(sub > 0, pltpu.roll(block, 1, 0), 0.0)
+
+    for base in range(0, BATCH, PLANES):
+        held = {}
+
+        def tile(j, i):
+            if (j, i) not in held:
+                if i < 0:
+                    held[j, i] = earlier(tile(j, i + groups))
+                elif i >= groups:
+                    held[j, i] = later(tile(j, i - groups))
+                else:
+                    held[j, i] = field[z + j + 2, i * 8 : (i + 1) * 8]
+            return held[j, i]
+
+        def load(i):
+            found = []
+            for j in range(base, base + PLANES):
+                center = tile(j, i)
+                near = (tile(j, i - 1), tile(j, i + 1), tile(j - 1, i), tile(j + 1, i))
+                far = (tile(j, i - 2), tile(j, i + 2), tile(j - 2, i), tile(j + 2, i))
+                at = (j * groups + i) * 8
+                found.append((center, near, far, y_part[at : at + 8], fetch(j, slice(i * 8, i * 8 + 8))))
+            return found
+
+        ready = load(0)
+        for i in range(groups):
+            upcoming = load(i + 1) if i + 1 < groups else None
+            for j, (center, near, far, part, extra) in enumerate(ready):
+                near = (near[0] + near[1]) + (near[2] + near[3])
+                far = (far[0] + far[1]) + (far[2] + far[3])
+                finish(base + j, slice(i * 8, i * 8 + 8), center, 16.0 * near + (part - far), extra)
+            ready = upcoming
+
+
+def scatter_kernel(row_ref, y_ref, obs_ref, out_ref, mark, second, spread):
     receivers, steps = obs_ref.shape
     lanes = out_ref.shape[2]
     tile = out_ref.shape[1]
@@ -238,6 +258,7 @@
         spread[0:receivers, cols] = jnp.where(at, 1.0, 0.0).astype(jnp.bfloat16)
         spread[receivers:, cols] = jnp.zeros((receivers, lanes), jnp.bfloat16)
         mark[...] = jnp.zeros(mark.shape, jnp.float32)
+        second[...] = jnp.zeros(mark.shape, jnp.float32)
 
     ids = lax.broadcasted_iota(jnp.int32, (tile, receivers), 0) + pl.program_id(0) * tile
     chosen = jnp.where(ids == row_ref[...], 1.0, 0.0).astype(jnp.bfloat16)
@@ -265,13 +286,15 @@
         out_specs=[
             pl.BlockSpec((steps + 1, tile, rows_y), lambda t: (0, t, 0)),
             pl.BlockSpec((8, rows_y), lambda t: (0, 0)),
+            pl.BlockSpec((8, rows_y), lambda t: (0, 0)),
         ],
         out_shape=[
             jax.ShapeDtypeStruct((steps + 1, rows_all, rows_y), jnp.float32),
             jax.ShapeDtypeStruct((8, rows_y), jnp.float32),
+            jax.ShapeDtypeStruct((8, rows_y), jnp.float32),
         ],
         scratch_shapes=[pltpu.VMEM((2 * receivers, (steps + 1) * rows_y), jnp.bfloat16)],
-        compiler_params=pltpu.CompilerParams(vmem_limit_bytes=20 * 2**20),
+        compiler_params=pltpu.CompilerParams(vmem_limit_bytes=8 * 2**20),
         cost_estimate=pl.CostEstimate(
             flops=4 * rows_all * receivers * (steps + 1) * rows_y,
             bytes_accessed=4 * (steps + 1) * rows_all * rows_y,
@@ -302,21 +325,31 @@
 
 
 BATCH = 4
-
-
-def for_owned(mine, planes, body):
+PLANES = 2
+
+
+def sweep(core, planes, field, banded, y_first, y_second, work):
+    order = [(chip, owned) for owned in (True, False) for chip in (0, 1)]
+    parts = (y_first, y_second)
+
+    def first(chip, owned):
+        return (2 * chip + (core if owned else 1 - core)) * planes
+
+    along_y(field, first(*order[0]), banded, y_first)
     for owned in (True, False):
-        core = mine if owned else 1 - mine
-
-        @pl.loop(0, 2 * planes // BATCH)
-        def _(index):
-            chip, p = index // (planes // BATCH), (index % (planes // BATCH)) * BATCH
-            z = (2 * chip + core) * planes + p
-            body(z, chip if owned else None, p)
+
+        @pl.loop(0, 2)
+        def _(chip):
+            z = first(chip, owned)
+            onward = jnp.where(chip == 0, first(1, owned), first(0, False))
+            for n in range(planes // BATCH):
+                last = n == planes // BATCH - 1
+                along_y(field, onward if last else z + (n + 1) * BATCH, banded, parts[(n + 1) % 2])
+                work(z + n * BATCH, parts[n % 2], chip if owned else None, n * BATCH)
 
 
 def forward_kernel(
-    start, sources, own, mate, over, far, c0, c1, c2, c3, placed, laps, inject, cour, mark, even, odd, banded
+    start, sources, scattered, own, mate, over, far, c0, c1, c2, c3, placed, laps, inject, cour, mark, even, odd, banded, y0, y1
 ):
     planes, rows, lanes = c0.shape
     steps = laps.shape[0]
@@ -340,16 +373,21 @@
     source_slab, source_p = source_z // planes, lax.rem(source_z, planes)
 
     def advance(k, now, then):
-        def body(z, chip, p):
-            olds = [then[z + j + 2] for j in range(BATCH)]
-            for j, (center, lap) in enumerate(laps12(now, z, banded[...])):
+        def work(z, y_part, chip, p):
+            def fetch(j, rows):
+                return then[z + j + 2, rows], cour[z + j, rows], placed[k, z + j, rows], placed[steps, z + j, rows]
+
+            def finish(j, rows, center, lap, extra):
+                old, speed, traces, count = extra
                 if chip is not None:
-                    laps[k, p + j, chip] = lap
-                newer = 2.0 * center - olds[j] + cour[z + j] * lap
-                then[z + j + 2] = newer
-                inject[k, z + j] = placed[k, z + j] - placed[steps, z + j] * newer
-
-        for_owned(core, planes, body)
+                    laps[k, p + j, chip, rows] = lap
+                newer = 2.0 * center - old + speed * lap
+                then[z + j + 2, rows] = newer
+                inject[k, z + j, rows] = traces - count * newer
+
+            laps12(now, z, y_part, fetch, finish)
+
+        sweep(core, planes, now, banded, y0, y1, work)
 
         cycle = (start[0] + k) % 48
         phase = (jnp.full((8, lanes), cycle, jnp.int32).astype(jnp.float32) - 24.0) / 12.0
@@ -370,7 +408,7 @@
         advance(2 * pair + 1, odd, even)
 
 
-def adjoint_kernel(mark, own, mate, over, far, cour, laps, inject, keep_ref, send_ref, even, odd, total, banded):
+def adjoint_kernel(mark, own, mate, over, far, cour, laps, inject, keep_a, send_a, keep_b, send_b, even, odd, total, banded, y0, y1):
     planes, rows, lanes = own.shape[1:]
     steps = laps.shape[0]
     groups = rows // 8
@@ -388,44 +426,71 @@
         total[index] = jnp.zeros((rows, lanes), jnp.float32)
 
     def advance(k, now, then):
-        def body(z, chip, p):
-            olds = [then[z + j + 2] for j in range(BATCH)]
-            if chip is not None:
-                sums = [total[chip * planes + p + j] for j in range(BATCH)]
-            for j, (center, lap) in enumerate(laps12(now, z, banded[...])):
-                newer = 2.0 * center - olds[j] + cour[z + j] * (lap - inject[k, z + j])
-                then[z + j + 2] = newer
+        def work(z, y_part, chip, p):
+            def fetch(j, rows):
+                extra = (then[z + j + 2, rows], cour[z + j, rows], inject[k, z + j, rows])
                 if chip is not None:
-                    total[chip * planes + p + j] = sums[j] + newer * laps[k, p + j, chip]
-
-        for_owned(core, planes, body)
+                    extra += (total[chip * planes + p + j, rows], laps[k, p + j, chip, rows])
+                return extra
+
+            def finish(j, rows, center, lap, extra):
+                newer = 2.0 * center - extra[0] + extra[1] * (lap - extra[2])
+                then[z + j + 2, rows] = newer
+                if chip is not None:
+                    total[chip * planes + p + j, rows] = extra[3] + newer * extra[4]
+
+            laps12(now, z, y_part, fetch, finish)
+
+        sweep(core, planes, now, banded, y0, y1, work)
 
     @pl.loop(0, steps // 2)
     def _(pair):
         advance(steps - 1 - 2 * pair, even, odd)
         advance(steps - 2 - 2 * pair, odd, even)
 
-    for ref, chip in ((keep_ref, chip_here), (send_ref, 1 - chip_here)):
-
-        @pl.loop(0, planes)
-        def _(p):
+    half, quarter = planes // 2, planes // 4
+    y = lax.axis_index("shot") % 2
+    here, there = chip_here, 1 - chip_here
+    runs = [(keep_a, 0, half, here, 0), (send_a, 0, half, there, 0)]
+    for ref, side in ((keep_b, y), (send_b, 1 - y)):
+        runs += [(ref, 0, quarter, here, half + side * quarter), (ref, quarter, quarter, there, half + side * quarter)]
+    for ref, at, count, chip, start in runs:
+
+        @pl.loop(0, count)
+        def _(n):
+            p = start + n
             z = (2 * chip + core) * planes + p
             weight = 1.0 + 2.0 * jnp.full((rows, lanes), z, jnp.int32).astype(jnp.float32) / (4 * planes - 1)
             value = weight * total[chip * planes + p] / (12.0 * cour[z])
             for i in range(groups):
-                ref[p, pl.ds(i, 8, stride=groups), :] = value[i * 8 : (i + 1) * 8]
-
-
-def halve_kernel(bit, mine, other, keep, send):
-    half = lax.axis_index("shot") // bit % 2
-    count = keep.shape[0]
-    for ref, part in ((keep, half), (send, 1 - half)):
+                ref[at + n, pl.ds(i, 8, stride=groups), :] = value[i * 8 : (i + 1) * 8]
+
+
+def cross_kernel(keep_a, other_a, keep_b, other_b, next_a, send_a, next_b, send_b):
+    y = lax.axis_index("shot") % 2
+    count = next_a.shape[0]
+    for ref, part in ((next_a, y), (send_a, 1 - y)):
         for p in range(count):
-            ref[p] = mine[part * count + p] + other[part * count + p]
+            ref[p] = keep_a[part * count + p] + other_a[part * count + p]
+    for ref, part in ((next_b, 0), (send_b, 1)):
+        for p in range(count):
+            ref[p] = keep_b[part * count + p] + other_b[part * count + p]
+
+
+def choose_kernel(keep_a, other_a, keep_b, other_b, keep, send):
+    second = lax.axis_index("shot") // 2 % 2 == 1
+    first_half = keep_a[...] + other_a[...]
+    second_half = keep_b[...] + other_b[...]
+    keep[...] = jnp.where(second, second_half, first_half)
+    send[...] = jnp.where(second, first_half, second_half)
 
 
 def add_kernel(mine, other, out):
     out[...] = mine[...] + other[...]
+
+
+def add_sums_kernel(s0, s1, s2, s3, out):
+    out[...] = (s0[...] + s1[...]) + (s2[...] + s3[...])
 
 
 def flip(index, bits):
@@ -437,16 +502,14 @@
 
 
 def arrange_kernel(mine, other, out):
-    shot = lax.axis_index("shot")
-    z, y = shot // 2, shot % 2
-    quarter = mine.shape[0]
-    for part, half in ((mine, y), (other, 1 - y)):
-        for j in range(quarter):
-            out[half * quarter + flip(z, j)] = part[j]
+    y = lax.axis_index("shot") % 2
+    count = mine.shape[0]
+    out[pl.ds(y * count, count)] = mine[...]
+    out[pl.ds((1 - y) * count, count)] = other[...]
 
 
 def first_plane(shot, planes):
-    return (shot % 2) * (planes // 2) + (shot // 2 % 2) * (planes // 4)
+    return (shot // 2 % 2) * (planes // 2) + (shot % 2) * (planes // 4)
 
 
 def sums_kernel(mine, other, momentum, data, sums):
@@ -457,7 +520,7 @@
     parts = [jnp.zeros((rows, lanes), jnp.float32)] * 4
     for j in range(count):
         scaled = mine[j] + other[j]
-        data[j * rows : (j + 1) * rows] = scaled
+        data[j] = scaled
         z = (2 * chip + core) * planes + first + j
         weight = 1.0 + 2.0 * jnp.full((1, lanes), z, jnp.int32).astype(jnp.float32) / (4 * planes - 1)
         moment = momentum[first + j]
@@ -469,38 +532,25 @@
         by_lane = jnp.sum(value, axis=0, keepdims=True)
         return jnp.broadcast_to(jnp.sum(by_lane, axis=1, keepdims=True), (1, lanes))
 
-    value = jnp.concatenate([total(part) for part in parts] + [jnp.zeros((4, lanes), jnp.float32)], 0)
-    data[count * rows :] = value
-    sums[...] = value
-
-
-def join_kernel(mine, other, s0, s1, s2, data, sums):
-    rows = mine.shape[0] - 8
-    data[0:rows] = mine[0:rows]
-    data[rows : 2 * rows] = other[0:rows]
-    value = (s0[...] + s1[...]) + (other[rows:] + s2[...])
-    data[2 * rows :] = value
-    sums[...] = value
-
-
-def finish_kernel(mine, other, momentum, s0, s1, s2, out, kinetic):
+    sums[...] = jnp.concatenate([total(part) for part in parts] + [jnp.zeros((4, lanes), jnp.float32)], 0)
+
+
+def finish_kernel(d0, d1, d2, d3, momentum, s0, s1, s2, s3, out, kinetic):
     planes, rows, lanes = momentum.shape
     cells = 4.0 * planes * rows * lanes
     shot = lax.axis_index("shot")
-    sums = (s0[...] + s1[...]) + (other[planes // 2 * rows :] + s2[...])
+    sums = (s0[...] + s1[...]) + (s2[...] + s3[...])
     factor = lax.rsqrt(sums[0:1] / cells + EPSILON)
     energy = 0.5 * (sums[1:2] - factor * sums[2:3] + 0.25 * factor * factor * sums[3:4]) / cells
     kinetic[0] = energy[0, 0]
     step = 0.5 * factor
-    quarter = planes // 4
-    for part, group in ((mine, shot), (other, flip(shot, 1))):
-        for number, first in enumerate((first_plane(group, planes), first_plane(flip(group, 2), planes))):
-            for j in range(quarter):
-                at = (number * quarter + j) * rows
-                out[first + j] = momentum[first + j] - step * part[at : at + rows]
-
-
-def local(kernel, outs, *arrays, name=None, limit=8):
+    for bits, data in enumerate((d0, d1, d2, d3)):
+        first = first_plane(flip(shot, bits), planes)
+        for j in range(planes // 4):
+            out[first + j] = momentum[first + j] - step * data[j]
+
+
+def local(kernel, outs, *arrays):
     vmem = pl.BlockSpec(memory_space=pltpu.VMEM)
     shapes = [jax.ShapeDtypeStruct(shape, jnp.float32) for shape in outs]
     single = len(outs) == 1
@@ -509,8 +559,8 @@
         in_specs=[vmem] * len(arrays),
         out_specs=vmem if single else [vmem] * len(outs),
         out_shape=shapes[0] if single else shapes,
-        compiler_params=pltpu.CompilerParams(vmem_limit_bytes=limit * 2**20),
-        name=name or kernel.__name__,
+        compiler_params=pltpu.CompilerParams(vmem_limit_bytes=4 * 2**20),
+        name=kernel.__name__,
     )(*arrays)
 
 
@@ -532,36 +582,36 @@
     cells_all = planes_all * rows_x * rows_y
     vmem, smem = pl.BlockSpec(memory_space=pltpu.VMEM), pl.BlockSpec(memory_space=pltpu.SMEM)
 
-    (outgoing,) = pick((fwd_prev, fwd_cur, True))
+    (outgoing,) = pick((fwd_prev, fwd_cur, True), grant=62)
     over = exchange(outgoing, CHIP)
 
-    c0, piece = local(courant_kernel, [courant_sq.shape, (1, rows_x, rows_y)], courant_sq)
+    c0, piece = local(courant_kernel, [courant_sq.shape, (planes // 2, rows_x, rows_y)], courant_sq)
     piece = exchange(piece, CHIP)
     (own,) = pick((fwd_prev, fwd_cur, False))
     mate = exchange(own, CORE)
     c1 = exchange(c0, CORE)
-    quarter = jnp.concatenate([piece] + [exchange(piece, j * NEAR_Z) for j in (1, 2, 3)], 0)
-    other = exchange(quarter, Y)
-    c2 = local(arrange_kernel, [courant_sq.shape], quarter, other)
+    c2 = local(arrange_kernel, [courant_sq.shape], piece, exchange(piece, Y))
     c3 = exchange(c2, CORE)
 
     cells = lax.dynamic_index_in_dim(rec_cells, chip, 0, keepdims=False)
     traces = lax.dynamic_index_in_dim(observed, chip, 0, keepdims=False)
-    placed, mark = scatter(cells, traces, planes_all, rows_x, rows_y)
+    placed, mark, second = scatter(cells, traces, planes_all, rows_x, rows_y)
     placed = placed.reshape(steps + 1, planes_all, rows_x, rows_y)
 
     adj_outgoing, adj_own = pick((adj_next, adj_cur, True), (adj_next, adj_cur, False), after=mark)
+    over, second = lax.optimization_barrier((over, second))
     far = exchange(over, CORE)
     adj_over = exchange(adj_outgoing, CHIP)
     adj_mate = exchange(adj_own, CORE)
 
     scratch = pltpu.VMEM((planes_all + 4, rows_x, rows_y), jnp.float32)
-    band_scratch = pltpu.VMEM((2 * rows_y, rows_y), jnp.bfloat16)
-    params = pltpu.CompilerParams(vmem_limit_bytes=20 * 2**20)
+    y_scratch = pltpu.VMEM((BATCH * rows_x, rows_y), jnp.float32)
+    step_scratch = [scratch, scratch, pltpu.VMEM((2 * rows_y, rows_y), jnp.bfloat16), y_scratch, y_scratch]
+    params = pltpu.CompilerParams(vmem_limit_bytes=6 * 2**20)
     cost = pl.CostEstimate(flops=30 * steps * cells_all, bytes_accessed=16 * steps * cells_all, transcendentals=0)
     laps, inject, cour, mark = pl.pallas_call(
         forward_kernel,
-        in_specs=[smem, smem] + [vmem] * 9,
+        in_specs=[smem, smem, pl.BlockSpec(memory_space=pl.ANY)] + [vmem] * 9,
         out_specs=[vmem] * 4,
         out_shape=[
             jax.ShapeDtypeStruct((steps, planes, 2, rows_x, rows_y), jnp.float32),
@@ -569,45 +619,47 @@
             jax.ShapeDtypeStruct((planes_all, rows_x, rows_y), jnp.float32),
             jax.ShapeDtypeStruct((8, rows_y), jnp.float32),
         ],
-        scratch_shapes=[scratch, scratch, band_scratch],
+        scratch_shapes=step_scratch,
         compiler_params=params,
         cost_estimate=cost,
         name="forward_steps",
-    )(ckpt_step[None], src_cells, own, mate, over, far, c0, c1, c2, c3, placed)
+    )(ckpt_step[None], src_cells, second, own, mate, over, far, c0, c1, c2, c3, placed)
 
     adj_over, mark = lax.optimization_barrier((adj_over, mark))
     adj_far = exchange(adj_over, CORE)
     slab = jax.ShapeDtypeStruct(courant_sq.shape, jnp.float32)
-    keep, send = pl.pallas_call(
+    half, quarter = (planes // 2, rows_x, rows_y), (planes // 4, rows_x, rows_y)
+    keep_a, send_a, keep_b, send_b = pl.pallas_call(
         adjoint_kernel,
         in_specs=[pl.BlockSpec(memory_space=pl.ANY)] + [vmem] * 7,
-        out_specs=[vmem, vmem],
-        out_shape=[slab, slab],
-        scratch_shapes=[scratch, scratch, pltpu.VMEM((2 * planes, rows_x, rows_y), jnp.float32), band_scratch],
+        out_specs=[vmem] * 4,
+        out_shape=[jax.ShapeDtypeStruct(half, jnp.float32)] * 4,
+        scratch_shapes=step_scratch[:2] + [pltpu.VMEM((2 * planes, rows_x, rows_y), jnp.float32)] + step_scratch[2:],
         compiler_params=params,
         cost_estimate=cost,
         name="adjoint_steps",
     )(mark, adj_own, adj_mate, adj_over, adj_far, cour, laps, inject)
 
-    half, quarter = (planes // 2, rows_x, rows_y), (planes // 4, rows_x, rows_y)
-    keep, send = local(functools.partial(halve_kernel, 1), [half] * 2, keep, exchange(send, CHIP), name="halve_y")
-    keep, send = local(functools.partial(halve_kernel, 2), [quarter] * 2, keep, exchange(send, Y), name="halve_z")
+    other_a, other_b = exchange(send_a, CHIP), exchange(send_b, Y)
+    keep_a, send_a, keep_b, send_b = local(cross_kernel, [quarter] * 4, keep_a, other_a, keep_b, other_b)
+    other_a, other_b = exchange(send_a, Y), exchange(send_b, CHIP)
+    keep, send = local(choose_kernel, [quarter] * 2, keep_a, other_a, keep_b, other_b)
     part = local(add_kernel, [quarter], keep, exchange(send, NEAR_Z))
-    rows, sums_shape = planes // 4 * rows_x, (8, rows_y)
-    data, sums = local(sums_kernel, [(rows + 8, rows_y), sums_shape], part, exchange(part, FAR_Z), momentum)
-    received = exchange(data, NEAR_Z)
-    others = [exchange(sums, CORE), exchange(sums, NEAR_Z + CORE)]
-    data, sums = local(join_kernel, [(2 * rows + 8, rows_y), sums_shape], data, received, sums, *others)
-    received = exchange(data, Y)
-    others = [exchange(sums, CHIP), exchange(sums, Y + CHIP)]
+    data, sums = local(sums_kernel, [quarter, (8, rows_y)], part, exchange(part, FAR_Z), momentum)
+
+    planes_back = [data] + [exchange(data, bits) for bits in (NEAR_Z, Y, NEAR_Z + Y)]
+    sums = [sums] + [exchange(sums, bits) for bits in (CORE, CHIP, CORE + CHIP)]
+    sums = local(add_sums_kernel, [(8, rows_y)], *sums)
+    sums = [sums] + [exchange(sums, bits) for bits in (NEAR_Z, Y, NEAR_Z + Y)]
+    back = (0, 2, 1, 3)
     momentum_half, kinetic = pl.pallas_call(
         finish_kernel,
-        in_specs=[vmem] * 6,
+        in_specs=[vmem] * 9,
         out_specs=[vmem, smem],
-        out_shape=[slab, jax.ShapeDtypeStruct((1,), jnp.float32)],
-        compiler_params=pltpu.CompilerParams(vmem_limit_bytes=8 * 2**20),
+        out_shape=[jax.ShapeDtypeStruct(momentum.shape, jnp.float32), jax.ShapeDtypeStruct((1,), jnp.float32)],
+        compiler_params=pltpu.CompilerParams(vmem_limit_bytes=4 * 2**20),
         name="finish",
-    )(data, received, momentum, sums, *others)
+    )(*[planes_back[n] for n in back], momentum, *[sums[n] for n in back])
     return momentum_half, kinetic[0]
 
 

time: 109 us -> 98.9 us (0.907)
  waiting for transfers between devices: 32.6 us -> 24.1 us
  Pallas kernels: 38 us -> 34.1 us
  starting transfers between devices: 25.1 us -> 27.4 us
    ppermute x23 -> x25, waiting for transfers between devices: 32.6 us -> 24.1 us  [exchange(): lax.ppermute(value, axes, [(i, i ^ bits) for i in range(lax.axis_size(axe...]
    pallas_call x1, Pallas kernels: 12.9 us -> 10.2 us  [whole_shards(): pl.pallas_call(adjoint_kernel, in_specs=[pl.BlockSpec(memory_space=pl.ANY...]
    ppermute x23 -> x25, starting transfers between devices: 25.1 us -> 27.4 us  [exchange(): lax.ppermute(value, axes, [(i, i ^ bits) for i in range(lax.axis_size(axe...]
    unnamed x23 -> x20, local copies, waits for them, and re-layouts: 10.4 us -> 10.4 us
  transfers between devices with their start and end apart: 23 -> 25, of which waited for: 12 -> 13; matrix products, arithmetic and copies ran while one was open for 1% -> 1% of each run, Pallas kernels for 21% -> 21%
where the time goes in v5:
time: 98.9 us; the launch traced here: 98.6 us
  Pallas kernels  34.1 us (34%)
  starting transfers between devices  27.4 us (28%)
  waiting for transfers between devices  24.1 us (24%)
  local copies, waits for them, and re-layouts  10.6 us (11%)
  between operations  1.53 us (2%)
    ppermute x25, starting transfers between devices, exchange(): lax.ppermute(value, axes, [(i, i ^ bits) for i in range(lax.axis_size(axe...  27.4 us
    ppermute x25, waiting for transfers between devices, exchange(): lax.ppermute(value, axes, [(i, i ^ bits) for i in range(lax.axis_size(axe...  24.1 us
    pallas_call x1, Pallas kernels, whole_shards(): pl.pallas_call(forward_kernel, in_specs=[smem, smem, pl.BlockSpec(memory_...  11.2 us
    unnamed x20, local copies, waits for them, and re-layouts  10.4 us
    pallas_call x1, Pallas kernels, whole_shards(): pl.pallas_call(adjoint_kernel, in_specs=[pl.BlockSpec(memory_space=pl.ANY...  10.2 us
    pallas_call x1, Pallas kernels, scatter(): pl.pallas_call(scatter_kernel, grid=(rows_all // tile,), in_specs=[pl.Blo...  8.34 us
    pallas_call x3, Pallas kernels, pick(): pl.pallas_call(lambda *refs: plain(*refs[len(marks):]), in_specs=[vmem] *...  3.28 us
  transfers between devices with their start and end apart: 25, of which 13 were waited for; matrix products, arithmetic and copies ran while one was open for 1% of the time, Pallas kernels for 21%

profile of v5, /device:TPU:0, one launch (start us, length us, event | category | flops | bytes accessed | tf_op | source)
XLA Modules:
  0.0 98.6 jit_solution(12661959355089924616)
XLA Ops:
  0.6 0.0 copy-start
  0.6 1.9 %pick.4 = f32[2,8,64,128]{3,2,1,0:T(8,128)} custom-call(f32[2,8,64,128]{3,2,1,0:T(8,128)} %refs_0_.3, f32[2,8,64,128]{3,2,1,0:T(8,128)} %refs_1_.5), custom_call_target="tpu_custom_call" | custom-call | tf_op jit(solution)/shard_map/pick/pallas_call | solution.py:167
  2.6 3.0 %collective-permute-start.1 = (f32[2,8,64,128]{3,2,1,0:T(8,128)}, f32[2,8,64,128]{3,2,1,0:T(8,128)S(1)}, u32[]{:S(2)}, u32[]{:S(2)}) collective-permute-start(f32[2,8,64,128]{3,2,1,0:T(8,128)} %pick.4), channel_id=1, source_target_pairs={{0,2},{1,3},{2,0},{3,1},{4,6},{5,7},{6,4},{7,5},{8,10},{9,11},{10,... | collective-permute-start | bytes 1572872 | tf_op jit(solution)/shard_map/ppermute | solution.py:569
  5.6 0.9 copy-done.8
  6.5 0.1 courant_kernel.1
  6.6 0.1 collective-permute-start.5
  6.7 1.0 %copy-done.3 = f32[2,8,64,128]{3,2,1,0:T(8,128)S(1)} copy-done((f32[2,8,64,128]{3,2,1,0:T(8,128)S(1)}, f32[2,8,64,128]{3,2,1,0:T(8,128)}, u32[]{:S(2)}) %copy-start.3) | copy-done | bytes 524312
  7.8 1.0 %copy-done.4 = f32[2,8,64,128]{3,2,1,0:T(8,128)S(1)} copy-done((f32[2,8,64,128]{3,2,1,0:T(8,128)S(1)}, f32[2,8,64,128]{3,2,1,0:T(8,128)}, u32[]{:S(2)}) %copy-start.4) | copy-done | bytes 524312
  8.8 0.2 pick.5.own
  9.0 0.1 collective-permute-start.2
  9.1 0.7 dynamic-slice_bitcast_fusion
  9.8 0.1 copy.13
  10.0 0.1 add_select_fusion.y_ref
  10.1 0.1 copy.16
  10.2 0.0 copy-start.5
  10.2 0.0 copy-start.6
  10.3 0.0 copy-start.9
  10.3 8.3 %receiver_scatter.1 = (f32[9,2048,128]{2,1,0:T(8,128)S(1)}, f32[8,128]{1,0:T(8,128)S(1)}, f32[8,128]{1,0:T(8,128)S(1)}) custom-call(s32[1,512]{1,0:T(1,128)S(1)} %get-tuple-element.61.row_ref, s32[512,1]{1,0:T(8,128)S(1)} %add_select_fusion.y_ref, f32[512,8]{1,0:T(8,128)S(1)} %bitcast.10), custom_call_target="tpu_custom_call" | custom-call | flops 4831838208 | bytes 9437184 | tf_op jit(solution)/shard_map/receiver_scatter/pallas_call | solution.py:278
  18.6 3.6 %copy-done.1 = f32[9,2048,128]{2,1,0:T(8,128)} copy-done((f32[9,2048,128]{2,1,0:T(8,128)}, f32[9,2048,128]{2,1,0:T(8,128)S(1)}, u32[]{:S(2)}) %copy-start.1) | copy-done | bytes 9437208
  22.3 0.5 collective-permute-start.3
  22.7 1.2 %pick.3 = (f32[2,8,64,128]{3,2,1,0:T(8,128)}, f32[2,8,64,128]{3,2,1,0:T(8,128)S(1)}) custom-call(f32[8,128]{1,0:T(8,128)S(1)} %get-tuple-element.31.refs_0_, f32[2,8,64,128]{3,2,1,0:T(8,128)S(1)} %copy-done.5, f32[2,8,64,128]{3,2,1,0:T(8,128)S(1)} %copy-done.6, f32[2,8,64,128]{3,2,1,0:T(8,128)S(1)} %copy-done.5, f32[2,8,64,128]{3,2,1,0:T(8,128)S(1)} %copy-done.6), custom_call_target="tpu_custom_call" | custom-call | tf_op jit(solution)/shard_map/pick/pallas_call | solution.py:167
  23.9 2.1 %collective-permute-start = (f32[2,8,64,128]{3,2,1,0:T(8,128)}, f32[2,8,64,128]{3,2,1,0:T(8,128)S(1)}, u32[]{:S(2)}, u32[]{:S(2)}) collective-permute-start(f32[2,8,64,128]{3,2,1,0:T(8,128)} %get-tuple-element.32), channel_id=1, source_target_pairs={{0,2},{1,3},{2,0},{3,1},{4,6},{5,7},{6,4},{7,5},{8,10},{9,11},{10,... | collective-permute-start | bytes 1572872 | tf_op jit(solution)/shard_map/ppermute | solution.py:569
  26.0 0.0 collective-permute-done.5.mine
  26.0 1.5 %collective-permute-start.6 = (f32[4,64,128]{2,1,0:T(8,128)S(1)}, f32[4,64,128]{2,1,0:T(8,128)S(1)}, u32[]{:S(2)}, u32[]{:S(2)}) collective-permute-start(f32[4,64,128]{2,1,0:T(8,128)S(1)} %collective-permute-done.5.mine), channel_id=1, source_target_pairs={{0,4},{1,5},{2,6},{3,7},{4,0},{5,1},{6,2},{7,3},{8,12},{9,13},{10,... | collective-permute-start | bytes 393224 | tf_op jit(solution)/shard_map/ppermute | solution.py:569
  27.5 0.0 collective-permute-start.4
  27.5 3.6 %collective-permute-done.6.other = f32[4,64,128]{2,1,0:T(8,128)S(1)} collective-permute-done((f32[4,64,128]{2,1,0:T(8,128)S(1)}, f32[4,64,128]{2,1,0:T(8,128)S(1)}, u32[]{:S(2)}, u32[]{:S(2)}) %collective-permute-start.6) | collective-permute-done | bytes 131104 | tf_op jit(solution)/shard_map/ppermute | solution.py:569
  31.2 0.1 collective-permute-start.7
  31.9 0.6 collective-permute-start.8
  32.5 0.4 collective-permute-done.7.c3
  32.9 0.0 collective-permute-done.2.mate
  32.9 0.0 collective-permute-done.3.far
  33.0 3.7 %copy-done.2 = f32[9,2048,128]{2,1,0:T(8,128)S(1)} copy-done((f32[9,2048,128]{2,1,0:T(8,128)S(1)}, f32[9,2048,128]{2,1,0:T(8,128)}, u32[]{:S(2)}) %copy-start.2) | copy-done | bytes 9437208
  36.6 11.2 %forward_steps.1 = (f32[8,8,2,64,128]{4,3,2,1,0:T(8,128)S(1)}, f32[8,32,64,128]{3,2,1,0:T(8,128)S(1)}, f32[32,64,128]{2,1,0:T(8,128)S(1)}, f32[8,128]{1,0:T(8,128)S(1)}) custom-call(s32[1]{0:T(128)} %bitcast.8.start, s32[2]{0:T(128)S(1)} %copy-done.9, f32[8,128]{1,0:T(8,128)S(1)} %get-tuple-element.34.scattered, f32[2,8,64,128]{3,2,1,0:T(8,128)S(1)} %pick.5.own, ...), custom_call_target="tpu_custom_call" | custom-call | flops 62914560 | bytes 33554432 | tf_op jit(solution)/shard_map/forward_steps/pallas_call | solution.py:612
  47.8 0.0 copy-start.7
  47.8 0.2 collective-permute-start.9
  48.0 1.8 %collective-permute-done.9.far = f32[2,8,64,128]{3,2,1,0:T(8,128)S(1)} collective-permute-done((f32[2,8,64,128]{3,2,1,0:T(8,128)S(1)}, f32[2,8,64,128]{3,2,1,0:T(8,128)S(1)}, u32[]{:S(2)}, u32[]{:S(2)}) %collective-permute-start.9) | collective-permute-done | bytes 524320 | tf_op jit(solution)/shard_map/ppermute | solution.py:569
  49.8 10.2 %adjoint_steps.1 = (f32[4,64,128]{2,1,0:T(8,128)S(1)}, f32[4,64,128]{2,1,0:T(8,128)S(1)}, f32[4,64,128]{2,1,0:T(8,128)S(1)}, f32[4,64,128]{2,1,0:T(8,128)S(1)}) custom-call(f32[8,128]{1,0:T(8,128)S(1)} %get-tuple-element.40.mark, f32[2,8,64,128]{3,2,1,0:T(8,128)S(1)} %get-tuple-element.41.own, f32[2,8,64,128]{3,2,1,0:T(8,128)S(1)} %collective-permute-done.8.mate, ...), custom_call_target="tpu_custom_call" | custom-call | flops 62914560 | bytes 33554432 | tf_op jit(solution)/shard_map/adjoint_steps/pallas_call | solution.py:632
  60.1 0.4 collective-permute-start.10
  60.5 1.7 %collective-permute-start.11 = (f32[4,64,128]{2,1,0:T(8,128)S(1)}, f32[4,64,128]{2,1,0:T(8,128)S(1)}, u32[]{:S(2)}, u32[]{:S(2)}) collective-permute-start(f32[4,64,128]{2,1,0:T(8,128)S(1)} %get-tuple-element.49), channel_id=1, source_target_pairs={{0,4},{1,5},{2,6},{3,7},{4,0},{5,1},{6,2},{7,3},{8,12},{9,13},{10,... | collective-permute-start | bytes 393224 | tf_op jit(solution)/shard_map/ppermute | solution.py:569
  62.2 3.5 %collective-permute-done.10.other_a = f32[4,64,128]{2,1,0:T(8,128)S(1)} collective-permute-done((f32[4,64,128]{2,1,0:T(8,128)S(1)}, f32[4,64,128]{2,1,0:T(8,128)S(1)}, u32[]{:S(2)}, u32[]{:S(2)}) %collective-permute-start.10) | collective-permute-done | bytes 131104 | tf_op jit(solution)/shard_map/ppermute | solution.py:569
  65.7 0.1 collective-permute-done.11.other_b
  65.8 1.8 %collective-permute-start.12 = (f32[2,64,128]{2,1,0:T(8,128)S(1)}, f32[2,64,128]{2,1,0:T(8,128)S(1)}, u32[]{:S(2)}, u32[]{:S(2)}) collective-permute-start(f32[2,64,128]{2,1,0:T(8,128)S(1)} %get-tuple-element.51), channel_id=1, source_target_pairs={{0,4},{1,5},{2,6},{3,7},{4,0},{5,1},{6,2},{7,3},{8,12},{9,13},{10,... | collective-permute-start | bytes 196616 | tf_op jit(solution)/shard_map/ppermute | solution.py:569
  67.5 1.5 %collective-permute-start.13 = (f32[2,64,128]{2,1,0:T(8,128)S(1)}, f32[2,64,128]{2,1,0:T(8,128)S(1)}, u32[]{:S(2)}, u32[]{:S(2)}) collective-permute-start(f32[2,64,128]{2,1,0:T(8,128)S(1)} %get-tuple-element.53), channel_id=1, source_target_pairs={{0,2},{1,3},{2,0},{3,1},{4,6},{5,7},{6,4},{7,5},{8,10},{9,11},{10,... | collective-permute-start | bytes 196616 | tf_op jit(solution)/shard_map/ppermute | solution.py:569
  69.0 1.1 %collective-permute-done.12.other_a = f32[2,64,128]{2,1,0:T(8,128)S(1)} collective-permute-done((f32[2,64,128]{2,1,0:T(8,128)S(1)}, f32[2,64,128]{2,1,0:T(8,128)S(1)}, u32[]{:S(2)}, u32[]{:S(2)}) %collective-permute-start.12) | collective-permute-done | bytes 65568 | tf_op jit(solution)/shard_map/ppermute | solution.py:569
  70.1 1.7 %collective-permute-done.13.other_b = f32[2,64,128]{2,1,0:T(8,128)S(1)} collective-permute-done((f32[2,64,128]{2,1,0:T(8,128)S(1)}, f32[2,64,128]{2,1,0:T(8,128)S(1)}, u32[]{:S(2)}, u32[]{:S(2)}) %collective-permute-start.13) | collective-permute-done | bytes 65568 | tf_op jit(solution)/shard_map/ppermute | solution.py:569
  71.8 1.7 %collective-permute-start.14 = (f32[2,64,128]{2,1,0:T(8,128)S(1)}, f32[2,64,128]{2,1,0:T(8,128)S(1)}, u32[]{:S(2)}, u32[]{:S(2)}) collective-permute-start(f32[2,64,128]{2,1,0:T(8,128)S(1)} %get-tuple-element.55), channel_id=1, source_target_pairs={{0,8},{1,9},{2,10},{3,11},{4,12},{5,13},{6,14},{7,15},{8,0},{9,1},... | collective-permute-start | bytes 196616 | tf_op jit(solution)/shard_map/ppermute | solution.py:569
  73.5 2.7 %collective-permute-done.14.other = f32[2,64,128]{2,1,0:T(8,128)S(1)} collective-permute-done((f32[2,64,128]{2,1,0:T(8,128)S(1)}, f32[2,64,128]{2,1,0:T(8,128)S(1)}, u32[]{:S(2)}, u32[]{:S(2)}) %collective-permute-start.14) | collective-permute-done | bytes 65568 | tf_op jit(solution)/shard_map/ppermute | solution.py:569
  76.2 3.3 %collective-permute-start.15 = (f32[2,64,128]{2,1,0:T(8,128)S(1)}, f32[2,64,128]{2,1,0:T(8,128)S(1)}, u32[]{:S(2)}, u32[]{:S(2)}) collective-permute-start(f32[2,64,128]{2,1,0:T(8,128)S(1)} %add_kernel.1.mine), channel_id=1, source_target_pairs={{0,16},{1,17},{2,18},{3,19},{4,20},{5,21},{6,22},{7,23},{8,24},{9,... | collective-permute-start | bytes 196616 | tf_op jit(solution)/shard_map/ppermute | solution.py:569
  79.5 2.4 %collective-permute-done.15.other = f32[2,64,128]{2,1,0:T(8,128)S(1)} collective-permute-done((f32[2,64,128]{2,1,0:T(8,128)S(1)}, f32[2,64,128]{2,1,0:T(8,128)S(1)}, u32[]{:S(2)}, u32[]{:S(2)}) %collective-permute-start.15) | collective-permute-done | bytes 65568 | tf_op jit(solution)/shard_map/ppermute | solution.py:569
  81.9 0.1 sums_kernel.1
  82.0 0.2 collective-permute-start.16
  82.2 1.5 %collective-permute-start.17 = (f32[2,64,128]{2,1,0:T(8,128)S(1)}, f32[2,64,128]{2,1,0:T(8,128)S(1)}, u32[]{:S(2)}, u32[]{:S(2)}) collective-permute-start(f32[2,64,128]{2,1,0:T(8,128)S(1)} %get-tuple-element.56.d0), channel_id=1, source_target_pairs={{0,8},{1,9},{2,10},{3,11},{4,12},{5,13},{6,14},{7,15},{8,0},{9,1},... | collective-permute-start | bytes 196616 | tf_op jit(solution)/shard_map/ppermute | solution.py:569
  83.6 1.9 %collective-permute-start.18 = (f32[2,64,128]{2,1,0:T(8,128)S(1)}, f32[2,64,128]{2,1,0:T(8,128)S(1)}, u32[]{:S(2)}, u32[]{:S(2)}) collective-permute-start(f32[2,64,128]{2,1,0:T(8,128)S(1)} %get-tuple-element.56.d0), channel_id=1, source_target_pairs={{0,12},{1,13},{2,14},{3,15},{4,8},{5,9},{6,10},{7,11},{8,4},{9,5},... | collective-permute-start | bytes 196616 | tf_op jit(solution)/shard_map/ppermute | solution.py:569
  85.5 1.1 %collective-permute-start.20 = (f32[8,128]{1,0:T(8,128)S(1)}, f32[8,128]{1,0:T(8,128)S(1)}, u32[]{:S(2)}, u32[]{:S(2)}) collective-permute-start(f32[8,128]{1,0:T(8,128)S(1)} %get-tuple-element.57.s0), channel_id=1, source_target_pairs={{0,2},{1,3},{2,0},{3,1},{4,6},{5,7},{6,4},{7,5},{8,10},{9,11},{10,... | collective-permute-start | bytes 12296 | tf_op jit(solution)/shard_map/ppermute | solution.py:569
  86.6 0.0 collective-permute-done.19.s1
  86.7 0.9 collective-permute-start.21
  87.6 1.5 %collective-permute-done.20.s2 = f32[8,128]{1,0:T(8,128)S(1)} collective-permute-done((f32[8,128]{1,0:T(8,128)S(1)}, f32[8,128]{1,0:T(8,128)S(1)}, u32[]{:S(2)}, u32[]{:S(2)}) %collective-permute-start.20) | collective-permute-done | bytes 4128 | tf_op jit(solution)/shard_map/ppermute | solution.py:569
  89.1 0.6 collective-permute-done.21.s3
  89.7 0.6 collective-permute-start.22
  90.3 1.3 %collective-permute-start.23 = (f32[8,128]{1,0:T(8,128)S(1)}, f32[8,128]{1,0:T(8,128)S(1)}, u32[]{:S(2)}, u32[]{:S(2)}) collective-permute-start(f32[8,128]{1,0:T(8,128)S(1)} %add_sums_kernel.1.s0), channel_id=1, source_target_pairs={{0,8},{1,9},{2,10},{3,11},{4,12},{5,13},{6,14},{7,15},{8,0},{9,1},... | collective-permute-start | bytes 12296 | tf_op jit(solution)/shard_map/ppermute | solution.py:569
  91.7 1.6 %collective-permute-done.22.s1 = f32[8,128]{1,0:T(8,128)S(1)} collective-permute-done((f32[8,128]{1,0:T(8,128)S(1)}, f32[8,128]{1,0:T(8,128)S(1)}, u32[]{:S(2)}, u32[]{:S(2)}) %collective-permute-start.22) | collective-permute-done | bytes 4128 | tf_op jit(solution)/shard_map/ppermute | solution.py:569
  93.3 1.4 %collective-permute-start.24 = (f32[8,128]{1,0:T(8,128)S(1)}, f32[8,128]{1,0:T(8,128)S(1)}, u32[]{:S(2)}, u32[]{:S(2)}) collective-permute-start(f32[8,128]{1,0:T(8,128)S(1)} %add_sums_kernel.1.s0), channel_id=1, source_target_pairs={{0,12},{1,13},{2,14},{3,15},{4,8},{5,9},{6,10},{7,11},{8,4},{9,5},... | collective-permute-start | bytes 12296 | tf_op jit(solution)/shard_map/ppermute | solution.py:569
  94.7 3.1 %collective-permute-done.24.s3 = f32[8,128]{1,0:T(8,128)S(1)} collective-permute-done((f32[8,128]{1,0:T(8,128)S(1)}, f32[8,128]{1,0:T(8,128)S(1)}, u32[]{:S(2)}, u32[]{:S(2)}) %collective-permute-start.24) | collective-permute-done | bytes 4128 | tf_op jit(solution)/shard_map/ppermute | solution.py:569
  97.8 0.8 finish.1
  (25 shorter events, 0.2 us)
Async XLA Ops:
  0.6 9.4 %copy-start = (f32[2,8,512]{2,1,0:T(8,128)S(1)}, f32[2,8,512]{2,1,0:T(8,128)}, u32[]{:S(2)}) copy-start(f32[2,8,512]{2,1,0:T(8,128)} %param.16) | copy-start | bytes 98308
  2.6 19.7 %collective-permute-start.1 = (f32[2,8,64,128]{3,2,1,0:T(8,128)}, f32[2,8,64,128]{3,2,1,0:T(8,128)S(1)}, u32[]{:S(2)}, u32[]{:S(2)}) collective-permute-start(f32[2,8,64,128]{3,2,1,0:T(8,128)} %pick.4), channel_id=1, source_target_pairs={{0,2},{1,3},{2,0},{3,1},{4,6},{5,7},{6,4},{7,5},{8,10},{9,11},{10,... | collective-permute-start | bytes 1572872 | tf_op jit(solution)/shard_map/ppermute | solution.py:569
  5.6 0.9 copy-start.8
  6.6 19.4 %collective-permute-start.5 = (f32[4,64,128]{2,1,0:T(8,128)S(1)}, f32[4,64,128]{2,1,0:T(8,128)S(1)}, u32[]{:S(2)}, u32[]{:S(2)}) collective-permute-start(f32[4,64,128]{2,1,0:T(8,128)S(1)} %get-tuple-element.37), channel_id=1, source_target_pairs={{0,2},{1,3},{2,0},{3,1},{4,6},{5,7},{6,4},{7,5},{8,10},{9,11},{10,... | collective-permute-start | bytes 393224 | tf_op jit(solution)/shard_map/ppermute | solution.py:569
  6.7 1.0 %copy-start.3 = (f32[2,8,64,128]{3,2,1,0:T(8,128)S(1)}, f32[2,8,64,128]{3,2,1,0:T(8,128)}, u32[]{:S(2)}) copy-start(f32[2,8,64,128]{3,2,1,0:T(8,128)} %refs_0_.3) | copy-start | bytes 1572868
  7.8 1.0 %copy-start.4 = (f32[2,8,64,128]{3,2,1,0:T(8,128)S(1)}, f32[2,8,64,128]{3,2,1,0:T(8,128)}, u32[]{:S(2)}) copy-start(f32[2,8,64,128]{3,2,1,0:T(8,128)} %refs_1_.5) | copy-start | bytes 1572868
  9.0 23.9 %collective-permute-start.2 = (f32[2,8,64,128]{3,2,1,0:T(8,128)S(1)}, f32[2,8,64,128]{3,2,1,0:T(8,128)S(1)}, u32[]{:S(2)}, u32[]{:S(2)}) collective-permute-start(f32[2,8,64,128]{3,2,1,0:T(8,128)S(1)} %pick.5.own), channel_id=1, source_target_pairs={{0,1},{1,0},{2,3},{3,2},{4,5},{5,4},{6,7},{7,6},{8,9},{9,8},{10,11... | collective-permute-start | bytes 1572872 | tf_op jit(solution)/shard_map/ppermute | solution.py:569
  10.2 12.5 %copy-start.5 = (f32[2,8,64,128]{3,2,1,0:T(8,128)S(1)}, f32[2,8,64,128]{3,2,1,0:T(8,128)}, u32[]{:S(2)}) copy-start(f32[2,8,64,128]{3,2,1,0:T(8,128)} %refs_3_.1) | copy-start | bytes 1572868
  10.2 12.5 %copy-start.6 = (f32[2,8,64,128]{3,2,1,0:T(8,128)S(1)}, f32[2,8,64,128]{3,2,1,0:T(8,128)}, u32[]{:S(2)}) copy-start(f32[2,8,64,128]{3,2,1,0:T(8,128)} %refs_4_.1) | copy-start | bytes 1572868
  10.3 22.7 %copy-start.9 = (s32[2]{0:T(128)S(1)}, s32[2]{0:T(128)}, u32[]{:S(2)}) copy-start(s32[2]{0:T(128)} %sources.1) | copy-start | bytes 28
  18.6 3.6 %copy-start.1 = (f32[9,2048,128]{2,1,0:T(8,128)}, f32[9,2048,128]{2,1,0:T(8,128)S(1)}, u32[]{:S(2)}) copy-start(f32[9,2048,128]{2,1,0:T(8,128)S(1)} %get-tuple-element.38) | copy-start | bytes 28311556
  22.3 10.7 %collective-permute-start.3 = (f32[2,8,64,128]{3,2,1,0:T(8,128)S(1)}, f32[2,8,64,128]{3,2,1,0:T(8,128)}, u32[]{:S(2)}, u32[]{:S(2)}) collective-permute-start(f32[2,8,64,128]{3,2,1,0:T(8,128)S(1)} %collective-permute-done.1.over), channel_id=1, source_target_pairs={{0,1},{1,0},{2,3},{3,2},{4,5},{5,4},{6,7},{7,6},{8,9},{9,8},{10,11... | collective-permute-start | bytes 1572872 | tf_op jit(solution)/shard_map/ppermute | solution.py:569
  23.9 23.9 %collective-permute-start = (f32[2,8,64,128]{3,2,1,0:T(8,128)}, f32[2,8,64,128]{3,2,1,0:T(8,128)S(1)}, u32[]{:S(2)}, u32[]{:S(2)}) collective-permute-start(f32[2,8,64,128]{3,2,1,0:T(8,128)} %get-tuple-element.32), channel_id=1, source_target_pairs={{0,2},{1,3},{2,0},{3,1},{4,6},{5,7},{6,4},{7,5},{8,10},{9,11},{10,... | collective-permute-start | bytes 1572872 | tf_op jit(solution)/shard_map/ppermute | solution.py:569
  26.0 5.2 %collective-permute-start.6 = (f32[4,64,128]{2,1,0:T(8,128)S(1)}, f32[4,64,128]{2,1,0:T(8,128)S(1)}, u32[]{:S(2)}, u32[]{:S(2)}) collective-permute-start(f32[4,64,128]{2,1,0:T(8,128)S(1)} %collective-permute-done.5.mine), channel_id=1, source_target_pairs={{0,4},{1,5},{2,6},{3,7},{4,0},{5,1},{6,2},{7,3},{8,12},{9,13},{10,... | collective-permute-start | bytes 393224 | tf_op jit(solution)/shard_map/ppermute | solution.py:569
  27.5 4.4 %collective-permute-start.4 = (f32[8,64,128]{2,1,0:T(8,128)S(1)}, f32[8,64,128]{2,1,0:T(8,128)}, u32[]{:S(2)}, u32[]{:S(2)}) collective-permute-start(f32[8,64,128]{2,1,0:T(8,128)S(1)} %get-tuple-element.36.c0), channel_id=1, source_target_pairs={{0,1},{1,0},{2,3},{3,2},{4,5},{5,4},{6,7},{7,6},{8,9},{9,8},{10,11... | collective-permute-start | bytes 786440 | tf_op jit(solution)/shard_map/ppermute | solution.py:569
  31.2 1.7 %collective-permute-start.7 = (f32[8,64,128]{2,1,0:T(8,128)S(1)}, f32[8,64,128]{2,1,0:T(8,128)}, u32[]{:S(2)}, u32[]{:S(2)}) collective-permute-start(f32[8,64,128]{2,1,0:T(8,128)S(1)} %arrange_kernel.1.c2), channel_id=1, source_target_pairs={{0,1},{1,0},{2,3},{3,2},{4,5},{5,4},{6,7},{7,6},{8,9},{9,8},{10,11... | collective-permute-start | bytes 786440 | tf_op jit(solution)/shard_map/ppermute | solution.py:569
  31.9 16.1 %collective-permute-start.8 = (f32[2,8,64,128]{3,2,1,0:T(8,128)S(1)}, f32[2,8,64,128]{3,2,1,0:T(8,128)S(1)}, u32[]{:S(2)}, u32[]{:S(2)}) collective-permute-start(f32[2,8,64,128]{3,2,1,0:T(8,128)S(1)} %get-tuple-element.41.own), channel_id=1, source_target_pairs={{0,1},{1,0},{2,3},{3,2},{4,5},{5,4},{6,7},{7,6},{8,9},{9,8},{10,11... | collective-permute-start | bytes 1572872 | tf_op jit(solution)/shard_map/ppermute | solution.py:569
  32.9 3.7 %copy-start.2 = (f32[9,2048,128]{2,1,0:T(8,128)S(1)}, f32[9,2048,128]{2,1,0:T(8,128)}, u32[]{:S(2)}) copy-start(f32[9,2048,128]{2,1,0:T(8,128)} %copy-done.1) | copy-start | bytes 28311556
  47.8 34.1 %copy-start.7 = (f32[8,64,128]{2,1,0:T(8,128)S(1)}, f32[8,64,128]{2,1,0:T(8,128)}, u32[]{:S(2)}) copy-start(f32[8,64,128]{2,1,0:T(8,128)} %momentum.3) | copy-start | bytes 786436
  47.8 2.0 %collective-permute-start.9 = (f32[2,8,64,128]{3,2,1,0:T(8,128)S(1)}, f32[2,8,64,128]{3,2,1,0:T(8,128)S(1)}, u32[]{:S(2)}, u32[]{:S(2)}) collective-permute-start(f32[2,8,64,128]{3,2,1,0:T(8,128)S(1)} %collective-permute-done.over), channel_id=1, source_target_pairs={{0,1},{1,0},{2,3},{3,2},{4,5},{5,4},{6,7},{7,6},{8,9},{9,8},{10,11... | collective-permute-start | bytes 1572872 | tf_op jit(solution)/shard_map/ppermute | solution.py:569
  60.1 5.6 %collective-permute-start.10 = (f32[4,64,128]{2,1,0:T(8,128)S(1)}, f32[4,64,128]{2,1,0:T(8,128)S(1)}, u32[]{:S(2)}, u32[]{:S(2)}) collective-permute-start(f32[4,64,128]{2,1,0:T(8,128)S(1)} %get-tuple-element.47), channel_id=1, source_target_pairs={{0,2},{1,3},{2,0},{3,1},{4,6},{5,7},{6,4},{7,5},{8,10},{9,11},{10,... | collective-permute-start | bytes 393224 | tf_op jit(solution)/shard_map/ppermute | solution.py:569
  60.5 5.3 %collective-permute-start.11 = (f32[4,64,128]{2,1,0:T(8,128)S(1)}, f32[4,64,128]{2,1,0:T(8,128)S(1)}, u32[]{:S(2)}, u32[]{:S(2)}) collective-permute-start(f32[4,64,128]{2,1,0:T(8,128)S(1)} %get-tuple-element.49), channel_id=1, source_target_pairs={{0,4},{1,5},{2,6},{3,7},{4,0},{5,1},{6,2},{7,3},{8,12},{9,13},{10,... | collective-permute-start | bytes 393224 | tf_op jit(solution)/shard_map/ppermute | solution.py:569
  65.8 4.3 %collective-permute-start.12 = (f32[2,64,128]{2,1,0:T(8,128)S(1)}, f32[2,64,128]{2,1,0:T(8,128)S(1)}, u32[]{:S(2)}, u32[]{:S(2)}) collective-permute-start(f32[2,64,128]{2,1,0:T(8,128)S(1)} %get-tuple-element.51), channel_id=1, source_target_pairs={{0,4},{1,5},{2,6},{3,7},{4,0},{5,1},{6,2},{7,3},{8,12},{9,13},{10,... | collective-permute-start | bytes 196616 | tf_op jit(solution)/shard_map/ppermute | solution.py:569
  67.5 4.3 %collective-permute-start.13 = (f32[2,64,128]{2,1,0:T(8,128)S(1)}, f32[2,64,128]{2,1,0:T(8,128)S(1)}, u32[]{:S(2)}, u32[]{:S(2)}) collective-permute-start(f32[2,64,128]{2,1,0:T(8,128)S(1)} %get-tuple-element.53), channel_id=1, source_target_pairs={{0,2},{1,3},{2,0},{3,1},{4,6},{5,7},{6,4},{7,5},{8,10},{9,11},{10,... | collective-permute-start | bytes 196616 | tf_op jit(solution)/shard_map/ppermute | solution.py:569
  71.8 4.3 %collective-permute-start.14 = (f32[2,64,128]{2,1,0:T(8,128)S(1)}, f32[2,64,128]{2,1,0:T(8,128)S(1)}, u32[]{:S(2)}, u32[]{:S(2)}) collective-permute-start(f32[2,64,128]{2,1,0:T(8,128)S(1)} %get-tuple-element.55), channel_id=1, source_target_pairs={{0,8},{1,9},{2,10},{3,11},{4,12},{5,13},{6,14},{7,15},{8,0},{9,1},... | collective-permute-start | bytes 196616 | tf_op jit(solution)/shard_map/ppermute | solution.py:569
  76.2 5.7 %collective-permute-start.15 = (f32[2,64,128]{2,1,0:T(8,128)S(1)}, f32[2,64,128]{2,1,0:T(8,128)S(1)}, u32[]{:S(2)}, u32[]{:S(2)}) collective-permute-start(f32[2,64,128]{2,1,0:T(8,128)S(1)} %add_kernel.1.mine), channel_id=1, source_target_pairs={{0,16},{1,17},{2,18},{3,19},{4,20},{5,21},{6,22},{7,23},{8,24},{9,... | collective-permute-start | bytes 196616 | tf_op jit(solution)/shard_map/ppermute | solution.py:569
  82.0 15.8 %collective-permute-start.16 = (f32[2,64,128]{2,1,0:T(8,128)S(1)}, f32[2,64,128]{2,1,0:T(8,128)S(1)}, u32[]{:S(2)}, u32[]{:S(2)}) collective-permute-start(f32[2,64,128]{2,1,0:T(8,128)S(1)} %get-tuple-element.56.d0), channel_id=1, source_target_pairs={{0,4},{1,5},{2,6},{3,7},{4,0},{5,1},{6,2},{7,3},{8,12},{9,13},{10,... | collective-permute-start | bytes 196616 | tf_op jit(solution)/shard_map/ppermute | solution.py:569
  82.2 15.7 %collective-permute-start.17 = (f32[2,64,128]{2,1,0:T(8,128)S(1)}, f32[2,64,128]{2,1,0:T(8,128)S(1)}, u32[]{:S(2)}, u32[]{:S(2)}) collective-permute-start(f32[2,64,128]{2,1,0:T(8,128)S(1)} %get-tuple-element.56.d0), channel_id=1, source_target_pairs={{0,8},{1,9},{2,10},{3,11},{4,12},{5,13},{6,14},{7,15},{8,0},{9,1},... | collective-permute-start | bytes 196616 | tf_op jit(solution)/shard_map/ppermute | solution.py:569
  83.6 14.2 %collective-permute-start.18 = (f32[2,64,128]{2,1,0:T(8,128)S(1)}, f32[2,64,128]{2,1,0:T(8,128)S(1)}, u32[]{:S(2)}, u32[]{:S(2)}) collective-permute-start(f32[2,64,128]{2,1,0:T(8,128)S(1)} %get-tuple-element.56.d0), channel_id=1, source_target_pairs={{0,12},{1,13},{2,14},{3,15},{4,8},{5,9},{6,10},{7,11},{8,4},{9,5},... | collective-permute-start | bytes 196616 | tf_op jit(solution)/shard_map/ppermute | solution.py:569
  85.5 1.2 %collective-permute-start.19 = (f32[8,128]{1,0:T(8,128)S(1)}, f32[8,128]{1,0:T(8,128)S(1)}, u32[]{:S(2)}, u32[]{:S(2)}) collective-permute-start(f32[8,128]{1,0:T(8,128)S(1)} %get-tuple-element.57.s0), channel_id=1, source_target_pairs={{0,1},{1,0},{2,3},{3,2},{4,5},{5,4},{6,7},{7,6},{8,9},{9,8},{10,11... | collective-permute-start | bytes 12296 | tf_op jit(solution)/shard_map/ppermute | solution.py:569
  85.5 3.6 %collective-permute-start.20 = (f32[8,128]{1,0:T(8,128)S(1)}, f32[8,128]{1,0:T(8,128)S(1)}, u32[]{:S(2)}, u32[]{:S(2)}) collective-permute-start(f32[8,128]{1,0:T(8,128)S(1)} %get-tuple-element.57.s0), channel_id=1, source_target_pairs={{0,2},{1,3},{2,0},{3,1},{4,6},{5,7},{6,4},{7,5},{8,10},{9,11},{10,... | collective-permute-start | bytes 12296 | tf_op jit(solution)/shard_map/ppermute | solution.py:569
  86.7 3.0 %collective-permute-start.21 = (f32[8,128]{1,0:T(8,128)S(1)}, f32[8,128]{1,0:T(8,128)S(1)}, u32[]{:S(2)}, u32[]{:S(2)}) collective-permute-start(f32[8,128]{1,0:T(8,128)S(1)} %get-tuple-element.57.s0), channel_id=1, source_target_pairs={{0,3},{1,2},{2,1},{3,0},{4,7},{5,6},{6,5},{7,4},{8,11},{9,10},{10,... | collective-permute-start | bytes 12296 | tf_op jit(solution)/shard_map/ppermute | solution.py:569
  89.7 3.6 %collective-permute-start.22 = (f32[8,128]{1,0:T(8,128)S(1)}, f32[8,128]{1,0:T(8,128)S(1)}, u32[]{:S(2)}, u32[]{:S(2)}) collective-permute-start(f32[8,128]{1,0:T(8,128)S(1)} %add_sums_kernel.1.s0), channel_id=1, source_target_pairs={{0,4},{1,5},{2,6},{3,7},{4,0},{5,1},{6,2},{7,3},{8,12},{9,13},{10,... | collective-permute-start | bytes 12296 | tf_op jit(solution)/shard_map/ppermute | solution.py:569
  90.3 4.4 %collective-permute-start.23 = (f32[8,128]{1,0:T(8,128)S(1)}, f32[8,128]{1,0:T(8,128)S(1)}, u32[]{:S(2)}, u32[]{:S(2)}) collective-permute-start(f32[8,128]{1,0:T(8,128)S(1)} %add_sums_kernel.1.s0), channel_id=1, source_target_pairs={{0,8},{1,9},{2,10},{3,11},{4,12},{5,13},{6,14},{7,15},{8,0},{9,1},... | collective-permute-start | bytes 12296 | tf_op jit(solution)/shard_map/ppermute | solution.py:569
  93.3 4.5 %collective-permute-start.24 = (f32[8,128]{1,0:T(8,128)S(1)}, f32[8,128]{1,0:T(8,128)S(1)}, u32[]{:S(2)}, u32[]{:S(2)}) collective-permute-start(f32[8,128]{1,0:T(8,128)S(1)} %add_sums_kernel.1.s0), channel_id=1, source_target_pairs={{0,12},{1,13},{2,14},{3,15},{4,8},{5,9},{6,10},{7,11},{8,4},{9,5},... | collective-permute-start | bytes 12296 | tf_op jit(solution)/shard_map/ppermute | solution.py:569

commit v6 on v5

--- a/solution.py
+++ b/solution.py
@@ -158,7 +158,7 @@
         interleave(outs[n // 2], (n % 2,), held.at[n])
 
 
-def pick(*pairs, after=None, grant=4):
+def pick(*pairs, after=None, grant=16):
     plain = functools.partial(pick_kernel, tuple(pair[2] for pair in pairs))
     fields = [field for pair in pairs for field in pair[:2]]
     shape = fields[0].shape[1:]
@@ -170,7 +170,7 @@
         out_specs=[vmem] * len(pairs),
         out_shape=[jax.ShapeDtypeStruct((2, *shape), jnp.float32)] * len(pairs),
         scratch_shapes=[pltpu.VMEM((len(fields), *shape), jnp.float32), pltpu.SemaphoreType.DMA((len(fields),))],
-        compiler_params=pltpu.CompilerParams(vmem_limit_bytes=grant * 2**20),
+        compiler_params=pltpu.CompilerParams(vmem_limit_bytes=grant * 2**18),
         name="pick",
     )(*marks, *fields)
 
@@ -192,6 +192,17 @@
     high = whole.astype(jnp.bfloat16)
     low = (whole - high.astype(jnp.float32)).astype(jnp.bfloat16)
     out[...] = jnp.dot(jnp.concatenate([high, low], 1), banded[...], preferred_element_type=jnp.float32)
+
+
+def y_shifts(center):
+    lanes = center.shape[1]
+    lane = lax.broadcasted_iota(jnp.int32, center.shape, 1)
+
+    def shift(by):
+        inside = lane >= by if by > 0 else lane < lanes + by
+        return jnp.where(inside, pltpu.roll(center, by % lanes, 1), 0.0)
+
+    return shift(1) + shift(-1), shift(2) + shift(-2)
 
 
 def laps12(field, z, y_part, fetch, finish):
@@ -225,7 +236,8 @@
                 near = (tile(j, i - 1), tile(j, i + 1), tile(j - 1, i), tile(j + 1, i))
                 far = (tile(j, i - 2), tile(j, i + 2), tile(j - 2, i), tile(j + 2, i))
                 at = (j * groups + i) * 8
-                found.append((center, near, far, y_part[at : at + 8], fetch(j, slice(i * 8, i * 8 + 8))))
+                part = y_shifts(center) if y_part is None else y_part[at : at + 8]
+                found.append((center, near, far, part, fetch(j, slice(i * 8, i * 8 + 8))))
             return found
 
         ready = load(0)
@@ -234,21 +246,39 @@
             for j, (center, near, far, part, extra) in enumerate(ready):
                 near = (near[0] + near[1]) + (near[2] + near[3])
                 far = (far[0] + far[1]) + (far[2] + far[3])
-                finish(base + j, slice(i * 8, i * 8 + 8), center, 16.0 * near + (part - far), extra)
+                if y_part is None:
+                    lap = 16.0 * (near + part[0]) - (far + part[1]) - 90.0 * center
+                else:
+                    lap = 16.0 * near + (part - far)
+                finish(base + j, slice(i * 8, i * 8 + 8), center, lap, extra)
             ready = upcoming
 
 
-def scatter_kernel(row_ref, y_ref, obs_ref, out_ref, mark, second, spread):
-    receivers, steps = obs_ref.shape
+def scatter_kernel(rows_x, cells_ref, observed_ref, out_ref, mark, second, row_ref, spread):
+    _, steps, receivers = observed_ref.shape
     lanes = out_ref.shape[2]
     tile = out_ref.shape[1]
+    groups = rows_x // 8
 
     @pl.when(pl.program_id(0) == 0)
     def _():
-        lane = lax.broadcasted_iota(jnp.int32, (receivers, lanes), 1)
-        at = lane == y_ref[...]
+        chip = lax.axis_index("chip")
+        cells = cells_ref[pl.ds(chip, 1)]
+        x = cells // lanes % rows_x
+        row_ref[...] = cells // (rows_x * lanes) * rows_x + x % groups * 8 + x // groups
+        on_lanes = jnp.concatenate(
+            [
+                observed_ref[chip],
+                jnp.broadcast_to((cells % lanes).astype(jnp.float32), (8, receivers)),
+                jnp.zeros((lanes - steps - 8, receivers), jnp.float32),
+            ],
+            0,
+        )
+        columns = on_lanes.T
+        lane = lax.broadcasted_iota(jnp.int32, (receivers, lanes), 1).astype(jnp.float32)
+        at = lane == columns[:, steps : steps + 1]
         for k in range(steps):
-            column = obs_ref[:, k : k + 1]
+            column = columns[:, k : k + 1]
             high = column.astype(jnp.bfloat16).astype(jnp.float32)
             low = column - high
             cols = pl.ds(k * lanes, lanes)
@@ -267,41 +297,33 @@
         out_ref[k] = total[:, k * lanes : (k + 1) * lanes]
 
 
-def scatter(cells, observed, planes_all, rows_x, rows_y):
-    steps, receivers = observed.shape
-    groups = rows_x // 8
-    x = (cells // rows_y) % rows_x
-    row = (cells // (rows_x * rows_y)) * rows_x + (x % groups) * 8 + x // groups
-    lanes = cells % rows_y
+def scatter(rec_cells, observed, planes_all, rows_x, rows_y):
+    _, steps, receivers = observed.shape
     rows_all = planes_all * rows_x
     tile = 256
+    mark = jax.ShapeDtypeStruct((8, rows_y), jnp.float32)
+    mark_block = pl.BlockSpec((8, rows_y), lambda t: (0, 0))
     return pl.pallas_call(
-        scatter_kernel,
+        functools.partial(scatter_kernel, rows_x),
         grid=(rows_all // tile,),
         in_specs=[
-            pl.BlockSpec((1, receivers), lambda t: (0, 0)),
-            pl.BlockSpec((receivers, 1), lambda t: (0, 0)),
-            pl.BlockSpec((receivers, steps), lambda t: (0, 0)),
+            pl.BlockSpec((2, receivers), lambda t: (0, 0)),
+            pl.BlockSpec((2, steps, receivers), lambda t: (0, 0, 0)),
         ],
-        out_specs=[
-            pl.BlockSpec((steps + 1, tile, rows_y), lambda t: (0, t, 0)),
-            pl.BlockSpec((8, rows_y), lambda t: (0, 0)),
-            pl.BlockSpec((8, rows_y), lambda t: (0, 0)),
+        out_specs=[pl.BlockSpec((steps + 1, tile, rows_y), lambda t: (0, t, 0)), mark_block, mark_block],
+        out_shape=[jax.ShapeDtypeStruct((steps + 1, rows_all, rows_y), jnp.float32), mark, mark],
+        scratch_shapes=[
+            pltpu.VMEM((1, receivers), jnp.int32),
+            pltpu.VMEM((2 * receivers, (steps + 1) * rows_y), jnp.bfloat16),
         ],
-        out_shape=[
-            jax.ShapeDtypeStruct((steps + 1, rows_all, rows_y), jnp.float32),
-            jax.ShapeDtypeStruct((8, rows_y), jnp.float32),
-            jax.ShapeDtypeStruct((8, rows_y), jnp.float32),
-        ],
-        scratch_shapes=[pltpu.VMEM((2 * receivers, (steps + 1) * rows_y), jnp.bfloat16)],
-        compiler_params=pltpu.CompilerParams(vmem_limit_bytes=8 * 2**20),
+        compiler_params=pltpu.CompilerParams(vmem_limit_bytes=56 * 2**20),
         cost_estimate=pl.CostEstimate(
             flops=4 * rows_all * receivers * (steps + 1) * rows_y,
             bytes_accessed=4 * (steps + 1) * rows_all * rows_y,
             transcendentals=0,
         ),
         name="receiver_scatter",
-    )(row[None, :], lanes[:, None], observed.T)
+    )(rec_cells, observed)
 
 
 def place(planes):
@@ -337,26 +359,42 @@
 
     along_y(field, first(*order[0]), banded, y_first)
     for owned in (True, False):
+        for chip in (0, 1):
+            z = first(chip, owned)
+            onward = first(1, owned) if chip == 0 else first(0, False)
+            for n in range(planes // BATCH):
+                last = n == planes // BATCH - 1
+                if not last or chip == 0 or owned:
+                    along_y(field, onward if last else z + (n + 1) * BATCH, banded, parts[(n + 1) % 2])
+                work(z + n * BATCH, parts[n % 2], chip if owned else None, n * BATCH)
+
+
+def sweep_shifts(core, planes, work):
+    for owned in (True, False):
 
         @pl.loop(0, 2)
         def _(chip):
-            z = first(chip, owned)
-            onward = jnp.where(chip == 0, first(1, owned), first(0, False))
-            for n in range(planes // BATCH):
-                last = n == planes // BATCH - 1
-                along_y(field, onward if last else z + (n + 1) * BATCH, banded, parts[(n + 1) % 2])
-                work(z + n * BATCH, parts[n % 2], chip if owned else None, n * BATCH)
+            z = (2 * chip + (core if owned else 1 - core)) * planes
+            for p in range(0, planes, BATCH):
+                work(z + p, None, chip if owned else None, p)
 
 
 def forward_kernel(
-    start, sources, scattered, own, mate, over, far, c0, c1, c2, c3, placed, laps, inject, cour, mark, even, odd, banded, y0, y1
+    start, sources, scattered, own, mate, over, far, c0, c1, c2, c3, placed, laps, inject, cour, mark, even, odd, traces_even, traces_odd, counts, sems
 ):
     planes, rows, lanes = c0.shape
     steps = laps.shape[0]
     groups = rows // 8
     chip_here, core, slabs = place(planes)
     mark[...] = jnp.zeros(mark.shape, jnp.float32)
-    banded[...] = band(lanes)
+
+    def copy(k, slot):
+        return pltpu.make_async_copy(placed.at[k], (traces_even, traces_odd)[slot], sems.at[slot])
+
+    copy(0, 0).start()
+    count_copy = pltpu.make_async_copy(placed.at[steps], counts, sems.at[2])
+    count_copy.start()
+    copy(1, 1).start()
     load_blocks(slabs, (own, mate, over, far), odd, even)
     for slab, block in zip(slabs, (c0, c1, c2, c3)):
 
@@ -372,10 +410,12 @@
     )
     source_slab, source_p = source_z // planes, lax.rem(source_z, planes)
 
-    def advance(k, now, then):
+    def advance(k, now, then, observed, slot):
+        copy(k, slot).wait()
+
         def work(z, y_part, chip, p):
             def fetch(j, rows):
-                return then[z + j + 2, rows], cour[z + j, rows], placed[k, z + j, rows], placed[steps, z + j, rows]
+                return then[z + j + 2, rows], cour[z + j, rows], observed[z + j, rows], counts[z + j, rows]
 
             def finish(j, rows, center, lap, extra):
                 old, speed, traces, count = extra
@@ -387,7 +427,11 @@
 
             laps12(now, z, y_part, fetch, finish)
 
-        sweep(core, planes, now, banded, y0, y1, work)
+        sweep_shifts(core, planes, work)
+
+        @pl.when(k + 2 < steps)
+        def _():
+            copy(k + 2, slot).start()
 
         cycle = (start[0] + k) % 48
         phase = (jnp.full((8, lanes), cycle, jnp.int32).astype(jnp.float32) - 24.0) / 12.0
@@ -400,12 +444,14 @@
 
         moved = cour[source_z, tile, :] * strength
         then[source_z + 2, tile, :] += moved
-        inject[k, source_z, tile, :] -= placed[steps, source_z, tile, :] * moved
+        inject[k, source_z, tile, :] -= counts[source_z, tile, :] * moved
+
+    count_copy.wait()
 
     @pl.loop(0, steps // 2)
     def _(pair):
-        advance(2 * pair, even, odd)
-        advance(2 * pair + 1, odd, even)
+        advance(2 * pair, even, odd, traces_even, 0)
+        advance(2 * pair + 1, odd, even, traces_odd, 1)
 
 
 def adjoint_kernel(mark, own, mate, over, far, cour, laps, inject, keep_a, send_a, keep_b, send_b, even, odd, total, banded, y0, y1):
@@ -489,10 +535,6 @@
     out[...] = mine[...] + other[...]
 
 
-def add_sums_kernel(s0, s1, s2, s3, out):
-    out[...] = (s0[...] + s1[...]) + (s2[...] + s3[...])
-
-
 def flip(index, bits):
     result = index
     for bit in (1, 2):
@@ -520,7 +562,7 @@
     parts = [jnp.zeros((rows, lanes), jnp.float32)] * 4
     for j in range(count):
         scaled = mine[j] + other[j]
-        data[j] = scaled
+        data[j * rows : (j + 1) * rows] = scaled
         z = (2 * chip + core) * planes + first + j
         weight = 1.0 + 2.0 * jnp.full((1, lanes), z, jnp.int32).astype(jnp.float32) / (4 * planes - 1)
         moment = momentum[first + j]
@@ -532,22 +574,35 @@
         by_lane = jnp.sum(value, axis=0, keepdims=True)
         return jnp.broadcast_to(jnp.sum(by_lane, axis=1, keepdims=True), (1, lanes))
 
-    sums[...] = jnp.concatenate([total(part) for part in parts] + [jnp.zeros((4, lanes), jnp.float32)], 0)
-
-
-def finish_kernel(d0, d1, d2, d3, momentum, s0, s1, s2, s3, out, kinetic):
+    value = jnp.concatenate([total(part) for part in parts] + [jnp.zeros((4, lanes), jnp.float32)], 0)
+    data[count * rows :] = value
+    sums[...] = value
+
+
+def join_kernel(mine, other, s0, s1, s2, data, sums):
+    rows = mine.shape[0] - 8
+    data[0:rows] = mine[0:rows]
+    data[rows : 2 * rows] = other[0:rows]
+    value = (s0[...] + s1[...]) + (other[rows:] + s2[...])
+    data[2 * rows :] = value
+    sums[...] = value
+
+
+def finish_kernel(mine, other, momentum, s0, s1, s2, out, kinetic):
     planes, rows, lanes = momentum.shape
     cells = 4.0 * planes * rows * lanes
     shot = lax.axis_index("shot")
-    sums = (s0[...] + s1[...]) + (s2[...] + s3[...])
+    sums = (s0[...] + s1[...]) + (other[planes // 2 * rows :] + s2[...])
     factor = lax.rsqrt(sums[0:1] / cells + EPSILON)
     energy = 0.5 * (sums[1:2] - factor * sums[2:3] + 0.25 * factor * factor * sums[3:4]) / cells
     kinetic[0] = energy[0, 0]
     step = 0.5 * factor
-    for bits, data in enumerate((d0, d1, d2, d3)):
-        first = first_plane(flip(shot, bits), planes)
-        for j in range(planes // 4):
-            out[first + j] = momentum[first + j] - step * data[j]
+    quarter = planes // 4
+    for part, group in ((mine, shot), (other, flip(shot, 1))):
+        for number, first in enumerate((first_plane(group, planes), first_plane(flip(group, 2), planes))):
+            for j in range(quarter):
+                at = (number * quarter + j) * rows
+                out[first + j] = momentum[first + j] - step * part[at : at + rows]
 
 
 def local(kernel, outs, *arrays):
@@ -577,12 +632,11 @@
 ):
     _, planes, rows_x, rows_y = fwd_cur.shape
     steps = observed.shape[1]
-    chip = lax.axis_index("chip")
     planes_all = 4 * planes
     cells_all = planes_all * rows_x * rows_y
     vmem, smem = pl.BlockSpec(memory_space=pltpu.VMEM), pl.BlockSpec(memory_space=pltpu.SMEM)
 
-    (outgoing,) = pick((fwd_prev, fwd_cur, True), grant=62)
+    (outgoing,) = pick((fwd_prev, fwd_cur, True), grant=253)
     over = exchange(outgoing, CHIP)
 
     c0, piece = local(courant_kernel, [courant_sq.shape, (planes // 2, rows_x, rows_y)], courant_sq)
@@ -593,9 +647,7 @@
     c2 = local(arrange_kernel, [courant_sq.shape], piece, exchange(piece, Y))
     c3 = exchange(c2, CORE)
 
-    cells = lax.dynamic_index_in_dim(rec_cells, chip, 0, keepdims=False)
-    traces = lax.dynamic_index_in_dim(observed, chip, 0, keepdims=False)
-    placed, mark, second = scatter(cells, traces, planes_all, rows_x, rows_y)
+    placed, mark, second = scatter(rec_cells, observed, planes_all, rows_x, rows_y)
     placed = placed.reshape(steps + 1, planes_all, rows_x, rows_y)
 
     adj_outgoing, adj_own = pick((adj_next, adj_cur, True), (adj_next, adj_cur, False), after=mark)
@@ -605,13 +657,14 @@
     adj_mate = exchange(adj_own, CORE)
 
     scratch = pltpu.VMEM((planes_all + 4, rows_x, rows_y), jnp.float32)
+    whole = pltpu.VMEM((planes_all, rows_x, rows_y), jnp.float32)
     y_scratch = pltpu.VMEM((BATCH * rows_x, rows_y), jnp.float32)
     step_scratch = [scratch, scratch, pltpu.VMEM((2 * rows_y, rows_y), jnp.bfloat16), y_scratch, y_scratch]
     params = pltpu.CompilerParams(vmem_limit_bytes=6 * 2**20)
     cost = pl.CostEstimate(flops=30 * steps * cells_all, bytes_accessed=16 * steps * cells_all, transcendentals=0)
     laps, inject, cour, mark = pl.pallas_call(
         forward_kernel,
-        in_specs=[smem, smem, pl.BlockSpec(memory_space=pl.ANY)] + [vmem] * 9,
+        in_specs=[smem, smem, pl.BlockSpec(memory_space=pl.ANY)] + [vmem] * 8 + [pl.BlockSpec(memory_space=pltpu.HBM)],
         out_specs=[vmem] * 4,
         out_shape=[
             jax.ShapeDtypeStruct((steps, planes, 2, rows_x, rows_y), jnp.float32),
@@ -619,8 +672,8 @@
             jax.ShapeDtypeStruct((planes_all, rows_x, rows_y), jnp.float32),
             jax.ShapeDtypeStruct((8, rows_y), jnp.float32),
         ],
-        scratch_shapes=step_scratch,
-        compiler_params=params,
+        scratch_shapes=[scratch, scratch, whole, whole, whole, pltpu.SemaphoreType.DMA((3,))],
+        compiler_params=pltpu.CompilerParams(vmem_limit_bytes=33 * 2**20),
         cost_estimate=cost,
         name="forward_steps",
     )(ckpt_step[None], src_cells, second, own, mate, over, far, c0, c1, c2, c3, placed)
@@ -645,21 +698,22 @@
     other_a, other_b = exchange(send_a, Y), exchange(send_b, CHIP)
     keep, send = local(choose_kernel, [quarter] * 2, keep_a, other_a, keep_b, other_b)
     part = local(add_kernel, [quarter], keep, exchange(send, NEAR_Z))
-    data, sums = local(sums_kernel, [quarter, (8, rows_y)], part, exchange(part, FAR_Z), momentum)
-
-    planes_back = [data] + [exchange(data, bits) for bits in (NEAR_Z, Y, NEAR_Z + Y)]
-    sums = [sums] + [exchange(sums, bits) for bits in (CORE, CHIP, CORE + CHIP)]
-    sums = local(add_sums_kernel, [(8, rows_y)], *sums)
-    sums = [sums] + [exchange(sums, bits) for bits in (NEAR_Z, Y, NEAR_Z + Y)]
-    back = (0, 2, 1, 3)
+    rows, sums_shape = planes // 4 * rows_x, (8, rows_y)
+    data, sums = local(sums_kernel, [(rows + 8, rows_y), sums_shape], part, exchange(part, FAR_Z), momentum)
+
+    received = exchange(data, NEAR_Z)
+    others = [exchange(sums, CORE), exchange(sums, NEAR_Z + CORE)]
+    data, sums = local(join_kernel, [(2 * rows + 8, rows_y), sums_shape], data, received, sums, *others)
+    received = exchange(data, Y)
+    others = [exchange(sums, CHIP), exchange(sums, Y + CHIP)]
     momentum_half, kinetic = pl.pallas_call(
         finish_kernel,
-        in_specs=[vmem] * 9,
+        in_specs=[vmem] * 6,
         out_specs=[vmem, smem],
         out_shape=[jax.ShapeDtypeStruct(momentum.shape, jnp.float32), jax.ShapeDtypeStruct((1,), jnp.float32)],
         compiler_params=pltpu.CompilerParams(vmem_limit_bytes=4 * 2**20),
         name="finish",
-    )(*[planes_back[n] for n in back], momentum, *[sums[n] for n in back])
+    )(data, received, momentum, sums, *others)
     return momentum_half, kinetic[0]
 
 

time: 98.9 us -> 89.1 us (0.901)
  local copies, waits for them, and re-layouts: 10.6 us -> 4.4 us
  starting transfers between devices: 27.4 us -> 24 us
  Pallas kernels: 34.1 us -> 36 us
  waiting for transfers between devices: 24.1 us -> 23 us
    unnamed x20 -> x18, local copies, waits for them, and re-layouts: 10.4 us -> 4.4 us
    ppermute x25 -> x22, starting transfers between devices: 27.4 us -> 24 us  [exchange(): lax.ppermute(value, axes, [(i, i ^ bits) for i in range(lax.axis_size(axe...]
    pallas_call x1, Pallas kernels: 10.2 us -> 6.99 us  [whole_shards(): pl.pallas_call(adjoint_kernel, in_specs=[pl.BlockSpec(memory_space=pl.ANY...]
    pallas_call x1, Pallas kernels: 11.2 us -> 13.9 us  [whole_shards(): pl.pallas_call(forward_kernel, in_specs=[smem, smem, pl.BlockSpec(memory_...]
    pallas_call x2, Pallas kernels: 9.12 us -> 10.8 us  [the longest x1 10 us: scatter(): pl.pallas_call(functools.partial(scatter_kernel, rows_x), grid=(rows_all...]
    ppermute x25 -> x22, waiting for transfers between devices: 24.1 us -> 23 us  [exchange(): lax.ppermute(value, axes, [(i, i ^ bits) for i in range(lax.axis_size(axe...]
  transfers between devices with their start and end apart: 25 -> 22, of which waited for: 13 -> 13; matrix products, arithmetic and copies ran while one was open for 1% -> 0% of each run, Pallas kernels for 21% -> 29%
where the time goes in v6:
time: 89.1 us; the launch traced here: 88.8 us
  Pallas kernels  36 us (40%)
  starting transfers between devices  24 us (27%)
  waiting for transfers between devices  23 us (26%)
  local copies, waits for them, and re-layouts  4.4 us (5%)
  between operations  1.44 us (2%)
    ppermute x22, starting transfers between devices, exchange(): lax.ppermute(value, axes, [(i, i ^ bits) for i in range(lax.axis_size(axe...  24 us
    ppermute x22, waiting for transfers between devices, exchange(): lax.ppermute(value, axes, [(i, i ^ bits) for i in range(lax.axis_size(axe...  23 us
    pallas_call x1, Pallas kernels, whole_shards(): pl.pallas_call(forward_kernel, in_specs=[smem, smem, pl.BlockSpec(memory_...  13.9 us
    pallas_call x1, Pallas kernels, scatter(): pl.pallas_call(functools.partial(scatter_kernel, rows_x), grid=(rows_all...  10 us
    pallas_call x1, Pallas kernels, whole_shards(): pl.pallas_call(adjoint_kernel, in_specs=[pl.BlockSpec(memory_space=pl.ANY...  6.99 us
    unnamed x18, local copies, waits for them, and re-layouts  4.4 us
    pallas_call x3, Pallas kernels, pick(): pl.pallas_call(lambda *refs: plain(*refs[len(marks):]), in_specs=[vmem] *...  3.24 us
  transfers between devices with their start and end apart: 22, of which 13 were waited for; matrix products, arithmetic and copies ran while one was open for 0% of the time, Pallas kernels for 29%

profile of v6, /device:TPU:0, one launch (start us, length us, event | category | flops | bytes accessed | tf_op | source)
XLA Modules:
  0.0 88.8 jit_solution(2403527102607769065)
XLA Ops:
  0.6 1.9 %pick.4 = f32[2,8,64,128]{3,2,1,0:T(8,128)} custom-call(f32[2,8,64,128]{3,2,1,0:T(8,128)} %refs_0_.3, f32[2,8,64,128]{3,2,1,0:T(8,128)} %refs_1_.5), custom_call_target="tpu_custom_call" | custom-call | tf_op jit(solution)/shard_map/pick/pallas_call | solution.py:167
  2.5 3.0 %collective-permute-start.1 = (f32[2,8,64,128]{3,2,1,0:T(8,128)}, f32[2,8,64,128]{3,2,1,0:T(8,128)S(1)}, u32[]{:S(2)}, u32[]{:S(2)}) collective-permute-start(f32[2,8,64,128]{3,2,1,0:T(8,128)} %pick.4), channel_id=1, source_target_pairs={{0,2},{1,3},{2,0},{3,1},{4,6},{5,7},{6,4},{7,5},{8,10},{9,11},{10,... | collective-permute-start | bytes 1572872 | tf_op jit(solution)/shard_map/ppermute | solution.py:624
  5.5 0.9 %copy-done.5 = f32[8,64,128]{2,1,0:T(8,128)S(1)} copy-done((f32[8,64,128]{2,1,0:T(8,128)S(1)}, f32[8,64,128]{2,1,0:T(8,128)}, u32[]{:S(2)}) %copy-start.5) | copy-done | bytes 262168
  6.5 0.8 courant_kernel.1
  7.3 0.0 collective-permute-start.5
  7.3 1.0 %copy-done = f32[2,8,64,128]{3,2,1,0:T(8,128)S(1)} copy-done((f32[2,8,64,128]{3,2,1,0:T(8,128)S(1)}, f32[2,8,64,128]{3,2,1,0:T(8,128)}, u32[]{:S(2)}) %copy-start) | copy-done | bytes 524312
  8.3 1.0 %copy-done.1 = f32[2,8,64,128]{3,2,1,0:T(8,128)S(1)} copy-done((f32[2,8,64,128]{3,2,1,0:T(8,128)S(1)}, f32[2,8,64,128]{3,2,1,0:T(8,128)}, u32[]{:S(2)}) %copy-start.1) | copy-done | bytes 524312
  9.4 0.2 pick.5.own
  9.6 0.0 copy-start.2
  9.6 0.0 copy-start.3
  9.6 0.0 copy-start.8
  9.6 0.1 collective-permute-start.2
  9.7 10.0 %receiver_scatter.1 = (f32[9,2048,128]{2,1,0:T(8,128)}, f32[8,128]{1,0:T(8,128)}, f32[8,128]{1,0:T(8,128)}) custom-call(s32[2,512]{1,0:T(2,128)} %cells_ref.1, f32[2,8,512]{2,1,0:T(8,128)} %observed_ref.1), custom_call_target="tpu_custom_call" | custom-call | flops 4831838208 | bytes 9437184 | tf_op jit(solution)/shard_map/receiver_scatter/pallas_call | solution.py:306
  19.7 0.0 collective-permute-done.1.over
  19.7 0.5 collective-permute-start.3
  20.2 0.0 copy-done.2
  20.2 0.0 copy-done.3
  20.2 0.7 copy-done.7
  20.9 1.2 %pick.3 = (f32[2,8,64,128]{3,2,1,0:T(8,128)}, f32[2,8,64,128]{3,2,1,0:T(8,128)S(1)}) custom-call(f32[8,128]{1,0:T(8,128)S(1)} %copy-done.7, f32[2,8,64,128]{3,2,1,0:T(8,128)S(1)} %copy-done.2, f32[2,8,64,128]{3,2,1,0:T(8,128)S(1)} %copy-done.3, f32[2,8,64,128]{3,2,1,0:T(8,128)S(1)} %copy-done.2, f32[2,8,64,128]{3,2,1,0:T(8,128)S(1)} %copy-done.3), custom_call_target="tpu_custom_call" | custom-call | tf_op jit(solution)/shard_map/pick/pallas_call | solution.py:167
  22.0 2.1 %collective-permute-start = (f32[2,8,64,128]{3,2,1,0:T(8,128)}, f32[2,8,64,128]{3,2,1,0:T(8,128)S(1)}, u32[]{:S(2)}, u32[]{:S(2)}) collective-permute-start(f32[2,8,64,128]{3,2,1,0:T(8,128)} %get-tuple-element.34), channel_id=1, source_target_pairs={{0,2},{1,3},{2,0},{3,1},{4,6},{5,7},{6,4},{7,5},{8,10},{9,11},{10,... | collective-permute-start | bytes 1572872 | tf_op jit(solution)/shard_map/ppermute | solution.py:624
  24.1 0.0 collective-permute-done.5.mine
  24.1 1.5 %collective-permute-start.6 = (f32[4,64,128]{2,1,0:T(8,128)S(1)}, f32[4,64,128]{2,1,0:T(8,128)S(1)}, u32[]{:S(2)}, u32[]{:S(2)}) collective-permute-start(f32[4,64,128]{2,1,0:T(8,128)S(1)} %collective-permute-done.5.mine), channel_id=1, source_target_pairs={{0,4},{1,5},{2,6},{3,7},{4,0},{5,1},{6,2},{7,3},{8,12},{9,13},{10,... | collective-permute-start | bytes 393224 | tf_op jit(solution)/shard_map/ppermute | solution.py:624
  25.6 0.0 collective-permute-start.4
  25.6 3.7 %collective-permute-done.6.other = f32[4,64,128]{2,1,0:T(8,128)S(1)} collective-permute-done((f32[4,64,128]{2,1,0:T(8,128)S(1)}, f32[4,64,128]{2,1,0:T(8,128)S(1)}, u32[]{:S(2)}, u32[]{:S(2)}) %collective-permute-start.6) | collective-permute-done | bytes 131104 | tf_op jit(solution)/shard_map/ppermute | solution.py:624
  29.4 0.1 collective-permute-start.7
  30.1 0.0 collective-permute-done.4.c1
  30.1 0.6 collective-permute-start.8
  30.7 0.4 collective-permute-done.7.c3
  31.1 0.0 collective-permute-done.2.mate
  31.1 0.0 collective-permute-done.3.far
  31.1 0.7 copy-done.6
  31.8 13.9 %forward_steps.1 = (f32[8,8,2,64,128]{4,3,2,1,0:T(8,128)S(1)}, f32[8,32,64,128]{3,2,1,0:T(8,128)S(1)}, f32[32,64,128]{2,1,0:T(8,128)S(1)}, f32[8,128]{1,0:T(8,128)S(1)}) custom-call(s32[1]{0:T(128)} %bitcast.3.start, s32[2]{0:T(128)S(1)} %copy-done.8, f32[8,128]{1,0:T(8,128)S(1)} %copy-done.6, f32[2,8,64,128]{3,2,1,0:T(8,128)S(1)} %pick.5.own, ...), custom_call_target="tpu_custom_call" | custom-call | flops 62914560 | bytes 33554432 | tf_op jit(solution)/shard_map/forward_steps/pallas_call | solution.py:665
  45.7 0.0 copy-start.4
  45.7 0.0 collective-permute-done.over
  45.7 0.2 collective-permute-start.9
  45.9 0.0 collective-permute-done.8.mate
  45.9 1.8 %collective-permute-done.9.far = f32[2,8,64,128]{3,2,1,0:T(8,128)S(1)} collective-permute-done((f32[2,8,64,128]{3,2,1,0:T(8,128)S(1)}, f32[2,8,64,128]{3,2,1,0:T(8,128)S(1)}, u32[]{:S(2)}, u32[]{:S(2)}) %collective-permute-start.9) | collective-permute-done | bytes 524320 | tf_op jit(solution)/shard_map/ppermute | solution.py:624
  47.7 7.0 %adjoint_steps.1 = (f32[4,64,128]{2,1,0:T(8,128)S(1)}, f32[4,64,128]{2,1,0:T(8,128)S(1)}, f32[4,64,128]{2,1,0:T(8,128)S(1)}, f32[4,64,128]{2,1,0:T(8,128)S(1)}) custom-call(f32[8,128]{1,0:T(8,128)S(1)} %get-tuple-element.42.mark, f32[2,8,64,128]{3,2,1,0:T(8,128)S(1)} %get-tuple-element.43.own, f32[2,8,64,128]{3,2,1,0:T(8,128)S(1)} %collective-permute-done.8.mate, ...), custom_call_target="tpu_custom_call" | custom-call | flops 62914560 | bytes 33554432 | tf_op jit(solution)/shard_map/adjoint_steps/pallas_call | solution.py:685
  54.7 0.4 collective-permute-start.10
  55.2 1.7 %collective-permute-start.11 = (f32[4,64,128]{2,1,0:T(8,128)S(1)}, f32[4,64,128]{2,1,0:T(8,128)S(1)}, u32[]{:S(2)}, u32[]{:S(2)}) collective-permute-start(f32[4,64,128]{2,1,0:T(8,128)S(1)} %get-tuple-element.51), channel_id=1, source_target_pairs={{0,4},{1,5},{2,6},{3,7},{4,0},{5,1},{6,2},{7,3},{8,12},{9,13},{10,... | collective-permute-start | bytes 393224 | tf_op jit(solution)/shard_map/ppermute | solution.py:624
  56.8 3.5 %collective-permute-done.10.other_a = f32[4,64,128]{2,1,0:T(8,128)S(1)} collective-permute-done((f32[4,64,128]{2,1,0:T(8,128)S(1)}, f32[4,64,128]{2,1,0:T(8,128)S(1)}, u32[]{:S(2)}, u32[]{:S(2)}) %collective-permute-start.10) | collective-permute-done | bytes 131104 | tf_op jit(solution)/shard_map/ppermute | solution.py:624
  60.3 0.1 collective-permute-done.11.other_b
  60.4 1.8 %collective-permute-start.12 = (f32[2,64,128]{2,1,0:T(8,128)S(1)}, f32[2,64,128]{2,1,0:T(8,128)S(1)}, u32[]{:S(2)}, u32[]{:S(2)}) collective-permute-start(f32[2,64,128]{2,1,0:T(8,128)S(1)} %get-tuple-element.53), channel_id=1, source_target_pairs={{0,4},{1,5},{2,6},{3,7},{4,0},{5,1},{6,2},{7,3},{8,12},{9,13},{10,... | collective-permute-start | bytes 196616 | tf_op jit(solution)/shard_map/ppermute | solution.py:624
  62.2 1.5 %collective-permute-start.13 = (f32[2,64,128]{2,1,0:T(8,128)S(1)}, f32[2,64,128]{2,1,0:T(8,128)S(1)}, u32[]{:S(2)}, u32[]{:S(2)}) collective-permute-start(f32[2,64,128]{2,1,0:T(8,128)S(1)} %get-tuple-element.55), channel_id=1, source_target_pairs={{0,2},{1,3},{2,0},{3,1},{4,6},{5,7},{6,4},{7,5},{8,10},{9,11},{10,... | collective-permute-start | bytes 196616 | tf_op jit(solution)/shard_map/ppermute | solution.py:624
  63.7 1.1 %collective-permute-done.12.other_a = f32[2,64,128]{2,1,0:T(8,128)S(1)} collective-permute-done((f32[2,64,128]{2,1,0:T(8,128)S(1)}, f32[2,64,128]{2,1,0:T(8,128)S(1)}, u32[]{:S(2)}, u32[]{:S(2)}) %collective-permute-start.12) | collective-permute-done | bytes 65568 | tf_op jit(solution)/shard_map/ppermute | solution.py:624
  64.8 1.7 %collective-permute-done.13.other_b = f32[2,64,128]{2,1,0:T(8,128)S(1)} collective-permute-done((f32[2,64,128]{2,1,0:T(8,128)S(1)}, f32[2,64,128]{2,1,0:T(8,128)S(1)}, u32[]{:S(2)}, u32[]{:S(2)}) %collective-permute-start.13) | collective-permute-done | bytes 65568 | tf_op jit(solution)/shard_map/ppermute | solution.py:624
  66.5 1.6 %collective-permute-start.14 = (f32[2,64,128]{2,1,0:T(8,128)S(1)}, f32[2,64,128]{2,1,0:T(8,128)S(1)}, u32[]{:S(2)}, u32[]{:S(2)}) collective-permute-start(f32[2,64,128]{2,1,0:T(8,128)S(1)} %get-tuple-element.57), channel_id=1, source_target_pairs={{0,8},{1,9},{2,10},{3,11},{4,12},{5,13},{6,14},{7,15},{8,0},{9,1},... | collective-permute-start | bytes 196616 | tf_op jit(solution)/shard_map/ppermute | solution.py:624
  68.1 2.7 %collective-permute-done.14.other = f32[2,64,128]{2,1,0:T(8,128)S(1)} collective-permute-done((f32[2,64,128]{2,1,0:T(8,128)S(1)}, f32[2,64,128]{2,1,0:T(8,128)S(1)}, u32[]{:S(2)}, u32[]{:S(2)}) %collective-permute-start.14) | collective-permute-done | bytes 65568 | tf_op jit(solution)/shard_map/ppermute | solution.py:624
  70.8 3.3 %collective-permute-start.15 = (f32[2,64,128]{2,1,0:T(8,128)S(1)}, f32[2,64,128]{2,1,0:T(8,128)S(1)}, u32[]{:S(2)}, u32[]{:S(2)}) collective-permute-start(f32[2,64,128]{2,1,0:T(8,128)S(1)} %add_kernel.1.mine), channel_id=1, source_target_pairs={{0,16},{1,17},{2,18},{3,19},{4,20},{5,21},{6,22},{7,23},{8,24},{9,... | collective-permute-start | bytes 196616 | tf_op jit(solution)/shard_map/ppermute | solution.py:624
  74.1 2.2 %collective-permute-done.15.other = f32[2,64,128]{2,1,0:T(8,128)S(1)} collective-permute-done((f32[2,64,128]{2,1,0:T(8,128)S(1)}, f32[2,64,128]{2,1,0:T(8,128)S(1)}, u32[]{:S(2)}, u32[]{:S(2)}) %collective-permute-start.15) | collective-permute-done | bytes 65568 | tf_op jit(solution)/shard_map/ppermute | solution.py:624
  76.4 0.1 sums_kernel.1
  76.5 1.6 %collective-permute-start.16 = (f32[136,128]{1,0:T(8,128)S(1)}, f32[136,128]{1,0:T(8,128)S(1)}, u32[]{:S(2)}, u32[]{:S(2)}) collective-permute-start(f32[136,128]{1,0:T(8,128)S(1)} %get-tuple-element.58.mine), channel_id=1, source_target_pairs={{0,8},{1,9},{2,10},{3,11},{4,12},{5,13},{6,14},{7,15},{8,0},{9,1},... | collective-permute-start | bytes 208904 | tf_op jit(solution)/shard_map/ppermute | solution.py:624
  78.1 0.0 collective-permute-start.17
  78.1 0.6 collective-permute-start.18
  78.7 0.6 collective-permute-done.17.s1
  79.2 1.9 %collective-permute-done.18.s2 = f32[8,128]{1,0:T(8,128)S(1)} collective-permute-done((f32[8,128]{1,0:T(8,128)S(1)}, f32[8,128]{1,0:T(8,128)S(1)}, u32[]{:S(2)}, u32[]{:S(2)}) %collective-permute-start.18) | collective-permute-done | bytes 4128 | tf_op jit(solution)/shard_map/ppermute | solution.py:624
  81.1 0.0 collective-permute-done.16.other
  81.1 0.8 collective-permute-start.19
  81.9 1.5 %collective-permute-start.20 = (f32[8,128]{1,0:T(8,128)S(1)}, f32[8,128]{1,0:T(8,128)S(1)}, u32[]{:S(2)}, u32[]{:S(2)}) collective-permute-start(f32[8,128]{1,0:T(8,128)S(1)} %get-tuple-element.61.s0), channel_id=1, source_target_pairs={{0,2},{1,3},{2,0},{3,1},{4,6},{5,7},{6,4},{7,5},{8,10},{9,11},{10,... | collective-permute-start | bytes 12296 | tf_op jit(solution)/shard_map/ppermute | solution.py:624
  83.5 1.2 %collective-permute-start.21 = (f32[8,128]{1,0:T(8,128)S(1)}, f32[8,128]{1,0:T(8,128)S(1)}, u32[]{:S(2)}, u32[]{:S(2)}) collective-permute-start(f32[8,128]{1,0:T(8,128)S(1)} %get-tuple-element.61.s0), channel_id=1, source_target_pairs={{0,6},{1,7},{2,4},{3,5},{4,2},{5,3},{6,0},{7,1},{8,14},{9,15},{10,... | collective-permute-start | bytes 12296 | tf_op jit(solution)/shard_map/ppermute | solution.py:624
  84.7 0.9 collective-permute-done.20.s1
  85.5 2.4 %collective-permute-done.21.s2 = f32[8,128]{1,0:T(8,128)S(1)} collective-permute-done((f32[8,128]{1,0:T(8,128)S(1)}, f32[8,128]{1,0:T(8,128)S(1)}, u32[]{:S(2)}, u32[]{:S(2)}) %collective-permute-start.21) | collective-permute-done | bytes 4128 | tf_op jit(solution)/shard_map/ppermute | solution.py:624
  88.0 0.0 collective-permute-done.19.other
  88.0 0.8 finish.1
  (12 shorter events, 0.1 us)
Async XLA Ops:
  2.5 17.2 %collective-permute-start.1 = (f32[2,8,64,128]{3,2,1,0:T(8,128)}, f32[2,8,64,128]{3,2,1,0:T(8,128)S(1)}, u32[]{:S(2)}, u32[]{:S(2)}) collective-permute-start(f32[2,8,64,128]{3,2,1,0:T(8,128)} %pick.4), channel_id=1, source_target_pairs={{0,2},{1,3},{2,0},{3,1},{4,6},{5,7},{6,4},{7,5},{8,10},{9,11},{10,... | collective-permute-start | bytes 1572872 | tf_op jit(solution)/shard_map/ppermute | solution.py:624
  5.5 0.9 %copy-start.5 = (f32[8,64,128]{2,1,0:T(8,128)S(1)}, f32[8,64,128]{2,1,0:T(8,128)}, u32[]{:S(2)}) copy-start(f32[8,64,128]{2,1,0:T(8,128)} %courant.1) | copy-start | bytes 786436
  7.3 16.8 %collective-permute-start.5 = (f32[4,64,128]{2,1,0:T(8,128)S(1)}, f32[4,64,128]{2,1,0:T(8,128)S(1)}, u32[]{:S(2)}, u32[]{:S(2)}) collective-permute-start(f32[4,64,128]{2,1,0:T(8,128)S(1)} %get-tuple-element.39), channel_id=1, source_target_pairs={{0,2},{1,3},{2,0},{3,1},{4,6},{5,7},{6,4},{7,5},{8,10},{9,11},{10,... | collective-permute-start | bytes 393224 | tf_op jit(solution)/shard_map/ppermute | solution.py:624
  7.3 1.0 %copy-start = (f32[2,8,64,128]{3,2,1,0:T(8,128)S(1)}, f32[2,8,64,128]{3,2,1,0:T(8,128)}, u32[]{:S(2)}) copy-start(f32[2,8,64,128]{3,2,1,0:T(8,128)} %refs_0_.3) | copy-start | bytes 1572868
  8.3 1.0 %copy-start.1 = (f32[2,8,64,128]{3,2,1,0:T(8,128)S(1)}, f32[2,8,64,128]{3,2,1,0:T(8,128)}, u32[]{:S(2)}) copy-start(f32[2,8,64,128]{3,2,1,0:T(8,128)} %refs_1_.5) | copy-start | bytes 1572868
  9.6 10.6 %copy-start.2 = (f32[2,8,64,128]{3,2,1,0:T(8,128)S(1)}, f32[2,8,64,128]{3,2,1,0:T(8,128)}, u32[]{:S(2)}) copy-start(f32[2,8,64,128]{3,2,1,0:T(8,128)} %refs_3_.1) | copy-start | bytes 1572868
  9.6 10.6 %copy-start.3 = (f32[2,8,64,128]{3,2,1,0:T(8,128)S(1)}, f32[2,8,64,128]{3,2,1,0:T(8,128)}, u32[]{:S(2)}) copy-start(f32[2,8,64,128]{3,2,1,0:T(8,128)} %refs_4_.1) | copy-start | bytes 1572868
  9.6 21.5 %copy-start.8 = (s32[2]{0:T(128)S(1)}, s32[2]{0:T(128)}, u32[]{:S(2)}) copy-start(s32[2]{0:T(128)} %sources.1) | copy-start | bytes 28
  9.6 21.5 %collective-permute-start.2 = (f32[2,8,64,128]{3,2,1,0:T(8,128)S(1)}, f32[2,8,64,128]{3,2,1,0:T(8,128)S(1)}, u32[]{:S(2)}, u32[]{:S(2)}) collective-permute-start(f32[2,8,64,128]{3,2,1,0:T(8,128)S(1)} %pick.5.own), channel_id=1, source_target_pairs={{0,1},{1,0},{2,3},{3,2},{4,5},{5,4},{6,7},{7,6},{8,9},{9,8},{10,11... | collective-permute-start | bytes 1572872 | tf_op jit(solution)/shard_map/ppermute | solution.py:624
  19.7 11.4 %collective-permute-start.3 = (f32[2,8,64,128]{3,2,1,0:T(8,128)S(1)}, f32[2,8,64,128]{3,2,1,0:T(8,128)S(1)}, u32[]{:S(2)}, u32[]{:S(2)}) collective-permute-start(f32[2,8,64,128]{3,2,1,0:T(8,128)S(1)} %collective-permute-done.1.over), channel_id=1, source_target_pairs={{0,1},{1,0},{2,3},{3,2},{4,5},{5,4},{6,7},{7,6},{8,9},{9,8},{10,11... | collective-permute-start | bytes 1572872 | tf_op jit(solution)/shard_map/ppermute | solution.py:624
  20.2 0.7 copy-start.7
  22.0 23.7 %collective-permute-start = (f32[2,8,64,128]{3,2,1,0:T(8,128)}, f32[2,8,64,128]{3,2,1,0:T(8,128)S(1)}, u32[]{:S(2)}, u32[]{:S(2)}) collective-permute-start(f32[2,8,64,128]{3,2,1,0:T(8,128)} %get-tuple-element.34), channel_id=1, source_target_pairs={{0,2},{1,3},{2,0},{3,1},{4,6},{5,7},{6,4},{7,5},{8,10},{9,11},{10,... | collective-permute-start | bytes 1572872 | tf_op jit(solution)/shard_map/ppermute | solution.py:624
  24.1 5.2 %collective-permute-start.6 = (f32[4,64,128]{2,1,0:T(8,128)S(1)}, f32[4,64,128]{2,1,0:T(8,128)S(1)}, u32[]{:S(2)}, u32[]{:S(2)}) collective-permute-start(f32[4,64,128]{2,1,0:T(8,128)S(1)} %collective-permute-done.5.mine), channel_id=1, source_target_pairs={{0,4},{1,5},{2,6},{3,7},{4,0},{5,1},{6,2},{7,3},{8,12},{9,13},{10,... | collective-permute-start | bytes 393224 | tf_op jit(solution)/shard_map/ppermute | solution.py:624
  25.6 4.5 %collective-permute-start.4 = (f32[8,64,128]{2,1,0:T(8,128)}, f32[8,64,128]{2,1,0:T(8,128)}, u32[]{:S(2)}, u32[]{:S(2)}) collective-permute-start(f32[8,64,128]{2,1,0:T(8,128)} %get-tuple-element.38.c0), channel_id=1, source_target_pairs={{0,1},{1,0},{2,3},{3,2},{4,5},{5,4},{6,7},{7,6},{8,9},{9,8},{10,11... | collective-permute-start | bytes 786440 | tf_op jit(solution)/shard_map/ppermute | solution.py:624
  29.4 1.7 %collective-permute-start.7 = (f32[8,64,128]{2,1,0:T(8,128)S(1)}, f32[8,64,128]{2,1,0:T(8,128)}, u32[]{:S(2)}, u32[]{:S(2)}) collective-permute-start(f32[8,64,128]{2,1,0:T(8,128)S(1)} %arrange_kernel.1.c2), channel_id=1, source_target_pairs={{0,1},{1,0},{2,3},{3,2},{4,5},{5,4},{6,7},{7,6},{8,9},{9,8},{10,11... | collective-permute-start | bytes 786440 | tf_op jit(solution)/shard_map/ppermute | solution.py:624
  30.1 15.8 %collective-permute-start.8 = (f32[2,8,64,128]{3,2,1,0:T(8,128)S(1)}, f32[2,8,64,128]{3,2,1,0:T(8,128)S(1)}, u32[]{:S(2)}, u32[]{:S(2)}) collective-permute-start(f32[2,8,64,128]{3,2,1,0:T(8,128)S(1)} %get-tuple-element.43.own), channel_id=1, source_target_pairs={{0,1},{1,0},{2,3},{3,2},{4,5},{5,4},{6,7},{7,6},{8,9},{9,8},{10,11... | collective-permute-start | bytes 1572872 | tf_op jit(solution)/shard_map/ppermute | solution.py:624
  31.1 0.7 copy-start.6
  45.7 30.7 %copy-start.4 = (f32[8,64,128]{2,1,0:T(8,128)S(1)}, f32[8,64,128]{2,1,0:T(8,128)}, u32[]{:S(2)}) copy-start(f32[8,64,128]{2,1,0:T(8,128)} %momentum.3) | copy-start | bytes 786436
  45.7 2.0 %collective-permute-start.9 = (f32[2,8,64,128]{3,2,1,0:T(8,128)S(1)}, f32[2,8,64,128]{3,2,1,0:T(8,128)S(1)}, u32[]{:S(2)}, u32[]{:S(2)}) collective-permute-start(f32[2,8,64,128]{3,2,1,0:T(8,128)S(1)} %collective-permute-done.over), channel_id=1, source_target_pairs={{0,1},{1,0},{2,3},{3,2},{4,5},{5,4},{6,7},{7,6},{8,9},{9,8},{10,11... | collective-permute-start | bytes 1572872 | tf_op jit(solution)/shard_map/ppermute | solution.py:624
  54.7 5.6 %collective-permute-start.10 = (f32[4,64,128]{2,1,0:T(8,128)S(1)}, f32[4,64,128]{2,1,0:T(8,128)S(1)}, u32[]{:S(2)}, u32[]{:S(2)}) collective-permute-start(f32[4,64,128]{2,1,0:T(8,128)S(1)} %get-tuple-element.49), channel_id=1, source_target_pairs={{0,2},{1,3},{2,0},{3,1},{4,6},{5,7},{6,4},{7,5},{8,10},{9,11},{10,... | collective-permute-start | bytes 393224 | tf_op jit(solution)/shard_map/ppermute | solution.py:624
  55.2 5.3 %collective-permute-start.11 = (f32[4,64,128]{2,1,0:T(8,128)S(1)}, f32[4,64,128]{2,1,0:T(8,128)S(1)}, u32[]{:S(2)}, u32[]{:S(2)}) collective-permute-start(f32[4,64,128]{2,1,0:T(8,128)S(1)} %get-tuple-element.51), channel_id=1, source_target_pairs={{0,4},{1,5},{2,6},{3,7},{4,0},{5,1},{6,2},{7,3},{8,12},{9,13},{10,... | collective-permute-start | bytes 393224 | tf_op jit(solution)/shard_map/ppermute | solution.py:624
  60.4 4.3 %collective-permute-start.12 = (f32[2,64,128]{2,1,0:T(8,128)S(1)}, f32[2,64,128]{2,1,0:T(8,128)S(1)}, u32[]{:S(2)}, u32[]{:S(2)}) collective-permute-start(f32[2,64,128]{2,1,0:T(8,128)S(1)} %get-tuple-element.53), channel_id=1, source_target_pairs={{0,4},{1,5},{2,6},{3,7},{4,0},{5,1},{6,2},{7,3},{8,12},{9,13},{10,... | collective-permute-start | bytes 196616 | tf_op jit(solution)/shard_map/ppermute | solution.py:624
  62.2 4.3 %collective-permute-start.13 = (f32[2,64,128]{2,1,0:T(8,128)S(1)}, f32[2,64,128]{2,1,0:T(8,128)S(1)}, u32[]{:S(2)}, u32[]{:S(2)}) collective-permute-start(f32[2,64,128]{2,1,0:T(8,128)S(1)} %get-tuple-element.55), channel_id=1, source_target_pairs={{0,2},{1,3},{2,0},{3,1},{4,6},{5,7},{6,4},{7,5},{8,10},{9,11},{10,... | collective-permute-start | bytes 196616 | tf_op jit(solution)/shard_map/ppermute | solution.py:624
  66.5 4.3 %collective-permute-start.14 = (f32[2,64,128]{2,1,0:T(8,128)S(1)}, f32[2,64,128]{2,1,0:T(8,128)S(1)}, u32[]{:S(2)}, u32[]{:S(2)}) collective-permute-start(f32[2,64,128]{2,1,0:T(8,128)S(1)} %get-tuple-element.57), channel_id=1, source_target_pairs={{0,8},{1,9},{2,10},{3,11},{4,12},{5,13},{6,14},{7,15},{8,0},{9,1},... | collective-permute-start | bytes 196616 | tf_op jit(solution)/shard_map/ppermute | solution.py:624
  70.8 5.5 %collective-permute-start.15 = (f32[2,64,128]{2,1,0:T(8,128)S(1)}, f32[2,64,128]{2,1,0:T(8,128)S(1)}, u32[]{:S(2)}, u32[]{:S(2)}) collective-permute-start(f32[2,64,128]{2,1,0:T(8,128)S(1)} %add_kernel.1.mine), channel_id=1, source_target_pairs={{0,16},{1,17},{2,18},{3,19},{4,20},{5,21},{6,22},{7,23},{8,24},{9,... | collective-permute-start | bytes 196616 | tf_op jit(solution)/shard_map/ppermute | solution.py:624
  76.5 4.6 %collective-permute-start.16 = (f32[136,128]{1,0:T(8,128)S(1)}, f32[136,128]{1,0:T(8,128)S(1)}, u32[]{:S(2)}, u32[]{:S(2)}) collective-permute-start(f32[136,128]{1,0:T(8,128)S(1)} %get-tuple-element.58.mine), channel_id=1, source_target_pairs={{0,8},{1,9},{2,10},{3,11},{4,12},{5,13},{6,14},{7,15},{8,0},{9,1},... | collective-permute-start | bytes 208904 | tf_op jit(solution)/shard_map/ppermute | solution.py:624
  78.1 1.2 %collective-permute-start.17 = (f32[8,128]{1,0:T(8,128)S(1)}, f32[8,128]{1,0:T(8,128)S(1)}, u32[]{:S(2)}, u32[]{:S(2)}) collective-permute-start(f32[8,128]{1,0:T(8,128)S(1)} %get-tuple-element.59.s0), channel_id=1, source_target_pairs={{0,1},{1,0},{2,3},{3,2},{4,5},{5,4},{6,7},{7,6},{8,9},{9,8},{10,11... | collective-permute-start | bytes 12296 | tf_op jit(solution)/shard_map/ppermute | solution.py:624
  78.1 3.0 %collective-permute-start.18 = (f32[8,128]{1,0:T(8,128)S(1)}, f32[8,128]{1,0:T(8,128)S(1)}, u32[]{:S(2)}, u32[]{:S(2)}) collective-permute-start(f32[8,128]{1,0:T(8,128)S(1)} %get-tuple-element.59.s0), channel_id=1, source_target_pairs={{0,9},{1,8},{2,11},{3,10},{4,13},{5,12},{6,15},{7,14},{8,1},{9,0},... | collective-permute-start | bytes 12296 | tf_op jit(solution)/shard_map/ppermute | solution.py:624
  81.1 6.8 %collective-permute-start.19 = (f32[264,128]{1,0:T(8,128)S(1)}, f32[264,128]{1,0:T(8,128)S(1)}, u32[]{:S(2)}, u32[]{:S(2)}) collective-permute-start(f32[264,128]{1,0:T(8,128)S(1)} %get-tuple-element.60.mine), channel_id=1, source_target_pairs={{0,4},{1,5},{2,6},{3,7},{4,0},{5,1},{6,2},{7,3},{8,12},{9,13},{10,... | collective-permute-start | bytes 405512 | tf_op jit(solution)/shard_map/ppermute | solution.py:624
  81.9 3.6 %collective-permute-start.20 = (f32[8,128]{1,0:T(8,128)S(1)}, f32[8,128]{1,0:T(8,128)S(1)}, u32[]{:S(2)}, u32[]{:S(2)}) collective-permute-start(f32[8,128]{1,0:T(8,128)S(1)} %get-tuple-element.61.s0), channel_id=1, source_target_pairs={{0,2},{1,3},{2,0},{3,1},{4,6},{5,7},{6,4},{7,5},{8,10},{9,11},{10,... | collective-permute-start | bytes 12296 | tf_op jit(solution)/shard_map/ppermute | solution.py:624
  83.5 4.5 %collective-permute-start.21 = (f32[8,128]{1,0:T(8,128)S(1)}, f32[8,128]{1,0:T(8,128)S(1)}, u32[]{:S(2)}, u32[]{:S(2)}) collective-permute-start(f32[8,128]{1,0:T(8,128)S(1)} %get-tuple-element.61.s0), channel_id=1, source_target_pairs={{0,6},{1,7},{2,4},{3,5},{4,2},{5,3},{6,0},{7,1},{8,14},{9,15},{10,... | collective-permute-start | bytes 12296 | tf_op jit(solution)/shard_map/ppermute | solution.py:624

commit v7 on v6

--- a/solution.py
+++ b/solution.py
@@ -158,25 +158,36 @@
         interleave(outs[n // 2], (n % 2,), held.at[n])
 
 
-def pick(*pairs, after=None, grant=16):
+def pick(*pairs, after):
     plain = functools.partial(pick_kernel, tuple(pair[2] for pair in pairs))
     fields = [field for pair in pairs for field in pair[:2]]
     shape = fields[0].shape[1:]
     vmem, hbm = pl.BlockSpec(memory_space=pltpu.VMEM), pl.BlockSpec(memory_space=pltpu.HBM)
-    marks = [] if after is None else [after]
     return pl.pallas_call(
-        lambda *refs: plain(*refs[len(marks) :]),
-        in_specs=[vmem] * len(marks) + [hbm] * len(fields),
+        lambda mark, *refs: plain(*refs),
+        in_specs=[vmem] + [hbm] * len(fields),
         out_specs=[vmem] * len(pairs),
         out_shape=[jax.ShapeDtypeStruct((2, *shape), jnp.float32)] * len(pairs),
         scratch_shapes=[pltpu.VMEM((len(fields), *shape), jnp.float32), pltpu.SemaphoreType.DMA((len(fields),))],
-        compiler_params=pltpu.CompilerParams(vmem_limit_bytes=grant * 2**18),
+        compiler_params=pltpu.CompilerParams(vmem_limit_bytes=4 * 2**20),
         name="pick",
-    )(*marks, *fields)
-
-
-def courant_kernel(courant, whole, piece):
-    interleave(whole, (), courant, 1.0 / 12.0)
+    )(after, *fields)
+
+
+def first_kernel(first, second, courant, outgoing, whole, piece, held, held_courant, sems):
+    shot = 1 - lax.axis_index("chip")
+    copies = [
+        pltpu.make_async_copy(first.at[shot], held.at[0], sems.at[0]),
+        pltpu.make_async_copy(second.at[shot], held.at[1], sems.at[1]),
+        pltpu.make_async_copy(courant, held_courant, sems.at[2]),
+    ]
+    for copy in copies:
+        copy.start()
+    for n in range(2):
+        copies[n].wait()
+        interleave(outgoing, (n,), held.at[n])
+    copies[2].wait()
+    interleave(whole, (), held_courant, 1.0 / 12.0)
     count = piece.shape[0]
     piece[...] = whole[pl.ds(lax.axis_index("shot") % 2 * count, count)]
 
@@ -192,17 +203,6 @@
     high = whole.astype(jnp.bfloat16)
     low = (whole - high.astype(jnp.float32)).astype(jnp.bfloat16)
     out[...] = jnp.dot(jnp.concatenate([high, low], 1), banded[...], preferred_element_type=jnp.float32)
-
-
-def y_shifts(center):
-    lanes = center.shape[1]
-    lane = lax.broadcasted_iota(jnp.int32, center.shape, 1)
-
-    def shift(by):
-        inside = lane >= by if by > 0 else lane < lanes + by
-        return jnp.where(inside, pltpu.roll(center, by % lanes, 1), 0.0)
-
-    return shift(1) + shift(-1), shift(2) + shift(-2)
 
 
 def laps12(field, z, y_part, fetch, finish):
@@ -236,8 +236,7 @@
                 near = (tile(j, i - 1), tile(j, i + 1), tile(j - 1, i), tile(j + 1, i))
                 far = (tile(j, i - 2), tile(j, i + 2), tile(j - 2, i), tile(j + 2, i))
                 at = (j * groups + i) * 8
-                part = y_shifts(center) if y_part is None else y_part[at : at + 8]
-                found.append((center, near, far, part, fetch(j, slice(i * 8, i * 8 + 8))))
+                found.append((center, near, far, y_part[at : at + 8], fetch(j, slice(i * 8, i * 8 + 8))))
             return found
 
         ready = load(0)
@@ -246,15 +245,11 @@
             for j, (center, near, far, part, extra) in enumerate(ready):
                 near = (near[0] + near[1]) + (near[2] + near[3])
                 far = (far[0] + far[1]) + (far[2] + far[3])
-                if y_part is None:
-                    lap = 16.0 * (near + part[0]) - (far + part[1]) - 90.0 * center
-                else:
-                    lap = 16.0 * near + (part - far)
-                finish(base + j, slice(i * 8, i * 8 + 8), center, lap, extra)
+                finish(base + j, slice(i * 8, i * 8 + 8), center, 16.0 * near + (part - far), extra)
             ready = upcoming
 
 
-def scatter_kernel(rows_x, cells_ref, observed_ref, out_ref, mark, second, row_ref, spread):
+def scatter_kernel(rows_x, cells_ref, observed_ref, out_ref, mark, row_ref, spread):
     _, steps, receivers = observed_ref.shape
     lanes = out_ref.shape[2]
     tile = out_ref.shape[1]
@@ -288,7 +283,6 @@
         spread[0:receivers, cols] = jnp.where(at, 1.0, 0.0).astype(jnp.bfloat16)
         spread[receivers:, cols] = jnp.zeros((receivers, lanes), jnp.bfloat16)
         mark[...] = jnp.zeros(mark.shape, jnp.float32)
-        second[...] = jnp.zeros(mark.shape, jnp.float32)
 
     ids = lax.broadcasted_iota(jnp.int32, (tile, receivers), 0) + pl.program_id(0) * tile
     chosen = jnp.where(ids == row_ref[...], 1.0, 0.0).astype(jnp.bfloat16)
@@ -300,7 +294,7 @@
 def scatter(rec_cells, observed, planes_all, rows_x, rows_y):
     _, steps, receivers = observed.shape
     rows_all = planes_all * rows_x
-    tile = 256
+    tile = 512
     mark = jax.ShapeDtypeStruct((8, rows_y), jnp.float32)
     mark_block = pl.BlockSpec((8, rows_y), lambda t: (0, 0))
     return pl.pallas_call(
@@ -310,8 +304,8 @@
             pl.BlockSpec((2, receivers), lambda t: (0, 0)),
             pl.BlockSpec((2, steps, receivers), lambda t: (0, 0, 0)),
         ],
-        out_specs=[pl.BlockSpec((steps + 1, tile, rows_y), lambda t: (0, t, 0)), mark_block, mark_block],
-        out_shape=[jax.ShapeDtypeStruct((steps + 1, rows_all, rows_y), jnp.float32), mark, mark],
+        out_specs=[pl.BlockSpec((steps + 1, tile, rows_y), lambda t: (0, t, 0)), mark_block],
+        out_shape=[jax.ShapeDtypeStruct((steps + 1, rows_all, rows_y), jnp.float32), mark],
         scratch_shapes=[
             pltpu.VMEM((1, receivers), jnp.int32),
             pltpu.VMEM((2 * receivers, (steps + 1) * rows_y), jnp.bfloat16),
@@ -369,18 +363,9 @@
                 work(z + n * BATCH, parts[n % 2], chip if owned else None, n * BATCH)
 
 
-def sweep_shifts(core, planes, work):
-    for owned in (True, False):
-
-        @pl.loop(0, 2)
-        def _(chip):
-            z = (2 * chip + (core if owned else 1 - core)) * planes
-            for p in range(0, planes, BATCH):
-                work(z + p, None, chip if owned else None, p)
-
-
 def forward_kernel(
-    start, sources, scattered, own, mate, over, far, c0, c1, c2, c3, placed, laps, inject, cour, mark, even, odd, traces_even, traces_odd, counts, sems
+    start, sources, arranged, own, mate, over, far, c0, c1, c2, c3, placed, laps, inject, cour, mark, even, odd, banded, y0, y1,
+    traces_even, traces_odd, counts, sems
 ):
     planes, rows, lanes = c0.shape
     steps = laps.shape[0]
@@ -395,6 +380,7 @@
     count_copy = pltpu.make_async_copy(placed.at[steps], counts, sems.at[2])
     count_copy.start()
     copy(1, 1).start()
+    banded[...] = band(lanes)
     load_blocks(slabs, (own, mate, over, far), odd, even)
     for slab, block in zip(slabs, (c0, c1, c2, c3)):
 
@@ -427,7 +413,7 @@
 
             laps12(now, z, y_part, fetch, finish)
 
-        sweep_shifts(core, planes, work)
+        sweep(core, planes, now, banded, y0, y1, work)
 
         @pl.when(k + 2 < steps)
         def _():
@@ -454,7 +440,7 @@
         advance(2 * pair + 1, odd, even, traces_odd, 1)
 
 
-def adjoint_kernel(mark, own, mate, over, far, cour, laps, inject, keep_a, send_a, keep_b, send_b, even, odd, total, banded, y0, y1):
+def adjoint_kernel(mark, own, mate, over, far, cour, laps, inject, keep, send_x, send_y, send_xy, even, odd, total, banded, y0, y1):
     planes, rows, lanes = own.shape[1:]
     steps = laps.shape[0]
     groups = rows // 8
@@ -494,13 +480,10 @@
         advance(steps - 1 - 2 * pair, even, odd)
         advance(steps - 2 - 2 * pair, odd, even)
 
-    half, quarter = planes // 2, planes // 4
-    y = lax.axis_index("shot") % 2
+    count = keep.shape[0]
+    mine, others = lax.axis_index("shot") % 2 * count, (1 - lax.axis_index("shot") % 2) * count
     here, there = chip_here, 1 - chip_here
-    runs = [(keep_a, 0, half, here, 0), (send_a, 0, half, there, 0)]
-    for ref, side in ((keep_b, y), (send_b, 1 - y)):
-        runs += [(ref, 0, quarter, here, half + side * quarter), (ref, quarter, quarter, there, half + side * quarter)]
-    for ref, at, count, chip, start in runs:
+    for ref, chip, start in ((keep, here, mine), (send_x, there, mine), (send_y, here, others), (send_xy, there, others)):
 
         @pl.loop(0, count)
         def _(n):
@@ -509,26 +492,16 @@
             weight = 1.0 + 2.0 * jnp.full((rows, lanes), z, jnp.int32).astype(jnp.float32) / (4 * planes - 1)
             value = weight * total[chip * planes + p] / (12.0 * cour[z])
             for i in range(groups):
-                ref[at + n, pl.ds(i, 8, stride=groups), :] = value[i * 8 : (i + 1) * 8]
-
-
-def cross_kernel(keep_a, other_a, keep_b, other_b, next_a, send_a, next_b, send_b):
-    y = lax.axis_index("shot") % 2
-    count = next_a.shape[0]
-    for ref, part in ((next_a, y), (send_a, 1 - y)):
+                ref[n, pl.ds(i, 8, stride=groups), :] = value[i * 8 : (i + 1) * 8]
+
+
+def square_kernel(mine, by_x, by_y, by_xy, keep, send):
+    half = lax.axis_index("shot") // 2 % 2
+    count = keep.shape[0]
+    for ref, part in ((keep, half), (send, 1 - half)):
         for p in range(count):
-            ref[p] = keep_a[part * count + p] + other_a[part * count + p]
-    for ref, part in ((next_b, 0), (send_b, 1)):
-        for p in range(count):
-            ref[p] = keep_b[part * count + p] + other_b[part * count + p]
-
-
-def choose_kernel(keep_a, other_a, keep_b, other_b, keep, send):
-    second = lax.axis_index("shot") // 2 % 2 == 1
-    first_half = keep_a[...] + other_a[...]
-    second_half = keep_b[...] + other_b[...]
-    keep[...] = jnp.where(second, second_half, first_half)
-    send[...] = jnp.where(second, first_half, second_half)
+            at = part * count + p
+            ref[p] = (mine[at] + by_x[at]) + (by_y[at] + by_xy[at])
 
 
 def add_kernel(mine, other, out):
@@ -543,7 +516,12 @@
     return result
 
 
-def arrange_kernel(mine, other, out):
+def after_kernel(mark, value, out):
+    out[...] = value[...]
+
+
+def arrange_kernel(mine, other, out, mark):
+    mark[...] = jnp.zeros(mark.shape, jnp.float32)
     y = lax.axis_index("shot") % 2
     count = mine.shape[0]
     out[pl.ds(y * count, count)] = mine[...]
@@ -551,7 +529,7 @@
 
 
 def first_plane(shot, planes):
-    return (shot // 2 % 2) * (planes // 2) + (shot % 2) * (planes // 4)
+    return (shot % 2) * (planes // 2) + (shot // 2 % 2) * (planes // 4)
 
 
 def sums_kernel(mine, other, momentum, data, sums):
@@ -636,22 +614,39 @@
     cells_all = planes_all * rows_x * rows_y
     vmem, smem = pl.BlockSpec(memory_space=pltpu.VMEM), pl.BlockSpec(memory_space=pltpu.SMEM)
 
-    (outgoing,) = pick((fwd_prev, fwd_cur, True), grant=253)
+    hbm = pl.BlockSpec(memory_space=pltpu.HBM)
+    outgoing, c0, piece = pl.pallas_call(
+        first_kernel,
+        in_specs=[hbm] * 3,
+        out_specs=[vmem] * 3,
+        out_shape=[
+            jax.ShapeDtypeStruct((2, planes, rows_x, rows_y), jnp.float32),
+            jax.ShapeDtypeStruct(courant_sq.shape, jnp.float32),
+            jax.ShapeDtypeStruct((planes // 2, rows_x, rows_y), jnp.float32),
+        ],
+        scratch_shapes=[
+            pltpu.VMEM((2, planes, rows_x, rows_y), jnp.float32),
+            pltpu.VMEM(courant_sq.shape, jnp.float32),
+            pltpu.SemaphoreType.DMA((3,)),
+        ],
+        compiler_params=pltpu.CompilerParams(vmem_limit_bytes=63 * 2**20),
+        name="first_to_cross",
+    )(fwd_prev, fwd_cur, courant_sq)
+
     over = exchange(outgoing, CHIP)
-
-    c0, piece = local(courant_kernel, [courant_sq.shape, (planes // 2, rows_x, rows_y)], courant_sq)
     piece = exchange(piece, CHIP)
-    (own,) = pick((fwd_prev, fwd_cur, False))
+
+    placed, mark = scatter(rec_cells, observed, planes_all, rows_x, rows_y)
+    placed = placed.reshape(steps + 1, planes_all, rows_x, rows_y)
+
+    adj_outgoing, adj_own, own = pick(
+        (adj_next, adj_cur, True), (adj_next, adj_cur, False), (fwd_prev, fwd_cur, False), after=mark
+    )
     mate = exchange(own, CORE)
-    c1 = exchange(c0, CORE)
-    c2 = local(arrange_kernel, [courant_sq.shape], piece, exchange(piece, Y))
-    c3 = exchange(c2, CORE)
-
-    placed, mark, second = scatter(rec_cells, observed, planes_all, rows_x, rows_y)
-    placed = placed.reshape(steps + 1, planes_all, rows_x, rows_y)
-
-    adj_outgoing, adj_own = pick((adj_next, adj_cur, True), (adj_next, adj_cur, False), after=mark)
-    over, second = lax.optimization_barrier((over, second))
+    piece = local(after_kernel, [piece.shape], mark, piece)
+    c2, arranged = local(arrange_kernel, [courant_sq.shape, (8, rows_y)], piece, exchange(piece, Y))
+    c1, c3 = exchange(c0, CORE), exchange(c2, CORE)
+    over, arranged = lax.optimization_barrier((over, arranged))
     far = exchange(over, CORE)
     adj_over = exchange(adj_outgoing, CHIP)
     adj_mate = exchange(adj_own, CORE)
@@ -672,17 +667,17 @@
             jax.ShapeDtypeStruct((planes_all, rows_x, rows_y), jnp.float32),
             jax.ShapeDtypeStruct((8, rows_y), jnp.float32),
         ],
-        scratch_shapes=[scratch, scratch, whole, whole, whole, pltpu.SemaphoreType.DMA((3,))],
+        scratch_shapes=step_scratch + [whole, whole, whole, pltpu.SemaphoreType.DMA((3,))],
         compiler_params=pltpu.CompilerParams(vmem_limit_bytes=33 * 2**20),
         cost_estimate=cost,
         name="forward_steps",
-    )(ckpt_step[None], src_cells, second, own, mate, over, far, c0, c1, c2, c3, placed)
+    )(ckpt_step[None], src_cells, arranged, own, mate, over, far, c0, c1, c2, c3, placed)
 
     adj_over, mark = lax.optimization_barrier((adj_over, mark))
     adj_far = exchange(adj_over, CORE)
     slab = jax.ShapeDtypeStruct(courant_sq.shape, jnp.float32)
     half, quarter = (planes // 2, rows_x, rows_y), (planes // 4, rows_x, rows_y)
-    keep_a, send_a, keep_b, send_b = pl.pallas_call(
+    keep, send_x, send_y, send_xy = pl.pallas_call(
         adjoint_kernel,
         in_specs=[pl.BlockSpec(memory_space=pl.ANY)] + [vmem] * 7,
         out_specs=[vmem] * 4,
@@ -693,10 +688,8 @@
         name="adjoint_steps",
     )(mark, adj_own, adj_mate, adj_over, adj_far, cour, laps, inject)
 
-    other_a, other_b = exchange(send_a, CHIP), exchange(send_b, Y)
-    keep_a, send_a, keep_b, send_b = local(cross_kernel, [quarter] * 4, keep_a, other_a, keep_b, other_b)
-    other_a, other_b = exchange(send_a, Y), exchange(send_b, CHIP)
-    keep, send = local(choose_kernel, [quarter] * 2, keep_a, other_a, keep_b, other_b)
+    by_xy, by_x, by_y = exchange(send_xy, CHIP + Y), exchange(send_x, CHIP), exchange(send_y, Y)
+    keep, send = local(square_kernel, [quarter] * 2, keep, by_x, by_y, by_xy)
     part = local(add_kernel, [quarter], keep, exchange(send, NEAR_Z))
     rows, sums_shape = planes // 4 * rows_x, (8, rows_y)
     data, sums = local(sums_kernel, [(rows + 8, rows_y), sums_shape], part, exchange(part, FAR_Z), momentum)

time: 89.1 us -> 77.8 us (0.87)
  local copies, waits for them, and re-layouts: 4.4 us -> 0.72 us
  Pallas kernels: 36 us -> 32.5 us
  starting transfers between devices: 24 us -> 21.6 us
  waiting for transfers between devices: 23 us -> 21.2 us
    unnamed x18 -> x16, local copies, waits for them, and re-layouts: 4.4 us -> 0.72 us
    pallas_call x1, Pallas kernels: 13.9 us -> 10.6 us  [whole_shards(): pl.pallas_call(forward_kernel, in_specs=[smem, smem, pl.BlockSpec(memory_...]
    ppermute x22 -> x21, starting transfers between devices: 24 us -> 21.6 us  [exchange(): lax.ppermute(value, axes, [(i, i ^ bits) for i in range(lax.axis_size(axe...]
    ppermute x22 -> x21, waiting for transfers between devices: 23 us -> 21.2 us  [exchange(): lax.ppermute(value, axes, [(i, i ^ bits) for i in range(lax.axis_size(axe...]
    pallas_call x3 -> x2, Pallas kernels: 3.24 us -> 3.47 us  [the longest x1 2.12 us: whole_shards(): pl.pallas_call(first_kernel, in_specs=[hbm] * 3, out_specs=[vmem] * 3, ou...]
  transfers between devices with their start and end apart: 22 -> 21, of which waited for: 13 -> 12; matrix products, arithmetic and copies ran while one was open for 0% -> 0% of each run, Pallas kernels for 29% -> 28%
where the time goes in v7:
time: 77.8 us; the launch traced here: 77.5 us
  Pallas kernels  32.5 us (42%)
  starting transfers between devices  21.6 us (28%)
  waiting for transfers between devices  21.2 us (27%)
  between operations  1.4 us (2%)
    ppermute x21, starting transfers between devices, exchange(): lax.ppermute(value, axes, [(i, i ^ bits) for i in range(lax.axis_size(axe...  21.6 us
    ppermute x21, waiting for transfers between devices, exchange(): lax.ppermute(value, axes, [(i, i ^ bits) for i in range(lax.axis_size(axe...  21.2 us
    pallas_call x1, Pallas kernels, whole_shards(): pl.pallas_call(forward_kernel, in_specs=[smem, smem, pl.BlockSpec(memory_...  10.6 us
    pallas_call x1, Pallas kernels, scatter(): pl.pallas_call(functools.partial(scatter_kernel, rows_x), grid=(rows_all...  9.27 us
    pallas_call x1, Pallas kernels, whole_shards(): pl.pallas_call(adjoint_kernel, in_specs=[pl.BlockSpec(memory_space=pl.ANY...  7.5 us
    pallas_call x1, Pallas kernels, whole_shards(): pl.pallas_call(first_kernel, in_specs=[hbm] * 3, out_specs=[vmem] * 3, ou...  2.12 us
  transfers between devices with their start and end apart: 21, of which 12 were waited for; matrix products, arithmetic and copies ran while one was open for 0% of the time, Pallas kernels for 28%

profile of v7, /device:TPU:0, one launch (start us, length us, event | category | flops | bytes accessed | tf_op | source)
XLA Modules:
  0.0 77.5 jit_solution(446371434015642430)
XLA Ops:
  0.6 2.1 %first_to_cross.1 = (f32[2,8,64,128]{3,2,1,0:T(8,128)}, f32[8,64,128]{2,1,0:T(8,128)}, f32[4,64,128]{2,1,0:T(8,128)}) custom-call(f32[2,8,64,128]{3,2,1,0:T(8,128)} %first.1, f32[2,8,64,128]{3,2,1,0:T(8,128)} %second.1, f32[8,64,128]{2,1,0:T(8,128)} %courant.1), custom_call_target="tpu_custom_call" | custom-call | tf_op jit(solution)/shard_map/first_to_cross/pallas_call | solution.py:618
  2.8 3.0 %collective-permute-start.2 = (f32[4,64,128]{2,1,0:T(8,128)}, f32[4,64,128]{2,1,0:T(8,128)S(1)}, u32[]{:S(2)}, u32[]{:S(2)}) collective-permute-start(f32[4,64,128]{2,1,0:T(8,128)} %get-tuple-element.35), channel_id=1, source_target_pairs={{0,2},{1,3},{2,0},{3,1},{4,6},{5,7},{6,4},{7,5},{8,10},{9,11},{10,... | collective-permute-start | bytes 393224 | tf_op jit(solution)/shard_map/ppermute | solution.py:602
  5.8 0.0 copy-start
  5.8 0.0 copy-start.1
  5.8 0.0 copy-start.2
  5.8 0.0 copy-start.5
  5.8 0.0 copy-start.7
  5.8 0.1 collective-permute-start.1
  5.9 9.3 %receiver_scatter.1 = (f32[9,2048,128]{2,1,0:T(8,128)}, f32[8,128]{1,0:T(8,128)}) custom-call(s32[2,512]{1,0:T(2,128)} %cells_ref.1, f32[2,8,512]{2,1,0:T(8,128)} %observed_ref.1), custom_call_target="tpu_custom_call" | custom-call | flops 4831838208 | bytes 9437184 | tf_op jit(solution)/shard_map/receiver_scatter/pallas_call | solution.py:300
  15.2 0.0 collective-permute-done.2.value
  15.2 0.7 copy-done.6
  15.9 2.0 %collective-permute-start.3 = (f32[4,64,128]{2,1,0:T(8,128)S(1)}, f32[4,64,128]{2,1,0:T(8,128)S(1)}, u32[]{:S(2)}, u32[]{:S(2)}) collective-permute-start(f32[4,64,128]{2,1,0:T(8,128)S(1)} %after_kernel.1.mine), channel_id=1, source_target_pairs={{0,4},{1,5},{2,6},{3,7},{4,0},{5,1},{6,2},{7,3},{8,12},{9,13},{10,... | collective-permute-start | bytes 393224 | tf_op jit(solution)/shard_map/ppermute | solution.py:602
  17.9 0.0 copy-done
  17.9 0.0 copy-done.1
  17.9 0.0 copy-done.2
  17.9 0.0 copy-done.3
  17.9 1.4 %pick.1 = (f32[2,8,64,128]{3,2,1,0:T(8,128)}, f32[2,8,64,128]{3,2,1,0:T(8,128)S(1)}, f32[2,8,64,128]{3,2,1,0:T(8,128)S(1)}) custom-call(f32[8,128]{1,0:T(8,128)S(1)} %copy-done.6, f32[2,8,64,128]{3,2,1,0:T(8,128)S(1)} %copy-done.2, f32[2,8,64,128]{3,2,1,0:T(8,128)S(1)} %copy-done.3, f32[2,8,64,128]{3,2,1,0:T(8,128)S(1)} %copy-done.2, ...), custom_call_target="tpu_custom_call" | custom-call | tf_op jit(solution)/shard_map/pick/pallas_call | solution.py:166
  19.3 0.1 collective-permute-start.4
  19.4 1.6 %collective-permute-done.3.other = f32[4,64,128]{2,1,0:T(8,128)S(1)} collective-permute-done((f32[4,64,128]{2,1,0:T(8,128)S(1)}, f32[4,64,128]{2,1,0:T(8,128)S(1)}, u32[]{:S(2)}, u32[]{:S(2)}) %collective-permute-start.3) | collective-permute-done | bytes 131104 | tf_op jit(solution)/shard_map/ppermute | solution.py:602
  20.9 0.7 arrange_kernel.1
  21.7 0.0 collective-permute-done.1.over
  21.7 0.0 collective-permute-start.5
  21.7 1.8 %collective-permute-start = (f32[2,8,64,128]{3,2,1,0:T(8,128)}, f32[2,8,64,128]{3,2,1,0:T(8,128)S(1)}, u32[]{:S(2)}, u32[]{:S(2)}) collective-permute-start(f32[2,8,64,128]{3,2,1,0:T(8,128)} %get-tuple-element.33), channel_id=1, source_target_pairs={{0,2},{1,3},{2,0},{3,1},{4,6},{5,7},{6,4},{7,5},{8,10},{9,11},{10,... | collective-permute-start | bytes 1572872 | tf_op jit(solution)/shard_map/ppermute | solution.py:602
  23.5 0.0 copy-done.5
  23.5 0.2 collective-permute-start.6
  23.7 0.3 collective-permute-start.7
  24.7 0.5 collective-permute-done.6.c1
  25.2 0.2 collective-permute-start.8
  25.4 0.4 collective-permute-done.7.c3
  25.8 0.0 collective-permute-done.4.mate
  25.8 0.0 collective-permute-done.5.far
  25.8 0.0 copy-done.7
  25.8 10.6 %forward_steps.1 = (f32[8,8,2,64,128]{4,3,2,1,0:T(8,128)S(1)}, f32[8,32,64,128]{3,2,1,0:T(8,128)S(1)}, f32[32,64,128]{2,1,0:T(8,128)S(1)}, f32[8,128]{1,0:T(8,128)S(1)}) custom-call(s32[1]{0:T(128)} %bitcast.3.start, s32[2]{0:T(128)S(1)} %copy-done.7, f32[8,128]{1,0:T(8,128)S(1)} %get-tuple-element.37.arranged, f32[2,8,64,128]{3,2,1,0:T(8,128)S(1)} %get-tuple-element.38.own, ...), custom_call_target="tpu_custom_call" | custom-call | flops 62914560 | bytes 33554432 | tf_op jit(solution)/shard_map/forward_steps/pallas_call | solution.py:660
  36.3 0.0 copy-start.4
  36.4 0.0 collective-permute-done.over
  36.4 0.3 collective-permute-start.9
  36.7 0.0 collective-permute-done.8.mate
  36.7 1.7 %collective-permute-done.9.far = f32[2,8,64,128]{3,2,1,0:T(8,128)S(1)} collective-permute-done((f32[2,8,64,128]{3,2,1,0:T(8,128)S(1)}, f32[2,8,64,128]{3,2,1,0:T(8,128)S(1)}, u32[]{:S(2)}, u32[]{:S(2)}) %collective-permute-start.9) | collective-permute-done | bytes 524320 | tf_op jit(solution)/shard_map/ppermute | solution.py:602
  38.3 7.5 %adjoint_steps.1 = (f32[4,64,128]{2,1,0:T(8,128)S(1)}, f32[4,64,128]{2,1,0:T(8,128)S(1)}, f32[4,64,128]{2,1,0:T(8,128)S(1)}, f32[4,64,128]{2,1,0:T(8,128)S(1)}) custom-call(f32[8,128]{1,0:T(8,128)S(1)} %get-tuple-element.44.mark, f32[2,8,64,128]{3,2,1,0:T(8,128)S(1)} %get-tuple-element.45.own, f32[2,8,64,128]{3,2,1,0:T(8,128)S(1)} %collective-permute-done.8.mate, ...), custom_call_target="tpu_custom_call" | custom-call | flops 62914560 | bytes 33554432 | tf_op jit(solution)/shard_map/adjoint_steps/pallas_call | solution.py:680
  45.9 1.7 %collective-permute-start.10 = (f32[4,64,128]{2,1,0:T(8,128)S(1)}, f32[4,64,128]{2,1,0:T(8,128)S(1)}, u32[]{:S(2)}, u32[]{:S(2)}) collective-permute-start(f32[4,64,128]{2,1,0:T(8,128)S(1)} %get-tuple-element.51), channel_id=1, source_target_pairs={{0,2},{1,3},{2,0},{3,1},{4,6},{5,7},{6,4},{7,5},{8,10},{9,11},{10,... | collective-permute-start | bytes 393224 | tf_op jit(solution)/shard_map/ppermute | solution.py:602
  47.5 1.5 %collective-permute-start.11 = (f32[4,64,128]{2,1,0:T(8,128)S(1)}, f32[4,64,128]{2,1,0:T(8,128)S(1)}, u32[]{:S(2)}, u32[]{:S(2)}) collective-permute-start(f32[4,64,128]{2,1,0:T(8,128)S(1)} %get-tuple-element.52), channel_id=1, source_target_pairs={{0,4},{1,5},{2,6},{3,7},{4,0},{5,1},{6,2},{7,3},{8,12},{9,13},{10,... | collective-permute-start | bytes 393224 | tf_op jit(solution)/shard_map/ppermute | solution.py:602
  49.1 0.4 collective-permute-start.12
  49.4 2.5 %collective-permute-done.10.by_x = f32[4,64,128]{2,1,0:T(8,128)S(1)} collective-permute-done((f32[4,64,128]{2,1,0:T(8,128)S(1)}, f32[4,64,128]{2,1,0:T(8,128)S(1)}, u32[]{:S(2)}, u32[]{:S(2)}) %collective-permute-start.10) | collective-permute-done | bytes 131104 | tf_op jit(solution)/shard_map/ppermute | solution.py:602
  51.9 3.7 %collective-permute-done.11.by_y = f32[4,64,128]{2,1,0:T(8,128)S(1)} collective-permute-done((f32[4,64,128]{2,1,0:T(8,128)S(1)}, f32[4,64,128]{2,1,0:T(8,128)S(1)}, u32[]{:S(2)}, u32[]{:S(2)}) %collective-permute-start.11) | collective-permute-done | bytes 131104 | tf_op jit(solution)/shard_map/ppermute | solution.py:602
  55.6 0.0 collective-permute-done.12.by_xy
  55.6 1.6 %collective-permute-start.13 = (f32[2,64,128]{2,1,0:T(8,128)S(1)}, f32[2,64,128]{2,1,0:T(8,128)S(1)}, u32[]{:S(2)}, u32[]{:S(2)}) collective-permute-start(f32[2,64,128]{2,1,0:T(8,128)S(1)} %get-tuple-element.55), channel_id=1, source_target_pairs={{0,8},{1,9},{2,10},{3,11},{4,12},{5,13},{6,14},{7,15},{8,0},{9,1},... | collective-permute-start | bytes 196616 | tf_op jit(solution)/shard_map/ppermute | solution.py:602
  57.3 2.7 %collective-permute-done.13.other = f32[2,64,128]{2,1,0:T(8,128)S(1)} collective-permute-done((f32[2,64,128]{2,1,0:T(8,128)S(1)}, f32[2,64,128]{2,1,0:T(8,128)S(1)}, u32[]{:S(2)}, u32[]{:S(2)}) %collective-permute-start.13) | collective-permute-done | bytes 65568 | tf_op jit(solution)/shard_map/ppermute | solution.py:602
  60.0 2.7 %collective-permute-start.14 = (f32[2,64,128]{2,1,0:T(8,128)S(1)}, f32[2,64,128]{2,1,0:T(8,128)S(1)}, u32[]{:S(2)}, u32[]{:S(2)}) collective-permute-start(f32[2,64,128]{2,1,0:T(8,128)S(1)} %add_kernel.1.mine), channel_id=1, source_target_pairs={{0,16},{1,17},{2,18},{3,19},{4,20},{5,21},{6,22},{7,23},{8,24},{9,... | collective-permute-start | bytes 196616 | tf_op jit(solution)/shard_map/ppermute | solution.py:602
  62.6 2.6 %collective-permute-done.14.other = f32[2,64,128]{2,1,0:T(8,128)S(1)} collective-permute-done((f32[2,64,128]{2,1,0:T(8,128)S(1)}, f32[2,64,128]{2,1,0:T(8,128)S(1)}, u32[]{:S(2)}, u32[]{:S(2)}) %collective-permute-start.14) | collective-permute-done | bytes 65568 | tf_op jit(solution)/shard_map/ppermute | solution.py:602
  65.3 0.0 copy-done.4
  65.3 0.1 sums_kernel.1
  65.4 1.5 %collective-permute-start.15 = (f32[136,128]{1,0:T(8,128)S(1)}, f32[136,128]{1,0:T(8,128)S(1)}, u32[]{:S(2)}, u32[]{:S(2)}) collective-permute-start(f32[136,128]{1,0:T(8,128)S(1)} %get-tuple-element.56.mine), channel_id=1, source_target_pairs={{0,8},{1,9},{2,10},{3,11},{4,12},{5,13},{6,14},{7,15},{8,0},{9,1},... | collective-permute-start | bytes 208904 | tf_op jit(solution)/shard_map/ppermute | solution.py:602
  66.9 0.0 collective-permute-start.16
  66.9 0.6 collective-permute-start.17
  67.5 0.5 collective-permute-done.16.s1
  68.1 1.9 %collective-permute-done.17.s2 = f32[8,128]{1,0:T(8,128)S(1)} collective-permute-done((f32[8,128]{1,0:T(8,128)S(1)}, f32[8,128]{1,0:T(8,128)S(1)}, u32[]{:S(2)}, u32[]{:S(2)}) %collective-permute-start.17) | collective-permute-done | bytes 4128 | tf_op jit(solution)/shard_map/ppermute | solution.py:602
  69.9 0.0 collective-permute-done.15.other
  70.0 1.8 %collective-permute-start.18 = (f32[264,128]{1,0:T(8,128)S(1)}, f32[264,128]{1,0:T(8,128)S(1)}, u32[]{:S(2)}, u32[]{:S(2)}) collective-permute-start(f32[264,128]{1,0:T(8,128)S(1)} %get-tuple-element.58.mine), channel_id=1, source_target_pairs={{0,4},{1,5},{2,6},{3,7},{4,0},{5,1},{6,2},{7,3},{8,12},{9,13},{10,... | collective-permute-start | bytes 405512 | tf_op jit(solution)/shard_map/ppermute | solution.py:602
  71.7 0.4 collective-permute-start.19
  72.2 1.3 %collective-permute-start.20 = (f32[8,128]{1,0:T(8,128)S(1)}, f32[8,128]{1,0:T(8,128)S(1)}, u32[]{:S(2)}, u32[]{:S(2)}) collective-permute-start(f32[8,128]{1,0:T(8,128)S(1)} %get-tuple-element.59.s0), channel_id=1, source_target_pairs={{0,6},{1,7},{2,4},{3,5},{4,2},{5,3},{6,0},{7,1},{8,14},{9,15},{10,... | collective-permute-start | bytes 12296 | tf_op jit(solution)/shard_map/ppermute | solution.py:602
  73.5 1.8 %collective-permute-done.19.s1 = f32[8,128]{1,0:T(8,128)S(1)} collective-permute-done((f32[8,128]{1,0:T(8,128)S(1)}, f32[8,128]{1,0:T(8,128)S(1)}, u32[]{:S(2)}, u32[]{:S(2)}) %collective-permute-start.19) | collective-permute-done | bytes 4128 | tf_op jit(solution)/shard_map/ppermute | solution.py:602
  75.4 1.3 %collective-permute-done.20.s2 = f32[8,128]{1,0:T(8,128)S(1)} collective-permute-done((f32[8,128]{1,0:T(8,128)S(1)}, f32[8,128]{1,0:T(8,128)S(1)}, u32[]{:S(2)}, u32[]{:S(2)}) %collective-permute-start.20) | collective-permute-done | bytes 4128 | tf_op jit(solution)/shard_map/ppermute | solution.py:602
  76.7 0.0 collective-permute-done.18.other
  76.7 0.8 %finish.1 = (f32[8,64,128]{2,1,0:T(8,128)}, f32[1]{0:T(128)}) custom-call(f32[264,128]{1,0:T(8,128)S(1)} %get-tuple-element.58.mine, f32[264,128]{1,0:T(8,128)S(1)} %collective-permute-done.18.other, f32[8,64,128]{2,1,0:T(8,128)S(1)} %copy-done.4, f32[8,128]{1,0:T(8,128)S(1)} %get-tuple-element.59.s0, f32[8,128]{1,0:T(8,128)S(1)} %collective-permute-done.19.s1, ...), custom_call_target="tpu_custom_call" | custom-call | tf_op jit(solution)/shard_map/finish/pallas_call | solution.py:702
  (6 shorter events, 0.1 us)
Async XLA Ops:
  2.8 12.4 %collective-permute-start.2 = (f32[4,64,128]{2,1,0:T(8,128)}, f32[4,64,128]{2,1,0:T(8,128)S(1)}, u32[]{:S(2)}, u32[]{:S(2)}) collective-permute-start(f32[4,64,128]{2,1,0:T(8,128)} %get-tuple-element.35), channel_id=1, source_target_pairs={{0,2},{1,3},{2,0},{3,1},{4,6},{5,7},{6,4},{7,5},{8,10},{9,11},{10,... | collective-permute-start | bytes 393224 | tf_op jit(solution)/shard_map/ppermute | solution.py:602
  5.8 12.1 %copy-start = (f32[2,8,64,128]{3,2,1,0:T(8,128)S(1)}, f32[2,8,64,128]{3,2,1,0:T(8,128)}, u32[]{:S(2)}) copy-start(f32[2,8,64,128]{3,2,1,0:T(8,128)} %first.1) | copy-start | bytes 1572868
  5.8 12.1 %copy-start.1 = (f32[2,8,64,128]{3,2,1,0:T(8,128)S(1)}, f32[2,8,64,128]{3,2,1,0:T(8,128)}, u32[]{:S(2)}) copy-start(f32[2,8,64,128]{3,2,1,0:T(8,128)} %second.1) | copy-start | bytes 1572868
  5.8 12.1 %copy-start.2 = (f32[2,8,64,128]{3,2,1,0:T(8,128)S(1)}, f32[2,8,64,128]{3,2,1,0:T(8,128)}, u32[]{:S(2)}) copy-start(f32[2,8,64,128]{3,2,1,0:T(8,128)} %refs_2_.1) | copy-start | bytes 1572868
  5.8 12.1 %copy-start.3 = (f32[2,8,64,128]{3,2,1,0:T(8,128)S(1)}, f32[2,8,64,128]{3,2,1,0:T(8,128)}, u32[]{:S(2)}) copy-start(f32[2,8,64,128]{3,2,1,0:T(8,128)} %refs_3_.1) | copy-start | bytes 1572868
  5.8 17.7 %copy-start.5 = (f32[8,64,128]{2,1,0:T(8,128)S(1)}, f32[8,64,128]{2,1,0:T(8,128)}, u32[]{:S(2)}) copy-start(f32[8,64,128]{2,1,0:T(8,128)} %get-tuple-element.40.c0) | copy-start | bytes 786436
  5.8 20.0 %copy-start.7 = (s32[2]{0:T(128)S(1)}, s32[2]{0:T(128)}, u32[]{:S(2)}) copy-start(s32[2]{0:T(128)} %sources.1) | copy-start | bytes 28
  5.8 15.9 %collective-permute-start.1 = (f32[2,8,64,128]{3,2,1,0:T(8,128)}, f32[2,8,64,128]{3,2,1,0:T(8,128)S(1)}, u32[]{:S(2)}, u32[]{:S(2)}) collective-permute-start(f32[2,8,64,128]{3,2,1,0:T(8,128)} %get-tuple-element.34), channel_id=1, source_target_pairs={{0,2},{1,3},{2,0},{3,1},{4,6},{5,7},{6,4},{7,5},{8,10},{9,11},{10,... | collective-permute-start | bytes 1572872 | tf_op jit(solution)/shard_map/ppermute | solution.py:602
  15.2 0.7 copy-start.6
  15.9 5.0 %collective-permute-start.3 = (f32[4,64,128]{2,1,0:T(8,128)S(1)}, f32[4,64,128]{2,1,0:T(8,128)S(1)}, u32[]{:S(2)}, u32[]{:S(2)}) collective-permute-start(f32[4,64,128]{2,1,0:T(8,128)S(1)} %after_kernel.1.mine), channel_id=1, source_target_pairs={{0,4},{1,5},{2,6},{3,7},{4,0},{5,1},{6,2},{7,3},{8,12},{9,13},{10,... | collective-permute-start | bytes 393224 | tf_op jit(solution)/shard_map/ppermute | solution.py:602
  19.3 6.5 %collective-permute-start.4 = (f32[2,8,64,128]{3,2,1,0:T(8,128)S(1)}, f32[2,8,64,128]{3,2,1,0:T(8,128)S(1)}, u32[]{:S(2)}, u32[]{:S(2)}) collective-permute-start(f32[2,8,64,128]{3,2,1,0:T(8,128)S(1)} %get-tuple-element.38.own), channel_id=1, source_target_pairs={{0,1},{1,0},{2,3},{3,2},{4,5},{5,4},{6,7},{7,6},{8,9},{9,8},{10,11... | collective-permute-start | bytes 1572872 | tf_op jit(solution)/shard_map/ppermute | solution.py:602
  21.7 4.1 %collective-permute-start.5 = (f32[2,8,64,128]{3,2,1,0:T(8,128)S(1)}, f32[2,8,64,128]{3,2,1,0:T(8,128)S(1)}, u32[]{:S(2)}, u32[]{:S(2)}) collective-permute-start(f32[2,8,64,128]{3,2,1,0:T(8,128)S(1)} %collective-permute-done.1.over), channel_id=1, source_target_pairs={{0,1},{1,0},{2,3},{3,2},{4,5},{5,4},{6,7},{7,6},{8,9},{9,8},{10,11... | collective-permute-start | bytes 1572872 | tf_op jit(solution)/shard_map/ppermute | solution.py:602
  21.7 14.7 %collective-permute-start = (f32[2,8,64,128]{3,2,1,0:T(8,128)}, f32[2,8,64,128]{3,2,1,0:T(8,128)S(1)}, u32[]{:S(2)}, u32[]{:S(2)}) collective-permute-start(f32[2,8,64,128]{3,2,1,0:T(8,128)} %get-tuple-element.33), channel_id=1, source_target_pairs={{0,2},{1,3},{2,0},{3,1},{4,6},{5,7},{6,4},{7,5},{8,10},{9,11},{10,... | collective-permute-start | bytes 1572872 | tf_op jit(solution)/shard_map/ppermute | solution.py:602
  23.5 1.7 %collective-permute-start.6 = (f32[8,64,128]{2,1,0:T(8,128)S(1)}, f32[8,64,128]{2,1,0:T(8,128)}, u32[]{:S(2)}, u32[]{:S(2)}) collective-permute-start(f32[8,64,128]{2,1,0:T(8,128)S(1)} %copy-done.5), channel_id=1, source_target_pairs={{0,1},{1,0},{2,3},{3,2},{4,5},{5,4},{6,7},{7,6},{8,9},{9,8},{10,11... | collective-permute-start | bytes 786440 | tf_op jit(solution)/shard_map/ppermute | solution.py:602
  23.7 2.0 %collective-permute-start.7 = (f32[8,64,128]{2,1,0:T(8,128)}, f32[8,64,128]{2,1,0:T(8,128)}, u32[]{:S(2)}, u32[]{:S(2)}) collective-permute-start(f32[8,64,128]{2,1,0:T(8,128)} %get-tuple-element.41.c2), channel_id=1, source_target_pairs={{0,1},{1,0},{2,3},{3,2},{4,5},{5,4},{6,7},{7,6},{8,9},{9,8},{10,11... | collective-permute-start | bytes 786440 | tf_op jit(solution)/shard_map/ppermute | solution.py:602
  25.2 11.5 %collective-permute-start.8 = (f32[2,8,64,128]{3,2,1,0:T(8,128)S(1)}, f32[2,8,64,128]{3,2,1,0:T(8,128)S(1)}, u32[]{:S(2)}, u32[]{:S(2)}) collective-permute-start(f32[2,8,64,128]{3,2,1,0:T(8,128)S(1)} %get-tuple-element.45.own), channel_id=1, source_target_pairs={{0,1},{1,0},{2,3},{3,2},{4,5},{5,4},{6,7},{7,6},{8,9},{9,8},{10,11... | collective-permute-start | bytes 1572872 | tf_op jit(solution)/shard_map/ppermute | solution.py:602
  36.3 28.9 %copy-start.4 = (f32[8,64,128]{2,1,0:T(8,128)S(1)}, f32[8,64,128]{2,1,0:T(8,128)}, u32[]{:S(2)}) copy-start(f32[8,64,128]{2,1,0:T(8,128)} %momentum.3) | copy-start | bytes 786436
  36.4 2.0 %collective-permute-start.9 = (f32[2,8,64,128]{3,2,1,0:T(8,128)S(1)}, f32[2,8,64,128]{3,2,1,0:T(8,128)S(1)}, u32[]{:S(2)}, u32[]{:S(2)}) collective-permute-start(f32[2,8,64,128]{3,2,1,0:T(8,128)S(1)} %collective-permute-done.over), channel_id=1, source_target_pairs={{0,1},{1,0},{2,3},{3,2},{4,5},{5,4},{6,7},{7,6},{8,9},{9,8},{10,11... | collective-permute-start | bytes 1572872 | tf_op jit(solution)/shard_map/ppermute | solution.py:602
  45.9 6.0 %collective-permute-start.10 = (f32[4,64,128]{2,1,0:T(8,128)S(1)}, f32[4,64,128]{2,1,0:T(8,128)S(1)}, u32[]{:S(2)}, u32[]{:S(2)}) collective-permute-start(f32[4,64,128]{2,1,0:T(8,128)S(1)} %get-tuple-element.51), channel_id=1, source_target_pairs={{0,2},{1,3},{2,0},{3,1},{4,6},{5,7},{6,4},{7,5},{8,10},{9,11},{10,... | collective-permute-start | bytes 393224 | tf_op jit(solution)/shard_map/ppermute | solution.py:602
  47.5 8.1 %collective-permute-start.11 = (f32[4,64,128]{2,1,0:T(8,128)S(1)}, f32[4,64,128]{2,1,0:T(8,128)S(1)}, u32[]{:S(2)}, u32[]{:S(2)}) collective-permute-start(f32[4,64,128]{2,1,0:T(8,128)S(1)} %get-tuple-element.52), channel_id=1, source_target_pairs={{0,4},{1,5},{2,6},{3,7},{4,0},{5,1},{6,2},{7,3},{8,12},{9,13},{10,... | collective-permute-start | bytes 393224 | tf_op jit(solution)/shard_map/ppermute | solution.py:602
  49.1 6.5 %collective-permute-start.12 = (f32[4,64,128]{2,1,0:T(8,128)S(1)}, f32[4,64,128]{2,1,0:T(8,128)S(1)}, u32[]{:S(2)}, u32[]{:S(2)}) collective-permute-start(f32[4,64,128]{2,1,0:T(8,128)S(1)} %get-tuple-element.53), channel_id=1, source_target_pairs={{0,6},{1,7},{2,4},{3,5},{4,2},{5,3},{6,0},{7,1},{8,14},{9,15},{10,... | collective-permute-start | bytes 393224 | tf_op jit(solution)/shard_map/ppermute | solution.py:602
  55.6 4.3 %collective-permute-start.13 = (f32[2,64,128]{2,1,0:T(8,128)S(1)}, f32[2,64,128]{2,1,0:T(8,128)S(1)}, u32[]{:S(2)}, u32[]{:S(2)}) collective-permute-start(f32[2,64,128]{2,1,0:T(8,128)S(1)} %get-tuple-element.55), channel_id=1, source_target_pairs={{0,8},{1,9},{2,10},{3,11},{4,12},{5,13},{6,14},{7,15},{8,0},{9,1},... | collective-permute-start | bytes 196616 | tf_op jit(solution)/shard_map/ppermute | solution.py:602
  60.0 5.3 %collective-permute-start.14 = (f32[2,64,128]{2,1,0:T(8,128)S(1)}, f32[2,64,128]{2,1,0:T(8,128)S(1)}, u32[]{:S(2)}, u32[]{:S(2)}) collective-permute-start(f32[2,64,128]{2,1,0:T(8,128)S(1)} %add_kernel.1.mine), channel_id=1, source_target_pairs={{0,16},{1,17},{2,18},{3,19},{4,20},{5,21},{6,22},{7,23},{8,24},{9,... | collective-permute-start | bytes 196616 | tf_op jit(solution)/shard_map/ppermute | solution.py:602
  65.4 4.6 %collective-permute-start.15 = (f32[136,128]{1,0:T(8,128)S(1)}, f32[136,128]{1,0:T(8,128)S(1)}, u32[]{:S(2)}, u32[]{:S(2)}) collective-permute-start(f32[136,128]{1,0:T(8,128)S(1)} %get-tuple-element.56.mine), channel_id=1, source_target_pairs={{0,8},{1,9},{2,10},{3,11},{4,12},{5,13},{6,14},{7,15},{8,0},{9,1},... | collective-permute-start | bytes 208904 | tf_op jit(solution)/shard_map/ppermute | solution.py:602
  66.9 1.2 %collective-permute-start.16 = (f32[8,128]{1,0:T(8,128)S(1)}, f32[8,128]{1,0:T(8,128)S(1)}, u32[]{:S(2)}, u32[]{:S(2)}) collective-permute-start(f32[8,128]{1,0:T(8,128)S(1)} %get-tuple-element.57.s0), channel_id=1, source_target_pairs={{0,1},{1,0},{2,3},{3,2},{4,5},{5,4},{6,7},{7,6},{8,9},{9,8},{10,11... | collective-permute-start | bytes 12296 | tf_op jit(solution)/shard_map/ppermute | solution.py:602
  66.9 3.0 %collective-permute-start.17 = (f32[8,128]{1,0:T(8,128)S(1)}, f32[8,128]{1,0:T(8,128)S(1)}, u32[]{:S(2)}, u32[]{:S(2)}) collective-permute-start(f32[8,128]{1,0:T(8,128)S(1)} %get-tuple-element.57.s0), channel_id=1, source_target_pairs={{0,9},{1,8},{2,11},{3,10},{4,13},{5,12},{6,15},{7,14},{8,1},{9,0},... | collective-permute-start | bytes 12296 | tf_op jit(solution)/shard_map/ppermute | solution.py:602
  70.0 6.7 %collective-permute-start.18 = (f32[264,128]{1,0:T(8,128)S(1)}, f32[264,128]{1,0:T(8,128)S(1)}, u32[]{:S(2)}, u32[]{:S(2)}) collective-permute-start(f32[264,128]{1,0:T(8,128)S(1)} %get-tuple-element.58.mine), channel_id=1, source_target_pairs={{0,4},{1,5},{2,6},{3,7},{4,0},{5,1},{6,2},{7,3},{8,12},{9,13},{10,... | collective-permute-start | bytes 405512 | tf_op jit(solution)/shard_map/ppermute | solution.py:602
  71.7 3.6 %collective-permute-start.19 = (f32[8,128]{1,0:T(8,128)S(1)}, f32[8,128]{1,0:T(8,128)S(1)}, u32[]{:S(2)}, u32[]{:S(2)}) collective-permute-start(f32[8,128]{1,0:T(8,128)S(1)} %get-tuple-element.59.s0), channel_id=1, source_target_pairs={{0,2},{1,3},{2,0},{3,1},{4,6},{5,7},{6,4},{7,5},{8,10},{9,11},{10,... | collective-permute-start | bytes 12296 | tf_op jit(solution)/shard_map/ppermute | solution.py:602
  72.2 4.5 %collective-permute-start.20 = (f32[8,128]{1,0:T(8,128)S(1)}, f32[8,128]{1,0:T(8,128)S(1)}, u32[]{:S(2)}, u32[]{:S(2)}) collective-permute-start(f32[8,128]{1,0:T(8,128)S(1)} %get-tuple-element.59.s0), channel_id=1, source_target_pairs={{0,6},{1,7},{2,4},{3,5},{4,2},{5,3},{6,0},{7,1},{8,14},{9,15},{10,... | collective-permute-start | bytes 12296 | tf_op jit(solution)/shard_map/ppermute | solution.py:602

commit v8 on v7

--- a/solution.py
+++ b/solution.py
@@ -158,38 +158,37 @@
         interleave(outs[n // 2], (n % 2,), held.at[n])
 
 
-def pick(*pairs, after):
+def pick(*pairs, earlier):
     plain = functools.partial(pick_kernel, tuple(pair[2] for pair in pairs))
     fields = [field for pair in pairs for field in pair[:2]]
     shape = fields[0].shape[1:]
     vmem, hbm = pl.BlockSpec(memory_space=pltpu.VMEM), pl.BlockSpec(memory_space=pltpu.HBM)
     return pl.pallas_call(
-        lambda mark, *refs: plain(*refs),
-        in_specs=[vmem] + [hbm] * len(fields),
+        lambda earlier, *refs: plain(*refs),
+        in_specs=[pl.BlockSpec(memory_space=pl.ANY)] + [hbm] * len(fields),
         out_specs=[vmem] * len(pairs),
         out_shape=[jax.ShapeDtypeStruct((2, *shape), jnp.float32)] * len(pairs),
         scratch_shapes=[pltpu.VMEM((len(fields), *shape), jnp.float32), pltpu.SemaphoreType.DMA((len(fields),))],
         compiler_params=pltpu.CompilerParams(vmem_limit_bytes=4 * 2**20),
         name="pick",
-    )(after, *fields)
-
-
-def first_kernel(first, second, courant, outgoing, whole, piece, held, held_courant, sems):
+    )(earlier, *fields)
+
+
+def first_kernel(first, second, courant, outgoing, whole, piece, held_courant, sems):
     shot = 1 - lax.axis_index("chip")
     copies = [
-        pltpu.make_async_copy(first.at[shot], held.at[0], sems.at[0]),
-        pltpu.make_async_copy(second.at[shot], held.at[1], sems.at[1]),
-        pltpu.make_async_copy(courant, held_courant, sems.at[2]),
+        pltpu.make_async_copy(courant, held_courant, sems.at[0]),
+        pltpu.make_async_copy(first.at[shot], outgoing.at[0], sems.at[1]),
+        pltpu.make_async_copy(second.at[shot], outgoing.at[1], sems.at[2]),
     ]
     for copy in copies:
         copy.start()
-    for n in range(2):
-        copies[n].wait()
-        interleave(outgoing, (n,), held.at[n])
-    copies[2].wait()
+    copies[0].wait()
     interleave(whole, (), held_courant, 1.0 / 12.0)
     count = piece.shape[0]
     piece[...] = whole[pl.ds(lax.axis_index("shot") % 2 * count, count)]
+    copies[1].wait()
+    copies[2].wait()
 
 
 def band(lanes):
@@ -295,8 +294,6 @@
     _, steps, receivers = observed.shape
     rows_all = planes_all * rows_x
     tile = 512
-    mark = jax.ShapeDtypeStruct((8, rows_y), jnp.float32)
-    mark_block = pl.BlockSpec((8, rows_y), lambda t: (0, 0))
     return pl.pallas_call(
         functools.partial(scatter_kernel, rows_x),
         grid=(rows_all // tile,),
@@ -304,8 +301,14 @@
             pl.BlockSpec((2, receivers), lambda t: (0, 0)),
             pl.BlockSpec((2, steps, receivers), lambda t: (0, 0, 0)),
         ],
-        out_specs=[pl.BlockSpec((steps + 1, tile, rows_y), lambda t: (0, t, 0)), mark_block],
-        out_shape=[jax.ShapeDtypeStruct((steps + 1, rows_all, rows_y), jnp.float32), mark],
+        out_specs=[
+            pl.BlockSpec((steps + 1, tile, rows_y), lambda t: (0, t, 0)),
+            pl.BlockSpec((8, rows_y), lambda t: (0, 0)),
+        ],
+        out_shape=[
+            jax.ShapeDtypeStruct((steps + 1, rows_all, rows_y), jnp.float32),
+            jax.ShapeDtypeStruct((8, rows_y), jnp.float32),
+        ],
         scratch_shapes=[
             pltpu.VMEM((1, receivers), jnp.int32),
             pltpu.VMEM((2 * receivers, (steps + 1) * rows_y), jnp.bfloat16),
@@ -326,18 +329,25 @@
     return chip, core, [slab * planes for slab in slabs]
 
 
-def load_blocks(slabs, blocks, first, second):
-    ends = first.shape[0]
-    planes = blocks[0].shape[1]
+def load_blocks(slabs, blocks, first, second, raw=False, factor=None):
+    ends, rows, lanes = first.shape
+    planes, groups = blocks[0].shape[1], rows // 8
     for field in (first, second):
         for z in (0, 1, ends - 2, ends - 1):
-            field[z] = jnp.zeros(field.shape[1:], jnp.float32)
-    for slab, block in zip(slabs, blocks):
+            field[z] = jnp.zeros((rows, lanes), jnp.float32)
+    for b, (slab, block) in enumerate(zip(slabs, blocks)):
 
         @pl.loop(0, planes)
         def _(p):
-            first[slab + p + 2] = block[0, p]
-            second[slab + p + 2] = block[1, p]
+            for n, field in enumerate((first, second)):
+                if raw and b >= 2:
+                    tiles = [block[n, p, pl.ds(i, 8, stride=groups), :] for i in range(groups)]
+                    value = jnp.concatenate(tiles, 0)
+                else:
+                    value = block[n, p]
+                if factor is not None:
+                    value = value * factor[slab + p]
+                field[slab + p + 2] = value
 
 
 BATCH = 4
@@ -364,14 +374,13 @@
 
 
 def forward_kernel(
-    start, sources, arranged, own, mate, over, far, c0, c1, c2, c3, placed, laps, inject, cour, mark, even, odd, banded, y0, y1,
+    start, sources, own, mate, over, far, c0, c1, p0, p1, p2, p3, placed, laps, inject, cour, last, even, odd, banded, y0, y1,
     traces_even, traces_odd, counts, sems
 ):
     planes, rows, lanes = c0.shape
     steps = laps.shape[0]
     groups = rows // 8
     chip_here, core, slabs = place(planes)
-    mark[...] = jnp.zeros(mark.shape, jnp.float32)
 
     def copy(k, slot):
         return pltpu.make_async_copy(placed.at[k], (traces_even, traces_odd)[slot], sems.at[slot])
@@ -381,12 +390,21 @@
     count_copy.start()
     copy(1, 1).start()
     banded[...] = band(lanes)
-    load_blocks(slabs, (own, mate, over, far), odd, even)
-    for slab, block in zip(slabs, (c0, c1, c2, c3)):
-
-        @pl.loop(0, planes)
+    load_blocks(slabs, (own, mate, over, far), odd, even, raw=True)
+    mine = lax.axis_index("shot") % 2 * (planes // 2)
+    other = planes // 2 - mine
+    courant_at = (slabs[0], slabs[1], slabs[2] + mine, slabs[2] + other, slabs[3] + mine, slabs[3] + other)
+    for z, block in zip(courant_at, (c0, c1, p0, p1, p2, p3)):
+
+        @pl.loop(0, block.shape[0])
         def _(p):
-            cour[slab + p] = block[p]
+            cour[z + p] = block[p]
+
+    @pl.loop(0, 2 * planes)
+    def _(index):
+        z = (2 * (index // planes) + core) * planes + index % planes
+        weight = 1.0 + 2.0 * jnp.full((rows, lanes), z, jnp.int32).astype(jnp.float32) / (4 * planes - 1)
+        last[index] = weight / (12.0 * cour[z])
 
     cell = sources[chip_here]
     source_z, x, lane = cell // (rows * lanes), cell // lanes % rows, cell % lanes
@@ -413,24 +431,22 @@
 
             laps12(now, z, y_part, fetch, finish)
 
-        sweep(core, planes, now, banded, y0, y1, work)
-
-        @pl.when(k + 2 < steps)
-        def _():
-            copy(k + 2, slot).start()
-
         cycle = (start[0] + k) % 48
         phase = (jnp.full((8, lanes), cycle, jnp.int32).astype(jnp.float32) - 24.0) / 12.0
         wave = AMPLITUDE * (1.0 - 2.0 * phase * phase) * jnp.exp(-phase * phase)
         strength = jnp.where(here, 12.0 * wave, 0.0)
-
-        @pl.when(lax.rem(source_slab, 2) == core)
-        def _():
-            laps[k, source_p, source_slab // 2, tile, :] += strength
-
         moved = cour[source_z, tile, :] * strength
+
+        sweep(core, planes, now, banded, y0, y1, work)
+
+        owned = jnp.where(lax.rem(source_slab, 2) == core, strength, 0.0)
+        laps[k, source_p, source_slab // 2, tile, :] += owned
         then[source_z + 2, tile, :] += moved
         inject[k, source_z, tile, :] -= counts[source_z, tile, :] * moved
+
+        @pl.when(k + 2 < steps)
+        def _():
+            copy(k + 2, slot).start()
 
     count_copy.wait()
 
@@ -440,18 +456,13 @@
         advance(2 * pair + 1, odd, even, traces_odd, 1)
 
 
-def adjoint_kernel(mark, own, mate, over, far, cour, laps, inject, keep, send_x, send_y, send_xy, even, odd, total, banded, y0, y1):
+def adjoint_kernel(own, mate, over, far, cour, laps, inject, last, keep, send_x, send_y, send_xy, even, odd, total, banded, y0, y1):
     planes, rows, lanes = own.shape[1:]
     steps = laps.shape[0]
     groups = rows // 8
     chip_here, core, slabs = place(planes)
     banded[...] = band(lanes)
-    load_blocks(slabs, (own, mate, over, far), odd, even)
-
-    @pl.loop(0, 4 * planes)
-    def _(z):
-        even[z + 2] = even[z + 2] * cour[z]
-        odd[z + 2] = odd[z + 2] * cour[z]
+    load_blocks(slabs, (own, mate, over, far), odd, even, factor=cour)
 
     @pl.loop(0, 2 * planes)
     def _(index):
@@ -488,9 +499,7 @@
         @pl.loop(0, count)
         def _(n):
             p = start + n
-            z = (2 * chip + core) * planes + p
-            weight = 1.0 + 2.0 * jnp.full((rows, lanes), z, jnp.int32).astype(jnp.float32) / (4 * planes - 1)
-            value = weight * total[chip * planes + p] / (12.0 * cour[z])
+            value = total[chip * planes + p] * last[chip * planes + p]
             for i in range(groups):
                 ref[n, pl.ds(i, 8, stride=groups), :] = value[i * 8 : (i + 1) * 8]
 
@@ -516,16 +525,20 @@
     return result
 
 
-def after_kernel(mark, value, out):
+def after_kernel(earlier, value, out):
     out[...] = value[...]
 
 
-def arrange_kernel(mine, other, out, mark):
-    mark[...] = jnp.zeros(mark.shape, jnp.float32)
-    y = lax.axis_index("shot") % 2
-    count = mine.shape[0]
-    out[pl.ds(y * count, count)] = mine[...]
-    out[pl.ds((1 - y) * count, count)] = other[...]
+def after(earlier, value):
+    vmem, anywhere = pl.BlockSpec(memory_space=pltpu.VMEM), pl.BlockSpec(memory_space=pl.ANY)
+    return pl.pallas_call(
+        after_kernel,
+        in_specs=[anywhere, vmem],
+        out_specs=vmem,
+        out_shape=jax.ShapeDtypeStruct(value.shape, jnp.float32),
+        compiler_params=pltpu.CompilerParams(vmem_limit_bytes=4 * 2**20),
+        name="after",
+    )(earlier, value)
 
 
 def first_plane(shot, planes):
@@ -618,14 +631,13 @@
     outgoing, c0, piece = pl.pallas_call(
         first_kernel,
         in_specs=[hbm] * 3,
-        out_specs=[vmem] * 3,
+        out_specs=[hbm, vmem, vmem],
         out_shape=[
             jax.ShapeDtypeStruct((2, planes, rows_x, rows_y), jnp.float32),
             jax.ShapeDtypeStruct(courant_sq.shape, jnp.float32),
             jax.ShapeDtypeStruct((planes // 2, rows_x, rows_y), jnp.float32),
         ],
         scratch_shapes=[
-            pltpu.VMEM((2, planes, rows_x, rows_y), jnp.float32),
             pltpu.VMEM(courant_sq.shape, jnp.float32),
             pltpu.SemaphoreType.DMA((3,)),
         ],
@@ -640,13 +652,13 @@
     placed = placed.reshape(steps + 1, planes_all, rows_x, rows_y)
 
     adj_outgoing, adj_own, own = pick(
-        (adj_next, adj_cur, True), (adj_next, adj_cur, False), (fwd_prev, fwd_cur, False), after=mark
+        (adj_next, adj_cur, True), (adj_next, adj_cur, False), (fwd_prev, fwd_cur, False), earlier=mark
     )
     mate = exchange(own, CORE)
-    piece = local(after_kernel, [piece.shape], mark, piece)
-    c2, arranged = local(arrange_kernel, [courant_sq.shape, (8, rows_y)], piece, exchange(piece, Y))
-    c1, c3 = exchange(c0, CORE), exchange(c2, CORE)
-    over, arranged = lax.optimization_barrier((over, arranged))
+    piece = after(adj_own, piece)
+    pieces = [piece, exchange(piece, Y), exchange(piece, CORE), exchange(piece, Y + CORE)]
+    c1 = exchange(c0, CORE)
+    over = after(pieces[3], over)
     far = exchange(over, CORE)
     adj_over = exchange(adj_outgoing, CHIP)
     adj_mate = exchange(adj_own, CORE)
@@ -657,36 +669,36 @@
     step_scratch = [scratch, scratch, pltpu.VMEM((2 * rows_y, rows_y), jnp.bfloat16), y_scratch, y_scratch]
     params = pltpu.CompilerParams(vmem_limit_bytes=6 * 2**20)
     cost = pl.CostEstimate(flops=30 * steps * cells_all, bytes_accessed=16 * steps * cells_all, transcendentals=0)
-    laps, inject, cour, mark = pl.pallas_call(
+    laps, inject, cour, last = pl.pallas_call(
         forward_kernel,
-        in_specs=[smem, smem, pl.BlockSpec(memory_space=pl.ANY)] + [vmem] * 8 + [pl.BlockSpec(memory_space=pltpu.HBM)],
+        in_specs=[smem, smem] + [vmem] * 10 + [pl.BlockSpec(memory_space=pltpu.HBM)],
         out_specs=[vmem] * 4,
         out_shape=[
             jax.ShapeDtypeStruct((steps, planes, 2, rows_x, rows_y), jnp.float32),
             jax.ShapeDtypeStruct((steps, planes_all, rows_x, rows_y), jnp.float32),
             jax.ShapeDtypeStruct((planes_all, rows_x, rows_y), jnp.float32),
-            jax.ShapeDtypeStruct((8, rows_y), jnp.float32),
+            jax.ShapeDtypeStruct((2 * planes, rows_x, rows_y), jnp.float32),
         ],
         scratch_shapes=step_scratch + [whole, whole, whole, pltpu.SemaphoreType.DMA((3,))],
         compiler_params=pltpu.CompilerParams(vmem_limit_bytes=33 * 2**20),
-        cost_estimate=cost,
+        cost_estimate=pl.CostEstimate(flops=1000, bytes_accessed=1000, transcendentals=0),
         name="forward_steps",
-    )(ckpt_step[None], src_cells, arranged, own, mate, over, far, c0, c1, c2, c3, placed)
-
-    adj_over, mark = lax.optimization_barrier((adj_over, mark))
+    )(ckpt_step[None], src_cells, own, mate, over, far, c0, c1, *pieces, placed)
+
+    adj_over = after(laps, adj_over)
     adj_far = exchange(adj_over, CORE)
     slab = jax.ShapeDtypeStruct(courant_sq.shape, jnp.float32)
     half, quarter = (planes // 2, rows_x, rows_y), (planes // 4, rows_x, rows_y)
     keep, send_x, send_y, send_xy = pl.pallas_call(
         adjoint_kernel,
-        in_specs=[pl.BlockSpec(memory_space=pl.ANY)] + [vmem] * 7,
+        in_specs=[vmem] * 8,
         out_specs=[vmem] * 4,
         out_shape=[jax.ShapeDtypeStruct(half, jnp.float32)] * 4,
         scratch_shapes=step_scratch[:2] + [pltpu.VMEM((2 * planes, rows_x, rows_y), jnp.float32)] + step_scratch[2:],
         compiler_params=params,
         cost_estimate=cost,
         name="adjoint_steps",
-    )(mark, adj_own, adj_mate, adj_over, adj_far, cour, laps, inject)
+    )(adj_own, adj_mate, adj_over, adj_far, cour, laps, inject, last)
 
     by_xy, by_x, by_y = exchange(send_xy, CHIP + Y), exchange(send_x, CHIP), exchange(send_y, Y)
     keep, send = local(square_kernel, [quarter] * 2, keep, by_x, by_y, by_xy)

time: 77.8 us -> 101 us (1.30)
  Pallas kernels: 32.5 us -> 48.5 us
  waiting for transfers between devices: 21.2 us -> 26.9 us
  starting transfers between devices: 21.6 us -> 22.7 us
    pallas_call x4 -> x7, Pallas kernels: 21.5 us -> 38.3 us  [the longest x1 17.8 us: whole_shards(): pl.pallas_call(first_kernel, in_specs=[hbm] * 3, out_specs=[hbm, vmem, vm...]
    ppermute x21 -> x22, waiting for transfers between devices: 21.2 us -> 26.9 us  [exchange(): lax.ppermute(value, axes, [(i, i ^ bits) for i in range(lax.axis_size(axe...]
    ppermute x21 -> x22, starting transfers between devices: 21.6 us -> 22.7 us  [exchange(): lax.ppermute(value, axes, [(i, i ^ bits) for i in range(lax.axis_size(axe...]
  transfers between devices with their start and end apart: 21 -> 22, of which waited for: 12 -> 12; matrix products, arithmetic and copies ran while one was open for 0% -> 0% of each run, Pallas kernels for 28% -> 21%
where the time goes in v8:
time: 101 us; the launch traced here: 100 us
  Pallas kernels  48.5 us (48%)
  waiting for transfers between devices  26.9 us (27%)
  starting transfers between devices  22.7 us (22%)
  between operations  1.43 us (1%)
    ppermute x22, waiting for transfers between devices, exchange(): lax.ppermute(value, axes, [(i, i ^ bits) for i in range(lax.axis_size(axe...  26.9 us
    ppermute x22, starting transfers between devices, exchange(): lax.ppermute(value, axes, [(i, i ^ bits) for i in range(lax.axis_size(axe...  22.7 us
    pallas_call x1, Pallas kernels, whole_shards(): pl.pallas_call(first_kernel, in_specs=[hbm] * 3, out_specs=[hbm, vmem, vm...  17.8 us
    pallas_call x1, Pallas kernels, whole_shards(): pl.pallas_call(forward_kernel, in_specs=[smem, smem] + [vmem] * 10 + [pl....  10.8 us
    pallas_call x1, Pallas kernels, scatter(): pl.pallas_call(functools.partial(scatter_kernel, rows_x), grid=(rows_all...  9.27 us
    pallas_call x1, Pallas kernels, whole_shards(): pl.pallas_call(adjoint_kernel, in_specs=[vmem] * 8, out_specs=[vmem] * 4,...  8.33 us
  transfers between devices with their start and end apart: 22, of which 12 were waited for; matrix products, arithmetic and copies ran while one was open for 0% of the time, Pallas kernels for 21%

profile of v8, /device:TPU:0, one launch (start us, length us, event | category | flops | bytes accessed | tf_op | source)
XLA Modules:
  0.0 100.3 jit_solution(14008262594723654766)
XLA Ops:
  0.6 17.8 %first_to_cross.1 = (f32[2,8,64,128]{3,2,1,0:T(8,128)}, f32[8,64,128]{2,1,0:T(8,128)}, f32[4,64,128]{2,1,0:T(8,128)}) custom-call(f32[2,8,64,128]{3,2,1,0:T(8,128)} %first.1, f32[2,8,64,128]{3,2,1,0:T(8,128)} %second.1, f32[8,64,128]{2,1,0:T(8,128)} %courant.1), custom_call_target="tpu_custom_call" | custom-call | tf_op jit(solution)/shard_map/first_to_cross/pallas_call | solution.py:631
  18.4 3.0 %collective-permute-start.2 = (f32[4,64,128]{2,1,0:T(8,128)}, f32[4,64,128]{2,1,0:T(8,128)S(1)}, u32[]{:S(2)}, u32[]{:S(2)}) collective-permute-start(f32[4,64,128]{2,1,0:T(8,128)} %get-tuple-element.29), channel_id=1, source_target_pairs={{0,2},{1,3},{2,0},{3,1},{4,6},{5,7},{6,4},{7,5},{8,10},{9,11},{10,... | collective-permute-start | bytes 393224 | tf_op jit(solution)/shard_map/ppermute | solution.py:615
  21.4 0.0 copy-start
  21.4 0.0 copy-start.1
  21.4 0.0 copy-start.2
  21.4 0.0 copy-start.3
  21.4 0.0 copy-start.6
  21.4 0.1 collective-permute-start.4
  21.5 9.3 %receiver_scatter.1 = (f32[9,2048,128]{2,1,0:T(8,128)}, f32[8,128]{1,0:T(8,128)}) custom-call(s32[2,512]{1,0:T(2,128)} %cells_ref.1, f32[2,8,512]{2,1,0:T(8,128)} %observed_ref.1), custom_call_target="tpu_custom_call" | custom-call | flops 4831838208 | bytes 9437184 | tf_op jit(solution)/shard_map/receiver_scatter/pallas_call | solution.py:297
  30.8 0.0 copy-done
  30.8 0.0 copy-done.1
  30.8 0.0 copy-done.2
  30.8 0.0 copy-done.3
  30.8 0.0 copy-start.5
  30.8 0.7 copy-done.5
  31.5 1.3 %pick.1 = (f32[2,8,64,128]{3,2,1,0:T(8,128)}, f32[2,8,64,128]{3,2,1,0:T(8,128)S(1)}, f32[2,8,64,128]{3,2,1,0:T(8,128)S(1)}) custom-call(f32[8,128]{1,0:T(8,128)S(1)} %copy-done.5, f32[2,8,64,128]{3,2,1,0:T(8,128)S(1)} %copy-done.2, f32[2,8,64,128]{3,2,1,0:T(8,128)S(1)} %copy-done.3, f32[2,8,64,128]{3,2,1,0:T(8,128)S(1)} %copy-done.2, ...), custom_call_target="tpu_custom_call" | custom-call | tf_op jit(solution)/shard_map/pick/pallas_call | solution.py:166
  32.8 0.0 collective-permute-done.2.value
  32.9 1.0 collective-permute-start.3
  33.9 1.1 %collective-permute-start.1 = (f32[2,8,64,128]{3,2,1,0:T(8,128)S(1)}, f32[2,8,64,128]{3,2,1,0:T(8,128)S(1)}, u32[]{:S(2)}, u32[]{:S(2)}) collective-permute-start(f32[2,8,64,128]{3,2,1,0:T(8,128)S(1)} %get-tuple-element.28.own), channel_id=1, source_target_pairs={{0,1},{1,0},{2,3},{3,2},{4,5},{5,4},{6,7},{7,6},{8,9},{9,8},{10,11... | collective-permute-start | bytes 1572872 | tf_op jit(solution)/shard_map/ppermute | solution.py:615
  35.0 3.4 %collective-permute-done.3.earlier.p3 = f32[4,64,128]{2,1,0:T(8,128)S(1)} collective-permute-done((f32[4,64,128]{2,1,0:T(8,128)S(1)}, f32[4,64,128]{2,1,0:T(8,128)S(1)}, u32[]{:S(2)}, u32[]{:S(2)}) %collective-permute-start.3) | collective-permute-done | bytes 131104 | tf_op jit(solution)/shard_map/ppermute | solution.py:615
  38.3 0.0 collective-permute-done.4.value
  38.4 0.3 collective-permute-start.5
  38.7 2.1 %collective-permute-start.9 = (f32[2,8,64,128]{3,2,1,0:T(8,128)}, f32[2,8,64,128]{3,2,1,0:T(8,128)S(1)}, u32[]{:S(2)}, u32[]{:S(2)}) collective-permute-start(f32[2,8,64,128]{3,2,1,0:T(8,128)} %get-tuple-element.34), channel_id=1, source_target_pairs={{0,2},{1,3},{2,0},{3,1},{4,6},{5,7},{6,4},{7,5},{8,10},{9,11},{10,... | collective-permute-start | bytes 1572872 | tf_op jit(solution)/shard_map/ppermute | solution.py:615
  40.8 1.0 collective-permute-start.7
  41.7 0.0 collective-permute-start.6
  41.7 4.5 %collective-permute-done.7.p1 = f32[4,64,128]{2,1,0:T(8,128)S(1)} collective-permute-done((f32[4,64,128]{2,1,0:T(8,128)S(1)}, f32[4,64,128]{2,1,0:T(8,128)S(1)}, u32[]{:S(2)}, u32[]{:S(2)}) %collective-permute-start.7) | collective-permute-done | bytes 131104 | tf_op jit(solution)/shard_map/ppermute | solution.py:615
  46.2 0.0 collective-permute-start.8
  46.9 0.8 collective-permute-done.8.p2
  47.7 0.1 collective-permute-start
  47.9 0.0 collective-permute-done.6.c1
  47.9 0.0 collective-permute-done.1.mate
  47.9 0.0 collective-permute-done.5.far
  47.9 0.0 copy-done.6
  47.9 10.8 %forward_steps.1 = (f32[8,8,2,64,128]{4,3,2,1,0:T(8,128)S(1)}, f32[8,32,64,128]{3,2,1,0:T(8,128)S(1)}, f32[32,64,128]{2,1,0:T(8,128)S(1)}, f32[16,64,128]{2,1,0:T(8,128)S(1)}) custom-call(s32[1]{0:T(128)} %bitcast.3.start, s32[2]{0:T(128)S(1)} %copy-done.6, f32[2,8,64,128]{3,2,1,0:T(8,128)S(1)} %get-tuple-element.28.own, ...), custom_call_target="tpu_custom_call" | custom-call | flops 1000 | bytes 1000 | tf_op jit(solution)/shard_map/forward_steps/pallas_call | solution.py:672
  58.7 0.0 collective-permute-done.9.value
  58.8 0.4 collective-permute-start.10
  59.2 0.0 collective-permute-done.mate
  59.2 1.5 %collective-permute-done.10.far = f32[2,8,64,128]{3,2,1,0:T(8,128)S(1)} collective-permute-done((f32[2,8,64,128]{3,2,1,0:T(8,128)S(1)}, f32[2,8,64,128]{3,2,1,0:T(8,128)S(1)}, u32[]{:S(2)}, u32[]{:S(2)}) %collective-permute-start.10) | collective-permute-done | bytes 524320 | tf_op jit(solution)/shard_map/ppermute | solution.py:615
  60.8 8.3 %adjoint_steps.1 = (f32[4,64,128]{2,1,0:T(8,128)S(1)}, f32[4,64,128]{2,1,0:T(8,128)S(1)}, f32[4,64,128]{2,1,0:T(8,128)S(1)}, f32[4,64,128]{2,1,0:T(8,128)S(1)}) custom-call(f32[2,8,64,128]{3,2,1,0:T(8,128)S(1)} %get-tuple-element.27.earlier.own, f32[2,8,64,128]{3,2,1,0:T(8,128)S(1)} %collective-permute-done.mate, f32[2,8,64,128]{3,2,1,0:T(8,128)S(1)} %after.5.over, ...), custom_call_target="tpu_custom_call" | custom-call | flops 62914560 | bytes 33554432 | tf_op jit(solution)/shard_map/adjoint_steps/pallas_call | solution.py:692
  69.1 0.4 collective-permute-start.11
  69.5 1.5 %collective-permute-start.12 = (f32[4,64,128]{2,1,0:T(8,128)S(1)}, f32[4,64,128]{2,1,0:T(8,128)S(1)}, u32[]{:S(2)}, u32[]{:S(2)}) collective-permute-start(f32[4,64,128]{2,1,0:T(8,128)S(1)} %get-tuple-element.40), channel_id=1, source_target_pairs={{0,4},{1,5},{2,6},{3,7},{4,0},{5,1},{6,2},{7,3},{8,12},{9,13},{10,... | collective-permute-start | bytes 393224 | tf_op jit(solution)/shard_map/ppermute | solution.py:615
  70.9 1.7 %collective-permute-start.13 = (f32[4,64,128]{2,1,0:T(8,128)S(1)}, f32[4,64,128]{2,1,0:T(8,128)S(1)}, u32[]{:S(2)}, u32[]{:S(2)}) collective-permute-start(f32[4,64,128]{2,1,0:T(8,128)S(1)} %get-tuple-element.41), channel_id=1, source_target_pairs={{0,6},{1,7},{2,4},{3,5},{4,2},{5,3},{6,0},{7,1},{8,14},{9,15},{10,... | collective-permute-start | bytes 393224 | tf_op jit(solution)/shard_map/ppermute | solution.py:615
  72.7 2.8 %collective-permute-done.11.by_x = f32[4,64,128]{2,1,0:T(8,128)S(1)} collective-permute-done((f32[4,64,128]{2,1,0:T(8,128)S(1)}, f32[4,64,128]{2,1,0:T(8,128)S(1)}, u32[]{:S(2)}, u32[]{:S(2)}) %collective-permute-start.11) | collective-permute-done | bytes 131104 | tf_op jit(solution)/shard_map/ppermute | solution.py:615
  75.5 0.0 collective-permute-done.12.by_y
  75.5 2.7 %collective-permute-done.13.by_xy = f32[4,64,128]{2,1,0:T(8,128)S(1)} collective-permute-done((f32[4,64,128]{2,1,0:T(8,128)S(1)}, f32[4,64,128]{2,1,0:T(8,128)S(1)}, u32[]{:S(2)}, u32[]{:S(2)}) %collective-permute-start.13) | collective-permute-done | bytes 131104 | tf_op jit(solution)/shard_map/ppermute | solution.py:615
  78.3 1.6 %collective-permute-start.14 = (f32[2,64,128]{2,1,0:T(8,128)S(1)}, f32[2,64,128]{2,1,0:T(8,128)S(1)}, u32[]{:S(2)}, u32[]{:S(2)}) collective-permute-start(f32[2,64,128]{2,1,0:T(8,128)S(1)} %get-tuple-element.43), channel_id=1, source_target_pairs={{0,8},{1,9},{2,10},{3,11},{4,12},{5,13},{6,14},{7,15},{8,0},{9,1},... | collective-permute-start | bytes 196616 | tf_op jit(solution)/shard_map/ppermute | solution.py:615
  79.9 2.7 %collective-permute-done.14.other = f32[2,64,128]{2,1,0:T(8,128)S(1)} collective-permute-done((f32[2,64,128]{2,1,0:T(8,128)S(1)}, f32[2,64,128]{2,1,0:T(8,128)S(1)}, u32[]{:S(2)}, u32[]{:S(2)}) %collective-permute-start.14) | collective-permute-done | bytes 65568 | tf_op jit(solution)/shard_map/ppermute | solution.py:615
  82.6 2.7 %collective-permute-start.15 = (f32[2,64,128]{2,1,0:T(8,128)S(1)}, f32[2,64,128]{2,1,0:T(8,128)S(1)}, u32[]{:S(2)}, u32[]{:S(2)}) collective-permute-start(f32[2,64,128]{2,1,0:T(8,128)S(1)} %add_kernel.1.mine), channel_id=1, source_target_pairs={{0,16},{1,17},{2,18},{3,19},{4,20},{5,21},{6,22},{7,23},{8,24},{9,... | collective-permute-start | bytes 196616 | tf_op jit(solution)/shard_map/ppermute | solution.py:615
  85.3 2.6 %collective-permute-done.15.other = f32[2,64,128]{2,1,0:T(8,128)S(1)} collective-permute-done((f32[2,64,128]{2,1,0:T(8,128)S(1)}, f32[2,64,128]{2,1,0:T(8,128)S(1)}, u32[]{:S(2)}, u32[]{:S(2)}) %collective-permute-start.15) | collective-permute-done | bytes 65568 | tf_op jit(solution)/shard_map/ppermute | solution.py:615
  87.8 0.0 copy-done.4
  87.8 0.1 sums_kernel.1
  87.9 1.6 %collective-permute-start.16 = (f32[136,128]{1,0:T(8,128)S(1)}, f32[136,128]{1,0:T(8,128)S(1)}, u32[]{:S(2)}, u32[]{:S(2)}) collective-permute-start(f32[136,128]{1,0:T(8,128)S(1)} %get-tuple-element.44.mine), channel_id=1, source_target_pairs={{0,8},{1,9},{2,10},{3,11},{4,12},{5,13},{6,14},{7,15},{8,0},{9,1},... | collective-permute-start | bytes 208904 | tf_op jit(solution)/shard_map/ppermute | solution.py:615
  89.6 0.0 collective-permute-start.17
  89.6 0.6 collective-permute-start.18
  90.1 0.6 collective-permute-done.17.s1
  90.7 1.9 %collective-permute-done.18.s2 = f32[8,128]{1,0:T(8,128)S(1)} collective-permute-done((f32[8,128]{1,0:T(8,128)S(1)}, f32[8,128]{1,0:T(8,128)S(1)}, u32[]{:S(2)}, u32[]{:S(2)}) %collective-permute-start.18) | collective-permute-done | bytes 4128 | tf_op jit(solution)/shard_map/ppermute | solution.py:615
  92.6 0.0 collective-permute-done.16.other
  92.6 1.1 %collective-permute-start.19 = (f32[264,128]{1,0:T(8,128)S(1)}, f32[264,128]{1,0:T(8,128)S(1)}, u32[]{:S(2)}, u32[]{:S(2)}) collective-permute-start(f32[264,128]{1,0:T(8,128)S(1)} %get-tuple-element.46.mine), channel_id=1, source_target_pairs={{0,4},{1,5},{2,6},{3,7},{4,0},{5,1},{6,2},{7,3},{8,12},{9,13},{10,... | collective-permute-start | bytes 405512 | tf_op jit(solution)/shard_map/ppermute | solution.py:615
  93.7 1.3 %collective-permute-start.20 = (f32[8,128]{1,0:T(8,128)S(1)}, f32[8,128]{1,0:T(8,128)S(1)}, u32[]{:S(2)}, u32[]{:S(2)}) collective-permute-start(f32[8,128]{1,0:T(8,128)S(1)} %get-tuple-element.47.s0), channel_id=1, source_target_pairs={{0,2},{1,3},{2,0},{3,1},{4,6},{5,7},{6,4},{7,5},{8,10},{9,11},{10,... | collective-permute-start | bytes 12296 | tf_op jit(solution)/shard_map/ppermute | solution.py:615
  95.0 1.2 %collective-permute-start.21 = (f32[8,128]{1,0:T(8,128)S(1)}, f32[8,128]{1,0:T(8,128)S(1)}, u32[]{:S(2)}, u32[]{:S(2)}) collective-permute-start(f32[8,128]{1,0:T(8,128)S(1)} %get-tuple-element.47.s0), channel_id=1, source_target_pairs={{0,6},{1,7},{2,4},{3,5},{4,2},{5,3},{6,0},{7,1},{8,14},{9,15},{10,... | collective-permute-start | bytes 12296 | tf_op jit(solution)/shard_map/ppermute | solution.py:615
  96.2 1.1 %collective-permute-done.20.s1 = f32[8,128]{1,0:T(8,128)S(1)} collective-permute-done((f32[8,128]{1,0:T(8,128)S(1)}, f32[8,128]{1,0:T(8,128)S(1)}, u32[]{:S(2)}, u32[]{:S(2)}) %collective-permute-start.20) | collective-permute-done | bytes 4128 | tf_op jit(solution)/shard_map/ppermute | solution.py:615
  97.3 2.2 %collective-permute-done.21.s2 = f32[8,128]{1,0:T(8,128)S(1)} collective-permute-done((f32[8,128]{1,0:T(8,128)S(1)}, f32[8,128]{1,0:T(8,128)S(1)}, u32[]{:S(2)}, u32[]{:S(2)}) %collective-permute-start.21) | collective-permute-done | bytes 4128 | tf_op jit(solution)/shard_map/ppermute | solution.py:615
  99.5 0.0 collective-permute-done.19.other
  99.5 0.8 finish.1
  (7 shorter events, 0.1 us)
Async XLA Ops:
  18.4 14.4 %collective-permute-start.2 = (f32[4,64,128]{2,1,0:T(8,128)}, f32[4,64,128]{2,1,0:T(8,128)S(1)}, u32[]{:S(2)}, u32[]{:S(2)}) collective-permute-start(f32[4,64,128]{2,1,0:T(8,128)} %get-tuple-element.29), channel_id=1, source_target_pairs={{0,2},{1,3},{2,0},{3,1},{4,6},{5,7},{6,4},{7,5},{8,10},{9,11},{10,... | collective-permute-start | bytes 393224 | tf_op jit(solution)/shard_map/ppermute | solution.py:615
  21.4 9.4 %copy-start = (f32[2,8,64,128]{3,2,1,0:T(8,128)S(1)}, f32[2,8,64,128]{3,2,1,0:T(8,128)}, u32[]{:S(2)}) copy-start(f32[2,8,64,128]{3,2,1,0:T(8,128)} %first.1) | copy-start | bytes 1572868
  21.4 9.4 %copy-start.1 = (f32[2,8,64,128]{3,2,1,0:T(8,128)S(1)}, f32[2,8,64,128]{3,2,1,0:T(8,128)}, u32[]{:S(2)}) copy-start(f32[2,8,64,128]{3,2,1,0:T(8,128)} %second.1) | copy-start | bytes 1572868
  21.4 9.4 %copy-start.2 = (f32[2,8,64,128]{3,2,1,0:T(8,128)S(1)}, f32[2,8,64,128]{3,2,1,0:T(8,128)}, u32[]{:S(2)}) copy-start(f32[2,8,64,128]{3,2,1,0:T(8,128)} %refs_2_.1) | copy-start | bytes 1572868
  21.4 9.4 %copy-start.3 = (f32[2,8,64,128]{3,2,1,0:T(8,128)S(1)}, f32[2,8,64,128]{3,2,1,0:T(8,128)}, u32[]{:S(2)}) copy-start(f32[2,8,64,128]{3,2,1,0:T(8,128)} %refs_3_.1) | copy-start | bytes 1572868
  21.4 26.5 %copy-start.6 = (s32[2]{0:T(128)S(1)}, s32[2]{0:T(128)}, u32[]{:S(2)}) copy-start(s32[2]{0:T(128)} %sources.1) | copy-start | bytes 28
  21.4 16.9 %collective-permute-start.4 = (f32[2,8,64,128]{3,2,1,0:T(8,128)}, f32[2,8,64,128]{3,2,1,0:T(8,128)S(1)}, u32[]{:S(2)}, u32[]{:S(2)}) collective-permute-start(f32[2,8,64,128]{3,2,1,0:T(8,128)} %get-tuple-element.30), channel_id=1, source_target_pairs={{0,2},{1,3},{2,0},{3,1},{4,6},{5,7},{6,4},{7,5},{8,10},{9,11},{10,... | collective-permute-start | bytes 1572872 | tf_op jit(solution)/shard_map/ppermute | solution.py:615
  30.8 0.7 copy-start.5
  32.9 5.5 %collective-permute-start.3 = (f32[4,64,128]{2,1,0:T(8,128)S(1)}, f32[4,64,128]{2,1,0:T(8,128)S(1)}, u32[]{:S(2)}, u32[]{:S(2)}) collective-permute-start(f32[4,64,128]{2,1,0:T(8,128)S(1)} %after.3.p0), channel_id=1, source_target_pairs={{0,5},{1,4},{2,7},{3,6},{4,1},{5,0},{6,3},{7,2},{8,13},{9,12},{10,... | collective-permute-start | bytes 393224 | tf_op jit(solution)/shard_map/ppermute | solution.py:615
  33.9 14.0 %collective-permute-start.1 = (f32[2,8,64,128]{3,2,1,0:T(8,128)S(1)}, f32[2,8,64,128]{3,2,1,0:T(8,128)S(1)}, u32[]{:S(2)}, u32[]{:S(2)}) collective-permute-start(f32[2,8,64,128]{3,2,1,0:T(8,128)S(1)} %get-tuple-element.28.own), channel_id=1, source_target_pairs={{0,1},{1,0},{2,3},{3,2},{4,5},{5,4},{6,7},{7,6},{8,9},{9,8},{10,11... | collective-permute-start | bytes 1572872 | tf_op jit(solution)/shard_map/ppermute | solution.py:615
  38.4 9.5 %collective-permute-start.5 = (f32[2,8,64,128]{3,2,1,0:T(8,128)S(1)}, f32[2,8,64,128]{3,2,1,0:T(8,128)S(1)}, u32[]{:S(2)}, u32[]{:S(2)}) collective-permute-start(f32[2,8,64,128]{3,2,1,0:T(8,128)S(1)} %after.4.over), channel_id=1, source_target_pairs={{0,1},{1,0},{2,3},{3,2},{4,5},{5,4},{6,7},{7,6},{8,9},{9,8},{10,11... | collective-permute-start | bytes 1572872 | tf_op jit(solution)/shard_map/ppermute | solution.py:615
  38.7 20.1 %collective-permute-start.9 = (f32[2,8,64,128]{3,2,1,0:T(8,128)}, f32[2,8,64,128]{3,2,1,0:T(8,128)S(1)}, u32[]{:S(2)}, u32[]{:S(2)}) collective-permute-start(f32[2,8,64,128]{3,2,1,0:T(8,128)} %get-tuple-element.34), channel_id=1, source_target_pairs={{0,2},{1,3},{2,0},{3,1},{4,6},{5,7},{6,4},{7,5},{8,10},{9,11},{10,... | collective-permute-start | bytes 1572872 | tf_op jit(solution)/shard_map/ppermute | solution.py:615
  40.8 5.5 %collective-permute-start.7 = (f32[4,64,128]{2,1,0:T(8,128)S(1)}, f32[4,64,128]{2,1,0:T(8,128)S(1)}, u32[]{:S(2)}, u32[]{:S(2)}) collective-permute-start(f32[4,64,128]{2,1,0:T(8,128)S(1)} %after.3.p0), channel_id=1, source_target_pairs={{0,4},{1,5},{2,6},{3,7},{4,0},{5,1},{6,2},{7,3},{8,12},{9,13},{10,... | collective-permute-start | bytes 393224 | tf_op jit(solution)/shard_map/ppermute | solution.py:615
  41.7 6.1 %collective-permute-start.6 = (f32[8,64,128]{2,1,0:T(8,128)}, f32[8,64,128]{2,1,0:T(8,128)}, u32[]{:S(2)}, u32[]{:S(2)}) collective-permute-start(f32[8,64,128]{2,1,0:T(8,128)} %get-tuple-element.31.c0), channel_id=1, source_target_pairs={{0,1},{1,0},{2,3},{3,2},{4,5},{5,4},{6,7},{7,6},{8,9},{9,8},{10,11... | collective-permute-start | bytes 786440 | tf_op jit(solution)/shard_map/ppermute | solution.py:615
  46.2 1.5 %collective-permute-start.8 = (f32[4,64,128]{2,1,0:T(8,128)S(1)}, f32[4,64,128]{2,1,0:T(8,128)}, u32[]{:S(2)}, u32[]{:S(2)}) collective-permute-start(f32[4,64,128]{2,1,0:T(8,128)S(1)} %after.3.p0), channel_id=1, source_target_pairs={{0,1},{1,0},{2,3},{3,2},{4,5},{5,4},{6,7},{7,6},{8,9},{9,8},{10,11... | collective-permute-start | bytes 393224 | tf_op jit(solution)/shard_map/ppermute | solution.py:615
  47.7 11.5 %collective-permute-start = (f32[2,8,64,128]{3,2,1,0:T(8,128)S(1)}, f32[2,8,64,128]{3,2,1,0:T(8,128)S(1)}, u32[]{:S(2)}, u32[]{:S(2)}) collective-permute-start(f32[2,8,64,128]{3,2,1,0:T(8,128)S(1)} %get-tuple-element.27.earlier.own), channel_id=1, source_target_pairs={{0,1},{1,0},{2,3},{3,2},{4,5},{5,4},{6,7},{7,6},{8,9},{9,8},{10,11... | collective-permute-start | bytes 1572872 | tf_op jit(solution)/shard_map/ppermute | solution.py:615
  58.8 2.0 %collective-permute-start.10 = (f32[2,8,64,128]{3,2,1,0:T(8,128)S(1)}, f32[2,8,64,128]{3,2,1,0:T(8,128)S(1)}, u32[]{:S(2)}, u32[]{:S(2)}) collective-permute-start(f32[2,8,64,128]{3,2,1,0:T(8,128)S(1)} %after.5.over), channel_id=1, source_target_pairs={{0,1},{1,0},{2,3},{3,2},{4,5},{5,4},{6,7},{7,6},{8,9},{9,8},{10,11... | collective-permute-start | bytes 1572872 | tf_op jit(solution)/shard_map/ppermute | solution.py:615
  60.8 27.1 %copy-start.4 = (f32[8,64,128]{2,1,0:T(8,128)S(1)}, f32[8,64,128]{2,1,0:T(8,128)}, u32[]{:S(2)}) copy-start(f32[8,64,128]{2,1,0:T(8,128)} %momentum.3) | copy-start | bytes 786436
  69.1 6.4 %collective-permute-start.11 = (f32[4,64,128]{2,1,0:T(8,128)S(1)}, f32[4,64,128]{2,1,0:T(8,128)S(1)}, u32[]{:S(2)}, u32[]{:S(2)}) collective-permute-start(f32[4,64,128]{2,1,0:T(8,128)S(1)} %get-tuple-element.39), channel_id=1, source_target_pairs={{0,2},{1,3},{2,0},{3,1},{4,6},{5,7},{6,4},{7,5},{8,10},{9,11},{10,... | collective-permute-start | bytes 393224 | tf_op jit(solution)/shard_map/ppermute | solution.py:615
  69.5 6.0 %collective-permute-start.12 = (f32[4,64,128]{2,1,0:T(8,128)S(1)}, f32[4,64,128]{2,1,0:T(8,128)S(1)}, u32[]{:S(2)}, u32[]{:S(2)}) collective-permute-start(f32[4,64,128]{2,1,0:T(8,128)S(1)} %get-tuple-element.40), channel_id=1, source_target_pairs={{0,4},{1,5},{2,6},{3,7},{4,0},{5,1},{6,2},{7,3},{8,12},{9,13},{10,... | collective-permute-start | bytes 393224 | tf_op jit(solution)/shard_map/ppermute | solution.py:615
  70.9 7.3 %collective-permute-start.13 = (f32[4,64,128]{2,1,0:T(8,128)S(1)}, f32[4,64,128]{2,1,0:T(8,128)S(1)}, u32[]{:S(2)}, u32[]{:S(2)}) collective-permute-start(f32[4,64,128]{2,1,0:T(8,128)S(1)} %get-tuple-element.41), channel_id=1, source_target_pairs={{0,6},{1,7},{2,4},{3,5},{4,2},{5,3},{6,0},{7,1},{8,14},{9,15},{10,... | collective-permute-start | bytes 393224 | tf_op jit(solution)/shard_map/ppermute | solution.py:615
  78.3 4.3 %collective-permute-start.14 = (f32[2,64,128]{2,1,0:T(8,128)S(1)}, f32[2,64,128]{2,1,0:T(8,128)S(1)}, u32[]{:S(2)}, u32[]{:S(2)}) collective-permute-start(f32[2,64,128]{2,1,0:T(8,128)S(1)} %get-tuple-element.43), channel_id=1, source_target_pairs={{0,8},{1,9},{2,10},{3,11},{4,12},{5,13},{6,14},{7,15},{8,0},{9,1},... | collective-permute-start | bytes 196616 | tf_op jit(solution)/shard_map/ppermute | solution.py:615
  82.6 5.2 %collective-permute-start.15 = (f32[2,64,128]{2,1,0:T(8,128)S(1)}, f32[2,64,128]{2,1,0:T(8,128)S(1)}, u32[]{:S(2)}, u32[]{:S(2)}) collective-permute-start(f32[2,64,128]{2,1,0:T(8,128)S(1)} %add_kernel.1.mine), channel_id=1, source_target_pairs={{0,16},{1,17},{2,18},{3,19},{4,20},{5,21},{6,22},{7,23},{8,24},{9,... | collective-permute-start | bytes 196616 | tf_op jit(solution)/shard_map/ppermute | solution.py:615
  87.9 4.6 %collective-permute-start.16 = (f32[136,128]{1,0:T(8,128)S(1)}, f32[136,128]{1,0:T(8,128)S(1)}, u32[]{:S(2)}, u32[]{:S(2)}) collective-permute-start(f32[136,128]{1,0:T(8,128)S(1)} %get-tuple-element.44.mine), channel_id=1, source_target_pairs={{0,8},{1,9},{2,10},{3,11},{4,12},{5,13},{6,14},{7,15},{8,0},{9,1},... | collective-permute-start | bytes 208904 | tf_op jit(solution)/shard_map/ppermute | solution.py:615
  89.6 1.2 %collective-permute-start.17 = (f32[8,128]{1,0:T(8,128)S(1)}, f32[8,128]{1,0:T(8,128)S(1)}, u32[]{:S(2)}, u32[]{:S(2)}) collective-permute-start(f32[8,128]{1,0:T(8,128)S(1)} %get-tuple-element.45.s0), channel_id=1, source_target_pairs={{0,1},{1,0},{2,3},{3,2},{4,5},{5,4},{6,7},{7,6},{8,9},{9,8},{10,11... | collective-permute-start | bytes 12296 | tf_op jit(solution)/shard_map/ppermute | solution.py:615
  89.6 3.0 %collective-permute-start.18 = (f32[8,128]{1,0:T(8,128)S(1)}, f32[8,128]{1,0:T(8,128)S(1)}, u32[]{:S(2)}, u32[]{:S(2)}) collective-permute-start(f32[8,128]{1,0:T(8,128)S(1)} %get-tuple-element.45.s0), channel_id=1, source_target_pairs={{0,9},{1,8},{2,11},{3,10},{4,13},{5,12},{6,15},{7,14},{8,1},{9,0},... | collective-permute-start | bytes 12296 | tf_op jit(solution)/shard_map/ppermute | solution.py:615
  92.6 6.9 %collective-permute-start.19 = (f32[264,128]{1,0:T(8,128)S(1)}, f32[264,128]{1,0:T(8,128)S(1)}, u32[]{:S(2)}, u32[]{:S(2)}) collective-permute-start(f32[264,128]{1,0:T(8,128)S(1)} %get-tuple-element.46.mine), channel_id=1, source_target_pairs={{0,4},{1,5},{2,6},{3,7},{4,0},{5,1},{6,2},{7,3},{8,12},{9,13},{10,... | collective-permute-start | bytes 405512 | tf_op jit(solution)/shard_map/ppermute | solution.py:615
  93.7 3.6 %collective-permute-start.20 = (f32[8,128]{1,0:T(8,128)S(1)}, f32[8,128]{1,0:T(8,128)S(1)}, u32[]{:S(2)}, u32[]{:S(2)}) collective-permute-start(f32[8,128]{1,0:T(8,128)S(1)} %get-tuple-element.47.s0), channel_id=1, source_target_pairs={{0,2},{1,3},{2,0},{3,1},{4,6},{5,7},{6,4},{7,5},{8,10},{9,11},{10,... | collective-permute-start | bytes 12296 | tf_op jit(solution)/shard_map/ppermute | solution.py:615
  95.0 4.5 %collective-permute-start.21 = (f32[8,128]{1,0:T(8,128)S(1)}, f32[8,128]{1,0:T(8,128)S(1)}, u32[]{:S(2)}, u32[]{:S(2)}) collective-permute-start(f32[8,128]{1,0:T(8,128)S(1)} %get-tuple-element.47.s0), channel_id=1, source_target_pairs={{0,6},{1,7},{2,4},{3,5},{4,2},{5,3},{6,0},{7,1},{8,14},{9,15},{10,... | collective-permute-start | bytes 12296 | tf_op jit(solution)/shard_map/ppermute | solution.py:615

commit v9 on v8

--- a/solution.py
+++ b/solution.py
@@ -174,21 +174,22 @@
     )(earlier, *fields)
 
 
-def first_kernel(first, second, courant, outgoing, whole, piece, held_courant, sems):
+def first_kernel(first, second, courant, outgoing, whole, piece, held, held_courant, sems):
     shot = 1 - lax.axis_index("chip")
     copies = [
-        pltpu.make_async_copy(courant, held_courant, sems.at[0]),
-        pltpu.make_async_copy(first.at[shot], outgoing.at[0], sems.at[1]),
-        pltpu.make_async_copy(second.at[shot], outgoing.at[1], sems.at[2]),
+        pltpu.make_async_copy(first.at[shot], held.at[0], sems.at[0]),
+        pltpu.make_async_copy(second.at[shot], held.at[1], sems.at[1]),
+        pltpu.make_async_copy(courant, held_courant, sems.at[2]),
     ]
     for copy in copies:
         copy.start()
-    copies[0].wait()
+    for n in range(2):
+        copies[n].wait()
+        interleave(outgoing, (n,), held.at[n])
+    copies[2].wait()
     interleave(whole, (), held_courant, 1.0 / 12.0)
     count = piece.shape[0]
     piece[...] = whole[pl.ds(lax.axis_index("shot") % 2 * count, count)]
-    copies[1].wait()
-    copies[2].wait()
 
 
 def band(lanes):
@@ -329,25 +330,19 @@
     return chip, core, [slab * planes for slab in slabs]
 
 
-def load_blocks(slabs, blocks, first, second, raw=False, factor=None):
+def load_blocks(slabs, blocks, first, second, factor=None):
     ends, rows, lanes = first.shape
-    planes, groups = blocks[0].shape[1], rows // 8
+    planes = blocks[0].shape[1]
     for field in (first, second):
         for z in (0, 1, ends - 2, ends - 1):
             field[z] = jnp.zeros((rows, lanes), jnp.float32)
-    for b, (slab, block) in enumerate(zip(slabs, blocks)):
-
-        @pl.loop(0, planes)
-        def _(p):
-            for n, field in enumerate((first, second)):
-                if raw and b >= 2:
-                    tiles = [block[n, p, pl.ds(i, 8, stride=groups), :] for i in range(groups)]
-                    value = jnp.concatenate(tiles, 0)
-                else:
-                    value = block[n, p]
-                if factor is not None:
-                    value = value * factor[slab + p]
-                field[slab + p + 2] = value
+    for slab, block in zip(slabs, blocks):
+        for p in range(planes):
+            values = block[0, p], block[1, p]
+            if factor is not None:
+                speed = factor[slab + p]
+                values = values[0] * speed, values[1] * speed
+            first[slab + p + 2], second[slab + p + 2] = values
 
 
 BATCH = 4
@@ -374,34 +369,29 @@
 
 
 def forward_kernel(
-    start, sources, own, mate, over, far, c0, c1, p0, p1, p2, p3, placed, laps, inject, cour, last, even, odd, banded, y0, y1,
-    traces_even, traces_odd, counts, sems
+    start, sources, own, mate, over, far, c0, c1, c2, c3, placed, laps, inject, cour, last, even, odd, banded, y0, y1,
+    held, sems
 ):
     planes, rows, lanes = c0.shape
     steps = laps.shape[0]
     groups = rows // 8
     chip_here, core, slabs = place(planes)
 
-    def copy(k, slot):
-        return pltpu.make_async_copy(placed.at[k], (traces_even, traces_odd)[slot], sems.at[slot])
-
-    copy(0, 0).start()
-    count_copy = pltpu.make_async_copy(placed.at[steps], counts, sems.at[2])
-    count_copy.start()
-    copy(1, 1).start()
+    def parts(k):
+        for n in range(4):
+            at = pl.ds(n * planes, planes)
+            yield pltpu.make_async_copy(placed.at[k, at], held.at[k, at], sems.at[k, n])
+
+    for k in (steps, 0, 1, 2):
+        for part in parts(k):
+            part.start()
     banded[...] = band(lanes)
-    load_blocks(slabs, (own, mate, over, far), odd, even, raw=True)
-    mine = lax.axis_index("shot") % 2 * (planes // 2)
-    other = planes // 2 - mine
-    courant_at = (slabs[0], slabs[1], slabs[2] + mine, slabs[2] + other, slabs[3] + mine, slabs[3] + other)
-    for z, block in zip(courant_at, (c0, c1, p0, p1, p2, p3)):
-
-        @pl.loop(0, block.shape[0])
-        def _(p):
-            cour[z + p] = block[p]
-
-    @pl.loop(0, 2 * planes)
-    def _(index):
+    load_blocks(slabs, (own, mate, over, far), odd, even)
+    for slab, block in zip(slabs, (c0, c1, c2, c3)):
+        for p in range(planes):
+            cour[slab + p] = block[p]
+
+    for index in range(2 * planes):
         z = (2 * (index // planes) + core) * planes + index % planes
         weight = 1.0 + 2.0 * jnp.full((rows, lanes), z, jnp.int32).astype(jnp.float32) / (4 * planes - 1)
         last[index] = weight / (12.0 * cour[z])
@@ -414,12 +404,18 @@
     )
     source_slab, source_p = source_z // planes, lax.rem(source_z, planes)
 
-    def advance(k, now, then, observed, slot):
-        copy(k, slot).wait()
+    def advance(k, now, then):
+        @pl.when(k + 3 < steps)
+        def _():
+            for part in parts(k + 3):
+                part.start()
+
+        for part in parts(k):
+            part.wait()
 
         def work(z, y_part, chip, p):
             def fetch(j, rows):
-                return then[z + j + 2, rows], cour[z + j, rows], observed[z + j, rows], counts[z + j, rows]
+                return then[z + j + 2, rows], cour[z + j, rows], held[k, z + j, rows], held[steps, z + j, rows]
 
             def finish(j, rows, center, lap, extra):
                 old, speed, traces, count = extra
@@ -442,18 +438,15 @@
         owned = jnp.where(lax.rem(source_slab, 2) == core, strength, 0.0)
         laps[k, source_p, source_slab // 2, tile, :] += owned
         then[source_z + 2, tile, :] += moved
-        inject[k, source_z, tile, :] -= counts[source_z, tile, :] * moved
-
-        @pl.when(k + 2 < steps)
-        def _():
-            copy(k + 2, slot).start()
-
-    count_copy.wait()
+        inject[k, source_z, tile, :] -= held[steps, source_z, tile, :] * moved
+
+    for part in parts(steps):
+        part.wait()
 
     @pl.loop(0, steps // 2)
     def _(pair):
-        advance(2 * pair, even, odd, traces_even, 0)
-        advance(2 * pair + 1, odd, even, traces_odd, 1)
+        advance(2 * pair, even, odd)
+        advance(2 * pair + 1, odd, even)
 
 
 def adjoint_kernel(own, mate, over, far, cour, laps, inject, last, keep, send_x, send_y, send_xy, even, odd, total, banded, y0, y1):
@@ -464,9 +457,7 @@
     banded[...] = band(lanes)
     load_blocks(slabs, (own, mate, over, far), odd, even, factor=cour)
 
-    @pl.loop(0, 2 * planes)
-    def _(index):
-        total[index] = jnp.zeros((rows, lanes), jnp.float32)
+    total[...] = jnp.zeros(total.shape, jnp.float32)
 
     def advance(k, now, then):
         def work(z, y_part, chip, p):
@@ -539,6 +530,13 @@
         compiler_params=pltpu.CompilerParams(vmem_limit_bytes=4 * 2**20),
         name="after",
     )(earlier, value)
+
+
+def arrange_kernel(mine, other, out):
+    y = lax.axis_index("shot") % 2
+    count = mine.shape[0]
+    out[pl.ds(y * count, count)] = mine[...]
+    out[pl.ds((1 - y) * count, count)] = other[...]
 
 
 def first_plane(shot, planes):
@@ -631,13 +629,14 @@
     outgoing, c0, piece = pl.pallas_call(
         first_kernel,
         in_specs=[hbm] * 3,
-        out_specs=[hbm, vmem, vmem],
+        out_specs=[vmem] * 3,
         out_shape=[
             jax.ShapeDtypeStruct((2, planes, rows_x, rows_y), jnp.float32),
             jax.ShapeDtypeStruct(courant_sq.shape, jnp.float32),
             jax.ShapeDtypeStruct((planes // 2, rows_x, rows_y), jnp.float32),
         ],
         scratch_shapes=[
+            pltpu.VMEM((2, planes, rows_x, rows_y), jnp.float32),
             pltpu.VMEM(courant_sq.shape, jnp.float32),
             pltpu.SemaphoreType.DMA((3,)),
         ],
@@ -651,27 +650,26 @@
     placed, mark = scatter(rec_cells, observed, planes_all, rows_x, rows_y)
     placed = placed.reshape(steps + 1, planes_all, rows_x, rows_y)
 
+    piece = after(mark, piece)
     adj_outgoing, adj_own, own = pick(
-        (adj_next, adj_cur, True), (adj_next, adj_cur, False), (fwd_prev, fwd_cur, False), earlier=mark
+        (adj_next, adj_cur, True), (adj_next, adj_cur, False), (fwd_prev, fwd_cur, False), earlier=piece
     )
     mate = exchange(own, CORE)
-    piece = after(adj_own, piece)
-    pieces = [piece, exchange(piece, Y), exchange(piece, CORE), exchange(piece, Y + CORE)]
-    c1 = exchange(c0, CORE)
-    over = after(pieces[3], over)
+    c2 = local(arrange_kernel, [courant_sq.shape], piece, exchange(piece, Y))
+    c1, c3 = exchange(c0, CORE), exchange(c2, CORE)
+    over = after(c2, over)
     far = exchange(over, CORE)
     adj_over = exchange(adj_outgoing, CHIP)
     adj_mate = exchange(adj_own, CORE)
 
     scratch = pltpu.VMEM((planes_all + 4, rows_x, rows_y), jnp.float32)
-    whole = pltpu.VMEM((planes_all, rows_x, rows_y), jnp.float32)
     y_scratch = pltpu.VMEM((BATCH * rows_x, rows_y), jnp.float32)
     step_scratch = [scratch, scratch, pltpu.VMEM((2 * rows_y, rows_y), jnp.bfloat16), y_scratch, y_scratch]
     params = pltpu.CompilerParams(vmem_limit_bytes=6 * 2**20)
     cost = pl.CostEstimate(flops=30 * steps * cells_all, bytes_accessed=16 * steps * cells_all, transcendentals=0)
     laps, inject, cour, last = pl.pallas_call(
         forward_kernel,
-        in_specs=[smem, smem] + [vmem] * 10 + [pl.BlockSpec(memory_space=pltpu.HBM)],
+        in_specs=[smem, smem] + [vmem] * 8 + [pl.BlockSpec(memory_space=pltpu.HBM)],
         out_specs=[vmem] * 4,
         out_shape=[
             jax.ShapeDtypeStruct((steps, planes, 2, rows_x, rows_y), jnp.float32),
@@ -679,11 +677,12 @@
             jax.ShapeDtypeStruct((planes_all, rows_x, rows_y), jnp.float32),
             jax.ShapeDtypeStruct((2 * planes, rows_x, rows_y), jnp.float32),
         ],
-        scratch_shapes=step_scratch + [whole, whole, whole, pltpu.SemaphoreType.DMA((3,))],
+        scratch_shapes=step_scratch
+        + [pltpu.VMEM((steps + 1, planes_all, rows_x, rows_y), jnp.float32), pltpu.SemaphoreType.DMA((steps + 1, 4))],
         compiler_params=pltpu.CompilerParams(vmem_limit_bytes=33 * 2**20),
         cost_estimate=pl.CostEstimate(flops=1000, bytes_accessed=1000, transcendentals=0),
         name="forward_steps",
-    )(ckpt_step[None], src_cells, own, mate, over, far, c0, c1, *pieces, placed)
+    )(ckpt_step[None], src_cells, own, mate, over, far, c0, c1, c2, c3, placed)
 
     adj_over = after(laps, adj_over)
     adj_far = exchange(adj_over, CORE)

time: 101 us -> 77.8 us (0.77)
  Pallas kernels: 48.5 us -> 32.2 us
  waiting for transfers between devices: 26.9 us -> 21.8 us
  starting transfers between devices: 22.7 us -> 21.5 us
    pallas_call x2, Pallas kernels: 28.6 us -> 12.4 us  [the longest x1 10.2 us: whole_shards(): pl.pallas_call(forward_kernel, in_specs=[smem, smem] + [vmem] * 8 + [pl.B...]
    ppermute x22 -> x21, waiting for transfers between devices: 26.9 us -> 21.8 us  [exchange(): lax.ppermute(value, axes, [(i, i ^ bits) for i in range(lax.axis_size(axe...]
    ppermute x22 -> x21, starting transfers between devices: 22.7 us -> 21.5 us  [exchange(): lax.ppermute(value, axes, [(i, i ^ bits) for i in range(lax.axis_size(axe...]
  transfers between devices with their start and end apart: 22 -> 21, of which waited for: 12 -> 12; matrix products, arithmetic and copies ran while one was open for 0% -> 0% of each run, Pallas kernels for 21% -> 27%
where the time goes in v9:
time: 77.8 us; the launch traced here: 77.6 us
  Pallas kernels  32.2 us (41%)
  waiting for transfers between devices  21.8 us (28%)
  starting transfers between devices  21.5 us (28%)
  between operations  1.43 us (2%)
    ppermute x21, waiting for transfers between devices, exchange(): lax.ppermute(value, axes, [(i, i ^ bits) for i in range(lax.axis_size(axe...  21.8 us
    ppermute x21, starting transfers between devices, exchange(): lax.ppermute(value, axes, [(i, i ^ bits) for i in range(lax.axis_size(axe...  21.5 us
    pallas_call x1, Pallas kernels, whole_shards(): pl.pallas_call(forward_kernel, in_specs=[smem, smem] + [vmem] * 8 + [pl.B...  10.2 us
    pallas_call x1, Pallas kernels, scatter(): pl.pallas_call(functools.partial(scatter_kernel, rows_x), grid=(rows_all...  9.25 us
    pallas_call x1, Pallas kernels, whole_shards(): pl.pallas_call(adjoint_kernel, in_specs=[vmem] * 8, out_specs=[vmem] * 4,...  8.17 us
    pallas_call x1, Pallas kernels, whole_shards(): pl.pallas_call(first_kernel, in_specs=[hbm] * 3, out_specs=[vmem] * 3, ou...  2.13 us
  transfers between devices with their start and end apart: 21, of which 12 were waited for; matrix products, arithmetic and copies ran while one was open for 0% of the time, Pallas kernels for 27%

profile of v9, /device:TPU:0, one launch (start us, length us, event | category | flops | bytes accessed | tf_op | source)
XLA Modules:
  0.0 77.6 jit_solution(12324607175603597342)
XLA Ops:
  0.6 2.1 %first_to_cross.1 = (f32[2,8,64,128]{3,2,1,0:T(8,128)}, f32[8,64,128]{2,1,0:T(8,128)}, f32[4,64,128]{2,1,0:T(8,128)}) custom-call(f32[2,8,64,128]{3,2,1,0:T(8,128)} %refs_4_.1, f32[2,8,64,128]{3,2,1,0:T(8,128)} %refs_5_.1, f32[8,64,128]{2,1,0:T(8,128)} %courant.1), custom_call_target="tpu_custom_call" | custom-call | tf_op jit(solution)/shard_map/first_to_cross/pallas_call | solution.py:629
  2.8 3.0 %collective-permute-start = (f32[4,64,128]{2,1,0:T(8,128)}, f32[4,64,128]{2,1,0:T(8,128)S(1)}, u32[]{:S(2)}, u32[]{:S(2)}) collective-permute-start(f32[4,64,128]{2,1,0:T(8,128)} %get-tuple-element.27), channel_id=1, source_target_pairs={{0,2},{1,3},{2,0},{3,1},{4,6},{5,7},{6,4},{7,5},{8,10},{9,11},{10,... | collective-permute-start | bytes 393224 | tf_op jit(solution)/shard_map/ppermute | solution.py:613
  5.8 0.0 copy-start
  5.8 0.0 copy-start.1
  5.8 0.0 copy-start.2
  5.8 0.0 copy-start.3
  5.8 0.0 copy-start.6
  5.8 0.1 collective-permute-start.4
  5.9 9.2 %receiver_scatter.1 = (f32[9,2048,128]{2,1,0:T(8,128)}, f32[8,128]{1,0:T(8,128)}) custom-call(s32[2,512]{1,0:T(2,128)} %cells_ref.1, f32[2,8,512]{2,1,0:T(8,128)} %observed_ref.1), custom_call_target="tpu_custom_call" | custom-call | flops 4831838208 | bytes 9437184 | tf_op jit(solution)/shard_map/receiver_scatter/pallas_call | solution.py:298
  15.2 0.0 collective-permute-done.value
  15.2 0.0 copy-start.5
  15.2 0.7 copy-done.5
  15.8 2.0 %collective-permute-start.3 = (f32[4,64,128]{2,1,0:T(8,128)S(1)}, f32[4,64,128]{2,1,0:T(8,128)S(1)}, u32[]{:S(2)}, u32[]{:S(2)}) collective-permute-start(f32[4,64,128]{2,1,0:T(8,128)S(1)} %after.3.earlier.mine), channel_id=1, source_target_pairs={{0,4},{1,5},{2,6},{3,7},{4,0},{5,1},{6,2},{7,3},{8,12},{9,13},{10,... | collective-permute-start | bytes 393224 | tf_op jit(solution)/shard_map/ppermute | solution.py:613
  17.8 0.0 copy-done
  17.8 0.0 copy-done.1
  17.8 0.0 copy-done.2
  17.8 0.0 copy-done.3
  17.8 1.3 %pick.1 = (f32[2,8,64,128]{3,2,1,0:T(8,128)}, f32[2,8,64,128]{3,2,1,0:T(8,128)S(1)}, f32[2,8,64,128]{3,2,1,0:T(8,128)S(1)}) custom-call(f32[4,64,128]{2,1,0:T(8,128)S(1)} %after.3.earlier.mine, f32[2,8,64,128]{3,2,1,0:T(8,128)S(1)} %copy-done, f32[2,8,64,128]{3,2,1,0:T(8,128)S(1)} %copy-done.1, f32[2,8,64,128]{3,2,1,0:T(8,128)S(1)} %copy-done, ...), custom_call_target="tpu_custom_call" | custom-call | tf_op jit(solution)/shard_map/pick/pallas_call | solution.py:166
  19.2 0.1 collective-permute-start.2
  19.3 1.6 %collective-permute-done.3.other = f32[4,64,128]{2,1,0:T(8,128)S(1)} collective-permute-done((f32[4,64,128]{2,1,0:T(8,128)S(1)}, f32[4,64,128]{2,1,0:T(8,128)S(1)}, u32[]{:S(2)}, u32[]{:S(2)}) %collective-permute-start.3) | collective-permute-done | bytes 131104 | tf_op jit(solution)/shard_map/ppermute | solution.py:613
  20.9 0.0 collective-permute-done.4.value
  21.0 0.1 collective-permute-start.5
  21.1 1.9 %collective-permute-start.8 = (f32[2,8,64,128]{3,2,1,0:T(8,128)}, f32[2,8,64,128]{3,2,1,0:T(8,128)S(1)}, u32[]{:S(2)}, u32[]{:S(2)}) collective-permute-start(f32[2,8,64,128]{3,2,1,0:T(8,128)} %get-tuple-element.34), channel_id=1, source_target_pairs={{0,2},{1,3},{2,0},{3,1},{4,6},{5,7},{6,4},{7,5},{8,10},{9,11},{10,... | collective-permute-start | bytes 1572872 | tf_op jit(solution)/shard_map/ppermute | solution.py:613
  23.0 0.2 collective-permute-start.6
  23.1 0.3 collective-permute-start.7
  24.1 0.7 collective-permute-done.6.c1
  24.8 0.2 collective-permute-start.1
  25.0 0.0 collective-permute-done.7.c3
  25.0 0.0 collective-permute-done.2.mate
  25.0 0.0 collective-permute-done.5.far
  25.0 0.0 copy-done.6
  25.0 10.2 %forward_steps.1 = (f32[8,8,2,64,128]{4,3,2,1,0:T(8,128)S(1)}, f32[8,32,64,128]{3,2,1,0:T(8,128)S(1)}, f32[32,64,128]{2,1,0:T(8,128)S(1)}, f32[16,64,128]{2,1,0:T(8,128)S(1)}) custom-call(s32[1]{0:T(128)} %bitcast.3.start, s32[2]{0:T(128)S(1)} %copy-done.6, f32[2,8,64,128]{3,2,1,0:T(8,128)S(1)} %get-tuple-element.29.own, ...), custom_call_target="tpu_custom_call" | custom-call | flops 1000 | bytes 1000 | tf_op jit(solution)/shard_map/forward_steps/pallas_call | solution.py:670
  35.3 0.4 collective-permute-done.8.value
  35.7 0.1 collective-permute-start.9
  35.8 0.0 collective-permute-done.1.mate
  35.8 1.9 %collective-permute-done.9.far = f32[2,8,64,128]{3,2,1,0:T(8,128)S(1)} collective-permute-done((f32[2,8,64,128]{3,2,1,0:T(8,128)S(1)}, f32[2,8,64,128]{3,2,1,0:T(8,128)S(1)}, u32[]{:S(2)}, u32[]{:S(2)}) %collective-permute-start.9) | collective-permute-done | bytes 524320 | tf_op jit(solution)/shard_map/ppermute | solution.py:613
  37.7 0.0 copy-start.4
  37.7 8.2 %adjoint_steps.1 = (f32[4,64,128]{2,1,0:T(8,128)S(1)}, f32[4,64,128]{2,1,0:T(8,128)S(1)}, f32[4,64,128]{2,1,0:T(8,128)S(1)}, f32[4,64,128]{2,1,0:T(8,128)S(1)}) custom-call(f32[2,8,64,128]{3,2,1,0:T(8,128)S(1)} %get-tuple-element.28.own, f32[2,8,64,128]{3,2,1,0:T(8,128)S(1)} %collective-permute-done.1.mate, f32[2,8,64,128]{3,2,1,0:T(8,128)S(1)} %after.5.over, ...), custom_call_target="tpu_custom_call" | custom-call | flops 62914560 | bytes 33554432 | tf_op jit(solution)/shard_map/adjoint_steps/pallas_call | solution.py:691
  45.9 1.8 %collective-permute-start.10 = (f32[4,64,128]{2,1,0:T(8,128)S(1)}, f32[4,64,128]{2,1,0:T(8,128)S(1)}, u32[]{:S(2)}, u32[]{:S(2)}) collective-permute-start(f32[4,64,128]{2,1,0:T(8,128)S(1)} %get-tuple-element.39), channel_id=1, source_target_pairs={{0,2},{1,3},{2,0},{3,1},{4,6},{5,7},{6,4},{7,5},{8,10},{9,11},{10,... | collective-permute-start | bytes 393224 | tf_op jit(solution)/shard_map/ppermute | solution.py:613
  47.7 1.5 %collective-permute-start.11 = (f32[4,64,128]{2,1,0:T(8,128)S(1)}, f32[4,64,128]{2,1,0:T(8,128)S(1)}, u32[]{:S(2)}, u32[]{:S(2)}) collective-permute-start(f32[4,64,128]{2,1,0:T(8,128)S(1)} %get-tuple-element.40), channel_id=1, source_target_pairs={{0,4},{1,5},{2,6},{3,7},{4,0},{5,1},{6,2},{7,3},{8,12},{9,13},{10,... | collective-permute-start | bytes 393224 | tf_op jit(solution)/shard_map/ppermute | solution.py:613
  49.2 0.2 collective-permute-start.12
  49.4 2.2 %collective-permute-done.10.by_x = f32[4,64,128]{2,1,0:T(8,128)S(1)} collective-permute-done((f32[4,64,128]{2,1,0:T(8,128)S(1)}, f32[4,64,128]{2,1,0:T(8,128)S(1)}, u32[]{:S(2)}, u32[]{:S(2)}) %collective-permute-start.10) | collective-permute-done | bytes 131104 | tf_op jit(solution)/shard_map/ppermute | solution.py:613
  51.6 4.2 %collective-permute-done.11.by_y = f32[4,64,128]{2,1,0:T(8,128)S(1)} collective-permute-done((f32[4,64,128]{2,1,0:T(8,128)S(1)}, f32[4,64,128]{2,1,0:T(8,128)S(1)}, u32[]{:S(2)}, u32[]{:S(2)}) %collective-permute-start.11) | collective-permute-done | bytes 131104 | tf_op jit(solution)/shard_map/ppermute | solution.py:613
  55.8 0.0 collective-permute-done.12.by_xy
  55.8 1.6 %collective-permute-start.13 = (f32[2,64,128]{2,1,0:T(8,128)S(1)}, f32[2,64,128]{2,1,0:T(8,128)S(1)}, u32[]{:S(2)}, u32[]{:S(2)}) collective-permute-start(f32[2,64,128]{2,1,0:T(8,128)S(1)} %get-tuple-element.43), channel_id=1, source_target_pairs={{0,8},{1,9},{2,10},{3,11},{4,12},{5,13},{6,14},{7,15},{8,0},{9,1},... | collective-permute-start | bytes 196616 | tf_op jit(solution)/shard_map/ppermute | solution.py:613
  57.5 2.7 %collective-permute-done.13.other = f32[2,64,128]{2,1,0:T(8,128)S(1)} collective-permute-done((f32[2,64,128]{2,1,0:T(8,128)S(1)}, f32[2,64,128]{2,1,0:T(8,128)S(1)}, u32[]{:S(2)}, u32[]{:S(2)}) %collective-permute-start.13) | collective-permute-done | bytes 65568 | tf_op jit(solution)/shard_map/ppermute | solution.py:613
  60.2 2.6 %collective-permute-start.14 = (f32[2,64,128]{2,1,0:T(8,128)S(1)}, f32[2,64,128]{2,1,0:T(8,128)S(1)}, u32[]{:S(2)}, u32[]{:S(2)}) collective-permute-start(f32[2,64,128]{2,1,0:T(8,128)S(1)} %add_kernel.1.mine), channel_id=1, source_target_pairs={{0,16},{1,17},{2,18},{3,19},{4,20},{5,21},{6,22},{7,23},{8,24},{9,... | collective-permute-start | bytes 196616 | tf_op jit(solution)/shard_map/ppermute | solution.py:613
  62.8 2.7 %collective-permute-done.14.other = f32[2,64,128]{2,1,0:T(8,128)S(1)} collective-permute-done((f32[2,64,128]{2,1,0:T(8,128)S(1)}, f32[2,64,128]{2,1,0:T(8,128)S(1)}, u32[]{:S(2)}, u32[]{:S(2)}) %collective-permute-start.14) | collective-permute-done | bytes 65568 | tf_op jit(solution)/shard_map/ppermute | solution.py:613
  65.5 0.0 copy-done.4
  65.5 0.1 sums_kernel.1
  65.6 1.5 %collective-permute-start.15 = (f32[136,128]{1,0:T(8,128)S(1)}, f32[136,128]{1,0:T(8,128)S(1)}, u32[]{:S(2)}, u32[]{:S(2)}) collective-permute-start(f32[136,128]{1,0:T(8,128)S(1)} %get-tuple-element.44.mine), channel_id=1, source_target_pairs={{0,8},{1,9},{2,10},{3,11},{4,12},{5,13},{6,14},{7,15},{8,0},{9,1},... | collective-permute-start | bytes 208904 | tf_op jit(solution)/shard_map/ppermute | solution.py:613
  67.1 0.0 collective-permute-start.16
  67.1 0.6 collective-permute-start.17
  67.7 0.5 collective-permute-done.16.s1
  68.3 1.9 %collective-permute-done.17.s2 = f32[8,128]{1,0:T(8,128)S(1)} collective-permute-done((f32[8,128]{1,0:T(8,128)S(1)}, f32[8,128]{1,0:T(8,128)S(1)}, u32[]{:S(2)}, u32[]{:S(2)}) %collective-permute-start.17) | collective-permute-done | bytes 4128 | tf_op jit(solution)/shard_map/ppermute | solution.py:613
  70.1 0.0 collective-permute-done.15.other
  70.2 1.6 %collective-permute-start.18 = (f32[264,128]{1,0:T(8,128)S(1)}, f32[264,128]{1,0:T(8,128)S(1)}, u32[]{:S(2)}, u32[]{:S(2)}) collective-permute-start(f32[264,128]{1,0:T(8,128)S(1)} %get-tuple-element.46.mine), channel_id=1, source_target_pairs={{0,4},{1,5},{2,6},{3,7},{4,0},{5,1},{6,2},{7,3},{8,12},{9,13},{10,... | collective-permute-start | bytes 405512 | tf_op jit(solution)/shard_map/ppermute | solution.py:613
  71.7 0.6 collective-permute-start.19
  72.3 1.4 %collective-permute-start.20 = (f32[8,128]{1,0:T(8,128)S(1)}, f32[8,128]{1,0:T(8,128)S(1)}, u32[]{:S(2)}, u32[]{:S(2)}) collective-permute-start(f32[8,128]{1,0:T(8,128)S(1)} %get-tuple-element.47.s0), channel_id=1, source_target_pairs={{0,6},{1,7},{2,4},{3,5},{4,2},{5,3},{6,0},{7,1},{8,14},{9,15},{10,... | collective-permute-start | bytes 12296 | tf_op jit(solution)/shard_map/ppermute | solution.py:613
  73.7 1.6 %collective-permute-done.19.s1 = f32[8,128]{1,0:T(8,128)S(1)} collective-permute-done((f32[8,128]{1,0:T(8,128)S(1)}, f32[8,128]{1,0:T(8,128)S(1)}, u32[]{:S(2)}, u32[]{:S(2)}) %collective-permute-start.19) | collective-permute-done | bytes 4128 | tf_op jit(solution)/shard_map/ppermute | solution.py:613
  75.4 1.5 %collective-permute-done.20.s2 = f32[8,128]{1,0:T(8,128)S(1)} collective-permute-done((f32[8,128]{1,0:T(8,128)S(1)}, f32[8,128]{1,0:T(8,128)S(1)}, u32[]{:S(2)}, u32[]{:S(2)}) %collective-permute-start.20) | collective-permute-done | bytes 4128 | tf_op jit(solution)/shard_map/ppermute | solution.py:613
  76.8 0.0 collective-permute-done.18.other
  76.8 0.8 %finish.1 = (f32[8,64,128]{2,1,0:T(8,128)}, f32[1]{0:T(128)}) custom-call(f32[264,128]{1,0:T(8,128)S(1)} %get-tuple-element.46.mine, f32[264,128]{1,0:T(8,128)S(1)} %collective-permute-done.18.other, f32[8,64,128]{2,1,0:T(8,128)S(1)} %copy-done.4, f32[8,128]{1,0:T(8,128)S(1)} %get-tuple-element.47.s0, f32[8,128]{1,0:T(8,128)S(1)} %collective-permute-done.19.s1, ...), custom_call_target="tpu_custom_call" | custom-call | tf_op jit(solution)/shard_map/finish/pallas_call | solution.py:713
  (7 shorter events, 0.2 us)
Async XLA Ops:
  2.8 12.4 %collective-permute-start = (f32[4,64,128]{2,1,0:T(8,128)}, f32[4,64,128]{2,1,0:T(8,128)S(1)}, u32[]{:S(2)}, u32[]{:S(2)}) collective-permute-start(f32[4,64,128]{2,1,0:T(8,128)} %get-tuple-element.27), channel_id=1, source_target_pairs={{0,2},{1,3},{2,0},{3,1},{4,6},{5,7},{6,4},{7,5},{8,10},{9,11},{10,... | collective-permute-start | bytes 393224 | tf_op jit(solution)/shard_map/ppermute | solution.py:613
  5.8 12.1 %copy-start = (f32[2,8,64,128]{3,2,1,0:T(8,128)S(1)}, f32[2,8,64,128]{3,2,1,0:T(8,128)}, u32[]{:S(2)}) copy-start(f32[2,8,64,128]{3,2,1,0:T(8,128)} %refs_2_.1) | copy-start | bytes 1572868
  5.8 12.1 %copy-start.1 = (f32[2,8,64,128]{3,2,1,0:T(8,128)S(1)}, f32[2,8,64,128]{3,2,1,0:T(8,128)}, u32[]{:S(2)}) copy-start(f32[2,8,64,128]{3,2,1,0:T(8,128)} %refs_3_.1) | copy-start | bytes 1572868
  5.8 12.1 %copy-start.2 = (f32[2,8,64,128]{3,2,1,0:T(8,128)S(1)}, f32[2,8,64,128]{3,2,1,0:T(8,128)}, u32[]{:S(2)}) copy-start(f32[2,8,64,128]{3,2,1,0:T(8,128)} %refs_4_.1) | copy-start | bytes 1572868
  5.8 12.1 %copy-start.3 = (f32[2,8,64,128]{3,2,1,0:T(8,128)S(1)}, f32[2,8,64,128]{3,2,1,0:T(8,128)}, u32[]{:S(2)}) copy-start(f32[2,8,64,128]{3,2,1,0:T(8,128)} %refs_5_.1) | copy-start | bytes 1572868
  5.8 19.3 %copy-start.6 = (s32[2]{0:T(128)S(1)}, s32[2]{0:T(128)}, u32[]{:S(2)}) copy-start(s32[2]{0:T(128)} %sources.1) | copy-start | bytes 28
  5.8 15.1 %collective-permute-start.4 = (f32[2,8,64,128]{3,2,1,0:T(8,128)}, f32[2,8,64,128]{3,2,1,0:T(8,128)S(1)}, u32[]{:S(2)}, u32[]{:S(2)}) collective-permute-start(f32[2,8,64,128]{3,2,1,0:T(8,128)} %get-tuple-element.30), channel_id=1, source_target_pairs={{0,2},{1,3},{2,0},{3,1},{4,6},{5,7},{6,4},{7,5},{8,10},{9,11},{10,... | collective-permute-start | bytes 1572872 | tf_op jit(solution)/shard_map/ppermute | solution.py:613
  15.2 0.7 copy-start.5
  15.8 5.1 %collective-permute-start.3 = (f32[4,64,128]{2,1,0:T(8,128)S(1)}, f32[4,64,128]{2,1,0:T(8,128)S(1)}, u32[]{:S(2)}, u32[]{:S(2)}) collective-permute-start(f32[4,64,128]{2,1,0:T(8,128)S(1)} %after.3.earlier.mine), channel_id=1, source_target_pairs={{0,4},{1,5},{2,6},{3,7},{4,0},{5,1},{6,2},{7,3},{8,12},{9,13},{10,... | collective-permute-start | bytes 393224 | tf_op jit(solution)/shard_map/ppermute | solution.py:613
  19.2 5.8 %collective-permute-start.2 = (f32[2,8,64,128]{3,2,1,0:T(8,128)S(1)}, f32[2,8,64,128]{3,2,1,0:T(8,128)S(1)}, u32[]{:S(2)}, u32[]{:S(2)}) collective-permute-start(f32[2,8,64,128]{3,2,1,0:T(8,128)S(1)} %get-tuple-element.29.own), channel_id=1, source_target_pairs={{0,1},{1,0},{2,3},{3,2},{4,5},{5,4},{6,7},{7,6},{8,9},{9,8},{10,11... | collective-permute-start | bytes 1572872 | tf_op jit(solution)/shard_map/ppermute | solution.py:613
  21.0 4.0 %collective-permute-start.5 = (f32[2,8,64,128]{3,2,1,0:T(8,128)S(1)}, f32[2,8,64,128]{3,2,1,0:T(8,128)S(1)}, u32[]{:S(2)}, u32[]{:S(2)}) collective-permute-start(f32[2,8,64,128]{3,2,1,0:T(8,128)S(1)} %after.4.over), channel_id=1, source_target_pairs={{0,1},{1,0},{2,3},{3,2},{4,5},{5,4},{6,7},{7,6},{8,9},{9,8},{10,11... | collective-permute-start | bytes 1572872 | tf_op jit(solution)/shard_map/ppermute | solution.py:613
  21.1 14.6 %collective-permute-start.8 = (f32[2,8,64,128]{3,2,1,0:T(8,128)}, f32[2,8,64,128]{3,2,1,0:T(8,128)S(1)}, u32[]{:S(2)}, u32[]{:S(2)}) collective-permute-start(f32[2,8,64,128]{3,2,1,0:T(8,128)} %get-tuple-element.34), channel_id=1, source_target_pairs={{0,2},{1,3},{2,0},{3,1},{4,6},{5,7},{6,4},{7,5},{8,10},{9,11},{10,... | collective-permute-start | bytes 1572872 | tf_op jit(solution)/shard_map/ppermute | solution.py:613
  23.0 1.9 %collective-permute-start.6 = (f32[8,64,128]{2,1,0:T(8,128)}, f32[8,64,128]{2,1,0:T(8,128)}, u32[]{:S(2)}, u32[]{:S(2)}) collective-permute-start(f32[8,64,128]{2,1,0:T(8,128)} %get-tuple-element.31.c0), channel_id=1, source_target_pairs={{0,1},{1,0},{2,3},{3,2},{4,5},{5,4},{6,7},{7,6},{8,9},{9,8},{10,11... | collective-permute-start | bytes 786440 | tf_op jit(solution)/shard_map/ppermute | solution.py:613
  23.1 1.9 %collective-permute-start.7 = (f32[8,64,128]{2,1,0:T(8,128)S(1)}, f32[8,64,128]{2,1,0:T(8,128)}, u32[]{:S(2)}, u32[]{:S(2)}) collective-permute-start(f32[8,64,128]{2,1,0:T(8,128)S(1)} %arrange_kernel.1.earlier.c2), channel_id=1, source_target_pairs={{0,1},{1,0},{2,3},{3,2},{4,5},{5,4},{6,7},{7,6},{8,9},{9,8},{10,11... | collective-permute-start | bytes 786440 | tf_op jit(solution)/shard_map/ppermute | solution.py:613
  24.8 11.0 %collective-permute-start.1 = (f32[2,8,64,128]{3,2,1,0:T(8,128)S(1)}, f32[2,8,64,128]{3,2,1,0:T(8,128)S(1)}, u32[]{:S(2)}, u32[]{:S(2)}) collective-permute-start(f32[2,8,64,128]{3,2,1,0:T(8,128)S(1)} %get-tuple-element.28.own), channel_id=1, source_target_pairs={{0,1},{1,0},{2,3},{3,2},{4,5},{5,4},{6,7},{7,6},{8,9},{9,8},{10,11... | collective-permute-start | bytes 1572872 | tf_op jit(solution)/shard_map/ppermute | solution.py:613
  35.7 2.0 %collective-permute-start.9 = (f32[2,8,64,128]{3,2,1,0:T(8,128)S(1)}, f32[2,8,64,128]{3,2,1,0:T(8,128)S(1)}, u32[]{:S(2)}, u32[]{:S(2)}) collective-permute-start(f32[2,8,64,128]{3,2,1,0:T(8,128)S(1)} %after.5.over), channel_id=1, source_target_pairs={{0,1},{1,0},{2,3},{3,2},{4,5},{5,4},{6,7},{7,6},{8,9},{9,8},{10,11... | collective-permute-start | bytes 1572872 | tf_op jit(solution)/shard_map/ppermute | solution.py:613
  37.7 27.8 %copy-start.4 = (f32[8,64,128]{2,1,0:T(8,128)S(1)}, f32[8,64,128]{2,1,0:T(8,128)}, u32[]{:S(2)}) copy-start(f32[8,64,128]{2,1,0:T(8,128)} %momentum.3) | copy-start | bytes 786436
  45.9 5.7 %collective-permute-start.10 = (f32[4,64,128]{2,1,0:T(8,128)S(1)}, f32[4,64,128]{2,1,0:T(8,128)S(1)}, u32[]{:S(2)}, u32[]{:S(2)}) collective-permute-start(f32[4,64,128]{2,1,0:T(8,128)S(1)} %get-tuple-element.39), channel_id=1, source_target_pairs={{0,2},{1,3},{2,0},{3,1},{4,6},{5,7},{6,4},{7,5},{8,10},{9,11},{10,... | collective-permute-start | bytes 393224 | tf_op jit(solution)/shard_map/ppermute | solution.py:613
  47.7 8.1 %collective-permute-start.11 = (f32[4,64,128]{2,1,0:T(8,128)S(1)}, f32[4,64,128]{2,1,0:T(8,128)S(1)}, u32[]{:S(2)}, u32[]{:S(2)}) collective-permute-start(f32[4,64,128]{2,1,0:T(8,128)S(1)} %get-tuple-element.40), channel_id=1, source_target_pairs={{0,4},{1,5},{2,6},{3,7},{4,0},{5,1},{6,2},{7,3},{8,12},{9,13},{10,... | collective-permute-start | bytes 393224 | tf_op jit(solution)/shard_map/ppermute | solution.py:613
  49.2 6.6 %collective-permute-start.12 = (f32[4,64,128]{2,1,0:T(8,128)S(1)}, f32[4,64,128]{2,1,0:T(8,128)S(1)}, u32[]{:S(2)}, u32[]{:S(2)}) collective-permute-start(f32[4,64,128]{2,1,0:T(8,128)S(1)} %get-tuple-element.41), channel_id=1, source_target_pairs={{0,6},{1,7},{2,4},{3,5},{4,2},{5,3},{6,0},{7,1},{8,14},{9,15},{10,... | collective-permute-start | bytes 393224 | tf_op jit(solution)/shard_map/ppermute | solution.py:613
  55.8 4.3 %collective-permute-start.13 = (f32[2,64,128]{2,1,0:T(8,128)S(1)}, f32[2,64,128]{2,1,0:T(8,128)S(1)}, u32[]{:S(2)}, u32[]{:S(2)}) collective-permute-start(f32[2,64,128]{2,1,0:T(8,128)S(1)} %get-tuple-element.43), channel_id=1, source_target_pairs={{0,8},{1,9},{2,10},{3,11},{4,12},{5,13},{6,14},{7,15},{8,0},{9,1},... | collective-permute-start | bytes 196616 | tf_op jit(solution)/shard_map/ppermute | solution.py:613
  60.2 5.3 %collective-permute-start.14 = (f32[2,64,128]{2,1,0:T(8,128)S(1)}, f32[2,64,128]{2,1,0:T(8,128)S(1)}, u32[]{:S(2)}, u32[]{:S(2)}) collective-permute-start(f32[2,64,128]{2,1,0:T(8,128)S(1)} %add_kernel.1.mine), channel_id=1, source_target_pairs={{0,16},{1,17},{2,18},{3,19},{4,20},{5,21},{6,22},{7,23},{8,24},{9,... | collective-permute-start | bytes 196616 | tf_op jit(solution)/shard_map/ppermute | solution.py:613
  65.6 4.6 %collective-permute-start.15 = (f32[136,128]{1,0:T(8,128)S(1)}, f32[136,128]{1,0:T(8,128)S(1)}, u32[]{:S(2)}, u32[]{:S(2)}) collective-permute-start(f32[136,128]{1,0:T(8,128)S(1)} %get-tuple-element.44.mine), channel_id=1, source_target_pairs={{0,8},{1,9},{2,10},{3,11},{4,12},{5,13},{6,14},{7,15},{8,0},{9,1},... | collective-permute-start | bytes 208904 | tf_op jit(solution)/shard_map/ppermute | solution.py:613
  67.1 1.2 %collective-permute-start.16 = (f32[8,128]{1,0:T(8,128)S(1)}, f32[8,128]{1,0:T(8,128)S(1)}, u32[]{:S(2)}, u32[]{:S(2)}) collective-permute-start(f32[8,128]{1,0:T(8,128)S(1)} %get-tuple-element.45.s0), channel_id=1, source_target_pairs={{0,1},{1,0},{2,3},{3,2},{4,5},{5,4},{6,7},{7,6},{8,9},{9,8},{10,11... | collective-permute-start | bytes 12296 | tf_op jit(solution)/shard_map/ppermute | solution.py:613
  67.1 3.0 %collective-permute-start.17 = (f32[8,128]{1,0:T(8,128)S(1)}, f32[8,128]{1,0:T(8,128)S(1)}, u32[]{:S(2)}, u32[]{:S(2)}) collective-permute-start(f32[8,128]{1,0:T(8,128)S(1)} %get-tuple-element.45.s0), channel_id=1, source_target_pairs={{0,9},{1,8},{2,11},{3,10},{4,13},{5,12},{6,15},{7,14},{8,1},{9,0},... | collective-permute-start | bytes 12296 | tf_op jit(solution)/shard_map/ppermute | solution.py:613
  70.2 6.7 %collective-permute-start.18 = (f32[264,128]{1,0:T(8,128)S(1)}, f32[264,128]{1,0:T(8,128)S(1)}, u32[]{:S(2)}, u32[]{:S(2)}) collective-permute-start(f32[264,128]{1,0:T(8,128)S(1)} %get-tuple-element.46.mine), channel_id=1, source_target_pairs={{0,4},{1,5},{2,6},{3,7},{4,0},{5,1},{6,2},{7,3},{8,12},{9,13},{10,... | collective-permute-start | bytes 405512 | tf_op jit(solution)/shard_map/ppermute | solution.py:613
  71.7 3.6 %collective-permute-start.19 = (f32[8,128]{1,0:T(8,128)S(1)}, f32[8,128]{1,0:T(8,128)S(1)}, u32[]{:S(2)}, u32[]{:S(2)}) collective-permute-start(f32[8,128]{1,0:T(8,128)S(1)} %get-tuple-element.47.s0), channel_id=1, source_target_pairs={{0,2},{1,3},{2,0},{3,1},{4,6},{5,7},{6,4},{7,5},{8,10},{9,11},{10,... | collective-permute-start | bytes 12296 | tf_op jit(solution)/shard_map/ppermute | solution.py:613
  72.3 4.5 %collective-permute-start.20 = (f32[8,128]{1,0:T(8,128)S(1)}, f32[8,128]{1,0:T(8,128)S(1)}, u32[]{:S(2)}, u32[]{:S(2)}) collective-permute-start(f32[8,128]{1,0:T(8,128)S(1)} %get-tuple-element.47.s0), channel_id=1, source_target_pairs={{0,6},{1,7},{2,4},{3,5},{4,2},{5,3},{6,0},{7,1},{8,14},{9,15},{10,... | collective-permute-start | bytes 12296 | tf_op jit(solution)/shard_map/ppermute | solution.py:613

commit v10 on v9

--- a/solution.py
+++ b/solution.py
@@ -369,22 +369,26 @@
 
 
 def forward_kernel(
-    start, sources, own, mate, over, far, c0, c1, c2, c3, placed, laps, inject, cour, last, even, odd, banded, y0, y1,
-    held, sems
+    start, sources, own, mate, over, far, c0, c1, c2, c3, placed, laps, history, held, cour, last,
+    even, odd, banded, y0, y1, sems, sems_even, sems_odd
 ):
     planes, rows, lanes = c0.shape
     steps = laps.shape[0]
     groups = rows // 8
     chip_here, core, slabs = place(planes)
 
-    def parts(k):
+    fetches = []
+    for k in range(steps + 1):
         for n in range(4):
             at = pl.ds(n * planes, planes)
-            yield pltpu.make_async_copy(placed.at[k, at], held.at[k, at], sems.at[k, n])
-
-    for k in (steps, 0, 1, 2):
-        for part in parts(k):
-            part.start()
+            fetches.append(pltpu.make_async_copy(placed.at[k, at], held.at[k, at], sems.at[k, n]))
+            fetches[-1].start()
+
+    def keep(k, field, done):
+        for n in range(4):
+            source = field.at[pl.ds(n * planes + 2, planes)]
+            yield pltpu.make_async_copy(source, history.at[k, pl.ds(n * planes, planes)], done.at[n])
+
     banded[...] = band(lanes)
     load_blocks(slabs, (own, mate, over, far), odd, even)
     for slab, block in zip(slabs, (c0, c1, c2, c3)):
@@ -404,26 +408,21 @@
     )
     source_slab, source_p = source_z // planes, lax.rem(source_z, planes)
 
-    def advance(k, now, then):
-        @pl.when(k + 3 < steps)
+    def advance(k, now, then, done):
+        @pl.when(k >= 2)
         def _():
-            for part in parts(k + 3):
-                part.start()
-
-        for part in parts(k):
-            part.wait()
+            for copy in keep(k - 2, then, done):
+                copy.wait()
 
         def work(z, y_part, chip, p):
             def fetch(j, rows):
-                return then[z + j + 2, rows], cour[z + j, rows], held[k, z + j, rows], held[steps, z + j, rows]
+                return then[z + j + 2, rows], cour[z + j, rows]
 
             def finish(j, rows, center, lap, extra):
-                old, speed, traces, count = extra
+                old, speed = extra
                 if chip is not None:
                     laps[k, p + j, chip, rows] = lap
-                newer = 2.0 * center - old + speed * lap
-                then[z + j + 2, rows] = newer
-                inject[k, z + j, rows] = traces - count * newer
+                then[z + j + 2, rows] = 2.0 * center - old + speed * lap
 
             laps12(now, z, y_part, fetch, finish)
 
@@ -438,15 +437,29 @@
         owned = jnp.where(lax.rem(source_slab, 2) == core, strength, 0.0)
         laps[k, source_p, source_slab // 2, tile, :] += owned
         then[source_z + 2, tile, :] += moved
-        inject[k, source_z, tile, :] -= held[steps, source_z, tile, :] * moved
-
-    for part in parts(steps):
-        part.wait()
+        for copy in keep(k, then, done):
+            copy.start()
 
     @pl.loop(0, steps // 2)
     def _(pair):
-        advance(2 * pair, even, odd)
-        advance(2 * pair + 1, odd, even)
+        advance(2 * pair, even, odd, sems_odd)
+        advance(2 * pair + 1, odd, even, sems_even)
+
+    for k, field, done in ((steps - 2, odd, sems_odd), (steps - 1, even, sems_even)):
+        for copy in keep(k, field, done):
+            copy.wait()
+    for fetch in fetches:
+        fetch.wait()
+
+
+def inject_kernel(held, history, inject):
+    steps, planes_all = history.shape[:2]
+
+    @pl.loop(0, planes_all)
+    def _(z):
+        count = held[steps, z]
+        for k in range(steps):
+            inject[k, z] = held[k, z] - count * history[k, z]
 
 
 def adjoint_kernel(own, mate, over, far, cour, laps, inject, last, keep, send_x, send_y, send_xy, even, odd, total, banded, y0, y1):
@@ -667,25 +680,38 @@
     step_scratch = [scratch, scratch, pltpu.VMEM((2 * rows_y, rows_y), jnp.bfloat16), y_scratch, y_scratch]
     params = pltpu.CompilerParams(vmem_limit_bytes=6 * 2**20)
     cost = pl.CostEstimate(flops=30 * steps * cells_all, bytes_accessed=16 * steps * cells_all, transcendentals=0)
-    laps, inject, cour, last = pl.pallas_call(
+    laps, history, held, cour, last = pl.pallas_call(
         forward_kernel,
         in_specs=[smem, smem] + [vmem] * 8 + [pl.BlockSpec(memory_space=pltpu.HBM)],
-        out_specs=[vmem] * 4,
+        out_specs=[vmem] * 5,
         out_shape=[
             jax.ShapeDtypeStruct((steps, planes, 2, rows_x, rows_y), jnp.float32),
             jax.ShapeDtypeStruct((steps, planes_all, rows_x, rows_y), jnp.float32),
+            jax.ShapeDtypeStruct((steps + 1, planes_all, rows_x, rows_y), jnp.float32),
             jax.ShapeDtypeStruct((planes_all, rows_x, rows_y), jnp.float32),
             jax.ShapeDtypeStruct((2 * planes, rows_x, rows_y), jnp.float32),
         ],
         scratch_shapes=step_scratch
-        + [pltpu.VMEM((steps + 1, planes_all, rows_x, rows_y), jnp.float32), pltpu.SemaphoreType.DMA((steps + 1, 4))],
-        compiler_params=pltpu.CompilerParams(vmem_limit_bytes=33 * 2**20),
+        + [
+            pltpu.SemaphoreType.DMA((steps + 1, 4)),
+            pltpu.SemaphoreType.DMA((4,)),
+            pltpu.SemaphoreType.DMA((4,)),
+        ],
+        compiler_params=pltpu.CompilerParams(vmem_limit_bytes=30 * 2**20),
         cost_estimate=pl.CostEstimate(flops=1000, bytes_accessed=1000, transcendentals=0),
         name="forward_steps",
     )(ckpt_step[None], src_cells, own, mate, over, far, c0, c1, c2, c3, placed)
 
     adj_over = after(laps, adj_over)
     adj_far = exchange(adj_over, CORE)
+    inject = pl.pallas_call(
+        inject_kernel,
+        in_specs=[vmem] * 2,
+        out_specs=vmem,
+        out_shape=jax.ShapeDtypeStruct(history.shape, jnp.float32),
+        compiler_params=pltpu.CompilerParams(vmem_limit_bytes=4 * 2**20),
+        name="inject",
+    )(held, history)
     slab = jax.ShapeDtypeStruct(courant_sq.shape, jnp.float32)
     half, quarter = (planes // 2, rows_x, rows_y), (planes // 4, rows_x, rows_y)
     keep, send_x, send_y, send_xy = pl.pallas_call(

time: 77.8 us -> 83.4 us (1.072)
  Pallas kernels: 32.2 us -> 36.2 us
  local copies, waits for them, and re-layouts: 0.7 us -> 4.39 us
  waiting for transfers between devices: 21.8 us -> 19.2 us
    unnamed x14 -> x16, local copies, waits for them, and re-layouts: 0.7 us -> 4.39 us
    pallas_call x1, Pallas kernels: 10.2 us -> 13.4 us  [whole_shards(): pl.pallas_call(forward_kernel, in_specs=[smem, smem] + [vmem] * 8 + [pl.B...]
    ppermute x21, waiting for transfers between devices: 21.8 us -> 19.2 us  [exchange(): lax.ppermute(value, axes, [(i, i ^ bits) for i in range(lax.axis_size(axe...]
    pallas_call x0 -> x1, Pallas kernels: none -> 1.33 us  [whole_shards(): pl.pallas_call(inject_kernel, in_specs=[vmem] * 2, out_specs=vmem, out_sh...]
  transfers between devices with their start and end apart: 21 -> 21, of which waited for: 12 -> 11; matrix products, arithmetic and copies ran while one was open for 0% -> 0% of each run, Pallas kernels for 27% -> 31%
where the time goes in v10:
time: 83.4 us; the launch traced here: 83.1 us
  Pallas kernels  36.2 us (43%)
  starting transfers between devices  21.8 us (26%)
  waiting for transfers between devices  19.2 us (23%)
  local copies, waits for them, and re-layouts  4.39 us (5%)
  between operations  1.45 us (2%)
    ppermute x21, starting transfers between devices, exchange(): lax.ppermute(value, axes, [(i, i ^ bits) for i in range(lax.axis_size(axe...  21.8 us
    ppermute x21, waiting for transfers between devices, exchange(): lax.ppermute(value, axes, [(i, i ^ bits) for i in range(lax.axis_size(axe...  19.2 us
    pallas_call x1, Pallas kernels, whole_shards(): pl.pallas_call(forward_kernel, in_specs=[smem, smem] + [vmem] * 8 + [pl.B...  13.4 us
    pallas_call x1, Pallas kernels, scatter(): pl.pallas_call(functools.partial(scatter_kernel, rows_x), grid=(rows_all...  9.27 us
    pallas_call x1, Pallas kernels, whole_shards(): pl.pallas_call(adjoint_kernel, in_specs=[vmem] * 8, out_specs=[vmem] * 4,...  7.64 us
    unnamed x16, local copies, waits for them, and re-layouts  4.39 us
    pallas_call x1, Pallas kernels, whole_shards(): pl.pallas_call(first_kernel, in_specs=[hbm] * 3, out_specs=[vmem] * 3, ou...  2.13 us
  transfers between devices with their start and end apart: 21, of which 11 were waited for; matrix products, arithmetic and copies ran while one was open for 0% of the time, Pallas kernels for 31%

profile of v10, /device:TPU:0, one launch (start us, length us, event | category | flops | bytes accessed | tf_op | source)
XLA Modules:
  0.0 83.1 jit_solution(13233529017628629479)
XLA Ops:
  0.6 2.1 %first_to_cross.1 = (f32[2,8,64,128]{3,2,1,0:T(8,128)}, f32[8,64,128]{2,1,0:T(8,128)}, f32[4,64,128]{2,1,0:T(8,128)}) custom-call(f32[2,8,64,128]{3,2,1,0:T(8,128)} %refs_4_.1, f32[2,8,64,128]{3,2,1,0:T(8,128)} %refs_5_.1, f32[8,64,128]{2,1,0:T(8,128)} %courant.1), custom_call_target="tpu_custom_call" | custom-call | tf_op jit(solution)/shard_map/first_to_cross/pallas_call | solution.py:642
  2.8 3.0 %collective-permute-start = (f32[4,64,128]{2,1,0:T(8,128)}, f32[4,64,128]{2,1,0:T(8,128)S(1)}, u32[]{:S(2)}, u32[]{:S(2)}) collective-permute-start(f32[4,64,128]{2,1,0:T(8,128)} %get-tuple-element.28), channel_id=1, source_target_pairs={{0,2},{1,3},{2,0},{3,1},{4,6},{5,7},{6,4},{7,5},{8,10},{9,11},{10,... | collective-permute-start | bytes 393224 | tf_op jit(solution)/shard_map/ppermute | solution.py:626
  5.8 0.0 copy-start.1
  5.8 0.0 copy-start.3
  5.8 0.0 copy-start.4
  5.8 0.0 copy-start.7
  5.8 0.1 collective-permute-start.4
  5.9 9.3 %receiver_scatter.1 = (f32[9,2048,128]{2,1,0:T(8,128)}, f32[8,128]{1,0:T(8,128)}) custom-call(s32[2,512]{1,0:T(2,128)} %cells_ref.1, f32[2,8,512]{2,1,0:T(8,128)} %observed_ref.1), custom_call_target="tpu_custom_call" | custom-call | flops 4831838208 | bytes 9437184 | tf_op jit(solution)/shard_map/receiver_scatter/pallas_call | solution.py:298
  15.2 0.0 collective-permute-done.value
  15.2 0.0 copy-start.6
  15.2 0.7 copy-done.6
  15.9 2.0 %collective-permute-start.3 = (f32[4,64,128]{2,1,0:T(8,128)S(1)}, f32[4,64,128]{2,1,0:T(8,128)S(1)}, u32[]{:S(2)}, u32[]{:S(2)}) collective-permute-start(f32[4,64,128]{2,1,0:T(8,128)S(1)} %after.3.earlier.mine), channel_id=1, source_target_pairs={{0,4},{1,5},{2,6},{3,7},{4,0},{5,1},{6,2},{7,3},{8,12},{9,13},{10,... | collective-permute-start | bytes 393224 | tf_op jit(solution)/shard_map/ppermute | solution.py:626
  17.8 0.0 copy-done.1
  17.9 0.0 copy-done.2
  17.9 0.0 copy-done.3
  17.9 0.0 copy-done.4
  17.9 1.4 %pick.1 = (f32[2,8,64,128]{3,2,1,0:T(8,128)}, f32[2,8,64,128]{3,2,1,0:T(8,128)S(1)}, f32[2,8,64,128]{3,2,1,0:T(8,128)S(1)}) custom-call(f32[4,64,128]{2,1,0:T(8,128)S(1)} %after.3.earlier.mine, f32[2,8,64,128]{3,2,1,0:T(8,128)S(1)} %copy-done.1, f32[2,8,64,128]{3,2,1,0:T(8,128)S(1)} %copy-done.2, f32[2,8,64,128]{3,2,1,0:T(8,128)S(1)} %copy-done.1, ...), custom_call_target="tpu_custom_call" | custom-call | tf_op jit(solution)/shard_map/pick/pallas_call | solution.py:166
  19.2 0.1 collective-permute-start.2
  19.3 1.6 %collective-permute-done.3.other = f32[4,64,128]{2,1,0:T(8,128)S(1)} collective-permute-done((f32[4,64,128]{2,1,0:T(8,128)S(1)}, f32[4,64,128]{2,1,0:T(8,128)S(1)}, u32[]{:S(2)}, u32[]{:S(2)}) %collective-permute-start.3) | collective-permute-done | bytes 131104 | tf_op jit(solution)/shard_map/ppermute | solution.py:626
  21.0 0.0 collective-permute-done.4.value
  21.0 0.1 collective-permute-start.5
  21.1 1.9 %collective-permute-start.8 = (f32[2,8,64,128]{3,2,1,0:T(8,128)}, f32[2,8,64,128]{3,2,1,0:T(8,128)S(1)}, u32[]{:S(2)}, u32[]{:S(2)}) collective-permute-start(f32[2,8,64,128]{3,2,1,0:T(8,128)} %get-tuple-element.35), channel_id=1, source_target_pairs={{0,2},{1,3},{2,0},{3,1},{4,6},{5,7},{6,4},{7,5},{8,10},{9,11},{10,... | collective-permute-start | bytes 1572872 | tf_op jit(solution)/shard_map/ppermute | solution.py:626
  23.0 0.2 collective-permute-start.6
  23.2 0.3 collective-permute-start.7
  24.2 0.7 collective-permute-done.6.c1
  24.9 0.2 collective-permute-start.1
  25.0 0.0 collective-permute-done.7.c3
  25.0 0.0 collective-permute-done.2.mate
  25.0 0.0 collective-permute-done.5.far
  25.1 0.0 copy-done.7
  25.1 13.4 %forward_steps.1 = (f32[8,8,2,64,128]{4,3,2,1,0:T(8,128)S(1)}, f32[8,32,64,128]{3,2,1,0:T(8,128)S(1)}, f32[9,32,64,128]{3,2,1,0:T(8,128)}, f32[32,64,128]{2,1,0:T(8,128)S(1)}, f32[16,64,128]{2,1,0:T(8,128)S(1)}) custom-call(s32[1]{0:T(128)} %bitcast.3.start, s32[2]{0:T(128)S(1)} %copy-done.7, f32[2,8,64,128]{3,2,1,0:T(8,128)S(1)} %get-tuple-element.30.own, ...), custom_call_target="tpu_custom_call" | custom-call | flops 1000 | bytes 1000 | tf_op jit(solution)/shard_map/forward_steps/pallas_call | solution.py:683
  38.5 0.0 collective-permute-done.8.value
  38.5 0.4 collective-permute-start.9
  39.0 3.7 %copy-done = f32[9,32,64,128]{3,2,1,0:T(8,128)S(1)} copy-done((f32[9,32,64,128]{3,2,1,0:T(8,128)S(1)}, f32[9,32,64,128]{3,2,1,0:T(8,128)}, u32[]{:S(2)}) %copy-start) | copy-done | bytes 9437208
  42.6 1.3 %inject.1 = f32[8,32,64,128]{3,2,1,0:T(8,128)S(1)} custom-call(f32[9,32,64,128]{3,2,1,0:T(8,128)S(1)} %copy-done, f32[8,32,64,128]{3,2,1,0:T(8,128)S(1)} %get-tuple-element.38.history), custom_call_target="tpu_custom_call" | custom-call | tf_op jit(solution)/shard_map/inject/pallas_call | solution.py:707
  44.0 0.0 collective-permute-done.1.mate
  44.0 0.0 collective-permute-done.9.far
  44.0 0.0 copy-start.5
  44.0 7.6 %adjoint_steps.1 = (f32[4,64,128]{2,1,0:T(8,128)S(1)}, f32[4,64,128]{2,1,0:T(8,128)S(1)}, f32[4,64,128]{2,1,0:T(8,128)S(1)}, f32[4,64,128]{2,1,0:T(8,128)S(1)}) custom-call(f32[2,8,64,128]{3,2,1,0:T(8,128)S(1)} %get-tuple-element.29.own, f32[2,8,64,128]{3,2,1,0:T(8,128)S(1)} %collective-permute-done.1.mate, f32[2,8,64,128]{3,2,1,0:T(8,128)S(1)} %after.5.over, ...), custom_call_target="tpu_custom_call" | custom-call | flops 62914560 | bytes 33554432 | tf_op jit(solution)/shard_map/adjoint_steps/pallas_call | solution.py:717
  51.6 1.1 %collective-permute-start.10 = (f32[4,64,128]{2,1,0:T(8,128)S(1)}, f32[4,64,128]{2,1,0:T(8,128)S(1)}, u32[]{:S(2)}, u32[]{:S(2)}) collective-permute-start(f32[4,64,128]{2,1,0:T(8,128)S(1)} %get-tuple-element.41), channel_id=1, source_target_pairs={{0,2},{1,3},{2,0},{3,1},{4,6},{5,7},{6,4},{7,5},{8,10},{9,11},{10,... | collective-permute-start | bytes 393224 | tf_op jit(solution)/shard_map/ppermute | solution.py:626
  52.7 1.1 %collective-permute-start.11 = (f32[4,64,128]{2,1,0:T(8,128)S(1)}, f32[4,64,128]{2,1,0:T(8,128)S(1)}, u32[]{:S(2)}, u32[]{:S(2)}) collective-permute-start(f32[4,64,128]{2,1,0:T(8,128)S(1)} %get-tuple-element.42), channel_id=1, source_target_pairs={{0,4},{1,5},{2,6},{3,7},{4,0},{5,1},{6,2},{7,3},{8,12},{9,13},{10,... | collective-permute-start | bytes 393224 | tf_op jit(solution)/shard_map/ppermute | solution.py:626
  53.9 1.3 %collective-permute-start.12 = (f32[4,64,128]{2,1,0:T(8,128)S(1)}, f32[4,64,128]{2,1,0:T(8,128)S(1)}, u32[]{:S(2)}, u32[]{:S(2)}) collective-permute-start(f32[4,64,128]{2,1,0:T(8,128)S(1)} %get-tuple-element.43), channel_id=1, source_target_pairs={{0,6},{1,7},{2,4},{3,5},{4,2},{5,3},{6,0},{7,1},{8,14},{9,15},{10,... | collective-permute-start | bytes 393224 | tf_op jit(solution)/shard_map/ppermute | solution.py:626
  55.2 2.8 %collective-permute-done.10.by_x = f32[4,64,128]{2,1,0:T(8,128)S(1)} collective-permute-done((f32[4,64,128]{2,1,0:T(8,128)S(1)}, f32[4,64,128]{2,1,0:T(8,128)S(1)}, u32[]{:S(2)}, u32[]{:S(2)}) %collective-permute-start.10) | collective-permute-done | bytes 131104 | tf_op jit(solution)/shard_map/ppermute | solution.py:626
  58.0 1.5 %collective-permute-done.11.by_y = f32[4,64,128]{2,1,0:T(8,128)S(1)} collective-permute-done((f32[4,64,128]{2,1,0:T(8,128)S(1)}, f32[4,64,128]{2,1,0:T(8,128)S(1)}, u32[]{:S(2)}, u32[]{:S(2)}) %collective-permute-start.11) | collective-permute-done | bytes 131104 | tf_op jit(solution)/shard_map/ppermute | solution.py:626
  59.5 1.5 %collective-permute-done.12.by_xy = f32[4,64,128]{2,1,0:T(8,128)S(1)} collective-permute-done((f32[4,64,128]{2,1,0:T(8,128)S(1)}, f32[4,64,128]{2,1,0:T(8,128)S(1)}, u32[]{:S(2)}, u32[]{:S(2)}) %collective-permute-start.12) | collective-permute-done | bytes 131104 | tf_op jit(solution)/shard_map/ppermute | solution.py:626
  61.1 1.6 %collective-permute-start.13 = (f32[2,64,128]{2,1,0:T(8,128)S(1)}, f32[2,64,128]{2,1,0:T(8,128)S(1)}, u32[]{:S(2)}, u32[]{:S(2)}) collective-permute-start(f32[2,64,128]{2,1,0:T(8,128)S(1)} %get-tuple-element.45), channel_id=1, source_target_pairs={{0,8},{1,9},{2,10},{3,11},{4,12},{5,13},{6,14},{7,15},{8,0},{9,1},... | collective-permute-start | bytes 196616 | tf_op jit(solution)/shard_map/ppermute | solution.py:626
  62.7 2.7 %collective-permute-done.13.other = f32[2,64,128]{2,1,0:T(8,128)S(1)} collective-permute-done((f32[2,64,128]{2,1,0:T(8,128)S(1)}, f32[2,64,128]{2,1,0:T(8,128)S(1)}, u32[]{:S(2)}, u32[]{:S(2)}) %collective-permute-start.13) | collective-permute-done | bytes 65568 | tf_op jit(solution)/shard_map/ppermute | solution.py:626
  65.4 2.6 %collective-permute-start.14 = (f32[2,64,128]{2,1,0:T(8,128)S(1)}, f32[2,64,128]{2,1,0:T(8,128)S(1)}, u32[]{:S(2)}, u32[]{:S(2)}) collective-permute-start(f32[2,64,128]{2,1,0:T(8,128)S(1)} %add_kernel.1.mine), channel_id=1, source_target_pairs={{0,16},{1,17},{2,18},{3,19},{4,20},{5,21},{6,22},{7,23},{8,24},{9,... | collective-permute-start | bytes 196616 | tf_op jit(solution)/shard_map/ppermute | solution.py:626
  68.1 2.6 %collective-permute-done.14.other = f32[2,64,128]{2,1,0:T(8,128)S(1)} collective-permute-done((f32[2,64,128]{2,1,0:T(8,128)S(1)}, f32[2,64,128]{2,1,0:T(8,128)S(1)}, u32[]{:S(2)}, u32[]{:S(2)}) %collective-permute-start.14) | collective-permute-done | bytes 65568 | tf_op jit(solution)/shard_map/ppermute | solution.py:626
  70.7 0.0 copy-done.5
  70.7 0.1 sums_kernel.1
  70.8 1.6 %collective-permute-start.15 = (f32[136,128]{1,0:T(8,128)S(1)}, f32[136,128]{1,0:T(8,128)S(1)}, u32[]{:S(2)}, u32[]{:S(2)}) collective-permute-start(f32[136,128]{1,0:T(8,128)S(1)} %get-tuple-element.46.mine), channel_id=1, source_target_pairs={{0,8},{1,9},{2,10},{3,11},{4,12},{5,13},{6,14},{7,15},{8,0},{9,1},... | collective-permute-start | bytes 208904 | tf_op jit(solution)/shard_map/ppermute | solution.py:626
  72.3 0.0 collective-permute-start.16
  72.3 0.6 collective-permute-start.17
  72.9 0.6 collective-permute-done.16.s1
  73.5 1.9 %collective-permute-done.17.s2 = f32[8,128]{1,0:T(8,128)S(1)} collective-permute-done((f32[8,128]{1,0:T(8,128)S(1)}, f32[8,128]{1,0:T(8,128)S(1)}, u32[]{:S(2)}, u32[]{:S(2)}) %collective-permute-start.17) | collective-permute-done | bytes 4128 | tf_op jit(solution)/shard_map/ppermute | solution.py:626
  75.4 0.0 collective-permute-done.15.other
  75.4 1.0 %collective-permute-start.18 = (f32[264,128]{1,0:T(8,128)S(1)}, f32[264,128]{1,0:T(8,128)S(1)}, u32[]{:S(2)}, u32[]{:S(2)}) collective-permute-start(f32[264,128]{1,0:T(8,128)S(1)} %get-tuple-element.48.mine), channel_id=1, source_target_pairs={{0,4},{1,5},{2,6},{3,7},{4,0},{5,1},{6,2},{7,3},{8,12},{9,13},{10,... | collective-permute-start | bytes 405512 | tf_op jit(solution)/shard_map/ppermute | solution.py:626
  76.4 1.4 %collective-permute-start.19 = (f32[8,128]{1,0:T(8,128)S(1)}, f32[8,128]{1,0:T(8,128)S(1)}, u32[]{:S(2)}, u32[]{:S(2)}) collective-permute-start(f32[8,128]{1,0:T(8,128)S(1)} %get-tuple-element.49.s0), channel_id=1, source_target_pairs={{0,2},{1,3},{2,0},{3,1},{4,6},{5,7},{6,4},{7,5},{8,10},{9,11},{10,... | collective-permute-start | bytes 12296 | tf_op jit(solution)/shard_map/ppermute | solution.py:626
  77.8 1.2 %collective-permute-start.20 = (f32[8,128]{1,0:T(8,128)S(1)}, f32[8,128]{1,0:T(8,128)S(1)}, u32[]{:S(2)}, u32[]{:S(2)}) collective-permute-start(f32[8,128]{1,0:T(8,128)S(1)} %get-tuple-element.49.s0), channel_id=1, source_target_pairs={{0,6},{1,7},{2,4},{3,5},{4,2},{5,3},{6,0},{7,1},{8,14},{9,15},{10,... | collective-permute-start | bytes 12296 | tf_op jit(solution)/shard_map/ppermute | solution.py:626
  79.0 1.1 %collective-permute-done.19.s1 = f32[8,128]{1,0:T(8,128)S(1)} collective-permute-done((f32[8,128]{1,0:T(8,128)S(1)}, f32[8,128]{1,0:T(8,128)S(1)}, u32[]{:S(2)}, u32[]{:S(2)}) %collective-permute-start.19) | collective-permute-done | bytes 4128 | tf_op jit(solution)/shard_map/ppermute | solution.py:626
  80.0 2.3 %collective-permute-done.20.s2 = f32[8,128]{1,0:T(8,128)S(1)} collective-permute-done((f32[8,128]{1,0:T(8,128)S(1)}, f32[8,128]{1,0:T(8,128)S(1)}, u32[]{:S(2)}, u32[]{:S(2)}) %collective-permute-start.20) | collective-permute-done | bytes 4128 | tf_op jit(solution)/shard_map/ppermute | solution.py:626
  82.3 0.0 collective-permute-done.18.other
  82.3 0.8 finish.1
  (9 shorter events, 0.2 us)
Async XLA Ops:
  2.8 12.4 %collective-permute-start = (f32[4,64,128]{2,1,0:T(8,128)}, f32[4,64,128]{2,1,0:T(8,128)S(1)}, u32[]{:S(2)}, u32[]{:S(2)}) collective-permute-start(f32[4,64,128]{2,1,0:T(8,128)} %get-tuple-element.28), channel_id=1, source_target_pairs={{0,2},{1,3},{2,0},{3,1},{4,6},{5,7},{6,4},{7,5},{8,10},{9,11},{10,... | collective-permute-start | bytes 393224 | tf_op jit(solution)/shard_map/ppermute | solution.py:626
  5.8 12.1 %copy-start.1 = (f32[2,8,64,128]{3,2,1,0:T(8,128)S(1)}, f32[2,8,64,128]{3,2,1,0:T(8,128)}, u32[]{:S(2)}) copy-start(f32[2,8,64,128]{3,2,1,0:T(8,128)} %refs_2_.1) | copy-start | bytes 1572868
  5.8 12.1 %copy-start.2 = (f32[2,8,64,128]{3,2,1,0:T(8,128)S(1)}, f32[2,8,64,128]{3,2,1,0:T(8,128)}, u32[]{:S(2)}) copy-start(f32[2,8,64,128]{3,2,1,0:T(8,128)} %refs_3_.1) | copy-start | bytes 1572868
  5.8 12.1 %copy-start.3 = (f32[2,8,64,128]{3,2,1,0:T(8,128)S(1)}, f32[2,8,64,128]{3,2,1,0:T(8,128)}, u32[]{:S(2)}) copy-start(f32[2,8,64,128]{3,2,1,0:T(8,128)} %refs_4_.1) | copy-start | bytes 1572868
  5.8 12.1 %copy-start.4 = (f32[2,8,64,128]{3,2,1,0:T(8,128)S(1)}, f32[2,8,64,128]{3,2,1,0:T(8,128)}, u32[]{:S(2)}) copy-start(f32[2,8,64,128]{3,2,1,0:T(8,128)} %refs_5_.1) | copy-start | bytes 1572868
  5.8 19.3 %copy-start.7 = (s32[2]{0:T(128)S(1)}, s32[2]{0:T(128)}, u32[]{:S(2)}) copy-start(s32[2]{0:T(128)} %sources.1) | copy-start | bytes 28
  5.8 15.2 %collective-permute-start.4 = (f32[2,8,64,128]{3,2,1,0:T(8,128)}, f32[2,8,64,128]{3,2,1,0:T(8,128)S(1)}, u32[]{:S(2)}, u32[]{:S(2)}) collective-permute-start(f32[2,8,64,128]{3,2,1,0:T(8,128)} %get-tuple-element.31), channel_id=1, source_target_pairs={{0,2},{1,3},{2,0},{3,1},{4,6},{5,7},{6,4},{7,5},{8,10},{9,11},{10,... | collective-permute-start | bytes 1572872 | tf_op jit(solution)/shard_map/ppermute | solution.py:626
  15.2 0.7 copy-start.6
  15.9 5.0 %collective-permute-start.3 = (f32[4,64,128]{2,1,0:T(8,128)S(1)}, f32[4,64,128]{2,1,0:T(8,128)S(1)}, u32[]{:S(2)}, u32[]{:S(2)}) collective-permute-start(f32[4,64,128]{2,1,0:T(8,128)S(1)} %after.3.earlier.mine), channel_id=1, source_target_pairs={{0,4},{1,5},{2,6},{3,7},{4,0},{5,1},{6,2},{7,3},{8,12},{9,13},{10,... | collective-permute-start | bytes 393224 | tf_op jit(solution)/shard_map/ppermute | solution.py:626
  19.2 5.8 %collective-permute-start.2 = (f32[2,8,64,128]{3,2,1,0:T(8,128)S(1)}, f32[2,8,64,128]{3,2,1,0:T(8,128)S(1)}, u32[]{:S(2)}, u32[]{:S(2)}) collective-permute-start(f32[2,8,64,128]{3,2,1,0:T(8,128)S(1)} %get-tuple-element.30.own), channel_id=1, source_target_pairs={{0,1},{1,0},{2,3},{3,2},{4,5},{5,4},{6,7},{7,6},{8,9},{9,8},{10,11... | collective-permute-start | bytes 1572872 | tf_op jit(solution)/shard_map/ppermute | solution.py:626
  21.0 4.0 %collective-permute-start.5 = (f32[2,8,64,128]{3,2,1,0:T(8,128)S(1)}, f32[2,8,64,128]{3,2,1,0:T(8,128)S(1)}, u32[]{:S(2)}, u32[]{:S(2)}) collective-permute-start(f32[2,8,64,128]{3,2,1,0:T(8,128)S(1)} %after.4.over), channel_id=1, source_target_pairs={{0,1},{1,0},{2,3},{3,2},{4,5},{5,4},{6,7},{7,6},{8,9},{9,8},{10,11... | collective-permute-start | bytes 1572872 | tf_op jit(solution)/shard_map/ppermute | solution.py:626
  21.1 17.4 %collective-permute-start.8 = (f32[2,8,64,128]{3,2,1,0:T(8,128)}, f32[2,8,64,128]{3,2,1,0:T(8,128)S(1)}, u32[]{:S(2)}, u32[]{:S(2)}) collective-permute-start(f32[2,8,64,128]{3,2,1,0:T(8,128)} %get-tuple-element.35), channel_id=1, source_target_pairs={{0,2},{1,3},{2,0},{3,1},{4,6},{5,7},{6,4},{7,5},{8,10},{9,11},{10,... | collective-permute-start | bytes 1572872 | tf_op jit(solution)/shard_map/ppermute | solution.py:626
  23.0 1.9 %collective-permute-start.6 = (f32[8,64,128]{2,1,0:T(8,128)}, f32[8,64,128]{2,1,0:T(8,128)}, u32[]{:S(2)}, u32[]{:S(2)}) collective-permute-start(f32[8,64,128]{2,1,0:T(8,128)} %get-tuple-element.32.c0), channel_id=1, source_target_pairs={{0,1},{1,0},{2,3},{3,2},{4,5},{5,4},{6,7},{7,6},{8,9},{9,8},{10,11... | collective-permute-start | bytes 786440 | tf_op jit(solution)/shard_map/ppermute | solution.py:626
  23.2 1.9 %collective-permute-start.7 = (f32[8,64,128]{2,1,0:T(8,128)S(1)}, f32[8,64,128]{2,1,0:T(8,128)}, u32[]{:S(2)}, u32[]{:S(2)}) collective-permute-start(f32[8,64,128]{2,1,0:T(8,128)S(1)} %arrange_kernel.1.earlier.c2), channel_id=1, source_target_pairs={{0,1},{1,0},{2,3},{3,2},{4,5},{5,4},{6,7},{7,6},{8,9},{9,8},{10,11... | collective-permute-start | bytes 786440 | tf_op jit(solution)/shard_map/ppermute | solution.py:626
  24.9 19.1 %collective-permute-start.1 = (f32[2,8,64,128]{3,2,1,0:T(8,128)S(1)}, f32[2,8,64,128]{3,2,1,0:T(8,128)S(1)}, u32[]{:S(2)}, u32[]{:S(2)}) collective-permute-start(f32[2,8,64,128]{3,2,1,0:T(8,128)S(1)} %get-tuple-element.29.own), channel_id=1, source_target_pairs={{0,1},{1,0},{2,3},{3,2},{4,5},{5,4},{6,7},{7,6},{8,9},{9,8},{10,11... | collective-permute-start | bytes 1572872 | tf_op jit(solution)/shard_map/ppermute | solution.py:626
  38.5 5.4 %collective-permute-start.9 = (f32[2,8,64,128]{3,2,1,0:T(8,128)S(1)}, f32[2,8,64,128]{3,2,1,0:T(8,128)S(1)}, u32[]{:S(2)}, u32[]{:S(2)}) collective-permute-start(f32[2,8,64,128]{3,2,1,0:T(8,128)S(1)} %after.5.over), channel_id=1, source_target_pairs={{0,1},{1,0},{2,3},{3,2},{4,5},{5,4},{6,7},{7,6},{8,9},{9,8},{10,11... | collective-permute-start | bytes 1572872 | tf_op jit(solution)/shard_map/ppermute | solution.py:626
  39.0 3.7 %copy-start = (f32[9,32,64,128]{3,2,1,0:T(8,128)S(1)}, f32[9,32,64,128]{3,2,1,0:T(8,128)}, u32[]{:S(2)}) copy-start(f32[9,32,64,128]{3,2,1,0:T(8,128)} %get-tuple-element.37.held) | copy-start | bytes 28311556
  44.0 26.7 %copy-start.5 = (f32[8,64,128]{2,1,0:T(8,128)S(1)}, f32[8,64,128]{2,1,0:T(8,128)}, u32[]{:S(2)}) copy-start(f32[8,64,128]{2,1,0:T(8,128)} %momentum.3) | copy-start | bytes 786436
  51.6 6.4 %collective-permute-start.10 = (f32[4,64,128]{2,1,0:T(8,128)S(1)}, f32[4,64,128]{2,1,0:T(8,128)S(1)}, u32[]{:S(2)}, u32[]{:S(2)}) collective-permute-start(f32[4,64,128]{2,1,0:T(8,128)S(1)} %get-tuple-element.41), channel_id=1, source_target_pairs={{0,2},{1,3},{2,0},{3,1},{4,6},{5,7},{6,4},{7,5},{8,10},{9,11},{10,... | collective-permute-start | bytes 393224 | tf_op jit(solution)/shard_map/ppermute | solution.py:626
  52.7 6.8 %collective-permute-start.11 = (f32[4,64,128]{2,1,0:T(8,128)S(1)}, f32[4,64,128]{2,1,0:T(8,128)S(1)}, u32[]{:S(2)}, u32[]{:S(2)}) collective-permute-start(f32[4,64,128]{2,1,0:T(8,128)S(1)} %get-tuple-element.42), channel_id=1, source_target_pairs={{0,4},{1,5},{2,6},{3,7},{4,0},{5,1},{6,2},{7,3},{8,12},{9,13},{10,... | collective-permute-start | bytes 393224 | tf_op jit(solution)/shard_map/ppermute | solution.py:626
  53.9 7.1 %collective-permute-start.12 = (f32[4,64,128]{2,1,0:T(8,128)S(1)}, f32[4,64,128]{2,1,0:T(8,128)S(1)}, u32[]{:S(2)}, u32[]{:S(2)}) collective-permute-start(f32[4,64,128]{2,1,0:T(8,128)S(1)} %get-tuple-element.43), channel_id=1, source_target_pairs={{0,6},{1,7},{2,4},{3,5},{4,2},{5,3},{6,0},{7,1},{8,14},{9,15},{10,... | collective-permute-start | bytes 393224 | tf_op jit(solution)/shard_map/ppermute | solution.py:626
  61.1 4.3 %collective-permute-start.13 = (f32[2,64,128]{2,1,0:T(8,128)S(1)}, f32[2,64,128]{2,1,0:T(8,128)S(1)}, u32[]{:S(2)}, u32[]{:S(2)}) collective-permute-start(f32[2,64,128]{2,1,0:T(8,128)S(1)} %get-tuple-element.45), channel_id=1, source_target_pairs={{0,8},{1,9},{2,10},{3,11},{4,12},{5,13},{6,14},{7,15},{8,0},{9,1},... | collective-permute-start | bytes 196616 | tf_op jit(solution)/shard_map/ppermute | solution.py:626
  65.4 5.3 %collective-permute-start.14 = (f32[2,64,128]{2,1,0:T(8,128)S(1)}, f32[2,64,128]{2,1,0:T(8,128)S(1)}, u32[]{:S(2)}, u32[]{:S(2)}) collective-permute-start(f32[2,64,128]{2,1,0:T(8,128)S(1)} %add_kernel.1.mine), channel_id=1, source_target_pairs={{0,16},{1,17},{2,18},{3,19},{4,20},{5,21},{6,22},{7,23},{8,24},{9,... | collective-permute-start | bytes 196616 | tf_op jit(solution)/shard_map/ppermute | solution.py:626
  70.8 4.6 %collective-permute-start.15 = (f32[136,128]{1,0:T(8,128)S(1)}, f32[136,128]{1,0:T(8,128)S(1)}, u32[]{:S(2)}, u32[]{:S(2)}) collective-permute-start(f32[136,128]{1,0:T(8,128)S(1)} %get-tuple-element.46.mine), channel_id=1, source_target_pairs={{0,8},{1,9},{2,10},{3,11},{4,12},{5,13},{6,14},{7,15},{8,0},{9,1},... | collective-permute-start | bytes 208904 | tf_op jit(solution)/shard_map/ppermute | solution.py:626
  72.3 1.2 %collective-permute-start.16 = (f32[8,128]{1,0:T(8,128)S(1)}, f32[8,128]{1,0:T(8,128)S(1)}, u32[]{:S(2)}, u32[]{:S(2)}) collective-permute-start(f32[8,128]{1,0:T(8,128)S(1)} %get-tuple-element.47.s0), channel_id=1, source_target_pairs={{0,1},{1,0},{2,3},{3,2},{4,5},{5,4},{6,7},{7,6},{8,9},{9,8},{10,11... | collective-permute-start | bytes 12296 | tf_op jit(solution)/shard_map/ppermute | solution.py:626
  72.3 3.0 %collective-permute-start.17 = (f32[8,128]{1,0:T(8,128)S(1)}, f32[8,128]{1,0:T(8,128)S(1)}, u32[]{:S(2)}, u32[]{:S(2)}) collective-permute-start(f32[8,128]{1,0:T(8,128)S(1)} %get-tuple-element.47.s0), channel_id=1, source_target_pairs={{0,9},{1,8},{2,11},{3,10},{4,13},{5,12},{6,15},{7,14},{8,1},{9,0},... | collective-permute-start | bytes 12296 | tf_op jit(solution)/shard_map/ppermute | solution.py:626
  75.4 6.9 %collective-permute-start.18 = (f32[264,128]{1,0:T(8,128)S(1)}, f32[264,128]{1,0:T(8,128)S(1)}, u32[]{:S(2)}, u32[]{:S(2)}) collective-permute-start(f32[264,128]{1,0:T(8,128)S(1)} %get-tuple-element.48.mine), channel_id=1, source_target_pairs={{0,4},{1,5},{2,6},{3,7},{4,0},{5,1},{6,2},{7,3},{8,12},{9,13},{10,... | collective-permute-start | bytes 405512 | tf_op jit(solution)/shard_map/ppermute | solution.py:626
  76.4 3.6 %collective-permute-start.19 = (f32[8,128]{1,0:T(8,128)S(1)}, f32[8,128]{1,0:T(8,128)S(1)}, u32[]{:S(2)}, u32[]{:S(2)}) collective-permute-start(f32[8,128]{1,0:T(8,128)S(1)} %get-tuple-element.49.s0), channel_id=1, source_target_pairs={{0,2},{1,3},{2,0},{3,1},{4,6},{5,7},{6,4},{7,5},{8,10},{9,11},{10,... | collective-permute-start | bytes 12296 | tf_op jit(solution)/shard_map/ppermute | solution.py:626
  77.8 4.5 %collective-permute-start.20 = (f32[8,128]{1,0:T(8,128)S(1)}, f32[8,128]{1,0:T(8,128)S(1)}, u32[]{:S(2)}, u32[]{:S(2)}) collective-permute-start(f32[8,128]{1,0:T(8,128)S(1)} %get-tuple-element.49.s0), channel_id=1, source_target_pairs={{0,6},{1,7},{2,4},{3,5},{4,2},{5,3},{6,0},{7,1},{8,14},{9,15},{10,... | collective-permute-start | bytes 12296 | tf_op jit(solution)/shard_map/ppermute | solution.py:626

commit v11 on v10

--- a/solution.py
+++ b/solution.py
@@ -369,20 +369,13 @@
 
 
 def forward_kernel(
-    start, sources, own, mate, over, far, c0, c1, c2, c3, placed, laps, history, held, cour, last,
-    even, odd, banded, y0, y1, sems, sems_even, sems_odd
+    start, sources, own, mate, over, far, c0, c1, c2, c3, laps, history, cour, last,
+    even, odd, banded, y0, y1, sems_even, sems_odd
 ):
     planes, rows, lanes = c0.shape
     steps = laps.shape[0]
     groups = rows // 8
     chip_here, core, slabs = place(planes)
-
-    fetches = []
-    for k in range(steps + 1):
-        for n in range(4):
-            at = pl.ds(n * planes, planes)
-            fetches.append(pltpu.make_async_copy(placed.at[k, at], held.at[k, at], sems.at[k, n]))
-            fetches[-1].start()
 
     def keep(k, field, done):
         for n in range(4):
@@ -448,18 +441,16 @@
     for k, field, done in ((steps - 2, odd, sems_odd), (steps - 1, even, sems_even)):
         for copy in keep(k, field, done):
             copy.wait()
-    for fetch in fetches:
-        fetch.wait()
-
-
-def inject_kernel(held, history, inject):
+
+
+def inject_kernel(placed, history, inject):
     steps, planes_all = history.shape[:2]
 
     @pl.loop(0, planes_all)
     def _(z):
-        count = held[steps, z]
+        count = placed[steps, z]
         for k in range(steps):
-            inject[k, z] = held[k, z] - count * history[k, z]
+            inject[k, z] = placed[k, z] - count * history[k, z]
 
 
 def adjoint_kernel(own, mate, over, far, cour, laps, inject, last, keep, send_x, send_y, send_xy, even, odd, total, banded, y0, y1):
@@ -680,27 +671,25 @@
     step_scratch = [scratch, scratch, pltpu.VMEM((2 * rows_y, rows_y), jnp.bfloat16), y_scratch, y_scratch]
     params = pltpu.CompilerParams(vmem_limit_bytes=6 * 2**20)
     cost = pl.CostEstimate(flops=30 * steps * cells_all, bytes_accessed=16 * steps * cells_all, transcendentals=0)
-    laps, history, held, cour, last = pl.pallas_call(
+    laps, history, cour, last = pl.pallas_call(
         forward_kernel,
-        in_specs=[smem, smem] + [vmem] * 8 + [pl.BlockSpec(memory_space=pltpu.HBM)],
-        out_specs=[vmem] * 5,
+        in_specs=[smem, smem] + [vmem] * 8,
+        out_specs=[vmem] * 4,
         out_shape=[
             jax.ShapeDtypeStruct((steps, planes, 2, rows_x, rows_y), jnp.float32),
             jax.ShapeDtypeStruct((steps, planes_all, rows_x, rows_y), jnp.float32),
-            jax.ShapeDtypeStruct((steps + 1, planes_all, rows_x, rows_y), jnp.float32),
             jax.ShapeDtypeStruct((planes_all, rows_x, rows_y), jnp.float32),
             jax.ShapeDtypeStruct((2 * planes, rows_x, rows_y), jnp.float32),
         ],
         scratch_shapes=step_scratch
         + [
-            pltpu.SemaphoreType.DMA((steps + 1, 4)),
             pltpu.SemaphoreType.DMA((4,)),
             pltpu.SemaphoreType.DMA((4,)),
         ],
-        compiler_params=pltpu.CompilerParams(vmem_limit_bytes=30 * 2**20),
+        compiler_params=pltpu.CompilerParams(vmem_limit_bytes=8 * 2**20),
         cost_estimate=pl.CostEstimate(flops=1000, bytes_accessed=1000, transcendentals=0),
         name="forward_steps",
-    )(ckpt_step[None], src_cells, own, mate, over, far, c0, c1, c2, c3, placed)
+    )(ckpt_step[None], src_cells, own, mate, over, far, c0, c1, c2, c3)
 
     adj_over = after(laps, adj_over)
     adj_far = exchange(adj_over, CORE)
@@ -711,7 +700,7 @@
         out_shape=jax.ShapeDtypeStruct(history.shape, jnp.float32),
         compiler_params=pltpu.CompilerParams(vmem_limit_bytes=4 * 2**20),
         name="inject",
-    )(held, history)
+    )(placed, history)
     slab = jax.ShapeDtypeStruct(courant_sq.shape, jnp.float32)
     half, quarter = (planes // 2, rows_x, rows_y), (planes // 4, rows_x, rows_y)
     keep, send_x, send_y, send_xy = pl.pallas_call(

time: 83.4 us -> 79 us (0.947)
  Pallas kernels: 36.2 us -> 30.1 us
  waiting for transfers between devices: 19.2 us -> 21.4 us
    pallas_call x1, Pallas kernels: 13.4 us -> 8.82 us  [whole_shards(): pl.pallas_call(forward_kernel, in_specs=[smem, smem] + [vmem] * 8, out_sp...]
    ppermute x21, waiting for transfers between devices: 19.2 us -> 21.4 us  [exchange(): lax.ppermute(value, axes, [(i, i ^ bits) for i in range(lax.axis_size(axe...]
    pallas_call x1, Pallas kernels: 7.64 us -> 6.44 us  [whole_shards(): pl.pallas_call(adjoint_kernel, in_specs=[vmem] * 8, out_specs=[vmem] * 4,...]
  transfers between devices with their start and end apart: 21 -> 21, of which waited for: 11 -> 10; matrix products, arithmetic and copies ran while one was open for 0% -> 0% of each run, Pallas kernels for 31% -> 26%
where the time goes in v11:
time: 79 us; the launch traced here: 78.8 us
  Pallas kernels  30.1 us (38%)
  starting transfers between devices  21.5 us (27%)
  waiting for transfers between devices  21.4 us (27%)
  local copies, waits for them, and re-layouts  4.38 us (6%)
  between operations  1.47 us (2%)
    ppermute x21, starting transfers between devices, exchange(): lax.ppermute(value, axes, [(i, i ^ bits) for i in range(lax.axis_size(axe...  21.5 us
    ppermute x21, waiting for transfers between devices, exchange(): lax.ppermute(value, axes, [(i, i ^ bits) for i in range(lax.axis_size(axe...  21.4 us
    pallas_call x1, Pallas kernels, scatter(): pl.pallas_call(functools.partial(scatter_kernel, rows_x), grid=(rows_all...  9.27 us
    pallas_call x1, Pallas kernels, whole_shards(): pl.pallas_call(forward_kernel, in_specs=[smem, smem] + [vmem] * 8, out_sp...  8.82 us
    pallas_call x1, Pallas kernels, whole_shards(): pl.pallas_call(adjoint_kernel, in_specs=[vmem] * 8, out_specs=[vmem] * 4,...  6.44 us
    unnamed x16, local copies, waits for them, and re-layouts  4.38 us
    pallas_call x1, Pallas kernels, whole_shards(): pl.pallas_call(first_kernel, in_specs=[hbm] * 3, out_specs=[vmem] * 3, ou...  2.13 us
  transfers between devices with their start and end apart: 21, of which 10 were waited for; matrix products, arithmetic and copies ran while one was open for 0% of the time, Pallas kernels for 26%

profile of v11, /device:TPU:0, one launch (start us, length us, event | category | flops | bytes accessed | tf_op | source)
XLA Modules:
  0.0 78.8 jit_solution(880555648603255001)
XLA Ops:
  0.6 2.1 %first_to_cross.1 = (f32[2,8,64,128]{3,2,1,0:T(8,128)}, f32[8,64,128]{2,1,0:T(8,128)}, f32[4,64,128]{2,1,0:T(8,128)}) custom-call(f32[2,8,64,128]{3,2,1,0:T(8,128)} %refs_4_.1, f32[2,8,64,128]{3,2,1,0:T(8,128)} %refs_5_.1, f32[8,64,128]{2,1,0:T(8,128)} %courant.1), custom_call_target="tpu_custom_call" | custom-call | tf_op jit(solution)/shard_map/first_to_cross/pallas_call | solution.py:633
  2.8 3.0 %collective-permute-start = (f32[4,64,128]{2,1,0:T(8,128)}, f32[4,64,128]{2,1,0:T(8,128)S(1)}, u32[]{:S(2)}, u32[]{:S(2)}) collective-permute-start(f32[4,64,128]{2,1,0:T(8,128)} %get-tuple-element.27), channel_id=1, source_target_pairs={{0,2},{1,3},{2,0},{3,1},{4,6},{5,7},{6,4},{7,5},{8,10},{9,11},{10,... | collective-permute-start | bytes 393224 | tf_op jit(solution)/shard_map/ppermute | solution.py:617
  5.8 0.0 copy-start.1
  5.8 0.0 copy-start.2
  5.8 0.0 copy-start.3
  5.8 0.0 copy-start.7
  5.8 0.1 collective-permute-start.4
  5.9 9.3 %receiver_scatter.1 = (f32[9,2048,128]{2,1,0:T(8,128)}, f32[8,128]{1,0:T(8,128)}) custom-call(s32[2,512]{1,0:T(2,128)} %cells_ref.1, f32[2,8,512]{2,1,0:T(8,128)} %observed_ref.1), custom_call_target="tpu_custom_call" | custom-call | flops 4831838208 | bytes 9437184 | tf_op jit(solution)/shard_map/receiver_scatter/pallas_call | solution.py:298
  15.2 0.0 collective-permute-done.value
  15.2 0.7 copy-done.6
  15.9 2.0 %collective-permute-start.3 = (f32[4,64,128]{2,1,0:T(8,128)S(1)}, f32[4,64,128]{2,1,0:T(8,128)S(1)}, u32[]{:S(2)}, u32[]{:S(2)}) collective-permute-start(f32[4,64,128]{2,1,0:T(8,128)S(1)} %after.3.earlier.mine), channel_id=1, source_target_pairs={{0,4},{1,5},{2,6},{3,7},{4,0},{5,1},{6,2},{7,3},{8,12},{9,13},{10,... | collective-permute-start | bytes 393224 | tf_op jit(solution)/shard_map/ppermute | solution.py:617
  17.8 0.0 copy-done.1
  17.9 0.0 copy-done.2
  17.9 0.0 copy-done.3
  17.9 0.0 copy-done.4
  17.9 1.4 %pick.1 = (f32[2,8,64,128]{3,2,1,0:T(8,128)}, f32[2,8,64,128]{3,2,1,0:T(8,128)S(1)}, f32[2,8,64,128]{3,2,1,0:T(8,128)S(1)}) custom-call(f32[4,64,128]{2,1,0:T(8,128)S(1)} %after.3.earlier.mine, f32[2,8,64,128]{3,2,1,0:T(8,128)S(1)} %copy-done.1, f32[2,8,64,128]{3,2,1,0:T(8,128)S(1)} %copy-done.2, f32[2,8,64,128]{3,2,1,0:T(8,128)S(1)} %copy-done.1, ...), custom_call_target="tpu_custom_call" | custom-call | tf_op jit(solution)/shard_map/pick/pallas_call | solution.py:166
  19.3 0.1 collective-permute-start.2
  19.3 1.6 %collective-permute-done.3.other = f32[4,64,128]{2,1,0:T(8,128)S(1)} collective-permute-done((f32[4,64,128]{2,1,0:T(8,128)S(1)}, f32[4,64,128]{2,1,0:T(8,128)S(1)}, u32[]{:S(2)}, u32[]{:S(2)}) %collective-permute-start.3) | collective-permute-done | bytes 131104 | tf_op jit(solution)/shard_map/ppermute | solution.py:617
  21.0 0.0 collective-permute-done.4.value
  21.0 0.1 collective-permute-start.5
  21.1 1.9 %collective-permute-start.8 = (f32[2,8,64,128]{3,2,1,0:T(8,128)}, f32[2,8,64,128]{3,2,1,0:T(8,128)S(1)}, u32[]{:S(2)}, u32[]{:S(2)}) collective-permute-start(f32[2,8,64,128]{3,2,1,0:T(8,128)} %get-tuple-element.33), channel_id=1, source_target_pairs={{0,2},{1,3},{2,0},{3,1},{4,6},{5,7},{6,4},{7,5},{8,10},{9,11},{10,... | collective-permute-start | bytes 1572872 | tf_op jit(solution)/shard_map/ppermute | solution.py:617
  23.0 0.2 collective-permute-start.6
  23.2 0.3 collective-permute-start.7
  24.2 0.7 collective-permute-done.6.c1
  24.9 0.2 collective-permute-start.1
  25.0 0.0 collective-permute-done.7.c3
  25.0 0.0 collective-permute-done.2.mate
  25.0 0.0 collective-permute-done.5.far
  25.1 0.0 copy-done.7
  25.1 8.8 %forward_steps.1 = (f32[8,8,2,64,128]{4,3,2,1,0:T(8,128)S(1)}, f32[8,32,64,128]{3,2,1,0:T(8,128)S(1)}, f32[32,64,128]{2,1,0:T(8,128)S(1)}, f32[16,64,128]{2,1,0:T(8,128)S(1)}) custom-call(s32[1]{0:T(128)} %bitcast.3.start, s32[2]{0:T(128)S(1)} %copy-done.7, f32[2,8,64,128]{3,2,1,0:T(8,128)S(1)} %get-tuple-element.29.own, ...), custom_call_target="tpu_custom_call" | custom-call | flops 1000 | bytes 1000 | tf_op jit(solution)/shard_map/forward_steps/pallas_call | solution.py:674
  33.9 1.8 %collective-permute-done.8.value = f32[2,8,64,128]{3,2,1,0:T(8,128)S(1)} collective-permute-done((f32[2,8,64,128]{3,2,1,0:T(8,128)}, f32[2,8,64,128]{3,2,1,0:T(8,128)S(1)}, u32[]{:S(2)}, u32[]{:S(2)}) %collective-permute-start.8) | collective-permute-done | bytes 524320 | tf_op jit(solution)/shard_map/ppermute | solution.py:617
  35.8 0.1 collective-permute-start.9
  35.8 0.0 copy-start
  35.9 3.7 %copy-done = f32[9,2048,128]{2,1,0:T(8,128)S(1)} copy-done((f32[9,2048,128]{2,1,0:T(8,128)S(1)}, f32[9,2048,128]{2,1,0:T(8,128)}, u32[]{:S(2)}) %copy-start) | copy-done | bytes 9437208
  39.5 1.0 %inject.1 = f32[8,32,64,128]{3,2,1,0:T(8,128)S(1)} custom-call(f32[9,32,64,128]{3,2,1,0:T(8,128)S(1)} %bitcast.4, f32[8,32,64,128]{3,2,1,0:T(8,128)S(1)} %get-tuple-element.36.history), custom_call_target="tpu_custom_call" | custom-call | tf_op jit(solution)/shard_map/inject/pallas_call | solution.py:696
  40.5 0.0 collective-permute-done.1.mate
  40.5 0.0 collective-permute-done.9.far
  40.5 0.0 copy-start.5
  40.5 6.4 %adjoint_steps.1 = (f32[4,64,128]{2,1,0:T(8,128)S(1)}, f32[4,64,128]{2,1,0:T(8,128)S(1)}, f32[4,64,128]{2,1,0:T(8,128)S(1)}, f32[4,64,128]{2,1,0:T(8,128)S(1)}) custom-call(f32[2,8,64,128]{3,2,1,0:T(8,128)S(1)} %get-tuple-element.28.own, f32[2,8,64,128]{3,2,1,0:T(8,128)S(1)} %collective-permute-done.1.mate, f32[2,8,64,128]{3,2,1,0:T(8,128)S(1)} %after.5.over, ...), custom_call_target="tpu_custom_call" | custom-call | flops 62914560 | bytes 33554432 | tf_op jit(solution)/shard_map/adjoint_steps/pallas_call | solution.py:706
  47.0 1.8 %collective-permute-start.10 = (f32[4,64,128]{2,1,0:T(8,128)S(1)}, f32[4,64,128]{2,1,0:T(8,128)S(1)}, u32[]{:S(2)}, u32[]{:S(2)}) collective-permute-start(f32[4,64,128]{2,1,0:T(8,128)S(1)} %get-tuple-element.39), channel_id=1, source_target_pairs={{0,2},{1,3},{2,0},{3,1},{4,6},{5,7},{6,4},{7,5},{8,10},{9,11},{10,... | collective-permute-start | bytes 393224 | tf_op jit(solution)/shard_map/ppermute | solution.py:617
  48.8 1.5 %collective-permute-start.11 = (f32[4,64,128]{2,1,0:T(8,128)S(1)}, f32[4,64,128]{2,1,0:T(8,128)S(1)}, u32[]{:S(2)}, u32[]{:S(2)}) collective-permute-start(f32[4,64,128]{2,1,0:T(8,128)S(1)} %get-tuple-element.40), channel_id=1, source_target_pairs={{0,4},{1,5},{2,6},{3,7},{4,0},{5,1},{6,2},{7,3},{8,12},{9,13},{10,... | collective-permute-start | bytes 393224 | tf_op jit(solution)/shard_map/ppermute | solution.py:617
  50.3 0.2 collective-permute-start.12
  50.5 2.5 %collective-permute-done.10.by_x = f32[4,64,128]{2,1,0:T(8,128)S(1)} collective-permute-done((f32[4,64,128]{2,1,0:T(8,128)S(1)}, f32[4,64,128]{2,1,0:T(8,128)S(1)}, u32[]{:S(2)}, u32[]{:S(2)}) %collective-permute-start.10) | collective-permute-done | bytes 131104 | tf_op jit(solution)/shard_map/ppermute | solution.py:617
  53.1 4.2 %collective-permute-done.11.by_y = f32[4,64,128]{2,1,0:T(8,128)S(1)} collective-permute-done((f32[4,64,128]{2,1,0:T(8,128)S(1)}, f32[4,64,128]{2,1,0:T(8,128)S(1)}, u32[]{:S(2)}, u32[]{:S(2)}) %collective-permute-start.11) | collective-permute-done | bytes 131104 | tf_op jit(solution)/shard_map/ppermute | solution.py:617
  57.2 0.0 collective-permute-done.12.by_xy
  57.3 1.6 %collective-permute-start.13 = (f32[2,64,128]{2,1,0:T(8,128)S(1)}, f32[2,64,128]{2,1,0:T(8,128)S(1)}, u32[]{:S(2)}, u32[]{:S(2)}) collective-permute-start(f32[2,64,128]{2,1,0:T(8,128)S(1)} %get-tuple-element.43), channel_id=1, source_target_pairs={{0,8},{1,9},{2,10},{3,11},{4,12},{5,13},{6,14},{7,15},{8,0},{9,1},... | collective-permute-start | bytes 196616 | tf_op jit(solution)/shard_map/ppermute | solution.py:617
  58.9 2.7 %collective-permute-done.13.other = f32[2,64,128]{2,1,0:T(8,128)S(1)} collective-permute-done((f32[2,64,128]{2,1,0:T(8,128)S(1)}, f32[2,64,128]{2,1,0:T(8,128)S(1)}, u32[]{:S(2)}, u32[]{:S(2)}) %collective-permute-start.13) | collective-permute-done | bytes 65568 | tf_op jit(solution)/shard_map/ppermute | solution.py:617
  61.6 2.7 %collective-permute-start.14 = (f32[2,64,128]{2,1,0:T(8,128)S(1)}, f32[2,64,128]{2,1,0:T(8,128)S(1)}, u32[]{:S(2)}, u32[]{:S(2)}) collective-permute-start(f32[2,64,128]{2,1,0:T(8,128)S(1)} %add_kernel.1.mine), channel_id=1, source_target_pairs={{0,16},{1,17},{2,18},{3,19},{4,20},{5,21},{6,22},{7,23},{8,24},{9,... | collective-permute-start | bytes 196616 | tf_op jit(solution)/shard_map/ppermute | solution.py:617
  64.3 2.6 %collective-permute-done.14.other = f32[2,64,128]{2,1,0:T(8,128)S(1)} collective-permute-done((f32[2,64,128]{2,1,0:T(8,128)S(1)}, f32[2,64,128]{2,1,0:T(8,128)S(1)}, u32[]{:S(2)}, u32[]{:S(2)}) %collective-permute-start.14) | collective-permute-done | bytes 65568 | tf_op jit(solution)/shard_map/ppermute | solution.py:617
  66.9 0.0 copy-done.5
  66.9 0.1 sums_kernel.1
  67.0 1.6 %collective-permute-start.15 = (f32[136,128]{1,0:T(8,128)S(1)}, f32[136,128]{1,0:T(8,128)S(1)}, u32[]{:S(2)}, u32[]{:S(2)}) collective-permute-start(f32[136,128]{1,0:T(8,128)S(1)} %get-tuple-element.44.mine), channel_id=1, source_target_pairs={{0,8},{1,9},{2,10},{3,11},{4,12},{5,13},{6,14},{7,15},{8,0},{9,1},... | collective-permute-start | bytes 208904 | tf_op jit(solution)/shard_map/ppermute | solution.py:617
  68.6 0.0 collective-permute-start.17
  68.6 0.6 collective-permute-start.16
  69.1 2.4 %collective-permute-done.17.s2 = f32[8,128]{1,0:T(8,128)S(1)} collective-permute-done((f32[8,128]{1,0:T(8,128)S(1)}, f32[8,128]{1,0:T(8,128)S(1)}, u32[]{:S(2)}, u32[]{:S(2)}) %collective-permute-start.17) | collective-permute-done | bytes 4128 | tf_op jit(solution)/shard_map/ppermute | solution.py:617
  71.6 0.0 collective-permute-done.16.s1
  71.6 0.0 collective-permute-done.15.other
  71.6 1.6 %collective-permute-start.18 = (f32[264,128]{1,0:T(8,128)S(1)}, f32[264,128]{1,0:T(8,128)S(1)}, u32[]{:S(2)}, u32[]{:S(2)}) collective-permute-start(f32[264,128]{1,0:T(8,128)S(1)} %get-tuple-element.46.mine), channel_id=1, source_target_pairs={{0,4},{1,5},{2,6},{3,7},{4,0},{5,1},{6,2},{7,3},{8,12},{9,13},{10,... | collective-permute-start | bytes 405512 | tf_op jit(solution)/shard_map/ppermute | solution.py:617
  73.2 1.2 %collective-permute-start.20 = (f32[8,128]{1,0:T(8,128)S(1)}, f32[8,128]{1,0:T(8,128)S(1)}, u32[]{:S(2)}, u32[]{:S(2)}) collective-permute-start(f32[8,128]{1,0:T(8,128)S(1)} %get-tuple-element.47.s0), channel_id=1, source_target_pairs={{0,6},{1,7},{2,4},{3,5},{4,2},{5,3},{6,0},{7,1},{8,14},{9,15},{10,... | collective-permute-start | bytes 12296 | tf_op jit(solution)/shard_map/ppermute | solution.py:617
  74.4 0.8 %collective-permute-start.19 = (f32[8,128]{1,0:T(8,128)S(1)}, f32[8,128]{1,0:T(8,128)S(1)}, u32[]{:S(2)}, u32[]{:S(2)}) collective-permute-start(f32[8,128]{1,0:T(8,128)S(1)} %get-tuple-element.47.s0), channel_id=1, source_target_pairs={{0,2},{1,3},{2,0},{3,1},{4,6},{5,7},{6,4},{7,5},{8,10},{9,11},{10,... | collective-permute-start | bytes 12296 | tf_op jit(solution)/shard_map/ppermute | solution.py:617
  75.2 2.5 %collective-permute-done.20.s2 = f32[8,128]{1,0:T(8,128)S(1)} collective-permute-done((f32[8,128]{1,0:T(8,128)S(1)}, f32[8,128]{1,0:T(8,128)S(1)}, u32[]{:S(2)}, u32[]{:S(2)}) %collective-permute-start.20) | collective-permute-done | bytes 4128 | tf_op jit(solution)/shard_map/ppermute | solution.py:617
  77.7 0.3 collective-permute-done.19.s1
  78.0 0.0 collective-permute-done.18.other
  78.0 0.8 finish.1
  (9 shorter events, 0.2 us)
Async XLA Ops:
  2.8 12.4 %collective-permute-start = (f32[4,64,128]{2,1,0:T(8,128)}, f32[4,64,128]{2,1,0:T(8,128)S(1)}, u32[]{:S(2)}, u32[]{:S(2)}) collective-permute-start(f32[4,64,128]{2,1,0:T(8,128)} %get-tuple-element.27), channel_id=1, source_target_pairs={{0,2},{1,3},{2,0},{3,1},{4,6},{5,7},{6,4},{7,5},{8,10},{9,11},{10,... | collective-permute-start | bytes 393224 | tf_op jit(solution)/shard_map/ppermute | solution.py:617
  5.8 12.1 %copy-start.1 = (f32[2,8,64,128]{3,2,1,0:T(8,128)S(1)}, f32[2,8,64,128]{3,2,1,0:T(8,128)}, u32[]{:S(2)}) copy-start(f32[2,8,64,128]{3,2,1,0:T(8,128)} %refs_2_.1) | copy-start | bytes 1572868
  5.8 12.1 %copy-start.2 = (f32[2,8,64,128]{3,2,1,0:T(8,128)S(1)}, f32[2,8,64,128]{3,2,1,0:T(8,128)}, u32[]{:S(2)}) copy-start(f32[2,8,64,128]{3,2,1,0:T(8,128)} %refs_3_.1) | copy-start | bytes 1572868
  5.8 12.1 %copy-start.3 = (f32[2,8,64,128]{3,2,1,0:T(8,128)S(1)}, f32[2,8,64,128]{3,2,1,0:T(8,128)}, u32[]{:S(2)}) copy-start(f32[2,8,64,128]{3,2,1,0:T(8,128)} %refs_4_.1) | copy-start | bytes 1572868
  5.8 12.1 %copy-start.4 = (f32[2,8,64,128]{3,2,1,0:T(8,128)S(1)}, f32[2,8,64,128]{3,2,1,0:T(8,128)}, u32[]{:S(2)}) copy-start(f32[2,8,64,128]{3,2,1,0:T(8,128)} %refs_5_.1) | copy-start | bytes 1572868
  5.8 19.3 %copy-start.7 = (s32[2]{0:T(128)S(1)}, s32[2]{0:T(128)}, u32[]{:S(2)}) copy-start(s32[2]{0:T(128)} %sources.1) | copy-start | bytes 28
  5.8 15.2 %collective-permute-start.4 = (f32[2,8,64,128]{3,2,1,0:T(8,128)}, f32[2,8,64,128]{3,2,1,0:T(8,128)S(1)}, u32[]{:S(2)}, u32[]{:S(2)}) collective-permute-start(f32[2,8,64,128]{3,2,1,0:T(8,128)} %get-tuple-element.30), channel_id=1, source_target_pairs={{0,2},{1,3},{2,0},{3,1},{4,6},{5,7},{6,4},{7,5},{8,10},{9,11},{10,... | collective-permute-start | bytes 1572872 | tf_op jit(solution)/shard_map/ppermute | solution.py:617
  15.2 0.7 copy-start.6
  15.9 5.0 %collective-permute-start.3 = (f32[4,64,128]{2,1,0:T(8,128)S(1)}, f32[4,64,128]{2,1,0:T(8,128)S(1)}, u32[]{:S(2)}, u32[]{:S(2)}) collective-permute-start(f32[4,64,128]{2,1,0:T(8,128)S(1)} %after.3.earlier.mine), channel_id=1, source_target_pairs={{0,4},{1,5},{2,6},{3,7},{4,0},{5,1},{6,2},{7,3},{8,12},{9,13},{10,... | collective-permute-start | bytes 393224 | tf_op jit(solution)/shard_map/ppermute | solution.py:617
  19.3 5.8 %collective-permute-start.2 = (f32[2,8,64,128]{3,2,1,0:T(8,128)S(1)}, f32[2,8,64,128]{3,2,1,0:T(8,128)S(1)}, u32[]{:S(2)}, u32[]{:S(2)}) collective-permute-start(f32[2,8,64,128]{3,2,1,0:T(8,128)S(1)} %get-tuple-element.29.own), channel_id=1, source_target_pairs={{0,1},{1,0},{2,3},{3,2},{4,5},{5,4},{6,7},{7,6},{8,9},{9,8},{10,11... | collective-permute-start | bytes 1572872 | tf_op jit(solution)/shard_map/ppermute | solution.py:617
  21.0 4.0 %collective-permute-start.5 = (f32[2,8,64,128]{3,2,1,0:T(8,128)S(1)}, f32[2,8,64,128]{3,2,1,0:T(8,128)S(1)}, u32[]{:S(2)}, u32[]{:S(2)}) collective-permute-start(f32[2,8,64,128]{3,2,1,0:T(8,128)S(1)} %after.4.over), channel_id=1, source_target_pairs={{0,1},{1,0},{2,3},{3,2},{4,5},{5,4},{6,7},{7,6},{8,9},{9,8},{10,11... | collective-permute-start | bytes 1572872 | tf_op jit(solution)/shard_map/ppermute | solution.py:617
  21.1 14.6 %collective-permute-start.8 = (f32[2,8,64,128]{3,2,1,0:T(8,128)}, f32[2,8,64,128]{3,2,1,0:T(8,128)S(1)}, u32[]{:S(2)}, u32[]{:S(2)}) collective-permute-start(f32[2,8,64,128]{3,2,1,0:T(8,128)} %get-tuple-element.33), channel_id=1, source_target_pairs={{0,2},{1,3},{2,0},{3,1},{4,6},{5,7},{6,4},{7,5},{8,10},{9,11},{10,... | collective-permute-start | bytes 1572872 | tf_op jit(solution)/shard_map/ppermute | solution.py:617
  23.0 1.9 %collective-permute-start.6 = (f32[8,64,128]{2,1,0:T(8,128)}, f32[8,64,128]{2,1,0:T(8,128)}, u32[]{:S(2)}, u32[]{:S(2)}) collective-permute-start(f32[8,64,128]{2,1,0:T(8,128)} %get-tuple-element.31.c0), channel_id=1, source_target_pairs={{0,1},{1,0},{2,3},{3,2},{4,5},{5,4},{6,7},{7,6},{8,9},{9,8},{10,11... | collective-permute-start | bytes 786440 | tf_op jit(solution)/shard_map/ppermute | solution.py:617
  23.2 1.9 %collective-permute-start.7 = (f32[8,64,128]{2,1,0:T(8,128)S(1)}, f32[8,64,128]{2,1,0:T(8,128)}, u32[]{:S(2)}, u32[]{:S(2)}) collective-permute-start(f32[8,64,128]{2,1,0:T(8,128)S(1)} %arrange_kernel.1.earlier.c2), channel_id=1, source_target_pairs={{0,1},{1,0},{2,3},{3,2},{4,5},{5,4},{6,7},{7,6},{8,9},{9,8},{10,11... | collective-permute-start | bytes 786440 | tf_op jit(solution)/shard_map/ppermute | solution.py:617
  24.9 15.6 %collective-permute-start.1 = (f32[2,8,64,128]{3,2,1,0:T(8,128)S(1)}, f32[2,8,64,128]{3,2,1,0:T(8,128)S(1)}, u32[]{:S(2)}, u32[]{:S(2)}) collective-permute-start(f32[2,8,64,128]{3,2,1,0:T(8,128)S(1)} %get-tuple-element.28.own), channel_id=1, source_target_pairs={{0,1},{1,0},{2,3},{3,2},{4,5},{5,4},{6,7},{7,6},{8,9},{9,8},{10,11... | collective-permute-start | bytes 1572872 | tf_op jit(solution)/shard_map/ppermute | solution.py:617
  35.8 4.8 %collective-permute-start.9 = (f32[2,8,64,128]{3,2,1,0:T(8,128)S(1)}, f32[2,8,64,128]{3,2,1,0:T(8,128)S(1)}, u32[]{:S(2)}, u32[]{:S(2)}) collective-permute-start(f32[2,8,64,128]{3,2,1,0:T(8,128)S(1)} %after.5.over), channel_id=1, source_target_pairs={{0,1},{1,0},{2,3},{3,2},{4,5},{5,4},{6,7},{7,6},{8,9},{9,8},{10,11... | collective-permute-start | bytes 1572872 | tf_op jit(solution)/shard_map/ppermute | solution.py:617
  35.8 3.7 %copy-start = (f32[9,2048,128]{2,1,0:T(8,128)S(1)}, f32[9,2048,128]{2,1,0:T(8,128)}, u32[]{:S(2)}) copy-start(f32[9,2048,128]{2,1,0:T(8,128)} %get-tuple-element.35) | copy-start | bytes 28311556
  40.5 26.4 %copy-start.5 = (f32[8,64,128]{2,1,0:T(8,128)S(1)}, f32[8,64,128]{2,1,0:T(8,128)}, u32[]{:S(2)}) copy-start(f32[8,64,128]{2,1,0:T(8,128)} %momentum.3) | copy-start | bytes 786436
  47.0 6.1 %collective-permute-start.10 = (f32[4,64,128]{2,1,0:T(8,128)S(1)}, f32[4,64,128]{2,1,0:T(8,128)S(1)}, u32[]{:S(2)}, u32[]{:S(2)}) collective-permute-start(f32[4,64,128]{2,1,0:T(8,128)S(1)} %get-tuple-element.39), channel_id=1, source_target_pairs={{0,2},{1,3},{2,0},{3,1},{4,6},{5,7},{6,4},{7,5},{8,10},{9,11},{10,... | collective-permute-start | bytes 393224 | tf_op jit(solution)/shard_map/ppermute | solution.py:617
  48.8 8.4 %collective-permute-start.11 = (f32[4,64,128]{2,1,0:T(8,128)S(1)}, f32[4,64,128]{2,1,0:T(8,128)S(1)}, u32[]{:S(2)}, u32[]{:S(2)}) collective-permute-start(f32[4,64,128]{2,1,0:T(8,128)S(1)} %get-tuple-element.40), channel_id=1, source_target_pairs={{0,4},{1,5},{2,6},{3,7},{4,0},{5,1},{6,2},{7,3},{8,12},{9,13},{10,... | collective-permute-start | bytes 393224 | tf_op jit(solution)/shard_map/ppermute | solution.py:617
  50.3 6.9 %collective-permute-start.12 = (f32[4,64,128]{2,1,0:T(8,128)S(1)}, f32[4,64,128]{2,1,0:T(8,128)S(1)}, u32[]{:S(2)}, u32[]{:S(2)}) collective-permute-start(f32[4,64,128]{2,1,0:T(8,128)S(1)} %get-tuple-element.41), channel_id=1, source_target_pairs={{0,6},{1,7},{2,4},{3,5},{4,2},{5,3},{6,0},{7,1},{8,14},{9,15},{10,... | collective-permute-start | bytes 393224 | tf_op jit(solution)/shard_map/ppermute | solution.py:617
  57.3 4.3 %collective-permute-start.13 = (f32[2,64,128]{2,1,0:T(8,128)S(1)}, f32[2,64,128]{2,1,0:T(8,128)S(1)}, u32[]{:S(2)}, u32[]{:S(2)}) collective-permute-start(f32[2,64,128]{2,1,0:T(8,128)S(1)} %get-tuple-element.43), channel_id=1, source_target_pairs={{0,8},{1,9},{2,10},{3,11},{4,12},{5,13},{6,14},{7,15},{8,0},{9,1},... | collective-permute-start | bytes 196616 | tf_op jit(solution)/shard_map/ppermute | solution.py:617
  61.6 5.3 %collective-permute-start.14 = (f32[2,64,128]{2,1,0:T(8,128)S(1)}, f32[2,64,128]{2,1,0:T(8,128)S(1)}, u32[]{:S(2)}, u32[]{:S(2)}) collective-permute-start(f32[2,64,128]{2,1,0:T(8,128)S(1)} %add_kernel.1.mine), channel_id=1, source_target_pairs={{0,16},{1,17},{2,18},{3,19},{4,20},{5,21},{6,22},{7,23},{8,24},{9,... | collective-permute-start | bytes 196616 | tf_op jit(solution)/shard_map/ppermute | solution.py:617
  67.0 4.6 %collective-permute-start.15 = (f32[136,128]{1,0:T(8,128)S(1)}, f32[136,128]{1,0:T(8,128)S(1)}, u32[]{:S(2)}, u32[]{:S(2)}) collective-permute-start(f32[136,128]{1,0:T(8,128)S(1)} %get-tuple-element.44.mine), channel_id=1, source_target_pairs={{0,8},{1,9},{2,10},{3,11},{4,12},{5,13},{6,14},{7,15},{8,0},{9,1},... | collective-permute-start | bytes 208904 | tf_op jit(solution)/shard_map/ppermute | solution.py:617
  68.6 3.0 %collective-permute-start.17 = (f32[8,128]{1,0:T(8,128)S(1)}, f32[8,128]{1,0:T(8,128)S(1)}, u32[]{:S(2)}, u32[]{:S(2)}) collective-permute-start(f32[8,128]{1,0:T(8,128)S(1)} %get-tuple-element.45.s0), channel_id=1, source_target_pairs={{0,9},{1,8},{2,11},{3,10},{4,13},{5,12},{6,15},{7,14},{8,1},{9,0},... | collective-permute-start | bytes 12296 | tf_op jit(solution)/shard_map/ppermute | solution.py:617
  68.6 3.0 %collective-permute-start.16 = (f32[8,128]{1,0:T(8,128)S(1)}, f32[8,128]{1,0:T(8,128)S(1)}, u32[]{:S(2)}, u32[]{:S(2)}) collective-permute-start(f32[8,128]{1,0:T(8,128)S(1)} %get-tuple-element.45.s0), channel_id=1, source_target_pairs={{0,1},{1,0},{2,3},{3,2},{4,5},{5,4},{6,7},{7,6},{8,9},{9,8},{10,11... | collective-permute-start | bytes 12296 | tf_op jit(solution)/shard_map/ppermute | solution.py:617
  71.6 6.4 %collective-permute-start.18 = (f32[264,128]{1,0:T(8,128)S(1)}, f32[264,128]{1,0:T(8,128)S(1)}, u32[]{:S(2)}, u32[]{:S(2)}) collective-permute-start(f32[264,128]{1,0:T(8,128)S(1)} %get-tuple-element.46.mine), channel_id=1, source_target_pairs={{0,4},{1,5},{2,6},{3,7},{4,0},{5,1},{6,2},{7,3},{8,12},{9,13},{10,... | collective-permute-start | bytes 405512 | tf_op jit(solution)/shard_map/ppermute | solution.py:617
  73.2 4.5 %collective-permute-start.20 = (f32[8,128]{1,0:T(8,128)S(1)}, f32[8,128]{1,0:T(8,128)S(1)}, u32[]{:S(2)}, u32[]{:S(2)}) collective-permute-start(f32[8,128]{1,0:T(8,128)S(1)} %get-tuple-element.47.s0), channel_id=1, source_target_pairs={{0,6},{1,7},{2,4},{3,5},{4,2},{5,3},{6,0},{7,1},{8,14},{9,15},{10,... | collective-permute-start | bytes 12296 | tf_op jit(solution)/shard_map/ppermute | solution.py:617
  74.4 3.6 %collective-permute-start.19 = (f32[8,128]{1,0:T(8,128)S(1)}, f32[8,128]{1,0:T(8,128)S(1)}, u32[]{:S(2)}, u32[]{:S(2)}) collective-permute-start(f32[8,128]{1,0:T(8,128)S(1)} %get-tuple-element.47.s0), channel_id=1, source_target_pairs={{0,2},{1,3},{2,0},{3,1},{4,6},{5,7},{6,4},{7,5},{8,10},{9,11},{10,... | collective-permute-start | bytes 12296 | tf_op jit(solution)/shard_map/ppermute | solution.py:617

commit v12 on v10

--- a/solution.py
+++ b/solution.py
@@ -174,20 +174,8 @@
     )(earlier, *fields)
 
 
-def first_kernel(first, second, courant, outgoing, whole, piece, held, held_courant, sems):
-    shot = 1 - lax.axis_index("chip")
-    copies = [
-        pltpu.make_async_copy(first.at[shot], held.at[0], sems.at[0]),
-        pltpu.make_async_copy(second.at[shot], held.at[1], sems.at[1]),
-        pltpu.make_async_copy(courant, held_courant, sems.at[2]),
-    ]
-    for copy in copies:
-        copy.start()
-    for n in range(2):
-        copies[n].wait()
-        interleave(outgoing, (n,), held.at[n])
-    copies[2].wait()
-    interleave(whole, (), held_courant, 1.0 / 12.0)
+def courant_kernel(first, second, courant, whole, piece):
+    interleave(whole, (), courant, 1.0 / 12.0)
     count = piece.shape[0]
     piece[...] = whole[pl.ds(lax.axis_index("shot") % 2 * count, count)]
 
@@ -508,7 +496,7 @@
                 ref[n, pl.ds(i, 8, stride=groups), :] = value[i * 8 : (i + 1) * 8]
 
 
-def square_kernel(mine, by_x, by_y, by_xy, keep, send):
+def square_kernel(mine, by_xy, by_y, by_x, keep, send):
     half = lax.axis_index("shot") // 2 % 2
     count = keep.shape[0]
     for ref, part in ((keep, half), (send, 1 - half)):
@@ -529,20 +517,26 @@
     return result
 
 
-def after_kernel(earlier, value, out):
-    out[...] = value[...]
-
-
-def after(earlier, value):
+def after_kernel(earlier, *refs):
+    out = refs[-1]
+    if len(refs) == 2:
+        out[...] = refs[0][...]
+    else:
+        for n, value in enumerate(refs[:-1]):
+            interleave(out, (n,), value)
+
+
+def after(earlier, *values):
     vmem, anywhere = pl.BlockSpec(memory_space=pltpu.VMEM), pl.BlockSpec(memory_space=pl.ANY)
+    shape = values[0].shape if len(values) == 1 else (len(values), *values[0].shape)
     return pl.pallas_call(
         after_kernel,
-        in_specs=[anywhere, vmem],
+        in_specs=[anywhere] + [vmem] * len(values),
         out_specs=vmem,
-        out_shape=jax.ShapeDtypeStruct(value.shape, jnp.float32),
+        out_shape=jax.ShapeDtypeStruct(shape, jnp.float32),
         compiler_params=pltpu.CompilerParams(vmem_limit_bytes=4 * 2**20),
         name="after",
-    )(earlier, value)
+    )(earlier, *values)
 
 
 def arrange_kernel(mine, other, out):
@@ -638,26 +632,18 @@
     cells_all = planes_all * rows_x * rows_y
     vmem, smem = pl.BlockSpec(memory_space=pltpu.VMEM), pl.BlockSpec(memory_space=pltpu.SMEM)
 
-    hbm = pl.BlockSpec(memory_space=pltpu.HBM)
-    outgoing, c0, piece = pl.pallas_call(
-        first_kernel,
-        in_specs=[hbm] * 3,
-        out_specs=[vmem] * 3,
-        out_shape=[
-            jax.ShapeDtypeStruct((2, planes, rows_x, rows_y), jnp.float32),
-            jax.ShapeDtypeStruct(courant_sq.shape, jnp.float32),
-            jax.ShapeDtypeStruct((planes // 2, rows_x, rows_y), jnp.float32),
-        ],
-        scratch_shapes=[
-            pltpu.VMEM((2, planes, rows_x, rows_y), jnp.float32),
-            pltpu.VMEM(courant_sq.shape, jnp.float32),
-            pltpu.SemaphoreType.DMA((3,)),
-        ],
-        compiler_params=pltpu.CompilerParams(vmem_limit_bytes=63 * 2**20),
-        name="first_to_cross",
-    )(fwd_prev, fwd_cur, courant_sq)
-
-    over = exchange(outgoing, CHIP)
+    across = 1 - lax.axis_index("chip")
+    outgoing = [lax.dynamic_index_in_dim(field, across, 0, keepdims=False) for field in (fwd_prev, fwd_cur)]
+    over = [exchange(field, CHIP) for field in outgoing]
+    slab = jax.ShapeDtypeStruct(courant_sq.shape, jnp.float32)
+    c0, piece = pl.pallas_call(
+        courant_kernel,
+        in_specs=[pl.BlockSpec(memory_space=pl.ANY)] * 2 + [vmem],
+        out_specs=[vmem, vmem],
+        out_shape=[slab, jax.ShapeDtypeStruct((planes // 2, rows_x, rows_y), jnp.float32)],
+        compiler_params=pltpu.CompilerParams(vmem_limit_bytes=4 * 2**20),
+        name="courant",
+    )(*outgoing, courant_sq)
     piece = exchange(piece, CHIP)
 
     placed, mark = scatter(rec_cells, observed, planes_all, rows_x, rows_y)
@@ -670,7 +656,7 @@
     mate = exchange(own, CORE)
     c2 = local(arrange_kernel, [courant_sq.shape], piece, exchange(piece, Y))
     c1, c3 = exchange(c0, CORE), exchange(c2, CORE)
-    over = after(c2, over)
+    over = after(c2, *over)
     far = exchange(over, CORE)
     adj_over = exchange(adj_outgoing, CHIP)
     adj_mate = exchange(adj_own, CORE)
@@ -697,7 +683,7 @@
             pltpu.SemaphoreType.DMA((4,)),
             pltpu.SemaphoreType.DMA((4,)),
         ],
-        compiler_params=pltpu.CompilerParams(vmem_limit_bytes=30 * 2**20),
+        compiler_params=pltpu.CompilerParams(vmem_limit_bytes=25 * 2**20),
         cost_estimate=pl.CostEstimate(flops=1000, bytes_accessed=1000, transcendentals=0),
         name="forward_steps",
     )(ckpt_step[None], src_cells, own, mate, over, far, c0, c1, c2, c3, placed)
@@ -726,7 +712,7 @@
     )(adj_own, adj_mate, adj_over, adj_far, cour, laps, inject, last)
 
     by_xy, by_x, by_y = exchange(send_xy, CHIP + Y), exchange(send_x, CHIP), exchange(send_y, Y)
-    keep, send = local(square_kernel, [quarter] * 2, keep, by_x, by_y, by_xy)
+    keep, send = local(square_kernel, [quarter] * 2, keep, by_xy, by_y, by_x)
     part = local(add_kernel, [quarter], keep, exchange(send, NEAR_Z))
     rows, sums_shape = planes // 4 * rows_x, (8, rows_y)
     data, sums = local(sums_kernel, [(rows + 8, rows_y), sums_shape], part, exchange(part, FAR_Z), momentum)

time: 83.4 us -> 81.5 us (0.977)
  Pallas kernels: 36.2 us -> 30.8 us
  waiting for transfers between devices: 19.2 us -> 22.1 us
  starting transfers between devices: 21.8 us -> 23.3 us
    pallas_call x1, Pallas kernels: 13.4 us -> 9.77 us  [whole_shards(): pl.pallas_call(forward_kernel, in_specs=[smem, smem] + [vmem] * 8 + [pl.B...]
    ppermute x21 -> x22, waiting for transfers between devices: 19.2 us -> 22.1 us  [exchange(): lax.ppermute(value, axes, [(i, i ^ bits) for i in range(lax.axis_size(axe...]
    unnamed x16, local copies, waits for them, and re-layouts: 4.39 us -> 1.65 us
    squeeze x0 -> x2, local copies, waits for them, and re-layouts: none -> 1.94 us  [whole_shards(): lax.dynamic_index_in_dim(field, across, 0, keepdims=False)]
    ppermute x21 -> x22, starting transfers between devices: 21.8 us -> 23.3 us  [exchange(): lax.ppermute(value, axes, [(i, i ^ bits) for i in range(lax.axis_size(axe...]
    pallas_call x4, Pallas kernels: 2.21 us -> 0.95 us  [the longest x1 0.78 us: whole_shards(): pl.pallas_call(courant_kernel, in_specs=[pl.BlockSpec(memory_space=pl.ANY...]
  transfers between devices with their start and end apart: 21 -> 22, of which waited for: 11 -> 14; matrix products, arithmetic and copies ran while one was open for 0% -> 1% of each run, Pallas kernels for 31% -> 27%
where the time goes in v12:
time: 81.5 us; the launch traced here: 81.2 us
  Pallas kernels  30.8 us (38%)
  starting transfers between devices  23.3 us (29%)
  waiting for transfers between devices  22.1 us (27%)
  local copies, waits for them, and re-layouts  3.59 us (4%)
  between operations  1.46 us (2%)
    ppermute x22, starting transfers between devices, exchange(): lax.ppermute(value, axes, [(i, i ^ bits) for i in range(lax.axis_size(axe...  23.3 us
    ppermute x22, waiting for transfers between devices, exchange(): lax.ppermute(value, axes, [(i, i ^ bits) for i in range(lax.axis_size(axe...  22.1 us
    pallas_call x1, Pallas kernels, whole_shards(): pl.pallas_call(forward_kernel, in_specs=[smem, smem] + [vmem] * 8 + [pl.B...  9.77 us
    pallas_call x1, Pallas kernels, scatter(): pl.pallas_call(functools.partial(scatter_kernel, rows_x), grid=(rows_all...  9.13 us
    pallas_call x1, Pallas kernels, whole_shards(): pl.pallas_call(adjoint_kernel, in_specs=[vmem] * 8, out_specs=[vmem] * 4,...  7.66 us
    squeeze x2, local copies, waits for them, and re-layouts, whole_shards(): lax.dynamic_index_in_dim(field, across, 0, keepdims=False)  1.94 us
    unnamed x16, local copies, waits for them, and re-layouts  1.65 us
  transfers between devices with their start and end apart: 22, of which 14 were waited for; matrix products, arithmetic and copies ran while one was open for 1% of the time, Pallas kernels for 27%

profile of v12, /device:TPU:0, one launch (start us, length us, event | category | flops | bytes accessed | tf_op | source)
XLA Modules:
  0.0 81.2 jit_solution(16163956132173119687)
XLA Ops:
  0.6 1.0 %dynamic-slice_bitcast_fusion.1.first = f32[8,64,128]{2,1,0:T(8,128)S(1)} fusion(f32[2,8,64,128]{3,2,1,0:T(8,128)} %refs_4_.1, s32[]{:T(128)S(6)} %select_n.5), kind=kLoop, calls=%fused_computation.1 | loop fusion | bytes 524292 | tf_op jit(solution)/shard_map/jit(dynamic_index_in_dim)/squeeze | solution.py:636
  1.6 3.0 %collective-permute-start.4 = (f32[8,64,128]{2,1,0:T(8,128)S(1)}, f32[8,64,128]{2,1,0:T(8,128)S(1)}, u32[]{:S(2)}, u32[]{:S(2)}) collective-permute-start(f32[8,64,128]{2,1,0:T(8,128)S(1)} %dynamic-slice_bitcast_fusion.1.first), channel_id=1, source_target_pairs={{0,2},{1,3},{2,0},{3,1},{4,6},{5,7},{6,4},{7,5},{8,10},{9,11},{10,... | collective-permute-start | bytes 786440 | tf_op jit(solution)/shard_map/ppermute | solution.py:620
  4.6 1.0 %dynamic-slice_bitcast_fusion.second = f32[8,64,128]{2,1,0:T(8,128)S(1)} fusion(f32[2,8,64,128]{3,2,1,0:T(8,128)} %refs_5_.1, s32[]{:T(128)S(6)} %select_n.5), kind=kLoop, calls=%fused_computation | loop fusion | bytes 524292 | tf_op jit(solution)/shard_map/jit(dynamic_index_in_dim)/squeeze | solution.py:636
  5.6 0.1 collective-permute-start.5
  5.7 0.9 %copy-done.5 = f32[8,64,128]{2,1,0:T(8,128)S(1)} copy-done((f32[8,64,128]{2,1,0:T(8,128)S(1)}, f32[8,64,128]{2,1,0:T(8,128)}, u32[]{:S(2)}) %copy-start.5) | copy-done | bytes 262168
  6.6 0.8 courant.2
  7.4 0.0 copy-start.7
  7.4 2.1 %collective-permute-start = (f32[4,64,128]{2,1,0:T(8,128)S(1)}, f32[4,64,128]{2,1,0:T(8,128)S(1)}, u32[]{:S(2)}, u32[]{:S(2)}) collective-permute-start(f32[4,64,128]{2,1,0:T(8,128)S(1)} %get-tuple-element.27), channel_id=1, source_target_pairs={{0,2},{1,3},{2,0},{3,1},{4,6},{5,7},{6,4},{7,5},{8,10},{9,11},{10,... | collective-permute-start | bytes 393224 | tf_op jit(solution)/shard_map/ppermute | solution.py:620
  9.5 9.1 %receiver_scatter.1 = (f32[9,2048,128]{2,1,0:T(8,128)}, f32[8,128]{1,0:T(8,128)}) custom-call(s32[2,512]{1,0:T(2,128)} %cells_ref.1, f32[2,8,512]{2,1,0:T(8,128)} %observed_ref.1), custom_call_target="tpu_custom_call" | custom-call | flops 4831838208 | bytes 9437184 | tf_op jit(solution)/shard_map/receiver_scatter/pallas_call | solution.py:286
  18.6 0.7 collective-permute-done.refs_0_
  19.3 0.7 copy-done.6
  20.0 1.8 %collective-permute-start.3 = (f32[4,64,128]{2,1,0:T(8,128)S(1)}, f32[4,64,128]{2,1,0:T(8,128)S(1)}, u32[]{:S(2)}, u32[]{:S(2)}) collective-permute-start(f32[4,64,128]{2,1,0:T(8,128)S(1)} %after.3.earlier.mine), channel_id=1, source_target_pairs={{0,4},{1,5},{2,6},{3,7},{4,0},{5,1},{6,2},{7,3},{8,12},{9,13},{10,... | collective-permute-start | bytes 393224 | tf_op jit(solution)/shard_map/ppermute | solution.py:620
  21.9 0.0 copy-done
  21.9 0.0 copy-done.1
  21.9 0.0 copy-done.2
  21.9 0.0 copy-done.3
  21.9 1.4 %pick.1 = (f32[2,8,64,128]{3,2,1,0:T(8,128)}, f32[2,8,64,128]{3,2,1,0:T(8,128)S(1)}, f32[2,8,64,128]{3,2,1,0:T(8,128)S(1)}) custom-call(f32[4,64,128]{2,1,0:T(8,128)S(1)} %after.3.earlier.mine, f32[2,8,64,128]{3,2,1,0:T(8,128)S(1)} %copy-done, f32[2,8,64,128]{3,2,1,0:T(8,128)S(1)} %copy-done.1, f32[2,8,64,128]{3,2,1,0:T(8,128)S(1)} %copy-done, ...), custom_call_target="tpu_custom_call" | custom-call | tf_op jit(solution)/shard_map/pick/pallas_call | solution.py:166
  23.2 0.1 collective-permute-start.2
  23.3 1.7 %collective-permute-done.3.other = f32[4,64,128]{2,1,0:T(8,128)S(1)} collective-permute-done((f32[4,64,128]{2,1,0:T(8,128)S(1)}, f32[4,64,128]{2,1,0:T(8,128)S(1)}, u32[]{:S(2)}, u32[]{:S(2)}) %collective-permute-start.3) | collective-permute-done | bytes 131104 | tf_op jit(solution)/shard_map/ppermute | solution.py:620
  25.1 0.0 collective-permute-done.4.refs_0_
  25.1 0.0 collective-permute-done.5.refs_1_
  25.1 0.1 after.4.over
  25.3 0.1 collective-permute-start.6
  25.3 1.8 %collective-permute-start.9 = (f32[2,8,64,128]{3,2,1,0:T(8,128)}, f32[2,8,64,128]{3,2,1,0:T(8,128)S(1)}, u32[]{:S(2)}, u32[]{:S(2)}) collective-permute-start(f32[2,8,64,128]{3,2,1,0:T(8,128)} %get-tuple-element.33), channel_id=1, source_target_pairs={{0,2},{1,3},{2,0},{3,1},{4,6},{5,7},{6,4},{7,5},{8,10},{9,11},{10,... | collective-permute-start | bytes 1572872 | tf_op jit(solution)/shard_map/ppermute | solution.py:620
  27.2 0.2 collective-permute-start.7
  27.3 0.3 collective-permute-start.8
  28.3 0.7 collective-permute-done.7.c1
  29.0 0.2 collective-permute-start.1
  29.2 0.0 collective-permute-done.8.c3
  29.2 0.0 collective-permute-done.2.mate
  29.2 0.0 collective-permute-done.6.far
  29.2 0.0 copy-done.7
  29.2 9.8 %forward_steps.1 = (f32[8,8,2,64,128]{4,3,2,1,0:T(8,128)S(1)}, f32[8,32,64,128]{3,2,1,0:T(8,128)S(1)}, f32[9,32,64,128]{3,2,1,0:T(8,128)S(1)}, f32[32,64,128]{2,1,0:T(8,128)S(1)}, f32[16,64,128]{2,1,0:T(8,128)S(1)}) custom-call(s32[1]{0:T(128)} %bitcast.7.start, s32[2]{0:T(128)S(1)} %copy-done.7, f32[2,8,64,128]{3,2,1,0:T(8,128)S(1)} %get-tuple-element.29.own, ...), custom_call_target="tpu_custom_call" | custom-call | flops 1000 | bytes 1000 | tf_op jit(solution)/shard_map/forward_steps/pallas_call | solution.py:669
  39.0 0.9 %collective-permute-done.9.refs_0_ = f32[2,8,64,128]{3,2,1,0:T(8,128)S(1)} collective-permute-done((f32[2,8,64,128]{3,2,1,0:T(8,128)}, f32[2,8,64,128]{3,2,1,0:T(8,128)S(1)}, u32[]{:S(2)}, u32[]{:S(2)}) %collective-permute-start.9) | collective-permute-done | bytes 524320 | tf_op jit(solution)/shard_map/ppermute | solution.py:620
  39.9 0.1 collective-permute-start.10
  40.0 1.0 %inject.1 = f32[8,32,64,128]{3,2,1,0:T(8,128)S(1)} custom-call(f32[9,32,64,128]{3,2,1,0:T(8,128)S(1)} %get-tuple-element.35.held, f32[8,32,64,128]{3,2,1,0:T(8,128)S(1)} %get-tuple-element.36.history), custom_call_target="tpu_custom_call" | custom-call | tf_op jit(solution)/shard_map/inject/pallas_call | solution.py:693
  41.0 0.0 collective-permute-done.1.mate
  41.0 0.9 %collective-permute-done.10.far = f32[2,8,64,128]{3,2,1,0:T(8,128)S(1)} collective-permute-done((f32[2,8,64,128]{3,2,1,0:T(8,128)S(1)}, f32[2,8,64,128]{3,2,1,0:T(8,128)S(1)}, u32[]{:S(2)}, u32[]{:S(2)}) %collective-permute-start.10) | collective-permute-done | bytes 524320 | tf_op jit(solution)/shard_map/ppermute | solution.py:620
  41.9 7.7 %adjoint_steps.1 = (f32[4,64,128]{2,1,0:T(8,128)S(1)}, f32[4,64,128]{2,1,0:T(8,128)S(1)}, f32[4,64,128]{2,1,0:T(8,128)S(1)}, f32[4,64,128]{2,1,0:T(8,128)S(1)}) custom-call(f32[2,8,64,128]{3,2,1,0:T(8,128)S(1)} %get-tuple-element.28.own, f32[2,8,64,128]{3,2,1,0:T(8,128)S(1)} %collective-permute-done.1.mate, f32[2,8,64,128]{3,2,1,0:T(8,128)S(1)} %after.5.over, ...), custom_call_target="tpu_custom_call" | custom-call | flops 62914560 | bytes 33554432 | tf_op jit(solution)/shard_map/adjoint_steps/pallas_call | solution.py:703
  49.6 2.8 %collective-permute-start.11 = (f32[4,64,128]{2,1,0:T(8,128)S(1)}, f32[4,64,128]{2,1,0:T(8,128)S(1)}, u32[]{:S(2)}, u32[]{:S(2)}) collective-permute-start(f32[4,64,128]{2,1,0:T(8,128)S(1)} %get-tuple-element.39), channel_id=1, source_target_pairs={{0,6},{1,7},{2,4},{3,5},{4,2},{5,3},{6,0},{7,1},{8,14},{9,15},{10,... | collective-permute-start | bytes 393224 | tf_op jit(solution)/shard_map/ppermute | solution.py:620
  52.3 0.5 collective-permute-start.12
  52.9 0.3 collective-permute-start.13
  53.1 3.1 %collective-permute-done.11.by_xy = f32[4,64,128]{2,1,0:T(8,128)S(1)} collective-permute-done((f32[4,64,128]{2,1,0:T(8,128)S(1)}, f32[4,64,128]{2,1,0:T(8,128)S(1)}, u32[]{:S(2)}, u32[]{:S(2)}) %collective-permute-start.11) | collective-permute-done | bytes 131104 | tf_op jit(solution)/shard_map/ppermute | solution.py:620
  56.2 2.7 %collective-permute-done.12.by_y = f32[4,64,128]{2,1,0:T(8,128)S(1)} collective-permute-done((f32[4,64,128]{2,1,0:T(8,128)S(1)}, f32[4,64,128]{2,1,0:T(8,128)S(1)}, u32[]{:S(2)}, u32[]{:S(2)}) %collective-permute-start.12) | collective-permute-done | bytes 131104 | tf_op jit(solution)/shard_map/ppermute | solution.py:620
  58.9 0.3 collective-permute-done.13.by_x
  59.3 1.6 %collective-permute-start.14 = (f32[2,64,128]{2,1,0:T(8,128)S(1)}, f32[2,64,128]{2,1,0:T(8,128)S(1)}, u32[]{:S(2)}, u32[]{:S(2)}) collective-permute-start(f32[2,64,128]{2,1,0:T(8,128)S(1)} %get-tuple-element.43), channel_id=1, source_target_pairs={{0,8},{1,9},{2,10},{3,11},{4,12},{5,13},{6,14},{7,15},{8,0},{9,1},... | collective-permute-start | bytes 196616 | tf_op jit(solution)/shard_map/ppermute | solution.py:620
  60.9 2.7 %collective-permute-done.14.other = f32[2,64,128]{2,1,0:T(8,128)S(1)} collective-permute-done((f32[2,64,128]{2,1,0:T(8,128)S(1)}, f32[2,64,128]{2,1,0:T(8,128)S(1)}, u32[]{:S(2)}, u32[]{:S(2)}) %collective-permute-start.14) | collective-permute-done | bytes 65568 | tf_op jit(solution)/shard_map/ppermute | solution.py:620
  63.6 2.7 %collective-permute-start.15 = (f32[2,64,128]{2,1,0:T(8,128)S(1)}, f32[2,64,128]{2,1,0:T(8,128)S(1)}, u32[]{:S(2)}, u32[]{:S(2)}) collective-permute-start(f32[2,64,128]{2,1,0:T(8,128)S(1)} %add_kernel.1.mine), channel_id=1, source_target_pairs={{0,16},{1,17},{2,18},{3,19},{4,20},{5,21},{6,22},{7,23},{8,24},{9,... | collective-permute-start | bytes 196616 | tf_op jit(solution)/shard_map/ppermute | solution.py:620
  66.3 2.6 %collective-permute-done.15.other = f32[2,64,128]{2,1,0:T(8,128)S(1)} collective-permute-done((f32[2,64,128]{2,1,0:T(8,128)S(1)}, f32[2,64,128]{2,1,0:T(8,128)S(1)}, u32[]{:S(2)}, u32[]{:S(2)}) %collective-permute-start.15) | collective-permute-done | bytes 65568 | tf_op jit(solution)/shard_map/ppermute | solution.py:620
  68.8 0.0 copy-done.4
  68.8 0.1 sums_kernel.1
  68.9 1.6 %collective-permute-start.16 = (f32[136,128]{1,0:T(8,128)S(1)}, f32[136,128]{1,0:T(8,128)S(1)}, u32[]{:S(2)}, u32[]{:S(2)}) collective-permute-start(f32[136,128]{1,0:T(8,128)S(1)} %get-tuple-element.44.mine), channel_id=1, source_target_pairs={{0,8},{1,9},{2,10},{3,11},{4,12},{5,13},{6,14},{7,15},{8,0},{9,1},... | collective-permute-start | bytes 208904 | tf_op jit(solution)/shard_map/ppermute | solution.py:620
  70.5 0.0 collective-permute-start.17
  70.5 0.6 collective-permute-start.18
  71.1 0.6 collective-permute-done.17.s1
  71.7 1.9 %collective-permute-done.18.s2 = f32[8,128]{1,0:T(8,128)S(1)} collective-permute-done((f32[8,128]{1,0:T(8,128)S(1)}, f32[8,128]{1,0:T(8,128)S(1)}, u32[]{:S(2)}, u32[]{:S(2)}) %collective-permute-start.18) | collective-permute-done | bytes 4128 | tf_op jit(solution)/shard_map/ppermute | solution.py:620
  73.6 0.0 collective-permute-done.16.other
  73.6 1.5 %collective-permute-start.19 = (f32[264,128]{1,0:T(8,128)S(1)}, f32[264,128]{1,0:T(8,128)S(1)}, u32[]{:S(2)}, u32[]{:S(2)}) collective-permute-start(f32[264,128]{1,0:T(8,128)S(1)} %get-tuple-element.46.mine), channel_id=1, source_target_pairs={{0,4},{1,5},{2,6},{3,7},{4,0},{5,1},{6,2},{7,3},{8,12},{9,13},{10,... | collective-permute-start | bytes 405512 | tf_op jit(solution)/shard_map/ppermute | solution.py:620
  75.1 0.8 collective-permute-start.20
  75.9 1.3 %collective-permute-start.21 = (f32[8,128]{1,0:T(8,128)S(1)}, f32[8,128]{1,0:T(8,128)S(1)}, u32[]{:S(2)}, u32[]{:S(2)}) collective-permute-start(f32[8,128]{1,0:T(8,128)S(1)} %get-tuple-element.47.s0), channel_id=1, source_target_pairs={{0,6},{1,7},{2,4},{3,5},{4,2},{5,3},{6,0},{7,1},{8,14},{9,15},{10,... | collective-permute-start | bytes 12296 | tf_op jit(solution)/shard_map/ppermute | solution.py:620
  77.2 1.6 %collective-permute-done.20.s1 = f32[8,128]{1,0:T(8,128)S(1)} collective-permute-done((f32[8,128]{1,0:T(8,128)S(1)}, f32[8,128]{1,0:T(8,128)S(1)}, u32[]{:S(2)}, u32[]{:S(2)}) %collective-permute-start.20) | collective-permute-done | bytes 4128 | tf_op jit(solution)/shard_map/ppermute | solution.py:620
  78.7 1.7 %collective-permute-done.21.s2 = f32[8,128]{1,0:T(8,128)S(1)} collective-permute-done((f32[8,128]{1,0:T(8,128)S(1)}, f32[8,128]{1,0:T(8,128)S(1)}, u32[]{:S(2)}, u32[]{:S(2)}) %collective-permute-start.21) | collective-permute-done | bytes 4128 | tf_op jit(solution)/shard_map/ppermute | solution.py:620
  80.4 0.0 collective-permute-done.19.other
  80.4 0.8 finish.1
  (13 shorter events, 0.1 us)
Async XLA Ops:
  1.6 23.5 %collective-permute-start.4 = (f32[8,64,128]{2,1,0:T(8,128)S(1)}, f32[8,64,128]{2,1,0:T(8,128)S(1)}, u32[]{:S(2)}, u32[]{:S(2)}) collective-permute-start(f32[8,64,128]{2,1,0:T(8,128)S(1)} %dynamic-slice_bitcast_fusion.1.first), channel_id=1, source_target_pairs={{0,2},{1,3},{2,0},{3,1},{4,6},{5,7},{6,4},{7,5},{8,10},{9,11},{10,... | collective-permute-start | bytes 786440 | tf_op jit(solution)/shard_map/ppermute | solution.py:620
  5.6 19.5 %collective-permute-start.5 = (f32[8,64,128]{2,1,0:T(8,128)S(1)}, f32[8,64,128]{2,1,0:T(8,128)S(1)}, u32[]{:S(2)}, u32[]{:S(2)}) collective-permute-start(f32[8,64,128]{2,1,0:T(8,128)S(1)} %dynamic-slice_bitcast_fusion.second), channel_id=1, source_target_pairs={{0,2},{1,3},{2,0},{3,1},{4,6},{5,7},{6,4},{7,5},{8,10},{9,11},{10,... | collective-permute-start | bytes 786440 | tf_op jit(solution)/shard_map/ppermute | solution.py:620
  5.7 0.9 %copy-start.5 = (f32[8,64,128]{2,1,0:T(8,128)S(1)}, f32[8,64,128]{2,1,0:T(8,128)}, u32[]{:S(2)}) copy-start(f32[8,64,128]{2,1,0:T(8,128)} %courant.3) | copy-start | bytes 786436
  7.4 14.5 %copy-start = (f32[2,8,64,128]{3,2,1,0:T(8,128)S(1)}, f32[2,8,64,128]{3,2,1,0:T(8,128)}, u32[]{:S(2)}) copy-start(f32[2,8,64,128]{3,2,1,0:T(8,128)} %refs_2_.1) | copy-start | bytes 1572868
  7.4 14.5 %copy-start.1 = (f32[2,8,64,128]{3,2,1,0:T(8,128)S(1)}, f32[2,8,64,128]{3,2,1,0:T(8,128)}, u32[]{:S(2)}) copy-start(f32[2,8,64,128]{3,2,1,0:T(8,128)} %refs_3_.1) | copy-start | bytes 1572868
  7.4 14.5 %copy-start.2 = (f32[2,8,64,128]{3,2,1,0:T(8,128)S(1)}, f32[2,8,64,128]{3,2,1,0:T(8,128)}, u32[]{:S(2)}) copy-start(f32[2,8,64,128]{3,2,1,0:T(8,128)} %refs_4_.1) | copy-start | bytes 1572868
  7.4 14.5 %copy-start.3 = (f32[2,8,64,128]{3,2,1,0:T(8,128)S(1)}, f32[2,8,64,128]{3,2,1,0:T(8,128)}, u32[]{:S(2)}) copy-start(f32[2,8,64,128]{3,2,1,0:T(8,128)} %refs_5_.1) | copy-start | bytes 1572868
  7.4 21.8 %copy-start.7 = (s32[2]{0:T(128)S(1)}, s32[2]{0:T(128)}, u32[]{:S(2)}) copy-start(s32[2]{0:T(128)} %sources.1) | copy-start | bytes 28
  7.4 11.9 %collective-permute-start = (f32[4,64,128]{2,1,0:T(8,128)S(1)}, f32[4,64,128]{2,1,0:T(8,128)S(1)}, u32[]{:S(2)}, u32[]{:S(2)}) collective-permute-start(f32[4,64,128]{2,1,0:T(8,128)S(1)} %get-tuple-element.27), channel_id=1, source_target_pairs={{0,2},{1,3},{2,0},{3,1},{4,6},{5,7},{6,4},{7,5},{8,10},{9,11},{10,... | collective-permute-start | bytes 393224 | tf_op jit(solution)/shard_map/ppermute | solution.py:620
  19.3 0.7 copy-start.6
  20.0 5.0 %collective-permute-start.3 = (f32[4,64,128]{2,1,0:T(8,128)S(1)}, f32[4,64,128]{2,1,0:T(8,128)S(1)}, u32[]{:S(2)}, u32[]{:S(2)}) collective-permute-start(f32[4,64,128]{2,1,0:T(8,128)S(1)} %after.3.earlier.mine), channel_id=1, source_target_pairs={{0,4},{1,5},{2,6},{3,7},{4,0},{5,1},{6,2},{7,3},{8,12},{9,13},{10,... | collective-permute-start | bytes 393224 | tf_op jit(solution)/shard_map/ppermute | solution.py:620
  23.2 6.0 %collective-permute-start.2 = (f32[2,8,64,128]{3,2,1,0:T(8,128)S(1)}, f32[2,8,64,128]{3,2,1,0:T(8,128)S(1)}, u32[]{:S(2)}, u32[]{:S(2)}) collective-permute-start(f32[2,8,64,128]{3,2,1,0:T(8,128)S(1)} %get-tuple-element.29.own), channel_id=1, source_target_pairs={{0,1},{1,0},{2,3},{3,2},{4,5},{5,4},{6,7},{7,6},{8,9},{9,8},{10,11... | collective-permute-start | bytes 1572872 | tf_op jit(solution)/shard_map/ppermute | solution.py:620
  25.3 3.9 %collective-permute-start.6 = (f32[2,8,64,128]{3,2,1,0:T(8,128)S(1)}, f32[2,8,64,128]{3,2,1,0:T(8,128)S(1)}, u32[]{:S(2)}, u32[]{:S(2)}) collective-permute-start(f32[2,8,64,128]{3,2,1,0:T(8,128)S(1)} %after.4.over), channel_id=1, source_target_pairs={{0,1},{1,0},{2,3},{3,2},{4,5},{5,4},{6,7},{7,6},{8,9},{9,8},{10,11... | collective-permute-start | bytes 1572872 | tf_op jit(solution)/shard_map/ppermute | solution.py:620
  25.3 14.6 %collective-permute-start.9 = (f32[2,8,64,128]{3,2,1,0:T(8,128)}, f32[2,8,64,128]{3,2,1,0:T(8,128)S(1)}, u32[]{:S(2)}, u32[]{:S(2)}) collective-permute-start(f32[2,8,64,128]{3,2,1,0:T(8,128)} %get-tuple-element.33), channel_id=1, source_target_pairs={{0,2},{1,3},{2,0},{3,1},{4,6},{5,7},{6,4},{7,5},{8,10},{9,11},{10,... | collective-permute-start | bytes 1572872 | tf_op jit(solution)/shard_map/ppermute | solution.py:620
  27.2 1.9 %collective-permute-start.7 = (f32[8,64,128]{2,1,0:T(8,128)}, f32[8,64,128]{2,1,0:T(8,128)}, u32[]{:S(2)}, u32[]{:S(2)}) collective-permute-start(f32[8,64,128]{2,1,0:T(8,128)} %get-tuple-element.30.c0), channel_id=1, source_target_pairs={{0,1},{1,0},{2,3},{3,2},{4,5},{5,4},{6,7},{7,6},{8,9},{9,8},{10,11... | collective-permute-start | bytes 786440 | tf_op jit(solution)/shard_map/ppermute | solution.py:620
  27.3 1.9 %collective-permute-start.8 = (f32[8,64,128]{2,1,0:T(8,128)S(1)}, f32[8,64,128]{2,1,0:T(8,128)}, u32[]{:S(2)}, u32[]{:S(2)}) collective-permute-start(f32[8,64,128]{2,1,0:T(8,128)S(1)} %arrange_kernel.1.earlier.c2), channel_id=1, source_target_pairs={{0,1},{1,0},{2,3},{3,2},{4,5},{5,4},{6,7},{7,6},{8,9},{9,8},{10,11... | collective-permute-start | bytes 786440 | tf_op jit(solution)/shard_map/ppermute | solution.py:620
  29.0 12.0 %collective-permute-start.1 = (f32[2,8,64,128]{3,2,1,0:T(8,128)S(1)}, f32[2,8,64,128]{3,2,1,0:T(8,128)S(1)}, u32[]{:S(2)}, u32[]{:S(2)}) collective-permute-start(f32[2,8,64,128]{3,2,1,0:T(8,128)S(1)} %get-tuple-element.28.own), channel_id=1, source_target_pairs={{0,1},{1,0},{2,3},{3,2},{4,5},{5,4},{6,7},{7,6},{8,9},{9,8},{10,11... | collective-permute-start | bytes 1572872 | tf_op jit(solution)/shard_map/ppermute | solution.py:620
  39.9 2.0 %collective-permute-start.10 = (f32[2,8,64,128]{3,2,1,0:T(8,128)S(1)}, f32[2,8,64,128]{3,2,1,0:T(8,128)S(1)}, u32[]{:S(2)}, u32[]{:S(2)}) collective-permute-start(f32[2,8,64,128]{3,2,1,0:T(8,128)S(1)} %after.5.over), channel_id=1, source_target_pairs={{0,1},{1,0},{2,3},{3,2},{4,5},{5,4},{6,7},{7,6},{8,9},{9,8},{10,11... | collective-permute-start | bytes 1572872 | tf_op jit(solution)/shard_map/ppermute | solution.py:620
  41.9 26.9 %copy-start.4 = (f32[8,64,128]{2,1,0:T(8,128)S(1)}, f32[8,64,128]{2,1,0:T(8,128)}, u32[]{:S(2)}) copy-start(f32[8,64,128]{2,1,0:T(8,128)} %momentum.3) | copy-start | bytes 786436
  49.6 6.7 %collective-permute-start.11 = (f32[4,64,128]{2,1,0:T(8,128)S(1)}, f32[4,64,128]{2,1,0:T(8,128)S(1)}, u32[]{:S(2)}, u32[]{:S(2)}) collective-permute-start(f32[4,64,128]{2,1,0:T(8,128)S(1)} %get-tuple-element.39), channel_id=1, source_target_pairs={{0,6},{1,7},{2,4},{3,5},{4,2},{5,3},{6,0},{7,1},{8,14},{9,15},{10,... | collective-permute-start | bytes 393224 | tf_op jit(solution)/shard_map/ppermute | solution.py:620
  52.3 6.6 %collective-permute-start.12 = (f32[4,64,128]{2,1,0:T(8,128)S(1)}, f32[4,64,128]{2,1,0:T(8,128)S(1)}, u32[]{:S(2)}, u32[]{:S(2)}) collective-permute-start(f32[4,64,128]{2,1,0:T(8,128)S(1)} %get-tuple-element.40), channel_id=1, source_target_pairs={{0,4},{1,5},{2,6},{3,7},{4,0},{5,1},{6,2},{7,3},{8,12},{9,13},{10,... | collective-permute-start | bytes 393224 | tf_op jit(solution)/shard_map/ppermute | solution.py:620
  52.9 6.4 %collective-permute-start.13 = (f32[4,64,128]{2,1,0:T(8,128)S(1)}, f32[4,64,128]{2,1,0:T(8,128)S(1)}, u32[]{:S(2)}, u32[]{:S(2)}) collective-permute-start(f32[4,64,128]{2,1,0:T(8,128)S(1)} %get-tuple-element.41), channel_id=1, source_target_pairs={{0,2},{1,3},{2,0},{3,1},{4,6},{5,7},{6,4},{7,5},{8,10},{9,11},{10,... | collective-permute-start | bytes 393224 | tf_op jit(solution)/shard_map/ppermute | solution.py:620
  59.3 4.3 %collective-permute-start.14 = (f32[2,64,128]{2,1,0:T(8,128)S(1)}, f32[2,64,128]{2,1,0:T(8,128)S(1)}, u32[]{:S(2)}, u32[]{:S(2)}) collective-permute-start(f32[2,64,128]{2,1,0:T(8,128)S(1)} %get-tuple-element.43), channel_id=1, source_target_pairs={{0,8},{1,9},{2,10},{3,11},{4,12},{5,13},{6,14},{7,15},{8,0},{9,1},... | collective-permute-start | bytes 196616 | tf_op jit(solution)/shard_map/ppermute | solution.py:620
  63.6 5.2 %collective-permute-start.15 = (f32[2,64,128]{2,1,0:T(8,128)S(1)}, f32[2,64,128]{2,1,0:T(8,128)S(1)}, u32[]{:S(2)}, u32[]{:S(2)}) collective-permute-start(f32[2,64,128]{2,1,0:T(8,128)S(1)} %add_kernel.1.mine), channel_id=1, source_target_pairs={{0,16},{1,17},{2,18},{3,19},{4,20},{5,21},{6,22},{7,23},{8,24},{9,... | collective-permute-start | bytes 196616 | tf_op jit(solution)/shard_map/ppermute | solution.py:620
  68.9 4.6 %collective-permute-start.16 = (f32[136,128]{1,0:T(8,128)S(1)}, f32[136,128]{1,0:T(8,128)S(1)}, u32[]{:S(2)}, u32[]{:S(2)}) collective-permute-start(f32[136,128]{1,0:T(8,128)S(1)} %get-tuple-element.44.mine), channel_id=1, source_target_pairs={{0,8},{1,9},{2,10},{3,11},{4,12},{5,13},{6,14},{7,15},{8,0},{9,1},... | collective-permute-start | bytes 208904 | tf_op jit(solution)/shard_map/ppermute | solution.py:620
  70.5 1.2 %collective-permute-start.17 = (f32[8,128]{1,0:T(8,128)S(1)}, f32[8,128]{1,0:T(8,128)S(1)}, u32[]{:S(2)}, u32[]{:S(2)}) collective-permute-start(f32[8,128]{1,0:T(8,128)S(1)} %get-tuple-element.45.s0), channel_id=1, source_target_pairs={{0,1},{1,0},{2,3},{3,2},{4,5},{5,4},{6,7},{7,6},{8,9},{9,8},{10,11... | collective-permute-start | bytes 12296 | tf_op jit(solution)/shard_map/ppermute | solution.py:620
  70.5 3.0 %collective-permute-start.18 = (f32[8,128]{1,0:T(8,128)S(1)}, f32[8,128]{1,0:T(8,128)S(1)}, u32[]{:S(2)}, u32[]{:S(2)}) collective-permute-start(f32[8,128]{1,0:T(8,128)S(1)} %get-tuple-element.45.s0), channel_id=1, source_target_pairs={{0,9},{1,8},{2,11},{3,10},{4,13},{5,12},{6,15},{7,14},{8,1},{9,0},... | collective-permute-start | bytes 12296 | tf_op jit(solution)/shard_map/ppermute | solution.py:620
  73.6 6.8 %collective-permute-start.19 = (f32[264,128]{1,0:T(8,128)S(1)}, f32[264,128]{1,0:T(8,128)S(1)}, u32[]{:S(2)}, u32[]{:S(2)}) collective-permute-start(f32[264,128]{1,0:T(8,128)S(1)} %get-tuple-element.46.mine), channel_id=1, source_target_pairs={{0,4},{1,5},{2,6},{3,7},{4,0},{5,1},{6,2},{7,3},{8,12},{9,13},{10,... | collective-permute-start | bytes 405512 | tf_op jit(solution)/shard_map/ppermute | solution.py:620
  75.1 3.6 %collective-permute-start.20 = (f32[8,128]{1,0:T(8,128)S(1)}, f32[8,128]{1,0:T(8,128)S(1)}, u32[]{:S(2)}, u32[]{:S(2)}) collective-permute-start(f32[8,128]{1,0:T(8,128)S(1)} %get-tuple-element.47.s0), channel_id=1, source_target_pairs={{0,2},{1,3},{2,0},{3,1},{4,6},{5,7},{6,4},{7,5},{8,10},{9,11},{10,... | collective-permute-start | bytes 12296 | tf_op jit(solution)/shard_map/ppermute | solution.py:620
  75.9 4.5 %collective-permute-start.21 = (f32[8,128]{1,0:T(8,128)S(1)}, f32[8,128]{1,0:T(8,128)S(1)}, u32[]{:S(2)}, u32[]{:S(2)}) collective-permute-start(f32[8,128]{1,0:T(8,128)S(1)} %get-tuple-element.47.s0), channel_id=1, source_target_pairs={{0,6},{1,7},{2,4},{3,5},{4,2},{5,3},{6,0},{7,1},{8,14},{9,15},{10,... | collective-permute-start | bytes 12296 | tf_op jit(solution)/shard_map/ppermute | solution.py:620

commit v13 on v10

--- a/solution.py
+++ b/solution.py
@@ -198,15 +198,15 @@
 
 
 def along_y(field, z, banded, out):
-    rows, lanes = field.shape[1:]
-    whole = field[pl.ds(z + 2, BATCH)].reshape(BATCH * rows, lanes)
+    rows, lanes = field.shape[1] - 8, field.shape[2]
+    whole = field[pl.ds(z + 2, BATCH), 0:rows].reshape(BATCH * rows, lanes)
     high = whole.astype(jnp.bfloat16)
     low = (whole - high.astype(jnp.float32)).astype(jnp.bfloat16)
     out[...] = jnp.dot(jnp.concatenate([high, low], 1), banded[...], preferred_element_type=jnp.float32)
 
 
 def laps12(field, z, y_part, fetch, finish):
-    rows, lanes = field.shape[1:]
+    rows, lanes = field.shape[1] - 8, field.shape[2]
     groups = rows // 8
     sub = lax.broadcasted_iota(jnp.int32, (8, lanes), 0)
 
@@ -331,18 +331,19 @@
 
 
 def load_blocks(slabs, blocks, first, second, factor=None):
-    ends, rows, lanes = first.shape
-    planes = blocks[0].shape[1]
+    ends, rows, lanes = first.shape[0], first.shape[1] - 8, first.shape[2]
+    planes = (ends - 4) // 4
     for field in (first, second):
         for z in (0, 1, ends - 2, ends - 1):
-            field[z] = jnp.zeros((rows, lanes), jnp.float32)
+            field[z, 0:rows] = jnp.zeros((rows, lanes), jnp.float32)
     for slab, block in zip(slabs, blocks):
+        pair = block if isinstance(block, tuple) else (block.at[0], block.at[1])
         for p in range(planes):
-            values = block[0, p], block[1, p]
+            values = pair[0][p], pair[1][p]
             if factor is not None:
                 speed = factor[slab + p]
                 values = values[0] * speed, values[1] * speed
-            first[slab + p + 2], second[slab + p + 2] = values
+            first[slab + p + 2, 0:rows], second[slab + p + 2, 0:rows] = values
 
 
 BATCH = 4
@@ -369,7 +370,7 @@
 
 
 def forward_kernel(
-    start, sources, own, mate, over, far, c0, c1, c2, c3, placed, laps, history, held, cour, last,
+    start, sources, own, mate, over0, over1, far0, far1, c0, c1, c2, c3, placed, laps, history, held, cour, last,
     even, odd, banded, y0, y1, sems, sems_even, sems_odd
 ):
     planes, rows, lanes = c0.shape
@@ -386,11 +387,11 @@
 
     def keep(k, field, done):
         for n in range(4):
-            source = field.at[pl.ds(n * planes + 2, planes)]
+            source = field.at[pl.ds(n * planes + 2, planes), pl.ds(0, rows)]
             yield pltpu.make_async_copy(source, history.at[k, pl.ds(n * planes, planes)], done.at[n])
 
     banded[...] = band(lanes)
-    load_blocks(slabs, (own, mate, over, far), odd, even)
+    load_blocks(slabs, (own, mate, (over0, over1), (far0, far1)), odd, even)
     for slab, block in zip(slabs, (c0, c1, c2, c3)):
         for p in range(planes):
             cour[slab + p] = block[p]
@@ -508,7 +509,7 @@
                 ref[n, pl.ds(i, 8, stride=groups), :] = value[i * 8 : (i + 1) * 8]
 
 
-def square_kernel(mine, by_x, by_y, by_xy, keep, send):
+def square_kernel(mine, by_xy, by_y, by_x, keep, send):
     half = lax.axis_index("shot") // 2 % 2
     count = keep.shape[0]
     for ref, part in ((keep, half), (send, 1 - half)):
@@ -529,20 +530,26 @@
     return result
 
 
-def after_kernel(earlier, value, out):
-    out[...] = value[...]
-
-
-def after(earlier, value):
+def after_kernel(earlier, value, *outs):
+    if len(outs) == 1:
+        outs[0][...] = value[...]
+    else:
+        for n, out in enumerate(outs):
+            out[...] = value[n]
+
+
+def after(earlier, value, parts=1):
     vmem, anywhere = pl.BlockSpec(memory_space=pltpu.VMEM), pl.BlockSpec(memory_space=pl.ANY)
-    return pl.pallas_call(
+    shape = value.shape if parts == 1 else value.shape[1:]
+    results = pl.pallas_call(
         after_kernel,
         in_specs=[anywhere, vmem],
-        out_specs=vmem,
-        out_shape=jax.ShapeDtypeStruct(value.shape, jnp.float32),
+        out_specs=[vmem] * parts,
+        out_shape=[jax.ShapeDtypeStruct(shape, jnp.float32)] * parts,
         compiler_params=pltpu.CompilerParams(vmem_limit_bytes=4 * 2**20),
         name="after",
     )(earlier, value)
+    return results[0] if parts == 1 else results
 
 
 def arrange_kernel(mine, other, out):
@@ -670,19 +677,19 @@
     mate = exchange(own, CORE)
     c2 = local(arrange_kernel, [courant_sq.shape], piece, exchange(piece, Y))
     c1, c3 = exchange(c0, CORE), exchange(c2, CORE)
-    over = after(c2, over)
-    far = exchange(over, CORE)
+    over = after(c2, over, parts=2)
+    far = [exchange(field, CORE) for field in over]
     adj_over = exchange(adj_outgoing, CHIP)
     adj_mate = exchange(adj_own, CORE)
 
-    scratch = pltpu.VMEM((planes_all + 4, rows_x, rows_y), jnp.float32)
+    scratch = pltpu.VMEM((planes_all + 4, rows_x + 8, rows_y), jnp.float32)
     y_scratch = pltpu.VMEM((BATCH * rows_x, rows_y), jnp.float32)
     step_scratch = [scratch, scratch, pltpu.VMEM((2 * rows_y, rows_y), jnp.bfloat16), y_scratch, y_scratch]
     params = pltpu.CompilerParams(vmem_limit_bytes=6 * 2**20)
     cost = pl.CostEstimate(flops=30 * steps * cells_all, bytes_accessed=16 * steps * cells_all, transcendentals=0)
     laps, history, held, cour, last = pl.pallas_call(
         forward_kernel,
-        in_specs=[smem, smem] + [vmem] * 8 + [pl.BlockSpec(memory_space=pltpu.HBM)],
+        in_specs=[smem, smem] + [vmem] * 10 + [pl.BlockSpec(memory_space=pltpu.HBM)],
         out_specs=[vmem] * 5,
         out_shape=[
             jax.ShapeDtypeStruct((steps, planes, 2, rows_x, rows_y), jnp.float32),
@@ -697,10 +704,10 @@
             pltpu.SemaphoreType.DMA((4,)),
             pltpu.SemaphoreType.DMA((4,)),
         ],
-        compiler_params=pltpu.CompilerParams(vmem_limit_bytes=30 * 2**20),
+        compiler_params=pltpu.CompilerParams(vmem_limit_bytes=25 * 2**20),
         cost_estimate=pl.CostEstimate(flops=1000, bytes_accessed=1000, transcendentals=0),
         name="forward_steps",
-    )(ckpt_step[None], src_cells, own, mate, over, far, c0, c1, c2, c3, placed)
+    )(ckpt_step[None], src_cells, own, mate, *over, *far, c0, c1, c2, c3, placed)
 
     adj_over = after(laps, adj_over)
     adj_far = exchange(adj_over, CORE)
@@ -726,7 +733,7 @@
     )(adj_own, adj_mate, adj_over, adj_far, cour, laps, inject, last)
 
     by_xy, by_x, by_y = exchange(send_xy, CHIP + Y), exchange(send_x, CHIP), exchange(send_y, Y)
-    keep, send = local(square_kernel, [quarter] * 2, keep, by_x, by_y, by_xy)
+    keep, send = local(square_kernel, [quarter] * 2, keep, by_xy, by_y, by_x)
     part = local(add_kernel, [quarter], keep, exchange(send, NEAR_Z))
     rows, sums_shape = planes // 4 * rows_x, (8, rows_y)
     data, sums = local(sums_kernel, [(rows + 8, rows_y), sums_shape], part, exchange(part, FAR_Z), momentum)

time: 83.4 us -> 78.6 us (0.942)
  Pallas kernels: 36.2 us -> 32.2 us
  local copies, waits for them, and re-layouts: 4.39 us -> 0.71 us
  waiting for transfers between devices: 19.2 us -> 21.8 us
    unnamed x16, local copies, waits for them, and re-layouts: 4.39 us -> 0.71 us
    pallas_call x4, Pallas kernels: 13.5 us -> 10.5 us  [the longest x1 9.67 us: whole_shards(): pl.pallas_call(forward_kernel, in_specs=[smem, smem] + [vmem] * 10 + [pl....]
    ppermute x21 -> x22, waiting for transfers between devices: 19.2 us -> 21.8 us  [exchange(): lax.ppermute(value, axes, [(i, i ^ bits) for i in range(lax.axis_size(axe...]
    ppermute x21 -> x22, starting transfers between devices: 21.8 us -> 22.2 us  [exchange(): lax.ppermute(value, axes, [(i, i ^ bits) for i in range(lax.axis_size(axe...]
  transfers between devices with their start and end apart: 21 -> 22, of which waited for: 11 -> 13; matrix products, arithmetic and copies ran while one was open for 0% -> 0% of each run, Pallas kernels for 31% -> 28%
where the time goes in v13:
time: 78.6 us; the launch traced here: 78.4 us
  Pallas kernels  32.2 us (41%)
  starting transfers between devices  22.2 us (28%)
  waiting for transfers between devices  21.8 us (28%)
  between operations  1.47 us (2%)
    ppermute x22, starting transfers between devices, exchange(): lax.ppermute(value, axes, [(i, i ^ bits) for i in range(lax.axis_size(axe...  22.2 us
    ppermute x22, waiting for transfers between devices, exchange(): lax.ppermute(value, axes, [(i, i ^ bits) for i in range(lax.axis_size(axe...  21.8 us
    pallas_call x1, Pallas kernels, whole_shards(): pl.pallas_call(forward_kernel, in_specs=[smem, smem] + [vmem] * 10 + [pl....  9.67 us
    pallas_call x1, Pallas kernels, scatter(): pl.pallas_call(functools.partial(scatter_kernel, rows_x), grid=(rows_all...  9.3 us
    pallas_call x1, Pallas kernels, whole_shards(): pl.pallas_call(adjoint_kernel, in_specs=[vmem] * 8, out_specs=[vmem] * 4,...  7.02 us
    pallas_call x1, Pallas kernels, whole_shards(): pl.pallas_call(first_kernel, in_specs=[hbm] * 3, out_specs=[vmem] * 3, ou...  2.13 us
  transfers between devices with their start and end apart: 22, of which 13 were waited for; matrix products, arithmetic and copies ran while one was open for 0% of the time, Pallas kernels for 28%

profile of v13, /device:TPU:0, one launch (start us, length us, event | category | flops | bytes accessed | tf_op | source)
XLA Modules:
  0.0 78.4 jit_solution(8795274909862379324)
XLA Ops:
  0.6 2.1 %first_to_cross.1 = (f32[2,8,64,128]{3,2,1,0:T(8,128)}, f32[8,64,128]{2,1,0:T(8,128)}, f32[4,64,128]{2,1,0:T(8,128)}) custom-call(f32[2,8,64,128]{3,2,1,0:T(8,128)} %refs_4_.1, f32[2,8,64,128]{3,2,1,0:T(8,128)} %refs_5_.1, f32[8,64,128]{2,1,0:T(8,128)} %courant.1), custom_call_target="tpu_custom_call" | custom-call | tf_op jit(solution)/shard_map/first_to_cross/pallas_call | solution.py:649
  2.8 3.0 %collective-permute-start = (f32[4,64,128]{2,1,0:T(8,128)}, f32[4,64,128]{2,1,0:T(8,128)S(1)}, u32[]{:S(2)}, u32[]{:S(2)}) collective-permute-start(f32[4,64,128]{2,1,0:T(8,128)} %get-tuple-element.30), channel_id=1, source_target_pairs={{0,2},{1,3},{2,0},{3,1},{4,6},{5,7},{6,4},{7,5},{8,10},{9,11},{10,... | collective-permute-start | bytes 393224 | tf_op jit(solution)/shard_map/ppermute | solution.py:633
  5.8 0.1 collective-permute-start.4
  5.8 0.0 copy-start
  5.9 0.0 copy-start.5
  5.9 0.0 copy-start.7
  5.9 0.1 collective-permute-start.7
  6.0 9.3 %receiver_scatter.1 = (f32[9,2048,128]{2,1,0:T(8,128)}, f32[8,128]{1,0:T(8,128)}) custom-call(s32[2,512]{1,0:T(2,128)} %cells_ref.1, f32[2,8,512]{2,1,0:T(8,128)} %observed_ref.1), custom_call_target="tpu_custom_call" | custom-call | flops 4831838208 | bytes 9437184 | tf_op jit(solution)/shard_map/receiver_scatter/pallas_call | solution.py:298
  15.3 0.0 collective-permute-done.value
  15.3 0.7 copy-done.6
  16.0 0.0 copy-done
  16.0 0.0 copy-done.1
  16.0 0.0 copy-done.2
  16.0 0.0 copy-done.3
  16.0 1.3 %pick.1 = (f32[2,8,64,128]{3,2,1,0:T(8,128)}, f32[2,8,64,128]{3,2,1,0:T(8,128)S(1)}, f32[2,8,64,128]{3,2,1,0:T(8,128)S(1)}) custom-call(f32[4,64,128]{2,1,0:T(8,128)S(1)} %after.3.earlier.mine, f32[2,8,64,128]{3,2,1,0:T(8,128)S(1)} %copy-done, f32[2,8,64,128]{3,2,1,0:T(8,128)S(1)} %copy-done.1, f32[2,8,64,128]{3,2,1,0:T(8,128)S(1)} %copy-done, ...), custom_call_target="tpu_custom_call" | custom-call | tf_op jit(solution)/shard_map/pick/pallas_call | solution.py:166
  17.4 0.4 collective-permute-start.2
  17.8 1.9 %collective-permute-start.9 = (f32[2,8,64,128]{3,2,1,0:T(8,128)}, f32[2,8,64,128]{3,2,1,0:T(8,128)S(1)}, u32[]{:S(2)}, u32[]{:S(2)}) collective-permute-start(f32[2,8,64,128]{3,2,1,0:T(8,128)} %get-tuple-element.39), channel_id=1, source_target_pairs={{0,2},{1,3},{2,0},{3,1},{4,6},{5,7},{6,4},{7,5},{8,10},{9,11},{10,... | collective-permute-start | bytes 1572872 | tf_op jit(solution)/shard_map/ppermute | solution.py:633
  19.7 1.5 %collective-permute-start.3 = (f32[4,64,128]{2,1,0:T(8,128)S(1)}, f32[4,64,128]{2,1,0:T(8,128)S(1)}, u32[]{:S(2)}, u32[]{:S(2)}) collective-permute-start(f32[4,64,128]{2,1,0:T(8,128)S(1)} %after.3.earlier.mine), channel_id=1, source_target_pairs={{0,4},{1,5},{2,6},{3,7},{4,0},{5,1},{6,2},{7,3},{8,12},{9,13},{10,... | collective-permute-start | bytes 393224 | tf_op jit(solution)/shard_map/ppermute | solution.py:633
  21.2 3.8 %collective-permute-done.3.other = f32[4,64,128]{2,1,0:T(8,128)S(1)} collective-permute-done((f32[4,64,128]{2,1,0:T(8,128)S(1)}, f32[4,64,128]{2,1,0:T(8,128)S(1)}, u32[]{:S(2)}, u32[]{:S(2)}) %collective-permute-start.3) | collective-permute-done | bytes 131104 | tf_op jit(solution)/shard_map/ppermute | solution.py:633
  25.0 0.1 collective-permute-start.8
  25.1 0.0 collective-permute-done.4.value
  25.1 0.7 after.4
  25.9 0.5 collective-permute-start.5
  26.4 0.0 collective-permute-done.7.c1
  26.4 0.0 collective-permute-start.6
  27.0 0.0 collective-permute-done.8.c3
  27.0 0.6 collective-permute-start.1
  27.6 0.0 collective-permute-done.2.mate
  27.6 0.2 collective-permute-done.5.far0
  27.8 0.5 collective-permute-done.6.far1
  28.2 0.0 copy-done.5
  28.2 0.0 copy-done.7
  28.2 9.7 %forward_steps.1 = (f32[8,8,2,64,128]{4,3,2,1,0:T(8,128)S(1)}, f32[8,32,64,128]{3,2,1,0:T(8,128)S(1)}, f32[9,32,64,128]{3,2,1,0:T(8,128)S(1)}, f32[32,64,128]{2,1,0:T(8,128)S(1)}, f32[16,64,128]{2,1,0:T(8,128)S(1)}) custom-call(s32[1]{0:T(128)} %bitcast.3.start, s32[2]{0:T(128)S(1)} %copy-done.7, f32[2,8,64,128]{3,2,1,0:T(8,128)S(1)} %get-tuple-element.32.own, ...), custom_call_target="tpu_custom_call" | custom-call | flops 1000 | bytes 1000 | tf_op jit(solution)/shard_map/forward_steps/pallas_call | solution.py:690
  37.9 0.0 collective-permute-done.9.value
  38.0 0.4 collective-permute-start.10
  38.4 1.0 %inject.1 = f32[8,32,64,128]{3,2,1,0:T(8,128)S(1)} custom-call(f32[9,32,64,128]{3,2,1,0:T(8,128)S(1)} %get-tuple-element.41.held, f32[8,32,64,128]{3,2,1,0:T(8,128)S(1)} %get-tuple-element.42.history), custom_call_target="tpu_custom_call" | custom-call | tf_op jit(solution)/shard_map/inject/pallas_call | solution.py:714
  39.4 0.0 collective-permute-done.1.mate
  39.4 0.6 collective-permute-done.10.far
  40.0 7.0 %adjoint_steps.1 = (f32[4,64,128]{2,1,0:T(8,128)S(1)}, f32[4,64,128]{2,1,0:T(8,128)S(1)}, f32[4,64,128]{2,1,0:T(8,128)S(1)}, f32[4,64,128]{2,1,0:T(8,128)S(1)}) custom-call(f32[2,8,64,128]{3,2,1,0:T(8,128)S(1)} %get-tuple-element.31.own, f32[2,8,64,128]{3,2,1,0:T(8,128)S(1)} %collective-permute-done.1.mate, f32[2,8,64,128]{3,2,1,0:T(8,128)S(1)} %after.5.over, ...), custom_call_target="tpu_custom_call" | custom-call | flops 62914560 | bytes 33554432 | tf_op jit(solution)/shard_map/adjoint_steps/pallas_call | solution.py:724
  47.0 1.6 %collective-permute-start.11 = (f32[4,64,128]{2,1,0:T(8,128)S(1)}, f32[4,64,128]{2,1,0:T(8,128)S(1)}, u32[]{:S(2)}, u32[]{:S(2)}) collective-permute-start(f32[4,64,128]{2,1,0:T(8,128)S(1)} %get-tuple-element.45), channel_id=1, source_target_pairs={{0,6},{1,7},{2,4},{3,5},{4,2},{5,3},{6,0},{7,1},{8,14},{9,15},{10,... | collective-permute-start | bytes 393224 | tf_op jit(solution)/shard_map/ppermute | solution.py:633
  48.5 0.3 collective-permute-start.12
  48.8 1.7 %collective-permute-start.13 = (f32[4,64,128]{2,1,0:T(8,128)S(1)}, f32[4,64,128]{2,1,0:T(8,128)S(1)}, u32[]{:S(2)}, u32[]{:S(2)}) collective-permute-start(f32[4,64,128]{2,1,0:T(8,128)S(1)} %get-tuple-element.47), channel_id=1, source_target_pairs={{0,2},{1,3},{2,0},{3,1},{4,6},{5,7},{6,4},{7,5},{8,10},{9,11},{10,... | collective-permute-start | bytes 393224 | tf_op jit(solution)/shard_map/ppermute | solution.py:633
  50.6 3.8 %collective-permute-done.11.by_xy = f32[4,64,128]{2,1,0:T(8,128)S(1)} collective-permute-done((f32[4,64,128]{2,1,0:T(8,128)S(1)}, f32[4,64,128]{2,1,0:T(8,128)S(1)}, u32[]{:S(2)}, u32[]{:S(2)}) %collective-permute-start.11) | collective-permute-done | bytes 131104 | tf_op jit(solution)/shard_map/ppermute | solution.py:633
  54.3 2.2 %collective-permute-done.12.by_y = f32[4,64,128]{2,1,0:T(8,128)S(1)} collective-permute-done((f32[4,64,128]{2,1,0:T(8,128)S(1)}, f32[4,64,128]{2,1,0:T(8,128)S(1)}, u32[]{:S(2)}, u32[]{:S(2)}) %collective-permute-start.12) | collective-permute-done | bytes 131104 | tf_op jit(solution)/shard_map/ppermute | solution.py:633
  56.5 0.1 collective-permute-done.13.by_x
  56.7 1.7 %collective-permute-start.14 = (f32[2,64,128]{2,1,0:T(8,128)S(1)}, f32[2,64,128]{2,1,0:T(8,128)S(1)}, u32[]{:S(2)}, u32[]{:S(2)}) collective-permute-start(f32[2,64,128]{2,1,0:T(8,128)S(1)} %get-tuple-element.49), channel_id=1, source_target_pairs={{0,8},{1,9},{2,10},{3,11},{4,12},{5,13},{6,14},{7,15},{8,0},{9,1},... | collective-permute-start | bytes 196616 | tf_op jit(solution)/shard_map/ppermute | solution.py:633
  58.3 2.7 %collective-permute-done.14.other = f32[2,64,128]{2,1,0:T(8,128)S(1)} collective-permute-done((f32[2,64,128]{2,1,0:T(8,128)S(1)}, f32[2,64,128]{2,1,0:T(8,128)S(1)}, u32[]{:S(2)}, u32[]{:S(2)}) %collective-permute-start.14) | collective-permute-done | bytes 65568 | tf_op jit(solution)/shard_map/ppermute | solution.py:633
  61.0 2.6 %collective-permute-start.15 = (f32[2,64,128]{2,1,0:T(8,128)S(1)}, f32[2,64,128]{2,1,0:T(8,128)S(1)}, u32[]{:S(2)}, u32[]{:S(2)}) collective-permute-start(f32[2,64,128]{2,1,0:T(8,128)S(1)} %add_kernel.1.mine), channel_id=1, source_target_pairs={{0,16},{1,17},{2,18},{3,19},{4,20},{5,21},{6,22},{7,23},{8,24},{9,... | collective-permute-start | bytes 196616 | tf_op jit(solution)/shard_map/ppermute | solution.py:633
  63.7 2.6 %collective-permute-done.15.other = f32[2,64,128]{2,1,0:T(8,128)S(1)} collective-permute-done((f32[2,64,128]{2,1,0:T(8,128)S(1)}, f32[2,64,128]{2,1,0:T(8,128)S(1)}, u32[]{:S(2)}, u32[]{:S(2)}) %collective-permute-start.15) | collective-permute-done | bytes 65568 | tf_op jit(solution)/shard_map/ppermute | solution.py:633
  66.2 0.0 copy-done.4
  66.2 0.1 sums_kernel.1
  66.3 1.6 %collective-permute-start.16 = (f32[136,128]{1,0:T(8,128)S(1)}, f32[136,128]{1,0:T(8,128)S(1)}, u32[]{:S(2)}, u32[]{:S(2)}) collective-permute-start(f32[136,128]{1,0:T(8,128)S(1)} %get-tuple-element.50.mine), channel_id=1, source_target_pairs={{0,8},{1,9},{2,10},{3,11},{4,12},{5,13},{6,14},{7,15},{8,0},{9,1},... | collective-permute-start | bytes 208904 | tf_op jit(solution)/shard_map/ppermute | solution.py:633
  68.0 0.0 collective-permute-start.17
  68.0 0.5 collective-permute-start.18
  68.5 0.6 collective-permute-done.17.s1
  69.1 1.9 %collective-permute-done.18.s2 = f32[8,128]{1,0:T(8,128)S(1)} collective-permute-done((f32[8,128]{1,0:T(8,128)S(1)}, f32[8,128]{1,0:T(8,128)S(1)}, u32[]{:S(2)}, u32[]{:S(2)}) %collective-permute-start.18) | collective-permute-done | bytes 4128 | tf_op jit(solution)/shard_map/ppermute | solution.py:633
  71.0 0.0 collective-permute-done.16.other
  71.0 0.8 collective-permute-start.19
  71.8 1.3 %collective-permute-start.20 = (f32[8,128]{1,0:T(8,128)S(1)}, f32[8,128]{1,0:T(8,128)S(1)}, u32[]{:S(2)}, u32[]{:S(2)}) collective-permute-start(f32[8,128]{1,0:T(8,128)S(1)} %get-tuple-element.53.s0), channel_id=1, source_target_pairs={{0,2},{1,3},{2,0},{3,1},{4,6},{5,7},{6,4},{7,5},{8,10},{9,11},{10,... | collective-permute-start | bytes 12296 | tf_op jit(solution)/shard_map/ppermute | solution.py:633
  73.1 1.5 %collective-permute-start.21 = (f32[8,128]{1,0:T(8,128)S(1)}, f32[8,128]{1,0:T(8,128)S(1)}, u32[]{:S(2)}, u32[]{:S(2)}) collective-permute-start(f32[8,128]{1,0:T(8,128)S(1)} %get-tuple-element.53.s0), channel_id=1, source_target_pairs={{0,6},{1,7},{2,4},{3,5},{4,2},{5,3},{6,0},{7,1},{8,14},{9,15},{10,... | collective-permute-start | bytes 12296 | tf_op jit(solution)/shard_map/ppermute | solution.py:633
  74.6 0.8 %collective-permute-done.20.s1 = f32[8,128]{1,0:T(8,128)S(1)} collective-permute-done((f32[8,128]{1,0:T(8,128)S(1)}, f32[8,128]{1,0:T(8,128)S(1)}, u32[]{:S(2)}, u32[]{:S(2)}) %collective-permute-start.20) | collective-permute-done | bytes 4128 | tf_op jit(solution)/shard_map/ppermute | solution.py:633
  75.4 2.2 %collective-permute-done.21.s2 = f32[8,128]{1,0:T(8,128)S(1)} collective-permute-done((f32[8,128]{1,0:T(8,128)S(1)}, f32[8,128]{1,0:T(8,128)S(1)}, u32[]{:S(2)}, u32[]{:S(2)}) %collective-permute-start.21) | collective-permute-done | bytes 4128 | tf_op jit(solution)/shard_map/ppermute | solution.py:633
  77.6 0.0 collective-permute-done.19.other
  77.6 0.8 finish.1
  (11 shorter events, 0.1 us)
Async XLA Ops:
  2.8 12.5 %collective-permute-start = (f32[4,64,128]{2,1,0:T(8,128)}, f32[4,64,128]{2,1,0:T(8,128)S(1)}, u32[]{:S(2)}, u32[]{:S(2)}) collective-permute-start(f32[4,64,128]{2,1,0:T(8,128)} %get-tuple-element.30), channel_id=1, source_target_pairs={{0,2},{1,3},{2,0},{3,1},{4,6},{5,7},{6,4},{7,5},{8,10},{9,11},{10,... | collective-permute-start | bytes 393224 | tf_op jit(solution)/shard_map/ppermute | solution.py:633
  5.8 19.4 %collective-permute-start.4 = (f32[2,8,64,128]{3,2,1,0:T(8,128)}, f32[2,8,64,128]{3,2,1,0:T(8,128)S(1)}, u32[]{:S(2)}, u32[]{:S(2)}) collective-permute-start(f32[2,8,64,128]{3,2,1,0:T(8,128)} %get-tuple-element.33), channel_id=1, source_target_pairs={{0,2},{1,3},{2,0},{3,1},{4,6},{5,7},{6,4},{7,5},{8,10},{9,11},{10,... | collective-permute-start | bytes 1572872 | tf_op jit(solution)/shard_map/ppermute | solution.py:633
  5.8 10.1 %copy-start = (f32[2,8,64,128]{3,2,1,0:T(8,128)S(1)}, f32[2,8,64,128]{3,2,1,0:T(8,128)}, u32[]{:S(2)}) copy-start(f32[2,8,64,128]{3,2,1,0:T(8,128)} %refs_2_.1) | copy-start | bytes 1572868
  5.8 10.1 %copy-start.1 = (f32[2,8,64,128]{3,2,1,0:T(8,128)S(1)}, f32[2,8,64,128]{3,2,1,0:T(8,128)}, u32[]{:S(2)}) copy-start(f32[2,8,64,128]{3,2,1,0:T(8,128)} %refs_3_.1) | copy-start | bytes 1572868
  5.8 10.1 %copy-start.2 = (f32[2,8,64,128]{3,2,1,0:T(8,128)S(1)}, f32[2,8,64,128]{3,2,1,0:T(8,128)}, u32[]{:S(2)}) copy-start(f32[2,8,64,128]{3,2,1,0:T(8,128)} %refs_4_.1) | copy-start | bytes 1572868
  5.9 10.1 %copy-start.3 = (f32[2,8,64,128]{3,2,1,0:T(8,128)S(1)}, f32[2,8,64,128]{3,2,1,0:T(8,128)}, u32[]{:S(2)}) copy-start(f32[2,8,64,128]{3,2,1,0:T(8,128)} %refs_5_.1) | copy-start | bytes 1572868
  5.9 22.4 %copy-start.5 = (f32[8,64,128]{2,1,0:T(8,128)S(1)}, f32[8,64,128]{2,1,0:T(8,128)}, u32[]{:S(2)}) copy-start(f32[8,64,128]{2,1,0:T(8,128)} %get-tuple-element.36.c0) | copy-start | bytes 786436
  5.9 22.4 %copy-start.7 = (s32[2]{0:T(128)S(1)}, s32[2]{0:T(128)}, u32[]{:S(2)}) copy-start(s32[2]{0:T(128)} %sources.1) | copy-start | bytes 28
  5.9 20.5 %collective-permute-start.7 = (f32[8,64,128]{2,1,0:T(8,128)}, f32[8,64,128]{2,1,0:T(8,128)S(1)}, u32[]{:S(2)}, u32[]{:S(2)}) collective-permute-start(f32[8,64,128]{2,1,0:T(8,128)} %get-tuple-element.36.c0), channel_id=1, source_target_pairs={{0,1},{1,0},{2,3},{3,2},{4,5},{5,4},{6,7},{7,6},{8,9},{9,8},{10,11... | collective-permute-start | bytes 786440 | tf_op jit(solution)/shard_map/ppermute | solution.py:633
  15.3 0.7 copy-start.6
  17.4 10.2 %collective-permute-start.2 = (f32[2,8,64,128]{3,2,1,0:T(8,128)S(1)}, f32[2,8,64,128]{3,2,1,0:T(8,128)S(1)}, u32[]{:S(2)}, u32[]{:S(2)}) collective-permute-start(f32[2,8,64,128]{3,2,1,0:T(8,128)S(1)} %get-tuple-element.32.own), channel_id=1, source_target_pairs={{0,1},{1,0},{2,3},{3,2},{4,5},{5,4},{6,7},{7,6},{8,9},{9,8},{10,11... | collective-permute-start | bytes 1572872 | tf_op jit(solution)/shard_map/ppermute | solution.py:633
  17.8 20.2 %collective-permute-start.9 = (f32[2,8,64,128]{3,2,1,0:T(8,128)}, f32[2,8,64,128]{3,2,1,0:T(8,128)S(1)}, u32[]{:S(2)}, u32[]{:S(2)}) collective-permute-start(f32[2,8,64,128]{3,2,1,0:T(8,128)} %get-tuple-element.39), channel_id=1, source_target_pairs={{0,2},{1,3},{2,0},{3,1},{4,6},{5,7},{6,4},{7,5},{8,10},{9,11},{10,... | collective-permute-start | bytes 1572872 | tf_op jit(solution)/shard_map/ppermute | solution.py:633
  19.7 5.3 %collective-permute-start.3 = (f32[4,64,128]{2,1,0:T(8,128)S(1)}, f32[4,64,128]{2,1,0:T(8,128)S(1)}, u32[]{:S(2)}, u32[]{:S(2)}) collective-permute-start(f32[4,64,128]{2,1,0:T(8,128)S(1)} %after.3.earlier.mine), channel_id=1, source_target_pairs={{0,4},{1,5},{2,6},{3,7},{4,0},{5,1},{6,2},{7,3},{8,12},{9,13},{10,... | collective-permute-start | bytes 393224 | tf_op jit(solution)/shard_map/ppermute | solution.py:633
  25.0 2.0 %collective-permute-start.8 = (f32[8,64,128]{2,1,0:T(8,128)S(1)}, f32[8,64,128]{2,1,0:T(8,128)S(1)}, u32[]{:S(2)}, u32[]{:S(2)}) collective-permute-start(f32[8,64,128]{2,1,0:T(8,128)S(1)} %arrange_kernel.1.earlier.c2), channel_id=1, source_target_pairs={{0,1},{1,0},{2,3},{3,2},{4,5},{5,4},{6,7},{7,6},{8,9},{9,8},{10,11... | collective-permute-start | bytes 786440 | tf_op jit(solution)/shard_map/ppermute | solution.py:633
  25.9 1.9 %collective-permute-start.5 = (f32[8,64,128]{2,1,0:T(8,128)S(1)}, f32[8,64,128]{2,1,0:T(8,128)}, u32[]{:S(2)}, u32[]{:S(2)}) collective-permute-start(f32[8,64,128]{2,1,0:T(8,128)S(1)} %get-tuple-element.34.over0), channel_id=1, source_target_pairs={{0,1},{1,0},{2,3},{3,2},{4,5},{5,4},{6,7},{7,6},{8,9},{9,8},{10,11... | collective-permute-start | bytes 786440 | tf_op jit(solution)/shard_map/ppermute | solution.py:633
  26.4 1.9 %collective-permute-start.6 = (f32[8,64,128]{2,1,0:T(8,128)}, f32[8,64,128]{2,1,0:T(8,128)}, u32[]{:S(2)}, u32[]{:S(2)}) collective-permute-start(f32[8,64,128]{2,1,0:T(8,128)} %get-tuple-element.35.over1), channel_id=1, source_target_pairs={{0,1},{1,0},{2,3},{3,2},{4,5},{5,4},{6,7},{7,6},{8,9},{9,8},{10,11... | collective-permute-start | bytes 786440 | tf_op jit(solution)/shard_map/ppermute | solution.py:633
  27.0 12.3 %collective-permute-start.1 = (f32[2,8,64,128]{3,2,1,0:T(8,128)S(1)}, f32[2,8,64,128]{3,2,1,0:T(8,128)S(1)}, u32[]{:S(2)}, u32[]{:S(2)}) collective-permute-start(f32[2,8,64,128]{3,2,1,0:T(8,128)S(1)} %get-tuple-element.31.own), channel_id=1, source_target_pairs={{0,1},{1,0},{2,3},{3,2},{4,5},{5,4},{6,7},{7,6},{8,9},{9,8},{10,11... | collective-permute-start | bytes 1572872 | tf_op jit(solution)/shard_map/ppermute | solution.py:633
  38.0 2.0 %collective-permute-start.10 = (f32[2,8,64,128]{3,2,1,0:T(8,128)S(1)}, f32[2,8,64,128]{3,2,1,0:T(8,128)S(1)}, u32[]{:S(2)}, u32[]{:S(2)}) collective-permute-start(f32[2,8,64,128]{3,2,1,0:T(8,128)S(1)} %after.5.over), channel_id=1, source_target_pairs={{0,1},{1,0},{2,3},{3,2},{4,5},{5,4},{6,7},{7,6},{8,9},{9,8},{10,11... | collective-permute-start | bytes 1572872 | tf_op jit(solution)/shard_map/ppermute | solution.py:633
  40.0 26.3 %copy-start.4 = (f32[8,64,128]{2,1,0:T(8,128)S(1)}, f32[8,64,128]{2,1,0:T(8,128)}, u32[]{:S(2)}) copy-start(f32[8,64,128]{2,1,0:T(8,128)} %momentum.3) | copy-start | bytes 786436
  47.0 7.3 %collective-permute-start.11 = (f32[4,64,128]{2,1,0:T(8,128)S(1)}, f32[4,64,128]{2,1,0:T(8,128)S(1)}, u32[]{:S(2)}, u32[]{:S(2)}) collective-permute-start(f32[4,64,128]{2,1,0:T(8,128)S(1)} %get-tuple-element.45), channel_id=1, source_target_pairs={{0,6},{1,7},{2,4},{3,5},{4,2},{5,3},{6,0},{7,1},{8,14},{9,15},{10,... | collective-permute-start | bytes 393224 | tf_op jit(solution)/shard_map/ppermute | solution.py:633
  48.5 8.0 %collective-permute-start.12 = (f32[4,64,128]{2,1,0:T(8,128)S(1)}, f32[4,64,128]{2,1,0:T(8,128)S(1)}, u32[]{:S(2)}, u32[]{:S(2)}) collective-permute-start(f32[4,64,128]{2,1,0:T(8,128)S(1)} %get-tuple-element.46), channel_id=1, source_target_pairs={{0,4},{1,5},{2,6},{3,7},{4,0},{5,1},{6,2},{7,3},{8,12},{9,13},{10,... | collective-permute-start | bytes 393224 | tf_op jit(solution)/shard_map/ppermute | solution.py:633
  48.8 7.8 %collective-permute-start.13 = (f32[4,64,128]{2,1,0:T(8,128)S(1)}, f32[4,64,128]{2,1,0:T(8,128)S(1)}, u32[]{:S(2)}, u32[]{:S(2)}) collective-permute-start(f32[4,64,128]{2,1,0:T(8,128)S(1)} %get-tuple-element.47), channel_id=1, source_target_pairs={{0,2},{1,3},{2,0},{3,1},{4,6},{5,7},{6,4},{7,5},{8,10},{9,11},{10,... | collective-permute-start | bytes 393224 | tf_op jit(solution)/shard_map/ppermute | solution.py:633
  56.7 4.3 %collective-permute-start.14 = (f32[2,64,128]{2,1,0:T(8,128)S(1)}, f32[2,64,128]{2,1,0:T(8,128)S(1)}, u32[]{:S(2)}, u32[]{:S(2)}) collective-permute-start(f32[2,64,128]{2,1,0:T(8,128)S(1)} %get-tuple-element.49), channel_id=1, source_target_pairs={{0,8},{1,9},{2,10},{3,11},{4,12},{5,13},{6,14},{7,15},{8,0},{9,1},... | collective-permute-start | bytes 196616 | tf_op jit(solution)/shard_map/ppermute | solution.py:633
  61.0 5.2 %collective-permute-start.15 = (f32[2,64,128]{2,1,0:T(8,128)S(1)}, f32[2,64,128]{2,1,0:T(8,128)S(1)}, u32[]{:S(2)}, u32[]{:S(2)}) collective-permute-start(f32[2,64,128]{2,1,0:T(8,128)S(1)} %add_kernel.1.mine), channel_id=1, source_target_pairs={{0,16},{1,17},{2,18},{3,19},{4,20},{5,21},{6,22},{7,23},{8,24},{9,... | collective-permute-start | bytes 196616 | tf_op jit(solution)/shard_map/ppermute | solution.py:633
  66.3 4.7 %collective-permute-start.16 = (f32[136,128]{1,0:T(8,128)S(1)}, f32[136,128]{1,0:T(8,128)S(1)}, u32[]{:S(2)}, u32[]{:S(2)}) collective-permute-start(f32[136,128]{1,0:T(8,128)S(1)} %get-tuple-element.50.mine), channel_id=1, source_target_pairs={{0,8},{1,9},{2,10},{3,11},{4,12},{5,13},{6,14},{7,15},{8,0},{9,1},... | collective-permute-start | bytes 208904 | tf_op jit(solution)/shard_map/ppermute | solution.py:633
  68.0 1.2 %collective-permute-start.17 = (f32[8,128]{1,0:T(8,128)S(1)}, f32[8,128]{1,0:T(8,128)S(1)}, u32[]{:S(2)}, u32[]{:S(2)}) collective-permute-start(f32[8,128]{1,0:T(8,128)S(1)} %get-tuple-element.51.s0), channel_id=1, source_target_pairs={{0,1},{1,0},{2,3},{3,2},{4,5},{5,4},{6,7},{7,6},{8,9},{9,8},{10,11... | collective-permute-start | bytes 12296 | tf_op jit(solution)/shard_map/ppermute | solution.py:633
  68.0 3.0 %collective-permute-start.18 = (f32[8,128]{1,0:T(8,128)S(1)}, f32[8,128]{1,0:T(8,128)S(1)}, u32[]{:S(2)}, u32[]{:S(2)}) collective-permute-start(f32[8,128]{1,0:T(8,128)S(1)} %get-tuple-element.51.s0), channel_id=1, source_target_pairs={{0,9},{1,8},{2,11},{3,10},{4,13},{5,12},{6,15},{7,14},{8,1},{9,0},... | collective-permute-start | bytes 12296 | tf_op jit(solution)/shard_map/ppermute | solution.py:633
  71.0 6.6 %collective-permute-start.19 = (f32[264,128]{1,0:T(8,128)S(1)}, f32[264,128]{1,0:T(8,128)S(1)}, u32[]{:S(2)}, u32[]{:S(2)}) collective-permute-start(f32[264,128]{1,0:T(8,128)S(1)} %get-tuple-element.52.mine), channel_id=1, source_target_pairs={{0,4},{1,5},{2,6},{3,7},{4,0},{5,1},{6,2},{7,3},{8,12},{9,13},{10,... | collective-permute-start | bytes 405512 | tf_op jit(solution)/shard_map/ppermute | solution.py:633
  71.8 3.6 %collective-permute-start.20 = (f32[8,128]{1,0:T(8,128)S(1)}, f32[8,128]{1,0:T(8,128)S(1)}, u32[]{:S(2)}, u32[]{:S(2)}) collective-permute-start(f32[8,128]{1,0:T(8,128)S(1)} %get-tuple-element.53.s0), channel_id=1, source_target_pairs={{0,2},{1,3},{2,0},{3,1},{4,6},{5,7},{6,4},{7,5},{8,10},{9,11},{10,... | collective-permute-start | bytes 12296 | tf_op jit(solution)/shard_map/ppermute | solution.py:633
  73.1 4.5 %collective-permute-start.21 = (f32[8,128]{1,0:T(8,128)S(1)}, f32[8,128]{1,0:T(8,128)S(1)}, u32[]{:S(2)}, u32[]{:S(2)}) collective-permute-start(f32[8,128]{1,0:T(8,128)S(1)} %get-tuple-element.53.s0), channel_id=1, source_target_pairs={{0,6},{1,7},{2,4},{3,5},{4,2},{5,3},{6,0},{7,1},{8,14},{9,15},{10,... | collective-permute-start | bytes 12296 | tf_op jit(solution)/shard_map/ppermute | solution.py:633

commit v14 on v13

--- a/solution.py
+++ b/solution.py
@@ -370,10 +370,10 @@
 
 
 def forward_kernel(
-    start, sources, own, mate, over0, over1, far0, far1, c0, c1, c2, c3, placed, laps, history, held, cour, last,
+    start, sources, own, mate, over0, over1, far0, far1, large, small, large_mate, small_mate, placed, laps, history, held, cour, last,
     even, odd, banded, y0, y1, sems, sems_even, sems_odd
 ):
-    planes, rows, lanes = c0.shape
+    planes, rows, lanes = own.shape[1:]
     steps = laps.shape[0]
     groups = rows // 8
     chip_here, core, slabs = place(planes)
@@ -392,9 +392,11 @@
 
     banded[...] = band(lanes)
     load_blocks(slabs, (own, mate, (over0, over1), (far0, far1)), odd, even)
-    for slab, block in zip(slabs, (c0, c1, c2, c3)):
+    head = large.shape[0] - planes
+    for here, across, first, rest in ((slabs[0], slabs[2], large, small), (slabs[1], slabs[3], large_mate, small_mate)):
         for p in range(planes):
-            cour[slab + p] = block[p]
+            cour[across + p] = first[p]
+            cour[here + p] = first[planes + p] if p < head else rest[p - head]
 
     for index in range(2 * planes):
         z = (2 * (index // planes) + core) * planes + index % planes
@@ -552,11 +554,14 @@
     return results[0] if parts == 1 else results
 
 
-def arrange_kernel(mine, other, out):
+def arrange_kernel(own, mine, other, large, small):
     y = lax.axis_index("shot") % 2
-    count = mine.shape[0]
-    out[pl.ds(y * count, count)] = mine[...]
-    out[pl.ds((1 - y) * count, count)] = other[...]
+    count, planes = mine.shape[0], own.shape[0]
+    head = planes - small.shape[0]
+    large[pl.ds(y * count, count)] = mine[...]
+    large[pl.ds((1 - y) * count, count)] = other[...]
+    large[planes:] = own[0:head]
+    small[...] = own[head:]
 
 
 def first_plane(shot, planes):
@@ -675,9 +680,16 @@
         (adj_next, adj_cur, True), (adj_next, adj_cur, False), (fwd_prev, fwd_cur, False), earlier=piece
     )
     mate = exchange(own, CORE)
-    c2 = local(arrange_kernel, [courant_sq.shape], piece, exchange(piece, Y))
-    c1, c3 = exchange(c0, CORE), exchange(c2, CORE)
-    over = after(c2, over, parts=2)
+    head = planes * 5 // 8
+    large, small = local(
+        arrange_kernel,
+        [(planes + head, rows_x, rows_y), (planes - head, rows_x, rows_y)],
+        c0,
+        piece,
+        exchange(piece, Y),
+    )
+    speeds = [large, small, exchange(large, CORE), exchange(small, CORE)]
+    over = after(large, over, parts=2)
     far = [exchange(field, CORE) for field in over]
     adj_over = exchange(adj_outgoing, CHIP)
     adj_mate = exchange(adj_own, CORE)
@@ -707,7 +719,7 @@
         compiler_params=pltpu.CompilerParams(vmem_limit_bytes=25 * 2**20),
         cost_estimate=pl.CostEstimate(flops=1000, bytes_accessed=1000, transcendentals=0),
         name="forward_steps",
-    )(ckpt_step[None], src_cells, own, mate, *over, *far, c0, c1, c2, c3, placed)
+    )(ckpt_step[None], src_cells, own, mate, *over, *far, *speeds, placed)
 
     adj_over = after(laps, adj_over)
     adj_far = exchange(adj_over, CORE)

time: 78.6 us -> 77.8 us (0.990)
  local copies, waits for them, and re-layouts: 0.71 us -> 3.13 us
  waiting for transfers between devices: 21.8 us -> 19.7 us
  Pallas kernels: 32.2 us -> 31.4 us
    unnamed x16 -> x24, local copies, waits for them, and re-layouts: 0.71 us -> 3.13 us
    ppermute x22, waiting for transfers between devices: 21.8 us -> 19.7 us  [exchange(): lax.ppermute(value, axes, [(i, i ^ bits) for i in range(lax.axis_size(axe...]
where the time goes in v14:
time: 77.8 us; the launch traced here: 77.5 us
  Pallas kernels  31.4 us (40%)
  starting transfers between devices  21.8 us (28%)
  waiting for transfers between devices  19.7 us (25%)
  local copies, waits for them, and re-layouts  3.13 us (4%)
  between operations  1.44 us (2%)
    ppermute x22, starting transfers between devices, exchange(): lax.ppermute(value, axes, [(i, i ^ bits) for i in range(lax.axis_size(axe...  21.8 us
    ppermute x22, waiting for transfers between devices, exchange(): lax.ppermute(value, axes, [(i, i ^ bits) for i in range(lax.axis_size(axe...  19.7 us
    pallas_call x1, Pallas kernels, whole_shards(): pl.pallas_call(forward_kernel, in_specs=[smem, smem] + [vmem] * 10 + [pl....  9.59 us
    pallas_call x1, Pallas kernels, scatter(): pl.pallas_call(functools.partial(scatter_kernel, rows_x), grid=(rows_all...  9.3 us
    pallas_call x1, Pallas kernels, whole_shards(): pl.pallas_call(adjoint_kernel, in_specs=[vmem] * 8, out_specs=[vmem] * 4,...  7.02 us
    unnamed x24, local copies, waits for them, and re-layouts  3.13 us
    pallas_call x1, Pallas kernels, whole_shards(): pl.pallas_call(first_kernel, in_specs=[hbm] * 3, out_specs=[vmem] * 3, ou...  2.13 us
  transfers between devices with their start and end apart: 22, of which 13 were waited for; matrix products, arithmetic and copies ran while one was open for 0% of the time, Pallas kernels for 28%

profile of v14, /device:TPU:0, one launch (start us, length us, event | category | flops | bytes accessed | tf_op | source)
XLA Modules:
  0.0 77.5 jit_solution(3824131390387186444)
XLA Ops:
  0.6 2.1 %first_to_cross.1 = (f32[2,8,64,128]{3,2,1,0:T(8,128)}, f32[8,64,128]{2,1,0:T(8,128)}, f32[4,64,128]{2,1,0:T(8,128)}) custom-call(f32[2,8,64,128]{3,2,1,0:T(8,128)} %refs_4_.1, f32[2,8,64,128]{3,2,1,0:T(8,128)} %refs_5_.1, f32[8,64,128]{2,1,0:T(8,128)} %courant.1), custom_call_target="tpu_custom_call" | custom-call | tf_op jit(solution)/shard_map/first_to_cross/pallas_call | solution.py:654
  2.8 3.0 %collective-permute-start = (f32[4,64,128]{2,1,0:T(8,128)}, f32[4,64,128]{2,1,0:T(8,128)S(1)}, u32[]{:S(2)}, u32[]{:S(2)}) collective-permute-start(f32[4,64,128]{2,1,0:T(8,128)} %get-tuple-element.32), channel_id=1, source_target_pairs={{0,2},{1,3},{2,0},{3,1},{4,6},{5,7},{6,4},{7,5},{8,10},{9,11},{10,... | collective-permute-start | bytes 393224 | tf_op jit(solution)/shard_map/ppermute | solution.py:638
  5.8 0.0 copy-start.5
  5.8 0.0 copy-start.11
  5.8 0.1 collective-permute-start.4
  5.9 9.3 %receiver_scatter.1 = (f32[9,2048,128]{2,1,0:T(8,128)}, f32[8,128]{1,0:T(8,128)}) custom-call(s32[2,512]{1,0:T(2,128)} %cells_ref.1, f32[2,8,512]{2,1,0:T(8,128)} %observed_ref.1), custom_call_target="tpu_custom_call" | custom-call | flops 4831838208 | bytes 9437184 | tf_op jit(solution)/shard_map/receiver_scatter/pallas_call | solution.py:298
  15.2 0.0 collective-permute-done.value
  15.2 0.7 copy-done.10
  15.9 2.0 %collective-permute-start.3 = (f32[4,64,128]{2,1,0:T(8,128)S(1)}, f32[4,64,128]{2,1,0:T(8,128)S(1)}, u32[]{:S(2)}, u32[]{:S(2)}) collective-permute-start(f32[4,64,128]{2,1,0:T(8,128)S(1)} %after.3.earlier.mine), channel_id=1, source_target_pairs={{0,4},{1,5},{2,6},{3,7},{4,0},{5,1},{6,2},{7,3},{8,12},{9,13},{10,... | collective-permute-start | bytes 393224 | tf_op jit(solution)/shard_map/ppermute | solution.py:638
  17.9 0.0 copy-done
  17.9 0.0 copy-done.1
  17.9 1.4 %pick.1 = (f32[2,8,64,128]{3,2,1,0:T(8,128)}, f32[2,8,64,128]{3,2,1,0:T(8,128)S(1)}, f32[2,8,64,128]{3,2,1,0:T(8,128)S(1)}) custom-call(f32[4,64,128]{2,1,0:T(8,128)S(1)} %after.3.earlier.mine, f32[2,8,64,128]{3,2,1,0:T(8,128)S(1)} %copy-done, f32[2,8,64,128]{3,2,1,0:T(8,128)S(1)} %copy-done.1, f32[2,8,64,128]{3,2,1,0:T(8,128)S(1)} %copy-done, ...), custom_call_target="tpu_custom_call" | custom-call | tf_op jit(solution)/shard_map/pick/pallas_call | solution.py:166
  19.3 0.1 collective-permute-start.2
  19.4 1.5 %collective-permute-start.9 = (f32[2,8,64,128]{3,2,1,0:T(8,128)}, f32[2,8,64,128]{3,2,1,0:T(8,128)S(1)}, u32[]{:S(2)}, u32[]{:S(2)}) collective-permute-start(f32[2,8,64,128]{3,2,1,0:T(8,128)} %get-tuple-element.43), channel_id=1, source_target_pairs={{0,2},{1,3},{2,0},{3,1},{4,6},{5,7},{6,4},{7,5},{8,10},{9,11},{10,... | collective-permute-start | bytes 1572872 | tf_op jit(solution)/shard_map/ppermute | solution.py:638
  20.9 0.1 collective-permute-done.3.other
  21.0 0.1 arrange_kernel.1
  21.0 0.0 copy-start.6
  21.0 0.2 collective-permute-start.7
  21.2 0.4 collective-permute-start.8
  21.6 0.0 collective-permute-done.4.value
  21.6 0.2 collective-permute-start.5
  21.8 1.2 %collective-permute-done.8.small_mate = f32[3,64,128]{2,1,0:T(8,128)S(1)} collective-permute-done((f32[3,64,128]{2,1,0:T(8,128)S(1)}, f32[3,64,128]{2,1,0:T(8,128)S(1)}, u32[]{:S(2)}, u32[]{:S(2)}) %collective-permute-start.8) | collective-permute-done | bytes 98336 | tf_op jit(solution)/shard_map/ppermute | solution.py:638
  23.0 0.0 copy-done.6
  23.0 0.6 copy-done.8
  23.6 0.1 collective-permute-start.6
  24.4 0.0 collective-permute-done.2.mate
  24.4 0.4 collective-permute-start.1
  24.9 0.0 collective-permute-done.7.large_mate
  24.9 0.0 collective-permute-done.5.far0
  24.9 0.4 collective-permute-done.6.far1
  25.3 0.0 copy-done.11
  25.3 0.9 %copy-done.7 = f32[3,64,128]{2,1,0:T(8,128)S(1)} copy-done((f32[3,64,128]{2,1,0:T(8,128)S(1)}, f32[3,64,128]{2,1,0:T(8,128)}, u32[]{:S(2)}) %copy-start.7) | copy-done | bytes 98328
  26.2 0.9 %copy-done.9 = f32[3,64,128]{2,1,0:T(8,128)S(1)} copy-done((f32[3,64,128]{2,1,0:T(8,128)S(1)}, f32[3,64,128]{2,1,0:T(8,128)}, u32[]{:S(2)}) %copy-start.9) | copy-done | bytes 98328
  27.1 9.6 %forward_steps.1 = (f32[8,8,2,64,128]{4,3,2,1,0:T(8,128)S(1)}, f32[8,32,64,128]{3,2,1,0:T(8,128)S(1)}, f32[9,32,64,128]{3,2,1,0:T(8,128)S(1)}, f32[32,64,128]{2,1,0:T(8,128)S(1)}, f32[16,64,128]{2,1,0:T(8,128)S(1)}) custom-call(s32[1]{0:T(128)} %bitcast.3.start, s32[2]{0:T(128)S(1)} %copy-done.11, f32[2,8,64,128]{3,2,1,0:T(8,128)S(1)} %get-tuple-element.34.own, ...), custom_call_target="tpu_custom_call" | custom-call | flops 1000 | bytes 1000 | tf_op jit(solution)/shard_map/forward_steps/pallas_call | solution.py:702
  36.7 0.0 collective-permute-done.9.value
  36.7 0.2 collective-permute-start.10
  36.9 1.0 %inject.1 = f32[8,32,64,128]{3,2,1,0:T(8,128)S(1)} custom-call(f32[9,32,64,128]{3,2,1,0:T(8,128)S(1)} %get-tuple-element.45.held, f32[8,32,64,128]{3,2,1,0:T(8,128)S(1)} %get-tuple-element.46.history), custom_call_target="tpu_custom_call" | custom-call | tf_op jit(solution)/shard_map/inject/pallas_call | solution.py:726
  37.9 0.0 collective-permute-done.1.mate
  37.9 0.8 %collective-permute-done.10.far = f32[2,8,64,128]{3,2,1,0:T(8,128)S(1)} collective-permute-done((f32[2,8,64,128]{3,2,1,0:T(8,128)S(1)}, f32[2,8,64,128]{3,2,1,0:T(8,128)S(1)}, u32[]{:S(2)}, u32[]{:S(2)}) %collective-permute-start.10) | collective-permute-done | bytes 524320 | tf_op jit(solution)/shard_map/ppermute | solution.py:638
  38.7 7.0 %adjoint_steps.1 = (f32[4,64,128]{2,1,0:T(8,128)S(1)}, f32[4,64,128]{2,1,0:T(8,128)S(1)}, f32[4,64,128]{2,1,0:T(8,128)S(1)}, f32[4,64,128]{2,1,0:T(8,128)S(1)}) custom-call(f32[2,8,64,128]{3,2,1,0:T(8,128)S(1)} %get-tuple-element.33.own, f32[2,8,64,128]{3,2,1,0:T(8,128)S(1)} %collective-permute-done.1.mate, f32[2,8,64,128]{3,2,1,0:T(8,128)S(1)} %after.5.over, ...), custom_call_target="tpu_custom_call" | custom-call | flops 62914560 | bytes 33554432 | tf_op jit(solution)/shard_map/adjoint_steps/pallas_call | solution.py:736
  45.8 2.9 %collective-permute-start.11 = (f32[4,64,128]{2,1,0:T(8,128)S(1)}, f32[4,64,128]{2,1,0:T(8,128)S(1)}, u32[]{:S(2)}, u32[]{:S(2)}) collective-permute-start(f32[4,64,128]{2,1,0:T(8,128)S(1)} %get-tuple-element.49), channel_id=1, source_target_pairs={{0,6},{1,7},{2,4},{3,5},{4,2},{5,3},{6,0},{7,1},{8,14},{9,15},{10,... | collective-permute-start | bytes 393224 | tf_op jit(solution)/shard_map/ppermute | solution.py:638
  48.6 0.5 collective-permute-start.12
  49.1 0.2 collective-permute-start.13
  49.3 3.2 %collective-permute-done.11.by_xy = f32[4,64,128]{2,1,0:T(8,128)S(1)} collective-permute-done((f32[4,64,128]{2,1,0:T(8,128)S(1)}, f32[4,64,128]{2,1,0:T(8,128)S(1)}, u32[]{:S(2)}, u32[]{:S(2)}) %collective-permute-start.11) | collective-permute-done | bytes 131104 | tf_op jit(solution)/shard_map/ppermute | solution.py:638
  52.5 2.7 %collective-permute-done.12.by_y = f32[4,64,128]{2,1,0:T(8,128)S(1)} collective-permute-done((f32[4,64,128]{2,1,0:T(8,128)S(1)}, f32[4,64,128]{2,1,0:T(8,128)S(1)}, u32[]{:S(2)}, u32[]{:S(2)}) %collective-permute-start.12) | collective-permute-done | bytes 131104 | tf_op jit(solution)/shard_map/ppermute | solution.py:638
  55.2 0.4 collective-permute-done.13.by_x
  55.6 1.7 %collective-permute-start.14 = (f32[2,64,128]{2,1,0:T(8,128)S(1)}, f32[2,64,128]{2,1,0:T(8,128)S(1)}, u32[]{:S(2)}, u32[]{:S(2)}) collective-permute-start(f32[2,64,128]{2,1,0:T(8,128)S(1)} %get-tuple-element.53), channel_id=1, source_target_pairs={{0,8},{1,9},{2,10},{3,11},{4,12},{5,13},{6,14},{7,15},{8,0},{9,1},... | collective-permute-start | bytes 196616 | tf_op jit(solution)/shard_map/ppermute | solution.py:638
  57.3 2.6 %collective-permute-done.14.other = f32[2,64,128]{2,1,0:T(8,128)S(1)} collective-permute-done((f32[2,64,128]{2,1,0:T(8,128)S(1)}, f32[2,64,128]{2,1,0:T(8,128)S(1)}, u32[]{:S(2)}, u32[]{:S(2)}) %collective-permute-start.14) | collective-permute-done | bytes 65568 | tf_op jit(solution)/shard_map/ppermute | solution.py:638
  60.0 2.7 %collective-permute-start.15 = (f32[2,64,128]{2,1,0:T(8,128)S(1)}, f32[2,64,128]{2,1,0:T(8,128)S(1)}, u32[]{:S(2)}, u32[]{:S(2)}) collective-permute-start(f32[2,64,128]{2,1,0:T(8,128)S(1)} %add_kernel.1.mine), channel_id=1, source_target_pairs={{0,16},{1,17},{2,18},{3,19},{4,20},{5,21},{6,22},{7,23},{8,24},{9,... | collective-permute-start | bytes 196616 | tf_op jit(solution)/shard_map/ppermute | solution.py:638
  62.6 2.6 %collective-permute-done.15.other = f32[2,64,128]{2,1,0:T(8,128)S(1)} collective-permute-done((f32[2,64,128]{2,1,0:T(8,128)S(1)}, f32[2,64,128]{2,1,0:T(8,128)S(1)}, u32[]{:S(2)}, u32[]{:S(2)}) %collective-permute-start.15) | collective-permute-done | bytes 65568 | tf_op jit(solution)/shard_map/ppermute | solution.py:638
  65.2 0.1 sums_kernel.1
  65.3 1.7 %collective-permute-start.16 = (f32[136,128]{1,0:T(8,128)S(1)}, f32[136,128]{1,0:T(8,128)S(1)}, u32[]{:S(2)}, u32[]{:S(2)}) collective-permute-start(f32[136,128]{1,0:T(8,128)S(1)} %get-tuple-element.54.mine), channel_id=1, source_target_pairs={{0,8},{1,9},{2,10},{3,11},{4,12},{5,13},{6,14},{7,15},{8,0},{9,1},... | collective-permute-start | bytes 208904 | tf_op jit(solution)/shard_map/ppermute | solution.py:638
  67.0 0.0 collective-permute-start.17
  67.0 0.5 collective-permute-start.18
  67.5 0.7 collective-permute-done.17.s1
  68.1 1.9 %collective-permute-done.18.s2 = f32[8,128]{1,0:T(8,128)S(1)} collective-permute-done((f32[8,128]{1,0:T(8,128)S(1)}, f32[8,128]{1,0:T(8,128)S(1)}, u32[]{:S(2)}, u32[]{:S(2)}) %collective-permute-start.18) | collective-permute-done | bytes 4128 | tf_op jit(solution)/shard_map/ppermute | solution.py:638
  70.0 0.0 collective-permute-done.16.other
  70.0 1.5 %collective-permute-start.19 = (f32[264,128]{1,0:T(8,128)S(1)}, f32[264,128]{1,0:T(8,128)S(1)}, u32[]{:S(2)}, u32[]{:S(2)}) collective-permute-start(f32[264,128]{1,0:T(8,128)S(1)} %get-tuple-element.56.mine), channel_id=1, source_target_pairs={{0,4},{1,5},{2,6},{3,7},{4,0},{5,1},{6,2},{7,3},{8,12},{9,13},{10,... | collective-permute-start | bytes 405512 | tf_op jit(solution)/shard_map/ppermute | solution.py:638
  71.5 0.7 collective-permute-start.20
  72.2 1.3 %collective-permute-start.21 = (f32[8,128]{1,0:T(8,128)S(1)}, f32[8,128]{1,0:T(8,128)S(1)}, u32[]{:S(2)}, u32[]{:S(2)}) collective-permute-start(f32[8,128]{1,0:T(8,128)S(1)} %get-tuple-element.57.s0), channel_id=1, source_target_pairs={{0,6},{1,7},{2,4},{3,5},{4,2},{5,3},{6,0},{7,1},{8,14},{9,15},{10,... | collective-permute-start | bytes 12296 | tf_op jit(solution)/shard_map/ppermute | solution.py:638
  73.6 1.5 %collective-permute-done.20.s1 = f32[8,128]{1,0:T(8,128)S(1)} collective-permute-done((f32[8,128]{1,0:T(8,128)S(1)}, f32[8,128]{1,0:T(8,128)S(1)}, u32[]{:S(2)}, u32[]{:S(2)}) %collective-permute-start.20) | collective-permute-done | bytes 4128 | tf_op jit(solution)/shard_map/ppermute | solution.py:638
  75.1 1.6 %collective-permute-done.21.s2 = f32[8,128]{1,0:T(8,128)S(1)} collective-permute-done((f32[8,128]{1,0:T(8,128)S(1)}, f32[8,128]{1,0:T(8,128)S(1)}, u32[]{:S(2)}, u32[]{:S(2)}) %collective-permute-start.21) | collective-permute-done | bytes 4128 | tf_op jit(solution)/shard_map/ppermute | solution.py:638
  76.7 0.0 collective-permute-done.19.other
  76.8 0.8 %finish.1 = (f32[8,64,128]{2,1,0:T(8,128)}, f32[1]{0:T(128)}) custom-call(f32[264,128]{1,0:T(8,128)S(1)} %get-tuple-element.56.mine, f32[264,128]{1,0:T(8,128)S(1)} %collective-permute-done.19.other, f32[8,64,128]{2,1,0:T(8,128)S(1)} %copy-done.4, f32[8,128]{1,0:T(8,128)S(1)} %get-tuple-element.57.s0, f32[8,128]{1,0:T(8,128)S(1)} %collective-permute-done.20.s1, ...), custom_call_target="tpu_custom_call" | custom-call | tf_op jit(solution)/shard_map/finish/pallas_call | solution.py:758
  (19 shorter events, 0.2 us)
Async XLA Ops:
  2.8 12.5 %collective-permute-start = (f32[4,64,128]{2,1,0:T(8,128)}, f32[4,64,128]{2,1,0:T(8,128)S(1)}, u32[]{:S(2)}, u32[]{:S(2)}) collective-permute-start(f32[4,64,128]{2,1,0:T(8,128)} %get-tuple-element.32), channel_id=1, source_target_pairs={{0,2},{1,3},{2,0},{3,1},{4,6},{5,7},{6,4},{7,5},{8,10},{9,11},{10,... | collective-permute-start | bytes 393224 | tf_op jit(solution)/shard_map/ppermute | solution.py:638
  5.8 12.2 %copy-start = (f32[2,8,64,128]{3,2,1,0:T(8,128)S(1)}, f32[2,8,64,128]{3,2,1,0:T(8,128)}, u32[]{:S(2)}) copy-start(f32[2,8,64,128]{3,2,1,0:T(8,128)} %refs_2_.1) | copy-start | bytes 1572868
  5.8 12.2 %copy-start.1 = (f32[2,8,64,128]{3,2,1,0:T(8,128)S(1)}, f32[2,8,64,128]{3,2,1,0:T(8,128)}, u32[]{:S(2)}) copy-start(f32[2,8,64,128]{3,2,1,0:T(8,128)} %refs_3_.1) | copy-start | bytes 1572868
  5.8 12.2 %copy-start.2 = (f32[2,8,64,128]{3,2,1,0:T(8,128)S(1)}, f32[2,8,64,128]{3,2,1,0:T(8,128)}, u32[]{:S(2)}) copy-start(f32[2,8,64,128]{3,2,1,0:T(8,128)} %refs_4_.1) | copy-start | bytes 1572868
  5.8 12.2 %copy-start.3 = (f32[2,8,64,128]{3,2,1,0:T(8,128)S(1)}, f32[2,8,64,128]{3,2,1,0:T(8,128)}, u32[]{:S(2)}) copy-start(f32[2,8,64,128]{3,2,1,0:T(8,128)} %refs_5_.1) | copy-start | bytes 1572868
  5.8 15.2 %copy-start.5 = (f32[8,64,128]{2,1,0:T(8,128)S(1)}, f32[8,64,128]{2,1,0:T(8,128)}, u32[]{:S(2)}) copy-start(f32[8,64,128]{2,1,0:T(8,128)} %get-tuple-element.35.own) | copy-start | bytes 786436
  5.8 19.5 %copy-start.11 = (s32[2]{0:T(128)S(1)}, s32[2]{0:T(128)}, u32[]{:S(2)}) copy-start(s32[2]{0:T(128)} %sources.1) | copy-start | bytes 28
  5.8 15.8 %collective-permute-start.4 = (f32[2,8,64,128]{3,2,1,0:T(8,128)}, f32[2,8,64,128]{3,2,1,0:T(8,128)S(1)}, u32[]{:S(2)}, u32[]{:S(2)}) collective-permute-start(f32[2,8,64,128]{3,2,1,0:T(8,128)} %get-tuple-element.37), channel_id=1, source_target_pairs={{0,2},{1,3},{2,0},{3,1},{4,6},{5,7},{6,4},{7,5},{8,10},{9,11},{10,... | collective-permute-start | bytes 1572872 | tf_op jit(solution)/shard_map/ppermute | solution.py:638
  15.2 0.7 copy-start.10
  15.9 5.0 %collective-permute-start.3 = (f32[4,64,128]{2,1,0:T(8,128)S(1)}, f32[4,64,128]{2,1,0:T(8,128)S(1)}, u32[]{:S(2)}, u32[]{:S(2)}) collective-permute-start(f32[4,64,128]{2,1,0:T(8,128)S(1)} %after.3.earlier.mine), channel_id=1, source_target_pairs={{0,4},{1,5},{2,6},{3,7},{4,0},{5,1},{6,2},{7,3},{8,12},{9,13},{10,... | collective-permute-start | bytes 393224 | tf_op jit(solution)/shard_map/ppermute | solution.py:638
  19.3 5.1 %collective-permute-start.2 = (f32[2,8,64,128]{3,2,1,0:T(8,128)S(1)}, f32[2,8,64,128]{3,2,1,0:T(8,128)S(1)}, u32[]{:S(2)}, u32[]{:S(2)}) collective-permute-start(f32[2,8,64,128]{3,2,1,0:T(8,128)S(1)} %get-tuple-element.34.own), channel_id=1, source_target_pairs={{0,1},{1,0},{2,3},{3,2},{4,5},{5,4},{6,7},{7,6},{8,9},{9,8},{10,11... | collective-permute-start | bytes 1572872 | tf_op jit(solution)/shard_map/ppermute | solution.py:638
  19.4 17.3 %collective-permute-start.9 = (f32[2,8,64,128]{3,2,1,0:T(8,128)}, f32[2,8,64,128]{3,2,1,0:T(8,128)S(1)}, u32[]{:S(2)}, u32[]{:S(2)}) collective-permute-start(f32[2,8,64,128]{3,2,1,0:T(8,128)} %get-tuple-element.43), channel_id=1, source_target_pairs={{0,2},{1,3},{2,0},{3,1},{4,6},{5,7},{6,4},{7,5},{8,10},{9,11},{10,... | collective-permute-start | bytes 1572872 | tf_op jit(solution)/shard_map/ppermute | solution.py:638
  21.0 2.0 %copy-start.6 = (f32[3,64,128]{2,1,0:T(8,128)}, f32[3,64,128]{2,1,0:T(8,128)S(1)}, u32[]{:S(2)}) copy-start(f32[3,64,128]{2,1,0:T(8,128)S(1)} %get-tuple-element.40.small) | copy-start | bytes 294916
  21.0 3.9 %collective-permute-start.7 = (f32[13,64,128]{2,1,0:T(8,128)S(1)}, f32[13,64,128]{2,1,0:T(8,128)S(1)}, u32[]{:S(2)}, u32[]{:S(2)}) collective-permute-start(f32[13,64,128]{2,1,0:T(8,128)S(1)} %get-tuple-element.36.earlier.large), channel_id=1, source_target_pairs={{0,1},{1,0},{2,3},{3,2},{4,5},{5,4},{6,7},{7,6},{8,9},{9,8},{10,11... | collective-permute-start | bytes 1277960 | tf_op jit(solution)/shard_map/ppermute | solution.py:638
  21.2 1.8 %collective-permute-start.8 = (f32[3,64,128]{2,1,0:T(8,128)S(1)}, f32[3,64,128]{2,1,0:T(8,128)S(1)}, u32[]{:S(2)}, u32[]{:S(2)}) collective-permute-start(f32[3,64,128]{2,1,0:T(8,128)S(1)} %get-tuple-element.40.small), channel_id=1, source_target_pairs={{0,1},{1,0},{2,3},{3,2},{4,5},{5,4},{6,7},{7,6},{8,9},{9,8},{10,11... | collective-permute-start | bytes 294920 | tf_op jit(solution)/shard_map/ppermute | solution.py:638
  21.6 3.2 %collective-permute-start.5 = (f32[8,64,128]{2,1,0:T(8,128)S(1)}, f32[8,64,128]{2,1,0:T(8,128)}, u32[]{:S(2)}, u32[]{:S(2)}) collective-permute-start(f32[8,64,128]{2,1,0:T(8,128)S(1)} %get-tuple-element.38.over0), channel_id=1, source_target_pairs={{0,1},{1,0},{2,3},{3,2},{4,5},{5,4},{6,7},{7,6},{8,9},{9,8},{10,11... | collective-permute-start | bytes 786440 | tf_op jit(solution)/shard_map/ppermute | solution.py:638
  23.0 0.6 copy-start.8
  23.6 1.7 %collective-permute-start.6 = (f32[8,64,128]{2,1,0:T(8,128)S(1)}, f32[8,64,128]{2,1,0:T(8,128)}, u32[]{:S(2)}, u32[]{:S(2)}) collective-permute-start(f32[8,64,128]{2,1,0:T(8,128)S(1)} %get-tuple-element.39.over1), channel_id=1, source_target_pairs={{0,1},{1,0},{2,3},{3,2},{4,5},{5,4},{6,7},{7,6},{8,9},{9,8},{10,11... | collective-permute-start | bytes 786440 | tf_op jit(solution)/shard_map/ppermute | solution.py:638
  24.4 13.5 %collective-permute-start.1 = (f32[2,8,64,128]{3,2,1,0:T(8,128)S(1)}, f32[2,8,64,128]{3,2,1,0:T(8,128)S(1)}, u32[]{:S(2)}, u32[]{:S(2)}) collective-permute-start(f32[2,8,64,128]{3,2,1,0:T(8,128)S(1)} %get-tuple-element.33.own), channel_id=1, source_target_pairs={{0,1},{1,0},{2,3},{3,2},{4,5},{5,4},{6,7},{7,6},{8,9},{9,8},{10,11... | collective-permute-start | bytes 1572872 | tf_op jit(solution)/shard_map/ppermute | solution.py:638
  25.3 0.9 %copy-start.7 = (f32[3,64,128]{2,1,0:T(8,128)S(1)}, f32[3,64,128]{2,1,0:T(8,128)}, u32[]{:S(2)}) copy-start(f32[3,64,128]{2,1,0:T(8,128)} %copy-done.6) | copy-start | bytes 294916
  26.2 0.9 %copy-start.9 = (f32[3,64,128]{2,1,0:T(8,128)S(1)}, f32[3,64,128]{2,1,0:T(8,128)}, u32[]{:S(2)}) copy-start(f32[3,64,128]{2,1,0:T(8,128)} %copy-done.8) | copy-start | bytes 294916
  36.7 2.0 %collective-permute-start.10 = (f32[2,8,64,128]{3,2,1,0:T(8,128)S(1)}, f32[2,8,64,128]{3,2,1,0:T(8,128)S(1)}, u32[]{:S(2)}, u32[]{:S(2)}) collective-permute-start(f32[2,8,64,128]{3,2,1,0:T(8,128)S(1)} %after.5.over), channel_id=1, source_target_pairs={{0,1},{1,0},{2,3},{3,2},{4,5},{5,4},{6,7},{7,6},{8,9},{9,8},{10,11... | collective-permute-start | bytes 1572872 | tf_op jit(solution)/shard_map/ppermute | solution.py:638
  38.7 26.5 %copy-start.4 = (f32[8,64,128]{2,1,0:T(8,128)S(1)}, f32[8,64,128]{2,1,0:T(8,128)}, u32[]{:S(2)}) copy-start(f32[8,64,128]{2,1,0:T(8,128)} %momentum.3) | copy-start | bytes 786436
  45.8 6.8 %collective-permute-start.11 = (f32[4,64,128]{2,1,0:T(8,128)S(1)}, f32[4,64,128]{2,1,0:T(8,128)S(1)}, u32[]{:S(2)}, u32[]{:S(2)}) collective-permute-start(f32[4,64,128]{2,1,0:T(8,128)S(1)} %get-tuple-element.49), channel_id=1, source_target_pairs={{0,6},{1,7},{2,4},{3,5},{4,2},{5,3},{6,0},{7,1},{8,14},{9,15},{10,... | collective-permute-start | bytes 393224 | tf_op jit(solution)/shard_map/ppermute | solution.py:638
  48.6 6.6 %collective-permute-start.12 = (f32[4,64,128]{2,1,0:T(8,128)S(1)}, f32[4,64,128]{2,1,0:T(8,128)S(1)}, u32[]{:S(2)}, u32[]{:S(2)}) collective-permute-start(f32[4,64,128]{2,1,0:T(8,128)S(1)} %get-tuple-element.50), channel_id=1, source_target_pairs={{0,4},{1,5},{2,6},{3,7},{4,0},{5,1},{6,2},{7,3},{8,12},{9,13},{10,... | collective-permute-start | bytes 393224 | tf_op jit(solution)/shard_map/ppermute | solution.py:638
  49.1 6.4 %collective-permute-start.13 = (f32[4,64,128]{2,1,0:T(8,128)S(1)}, f32[4,64,128]{2,1,0:T(8,128)S(1)}, u32[]{:S(2)}, u32[]{:S(2)}) collective-permute-start(f32[4,64,128]{2,1,0:T(8,128)S(1)} %get-tuple-element.51), channel_id=1, source_target_pairs={{0,2},{1,3},{2,0},{3,1},{4,6},{5,7},{6,4},{7,5},{8,10},{9,11},{10,... | collective-permute-start | bytes 393224 | tf_op jit(solution)/shard_map/ppermute | solution.py:638
  55.6 4.3 %collective-permute-start.14 = (f32[2,64,128]{2,1,0:T(8,128)S(1)}, f32[2,64,128]{2,1,0:T(8,128)S(1)}, u32[]{:S(2)}, u32[]{:S(2)}) collective-permute-start(f32[2,64,128]{2,1,0:T(8,128)S(1)} %get-tuple-element.53), channel_id=1, source_target_pairs={{0,8},{1,9},{2,10},{3,11},{4,12},{5,13},{6,14},{7,15},{8,0},{9,1},... | collective-permute-start | bytes 196616 | tf_op jit(solution)/shard_map/ppermute | solution.py:638
  60.0 5.2 %collective-permute-start.15 = (f32[2,64,128]{2,1,0:T(8,128)S(1)}, f32[2,64,128]{2,1,0:T(8,128)S(1)}, u32[]{:S(2)}, u32[]{:S(2)}) collective-permute-start(f32[2,64,128]{2,1,0:T(8,128)S(1)} %add_kernel.1.mine), channel_id=1, source_target_pairs={{0,16},{1,17},{2,18},{3,19},{4,20},{5,21},{6,22},{7,23},{8,24},{9,... | collective-permute-start | bytes 196616 | tf_op jit(solution)/shard_map/ppermute | solution.py:638
  65.3 4.7 %collective-permute-start.16 = (f32[136,128]{1,0:T(8,128)S(1)}, f32[136,128]{1,0:T(8,128)S(1)}, u32[]{:S(2)}, u32[]{:S(2)}) collective-permute-start(f32[136,128]{1,0:T(8,128)S(1)} %get-tuple-element.54.mine), channel_id=1, source_target_pairs={{0,8},{1,9},{2,10},{3,11},{4,12},{5,13},{6,14},{7,15},{8,0},{9,1},... | collective-permute-start | bytes 208904 | tf_op jit(solution)/shard_map/ppermute | solution.py:638
  67.0 1.2 %collective-permute-start.17 = (f32[8,128]{1,0:T(8,128)S(1)}, f32[8,128]{1,0:T(8,128)S(1)}, u32[]{:S(2)}, u32[]{:S(2)}) collective-permute-start(f32[8,128]{1,0:T(8,128)S(1)} %get-tuple-element.55.s0), channel_id=1, source_target_pairs={{0,1},{1,0},{2,3},{3,2},{4,5},{5,4},{6,7},{7,6},{8,9},{9,8},{10,11... | collective-permute-start | bytes 12296 | tf_op jit(solution)/shard_map/ppermute | solution.py:638
  67.0 3.0 %collective-permute-start.18 = (f32[8,128]{1,0:T(8,128)S(1)}, f32[8,128]{1,0:T(8,128)S(1)}, u32[]{:S(2)}, u32[]{:S(2)}) collective-permute-start(f32[8,128]{1,0:T(8,128)S(1)} %get-tuple-element.55.s0), channel_id=1, source_target_pairs={{0,9},{1,8},{2,11},{3,10},{4,13},{5,12},{6,15},{7,14},{8,1},{9,0},... | collective-permute-start | bytes 12296 | tf_op jit(solution)/shard_map/ppermute | solution.py:638
  70.0 6.7 %collective-permute-start.19 = (f32[264,128]{1,0:T(8,128)S(1)}, f32[264,128]{1,0:T(8,128)S(1)}, u32[]{:S(2)}, u32[]{:S(2)}) collective-permute-start(f32[264,128]{1,0:T(8,128)S(1)} %get-tuple-element.56.mine), channel_id=1, source_target_pairs={{0,4},{1,5},{2,6},{3,7},{4,0},{5,1},{6,2},{7,3},{8,12},{9,13},{10,... | collective-permute-start | bytes 405512 | tf_op jit(solution)/shard_map/ppermute | solution.py:638
  71.5 3.6 %collective-permute-start.20 = (f32[8,128]{1,0:T(8,128)S(1)}, f32[8,128]{1,0:T(8,128)S(1)}, u32[]{:S(2)}, u32[]{:S(2)}) collective-permute-start(f32[8,128]{1,0:T(8,128)S(1)} %get-tuple-element.57.s0), channel_id=1, source_target_pairs={{0,2},{1,3},{2,0},{3,1},{4,6},{5,7},{6,4},{7,5},{8,10},{9,11},{10,... | collective-permute-start | bytes 12296 | tf_op jit(solution)/shard_map/ppermute | solution.py:638
  72.2 4.5 %collective-permute-start.21 = (f32[8,128]{1,0:T(8,128)S(1)}, f32[8,128]{1,0:T(8,128)S(1)}, u32[]{:S(2)}, u32[]{:S(2)}) collective-permute-start(f32[8,128]{1,0:T(8,128)S(1)} %get-tuple-element.57.s0), channel_id=1, source_target_pairs={{0,6},{1,7},{2,4},{3,5},{4,2},{5,3},{6,0},{7,1},{8,14},{9,15},{10,... | collective-permute-start | bytes 12296 | tf_op jit(solution)/shard_map/ppermute | solution.py:638

commit v15 on v14

--- a/solution.py
+++ b/solution.py
@@ -716,7 +716,7 @@
             pltpu.SemaphoreType.DMA((4,)),
             pltpu.SemaphoreType.DMA((4,)),
         ],
-        compiler_params=pltpu.CompilerParams(vmem_limit_bytes=25 * 2**20),
+        compiler_params=pltpu.CompilerParams(vmem_limit_bytes=21 * 2**20),
         cost_estimate=pl.CostEstimate(flops=1000, bytes_accessed=1000, transcendentals=0),
         name="forward_steps",
     )(ckpt_step[None], src_cells, own, mate, *over, *far, *speeds, placed)

time: 77.8 us -> 77.8 us (level)
  no operation moved by 1% of the time
where the time goes in v15:
time: 77.8 us; the launch traced here: 77.5 us
  Pallas kernels  31.4 us (40%)
  starting transfers between devices  21.8 us (28%)
  waiting for transfers between devices  19.7 us (25%)
  local copies, waits for them, and re-layouts  3.13 us (4%)
  between operations  1.44 us (2%)
    ppermute x22, starting transfers between devices, exchange(): lax.ppermute(value, axes, [(i, i ^ bits) for i in range(lax.axis_size(axe...  21.8 us
    ppermute x22, waiting for transfers between devices, exchange(): lax.ppermute(value, axes, [(i, i ^ bits) for i in range(lax.axis_size(axe...  19.7 us
    pallas_call x1, Pallas kernels, whole_shards(): pl.pallas_call(forward_kernel, in_specs=[smem, smem] + [vmem] * 10 + [pl....  9.59 us
    pallas_call x1, Pallas kernels, scatter(): pl.pallas_call(functools.partial(scatter_kernel, rows_x), grid=(rows_all...  9.3 us
    pallas_call x1, Pallas kernels, whole_shards(): pl.pallas_call(adjoint_kernel, in_specs=[vmem] * 8, out_specs=[vmem] * 4,...  7 us
    unnamed x24, local copies, waits for them, and re-layouts  3.13 us
    pallas_call x1, Pallas kernels, whole_shards(): pl.pallas_call(first_kernel, in_specs=[hbm] * 3, out_specs=[vmem] * 3, ou...  2.13 us
  transfers between devices with their start and end apart: 22, of which 13 were waited for; matrix products, arithmetic and copies ran while one was open for 0% of the time, Pallas kernels for 28%

profile of v15, /device:TPU:0, one launch (start us, length us, event | category | flops | bytes accessed | tf_op | source)
XLA Modules:
  0.0 77.5 jit_solution(9277537848113104975)
XLA Ops:
  0.6 2.1 %first_to_cross.1 = (f32[2,8,64,128]{3,2,1,0:T(8,128)}, f32[8,64,128]{2,1,0:T(8,128)}, f32[4,64,128]{2,1,0:T(8,128)}) custom-call(f32[2,8,64,128]{3,2,1,0:T(8,128)} %refs_4_.1, f32[2,8,64,128]{3,2,1,0:T(8,128)} %refs_5_.1, f32[8,64,128]{2,1,0:T(8,128)} %courant.1), custom_call_target="tpu_custom_call" | custom-call | tf_op jit(solution)/shard_map/first_to_cross/pallas_call | solution.py:654
  2.8 3.0 %collective-permute-start = (f32[4,64,128]{2,1,0:T(8,128)}, f32[4,64,128]{2,1,0:T(8,128)S(1)}, u32[]{:S(2)}, u32[]{:S(2)}) collective-permute-start(f32[4,64,128]{2,1,0:T(8,128)} %get-tuple-element.32), channel_id=1, source_target_pairs={{0,2},{1,3},{2,0},{3,1},{4,6},{5,7},{6,4},{7,5},{8,10},{9,11},{10,... | collective-permute-start | bytes 393224 | tf_op jit(solution)/shard_map/ppermute | solution.py:638
  5.8 0.0 copy-start.5
  5.8 0.0 copy-start.11
  5.8 0.1 collective-permute-start.4
  5.9 9.3 %receiver_scatter.1 = (f32[9,2048,128]{2,1,0:T(8,128)}, f32[8,128]{1,0:T(8,128)}) custom-call(s32[2,512]{1,0:T(2,128)} %cells_ref.1, f32[2,8,512]{2,1,0:T(8,128)} %observed_ref.1), custom_call_target="tpu_custom_call" | custom-call | flops 4831838208 | bytes 9437184 | tf_op jit(solution)/shard_map/receiver_scatter/pallas_call | solution.py:298
  15.2 0.0 collective-permute-done.value
  15.2 0.7 copy-done.10
  15.9 2.0 %collective-permute-start.3 = (f32[4,64,128]{2,1,0:T(8,128)S(1)}, f32[4,64,128]{2,1,0:T(8,128)S(1)}, u32[]{:S(2)}, u32[]{:S(2)}) collective-permute-start(f32[4,64,128]{2,1,0:T(8,128)S(1)} %after.3.earlier.mine), channel_id=1, source_target_pairs={{0,4},{1,5},{2,6},{3,7},{4,0},{5,1},{6,2},{7,3},{8,12},{9,13},{10,... | collective-permute-start | bytes 393224 | tf_op jit(solution)/shard_map/ppermute | solution.py:638
  17.9 0.0 copy-done
  17.9 0.0 copy-done.1
  17.9 0.0 copy-done.3
  17.9 1.4 %pick.1 = (f32[2,8,64,128]{3,2,1,0:T(8,128)}, f32[2,8,64,128]{3,2,1,0:T(8,128)S(1)}, f32[2,8,64,128]{3,2,1,0:T(8,128)S(1)}) custom-call(f32[4,64,128]{2,1,0:T(8,128)S(1)} %after.3.earlier.mine, f32[2,8,64,128]{3,2,1,0:T(8,128)S(1)} %copy-done, f32[2,8,64,128]{3,2,1,0:T(8,128)S(1)} %copy-done.1, f32[2,8,64,128]{3,2,1,0:T(8,128)S(1)} %copy-done, ...), custom_call_target="tpu_custom_call" | custom-call | tf_op jit(solution)/shard_map/pick/pallas_call | solution.py:166
  19.3 0.1 collective-permute-start.2
  19.4 1.5 %collective-permute-start.9 = (f32[2,8,64,128]{3,2,1,0:T(8,128)}, f32[2,8,64,128]{3,2,1,0:T(8,128)S(1)}, u32[]{:S(2)}, u32[]{:S(2)}) collective-permute-start(f32[2,8,64,128]{3,2,1,0:T(8,128)} %get-tuple-element.43), channel_id=1, source_target_pairs={{0,2},{1,3},{2,0},{3,1},{4,6},{5,7},{6,4},{7,5},{8,10},{9,11},{10,... | collective-permute-start | bytes 1572872 | tf_op jit(solution)/shard_map/ppermute | solution.py:638
  20.9 0.1 collective-permute-done.3.other
  21.0 0.1 arrange_kernel.1
  21.0 0.0 copy-start.6
  21.0 0.2 collective-permute-start.7
  21.2 0.4 collective-permute-start.8
  21.6 0.0 collective-permute-done.4.value
  21.6 0.2 collective-permute-start.5
  21.8 1.2 %collective-permute-done.8.small_mate = f32[3,64,128]{2,1,0:T(8,128)S(1)} collective-permute-done((f32[3,64,128]{2,1,0:T(8,128)S(1)}, f32[3,64,128]{2,1,0:T(8,128)S(1)}, u32[]{:S(2)}, u32[]{:S(2)}) %collective-permute-start.8) | collective-permute-done | bytes 98336 | tf_op jit(solution)/shard_map/ppermute | solution.py:638
  23.0 0.6 copy-done.8
  23.6 0.1 collective-permute-start.6
  24.4 0.0 collective-permute-done.2.mate
  24.4 0.4 collective-permute-start.1
  24.9 0.0 collective-permute-done.7.large_mate
  24.9 0.0 collective-permute-done.5.far0
  24.9 0.4 collective-permute-done.6.far1
  25.3 0.0 copy-done.11
  25.3 0.9 %copy-done.7 = f32[3,64,128]{2,1,0:T(8,128)S(1)} copy-done((f32[3,64,128]{2,1,0:T(8,128)S(1)}, f32[3,64,128]{2,1,0:T(8,128)}, u32[]{:S(2)}) %copy-start.7) | copy-done | bytes 98328
  26.2 0.9 %copy-done.9 = f32[3,64,128]{2,1,0:T(8,128)S(1)} copy-done((f32[3,64,128]{2,1,0:T(8,128)S(1)}, f32[3,64,128]{2,1,0:T(8,128)}, u32[]{:S(2)}) %copy-start.9) | copy-done | bytes 98328
  27.1 9.6 %forward_steps.1 = (f32[8,8,2,64,128]{4,3,2,1,0:T(8,128)S(1)}, f32[8,32,64,128]{3,2,1,0:T(8,128)S(1)}, f32[9,32,64,128]{3,2,1,0:T(8,128)S(1)}, f32[32,64,128]{2,1,0:T(8,128)S(1)}, f32[16,64,128]{2,1,0:T(8,128)S(1)}) custom-call(s32[1]{0:T(128)} %bitcast.3.start, s32[2]{0:T(128)S(1)} %copy-done.11, f32[2,8,64,128]{3,2,1,0:T(8,128)S(1)} %get-tuple-element.34.own, ...), custom_call_target="tpu_custom_call" | custom-call | flops 1000 | bytes 1000 | tf_op jit(solution)/shard_map/forward_steps/pallas_call | solution.py:702
  36.7 0.0 collective-permute-done.9.value
  36.7 0.2 collective-permute-start.10
  37.0 1.0 %inject.1 = f32[8,32,64,128]{3,2,1,0:T(8,128)S(1)} custom-call(f32[9,32,64,128]{3,2,1,0:T(8,128)S(1)} %get-tuple-element.45.held, f32[8,32,64,128]{3,2,1,0:T(8,128)S(1)} %get-tuple-element.46.history), custom_call_target="tpu_custom_call" | custom-call | tf_op jit(solution)/shard_map/inject/pallas_call | solution.py:726
  37.9 0.0 collective-permute-done.1.mate
  38.0 0.8 collective-permute-done.10.far
  38.7 7.0 %adjoint_steps.1 = (f32[4,64,128]{2,1,0:T(8,128)S(1)}, f32[4,64,128]{2,1,0:T(8,128)S(1)}, f32[4,64,128]{2,1,0:T(8,128)S(1)}, f32[4,64,128]{2,1,0:T(8,128)S(1)}) custom-call(f32[2,8,64,128]{3,2,1,0:T(8,128)S(1)} %get-tuple-element.33.own, f32[2,8,64,128]{3,2,1,0:T(8,128)S(1)} %collective-permute-done.1.mate, f32[2,8,64,128]{3,2,1,0:T(8,128)S(1)} %after.5.over, ...), custom_call_target="tpu_custom_call" | custom-call | flops 62914560 | bytes 33554432 | tf_op jit(solution)/shard_map/adjoint_steps/pallas_call | solution.py:736
  45.7 2.9 %collective-permute-start.11 = (f32[4,64,128]{2,1,0:T(8,128)S(1)}, f32[4,64,128]{2,1,0:T(8,128)S(1)}, u32[]{:S(2)}, u32[]{:S(2)}) collective-permute-start(f32[4,64,128]{2,1,0:T(8,128)S(1)} %get-tuple-element.49), channel_id=1, source_target_pairs={{0,6},{1,7},{2,4},{3,5},{4,2},{5,3},{6,0},{7,1},{8,14},{9,15},{10,... | collective-permute-start | bytes 393224 | tf_op jit(solution)/shard_map/ppermute | solution.py:638
  48.6 0.5 collective-permute-start.12
  49.1 0.2 collective-permute-start.13
  49.3 3.2 %collective-permute-done.11.by_xy = f32[4,64,128]{2,1,0:T(8,128)S(1)} collective-permute-done((f32[4,64,128]{2,1,0:T(8,128)S(1)}, f32[4,64,128]{2,1,0:T(8,128)S(1)}, u32[]{:S(2)}, u32[]{:S(2)}) %collective-permute-start.11) | collective-permute-done | bytes 131104 | tf_op jit(solution)/shard_map/ppermute | solution.py:638
  52.5 2.7 %collective-permute-done.12.by_y = f32[4,64,128]{2,1,0:T(8,128)S(1)} collective-permute-done((f32[4,64,128]{2,1,0:T(8,128)S(1)}, f32[4,64,128]{2,1,0:T(8,128)S(1)}, u32[]{:S(2)}, u32[]{:S(2)}) %collective-permute-start.12) | collective-permute-done | bytes 131104 | tf_op jit(solution)/shard_map/ppermute | solution.py:638
  55.2 0.4 collective-permute-done.13.by_x
  55.6 1.6 %collective-permute-start.14 = (f32[2,64,128]{2,1,0:T(8,128)S(1)}, f32[2,64,128]{2,1,0:T(8,128)S(1)}, u32[]{:S(2)}, u32[]{:S(2)}) collective-permute-start(f32[2,64,128]{2,1,0:T(8,128)S(1)} %get-tuple-element.53), channel_id=1, source_target_pairs={{0,8},{1,9},{2,10},{3,11},{4,12},{5,13},{6,14},{7,15},{8,0},{9,1},... | collective-permute-start | bytes 196616 | tf_op jit(solution)/shard_map/ppermute | solution.py:638
  57.2 2.7 %collective-permute-done.14.other = f32[2,64,128]{2,1,0:T(8,128)S(1)} collective-permute-done((f32[2,64,128]{2,1,0:T(8,128)S(1)}, f32[2,64,128]{2,1,0:T(8,128)S(1)}, u32[]{:S(2)}, u32[]{:S(2)}) %collective-permute-start.14) | collective-permute-done | bytes 65568 | tf_op jit(solution)/shard_map/ppermute | solution.py:638
  59.9 2.7 %collective-permute-start.15 = (f32[2,64,128]{2,1,0:T(8,128)S(1)}, f32[2,64,128]{2,1,0:T(8,128)S(1)}, u32[]{:S(2)}, u32[]{:S(2)}) collective-permute-start(f32[2,64,128]{2,1,0:T(8,128)S(1)} %add_kernel.1.mine), channel_id=1, source_target_pairs={{0,16},{1,17},{2,18},{3,19},{4,20},{5,21},{6,22},{7,23},{8,24},{9,... | collective-permute-start | bytes 196616 | tf_op jit(solution)/shard_map/ppermute | solution.py:638
  62.6 2.5 %collective-permute-done.15.other = f32[2,64,128]{2,1,0:T(8,128)S(1)} collective-permute-done((f32[2,64,128]{2,1,0:T(8,128)S(1)}, f32[2,64,128]{2,1,0:T(8,128)S(1)}, u32[]{:S(2)}, u32[]{:S(2)}) %collective-permute-start.15) | collective-permute-done | bytes 65568 | tf_op jit(solution)/shard_map/ppermute | solution.py:638
  65.2 0.1 sums_kernel.1
  65.3 1.6 %collective-permute-start.16 = (f32[136,128]{1,0:T(8,128)S(1)}, f32[136,128]{1,0:T(8,128)S(1)}, u32[]{:S(2)}, u32[]{:S(2)}) collective-permute-start(f32[136,128]{1,0:T(8,128)S(1)} %get-tuple-element.54.mine), channel_id=1, source_target_pairs={{0,8},{1,9},{2,10},{3,11},{4,12},{5,13},{6,14},{7,15},{8,0},{9,1},... | collective-permute-start | bytes 208904 | tf_op jit(solution)/shard_map/ppermute | solution.py:638
  66.9 0.0 collective-permute-start.17
  66.9 0.6 collective-permute-start.18
  67.4 0.6 collective-permute-done.17.s1
  68.0 1.9 %collective-permute-done.18.s2 = f32[8,128]{1,0:T(8,128)S(1)} collective-permute-done((f32[8,128]{1,0:T(8,128)S(1)}, f32[8,128]{1,0:T(8,128)S(1)}, u32[]{:S(2)}, u32[]{:S(2)}) %collective-permute-start.18) | collective-permute-done | bytes 4128 | tf_op jit(solution)/shard_map/ppermute | solution.py:638
  69.9 0.0 collective-permute-done.16.other
  69.9 1.5 %collective-permute-start.19 = (f32[264,128]{1,0:T(8,128)S(1)}, f32[264,128]{1,0:T(8,128)S(1)}, u32[]{:S(2)}, u32[]{:S(2)}) collective-permute-start(f32[264,128]{1,0:T(8,128)S(1)} %get-tuple-element.56.mine), channel_id=1, source_target_pairs={{0,4},{1,5},{2,6},{3,7},{4,0},{5,1},{6,2},{7,3},{8,12},{9,13},{10,... | collective-permute-start | bytes 405512 | tf_op jit(solution)/shard_map/ppermute | solution.py:638
  71.4 0.8 %collective-permute-start.20 = (f32[8,128]{1,0:T(8,128)S(1)}, f32[8,128]{1,0:T(8,128)S(1)}, u32[]{:S(2)}, u32[]{:S(2)}) collective-permute-start(f32[8,128]{1,0:T(8,128)S(1)} %get-tuple-element.57.s0), channel_id=1, source_target_pairs={{0,2},{1,3},{2,0},{3,1},{4,6},{5,7},{6,4},{7,5},{8,10},{9,11},{10,... | collective-permute-start | bytes 12296 | tf_op jit(solution)/shard_map/ppermute | solution.py:638
  72.2 1.3 %collective-permute-start.21 = (f32[8,128]{1,0:T(8,128)S(1)}, f32[8,128]{1,0:T(8,128)S(1)}, u32[]{:S(2)}, u32[]{:S(2)}) collective-permute-start(f32[8,128]{1,0:T(8,128)S(1)} %get-tuple-element.57.s0), channel_id=1, source_target_pairs={{0,6},{1,7},{2,4},{3,5},{4,2},{5,3},{6,0},{7,1},{8,14},{9,15},{10,... | collective-permute-start | bytes 12296 | tf_op jit(solution)/shard_map/ppermute | solution.py:638
  73.5 1.5 %collective-permute-done.20.s1 = f32[8,128]{1,0:T(8,128)S(1)} collective-permute-done((f32[8,128]{1,0:T(8,128)S(1)}, f32[8,128]{1,0:T(8,128)S(1)}, u32[]{:S(2)}, u32[]{:S(2)}) %collective-permute-start.20) | collective-permute-done | bytes 4128 | tf_op jit(solution)/shard_map/ppermute | solution.py:638
  75.0 1.7 %collective-permute-done.21.s2 = f32[8,128]{1,0:T(8,128)S(1)} collective-permute-done((f32[8,128]{1,0:T(8,128)S(1)}, f32[8,128]{1,0:T(8,128)S(1)}, u32[]{:S(2)}, u32[]{:S(2)}) %collective-permute-start.21) | collective-permute-done | bytes 4128 | tf_op jit(solution)/shard_map/ppermute | solution.py:638
  76.7 0.0 collective-permute-done.19.other
  76.7 0.8 %finish.1 = (f32[8,64,128]{2,1,0:T(8,128)}, f32[1]{0:T(128)}) custom-call(f32[264,128]{1,0:T(8,128)S(1)} %get-tuple-element.56.mine, f32[264,128]{1,0:T(8,128)S(1)} %collective-permute-done.19.other, f32[8,64,128]{2,1,0:T(8,128)S(1)} %copy-done.4, f32[8,128]{1,0:T(8,128)S(1)} %get-tuple-element.57.s0, f32[8,128]{1,0:T(8,128)S(1)} %collective-permute-done.20.s1, ...), custom_call_target="tpu_custom_call" | custom-call | tf_op jit(solution)/shard_map/finish/pallas_call | solution.py:758
  (19 shorter events, 0.2 us)
Async XLA Ops:
  2.8 12.5 %collective-permute-start = (f32[4,64,128]{2,1,0:T(8,128)}, f32[4,64,128]{2,1,0:T(8,128)S(1)}, u32[]{:S(2)}, u32[]{:S(2)}) collective-permute-start(f32[4,64,128]{2,1,0:T(8,128)} %get-tuple-element.32), channel_id=1, source_target_pairs={{0,2},{1,3},{2,0},{3,1},{4,6},{5,7},{6,4},{7,5},{8,10},{9,11},{10,... | collective-permute-start | bytes 393224 | tf_op jit(solution)/shard_map/ppermute | solution.py:638
  5.8 12.2 %copy-start = (f32[2,8,64,128]{3,2,1,0:T(8,128)S(1)}, f32[2,8,64,128]{3,2,1,0:T(8,128)}, u32[]{:S(2)}) copy-start(f32[2,8,64,128]{3,2,1,0:T(8,128)} %refs_2_.1) | copy-start | bytes 1572868
  5.8 12.2 %copy-start.1 = (f32[2,8,64,128]{3,2,1,0:T(8,128)S(1)}, f32[2,8,64,128]{3,2,1,0:T(8,128)}, u32[]{:S(2)}) copy-start(f32[2,8,64,128]{3,2,1,0:T(8,128)} %refs_3_.1) | copy-start | bytes 1572868
  5.8 12.2 %copy-start.2 = (f32[2,8,64,128]{3,2,1,0:T(8,128)S(1)}, f32[2,8,64,128]{3,2,1,0:T(8,128)}, u32[]{:S(2)}) copy-start(f32[2,8,64,128]{3,2,1,0:T(8,128)} %refs_4_.1) | copy-start | bytes 1572868
  5.8 12.2 %copy-start.3 = (f32[2,8,64,128]{3,2,1,0:T(8,128)S(1)}, f32[2,8,64,128]{3,2,1,0:T(8,128)}, u32[]{:S(2)}) copy-start(f32[2,8,64,128]{3,2,1,0:T(8,128)} %refs_5_.1) | copy-start | bytes 1572868
  5.8 15.2 %copy-start.5 = (f32[8,64,128]{2,1,0:T(8,128)S(1)}, f32[8,64,128]{2,1,0:T(8,128)}, u32[]{:S(2)}) copy-start(f32[8,64,128]{2,1,0:T(8,128)} %get-tuple-element.35.own) | copy-start | bytes 786436
  5.8 19.5 %copy-start.11 = (s32[2]{0:T(128)S(1)}, s32[2]{0:T(128)}, u32[]{:S(2)}) copy-start(s32[2]{0:T(128)} %sources.1) | copy-start | bytes 28
  5.8 15.8 %collective-permute-start.4 = (f32[2,8,64,128]{3,2,1,0:T(8,128)}, f32[2,8,64,128]{3,2,1,0:T(8,128)S(1)}, u32[]{:S(2)}, u32[]{:S(2)}) collective-permute-start(f32[2,8,64,128]{3,2,1,0:T(8,128)} %get-tuple-element.37), channel_id=1, source_target_pairs={{0,2},{1,3},{2,0},{3,1},{4,6},{5,7},{6,4},{7,5},{8,10},{9,11},{10,... | collective-permute-start | bytes 1572872 | tf_op jit(solution)/shard_map/ppermute | solution.py:638
  15.2 0.7 copy-start.10
  15.9 5.0 %collective-permute-start.3 = (f32[4,64,128]{2,1,0:T(8,128)S(1)}, f32[4,64,128]{2,1,0:T(8,128)S(1)}, u32[]{:S(2)}, u32[]{:S(2)}) collective-permute-start(f32[4,64,128]{2,1,0:T(8,128)S(1)} %after.3.earlier.mine), channel_id=1, source_target_pairs={{0,4},{1,5},{2,6},{3,7},{4,0},{5,1},{6,2},{7,3},{8,12},{9,13},{10,... | collective-permute-start | bytes 393224 | tf_op jit(solution)/shard_map/ppermute | solution.py:638
  19.3 5.1 %collective-permute-start.2 = (f32[2,8,64,128]{3,2,1,0:T(8,128)S(1)}, f32[2,8,64,128]{3,2,1,0:T(8,128)S(1)}, u32[]{:S(2)}, u32[]{:S(2)}) collective-permute-start(f32[2,8,64,128]{3,2,1,0:T(8,128)S(1)} %get-tuple-element.34.own), channel_id=1, source_target_pairs={{0,1},{1,0},{2,3},{3,2},{4,5},{5,4},{6,7},{7,6},{8,9},{9,8},{10,11... | collective-permute-start | bytes 1572872 | tf_op jit(solution)/shard_map/ppermute | solution.py:638
  19.4 17.3 %collective-permute-start.9 = (f32[2,8,64,128]{3,2,1,0:T(8,128)}, f32[2,8,64,128]{3,2,1,0:T(8,128)S(1)}, u32[]{:S(2)}, u32[]{:S(2)}) collective-permute-start(f32[2,8,64,128]{3,2,1,0:T(8,128)} %get-tuple-element.43), channel_id=1, source_target_pairs={{0,2},{1,3},{2,0},{3,1},{4,6},{5,7},{6,4},{7,5},{8,10},{9,11},{10,... | collective-permute-start | bytes 1572872 | tf_op jit(solution)/shard_map/ppermute | solution.py:638
  21.0 2.0 %copy-start.6 = (f32[3,64,128]{2,1,0:T(8,128)}, f32[3,64,128]{2,1,0:T(8,128)S(1)}, u32[]{:S(2)}) copy-start(f32[3,64,128]{2,1,0:T(8,128)S(1)} %get-tuple-element.40.small) | copy-start | bytes 294916
  21.0 3.9 %collective-permute-start.7 = (f32[13,64,128]{2,1,0:T(8,128)S(1)}, f32[13,64,128]{2,1,0:T(8,128)S(1)}, u32[]{:S(2)}, u32[]{:S(2)}) collective-permute-start(f32[13,64,128]{2,1,0:T(8,128)S(1)} %get-tuple-element.36.earlier.large), channel_id=1, source_target_pairs={{0,1},{1,0},{2,3},{3,2},{4,5},{5,4},{6,7},{7,6},{8,9},{9,8},{10,11... | collective-permute-start | bytes 1277960 | tf_op jit(solution)/shard_map/ppermute | solution.py:638
  21.2 1.8 %collective-permute-start.8 = (f32[3,64,128]{2,1,0:T(8,128)S(1)}, f32[3,64,128]{2,1,0:T(8,128)S(1)}, u32[]{:S(2)}, u32[]{:S(2)}) collective-permute-start(f32[3,64,128]{2,1,0:T(8,128)S(1)} %get-tuple-element.40.small), channel_id=1, source_target_pairs={{0,1},{1,0},{2,3},{3,2},{4,5},{5,4},{6,7},{7,6},{8,9},{9,8},{10,11... | collective-permute-start | bytes 294920 | tf_op jit(solution)/shard_map/ppermute | solution.py:638
  21.6 3.2 %collective-permute-start.5 = (f32[8,64,128]{2,1,0:T(8,128)S(1)}, f32[8,64,128]{2,1,0:T(8,128)}, u32[]{:S(2)}, u32[]{:S(2)}) collective-permute-start(f32[8,64,128]{2,1,0:T(8,128)S(1)} %get-tuple-element.38.over0), channel_id=1, source_target_pairs={{0,1},{1,0},{2,3},{3,2},{4,5},{5,4},{6,7},{7,6},{8,9},{9,8},{10,11... | collective-permute-start | bytes 786440 | tf_op jit(solution)/shard_map/ppermute | solution.py:638
  23.0 0.6 copy-start.8
  23.6 1.7 %collective-permute-start.6 = (f32[8,64,128]{2,1,0:T(8,128)S(1)}, f32[8,64,128]{2,1,0:T(8,128)}, u32[]{:S(2)}, u32[]{:S(2)}) collective-permute-start(f32[8,64,128]{2,1,0:T(8,128)S(1)} %get-tuple-element.39.over1), channel_id=1, source_target_pairs={{0,1},{1,0},{2,3},{3,2},{4,5},{5,4},{6,7},{7,6},{8,9},{9,8},{10,11... | collective-permute-start | bytes 786440 | tf_op jit(solution)/shard_map/ppermute | solution.py:638
  24.4 13.5 %collective-permute-start.1 = (f32[2,8,64,128]{3,2,1,0:T(8,128)S(1)}, f32[2,8,64,128]{3,2,1,0:T(8,128)S(1)}, u32[]{:S(2)}, u32[]{:S(2)}) collective-permute-start(f32[2,8,64,128]{3,2,1,0:T(8,128)S(1)} %get-tuple-element.33.own), channel_id=1, source_target_pairs={{0,1},{1,0},{2,3},{3,2},{4,5},{5,4},{6,7},{7,6},{8,9},{9,8},{10,11... | collective-permute-start | bytes 1572872 | tf_op jit(solution)/shard_map/ppermute | solution.py:638
  25.3 0.9 %copy-start.7 = (f32[3,64,128]{2,1,0:T(8,128)S(1)}, f32[3,64,128]{2,1,0:T(8,128)}, u32[]{:S(2)}) copy-start(f32[3,64,128]{2,1,0:T(8,128)} %copy-done.6) | copy-start | bytes 294916
  26.2 0.9 %copy-start.9 = (f32[3,64,128]{2,1,0:T(8,128)S(1)}, f32[3,64,128]{2,1,0:T(8,128)}, u32[]{:S(2)}) copy-start(f32[3,64,128]{2,1,0:T(8,128)} %copy-done.8) | copy-start | bytes 294916
  36.7 2.0 %collective-permute-start.10 = (f32[2,8,64,128]{3,2,1,0:T(8,128)S(1)}, f32[2,8,64,128]{3,2,1,0:T(8,128)S(1)}, u32[]{:S(2)}, u32[]{:S(2)}) collective-permute-start(f32[2,8,64,128]{3,2,1,0:T(8,128)S(1)} %after.5.over), channel_id=1, source_target_pairs={{0,1},{1,0},{2,3},{3,2},{4,5},{5,4},{6,7},{7,6},{8,9},{9,8},{10,11... | collective-permute-start | bytes 1572872 | tf_op jit(solution)/shard_map/ppermute | solution.py:638
  38.7 26.5 %copy-start.4 = (f32[8,64,128]{2,1,0:T(8,128)S(1)}, f32[8,64,128]{2,1,0:T(8,128)}, u32[]{:S(2)}) copy-start(f32[8,64,128]{2,1,0:T(8,128)} %momentum.3) | copy-start | bytes 786436
  45.7 6.8 %collective-permute-start.11 = (f32[4,64,128]{2,1,0:T(8,128)S(1)}, f32[4,64,128]{2,1,0:T(8,128)S(1)}, u32[]{:S(2)}, u32[]{:S(2)}) collective-permute-start(f32[4,64,128]{2,1,0:T(8,128)S(1)} %get-tuple-element.49), channel_id=1, source_target_pairs={{0,6},{1,7},{2,4},{3,5},{4,2},{5,3},{6,0},{7,1},{8,14},{9,15},{10,... | collective-permute-start | bytes 393224 | tf_op jit(solution)/shard_map/ppermute | solution.py:638
  48.6 6.6 %collective-permute-start.12 = (f32[4,64,128]{2,1,0:T(8,128)S(1)}, f32[4,64,128]{2,1,0:T(8,128)S(1)}, u32[]{:S(2)}, u32[]{:S(2)}) collective-permute-start(f32[4,64,128]{2,1,0:T(8,128)S(1)} %get-tuple-element.50), channel_id=1, source_target_pairs={{0,4},{1,5},{2,6},{3,7},{4,0},{5,1},{6,2},{7,3},{8,12},{9,13},{10,... | collective-permute-start | bytes 393224 | tf_op jit(solution)/shard_map/ppermute | solution.py:638
  49.1 6.5 %collective-permute-start.13 = (f32[4,64,128]{2,1,0:T(8,128)S(1)}, f32[4,64,128]{2,1,0:T(8,128)S(1)}, u32[]{:S(2)}, u32[]{:S(2)}) collective-permute-start(f32[4,64,128]{2,1,0:T(8,128)S(1)} %get-tuple-element.51), channel_id=1, source_target_pairs={{0,2},{1,3},{2,0},{3,1},{4,6},{5,7},{6,4},{7,5},{8,10},{9,11},{10,... | collective-permute-start | bytes 393224 | tf_op jit(solution)/shard_map/ppermute | solution.py:638
  55.6 4.3 %collective-permute-start.14 = (f32[2,64,128]{2,1,0:T(8,128)S(1)}, f32[2,64,128]{2,1,0:T(8,128)S(1)}, u32[]{:S(2)}, u32[]{:S(2)}) collective-permute-start(f32[2,64,128]{2,1,0:T(8,128)S(1)} %get-tuple-element.53), channel_id=1, source_target_pairs={{0,8},{1,9},{2,10},{3,11},{4,12},{5,13},{6,14},{7,15},{8,0},{9,1},... | collective-permute-start | bytes 196616 | tf_op jit(solution)/shard_map/ppermute | solution.py:638
  59.9 5.2 %collective-permute-start.15 = (f32[2,64,128]{2,1,0:T(8,128)S(1)}, f32[2,64,128]{2,1,0:T(8,128)S(1)}, u32[]{:S(2)}, u32[]{:S(2)}) collective-permute-start(f32[2,64,128]{2,1,0:T(8,128)S(1)} %add_kernel.1.mine), channel_id=1, source_target_pairs={{0,16},{1,17},{2,18},{3,19},{4,20},{5,21},{6,22},{7,23},{8,24},{9,... | collective-permute-start | bytes 196616 | tf_op jit(solution)/shard_map/ppermute | solution.py:638
  65.3 4.6 %collective-permute-start.16 = (f32[136,128]{1,0:T(8,128)S(1)}, f32[136,128]{1,0:T(8,128)S(1)}, u32[]{:S(2)}, u32[]{:S(2)}) collective-permute-start(f32[136,128]{1,0:T(8,128)S(1)} %get-tuple-element.54.mine), channel_id=1, source_target_pairs={{0,8},{1,9},{2,10},{3,11},{4,12},{5,13},{6,14},{7,15},{8,0},{9,1},... | collective-permute-start | bytes 208904 | tf_op jit(solution)/shard_map/ppermute | solution.py:638
  66.9 1.2 %collective-permute-start.17 = (f32[8,128]{1,0:T(8,128)S(1)}, f32[8,128]{1,0:T(8,128)S(1)}, u32[]{:S(2)}, u32[]{:S(2)}) collective-permute-start(f32[8,128]{1,0:T(8,128)S(1)} %get-tuple-element.55.s0), channel_id=1, source_target_pairs={{0,1},{1,0},{2,3},{3,2},{4,5},{5,4},{6,7},{7,6},{8,9},{9,8},{10,11... | collective-permute-start | bytes 12296 | tf_op jit(solution)/shard_map/ppermute | solution.py:638
  66.9 3.0 %collective-permute-start.18 = (f32[8,128]{1,0:T(8,128)S(1)}, f32[8,128]{1,0:T(8,128)S(1)}, u32[]{:S(2)}, u32[]{:S(2)}) collective-permute-start(f32[8,128]{1,0:T(8,128)S(1)} %get-tuple-element.55.s0), channel_id=1, source_target_pairs={{0,9},{1,8},{2,11},{3,10},{4,13},{5,12},{6,15},{7,14},{8,1},{9,0},... | collective-permute-start | bytes 12296 | tf_op jit(solution)/shard_map/ppermute | solution.py:638
  69.9 6.8 %collective-permute-start.19 = (f32[264,128]{1,0:T(8,128)S(1)}, f32[264,128]{1,0:T(8,128)S(1)}, u32[]{:S(2)}, u32[]{:S(2)}) collective-permute-start(f32[264,128]{1,0:T(8,128)S(1)} %get-tuple-element.56.mine), channel_id=1, source_target_pairs={{0,4},{1,5},{2,6},{3,7},{4,0},{5,1},{6,2},{7,3},{8,12},{9,13},{10,... | collective-permute-start | bytes 405512 | tf_op jit(solution)/shard_map/ppermute | solution.py:638
  71.4 3.6 %collective-permute-start.20 = (f32[8,128]{1,0:T(8,128)S(1)}, f32[8,128]{1,0:T(8,128)S(1)}, u32[]{:S(2)}, u32[]{:S(2)}) collective-permute-start(f32[8,128]{1,0:T(8,128)S(1)} %get-tuple-element.57.s0), channel_id=1, source_target_pairs={{0,2},{1,3},{2,0},{3,1},{4,6},{5,7},{6,4},{7,5},{8,10},{9,11},{10,... | collective-permute-start | bytes 12296 | tf_op jit(solution)/shard_map/ppermute | solution.py:638
  72.2 4.5 %collective-permute-start.21 = (f32[8,128]{1,0:T(8,128)S(1)}, f32[8,128]{1,0:T(8,128)S(1)}, u32[]{:S(2)}, u32[]{:S(2)}) collective-permute-start(f32[8,128]{1,0:T(8,128)S(1)} %get-tuple-element.57.s0), channel_id=1, source_target_pairs={{0,6},{1,7},{2,4},{3,5},{4,2},{5,3},{6,0},{7,1},{8,14},{9,15},{10,... | collective-permute-start | bytes 12296 | tf_op jit(solution)/shard_map/ppermute | solution.py:638

commit v16 on v13

--- a/solution.py
+++ b/solution.py
@@ -144,34 +144,41 @@
             dst[(*slab, p, pl.ds(i * 8, 8), slice(None))] = value
 
 
-def pick_kernel(across, *refs):
-    count = len(across)
-    fields, outs, (held, sems) = refs[: 2 * count], refs[2 * count : 3 * count], refs[3 * count :]
+def pick_kernel(earlier, adj_next, adj_cur, fwd_prev, fwd_cur, speed, adj_out, adj_own, prev_own, cur_own, held, sems):
     chip = lax.axis_index("chip")
+    planes = adj_own.shape[1]
+    wanted = (
+        (adj_next, 1 - chip, adj_out, (0,)),
+        (adj_cur, 1 - chip, adj_out, (1,)),
+        (adj_next, chip, adj_own, (0,)),
+        (adj_cur, chip, adj_own, (1,)),
+        (fwd_prev, chip, prev_own, ()),
+        (fwd_cur, chip, cur_own, ()),
+    )
     copies = []
-    for n in range(2 * count):
-        shot = 1 - chip if across[n // 2] else chip
-        copies.append(pltpu.make_async_copy(fields[n].at[shot], held.at[n], sems.at[n]))
+    for n, (field, shot, _, _) in enumerate(wanted):
+        copies.append(pltpu.make_async_copy(field.at[shot], held.at[n], sems.at[n]))
         copies[-1].start()
-    for n in range(2 * count):
+    for n, (_, _, out, slab) in enumerate(wanted):
         copies[n].wait()
-        interleave(outs[n // 2], (n % 2,), held.at[n])
-
-
-def pick(*pairs, earlier):
-    plain = functools.partial(pick_kernel, tuple(pair[2] for pair in pairs))
-    fields = [field for pair in pairs for field in pair[:2]]
-    shape = fields[0].shape[1:]
+        interleave(out, slab, held.at[n])
+    tail = cur_own.shape[0] - planes
+    cur_own[planes:] = speed[planes - tail :]
+
+
+def pick(adj_next, adj_cur, fwd_prev, fwd_cur, speed, tail, earlier):
+    planes, *plane = fwd_cur.shape[1:]
     vmem, hbm = pl.BlockSpec(memory_space=pltpu.VMEM), pl.BlockSpec(memory_space=pltpu.HBM)
+    shapes = [(2, planes, *plane), (2, planes, *plane), (planes, *plane), (planes + tail, *plane)]
     return pl.pallas_call(
-        lambda earlier, *refs: plain(*refs),
-        in_specs=[pl.BlockSpec(memory_space=pl.ANY)] + [hbm] * len(fields),
-        out_specs=[vmem] * len(pairs),
-        out_shape=[jax.ShapeDtypeStruct((2, *shape), jnp.float32)] * len(pairs),
-        scratch_shapes=[pltpu.VMEM((len(fields), *shape), jnp.float32), pltpu.SemaphoreType.DMA((len(fields),))],
+        pick_kernel,
+        in_specs=[pl.BlockSpec(memory_space=pl.ANY)] + [hbm] * 4 + [vmem],
+        out_specs=[vmem] * 4,
+        out_shape=[jax.ShapeDtypeStruct(shape, jnp.float32) for shape in shapes],
+        scratch_shapes=[pltpu.VMEM((6, planes, *plane), jnp.float32), pltpu.SemaphoreType.DMA((6,))],
         compiler_params=pltpu.CompilerParams(vmem_limit_bytes=4 * 2**20),
         name="pick",
-    )(earlier, *fields)
+    )(earlier, adj_next, adj_cur, fwd_prev, fwd_cur, speed)
 
 
 def first_kernel(first, second, courant, outgoing, whole, piece, held, held_courant, sems):
@@ -370,10 +377,10 @@
 
 
 def forward_kernel(
-    start, sources, own, mate, over0, over1, far0, far1, c0, c1, c2, c3, placed, laps, history, held, cour, last,
+    start, sources, own0, own1, mate0, mate1, over0, over1, far0, far1, speed, speed_mate, placed, laps, history, held, cour, last,
     even, odd, banded, y0, y1, sems, sems_even, sems_odd
 ):
-    planes, rows, lanes = c0.shape
+    planes, rows, lanes = own0.shape
     steps = laps.shape[0]
     groups = rows // 8
     chip_here, core, slabs = place(planes)
@@ -391,10 +398,12 @@
             yield pltpu.make_async_copy(source, history.at[k, pl.ds(n * planes, planes)], done.at[n])
 
     banded[...] = band(lanes)
-    load_blocks(slabs, (own, mate, (over0, over1), (far0, far1)), odd, even)
-    for slab, block in zip(slabs, (c0, c1, c2, c3)):
+    load_blocks(slabs, ((own0, own1), (mate0, mate1), (over0, over1), (far0, far1)), odd, even)
+    head = speed.shape[0] - planes
+    for here, across, first, rest in ((slabs[0], slabs[2], speed, own1), (slabs[1], slabs[3], speed_mate, mate1)):
         for p in range(planes):
-            cour[slab + p] = block[p]
+            cour[across + p] = first[p]
+            cour[here + p] = first[planes + p] if p < head else rest[planes + p - head]
 
     for index in range(2 * planes):
         z = (2 * (index // planes) + core) * planes + index % planes
@@ -552,11 +561,12 @@
     return results[0] if parts == 1 else results
 
 
-def arrange_kernel(mine, other, out):
+def arrange_kernel(own, mine, other, out):
     y = lax.axis_index("shot") % 2
-    count = mine.shape[0]
+    count, planes = mine.shape[0], own.shape[0]
     out[pl.ds(y * count, count)] = mine[...]
     out[pl.ds((1 - y) * count, count)] = other[...]
+    out[planes:] = own[0 : out.shape[0] - planes]
 
 
 def first_plane(shot, planes):
@@ -671,13 +681,12 @@
     placed = placed.reshape(steps + 1, planes_all, rows_x, rows_y)
 
     piece = after(mark, piece)
-    adj_outgoing, adj_own, own = pick(
-        (adj_next, adj_cur, True), (adj_next, adj_cur, False), (fwd_prev, fwd_cur, False), earlier=piece
-    )
-    mate = exchange(own, CORE)
-    c2 = local(arrange_kernel, [courant_sq.shape], piece, exchange(piece, Y))
-    c1, c3 = exchange(c0, CORE), exchange(c2, CORE)
-    over = after(c2, over, parts=2)
+    head = planes * 5 // 8
+    adj_outgoing, adj_own, *own = pick(adj_next, adj_cur, fwd_prev, fwd_cur, c0, planes - head, piece)
+    mate = [exchange(field, CORE) for field in own]
+    speed = local(arrange_kernel, [(planes + head, rows_x, rows_y)], c0, piece, exchange(piece, Y))
+    speed_mate = exchange(speed, CORE)
+    over = after(speed, over, parts=2)
     far = [exchange(field, CORE) for field in over]
     adj_over = exchange(adj_outgoing, CHIP)
     adj_mate = exchange(adj_own, CORE)
@@ -704,10 +713,10 @@
             pltpu.SemaphoreType.DMA((4,)),
             pltpu.SemaphoreType.DMA((4,)),
         ],
-        compiler_params=pltpu.CompilerParams(vmem_limit_bytes=25 * 2**20),
+        compiler_params=pltpu.CompilerParams(vmem_limit_bytes=21 * 2**20),
         cost_estimate=pl.CostEstimate(flops=1000, bytes_accessed=1000, transcendentals=0),
         name="forward_steps",
-    )(ckpt_step[None], src_cells, own, mate, *over, *far, c0, c1, c2, c3, placed)
+    )(ckpt_step[None], src_cells, *own, *mate, *over, *far, speed, speed_mate, placed)
 
     adj_over = after(laps, adj_over)
     adj_far = exchange(adj_over, CORE)

time: 78.6 us -> 75.3 us (0.958)
  waiting for transfers between devices: 21.8 us -> 19.1 us
    ppermute x22, waiting for transfers between devices: 21.8 us -> 19.1 us  [exchange(): lax.ppermute(value, axes, [(i, i ^ bits) for i in range(lax.axis_size(axe...]
  transfers between devices with their start and end apart: 22 -> 22, of which waited for: 13 -> 13; matrix products, arithmetic and copies ran while one was open for 0% -> 0% of each run, Pallas kernels for 28% -> 29%
where the time goes in v16:
time: 75.3 us; the launch traced here: 75.1 us
  Pallas kernels  32.2 us (43%)
  starting transfers between devices  21.6 us (29%)
  waiting for transfers between devices  19.1 us (25%)
  between operations  1.44 us (2%)
    ppermute x22, starting transfers between devices, exchange(): lax.ppermute(value, axes, [(i, i ^ bits) for i in range(lax.axis_size(axe...  21.6 us
    ppermute x22, waiting for transfers between devices, exchange(): lax.ppermute(value, axes, [(i, i ^ bits) for i in range(lax.axis_size(axe...  19.1 us
    pallas_call x1, Pallas kernels, whole_shards(): pl.pallas_call(forward_kernel, in_specs=[smem, smem] + [vmem] * 10 + [pl....  9.7 us
    pallas_call x1, Pallas kernels, scatter(): pl.pallas_call(functools.partial(scatter_kernel, rows_x), grid=(rows_all...  9.27 us
    pallas_call x1, Pallas kernels, whole_shards(): pl.pallas_call(adjoint_kernel, in_specs=[vmem] * 8, out_specs=[vmem] * 4,...  6.99 us
    pallas_call x1, Pallas kernels, whole_shards(): pl.pallas_call(first_kernel, in_specs=[hbm] * 3, out_specs=[vmem] * 3, ou...  2.13 us
  transfers between devices with their start and end apart: 22, of which 13 were waited for; matrix products, arithmetic and copies ran while one was open for 0% of the time, Pallas kernels for 29%

profile of v16, /device:TPU:0, one launch (start us, length us, event | category | flops | bytes accessed | tf_op | source)
XLA Modules:
  0.0 75.1 jit_solution(9532647020202516885)
XLA Ops:
  0.6 2.1 %first_to_cross.1 = (f32[2,8,64,128]{3,2,1,0:T(8,128)}, f32[8,64,128]{2,1,0:T(8,128)}, f32[4,64,128]{2,1,0:T(8,128)}) custom-call(f32[2,8,64,128]{3,2,1,0:T(8,128)} %fwd_prev.1, f32[2,8,64,128]{3,2,1,0:T(8,128)} %fwd_cur.1, f32[8,64,128]{2,1,0:T(8,128)} %courant.1), custom_call_target="tpu_custom_call" | custom-call | tf_op jit(solution)/shard_map/first_to_cross/pallas_call | solution.py:659
  2.8 3.0 %collective-permute-start = (f32[4,64,128]{2,1,0:T(8,128)}, f32[4,64,128]{2,1,0:T(8,128)S(1)}, u32[]{:S(2)}, u32[]{:S(2)}) collective-permute-start(f32[4,64,128]{2,1,0:T(8,128)} %get-tuple-element.31), channel_id=1, source_target_pairs={{0,2},{1,3},{2,0},{3,1},{4,6},{5,7},{6,4},{7,5},{8,10},{9,11},{10,... | collective-permute-start | bytes 393224 | tf_op jit(solution)/shard_map/ppermute | solution.py:643
  5.8 0.0 copy-start
  5.8 0.0 copy-start.5
  5.8 0.0 copy-start.7
  5.8 0.1 collective-permute-start.5
  5.9 9.3 %receiver_scatter.1 = (f32[9,2048,128]{2,1,0:T(8,128)}, f32[8,128]{1,0:T(8,128)}) custom-call(s32[2,512]{1,0:T(2,128)} %cells_ref.1, f32[2,8,512]{2,1,0:T(8,128)} %observed_ref.1), custom_call_target="tpu_custom_call" | custom-call | flops 4831838208 | bytes 9437184 | tf_op jit(solution)/shard_map/receiver_scatter/pallas_call | solution.py:305
  15.2 0.0 collective-permute-done.value
  15.2 0.7 copy-done.6
  15.9 2.0 %collective-permute-start.4 = (f32[4,64,128]{2,1,0:T(8,128)S(1)}, f32[4,64,128]{2,1,0:T(8,128)S(1)}, u32[]{:S(2)}, u32[]{:S(2)}) collective-permute-start(f32[4,64,128]{2,1,0:T(8,128)S(1)} %after.3.earlier.mine), channel_id=1, source_target_pairs={{0,4},{1,5},{2,6},{3,7},{4,0},{5,1},{6,2},{7,3},{8,12},{9,13},{10,... | collective-permute-start | bytes 393224 | tf_op jit(solution)/shard_map/ppermute | solution.py:643
  17.9 0.0 copy-done
  17.9 0.0 copy-done.1
  17.9 0.0 copy-done.3
  17.9 0.0 copy-done.4
  17.9 0.0 copy-done.5
  17.9 1.4 %pick.1 = (f32[2,8,64,128]{3,2,1,0:T(8,128)}, f32[2,8,64,128]{3,2,1,0:T(8,128)S(1)}, f32[8,64,128]{2,1,0:T(8,128)S(1)}, f32[11,64,128]{2,1,0:T(8,128)S(1)}) custom-call(f32[4,64,128]{2,1,0:T(8,128)S(1)} %after.3.earlier.mine, f32[2,8,64,128]{3,2,1,0:T(8,128)S(1)} %copy-done.4, f32[2,8,64,128]{3,2,1,0:T(8,128)S(1)} %copy-done.5, ...), custom_call_target="tpu_custom_call" | custom-call | tf_op jit(solution)/shard_map/pick/pallas_call | solution.py:173
  19.3 0.1 collective-permute-start.2
  19.4 1.5 %collective-permute-start.9 = (f32[2,8,64,128]{3,2,1,0:T(8,128)}, f32[2,8,64,128]{3,2,1,0:T(8,128)S(1)}, u32[]{:S(2)}, u32[]{:S(2)}) collective-permute-start(f32[2,8,64,128]{3,2,1,0:T(8,128)} %get-tuple-element.41), channel_id=1, source_target_pairs={{0,2},{1,3},{2,0},{3,1},{4,6},{5,7},{6,4},{7,5},{8,10},{9,11},{10,... | collective-permute-start | bytes 1572872 | tf_op jit(solution)/shard_map/ppermute | solution.py:643
  20.8 0.1 collective-permute-done.4.other
  21.0 0.1 collective-permute-start.8
  21.1 0.4 collective-permute-start.3
  21.6 0.0 collective-permute-done.5.value
  21.6 0.7 after.4
  22.3 0.1 collective-permute-start.6
  22.4 0.0 collective-permute-done.2.mate0
  22.4 0.4 collective-permute-start.7
  23.5 0.0 collective-permute-done.3.mate1
  23.5 0.1 collective-permute-start.1
  23.6 0.0 collective-permute-done.8.speed_mate
  23.6 0.3 collective-permute-done.6.far0
  24.0 0.6 collective-permute-done.7.far1
  24.6 0.0 copy-done.7
  24.6 9.7 %forward_steps.1 = (f32[8,8,2,64,128]{4,3,2,1,0:T(8,128)S(1)}, f32[8,32,64,128]{3,2,1,0:T(8,128)S(1)}, f32[9,32,64,128]{3,2,1,0:T(8,128)S(1)}, f32[32,64,128]{2,1,0:T(8,128)S(1)}, f32[16,64,128]{2,1,0:T(8,128)S(1)}) custom-call(s32[1]{0:T(128)} %bitcast.3.start, s32[2]{0:T(128)S(1)} %copy-done.7, f32[8,64,128]{2,1,0:T(8,128)S(1)} %get-tuple-element.34.own0, ...), custom_call_target="tpu_custom_call" | custom-call | flops 1000 | bytes 1000 | tf_op jit(solution)/shard_map/forward_steps/pallas_call | solution.py:699
  34.3 0.0 collective-permute-done.9.value
  34.3 0.2 collective-permute-start.10
  34.5 1.0 %inject.1 = f32[8,32,64,128]{3,2,1,0:T(8,128)S(1)} custom-call(f32[9,32,64,128]{3,2,1,0:T(8,128)S(1)} %get-tuple-element.43.held, f32[8,32,64,128]{3,2,1,0:T(8,128)S(1)} %get-tuple-element.44.history), custom_call_target="tpu_custom_call" | custom-call | tf_op jit(solution)/shard_map/inject/pallas_call | solution.py:723
  35.5 0.0 collective-permute-done.1.mate
  35.5 0.8 %collective-permute-done.10.far = f32[2,8,64,128]{3,2,1,0:T(8,128)S(1)} collective-permute-done((f32[2,8,64,128]{3,2,1,0:T(8,128)S(1)}, f32[2,8,64,128]{3,2,1,0:T(8,128)S(1)}, u32[]{:S(2)}, u32[]{:S(2)}) %collective-permute-start.10) | collective-permute-done | bytes 524320 | tf_op jit(solution)/shard_map/ppermute | solution.py:643
  36.3 7.0 %adjoint_steps.1 = (f32[4,64,128]{2,1,0:T(8,128)S(1)}, f32[4,64,128]{2,1,0:T(8,128)S(1)}, f32[4,64,128]{2,1,0:T(8,128)S(1)}, f32[4,64,128]{2,1,0:T(8,128)S(1)}) custom-call(f32[2,8,64,128]{3,2,1,0:T(8,128)S(1)} %get-tuple-element.33.own, f32[2,8,64,128]{3,2,1,0:T(8,128)S(1)} %collective-permute-done.1.mate, f32[2,8,64,128]{3,2,1,0:T(8,128)S(1)} %after.5.over, ...), custom_call_target="tpu_custom_call" | custom-call | flops 62914560 | bytes 33554432 | tf_op jit(solution)/shard_map/adjoint_steps/pallas_call | solution.py:733
  43.3 2.8 %collective-permute-start.11 = (f32[4,64,128]{2,1,0:T(8,128)S(1)}, f32[4,64,128]{2,1,0:T(8,128)S(1)}, u32[]{:S(2)}, u32[]{:S(2)}) collective-permute-start(f32[4,64,128]{2,1,0:T(8,128)S(1)} %get-tuple-element.47), channel_id=1, source_target_pairs={{0,6},{1,7},{2,4},{3,5},{4,2},{5,3},{6,0},{7,1},{8,14},{9,15},{10,... | collective-permute-start | bytes 393224 | tf_op jit(solution)/shard_map/ppermute | solution.py:643
  46.1 0.5 collective-permute-start.12
  46.6 0.2 collective-permute-start.13
  46.9 3.2 %collective-permute-done.11.by_xy = f32[4,64,128]{2,1,0:T(8,128)S(1)} collective-permute-done((f32[4,64,128]{2,1,0:T(8,128)S(1)}, f32[4,64,128]{2,1,0:T(8,128)S(1)}, u32[]{:S(2)}, u32[]{:S(2)}) %collective-permute-start.11) | collective-permute-done | bytes 131104 | tf_op jit(solution)/shard_map/ppermute | solution.py:643
  50.0 2.7 %collective-permute-done.12.by_y = f32[4,64,128]{2,1,0:T(8,128)S(1)} collective-permute-done((f32[4,64,128]{2,1,0:T(8,128)S(1)}, f32[4,64,128]{2,1,0:T(8,128)S(1)}, u32[]{:S(2)}, u32[]{:S(2)}) %collective-permute-start.12) | collective-permute-done | bytes 131104 | tf_op jit(solution)/shard_map/ppermute | solution.py:643
  52.7 0.4 collective-permute-done.13.by_x
  53.1 1.6 %collective-permute-start.14 = (f32[2,64,128]{2,1,0:T(8,128)S(1)}, f32[2,64,128]{2,1,0:T(8,128)S(1)}, u32[]{:S(2)}, u32[]{:S(2)}) collective-permute-start(f32[2,64,128]{2,1,0:T(8,128)S(1)} %get-tuple-element.51), channel_id=1, source_target_pairs={{0,8},{1,9},{2,10},{3,11},{4,12},{5,13},{6,14},{7,15},{8,0},{9,1},... | collective-permute-start | bytes 196616 | tf_op jit(solution)/shard_map/ppermute | solution.py:643
  54.8 2.7 %collective-permute-done.14.other = f32[2,64,128]{2,1,0:T(8,128)S(1)} collective-permute-done((f32[2,64,128]{2,1,0:T(8,128)S(1)}, f32[2,64,128]{2,1,0:T(8,128)S(1)}, u32[]{:S(2)}, u32[]{:S(2)}) %collective-permute-start.14) | collective-permute-done | bytes 65568 | tf_op jit(solution)/shard_map/ppermute | solution.py:643
  57.5 2.7 %collective-permute-start.15 = (f32[2,64,128]{2,1,0:T(8,128)S(1)}, f32[2,64,128]{2,1,0:T(8,128)S(1)}, u32[]{:S(2)}, u32[]{:S(2)}) collective-permute-start(f32[2,64,128]{2,1,0:T(8,128)S(1)} %add_kernel.1.mine), channel_id=1, source_target_pairs={{0,16},{1,17},{2,18},{3,19},{4,20},{5,21},{6,22},{7,23},{8,24},{9,... | collective-permute-start | bytes 196616 | tf_op jit(solution)/shard_map/ppermute | solution.py:643
  60.1 2.6 %collective-permute-done.15.other = f32[2,64,128]{2,1,0:T(8,128)S(1)} collective-permute-done((f32[2,64,128]{2,1,0:T(8,128)S(1)}, f32[2,64,128]{2,1,0:T(8,128)S(1)}, u32[]{:S(2)}, u32[]{:S(2)}) %collective-permute-start.15) | collective-permute-done | bytes 65568 | tf_op jit(solution)/shard_map/ppermute | solution.py:643
  62.7 0.0 copy-done.2
  62.7 0.1 sums_kernel.1
  62.8 1.6 %collective-permute-start.16 = (f32[136,128]{1,0:T(8,128)S(1)}, f32[136,128]{1,0:T(8,128)S(1)}, u32[]{:S(2)}, u32[]{:S(2)}) collective-permute-start(f32[136,128]{1,0:T(8,128)S(1)} %get-tuple-element.52.mine), channel_id=1, source_target_pairs={{0,8},{1,9},{2,10},{3,11},{4,12},{5,13},{6,14},{7,15},{8,0},{9,1},... | collective-permute-start | bytes 208904 | tf_op jit(solution)/shard_map/ppermute | solution.py:643
  64.4 0.0 collective-permute-start.17
  64.4 0.6 collective-permute-start.18
  65.0 0.6 collective-permute-done.17.s1
  65.6 1.9 %collective-permute-done.18.s2 = f32[8,128]{1,0:T(8,128)S(1)} collective-permute-done((f32[8,128]{1,0:T(8,128)S(1)}, f32[8,128]{1,0:T(8,128)S(1)}, u32[]{:S(2)}, u32[]{:S(2)}) %collective-permute-start.18) | collective-permute-done | bytes 4128 | tf_op jit(solution)/shard_map/ppermute | solution.py:643
  67.5 0.0 collective-permute-done.16.other
  67.5 1.5 %collective-permute-start.19 = (f32[264,128]{1,0:T(8,128)S(1)}, f32[264,128]{1,0:T(8,128)S(1)}, u32[]{:S(2)}, u32[]{:S(2)}) collective-permute-start(f32[264,128]{1,0:T(8,128)S(1)} %get-tuple-element.54.mine), channel_id=1, source_target_pairs={{0,4},{1,5},{2,6},{3,7},{4,0},{5,1},{6,2},{7,3},{8,12},{9,13},{10,... | collective-permute-start | bytes 405512 | tf_op jit(solution)/shard_map/ppermute | solution.py:643
  69.0 0.8 %collective-permute-start.20 = (f32[8,128]{1,0:T(8,128)S(1)}, f32[8,128]{1,0:T(8,128)S(1)}, u32[]{:S(2)}, u32[]{:S(2)}) collective-permute-start(f32[8,128]{1,0:T(8,128)S(1)} %get-tuple-element.55.s0), channel_id=1, source_target_pairs={{0,2},{1,3},{2,0},{3,1},{4,6},{5,7},{6,4},{7,5},{8,10},{9,11},{10,... | collective-permute-start | bytes 12296 | tf_op jit(solution)/shard_map/ppermute | solution.py:643
  69.8 1.3 %collective-permute-start.21 = (f32[8,128]{1,0:T(8,128)S(1)}, f32[8,128]{1,0:T(8,128)S(1)}, u32[]{:S(2)}, u32[]{:S(2)}) collective-permute-start(f32[8,128]{1,0:T(8,128)S(1)} %get-tuple-element.55.s0), channel_id=1, source_target_pairs={{0,6},{1,7},{2,4},{3,5},{4,2},{5,3},{6,0},{7,1},{8,14},{9,15},{10,... | collective-permute-start | bytes 12296 | tf_op jit(solution)/shard_map/ppermute | solution.py:643
  71.0 1.5 %collective-permute-done.20.s1 = f32[8,128]{1,0:T(8,128)S(1)} collective-permute-done((f32[8,128]{1,0:T(8,128)S(1)}, f32[8,128]{1,0:T(8,128)S(1)}, u32[]{:S(2)}, u32[]{:S(2)}) %collective-permute-start.20) | collective-permute-done | bytes 4128 | tf_op jit(solution)/shard_map/ppermute | solution.py:643
  72.6 1.7 %collective-permute-done.21.s2 = f32[8,128]{1,0:T(8,128)S(1)} collective-permute-done((f32[8,128]{1,0:T(8,128)S(1)}, f32[8,128]{1,0:T(8,128)S(1)}, u32[]{:S(2)}, u32[]{:S(2)}) %collective-permute-start.21) | collective-permute-done | bytes 4128 | tf_op jit(solution)/shard_map/ppermute | solution.py:643
  74.3 0.0 collective-permute-done.19.other
  74.3 0.8 %finish.1 = (f32[8,64,128]{2,1,0:T(8,128)}, f32[1]{0:T(128)}) custom-call(f32[264,128]{1,0:T(8,128)S(1)} %get-tuple-element.54.mine, f32[264,128]{1,0:T(8,128)S(1)} %collective-permute-done.19.other, f32[8,64,128]{2,1,0:T(8,128)S(1)} %copy-done.2, f32[8,128]{1,0:T(8,128)S(1)} %get-tuple-element.55.s0, f32[8,128]{1,0:T(8,128)S(1)} %collective-permute-done.20.s1, ...), custom_call_target="tpu_custom_call" | custom-call | tf_op jit(solution)/shard_map/finish/pallas_call | solution.py:755
  (11 shorter events, 0.2 us)
Async XLA Ops:
  2.8 12.4 %collective-permute-start = (f32[4,64,128]{2,1,0:T(8,128)}, f32[4,64,128]{2,1,0:T(8,128)S(1)}, u32[]{:S(2)}, u32[]{:S(2)}) collective-permute-start(f32[4,64,128]{2,1,0:T(8,128)} %get-tuple-element.31), channel_id=1, source_target_pairs={{0,2},{1,3},{2,0},{3,1},{4,6},{5,7},{6,4},{7,5},{8,10},{9,11},{10,... | collective-permute-start | bytes 393224 | tf_op jit(solution)/shard_map/ppermute | solution.py:643
  5.8 12.1 %copy-start = (f32[2,8,64,128]{3,2,1,0:T(8,128)S(1)}, f32[2,8,64,128]{3,2,1,0:T(8,128)}, u32[]{:S(2)}) copy-start(f32[2,8,64,128]{3,2,1,0:T(8,128)} %fwd_prev.1) | copy-start | bytes 1572868
  5.8 12.1 %copy-start.1 = (f32[2,8,64,128]{3,2,1,0:T(8,128)S(1)}, f32[2,8,64,128]{3,2,1,0:T(8,128)}, u32[]{:S(2)}) copy-start(f32[2,8,64,128]{3,2,1,0:T(8,128)} %fwd_cur.1) | copy-start | bytes 1572868
  5.8 12.1 %copy-start.3 = (f32[8,64,128]{2,1,0:T(8,128)S(1)}, f32[8,64,128]{2,1,0:T(8,128)}, u32[]{:S(2)}) copy-start(f32[8,64,128]{2,1,0:T(8,128)} %get-tuple-element.32.speed.own) | copy-start | bytes 786436
  5.8 12.1 %copy-start.4 = (f32[2,8,64,128]{3,2,1,0:T(8,128)S(1)}, f32[2,8,64,128]{3,2,1,0:T(8,128)}, u32[]{:S(2)}) copy-start(f32[2,8,64,128]{3,2,1,0:T(8,128)} %adj_next.1) | copy-start | bytes 1572868
  5.8 12.1 %copy-start.5 = (f32[2,8,64,128]{3,2,1,0:T(8,128)S(1)}, f32[2,8,64,128]{3,2,1,0:T(8,128)}, u32[]{:S(2)}) copy-start(f32[2,8,64,128]{3,2,1,0:T(8,128)} %adj_cur.1) | copy-start | bytes 1572868
  5.8 18.8 %copy-start.7 = (s32[2]{0:T(128)S(1)}, s32[2]{0:T(128)}, u32[]{:S(2)}) copy-start(s32[2]{0:T(128)} %sources.1) | copy-start | bytes 28
  5.8 15.8 %collective-permute-start.5 = (f32[2,8,64,128]{3,2,1,0:T(8,128)}, f32[2,8,64,128]{3,2,1,0:T(8,128)S(1)}, u32[]{:S(2)}, u32[]{:S(2)}) collective-permute-start(f32[2,8,64,128]{3,2,1,0:T(8,128)} %get-tuple-element.36), channel_id=1, source_target_pairs={{0,2},{1,3},{2,0},{3,1},{4,6},{5,7},{6,4},{7,5},{8,10},{9,11},{10,... | collective-permute-start | bytes 1572872 | tf_op jit(solution)/shard_map/ppermute | solution.py:643
  15.2 0.7 copy-start.6
  15.9 5.0 %collective-permute-start.4 = (f32[4,64,128]{2,1,0:T(8,128)S(1)}, f32[4,64,128]{2,1,0:T(8,128)S(1)}, u32[]{:S(2)}, u32[]{:S(2)}) collective-permute-start(f32[4,64,128]{2,1,0:T(8,128)S(1)} %after.3.earlier.mine), channel_id=1, source_target_pairs={{0,4},{1,5},{2,6},{3,7},{4,0},{5,1},{6,2},{7,3},{8,12},{9,13},{10,... | collective-permute-start | bytes 393224 | tf_op jit(solution)/shard_map/ppermute | solution.py:643
  19.3 3.1 %collective-permute-start.2 = (f32[8,64,128]{2,1,0:T(8,128)S(1)}, f32[8,64,128]{2,1,0:T(8,128)S(1)}, u32[]{:S(2)}, u32[]{:S(2)}) collective-permute-start(f32[8,64,128]{2,1,0:T(8,128)S(1)} %get-tuple-element.34.own0), channel_id=1, source_target_pairs={{0,1},{1,0},{2,3},{3,2},{4,5},{5,4},{6,7},{7,6},{8,9},{9,8},{10,11... | collective-permute-start | bytes 786440 | tf_op jit(solution)/shard_map/ppermute | solution.py:643
  19.4 14.9 %collective-permute-start.9 = (f32[2,8,64,128]{3,2,1,0:T(8,128)}, f32[2,8,64,128]{3,2,1,0:T(8,128)S(1)}, u32[]{:S(2)}, u32[]{:S(2)}) collective-permute-start(f32[2,8,64,128]{3,2,1,0:T(8,128)} %get-tuple-element.41), channel_id=1, source_target_pairs={{0,2},{1,3},{2,0},{3,1},{4,6},{5,7},{6,4},{7,5},{8,10},{9,11},{10,... | collective-permute-start | bytes 1572872 | tf_op jit(solution)/shard_map/ppermute | solution.py:643
  21.0 2.6 %collective-permute-start.8 = (f32[13,64,128]{2,1,0:T(8,128)S(1)}, f32[13,64,128]{2,1,0:T(8,128)S(1)}, u32[]{:S(2)}, u32[]{:S(2)}) collective-permute-start(f32[13,64,128]{2,1,0:T(8,128)S(1)} %arrange_kernel.1.earlier.speed), channel_id=1, source_target_pairs={{0,1},{1,0},{2,3},{3,2},{4,5},{5,4},{6,7},{7,6},{8,9},{9,8},{10,11... | collective-permute-start | bytes 1277960 | tf_op jit(solution)/shard_map/ppermute | solution.py:643
  21.1 2.3 %collective-permute-start.3 = (f32[11,64,128]{2,1,0:T(8,128)S(1)}, f32[11,64,128]{2,1,0:T(8,128)S(1)}, u32[]{:S(2)}, u32[]{:S(2)}) collective-permute-start(f32[11,64,128]{2,1,0:T(8,128)S(1)} %get-tuple-element.35.own1), channel_id=1, source_target_pairs={{0,1},{1,0},{2,3},{3,2},{4,5},{5,4},{6,7},{7,6},{8,9},{9,8},{10,11... | collective-permute-start | bytes 1081352 | tf_op jit(solution)/shard_map/ppermute | solution.py:643
  22.3 1.7 %collective-permute-start.6 = (f32[8,64,128]{2,1,0:T(8,128)S(1)}, f32[8,64,128]{2,1,0:T(8,128)}, u32[]{:S(2)}, u32[]{:S(2)}) collective-permute-start(f32[8,64,128]{2,1,0:T(8,128)S(1)} %get-tuple-element.37.over0), channel_id=1, source_target_pairs={{0,1},{1,0},{2,3},{3,2},{4,5},{5,4},{6,7},{7,6},{8,9},{9,8},{10,11... | collective-permute-start | bytes 786440 | tf_op jit(solution)/shard_map/ppermute | solution.py:643
  22.4 2.2 %collective-permute-start.7 = (f32[8,64,128]{2,1,0:T(8,128)}, f32[8,64,128]{2,1,0:T(8,128)}, u32[]{:S(2)}, u32[]{:S(2)}) collective-permute-start(f32[8,64,128]{2,1,0:T(8,128)} %get-tuple-element.38.over1), channel_id=1, source_target_pairs={{0,1},{1,0},{2,3},{3,2},{4,5},{5,4},{6,7},{7,6},{8,9},{9,8},{10,11... | collective-permute-start | bytes 786440 | tf_op jit(solution)/shard_map/ppermute | solution.py:643
  23.5 12.0 %collective-permute-start.1 = (f32[2,8,64,128]{3,2,1,0:T(8,128)S(1)}, f32[2,8,64,128]{3,2,1,0:T(8,128)S(1)}, u32[]{:S(2)}, u32[]{:S(2)}) collective-permute-start(f32[2,8,64,128]{3,2,1,0:T(8,128)S(1)} %get-tuple-element.33.own), channel_id=1, source_target_pairs={{0,1},{1,0},{2,3},{3,2},{4,5},{5,4},{6,7},{7,6},{8,9},{9,8},{10,11... | collective-permute-start | bytes 1572872 | tf_op jit(solution)/shard_map/ppermute | solution.py:643
  34.3 2.0 %collective-permute-start.10 = (f32[2,8,64,128]{3,2,1,0:T(8,128)S(1)}, f32[2,8,64,128]{3,2,1,0:T(8,128)S(1)}, u32[]{:S(2)}, u32[]{:S(2)}) collective-permute-start(f32[2,8,64,128]{3,2,1,0:T(8,128)S(1)} %after.5.over), channel_id=1, source_target_pairs={{0,1},{1,0},{2,3},{3,2},{4,5},{5,4},{6,7},{7,6},{8,9},{9,8},{10,11... | collective-permute-start | bytes 1572872 | tf_op jit(solution)/shard_map/ppermute | solution.py:643
  36.3 26.4 %copy-start.2 = (f32[8,64,128]{2,1,0:T(8,128)S(1)}, f32[8,64,128]{2,1,0:T(8,128)}, u32[]{:S(2)}) copy-start(f32[8,64,128]{2,1,0:T(8,128)} %momentum.3) | copy-start | bytes 786436
  43.3 6.7 %collective-permute-start.11 = (f32[4,64,128]{2,1,0:T(8,128)S(1)}, f32[4,64,128]{2,1,0:T(8,128)S(1)}, u32[]{:S(2)}, u32[]{:S(2)}) collective-permute-start(f32[4,64,128]{2,1,0:T(8,128)S(1)} %get-tuple-element.47), channel_id=1, source_target_pairs={{0,6},{1,7},{2,4},{3,5},{4,2},{5,3},{6,0},{7,1},{8,14},{9,15},{10,... | collective-permute-start | bytes 393224 | tf_op jit(solution)/shard_map/ppermute | solution.py:643
  46.1 6.6 %collective-permute-start.12 = (f32[4,64,128]{2,1,0:T(8,128)S(1)}, f32[4,64,128]{2,1,0:T(8,128)S(1)}, u32[]{:S(2)}, u32[]{:S(2)}) collective-permute-start(f32[4,64,128]{2,1,0:T(8,128)S(1)} %get-tuple-element.48), channel_id=1, source_target_pairs={{0,4},{1,5},{2,6},{3,7},{4,0},{5,1},{6,2},{7,3},{8,12},{9,13},{10,... | collective-permute-start | bytes 393224 | tf_op jit(solution)/shard_map/ppermute | solution.py:643
  46.6 6.5 %collective-permute-start.13 = (f32[4,64,128]{2,1,0:T(8,128)S(1)}, f32[4,64,128]{2,1,0:T(8,128)S(1)}, u32[]{:S(2)}, u32[]{:S(2)}) collective-permute-start(f32[4,64,128]{2,1,0:T(8,128)S(1)} %get-tuple-element.49), channel_id=1, source_target_pairs={{0,2},{1,3},{2,0},{3,1},{4,6},{5,7},{6,4},{7,5},{8,10},{9,11},{10,... | collective-permute-start | bytes 393224 | tf_op jit(solution)/shard_map/ppermute | solution.py:643
  53.1 4.3 %collective-permute-start.14 = (f32[2,64,128]{2,1,0:T(8,128)S(1)}, f32[2,64,128]{2,1,0:T(8,128)S(1)}, u32[]{:S(2)}, u32[]{:S(2)}) collective-permute-start(f32[2,64,128]{2,1,0:T(8,128)S(1)} %get-tuple-element.51), channel_id=1, source_target_pairs={{0,8},{1,9},{2,10},{3,11},{4,12},{5,13},{6,14},{7,15},{8,0},{9,1},... | collective-permute-start | bytes 196616 | tf_op jit(solution)/shard_map/ppermute | solution.py:643
  57.5 5.2 %collective-permute-start.15 = (f32[2,64,128]{2,1,0:T(8,128)S(1)}, f32[2,64,128]{2,1,0:T(8,128)S(1)}, u32[]{:S(2)}, u32[]{:S(2)}) collective-permute-start(f32[2,64,128]{2,1,0:T(8,128)S(1)} %add_kernel.1.mine), channel_id=1, source_target_pairs={{0,16},{1,17},{2,18},{3,19},{4,20},{5,21},{6,22},{7,23},{8,24},{9,... | collective-permute-start | bytes 196616 | tf_op jit(solution)/shard_map/ppermute | solution.py:643
  62.8 4.6 %collective-permute-start.16 = (f32[136,128]{1,0:T(8,128)S(1)}, f32[136,128]{1,0:T(8,128)S(1)}, u32[]{:S(2)}, u32[]{:S(2)}) collective-permute-start(f32[136,128]{1,0:T(8,128)S(1)} %get-tuple-element.52.mine), channel_id=1, source_target_pairs={{0,8},{1,9},{2,10},{3,11},{4,12},{5,13},{6,14},{7,15},{8,0},{9,1},... | collective-permute-start | bytes 208904 | tf_op jit(solution)/shard_map/ppermute | solution.py:643
  64.4 1.2 %collective-permute-start.17 = (f32[8,128]{1,0:T(8,128)S(1)}, f32[8,128]{1,0:T(8,128)S(1)}, u32[]{:S(2)}, u32[]{:S(2)}) collective-permute-start(f32[8,128]{1,0:T(8,128)S(1)} %get-tuple-element.53.s0), channel_id=1, source_target_pairs={{0,1},{1,0},{2,3},{3,2},{4,5},{5,4},{6,7},{7,6},{8,9},{9,8},{10,11... | collective-permute-start | bytes 12296 | tf_op jit(solution)/shard_map/ppermute | solution.py:643
  64.4 3.0 %collective-permute-start.18 = (f32[8,128]{1,0:T(8,128)S(1)}, f32[8,128]{1,0:T(8,128)S(1)}, u32[]{:S(2)}, u32[]{:S(2)}) collective-permute-start(f32[8,128]{1,0:T(8,128)S(1)} %get-tuple-element.53.s0), channel_id=1, source_target_pairs={{0,9},{1,8},{2,11},{3,10},{4,13},{5,12},{6,15},{7,14},{8,1},{9,0},... | collective-permute-start | bytes 12296 | tf_op jit(solution)/shard_map/ppermute | solution.py:643
  67.5 6.8 %collective-permute-start.19 = (f32[264,128]{1,0:T(8,128)S(1)}, f32[264,128]{1,0:T(8,128)S(1)}, u32[]{:S(2)}, u32[]{:S(2)}) collective-permute-start(f32[264,128]{1,0:T(8,128)S(1)} %get-tuple-element.54.mine), channel_id=1, source_target_pairs={{0,4},{1,5},{2,6},{3,7},{4,0},{5,1},{6,2},{7,3},{8,12},{9,13},{10,... | collective-permute-start | bytes 405512 | tf_op jit(solution)/shard_map/ppermute | solution.py:643
  69.0 3.6 %collective-permute-start.20 = (f32[8,128]{1,0:T(8,128)S(1)}, f32[8,128]{1,0:T(8,128)S(1)}, u32[]{:S(2)}, u32[]{:S(2)}) collective-permute-start(f32[8,128]{1,0:T(8,128)S(1)} %get-tuple-element.55.s0), channel_id=1, source_target_pairs={{0,2},{1,3},{2,0},{3,1},{4,6},{5,7},{6,4},{7,5},{8,10},{9,11},{10,... | collective-permute-start | bytes 12296 | tf_op jit(solution)/shard_map/ppermute | solution.py:643
  69.8 4.5 %collective-permute-start.21 = (f32[8,128]{1,0:T(8,128)S(1)}, f32[8,128]{1,0:T(8,128)S(1)}, u32[]{:S(2)}, u32[]{:S(2)}) collective-permute-start(f32[8,128]{1,0:T(8,128)S(1)} %get-tuple-element.55.s0), channel_id=1, source_target_pairs={{0,6},{1,7},{2,4},{3,5},{4,2},{5,3},{6,0},{7,1},{8,14},{9,15},{10,... | collective-permute-start | bytes 12296 | tf_op jit(solution)/shard_map/ppermute | solution.py:643

commit v17 on v16

--- a/solution.py
+++ b/solution.py
@@ -385,17 +385,12 @@
     groups = rows // 8
     chip_here, core, slabs = place(planes)
 
-    fetches = []
-    for k in range(steps + 1):
-        for n in range(4):
-            at = pl.ds(n * planes, planes)
-            fetches.append(pltpu.make_async_copy(placed.at[k, at], held.at[k, at], sems.at[k, n]))
-            fetches[-1].start()
+    fetch_all = pltpu.make_async_copy(placed, held, sems.at[0])
+    fetch_all.start()
 
     def keep(k, field, done):
-        for n in range(4):
-            source = field.at[pl.ds(n * planes + 2, planes), pl.ds(0, rows)]
-            yield pltpu.make_async_copy(source, history.at[k, pl.ds(n * planes, planes)], done.at[n])
+        source = field.at[pl.ds(2, 4 * planes), pl.ds(0, rows)]
+        return pltpu.make_async_copy(source, history.at[k], done.at[0])
 
     banded[...] = band(lanes)
     load_blocks(slabs, ((own0, own1), (mate0, mate1), (over0, over1), (far0, far1)), odd, even)
@@ -421,8 +416,7 @@
     def advance(k, now, then, done):
         @pl.when(k >= 2)
         def _():
-            for copy in keep(k - 2, then, done):
-                copy.wait()
+            keep(k - 2, then, done).wait()
 
         def work(z, y_part, chip, p):
             def fetch(j, rows):
@@ -447,8 +441,7 @@
         owned = jnp.where(lax.rem(source_slab, 2) == core, strength, 0.0)
         laps[k, source_p, source_slab // 2, tile, :] += owned
         then[source_z + 2, tile, :] += moved
-        for copy in keep(k, then, done):
-            copy.start()
+        keep(k, then, done).start()
 
     @pl.loop(0, steps // 2)
     def _(pair):
@@ -456,10 +449,8 @@
         advance(2 * pair + 1, odd, even, sems_even)
 
     for k, field, done in ((steps - 2, odd, sems_odd), (steps - 1, even, sems_even)):
-        for copy in keep(k, field, done):
-            copy.wait()
-    for fetch in fetches:
-        fetch.wait()
+        keep(k, field, done).wait()
+    fetch_all.wait()
 
 
 def inject_kernel(held, history, inject):
@@ -709,9 +700,9 @@
         ],
         scratch_shapes=step_scratch
         + [
-            pltpu.SemaphoreType.DMA((steps + 1, 4)),
-            pltpu.SemaphoreType.DMA((4,)),
-            pltpu.SemaphoreType.DMA((4,)),
+            pltpu.SemaphoreType.DMA((1,)),
+            pltpu.SemaphoreType.DMA((1,)),
+            pltpu.SemaphoreType.DMA((1,)),
         ],
         compiler_params=pltpu.CompilerParams(vmem_limit_bytes=21 * 2**20),
         cost_estimate=pl.CostEstimate(flops=1000, bytes_accessed=1000, transcendentals=0),

time: 75.3 us -> 74.8 us (level)
  transfers between devices with their start and end apart: 22 -> 22, of which waited for: 13 -> 14; matrix products, arithmetic and copies ran while one was open for 0% -> 0% of each run, Pallas kernels for 29% -> 29%
where the time goes in v17:
time: 74.8 us; the launch traced here: 74.6 us
  Pallas kernels  31.7 us (42%)
  starting transfers between devices  21.6 us (29%)
  waiting for transfers between devices  19.2 us (26%)
  between operations  1.43 us (2%)
    ppermute x22, starting transfers between devices, exchange(): lax.ppermute(value, axes, [(i, i ^ bits) for i in range(lax.axis_size(axe...  21.6 us
    ppermute x22, waiting for transfers between devices, exchange(): lax.ppermute(value, axes, [(i, i ^ bits) for i in range(lax.axis_size(axe...  19.2 us
    pallas_call x1, Pallas kernels, scatter(): pl.pallas_call(functools.partial(scatter_kernel, rows_x), grid=(rows_all...  9.27 us
    pallas_call x1, Pallas kernels, whole_shards(): pl.pallas_call(forward_kernel, in_specs=[smem, smem] + [vmem] * 10 + [pl....  9.17 us
    pallas_call x1, Pallas kernels, whole_shards(): pl.pallas_call(adjoint_kernel, in_specs=[vmem] * 8, out_specs=[vmem] * 4,...  6.99 us
    pallas_call x1, Pallas kernels, whole_shards(): pl.pallas_call(first_kernel, in_specs=[hbm] * 3, out_specs=[vmem] * 3, ou...  2.13 us
  transfers between devices with their start and end apart: 22, of which 14 were waited for; matrix products, arithmetic and copies ran while one was open for 0% of the time, Pallas kernels for 29%

profile of v17, /device:TPU:0, one launch (start us, length us, event | category | flops | bytes accessed | tf_op | source)
XLA Modules:
  0.0 74.6 jit_solution(3710493363707553721)
XLA Ops:
  0.6 2.1 %first_to_cross.1 = (f32[2,8,64,128]{3,2,1,0:T(8,128)}, f32[8,64,128]{2,1,0:T(8,128)}, f32[4,64,128]{2,1,0:T(8,128)}) custom-call(f32[2,8,64,128]{3,2,1,0:T(8,128)} %fwd_prev.1, f32[2,8,64,128]{3,2,1,0:T(8,128)} %fwd_cur.1, f32[8,64,128]{2,1,0:T(8,128)} %courant.1), custom_call_target="tpu_custom_call" | custom-call | tf_op jit(solution)/shard_map/first_to_cross/pallas_call | solution.py:650
  2.8 3.0 %collective-permute-start = (f32[4,64,128]{2,1,0:T(8,128)}, f32[4,64,128]{2,1,0:T(8,128)S(1)}, u32[]{:S(2)}, u32[]{:S(2)}) collective-permute-start(f32[4,64,128]{2,1,0:T(8,128)} %get-tuple-element.31), channel_id=1, source_target_pairs={{0,2},{1,3},{2,0},{3,1},{4,6},{5,7},{6,4},{7,5},{8,10},{9,11},{10,... | collective-permute-start | bytes 393224 | tf_op jit(solution)/shard_map/ppermute | solution.py:634
  5.8 0.0 copy-start
  5.8 0.0 copy-start.5
  5.8 0.0 copy-start.7
  5.8 0.1 collective-permute-start.5
  5.9 9.3 %receiver_scatter.1 = (f32[9,2048,128]{2,1,0:T(8,128)}, f32[8,128]{1,0:T(8,128)}) custom-call(s32[2,512]{1,0:T(2,128)} %cells_ref.1, f32[2,8,512]{2,1,0:T(8,128)} %observed_ref.1), custom_call_target="tpu_custom_call" | custom-call | flops 4831838208 | bytes 9437184 | tf_op jit(solution)/shard_map/receiver_scatter/pallas_call | solution.py:305
  15.2 0.0 collective-permute-done.value
  15.2 0.7 copy-done.6
  15.9 2.0 %collective-permute-start.4 = (f32[4,64,128]{2,1,0:T(8,128)S(1)}, f32[4,64,128]{2,1,0:T(8,128)S(1)}, u32[]{:S(2)}, u32[]{:S(2)}) collective-permute-start(f32[4,64,128]{2,1,0:T(8,128)S(1)} %after.3.earlier.mine), channel_id=1, source_target_pairs={{0,4},{1,5},{2,6},{3,7},{4,0},{5,1},{6,2},{7,3},{8,12},{9,13},{10,... | collective-permute-start | bytes 393224 | tf_op jit(solution)/shard_map/ppermute | solution.py:634
  17.9 0.0 copy-done
  17.9 0.0 copy-done.1
  17.9 0.0 copy-done.3
  17.9 0.0 copy-done.4
  17.9 0.0 copy-done.5
  17.9 1.4 %pick.1 = (f32[2,8,64,128]{3,2,1,0:T(8,128)}, f32[2,8,64,128]{3,2,1,0:T(8,128)S(1)}, f32[8,64,128]{2,1,0:T(8,128)S(1)}, f32[11,64,128]{2,1,0:T(8,128)S(1)}) custom-call(f32[4,64,128]{2,1,0:T(8,128)S(1)} %after.3.earlier.mine, f32[2,8,64,128]{3,2,1,0:T(8,128)S(1)} %copy-done.4, f32[2,8,64,128]{3,2,1,0:T(8,128)S(1)} %copy-done.5, ...), custom_call_target="tpu_custom_call" | custom-call | tf_op jit(solution)/shard_map/pick/pallas_call | solution.py:173
  19.3 0.1 collective-permute-start.2
  19.4 1.5 %collective-permute-start.9 = (f32[2,8,64,128]{3,2,1,0:T(8,128)}, f32[2,8,64,128]{3,2,1,0:T(8,128)S(1)}, u32[]{:S(2)}, u32[]{:S(2)}) collective-permute-start(f32[2,8,64,128]{3,2,1,0:T(8,128)} %get-tuple-element.41), channel_id=1, source_target_pairs={{0,2},{1,3},{2,0},{3,1},{4,6},{5,7},{6,4},{7,5},{8,10},{9,11},{10,... | collective-permute-start | bytes 1572872 | tf_op jit(solution)/shard_map/ppermute | solution.py:634
  20.8 0.1 collective-permute-done.4.other
  21.0 0.1 collective-permute-start.8
  21.1 0.4 collective-permute-start.3
  21.6 0.0 collective-permute-done.5.value
  21.6 0.7 after.4
  22.3 0.1 collective-permute-start.6
  22.4 0.0 collective-permute-done.2.mate0
  22.4 0.4 collective-permute-start.7
  23.5 0.0 collective-permute-done.3.mate1
  23.5 0.1 collective-permute-start.1
  23.6 0.0 collective-permute-done.8.speed_mate
  23.6 0.3 collective-permute-done.6.far0
  24.0 0.6 collective-permute-done.7.far1
  24.6 0.0 copy-done.7
  24.6 9.2 %forward_steps.1 = (f32[8,8,2,64,128]{4,3,2,1,0:T(8,128)S(1)}, f32[8,32,64,128]{3,2,1,0:T(8,128)S(1)}, f32[9,32,64,128]{3,2,1,0:T(8,128)S(1)}, f32[32,64,128]{2,1,0:T(8,128)S(1)}, f32[16,64,128]{2,1,0:T(8,128)S(1)}) custom-call(s32[1]{0:T(128)} %bitcast.3.start, s32[2]{0:T(128)S(1)} %copy-done.7, f32[8,64,128]{2,1,0:T(8,128)S(1)} %get-tuple-element.34.own0, ...), custom_call_target="tpu_custom_call" | custom-call | flops 1000 | bytes 1000 | tf_op jit(solution)/shard_map/forward_steps/pallas_call | solution.py:690
  33.7 0.2 collective-permute-done.9.value
  34.0 0.1 collective-permute-start.10
  34.0 1.0 %inject.1 = f32[8,32,64,128]{3,2,1,0:T(8,128)S(1)} custom-call(f32[9,32,64,128]{3,2,1,0:T(8,128)S(1)} %get-tuple-element.43.held, f32[8,32,64,128]{3,2,1,0:T(8,128)S(1)} %get-tuple-element.44.history), custom_call_target="tpu_custom_call" | custom-call | tf_op jit(solution)/shard_map/inject/pallas_call | solution.py:714
  35.0 0.0 collective-permute-done.1.mate
  35.0 0.9 %collective-permute-done.10.far = f32[2,8,64,128]{3,2,1,0:T(8,128)S(1)} collective-permute-done((f32[2,8,64,128]{3,2,1,0:T(8,128)S(1)}, f32[2,8,64,128]{3,2,1,0:T(8,128)S(1)}, u32[]{:S(2)}, u32[]{:S(2)}) %collective-permute-start.10) | collective-permute-done | bytes 524320 | tf_op jit(solution)/shard_map/ppermute | solution.py:634
  35.9 7.0 %adjoint_steps.1 = (f32[4,64,128]{2,1,0:T(8,128)S(1)}, f32[4,64,128]{2,1,0:T(8,128)S(1)}, f32[4,64,128]{2,1,0:T(8,128)S(1)}, f32[4,64,128]{2,1,0:T(8,128)S(1)}) custom-call(f32[2,8,64,128]{3,2,1,0:T(8,128)S(1)} %get-tuple-element.33.own, f32[2,8,64,128]{3,2,1,0:T(8,128)S(1)} %collective-permute-done.1.mate, f32[2,8,64,128]{3,2,1,0:T(8,128)S(1)} %after.5.over, ...), custom_call_target="tpu_custom_call" | custom-call | flops 62914560 | bytes 33554432 | tf_op jit(solution)/shard_map/adjoint_steps/pallas_call | solution.py:724
  42.9 2.7 %collective-permute-start.11 = (f32[4,64,128]{2,1,0:T(8,128)S(1)}, f32[4,64,128]{2,1,0:T(8,128)S(1)}, u32[]{:S(2)}, u32[]{:S(2)}) collective-permute-start(f32[4,64,128]{2,1,0:T(8,128)S(1)} %get-tuple-element.47), channel_id=1, source_target_pairs={{0,6},{1,7},{2,4},{3,5},{4,2},{5,3},{6,0},{7,1},{8,14},{9,15},{10,... | collective-permute-start | bytes 393224 | tf_op jit(solution)/shard_map/ppermute | solution.py:634
  45.6 0.5 collective-permute-start.12
  46.1 0.4 collective-permute-start.13
  46.5 3.1 %collective-permute-done.11.by_xy = f32[4,64,128]{2,1,0:T(8,128)S(1)} collective-permute-done((f32[4,64,128]{2,1,0:T(8,128)S(1)}, f32[4,64,128]{2,1,0:T(8,128)S(1)}, u32[]{:S(2)}, u32[]{:S(2)}) %collective-permute-start.11) | collective-permute-done | bytes 131104 | tf_op jit(solution)/shard_map/ppermute | solution.py:634
  49.6 2.7 %collective-permute-done.12.by_y = f32[4,64,128]{2,1,0:T(8,128)S(1)} collective-permute-done((f32[4,64,128]{2,1,0:T(8,128)S(1)}, f32[4,64,128]{2,1,0:T(8,128)S(1)}, u32[]{:S(2)}, u32[]{:S(2)}) %collective-permute-start.12) | collective-permute-done | bytes 131104 | tf_op jit(solution)/shard_map/ppermute | solution.py:634
  52.3 0.3 collective-permute-done.13.by_x
  52.6 1.7 %collective-permute-start.14 = (f32[2,64,128]{2,1,0:T(8,128)S(1)}, f32[2,64,128]{2,1,0:T(8,128)S(1)}, u32[]{:S(2)}, u32[]{:S(2)}) collective-permute-start(f32[2,64,128]{2,1,0:T(8,128)S(1)} %get-tuple-element.51), channel_id=1, source_target_pairs={{0,8},{1,9},{2,10},{3,11},{4,12},{5,13},{6,14},{7,15},{8,0},{9,1},... | collective-permute-start | bytes 196616 | tf_op jit(solution)/shard_map/ppermute | solution.py:634
  54.3 2.7 %collective-permute-done.14.other = f32[2,64,128]{2,1,0:T(8,128)S(1)} collective-permute-done((f32[2,64,128]{2,1,0:T(8,128)S(1)}, f32[2,64,128]{2,1,0:T(8,128)S(1)}, u32[]{:S(2)}, u32[]{:S(2)}) %collective-permute-start.14) | collective-permute-done | bytes 65568 | tf_op jit(solution)/shard_map/ppermute | solution.py:634
  57.0 2.7 %collective-permute-start.15 = (f32[2,64,128]{2,1,0:T(8,128)S(1)}, f32[2,64,128]{2,1,0:T(8,128)S(1)}, u32[]{:S(2)}, u32[]{:S(2)}) collective-permute-start(f32[2,64,128]{2,1,0:T(8,128)S(1)} %add_kernel.1.mine), channel_id=1, source_target_pairs={{0,16},{1,17},{2,18},{3,19},{4,20},{5,21},{6,22},{7,23},{8,24},{9,... | collective-permute-start | bytes 196616 | tf_op jit(solution)/shard_map/ppermute | solution.py:634
  59.6 2.6 %collective-permute-done.15.other = f32[2,64,128]{2,1,0:T(8,128)S(1)} collective-permute-done((f32[2,64,128]{2,1,0:T(8,128)S(1)}, f32[2,64,128]{2,1,0:T(8,128)S(1)}, u32[]{:S(2)}, u32[]{:S(2)}) %collective-permute-start.15) | collective-permute-done | bytes 65568 | tf_op jit(solution)/shard_map/ppermute | solution.py:634
  62.2 0.0 copy-done.2
  62.2 0.1 sums_kernel.1
  62.3 1.6 %collective-permute-start.16 = (f32[136,128]{1,0:T(8,128)S(1)}, f32[136,128]{1,0:T(8,128)S(1)}, u32[]{:S(2)}, u32[]{:S(2)}) collective-permute-start(f32[136,128]{1,0:T(8,128)S(1)} %get-tuple-element.52.mine), channel_id=1, source_target_pairs={{0,8},{1,9},{2,10},{3,11},{4,12},{5,13},{6,14},{7,15},{8,0},{9,1},... | collective-permute-start | bytes 208904 | tf_op jit(solution)/shard_map/ppermute | solution.py:634
  63.9 0.0 collective-permute-start.17
  63.9 0.5 collective-permute-start.18
  64.5 0.6 collective-permute-done.17.s1
  65.1 1.9 %collective-permute-done.18.s2 = f32[8,128]{1,0:T(8,128)S(1)} collective-permute-done((f32[8,128]{1,0:T(8,128)S(1)}, f32[8,128]{1,0:T(8,128)S(1)}, u32[]{:S(2)}, u32[]{:S(2)}) %collective-permute-start.18) | collective-permute-done | bytes 4128 | tf_op jit(solution)/shard_map/ppermute | solution.py:634
  67.0 0.0 collective-permute-done.16.other
  67.0 1.5 %collective-permute-start.19 = (f32[264,128]{1,0:T(8,128)S(1)}, f32[264,128]{1,0:T(8,128)S(1)}, u32[]{:S(2)}, u32[]{:S(2)}) collective-permute-start(f32[264,128]{1,0:T(8,128)S(1)} %get-tuple-element.54.mine), channel_id=1, source_target_pairs={{0,4},{1,5},{2,6},{3,7},{4,0},{5,1},{6,2},{7,3},{8,12},{9,13},{10,... | collective-permute-start | bytes 405512 | tf_op jit(solution)/shard_map/ppermute | solution.py:634
  68.5 0.8 %collective-permute-start.20 = (f32[8,128]{1,0:T(8,128)S(1)}, f32[8,128]{1,0:T(8,128)S(1)}, u32[]{:S(2)}, u32[]{:S(2)}) collective-permute-start(f32[8,128]{1,0:T(8,128)S(1)} %get-tuple-element.55.s0), channel_id=1, source_target_pairs={{0,2},{1,3},{2,0},{3,1},{4,6},{5,7},{6,4},{7,5},{8,10},{9,11},{10,... | collective-permute-start | bytes 12296 | tf_op jit(solution)/shard_map/ppermute | solution.py:634
  69.3 1.3 %collective-permute-start.21 = (f32[8,128]{1,0:T(8,128)S(1)}, f32[8,128]{1,0:T(8,128)S(1)}, u32[]{:S(2)}, u32[]{:S(2)}) collective-permute-start(f32[8,128]{1,0:T(8,128)S(1)} %get-tuple-element.55.s0), channel_id=1, source_target_pairs={{0,6},{1,7},{2,4},{3,5},{4,2},{5,3},{6,0},{7,1},{8,14},{9,15},{10,... | collective-permute-start | bytes 12296 | tf_op jit(solution)/shard_map/ppermute | solution.py:634
  70.5 1.5 %collective-permute-done.20.s1 = f32[8,128]{1,0:T(8,128)S(1)} collective-permute-done((f32[8,128]{1,0:T(8,128)S(1)}, f32[8,128]{1,0:T(8,128)S(1)}, u32[]{:S(2)}, u32[]{:S(2)}) %collective-permute-start.20) | collective-permute-done | bytes 4128 | tf_op jit(solution)/shard_map/ppermute | solution.py:634
  72.1 1.7 %collective-permute-done.21.s2 = f32[8,128]{1,0:T(8,128)S(1)} collective-permute-done((f32[8,128]{1,0:T(8,128)S(1)}, f32[8,128]{1,0:T(8,128)S(1)}, u32[]{:S(2)}, u32[]{:S(2)}) %collective-permute-start.21) | collective-permute-done | bytes 4128 | tf_op jit(solution)/shard_map/ppermute | solution.py:634
  73.8 0.0 collective-permute-done.19.other
  73.8 0.8 %finish.1 = (f32[8,64,128]{2,1,0:T(8,128)}, f32[1]{0:T(128)}) custom-call(f32[264,128]{1,0:T(8,128)S(1)} %get-tuple-element.54.mine, f32[264,128]{1,0:T(8,128)S(1)} %collective-permute-done.19.other, f32[8,64,128]{2,1,0:T(8,128)S(1)} %copy-done.2, f32[8,128]{1,0:T(8,128)S(1)} %get-tuple-element.55.s0, f32[8,128]{1,0:T(8,128)S(1)} %collective-permute-done.20.s1, ...), custom_call_target="tpu_custom_call" | custom-call | tf_op jit(solution)/shard_map/finish/pallas_call | solution.py:746
  (11 shorter events, 0.1 us)
Async XLA Ops:
  2.8 12.4 %collective-permute-start = (f32[4,64,128]{2,1,0:T(8,128)}, f32[4,64,128]{2,1,0:T(8,128)S(1)}, u32[]{:S(2)}, u32[]{:S(2)}) collective-permute-start(f32[4,64,128]{2,1,0:T(8,128)} %get-tuple-element.31), channel_id=1, source_target_pairs={{0,2},{1,3},{2,0},{3,1},{4,6},{5,7},{6,4},{7,5},{8,10},{9,11},{10,... | collective-permute-start | bytes 393224 | tf_op jit(solution)/shard_map/ppermute | solution.py:634
  5.8 12.1 %copy-start = (f32[2,8,64,128]{3,2,1,0:T(8,128)S(1)}, f32[2,8,64,128]{3,2,1,0:T(8,128)}, u32[]{:S(2)}) copy-start(f32[2,8,64,128]{3,2,1,0:T(8,128)} %fwd_prev.1) | copy-start | bytes 1572868
  5.8 12.1 %copy-start.1 = (f32[2,8,64,128]{3,2,1,0:T(8,128)S(1)}, f32[2,8,64,128]{3,2,1,0:T(8,128)}, u32[]{:S(2)}) copy-start(f32[2,8,64,128]{3,2,1,0:T(8,128)} %fwd_cur.1) | copy-start | bytes 1572868
  5.8 12.1 %copy-start.3 = (f32[8,64,128]{2,1,0:T(8,128)S(1)}, f32[8,64,128]{2,1,0:T(8,128)}, u32[]{:S(2)}) copy-start(f32[8,64,128]{2,1,0:T(8,128)} %get-tuple-element.32.speed.own) | copy-start | bytes 786436
  5.8 12.1 %copy-start.4 = (f32[2,8,64,128]{3,2,1,0:T(8,128)S(1)}, f32[2,8,64,128]{3,2,1,0:T(8,128)}, u32[]{:S(2)}) copy-start(f32[2,8,64,128]{3,2,1,0:T(8,128)} %adj_next.1) | copy-start | bytes 1572868
  5.8 12.1 %copy-start.5 = (f32[2,8,64,128]{3,2,1,0:T(8,128)S(1)}, f32[2,8,64,128]{3,2,1,0:T(8,128)}, u32[]{:S(2)}) copy-start(f32[2,8,64,128]{3,2,1,0:T(8,128)} %adj_cur.1) | copy-start | bytes 1572868
  5.8 18.8 %copy-start.7 = (s32[2]{0:T(128)S(1)}, s32[2]{0:T(128)}, u32[]{:S(2)}) copy-start(s32[2]{0:T(128)} %sources.1) | copy-start | bytes 28
  5.8 15.8 %collective-permute-start.5 = (f32[2,8,64,128]{3,2,1,0:T(8,128)}, f32[2,8,64,128]{3,2,1,0:T(8,128)S(1)}, u32[]{:S(2)}, u32[]{:S(2)}) collective-permute-start(f32[2,8,64,128]{3,2,1,0:T(8,128)} %get-tuple-element.36), channel_id=1, source_target_pairs={{0,2},{1,3},{2,0},{3,1},{4,6},{5,7},{6,4},{7,5},{8,10},{9,11},{10,... | collective-permute-start | bytes 1572872 | tf_op jit(solution)/shard_map/ppermute | solution.py:634
  15.2 0.7 copy-start.6
  15.9 5.0 %collective-permute-start.4 = (f32[4,64,128]{2,1,0:T(8,128)S(1)}, f32[4,64,128]{2,1,0:T(8,128)S(1)}, u32[]{:S(2)}, u32[]{:S(2)}) collective-permute-start(f32[4,64,128]{2,1,0:T(8,128)S(1)} %after.3.earlier.mine), channel_id=1, source_target_pairs={{0,4},{1,5},{2,6},{3,7},{4,0},{5,1},{6,2},{7,3},{8,12},{9,13},{10,... | collective-permute-start | bytes 393224 | tf_op jit(solution)/shard_map/ppermute | solution.py:634
  19.3 3.1 %collective-permute-start.2 = (f32[8,64,128]{2,1,0:T(8,128)S(1)}, f32[8,64,128]{2,1,0:T(8,128)S(1)}, u32[]{:S(2)}, u32[]{:S(2)}) collective-permute-start(f32[8,64,128]{2,1,0:T(8,128)S(1)} %get-tuple-element.34.own0), channel_id=1, source_target_pairs={{0,1},{1,0},{2,3},{3,2},{4,5},{5,4},{6,7},{7,6},{8,9},{9,8},{10,11... | collective-permute-start | bytes 786440 | tf_op jit(solution)/shard_map/ppermute | solution.py:634
  19.4 14.6 %collective-permute-start.9 = (f32[2,8,64,128]{3,2,1,0:T(8,128)}, f32[2,8,64,128]{3,2,1,0:T(8,128)S(1)}, u32[]{:S(2)}, u32[]{:S(2)}) collective-permute-start(f32[2,8,64,128]{3,2,1,0:T(8,128)} %get-tuple-element.41), channel_id=1, source_target_pairs={{0,2},{1,3},{2,0},{3,1},{4,6},{5,7},{6,4},{7,5},{8,10},{9,11},{10,... | collective-permute-start | bytes 1572872 | tf_op jit(solution)/shard_map/ppermute | solution.py:634
  21.0 2.6 %collective-permute-start.8 = (f32[13,64,128]{2,1,0:T(8,128)S(1)}, f32[13,64,128]{2,1,0:T(8,128)S(1)}, u32[]{:S(2)}, u32[]{:S(2)}) collective-permute-start(f32[13,64,128]{2,1,0:T(8,128)S(1)} %arrange_kernel.1.earlier.speed), channel_id=1, source_target_pairs={{0,1},{1,0},{2,3},{3,2},{4,5},{5,4},{6,7},{7,6},{8,9},{9,8},{10,11... | collective-permute-start | bytes 1277960 | tf_op jit(solution)/shard_map/ppermute | solution.py:634
  21.1 2.3 %collective-permute-start.3 = (f32[11,64,128]{2,1,0:T(8,128)S(1)}, f32[11,64,128]{2,1,0:T(8,128)S(1)}, u32[]{:S(2)}, u32[]{:S(2)}) collective-permute-start(f32[11,64,128]{2,1,0:T(8,128)S(1)} %get-tuple-element.35.own1), channel_id=1, source_target_pairs={{0,1},{1,0},{2,3},{3,2},{4,5},{5,4},{6,7},{7,6},{8,9},{9,8},{10,11... | collective-permute-start | bytes 1081352 | tf_op jit(solution)/shard_map/ppermute | solution.py:634
  22.3 1.7 %collective-permute-start.6 = (f32[8,64,128]{2,1,0:T(8,128)S(1)}, f32[8,64,128]{2,1,0:T(8,128)}, u32[]{:S(2)}, u32[]{:S(2)}) collective-permute-start(f32[8,64,128]{2,1,0:T(8,128)S(1)} %get-tuple-element.37.over0), channel_id=1, source_target_pairs={{0,1},{1,0},{2,3},{3,2},{4,5},{5,4},{6,7},{7,6},{8,9},{9,8},{10,11... | collective-permute-start | bytes 786440 | tf_op jit(solution)/shard_map/ppermute | solution.py:634
  22.4 2.2 %collective-permute-start.7 = (f32[8,64,128]{2,1,0:T(8,128)}, f32[8,64,128]{2,1,0:T(8,128)}, u32[]{:S(2)}, u32[]{:S(2)}) collective-permute-start(f32[8,64,128]{2,1,0:T(8,128)} %get-tuple-element.38.over1), channel_id=1, source_target_pairs={{0,1},{1,0},{2,3},{3,2},{4,5},{5,4},{6,7},{7,6},{8,9},{9,8},{10,11... | collective-permute-start | bytes 786440 | tf_op jit(solution)/shard_map/ppermute | solution.py:634
  23.5 11.6 %collective-permute-start.1 = (f32[2,8,64,128]{3,2,1,0:T(8,128)S(1)}, f32[2,8,64,128]{3,2,1,0:T(8,128)S(1)}, u32[]{:S(2)}, u32[]{:S(2)}) collective-permute-start(f32[2,8,64,128]{3,2,1,0:T(8,128)S(1)} %get-tuple-element.33.own), channel_id=1, source_target_pairs={{0,1},{1,0},{2,3},{3,2},{4,5},{5,4},{6,7},{7,6},{8,9},{9,8},{10,11... | collective-permute-start | bytes 1572872 | tf_op jit(solution)/shard_map/ppermute | solution.py:634
  34.0 2.0 %collective-permute-start.10 = (f32[2,8,64,128]{3,2,1,0:T(8,128)S(1)}, f32[2,8,64,128]{3,2,1,0:T(8,128)S(1)}, u32[]{:S(2)}, u32[]{:S(2)}) collective-permute-start(f32[2,8,64,128]{3,2,1,0:T(8,128)S(1)} %after.5.over), channel_id=1, source_target_pairs={{0,1},{1,0},{2,3},{3,2},{4,5},{5,4},{6,7},{7,6},{8,9},{9,8},{10,11... | collective-permute-start | bytes 1572872 | tf_op jit(solution)/shard_map/ppermute | solution.py:634
  35.9 26.3 %copy-start.2 = (f32[8,64,128]{2,1,0:T(8,128)S(1)}, f32[8,64,128]{2,1,0:T(8,128)}, u32[]{:S(2)}) copy-start(f32[8,64,128]{2,1,0:T(8,128)} %momentum.3) | copy-start | bytes 786436
  42.9 6.6 %collective-permute-start.11 = (f32[4,64,128]{2,1,0:T(8,128)S(1)}, f32[4,64,128]{2,1,0:T(8,128)S(1)}, u32[]{:S(2)}, u32[]{:S(2)}) collective-permute-start(f32[4,64,128]{2,1,0:T(8,128)S(1)} %get-tuple-element.47), channel_id=1, source_target_pairs={{0,6},{1,7},{2,4},{3,5},{4,2},{5,3},{6,0},{7,1},{8,14},{9,15},{10,... | collective-permute-start | bytes 393224 | tf_op jit(solution)/shard_map/ppermute | solution.py:634
  45.6 6.6 %collective-permute-start.12 = (f32[4,64,128]{2,1,0:T(8,128)S(1)}, f32[4,64,128]{2,1,0:T(8,128)S(1)}, u32[]{:S(2)}, u32[]{:S(2)}) collective-permute-start(f32[4,64,128]{2,1,0:T(8,128)S(1)} %get-tuple-element.48), channel_id=1, source_target_pairs={{0,4},{1,5},{2,6},{3,7},{4,0},{5,1},{6,2},{7,3},{8,12},{9,13},{10,... | collective-permute-start | bytes 393224 | tf_op jit(solution)/shard_map/ppermute | solution.py:634
  46.1 6.5 %collective-permute-start.13 = (f32[4,64,128]{2,1,0:T(8,128)S(1)}, f32[4,64,128]{2,1,0:T(8,128)S(1)}, u32[]{:S(2)}, u32[]{:S(2)}) collective-permute-start(f32[4,64,128]{2,1,0:T(8,128)S(1)} %get-tuple-element.49), channel_id=1, source_target_pairs={{0,2},{1,3},{2,0},{3,1},{4,6},{5,7},{6,4},{7,5},{8,10},{9,11},{10,... | collective-permute-start | bytes 393224 | tf_op jit(solution)/shard_map/ppermute | solution.py:634
  52.6 4.3 %collective-permute-start.14 = (f32[2,64,128]{2,1,0:T(8,128)S(1)}, f32[2,64,128]{2,1,0:T(8,128)S(1)}, u32[]{:S(2)}, u32[]{:S(2)}) collective-permute-start(f32[2,64,128]{2,1,0:T(8,128)S(1)} %get-tuple-element.51), channel_id=1, source_target_pairs={{0,8},{1,9},{2,10},{3,11},{4,12},{5,13},{6,14},{7,15},{8,0},{9,1},... | collective-permute-start | bytes 196616 | tf_op jit(solution)/shard_map/ppermute | solution.py:634
  57.0 5.2 %collective-permute-start.15 = (f32[2,64,128]{2,1,0:T(8,128)S(1)}, f32[2,64,128]{2,1,0:T(8,128)S(1)}, u32[]{:S(2)}, u32[]{:S(2)}) collective-permute-start(f32[2,64,128]{2,1,0:T(8,128)S(1)} %add_kernel.1.mine), channel_id=1, source_target_pairs={{0,16},{1,17},{2,18},{3,19},{4,20},{5,21},{6,22},{7,23},{8,24},{9,... | collective-permute-start | bytes 196616 | tf_op jit(solution)/shard_map/ppermute | solution.py:634
  62.3 4.7 %collective-permute-start.16 = (f32[136,128]{1,0:T(8,128)S(1)}, f32[136,128]{1,0:T(8,128)S(1)}, u32[]{:S(2)}, u32[]{:S(2)}) collective-permute-start(f32[136,128]{1,0:T(8,128)S(1)} %get-tuple-element.52.mine), channel_id=1, source_target_pairs={{0,8},{1,9},{2,10},{3,11},{4,12},{5,13},{6,14},{7,15},{8,0},{9,1},... | collective-permute-start | bytes 208904 | tf_op jit(solution)/shard_map/ppermute | solution.py:634
  63.9 1.2 %collective-permute-start.17 = (f32[8,128]{1,0:T(8,128)S(1)}, f32[8,128]{1,0:T(8,128)S(1)}, u32[]{:S(2)}, u32[]{:S(2)}) collective-permute-start(f32[8,128]{1,0:T(8,128)S(1)} %get-tuple-element.53.s0), channel_id=1, source_target_pairs={{0,1},{1,0},{2,3},{3,2},{4,5},{5,4},{6,7},{7,6},{8,9},{9,8},{10,11... | collective-permute-start | bytes 12296 | tf_op jit(solution)/shard_map/ppermute | solution.py:634
  63.9 3.0 %collective-permute-start.18 = (f32[8,128]{1,0:T(8,128)S(1)}, f32[8,128]{1,0:T(8,128)S(1)}, u32[]{:S(2)}, u32[]{:S(2)}) collective-permute-start(f32[8,128]{1,0:T(8,128)S(1)} %get-tuple-element.53.s0), channel_id=1, source_target_pairs={{0,9},{1,8},{2,11},{3,10},{4,13},{5,12},{6,15},{7,14},{8,1},{9,0},... | collective-permute-start | bytes 12296 | tf_op jit(solution)/shard_map/ppermute | solution.py:634
  67.0 6.8 %collective-permute-start.19 = (f32[264,128]{1,0:T(8,128)S(1)}, f32[264,128]{1,0:T(8,128)S(1)}, u32[]{:S(2)}, u32[]{:S(2)}) collective-permute-start(f32[264,128]{1,0:T(8,128)S(1)} %get-tuple-element.54.mine), channel_id=1, source_target_pairs={{0,4},{1,5},{2,6},{3,7},{4,0},{5,1},{6,2},{7,3},{8,12},{9,13},{10,... | collective-permute-start | bytes 405512 | tf_op jit(solution)/shard_map/ppermute | solution.py:634
  68.5 3.6 %collective-permute-start.20 = (f32[8,128]{1,0:T(8,128)S(1)}, f32[8,128]{1,0:T(8,128)S(1)}, u32[]{:S(2)}, u32[]{:S(2)}) collective-permute-start(f32[8,128]{1,0:T(8,128)S(1)} %get-tuple-element.55.s0), channel_id=1, source_target_pairs={{0,2},{1,3},{2,0},{3,1},{4,6},{5,7},{6,4},{7,5},{8,10},{9,11},{10,... | collective-permute-start | bytes 12296 | tf_op jit(solution)/shard_map/ppermute | solution.py:634
  69.3 4.5 %collective-permute-start.21 = (f32[8,128]{1,0:T(8,128)S(1)}, f32[8,128]{1,0:T(8,128)S(1)}, u32[]{:S(2)}, u32[]{:S(2)}) collective-permute-start(f32[8,128]{1,0:T(8,128)S(1)} %get-tuple-element.55.s0), channel_id=1, source_target_pairs={{0,6},{1,7},{2,4},{3,5},{4,2},{5,3},{6,0},{7,1},{8,14},{9,15},{10,... | collective-permute-start | bytes 12296 | tf_op jit(solution)/shard_map/ppermute | solution.py:634

commit v18 on v17

--- a/solution.py
+++ b/solution.py
@@ -598,7 +598,7 @@
     sums[...] = value
 
 
-def finish_kernel(mine, other, momentum, s0, s1, s2, out, kinetic):
+def finish_kernel(s2, other, s1, mine, momentum, s0, out, kinetic):
     planes, rows, lanes = momentum.shape
     cells = 4.0 * planes * rows * lanes
     shot = lax.axis_index("shot")
@@ -750,7 +750,7 @@
         out_shape=[jax.ShapeDtypeStruct(momentum.shape, jnp.float32), jax.ShapeDtypeStruct((1,), jnp.float32)],
         compiler_params=pltpu.CompilerParams(vmem_limit_bytes=4 * 2**20),
         name="finish",
-    )(data, received, momentum, sums, *others)
+    )(others[1], received, others[0], data, momentum, sums)
     return momentum_half, kinetic[0]
 
 

time: 74.8 us -> 74.6 us (level)
  no operation moved by 1% of the time
where the time goes in v18:
time: 74.6 us; the launch traced here: 74.4 us
  Pallas kernels  31.6 us (42%)
  starting transfers between devices  21.6 us (29%)
  waiting for transfers between devices  19 us (25%)
  between operations  1.43 us (2%)
    ppermute x22, starting transfers between devices, exchange(): lax.ppermute(value, axes, [(i, i ^ bits) for i in range(lax.axis_size(axe...  21.6 us
    ppermute x22, waiting for transfers between devices, exchange(): lax.ppermute(value, axes, [(i, i ^ bits) for i in range(lax.axis_size(axe...  19 us
    pallas_call x1, Pallas kernels, scatter(): pl.pallas_call(functools.partial(scatter_kernel, rows_x), grid=(rows_all...  9.27 us
    pallas_call x1, Pallas kernels, whole_shards(): pl.pallas_call(forward_kernel, in_specs=[smem, smem] + [vmem] * 10 + [pl....  9.16 us
    pallas_call x1, Pallas kernels, whole_shards(): pl.pallas_call(adjoint_kernel, in_specs=[vmem] * 8, out_specs=[vmem] * 4,...  6.99 us
    pallas_call x1, Pallas kernels, whole_shards(): pl.pallas_call(first_kernel, in_specs=[hbm] * 3, out_specs=[vmem] * 3, ou...  2.13 us
  transfers between devices with their start and end apart: 22, of which 14 were waited for; matrix products, arithmetic and copies ran while one was open for 0% of the time, Pallas kernels for 29%

profile of v18, /device:TPU:0, one launch (start us, length us, event | category | flops | bytes accessed | tf_op | source)
XLA Modules:
  0.0 74.4 jit_solution(2290324914431044314)
XLA Ops:
  0.6 2.1 %first_to_cross.1 = (f32[2,8,64,128]{3,2,1,0:T(8,128)}, f32[8,64,128]{2,1,0:T(8,128)}, f32[4,64,128]{2,1,0:T(8,128)}) custom-call(f32[2,8,64,128]{3,2,1,0:T(8,128)} %fwd_prev.1, f32[2,8,64,128]{3,2,1,0:T(8,128)} %fwd_cur.1, f32[8,64,128]{2,1,0:T(8,128)} %courant.1), custom_call_target="tpu_custom_call" | custom-call | tf_op jit(solution)/shard_map/first_to_cross/pallas_call | solution.py:650
  2.8 3.0 %collective-permute-start = (f32[4,64,128]{2,1,0:T(8,128)}, f32[4,64,128]{2,1,0:T(8,128)S(1)}, u32[]{:S(2)}, u32[]{:S(2)}) collective-permute-start(f32[4,64,128]{2,1,0:T(8,128)} %get-tuple-element.31), channel_id=1, source_target_pairs={{0,2},{1,3},{2,0},{3,1},{4,6},{5,7},{6,4},{7,5},{8,10},{9,11},{10,... | collective-permute-start | bytes 393224 | tf_op jit(solution)/shard_map/ppermute | solution.py:634
  5.8 0.0 copy-start
  5.8 0.0 copy-start.5
  5.8 0.0 copy-start.7
  5.8 0.1 collective-permute-start.5
  5.9 9.3 %receiver_scatter.1 = (f32[9,2048,128]{2,1,0:T(8,128)}, f32[8,128]{1,0:T(8,128)}) custom-call(s32[2,512]{1,0:T(2,128)} %cells_ref.1, f32[2,8,512]{2,1,0:T(8,128)} %observed_ref.1), custom_call_target="tpu_custom_call" | custom-call | flops 4831838208 | bytes 9437184 | tf_op jit(solution)/shard_map/receiver_scatter/pallas_call | solution.py:305
  15.2 0.0 collective-permute-done.value
  15.2 0.7 copy-done.6
  15.9 2.0 %collective-permute-start.4 = (f32[4,64,128]{2,1,0:T(8,128)S(1)}, f32[4,64,128]{2,1,0:T(8,128)S(1)}, u32[]{:S(2)}, u32[]{:S(2)}) collective-permute-start(f32[4,64,128]{2,1,0:T(8,128)S(1)} %after.3.earlier.mine), channel_id=1, source_target_pairs={{0,4},{1,5},{2,6},{3,7},{4,0},{5,1},{6,2},{7,3},{8,12},{9,13},{10,... | collective-permute-start | bytes 393224 | tf_op jit(solution)/shard_map/ppermute | solution.py:634
  17.9 0.0 copy-done
  17.9 0.0 copy-done.1
  17.9 0.0 copy-done.3
  17.9 0.0 copy-done.4
  17.9 0.0 copy-done.5
  17.9 1.4 %pick.1 = (f32[2,8,64,128]{3,2,1,0:T(8,128)}, f32[2,8,64,128]{3,2,1,0:T(8,128)S(1)}, f32[8,64,128]{2,1,0:T(8,128)S(1)}, f32[11,64,128]{2,1,0:T(8,128)S(1)}) custom-call(f32[4,64,128]{2,1,0:T(8,128)S(1)} %after.3.earlier.mine, f32[2,8,64,128]{3,2,1,0:T(8,128)S(1)} %copy-done.4, f32[2,8,64,128]{3,2,1,0:T(8,128)S(1)} %copy-done.5, ...), custom_call_target="tpu_custom_call" | custom-call | tf_op jit(solution)/shard_map/pick/pallas_call | solution.py:173
  19.3 0.1 collective-permute-start.2
  19.4 1.5 %collective-permute-start.9 = (f32[2,8,64,128]{3,2,1,0:T(8,128)}, f32[2,8,64,128]{3,2,1,0:T(8,128)S(1)}, u32[]{:S(2)}, u32[]{:S(2)}) collective-permute-start(f32[2,8,64,128]{3,2,1,0:T(8,128)} %get-tuple-element.41), channel_id=1, source_target_pairs={{0,2},{1,3},{2,0},{3,1},{4,6},{5,7},{6,4},{7,5},{8,10},{9,11},{10,... | collective-permute-start | bytes 1572872 | tf_op jit(solution)/shard_map/ppermute | solution.py:634
  20.8 0.1 collective-permute-done.4.other
  21.0 0.1 collective-permute-start.8
  21.1 0.4 collective-permute-start.3
  21.6 0.0 collective-permute-done.5.value
  21.6 0.7 after.4
  22.3 0.1 collective-permute-start.6
  22.4 0.0 collective-permute-done.2.mate0
  22.4 0.4 collective-permute-start.7
  23.5 0.0 collective-permute-done.3.mate1
  23.5 0.1 collective-permute-start.1
  23.6 0.0 collective-permute-done.8.speed_mate
  23.6 0.3 collective-permute-done.6.far0
  24.0 0.6 collective-permute-done.7.far1
  24.6 0.0 copy-done.7
  24.6 9.2 %forward_steps.1 = (f32[8,8,2,64,128]{4,3,2,1,0:T(8,128)S(1)}, f32[8,32,64,128]{3,2,1,0:T(8,128)S(1)}, f32[9,32,64,128]{3,2,1,0:T(8,128)S(1)}, f32[32,64,128]{2,1,0:T(8,128)S(1)}, f32[16,64,128]{2,1,0:T(8,128)S(1)}) custom-call(s32[1]{0:T(128)} %bitcast.3.start, s32[2]{0:T(128)S(1)} %copy-done.7, f32[8,64,128]{2,1,0:T(8,128)S(1)} %get-tuple-element.34.own0, ...), custom_call_target="tpu_custom_call" | custom-call | flops 1000 | bytes 1000 | tf_op jit(solution)/shard_map/forward_steps/pallas_call | solution.py:690
  33.7 0.2 collective-permute-done.9.value
  34.0 0.1 collective-permute-start.10
  34.0 1.0 %inject.1 = f32[8,32,64,128]{3,2,1,0:T(8,128)S(1)} custom-call(f32[9,32,64,128]{3,2,1,0:T(8,128)S(1)} %get-tuple-element.43.held, f32[8,32,64,128]{3,2,1,0:T(8,128)S(1)} %get-tuple-element.44.history), custom_call_target="tpu_custom_call" | custom-call | tf_op jit(solution)/shard_map/inject/pallas_call | solution.py:714
  35.0 0.0 collective-permute-done.1.mate
  35.0 0.9 %collective-permute-done.10.far = f32[2,8,64,128]{3,2,1,0:T(8,128)S(1)} collective-permute-done((f32[2,8,64,128]{3,2,1,0:T(8,128)S(1)}, f32[2,8,64,128]{3,2,1,0:T(8,128)S(1)}, u32[]{:S(2)}, u32[]{:S(2)}) %collective-permute-start.10) | collective-permute-done | bytes 524320 | tf_op jit(solution)/shard_map/ppermute | solution.py:634
  35.9 7.0 %adjoint_steps.1 = (f32[4,64,128]{2,1,0:T(8,128)S(1)}, f32[4,64,128]{2,1,0:T(8,128)S(1)}, f32[4,64,128]{2,1,0:T(8,128)S(1)}, f32[4,64,128]{2,1,0:T(8,128)S(1)}) custom-call(f32[2,8,64,128]{3,2,1,0:T(8,128)S(1)} %get-tuple-element.33.own, f32[2,8,64,128]{3,2,1,0:T(8,128)S(1)} %collective-permute-done.1.mate, f32[2,8,64,128]{3,2,1,0:T(8,128)S(1)} %after.5.over, ...), custom_call_target="tpu_custom_call" | custom-call | flops 62914560 | bytes 33554432 | tf_op jit(solution)/shard_map/adjoint_steps/pallas_call | solution.py:724
  42.9 2.7 %collective-permute-start.11 = (f32[4,64,128]{2,1,0:T(8,128)S(1)}, f32[4,64,128]{2,1,0:T(8,128)S(1)}, u32[]{:S(2)}, u32[]{:S(2)}) collective-permute-start(f32[4,64,128]{2,1,0:T(8,128)S(1)} %get-tuple-element.47), channel_id=1, source_target_pairs={{0,6},{1,7},{2,4},{3,5},{4,2},{5,3},{6,0},{7,1},{8,14},{9,15},{10,... | collective-permute-start | bytes 393224 | tf_op jit(solution)/shard_map/ppermute | solution.py:634
  45.6 0.5 collective-permute-start.12
  46.1 0.4 collective-permute-start.13
  46.5 3.1 %collective-permute-done.11.by_xy = f32[4,64,128]{2,1,0:T(8,128)S(1)} collective-permute-done((f32[4,64,128]{2,1,0:T(8,128)S(1)}, f32[4,64,128]{2,1,0:T(8,128)S(1)}, u32[]{:S(2)}, u32[]{:S(2)}) %collective-permute-start.11) | collective-permute-done | bytes 131104 | tf_op jit(solution)/shard_map/ppermute | solution.py:634
  49.6 2.7 %collective-permute-done.12.by_y = f32[4,64,128]{2,1,0:T(8,128)S(1)} collective-permute-done((f32[4,64,128]{2,1,0:T(8,128)S(1)}, f32[4,64,128]{2,1,0:T(8,128)S(1)}, u32[]{:S(2)}, u32[]{:S(2)}) %collective-permute-start.12) | collective-permute-done | bytes 131104 | tf_op jit(solution)/shard_map/ppermute | solution.py:634
  52.3 0.3 collective-permute-done.13.by_x
  52.6 1.6 %collective-permute-start.14 = (f32[2,64,128]{2,1,0:T(8,128)S(1)}, f32[2,64,128]{2,1,0:T(8,128)S(1)}, u32[]{:S(2)}, u32[]{:S(2)}) collective-permute-start(f32[2,64,128]{2,1,0:T(8,128)S(1)} %get-tuple-element.51), channel_id=1, source_target_pairs={{0,8},{1,9},{2,10},{3,11},{4,12},{5,13},{6,14},{7,15},{8,0},{9,1},... | collective-permute-start | bytes 196616 | tf_op jit(solution)/shard_map/ppermute | solution.py:634
  54.3 2.7 %collective-permute-done.14.other = f32[2,64,128]{2,1,0:T(8,128)S(1)} collective-permute-done((f32[2,64,128]{2,1,0:T(8,128)S(1)}, f32[2,64,128]{2,1,0:T(8,128)S(1)}, u32[]{:S(2)}, u32[]{:S(2)}) %collective-permute-start.14) | collective-permute-done | bytes 65568 | tf_op jit(solution)/shard_map/ppermute | solution.py:634
  57.0 2.7 %collective-permute-start.15 = (f32[2,64,128]{2,1,0:T(8,128)S(1)}, f32[2,64,128]{2,1,0:T(8,128)S(1)}, u32[]{:S(2)}, u32[]{:S(2)}) collective-permute-start(f32[2,64,128]{2,1,0:T(8,128)S(1)} %add_kernel.1.mine), channel_id=1, source_target_pairs={{0,16},{1,17},{2,18},{3,19},{4,20},{5,21},{6,22},{7,23},{8,24},{9,... | collective-permute-start | bytes 196616 | tf_op jit(solution)/shard_map/ppermute | solution.py:634
  59.6 2.6 %collective-permute-done.15.other = f32[2,64,128]{2,1,0:T(8,128)S(1)} collective-permute-done((f32[2,64,128]{2,1,0:T(8,128)S(1)}, f32[2,64,128]{2,1,0:T(8,128)S(1)}, u32[]{:S(2)}, u32[]{:S(2)}) %collective-permute-start.15) | collective-permute-done | bytes 65568 | tf_op jit(solution)/shard_map/ppermute | solution.py:634
  62.2 0.0 copy-done.2
  62.2 0.1 sums_kernel.1
  62.3 1.6 %collective-permute-start.16 = (f32[136,128]{1,0:T(8,128)S(1)}, f32[136,128]{1,0:T(8,128)S(1)}, u32[]{:S(2)}, u32[]{:S(2)}) collective-permute-start(f32[136,128]{1,0:T(8,128)S(1)} %get-tuple-element.52.mine), channel_id=1, source_target_pairs={{0,8},{1,9},{2,10},{3,11},{4,12},{5,13},{6,14},{7,15},{8,0},{9,1},... | collective-permute-start | bytes 208904 | tf_op jit(solution)/shard_map/ppermute | solution.py:634
  63.9 0.0 collective-permute-start.17
  63.9 0.6 collective-permute-start.18
  64.5 0.6 collective-permute-done.17.s1
  65.1 1.9 %collective-permute-done.18.s2 = f32[8,128]{1,0:T(8,128)S(1)} collective-permute-done((f32[8,128]{1,0:T(8,128)S(1)}, f32[8,128]{1,0:T(8,128)S(1)}, u32[]{:S(2)}, u32[]{:S(2)}) %collective-permute-start.18) | collective-permute-done | bytes 4128 | tf_op jit(solution)/shard_map/ppermute | solution.py:634
  66.9 0.0 collective-permute-done.16.other
  67.0 1.5 %collective-permute-start.20 = (f32[264,128]{1,0:T(8,128)S(1)}, f32[264,128]{1,0:T(8,128)S(1)}, u32[]{:S(2)}, u32[]{:S(2)}) collective-permute-start(f32[264,128]{1,0:T(8,128)S(1)} %get-tuple-element.55.mine), channel_id=1, source_target_pairs={{0,4},{1,5},{2,6},{3,7},{4,0},{5,1},{6,2},{7,3},{8,12},{9,13},{10,... | collective-permute-start | bytes 405512 | tf_op jit(solution)/shard_map/ppermute | solution.py:634
  68.5 1.5 %collective-permute-start.19 = (f32[8,128]{1,0:T(8,128)S(1)}, f32[8,128]{1,0:T(8,128)S(1)}, u32[]{:S(2)}, u32[]{:S(2)}) collective-permute-start(f32[8,128]{1,0:T(8,128)S(1)} %get-tuple-element.54.s0), channel_id=1, source_target_pairs={{0,6},{1,7},{2,4},{3,5},{4,2},{5,3},{6,0},{7,1},{8,14},{9,15},{10,... | collective-permute-start | bytes 12296 | tf_op jit(solution)/shard_map/ppermute | solution.py:634
  70.0 0.6 collective-permute-start.21
  70.5 2.5 %collective-permute-done.19.s2 = f32[8,128]{1,0:T(8,128)S(1)} collective-permute-done((f32[8,128]{1,0:T(8,128)S(1)}, f32[8,128]{1,0:T(8,128)S(1)}, u32[]{:S(2)}, u32[]{:S(2)}) %collective-permute-start.19) | collective-permute-done | bytes 4128 | tf_op jit(solution)/shard_map/ppermute | solution.py:634
  73.1 0.5 collective-permute-done.21.s1
  73.6 0.0 collective-permute-done.20.other
  73.6 0.8 %finish.1 = (f32[8,64,128]{2,1,0:T(8,128)}, f32[1]{0:T(128)}) custom-call(f32[8,128]{1,0:T(8,128)S(1)} %collective-permute-done.19.s2, f32[264,128]{1,0:T(8,128)S(1)} %collective-permute-done.20.other, f32[8,128]{1,0:T(8,128)S(1)} %collective-permute-done.21.s1, f32[264,128]{1,0:T(8,128)S(1)} %get-tuple-element.55.mine, f32[8,64,128]{2,1,0:T(8,128)S(1)} %copy-done.2, ...), custom_call_target="tpu_custom_call" | custom-call | tf_op jit(solution)/shard_map/finish/pallas_call | solution.py:746
  (11 shorter events, 0.1 us)
Async XLA Ops:
  2.8 12.4 %collective-permute-start = (f32[4,64,128]{2,1,0:T(8,128)}, f32[4,64,128]{2,1,0:T(8,128)S(1)}, u32[]{:S(2)}, u32[]{:S(2)}) collective-permute-start(f32[4,64,128]{2,1,0:T(8,128)} %get-tuple-element.31), channel_id=1, source_target_pairs={{0,2},{1,3},{2,0},{3,1},{4,6},{5,7},{6,4},{7,5},{8,10},{9,11},{10,... | collective-permute-start | bytes 393224 | tf_op jit(solution)/shard_map/ppermute | solution.py:634
  5.8 12.1 %copy-start = (f32[2,8,64,128]{3,2,1,0:T(8,128)S(1)}, f32[2,8,64,128]{3,2,1,0:T(8,128)}, u32[]{:S(2)}) copy-start(f32[2,8,64,128]{3,2,1,0:T(8,128)} %fwd_prev.1) | copy-start | bytes 1572868
  5.8 12.1 %copy-start.1 = (f32[2,8,64,128]{3,2,1,0:T(8,128)S(1)}, f32[2,8,64,128]{3,2,1,0:T(8,128)}, u32[]{:S(2)}) copy-start(f32[2,8,64,128]{3,2,1,0:T(8,128)} %fwd_cur.1) | copy-start | bytes 1572868
  5.8 12.1 %copy-start.3 = (f32[8,64,128]{2,1,0:T(8,128)S(1)}, f32[8,64,128]{2,1,0:T(8,128)}, u32[]{:S(2)}) copy-start(f32[8,64,128]{2,1,0:T(8,128)} %get-tuple-element.32.speed.own) | copy-start | bytes 786436
  5.8 12.1 %copy-start.4 = (f32[2,8,64,128]{3,2,1,0:T(8,128)S(1)}, f32[2,8,64,128]{3,2,1,0:T(8,128)}, u32[]{:S(2)}) copy-start(f32[2,8,64,128]{3,2,1,0:T(8,128)} %adj_next.1) | copy-start | bytes 1572868
  5.8 12.1 %copy-start.5 = (f32[2,8,64,128]{3,2,1,0:T(8,128)S(1)}, f32[2,8,64,128]{3,2,1,0:T(8,128)}, u32[]{:S(2)}) copy-start(f32[2,8,64,128]{3,2,1,0:T(8,128)} %adj_cur.1) | copy-start | bytes 1572868
  5.8 18.8 %copy-start.7 = (s32[2]{0:T(128)S(1)}, s32[2]{0:T(128)}, u32[]{:S(2)}) copy-start(s32[2]{0:T(128)} %sources.1) | copy-start | bytes 28
  5.8 15.8 %collective-permute-start.5 = (f32[2,8,64,128]{3,2,1,0:T(8,128)}, f32[2,8,64,128]{3,2,1,0:T(8,128)S(1)}, u32[]{:S(2)}, u32[]{:S(2)}) collective-permute-start(f32[2,8,64,128]{3,2,1,0:T(8,128)} %get-tuple-element.36), channel_id=1, source_target_pairs={{0,2},{1,3},{2,0},{3,1},{4,6},{5,7},{6,4},{7,5},{8,10},{9,11},{10,... | collective-permute-start | bytes 1572872 | tf_op jit(solution)/shard_map/ppermute | solution.py:634
  15.2 0.7 copy-start.6
  15.9 5.0 %collective-permute-start.4 = (f32[4,64,128]{2,1,0:T(8,128)S(1)}, f32[4,64,128]{2,1,0:T(8,128)S(1)}, u32[]{:S(2)}, u32[]{:S(2)}) collective-permute-start(f32[4,64,128]{2,1,0:T(8,128)S(1)} %after.3.earlier.mine), channel_id=1, source_target_pairs={{0,4},{1,5},{2,6},{3,7},{4,0},{5,1},{6,2},{7,3},{8,12},{9,13},{10,... | collective-permute-start | bytes 393224 | tf_op jit(solution)/shard_map/ppermute | solution.py:634
  19.3 3.1 %collective-permute-start.2 = (f32[8,64,128]{2,1,0:T(8,128)S(1)}, f32[8,64,128]{2,1,0:T(8,128)S(1)}, u32[]{:S(2)}, u32[]{:S(2)}) collective-permute-start(f32[8,64,128]{2,1,0:T(8,128)S(1)} %get-tuple-element.34.own0), channel_id=1, source_target_pairs={{0,1},{1,0},{2,3},{3,2},{4,5},{5,4},{6,7},{7,6},{8,9},{9,8},{10,11... | collective-permute-start | bytes 786440 | tf_op jit(solution)/shard_map/ppermute | solution.py:634
  19.4 14.6 %collective-permute-start.9 = (f32[2,8,64,128]{3,2,1,0:T(8,128)}, f32[2,8,64,128]{3,2,1,0:T(8,128)S(1)}, u32[]{:S(2)}, u32[]{:S(2)}) collective-permute-start(f32[2,8,64,128]{3,2,1,0:T(8,128)} %get-tuple-element.41), channel_id=1, source_target_pairs={{0,2},{1,3},{2,0},{3,1},{4,6},{5,7},{6,4},{7,5},{8,10},{9,11},{10,... | collective-permute-start | bytes 1572872 | tf_op jit(solution)/shard_map/ppermute | solution.py:634
  21.0 2.6 %collective-permute-start.8 = (f32[13,64,128]{2,1,0:T(8,128)S(1)}, f32[13,64,128]{2,1,0:T(8,128)S(1)}, u32[]{:S(2)}, u32[]{:S(2)}) collective-permute-start(f32[13,64,128]{2,1,0:T(8,128)S(1)} %arrange_kernel.1.earlier.speed), channel_id=1, source_target_pairs={{0,1},{1,0},{2,3},{3,2},{4,5},{5,4},{6,7},{7,6},{8,9},{9,8},{10,11... | collective-permute-start | bytes 1277960 | tf_op jit(solution)/shard_map/ppermute | solution.py:634
  21.1 2.3 %collective-permute-start.3 = (f32[11,64,128]{2,1,0:T(8,128)S(1)}, f32[11,64,128]{2,1,0:T(8,128)S(1)}, u32[]{:S(2)}, u32[]{:S(2)}) collective-permute-start(f32[11,64,128]{2,1,0:T(8,128)S(1)} %get-tuple-element.35.own1), channel_id=1, source_target_pairs={{0,1},{1,0},{2,3},{3,2},{4,5},{5,4},{6,7},{7,6},{8,9},{9,8},{10,11... | collective-permute-start | bytes 1081352 | tf_op jit(solution)/shard_map/ppermute | solution.py:634
  22.3 1.7 %collective-permute-start.6 = (f32[8,64,128]{2,1,0:T(8,128)S(1)}, f32[8,64,128]{2,1,0:T(8,128)}, u32[]{:S(2)}, u32[]{:S(2)}) collective-permute-start(f32[8,64,128]{2,1,0:T(8,128)S(1)} %get-tuple-element.37.over0), channel_id=1, source_target_pairs={{0,1},{1,0},{2,3},{3,2},{4,5},{5,4},{6,7},{7,6},{8,9},{9,8},{10,11... | collective-permute-start | bytes 786440 | tf_op jit(solution)/shard_map/ppermute | solution.py:634
  22.4 2.2 %collective-permute-start.7 = (f32[8,64,128]{2,1,0:T(8,128)}, f32[8,64,128]{2,1,0:T(8,128)}, u32[]{:S(2)}, u32[]{:S(2)}) collective-permute-start(f32[8,64,128]{2,1,0:T(8,128)} %get-tuple-element.38.over1), channel_id=1, source_target_pairs={{0,1},{1,0},{2,3},{3,2},{4,5},{5,4},{6,7},{7,6},{8,9},{9,8},{10,11... | collective-permute-start | bytes 786440 | tf_op jit(solution)/shard_map/ppermute | solution.py:634
  23.5 11.6 %collective-permute-start.1 = (f32[2,8,64,128]{3,2,1,0:T(8,128)S(1)}, f32[2,8,64,128]{3,2,1,0:T(8,128)S(1)}, u32[]{:S(2)}, u32[]{:S(2)}) collective-permute-start(f32[2,8,64,128]{3,2,1,0:T(8,128)S(1)} %get-tuple-element.33.own), channel_id=1, source_target_pairs={{0,1},{1,0},{2,3},{3,2},{4,5},{5,4},{6,7},{7,6},{8,9},{9,8},{10,11... | collective-permute-start | bytes 1572872 | tf_op jit(solution)/shard_map/ppermute | solution.py:634
  34.0 2.0 %collective-permute-start.10 = (f32[2,8,64,128]{3,2,1,0:T(8,128)S(1)}, f32[2,8,64,128]{3,2,1,0:T(8,128)S(1)}, u32[]{:S(2)}, u32[]{:S(2)}) collective-permute-start(f32[2,8,64,128]{3,2,1,0:T(8,128)S(1)} %after.5.over), channel_id=1, source_target_pairs={{0,1},{1,0},{2,3},{3,2},{4,5},{5,4},{6,7},{7,6},{8,9},{9,8},{10,11... | collective-permute-start | bytes 1572872 | tf_op jit(solution)/shard_map/ppermute | solution.py:634
  35.9 26.3 %copy-start.2 = (f32[8,64,128]{2,1,0:T(8,128)S(1)}, f32[8,64,128]{2,1,0:T(8,128)}, u32[]{:S(2)}) copy-start(f32[8,64,128]{2,1,0:T(8,128)} %momentum.3) | copy-start | bytes 786436
  42.9 6.6 %collective-permute-start.11 = (f32[4,64,128]{2,1,0:T(8,128)S(1)}, f32[4,64,128]{2,1,0:T(8,128)S(1)}, u32[]{:S(2)}, u32[]{:S(2)}) collective-permute-start(f32[4,64,128]{2,1,0:T(8,128)S(1)} %get-tuple-element.47), channel_id=1, source_target_pairs={{0,6},{1,7},{2,4},{3,5},{4,2},{5,3},{6,0},{7,1},{8,14},{9,15},{10,... | collective-permute-start | bytes 393224 | tf_op jit(solution)/shard_map/ppermute | solution.py:634
  45.6 6.6 %collective-permute-start.12 = (f32[4,64,128]{2,1,0:T(8,128)S(1)}, f32[4,64,128]{2,1,0:T(8,128)S(1)}, u32[]{:S(2)}, u32[]{:S(2)}) collective-permute-start(f32[4,64,128]{2,1,0:T(8,128)S(1)} %get-tuple-element.48), channel_id=1, source_target_pairs={{0,4},{1,5},{2,6},{3,7},{4,0},{5,1},{6,2},{7,3},{8,12},{9,13},{10,... | collective-permute-start | bytes 393224 | tf_op jit(solution)/shard_map/ppermute | solution.py:634
  46.1 6.5 %collective-permute-start.13 = (f32[4,64,128]{2,1,0:T(8,128)S(1)}, f32[4,64,128]{2,1,0:T(8,128)S(1)}, u32[]{:S(2)}, u32[]{:S(2)}) collective-permute-start(f32[4,64,128]{2,1,0:T(8,128)S(1)} %get-tuple-element.49), channel_id=1, source_target_pairs={{0,2},{1,3},{2,0},{3,1},{4,6},{5,7},{6,4},{7,5},{8,10},{9,11},{10,... | collective-permute-start | bytes 393224 | tf_op jit(solution)/shard_map/ppermute | solution.py:634
  52.6 4.3 %collective-permute-start.14 = (f32[2,64,128]{2,1,0:T(8,128)S(1)}, f32[2,64,128]{2,1,0:T(8,128)S(1)}, u32[]{:S(2)}, u32[]{:S(2)}) collective-permute-start(f32[2,64,128]{2,1,0:T(8,128)S(1)} %get-tuple-element.51), channel_id=1, source_target_pairs={{0,8},{1,9},{2,10},{3,11},{4,12},{5,13},{6,14},{7,15},{8,0},{9,1},... | collective-permute-start | bytes 196616 | tf_op jit(solution)/shard_map/ppermute | solution.py:634
  57.0 5.2 %collective-permute-start.15 = (f32[2,64,128]{2,1,0:T(8,128)S(1)}, f32[2,64,128]{2,1,0:T(8,128)S(1)}, u32[]{:S(2)}, u32[]{:S(2)}) collective-permute-start(f32[2,64,128]{2,1,0:T(8,128)S(1)} %add_kernel.1.mine), channel_id=1, source_target_pairs={{0,16},{1,17},{2,18},{3,19},{4,20},{5,21},{6,22},{7,23},{8,24},{9,... | collective-permute-start | bytes 196616 | tf_op jit(solution)/shard_map/ppermute | solution.py:634
  62.3 4.6 %collective-permute-start.16 = (f32[136,128]{1,0:T(8,128)S(1)}, f32[136,128]{1,0:T(8,128)S(1)}, u32[]{:S(2)}, u32[]{:S(2)}) collective-permute-start(f32[136,128]{1,0:T(8,128)S(1)} %get-tuple-element.52.mine), channel_id=1, source_target_pairs={{0,8},{1,9},{2,10},{3,11},{4,12},{5,13},{6,14},{7,15},{8,0},{9,1},... | collective-permute-start | bytes 208904 | tf_op jit(solution)/shard_map/ppermute | solution.py:634
  63.9 1.2 %collective-permute-start.17 = (f32[8,128]{1,0:T(8,128)S(1)}, f32[8,128]{1,0:T(8,128)S(1)}, u32[]{:S(2)}, u32[]{:S(2)}) collective-permute-start(f32[8,128]{1,0:T(8,128)S(1)} %get-tuple-element.53.s0), channel_id=1, source_target_pairs={{0,1},{1,0},{2,3},{3,2},{4,5},{5,4},{6,7},{7,6},{8,9},{9,8},{10,11... | collective-permute-start | bytes 12296 | tf_op jit(solution)/shard_map/ppermute | solution.py:634
  63.9 3.0 %collective-permute-start.18 = (f32[8,128]{1,0:T(8,128)S(1)}, f32[8,128]{1,0:T(8,128)S(1)}, u32[]{:S(2)}, u32[]{:S(2)}) collective-permute-start(f32[8,128]{1,0:T(8,128)S(1)} %get-tuple-element.53.s0), channel_id=1, source_target_pairs={{0,9},{1,8},{2,11},{3,10},{4,13},{5,12},{6,15},{7,14},{8,1},{9,0},... | collective-permute-start | bytes 12296 | tf_op jit(solution)/shard_map/ppermute | solution.py:634
  67.0 6.6 %collective-permute-start.20 = (f32[264,128]{1,0:T(8,128)S(1)}, f32[264,128]{1,0:T(8,128)S(1)}, u32[]{:S(2)}, u32[]{:S(2)}) collective-permute-start(f32[264,128]{1,0:T(8,128)S(1)} %get-tuple-element.55.mine), channel_id=1, source_target_pairs={{0,4},{1,5},{2,6},{3,7},{4,0},{5,1},{6,2},{7,3},{8,12},{9,13},{10,... | collective-permute-start | bytes 405512 | tf_op jit(solution)/shard_map/ppermute | solution.py:634
  68.5 4.6 %collective-permute-start.19 = (f32[8,128]{1,0:T(8,128)S(1)}, f32[8,128]{1,0:T(8,128)S(1)}, u32[]{:S(2)}, u32[]{:S(2)}) collective-permute-start(f32[8,128]{1,0:T(8,128)S(1)} %get-tuple-element.54.s0), channel_id=1, source_target_pairs={{0,6},{1,7},{2,4},{3,5},{4,2},{5,3},{6,0},{7,1},{8,14},{9,15},{10,... | collective-permute-start | bytes 12296 | tf_op jit(solution)/shard_map/ppermute | solution.py:634
  70.0 3.6 %collective-permute-start.21 = (f32[8,128]{1,0:T(8,128)S(1)}, f32[8,128]{1,0:T(8,128)S(1)}, u32[]{:S(2)}, u32[]{:S(2)}) collective-permute-start(f32[8,128]{1,0:T(8,128)S(1)} %get-tuple-element.54.s0), channel_id=1, source_target_pairs={{0,2},{1,3},{2,0},{3,1},{4,6},{5,7},{6,4},{7,5},{8,10},{9,11},{10,... | collective-permute-start | bytes 12296 | tf_op jit(solution)/shard_map/ppermute | solution.py:634

commit v19 on v17

--- a/solution.py
+++ b/solution.py
@@ -357,14 +357,15 @@
 PLANES = 2
 
 
-def sweep(core, planes, field, banded, y_first, y_second, work):
+def sweep(core, planes, field, banded, y_first, y_second, work, newer=None):
     order = [(chip, owned) for owned in (True, False) for chip in (0, 1)]
     parts = (y_first, y_second)
 
     def first(chip, owned):
         return (2 * chip + (core if owned else 1 - core)) * planes
 
-    along_y(field, first(*order[0]), banded, y_first)
+    if newer is None:
+        along_y(field, first(*order[0]), banded, y_first)
     for owned in (True, False):
         for chip in (0, 1):
             z = first(chip, owned)
@@ -373,6 +374,8 @@
                 last = n == planes // BATCH - 1
                 if not last or chip == 0 or owned:
                     along_y(field, onward if last else z + (n + 1) * BATCH, banded, parts[(n + 1) % 2])
+                elif newer is not None:
+                    along_y(newer, first(*order[0]), banded, y_first)
                 work(z + n * BATCH, parts[n % 2], chip if owned else None, n * BATCH)
 
 
@@ -489,7 +492,9 @@
 
             laps12(now, z, y_part, fetch, finish)
 
-        sweep(core, planes, now, banded, y0, y1, work)
+        sweep(core, planes, now, banded, y0, y1, work, then)
+
+    along_y(even, core * planes, banded, y0)
 
     @pl.loop(0, steps // 2)
     def _(pair):

time: 74.8 us -> 75.4 us (level)
  no operation moved by 1% of the time
where the time goes in v19:
time: 75.4 us; the launch traced here: 75.2 us
  Pallas kernels  32.3 us (43%)
  starting transfers between devices  21.6 us (29%)
  waiting for transfers between devices  19.2 us (25%)
  between operations  1.43 us (2%)
    ppermute x22, starting transfers between devices, exchange(): lax.ppermute(value, axes, [(i, i ^ bits) for i in range(lax.axis_size(axe...  21.6 us
    ppermute x22, waiting for transfers between devices, exchange(): lax.ppermute(value, axes, [(i, i ^ bits) for i in range(lax.axis_size(axe...  19.2 us
    pallas_call x1, Pallas kernels, scatter(): pl.pallas_call(functools.partial(scatter_kernel, rows_x), grid=(rows_all...  9.27 us
    pallas_call x1, Pallas kernels, whole_shards(): pl.pallas_call(forward_kernel, in_specs=[smem, smem] + [vmem] * 10 + [pl....  9.17 us
    pallas_call x1, Pallas kernels, whole_shards(): pl.pallas_call(adjoint_kernel, in_specs=[vmem] * 8, out_specs=[vmem] * 4,...  7.65 us
    pallas_call x1, Pallas kernels, whole_shards(): pl.pallas_call(first_kernel, in_specs=[hbm] * 3, out_specs=[vmem] * 3, ou...  2.13 us
  transfers between devices with their start and end apart: 22, of which 14 were waited for; matrix products, arithmetic and copies ran while one was open for 0% of the time, Pallas kernels for 29%

profile of v19, /device:TPU:0, one launch (start us, length us, event | category | flops | bytes accessed | tf_op | source)
XLA Modules:
  0.0 75.2 jit_solution(5430624968722829738)
XLA Ops:
  0.6 2.1 %first_to_cross.1 = (f32[2,8,64,128]{3,2,1,0:T(8,128)}, f32[8,64,128]{2,1,0:T(8,128)}, f32[4,64,128]{2,1,0:T(8,128)}) custom-call(f32[2,8,64,128]{3,2,1,0:T(8,128)} %fwd_prev.1, f32[2,8,64,128]{3,2,1,0:T(8,128)} %fwd_cur.1, f32[8,64,128]{2,1,0:T(8,128)} %courant.1), custom_call_target="tpu_custom_call" | custom-call | tf_op jit(solution)/shard_map/first_to_cross/pallas_call | solution.py:655
  2.8 3.0 %collective-permute-start = (f32[4,64,128]{2,1,0:T(8,128)}, f32[4,64,128]{2,1,0:T(8,128)S(1)}, u32[]{:S(2)}, u32[]{:S(2)}) collective-permute-start(f32[4,64,128]{2,1,0:T(8,128)} %get-tuple-element.31), channel_id=1, source_target_pairs={{0,2},{1,3},{2,0},{3,1},{4,6},{5,7},{6,4},{7,5},{8,10},{9,11},{10,... | collective-permute-start | bytes 393224 | tf_op jit(solution)/shard_map/ppermute | solution.py:639
  5.8 0.0 copy-start
  5.8 0.0 copy-start.5
  5.8 0.0 copy-start.7
  5.8 0.1 collective-permute-start.5
  5.9 9.3 %receiver_scatter.1 = (f32[9,2048,128]{2,1,0:T(8,128)}, f32[8,128]{1,0:T(8,128)}) custom-call(s32[2,512]{1,0:T(2,128)} %cells_ref.1, f32[2,8,512]{2,1,0:T(8,128)} %observed_ref.1), custom_call_target="tpu_custom_call" | custom-call | flops 4831838208 | bytes 9437184 | tf_op jit(solution)/shard_map/receiver_scatter/pallas_call | solution.py:305
  15.2 0.0 collective-permute-done.value
  15.2 0.7 copy-done.6
  15.9 2.0 %collective-permute-start.4 = (f32[4,64,128]{2,1,0:T(8,128)S(1)}, f32[4,64,128]{2,1,0:T(8,128)S(1)}, u32[]{:S(2)}, u32[]{:S(2)}) collective-permute-start(f32[4,64,128]{2,1,0:T(8,128)S(1)} %after.3.earlier.mine), channel_id=1, source_target_pairs={{0,4},{1,5},{2,6},{3,7},{4,0},{5,1},{6,2},{7,3},{8,12},{9,13},{10,... | collective-permute-start | bytes 393224 | tf_op jit(solution)/shard_map/ppermute | solution.py:639
  17.9 0.0 copy-done
  17.9 0.0 copy-done.1
  17.9 0.0 copy-done.3
  17.9 0.0 copy-done.4
  17.9 0.0 copy-done.5
  17.9 1.4 %pick.1 = (f32[2,8,64,128]{3,2,1,0:T(8,128)}, f32[2,8,64,128]{3,2,1,0:T(8,128)S(1)}, f32[8,64,128]{2,1,0:T(8,128)S(1)}, f32[11,64,128]{2,1,0:T(8,128)S(1)}) custom-call(f32[4,64,128]{2,1,0:T(8,128)S(1)} %after.3.earlier.mine, f32[2,8,64,128]{3,2,1,0:T(8,128)S(1)} %copy-done.4, f32[2,8,64,128]{3,2,1,0:T(8,128)S(1)} %copy-done.5, ...), custom_call_target="tpu_custom_call" | custom-call | tf_op jit(solution)/shard_map/pick/pallas_call | solution.py:173
  19.3 0.1 collective-permute-start.2
  19.4 1.5 %collective-permute-start.9 = (f32[2,8,64,128]{3,2,1,0:T(8,128)}, f32[2,8,64,128]{3,2,1,0:T(8,128)S(1)}, u32[]{:S(2)}, u32[]{:S(2)}) collective-permute-start(f32[2,8,64,128]{3,2,1,0:T(8,128)} %get-tuple-element.41), channel_id=1, source_target_pairs={{0,2},{1,3},{2,0},{3,1},{4,6},{5,7},{6,4},{7,5},{8,10},{9,11},{10,... | collective-permute-start | bytes 1572872 | tf_op jit(solution)/shard_map/ppermute | solution.py:639
  20.8 0.1 collective-permute-done.4.other
  21.0 0.1 collective-permute-start.8
  21.1 0.4 collective-permute-start.3
  21.6 0.0 collective-permute-done.5.value
  21.6 0.7 after.4
  22.3 0.1 collective-permute-start.6
  22.4 0.0 collective-permute-done.2.mate0
  22.4 0.4 collective-permute-start.7
  23.5 0.0 collective-permute-done.3.mate1
  23.5 0.1 collective-permute-start.1
  23.6 0.0 collective-permute-done.8.speed_mate
  23.6 0.3 collective-permute-done.6.far0
  24.0 0.6 collective-permute-done.7.far1
  24.6 0.0 copy-done.7
  24.6 9.2 %forward_steps.1 = (f32[8,8,2,64,128]{4,3,2,1,0:T(8,128)S(1)}, f32[8,32,64,128]{3,2,1,0:T(8,128)S(1)}, f32[9,32,64,128]{3,2,1,0:T(8,128)S(1)}, f32[32,64,128]{2,1,0:T(8,128)S(1)}, f32[16,64,128]{2,1,0:T(8,128)S(1)}) custom-call(s32[1]{0:T(128)} %bitcast.3.start, s32[2]{0:T(128)S(1)} %copy-done.7, f32[8,64,128]{2,1,0:T(8,128)S(1)} %get-tuple-element.34.own0, ...), custom_call_target="tpu_custom_call" | custom-call | flops 1000 | bytes 1000 | tf_op jit(solution)/shard_map/forward_steps/pallas_call | solution.py:695
  33.7 0.2 collective-permute-done.9.value
  34.0 0.1 collective-permute-start.10
  34.0 1.0 %inject.1 = f32[8,32,64,128]{3,2,1,0:T(8,128)S(1)} custom-call(f32[9,32,64,128]{3,2,1,0:T(8,128)S(1)} %get-tuple-element.43.held, f32[8,32,64,128]{3,2,1,0:T(8,128)S(1)} %get-tuple-element.44.history), custom_call_target="tpu_custom_call" | custom-call | tf_op jit(solution)/shard_map/inject/pallas_call | solution.py:719
  35.0 0.0 collective-permute-done.1.mate
  35.0 0.9 %collective-permute-done.10.far = f32[2,8,64,128]{3,2,1,0:T(8,128)S(1)} collective-permute-done((f32[2,8,64,128]{3,2,1,0:T(8,128)S(1)}, f32[2,8,64,128]{3,2,1,0:T(8,128)S(1)}, u32[]{:S(2)}, u32[]{:S(2)}) %collective-permute-start.10) | collective-permute-done | bytes 524320 | tf_op jit(solution)/shard_map/ppermute | solution.py:639
  35.9 7.6 %adjoint_steps.1 = (f32[4,64,128]{2,1,0:T(8,128)S(1)}, f32[4,64,128]{2,1,0:T(8,128)S(1)}, f32[4,64,128]{2,1,0:T(8,128)S(1)}, f32[4,64,128]{2,1,0:T(8,128)S(1)}) custom-call(f32[2,8,64,128]{3,2,1,0:T(8,128)S(1)} %get-tuple-element.33.own, f32[2,8,64,128]{3,2,1,0:T(8,128)S(1)} %collective-permute-done.1.mate, f32[2,8,64,128]{3,2,1,0:T(8,128)S(1)} %after.5.over, ...), custom_call_target="tpu_custom_call" | custom-call | flops 62914560 | bytes 33554432 | tf_op jit(solution)/shard_map/adjoint_steps/pallas_call | solution.py:729
  43.6 2.7 %collective-permute-start.11 = (f32[4,64,128]{2,1,0:T(8,128)S(1)}, f32[4,64,128]{2,1,0:T(8,128)S(1)}, u32[]{:S(2)}, u32[]{:S(2)}) collective-permute-start(f32[4,64,128]{2,1,0:T(8,128)S(1)} %get-tuple-element.47), channel_id=1, source_target_pairs={{0,6},{1,7},{2,4},{3,5},{4,2},{5,3},{6,0},{7,1},{8,14},{9,15},{10,... | collective-permute-start | bytes 393224 | tf_op jit(solution)/shard_map/ppermute | solution.py:639
  46.3 0.5 collective-permute-start.12
  46.8 0.4 collective-permute-start.13
  47.2 3.1 %collective-permute-done.11.by_xy = f32[4,64,128]{2,1,0:T(8,128)S(1)} collective-permute-done((f32[4,64,128]{2,1,0:T(8,128)S(1)}, f32[4,64,128]{2,1,0:T(8,128)S(1)}, u32[]{:S(2)}, u32[]{:S(2)}) %collective-permute-start.11) | collective-permute-done | bytes 131104 | tf_op jit(solution)/shard_map/ppermute | solution.py:639
  50.2 2.7 %collective-permute-done.12.by_y = f32[4,64,128]{2,1,0:T(8,128)S(1)} collective-permute-done((f32[4,64,128]{2,1,0:T(8,128)S(1)}, f32[4,64,128]{2,1,0:T(8,128)S(1)}, u32[]{:S(2)}, u32[]{:S(2)}) %collective-permute-start.12) | collective-permute-done | bytes 131104 | tf_op jit(solution)/shard_map/ppermute | solution.py:639
  52.9 0.3 collective-permute-done.13.by_x
  53.3 1.7 %collective-permute-start.14 = (f32[2,64,128]{2,1,0:T(8,128)S(1)}, f32[2,64,128]{2,1,0:T(8,128)S(1)}, u32[]{:S(2)}, u32[]{:S(2)}) collective-permute-start(f32[2,64,128]{2,1,0:T(8,128)S(1)} %get-tuple-element.51), channel_id=1, source_target_pairs={{0,8},{1,9},{2,10},{3,11},{4,12},{5,13},{6,14},{7,15},{8,0},{9,1},... | collective-permute-start | bytes 196616 | tf_op jit(solution)/shard_map/ppermute | solution.py:639
  54.9 2.7 %collective-permute-done.14.other = f32[2,64,128]{2,1,0:T(8,128)S(1)} collective-permute-done((f32[2,64,128]{2,1,0:T(8,128)S(1)}, f32[2,64,128]{2,1,0:T(8,128)S(1)}, u32[]{:S(2)}, u32[]{:S(2)}) %collective-permute-start.14) | collective-permute-done | bytes 65568 | tf_op jit(solution)/shard_map/ppermute | solution.py:639
  57.6 2.7 %collective-permute-start.15 = (f32[2,64,128]{2,1,0:T(8,128)S(1)}, f32[2,64,128]{2,1,0:T(8,128)S(1)}, u32[]{:S(2)}, u32[]{:S(2)}) collective-permute-start(f32[2,64,128]{2,1,0:T(8,128)S(1)} %add_kernel.1.mine), channel_id=1, source_target_pairs={{0,16},{1,17},{2,18},{3,19},{4,20},{5,21},{6,22},{7,23},{8,24},{9,... | collective-permute-start | bytes 196616 | tf_op jit(solution)/shard_map/ppermute | solution.py:639
  60.3 2.6 %collective-permute-done.15.other = f32[2,64,128]{2,1,0:T(8,128)S(1)} collective-permute-done((f32[2,64,128]{2,1,0:T(8,128)S(1)}, f32[2,64,128]{2,1,0:T(8,128)S(1)}, u32[]{:S(2)}, u32[]{:S(2)}) %collective-permute-start.15) | collective-permute-done | bytes 65568 | tf_op jit(solution)/shard_map/ppermute | solution.py:639
  62.9 0.0 copy-done.2
  62.9 0.1 sums_kernel.1
  63.0 1.6 %collective-permute-start.16 = (f32[136,128]{1,0:T(8,128)S(1)}, f32[136,128]{1,0:T(8,128)S(1)}, u32[]{:S(2)}, u32[]{:S(2)}) collective-permute-start(f32[136,128]{1,0:T(8,128)S(1)} %get-tuple-element.52.mine), channel_id=1, source_target_pairs={{0,8},{1,9},{2,10},{3,11},{4,12},{5,13},{6,14},{7,15},{8,0},{9,1},... | collective-permute-start | bytes 208904 | tf_op jit(solution)/shard_map/ppermute | solution.py:639
  64.6 0.0 collective-permute-start.17
  64.6 0.6 collective-permute-start.18
  65.1 0.6 collective-permute-done.17.s1
  65.8 1.9 %collective-permute-done.18.s2 = f32[8,128]{1,0:T(8,128)S(1)} collective-permute-done((f32[8,128]{1,0:T(8,128)S(1)}, f32[8,128]{1,0:T(8,128)S(1)}, u32[]{:S(2)}, u32[]{:S(2)}) %collective-permute-start.18) | collective-permute-done | bytes 4128 | tf_op jit(solution)/shard_map/ppermute | solution.py:639
  67.6 0.0 collective-permute-done.16.other
  67.6 1.5 %collective-permute-start.19 = (f32[264,128]{1,0:T(8,128)S(1)}, f32[264,128]{1,0:T(8,128)S(1)}, u32[]{:S(2)}, u32[]{:S(2)}) collective-permute-start(f32[264,128]{1,0:T(8,128)S(1)} %get-tuple-element.54.mine), channel_id=1, source_target_pairs={{0,4},{1,5},{2,6},{3,7},{4,0},{5,1},{6,2},{7,3},{8,12},{9,13},{10,... | collective-permute-start | bytes 405512 | tf_op jit(solution)/shard_map/ppermute | solution.py:639
  69.1 0.8 %collective-permute-start.20 = (f32[8,128]{1,0:T(8,128)S(1)}, f32[8,128]{1,0:T(8,128)S(1)}, u32[]{:S(2)}, u32[]{:S(2)}) collective-permute-start(f32[8,128]{1,0:T(8,128)S(1)} %get-tuple-element.55.s0), channel_id=1, source_target_pairs={{0,2},{1,3},{2,0},{3,1},{4,6},{5,7},{6,4},{7,5},{8,10},{9,11},{10,... | collective-permute-start | bytes 12296 | tf_op jit(solution)/shard_map/ppermute | solution.py:639
  69.9 1.3 %collective-permute-start.21 = (f32[8,128]{1,0:T(8,128)S(1)}, f32[8,128]{1,0:T(8,128)S(1)}, u32[]{:S(2)}, u32[]{:S(2)}) collective-permute-start(f32[8,128]{1,0:T(8,128)S(1)} %get-tuple-element.55.s0), channel_id=1, source_target_pairs={{0,6},{1,7},{2,4},{3,5},{4,2},{5,3},{6,0},{7,1},{8,14},{9,15},{10,... | collective-permute-start | bytes 12296 | tf_op jit(solution)/shard_map/ppermute | solution.py:639
  71.2 1.5 %collective-permute-done.20.s1 = f32[8,128]{1,0:T(8,128)S(1)} collective-permute-done((f32[8,128]{1,0:T(8,128)S(1)}, f32[8,128]{1,0:T(8,128)S(1)}, u32[]{:S(2)}, u32[]{:S(2)}) %collective-permute-start.20) | collective-permute-done | bytes 4128 | tf_op jit(solution)/shard_map/ppermute | solution.py:639
  72.7 1.7 %collective-permute-done.21.s2 = f32[8,128]{1,0:T(8,128)S(1)} collective-permute-done((f32[8,128]{1,0:T(8,128)S(1)}, f32[8,128]{1,0:T(8,128)S(1)}, u32[]{:S(2)}, u32[]{:S(2)}) %collective-permute-start.21) | collective-permute-done | bytes 4128 | tf_op jit(solution)/shard_map/ppermute | solution.py:639
  74.4 0.0 collective-permute-done.19.other
  74.4 0.8 %finish.1 = (f32[8,64,128]{2,1,0:T(8,128)}, f32[1]{0:T(128)}) custom-call(f32[264,128]{1,0:T(8,128)S(1)} %get-tuple-element.54.mine, f32[264,128]{1,0:T(8,128)S(1)} %collective-permute-done.19.other, f32[8,64,128]{2,1,0:T(8,128)S(1)} %copy-done.2, f32[8,128]{1,0:T(8,128)S(1)} %get-tuple-element.55.s0, f32[8,128]{1,0:T(8,128)S(1)} %collective-permute-done.20.s1, ...), custom_call_target="tpu_custom_call" | custom-call | tf_op jit(solution)/shard_map/finish/pallas_call | solution.py:751
  (11 shorter events, 0.1 us)
Async XLA Ops:
  2.8 12.4 %collective-permute-start = (f32[4,64,128]{2,1,0:T(8,128)}, f32[4,64,128]{2,1,0:T(8,128)S(1)}, u32[]{:S(2)}, u32[]{:S(2)}) collective-permute-start(f32[4,64,128]{2,1,0:T(8,128)} %get-tuple-element.31), channel_id=1, source_target_pairs={{0,2},{1,3},{2,0},{3,1},{4,6},{5,7},{6,4},{7,5},{8,10},{9,11},{10,... | collective-permute-start | bytes 393224 | tf_op jit(solution)/shard_map/ppermute | solution.py:639
  5.8 12.1 %copy-start = (f32[2,8,64,128]{3,2,1,0:T(8,128)S(1)}, f32[2,8,64,128]{3,2,1,0:T(8,128)}, u32[]{:S(2)}) copy-start(f32[2,8,64,128]{3,2,1,0:T(8,128)} %fwd_prev.1) | copy-start | bytes 1572868
  5.8 12.1 %copy-start.1 = (f32[2,8,64,128]{3,2,1,0:T(8,128)S(1)}, f32[2,8,64,128]{3,2,1,0:T(8,128)}, u32[]{:S(2)}) copy-start(f32[2,8,64,128]{3,2,1,0:T(8,128)} %fwd_cur.1) | copy-start | bytes 1572868
  5.8 12.1 %copy-start.3 = (f32[8,64,128]{2,1,0:T(8,128)S(1)}, f32[8,64,128]{2,1,0:T(8,128)}, u32[]{:S(2)}) copy-start(f32[8,64,128]{2,1,0:T(8,128)} %get-tuple-element.32.speed.own) | copy-start | bytes 786436
  5.8 12.1 %copy-start.4 = (f32[2,8,64,128]{3,2,1,0:T(8,128)S(1)}, f32[2,8,64,128]{3,2,1,0:T(8,128)}, u32[]{:S(2)}) copy-start(f32[2,8,64,128]{3,2,1,0:T(8,128)} %adj_next.1) | copy-start | bytes 1572868
  5.8 12.1 %copy-start.5 = (f32[2,8,64,128]{3,2,1,0:T(8,128)S(1)}, f32[2,8,64,128]{3,2,1,0:T(8,128)}, u32[]{:S(2)}) copy-start(f32[2,8,64,128]{3,2,1,0:T(8,128)} %adj_cur.1) | copy-start | bytes 1572868
  5.8 18.8 %copy-start.7 = (s32[2]{0:T(128)S(1)}, s32[2]{0:T(128)}, u32[]{:S(2)}) copy-start(s32[2]{0:T(128)} %sources.1) | copy-start | bytes 28
  5.8 15.8 %collective-permute-start.5 = (f32[2,8,64,128]{3,2,1,0:T(8,128)}, f32[2,8,64,128]{3,2,1,0:T(8,128)S(1)}, u32[]{:S(2)}, u32[]{:S(2)}) collective-permute-start(f32[2,8,64,128]{3,2,1,0:T(8,128)} %get-tuple-element.36), channel_id=1, source_target_pairs={{0,2},{1,3},{2,0},{3,1},{4,6},{5,7},{6,4},{7,5},{8,10},{9,11},{10,... | collective-permute-start | bytes 1572872 | tf_op jit(solution)/shard_map/ppermute | solution.py:639
  15.2 0.7 copy-start.6
  15.9 5.0 %collective-permute-start.4 = (f32[4,64,128]{2,1,0:T(8,128)S(1)}, f32[4,64,128]{2,1,0:T(8,128)S(1)}, u32[]{:S(2)}, u32[]{:S(2)}) collective-permute-start(f32[4,64,128]{2,1,0:T(8,128)S(1)} %after.3.earlier.mine), channel_id=1, source_target_pairs={{0,4},{1,5},{2,6},{3,7},{4,0},{5,1},{6,2},{7,3},{8,12},{9,13},{10,... | collective-permute-start | bytes 393224 | tf_op jit(solution)/shard_map/ppermute | solution.py:639
  19.3 3.1 %collective-permute-start.2 = (f32[8,64,128]{2,1,0:T(8,128)S(1)}, f32[8,64,128]{2,1,0:T(8,128)S(1)}, u32[]{:S(2)}, u32[]{:S(2)}) collective-permute-start(f32[8,64,128]{2,1,0:T(8,128)S(1)} %get-tuple-element.34.own0), channel_id=1, source_target_pairs={{0,1},{1,0},{2,3},{3,2},{4,5},{5,4},{6,7},{7,6},{8,9},{9,8},{10,11... | collective-permute-start | bytes 786440 | tf_op jit(solution)/shard_map/ppermute | solution.py:639
  19.4 14.6 %collective-permute-start.9 = (f32[2,8,64,128]{3,2,1,0:T(8,128)}, f32[2,8,64,128]{3,2,1,0:T(8,128)S(1)}, u32[]{:S(2)}, u32[]{:S(2)}) collective-permute-start(f32[2,8,64,128]{3,2,1,0:T(8,128)} %get-tuple-element.41), channel_id=1, source_target_pairs={{0,2},{1,3},{2,0},{3,1},{4,6},{5,7},{6,4},{7,5},{8,10},{9,11},{10,... | collective-permute-start | bytes 1572872 | tf_op jit(solution)/shard_map/ppermute | solution.py:639
  21.0 2.6 %collective-permute-start.8 = (f32[13,64,128]{2,1,0:T(8,128)S(1)}, f32[13,64,128]{2,1,0:T(8,128)S(1)}, u32[]{:S(2)}, u32[]{:S(2)}) collective-permute-start(f32[13,64,128]{2,1,0:T(8,128)S(1)} %arrange_kernel.1.earlier.speed), channel_id=1, source_target_pairs={{0,1},{1,0},{2,3},{3,2},{4,5},{5,4},{6,7},{7,6},{8,9},{9,8},{10,11... | collective-permute-start | bytes 1277960 | tf_op jit(solution)/shard_map/ppermute | solution.py:639
  21.1 2.3 %collective-permute-start.3 = (f32[11,64,128]{2,1,0:T(8,128)S(1)}, f32[11,64,128]{2,1,0:T(8,128)S(1)}, u32[]{:S(2)}, u32[]{:S(2)}) collective-permute-start(f32[11,64,128]{2,1,0:T(8,128)S(1)} %get-tuple-element.35.own1), channel_id=1, source_target_pairs={{0,1},{1,0},{2,3},{3,2},{4,5},{5,4},{6,7},{7,6},{8,9},{9,8},{10,11... | collective-permute-start | bytes 1081352 | tf_op jit(solution)/shard_map/ppermute | solution.py:639
  22.3 1.7 %collective-permute-start.6 = (f32[8,64,128]{2,1,0:T(8,128)S(1)}, f32[8,64,128]{2,1,0:T(8,128)}, u32[]{:S(2)}, u32[]{:S(2)}) collective-permute-start(f32[8,64,128]{2,1,0:T(8,128)S(1)} %get-tuple-element.37.over0), channel_id=1, source_target_pairs={{0,1},{1,0},{2,3},{3,2},{4,5},{5,4},{6,7},{7,6},{8,9},{9,8},{10,11... | collective-permute-start | bytes 786440 | tf_op jit(solution)/shard_map/ppermute | solution.py:639
  22.4 2.2 %collective-permute-start.7 = (f32[8,64,128]{2,1,0:T(8,128)}, f32[8,64,128]{2,1,0:T(8,128)}, u32[]{:S(2)}, u32[]{:S(2)}) collective-permute-start(f32[8,64,128]{2,1,0:T(8,128)} %get-tuple-element.38.over1), channel_id=1, source_target_pairs={{0,1},{1,0},{2,3},{3,2},{4,5},{5,4},{6,7},{7,6},{8,9},{9,8},{10,11... | collective-permute-start | bytes 786440 | tf_op jit(solution)/shard_map/ppermute | solution.py:639
  23.5 11.6 %collective-permute-start.1 = (f32[2,8,64,128]{3,2,1,0:T(8,128)S(1)}, f32[2,8,64,128]{3,2,1,0:T(8,128)S(1)}, u32[]{:S(2)}, u32[]{:S(2)}) collective-permute-start(f32[2,8,64,128]{3,2,1,0:T(8,128)S(1)} %get-tuple-element.33.own), channel_id=1, source_target_pairs={{0,1},{1,0},{2,3},{3,2},{4,5},{5,4},{6,7},{7,6},{8,9},{9,8},{10,11... | collective-permute-start | bytes 1572872 | tf_op jit(solution)/shard_map/ppermute | solution.py:639
  34.0 2.0 %collective-permute-start.10 = (f32[2,8,64,128]{3,2,1,0:T(8,128)S(1)}, f32[2,8,64,128]{3,2,1,0:T(8,128)S(1)}, u32[]{:S(2)}, u32[]{:S(2)}) collective-permute-start(f32[2,8,64,128]{3,2,1,0:T(8,128)S(1)} %after.5.over), channel_id=1, source_target_pairs={{0,1},{1,0},{2,3},{3,2},{4,5},{5,4},{6,7},{7,6},{8,9},{9,8},{10,11... | collective-permute-start | bytes 1572872 | tf_op jit(solution)/shard_map/ppermute | solution.py:639
  35.9 26.9 %copy-start.2 = (f32[8,64,128]{2,1,0:T(8,128)S(1)}, f32[8,64,128]{2,1,0:T(8,128)}, u32[]{:S(2)}) copy-start(f32[8,64,128]{2,1,0:T(8,128)} %momentum.3) | copy-start | bytes 786436
  43.6 6.6 %collective-permute-start.11 = (f32[4,64,128]{2,1,0:T(8,128)S(1)}, f32[4,64,128]{2,1,0:T(8,128)S(1)}, u32[]{:S(2)}, u32[]{:S(2)}) collective-permute-start(f32[4,64,128]{2,1,0:T(8,128)S(1)} %get-tuple-element.47), channel_id=1, source_target_pairs={{0,6},{1,7},{2,4},{3,5},{4,2},{5,3},{6,0},{7,1},{8,14},{9,15},{10,... | collective-permute-start | bytes 393224 | tf_op jit(solution)/shard_map/ppermute | solution.py:639
  46.3 6.6 %collective-permute-start.12 = (f32[4,64,128]{2,1,0:T(8,128)S(1)}, f32[4,64,128]{2,1,0:T(8,128)S(1)}, u32[]{:S(2)}, u32[]{:S(2)}) collective-permute-start(f32[4,64,128]{2,1,0:T(8,128)S(1)} %get-tuple-element.48), channel_id=1, source_target_pairs={{0,4},{1,5},{2,6},{3,7},{4,0},{5,1},{6,2},{7,3},{8,12},{9,13},{10,... | collective-permute-start | bytes 393224 | tf_op jit(solution)/shard_map/ppermute | solution.py:639
  46.8 6.5 %collective-permute-start.13 = (f32[4,64,128]{2,1,0:T(8,128)S(1)}, f32[4,64,128]{2,1,0:T(8,128)S(1)}, u32[]{:S(2)}, u32[]{:S(2)}) collective-permute-start(f32[4,64,128]{2,1,0:T(8,128)S(1)} %get-tuple-element.49), channel_id=1, source_target_pairs={{0,2},{1,3},{2,0},{3,1},{4,6},{5,7},{6,4},{7,5},{8,10},{9,11},{10,... | collective-permute-start | bytes 393224 | tf_op jit(solution)/shard_map/ppermute | solution.py:639
  53.3 4.3 %collective-permute-start.14 = (f32[2,64,128]{2,1,0:T(8,128)S(1)}, f32[2,64,128]{2,1,0:T(8,128)S(1)}, u32[]{:S(2)}, u32[]{:S(2)}) collective-permute-start(f32[2,64,128]{2,1,0:T(8,128)S(1)} %get-tuple-element.51), channel_id=1, source_target_pairs={{0,8},{1,9},{2,10},{3,11},{4,12},{5,13},{6,14},{7,15},{8,0},{9,1},... | collective-permute-start | bytes 196616 | tf_op jit(solution)/shard_map/ppermute | solution.py:639
  57.6 5.2 %collective-permute-start.15 = (f32[2,64,128]{2,1,0:T(8,128)S(1)}, f32[2,64,128]{2,1,0:T(8,128)S(1)}, u32[]{:S(2)}, u32[]{:S(2)}) collective-permute-start(f32[2,64,128]{2,1,0:T(8,128)S(1)} %add_kernel.1.mine), channel_id=1, source_target_pairs={{0,16},{1,17},{2,18},{3,19},{4,20},{5,21},{6,22},{7,23},{8,24},{9,... | collective-permute-start | bytes 196616 | tf_op jit(solution)/shard_map/ppermute | solution.py:639
  63.0 4.7 %collective-permute-start.16 = (f32[136,128]{1,0:T(8,128)S(1)}, f32[136,128]{1,0:T(8,128)S(1)}, u32[]{:S(2)}, u32[]{:S(2)}) collective-permute-start(f32[136,128]{1,0:T(8,128)S(1)} %get-tuple-element.52.mine), channel_id=1, source_target_pairs={{0,8},{1,9},{2,10},{3,11},{4,12},{5,13},{6,14},{7,15},{8,0},{9,1},... | collective-permute-start | bytes 208904 | tf_op jit(solution)/shard_map/ppermute | solution.py:639
  64.6 1.2 %collective-permute-start.17 = (f32[8,128]{1,0:T(8,128)S(1)}, f32[8,128]{1,0:T(8,128)S(1)}, u32[]{:S(2)}, u32[]{:S(2)}) collective-permute-start(f32[8,128]{1,0:T(8,128)S(1)} %get-tuple-element.53.s0), channel_id=1, source_target_pairs={{0,1},{1,0},{2,3},{3,2},{4,5},{5,4},{6,7},{7,6},{8,9},{9,8},{10,11... | collective-permute-start | bytes 12296 | tf_op jit(solution)/shard_map/ppermute | solution.py:639
  64.6 3.0 %collective-permute-start.18 = (f32[8,128]{1,0:T(8,128)S(1)}, f32[8,128]{1,0:T(8,128)S(1)}, u32[]{:S(2)}, u32[]{:S(2)}) collective-permute-start(f32[8,128]{1,0:T(8,128)S(1)} %get-tuple-element.53.s0), channel_id=1, source_target_pairs={{0,9},{1,8},{2,11},{3,10},{4,13},{5,12},{6,15},{7,14},{8,1},{9,0},... | collective-permute-start | bytes 12296 | tf_op jit(solution)/shard_map/ppermute | solution.py:639
  67.6 6.8 %collective-permute-start.19 = (f32[264,128]{1,0:T(8,128)S(1)}, f32[264,128]{1,0:T(8,128)S(1)}, u32[]{:S(2)}, u32[]{:S(2)}) collective-permute-start(f32[264,128]{1,0:T(8,128)S(1)} %get-tuple-element.54.mine), channel_id=1, source_target_pairs={{0,4},{1,5},{2,6},{3,7},{4,0},{5,1},{6,2},{7,3},{8,12},{9,13},{10,... | collective-permute-start | bytes 405512 | tf_op jit(solution)/shard_map/ppermute | solution.py:639
  69.1 3.6 %collective-permute-start.20 = (f32[8,128]{1,0:T(8,128)S(1)}, f32[8,128]{1,0:T(8,128)S(1)}, u32[]{:S(2)}, u32[]{:S(2)}) collective-permute-start(f32[8,128]{1,0:T(8,128)S(1)} %get-tuple-element.55.s0), channel_id=1, source_target_pairs={{0,2},{1,3},{2,0},{3,1},{4,6},{5,7},{6,4},{7,5},{8,10},{9,11},{10,... | collective-permute-start | bytes 12296 | tf_op jit(solution)/shard_map/ppermute | solution.py:639
  69.9 4.5 %collective-permute-start.21 = (f32[8,128]{1,0:T(8,128)S(1)}, f32[8,128]{1,0:T(8,128)S(1)}, u32[]{:S(2)}, u32[]{:S(2)}) collective-permute-start(f32[8,128]{1,0:T(8,128)S(1)} %get-tuple-element.55.s0), channel_id=1, source_target_pairs={{0,6},{1,7},{2,4},{3,5},{4,2},{5,3},{6,0},{7,1},{8,14},{9,15},{10,... | collective-permute-start | bytes 12296 | tf_op jit(solution)/shard_map/ppermute | solution.py:639

commit v20 on v17

--- a/solution.py
+++ b/solution.py
@@ -354,7 +354,7 @@
 
 
 BATCH = 4
-PLANES = 2
+PLANES = 4
 
 
 def sweep(core, planes, field, banded, y_first, y_second, work):

time: 74.8 us -> 74.9 us (level)
  no operation moved by 1% of the time
where the time goes in v20:
time: 74.9 us; the launch traced here: 74.6 us
  Pallas kernels  31.8 us (42%)
  starting transfers between devices  21.6 us (29%)
  waiting for transfers between devices  19.2 us (26%)
  between operations  1.43 us (2%)
    ppermute x22, starting transfers between devices, exchange(): lax.ppermute(value, axes, [(i, i ^ bits) for i in range(lax.axis_size(axe...  21.6 us
    ppermute x22, waiting for transfers between devices, exchange(): lax.ppermute(value, axes, [(i, i ^ bits) for i in range(lax.axis_size(axe...  19.2 us
    pallas_call x1, Pallas kernels, scatter(): pl.pallas_call(functools.partial(scatter_kernel, rows_x), grid=(rows_all...  9.27 us
    pallas_call x1, Pallas kernels, whole_shards(): pl.pallas_call(forward_kernel, in_specs=[smem, smem] + [vmem] * 10 + [pl....  9.21 us
    pallas_call x1, Pallas kernels, whole_shards(): pl.pallas_call(adjoint_kernel, in_specs=[vmem] * 8, out_specs=[vmem] * 4,...  7.04 us
    pallas_call x1, Pallas kernels, whole_shards(): pl.pallas_call(first_kernel, in_specs=[hbm] * 3, out_specs=[vmem] * 3, ou...  2.13 us
  transfers between devices with their start and end apart: 22, of which 14 were waited for; matrix products, arithmetic and copies ran while one was open for 0% of the time, Pallas kernels for 29%

profile of v20, /device:TPU:0, one launch (start us, length us, event | category | flops | bytes accessed | tf_op | source)
XLA Modules:
  0.0 74.6 jit_solution(5834339851169076346)
XLA Ops:
  0.6 2.1 %first_to_cross.1 = (f32[2,8,64,128]{3,2,1,0:T(8,128)}, f32[8,64,128]{2,1,0:T(8,128)}, f32[4,64,128]{2,1,0:T(8,128)}) custom-call(f32[2,8,64,128]{3,2,1,0:T(8,128)} %fwd_prev.1, f32[2,8,64,128]{3,2,1,0:T(8,128)} %fwd_cur.1, f32[8,64,128]{2,1,0:T(8,128)} %courant.1), custom_call_target="tpu_custom_call" | custom-call | tf_op jit(solution)/shard_map/first_to_cross/pallas_call | solution.py:650
  2.8 3.0 %collective-permute-start = (f32[4,64,128]{2,1,0:T(8,128)}, f32[4,64,128]{2,1,0:T(8,128)S(1)}, u32[]{:S(2)}, u32[]{:S(2)}) collective-permute-start(f32[4,64,128]{2,1,0:T(8,128)} %get-tuple-element.31), channel_id=1, source_target_pairs={{0,2},{1,3},{2,0},{3,1},{4,6},{5,7},{6,4},{7,5},{8,10},{9,11},{10,... | collective-permute-start | bytes 393224 | tf_op jit(solution)/shard_map/ppermute | solution.py:634
  5.8 0.0 copy-start
  5.8 0.0 copy-start.5
  5.8 0.0 copy-start.7
  5.8 0.1 collective-permute-start.5
  5.9 9.3 %receiver_scatter.1 = (f32[9,2048,128]{2,1,0:T(8,128)}, f32[8,128]{1,0:T(8,128)}) custom-call(s32[2,512]{1,0:T(2,128)} %cells_ref.1, f32[2,8,512]{2,1,0:T(8,128)} %observed_ref.1), custom_call_target="tpu_custom_call" | custom-call | flops 4831838208 | bytes 9437184 | tf_op jit(solution)/shard_map/receiver_scatter/pallas_call | solution.py:305
  15.2 0.0 collective-permute-done.value
  15.2 0.7 copy-done.6
  15.9 2.0 %collective-permute-start.4 = (f32[4,64,128]{2,1,0:T(8,128)S(1)}, f32[4,64,128]{2,1,0:T(8,128)S(1)}, u32[]{:S(2)}, u32[]{:S(2)}) collective-permute-start(f32[4,64,128]{2,1,0:T(8,128)S(1)} %after.3.earlier.mine), channel_id=1, source_target_pairs={{0,4},{1,5},{2,6},{3,7},{4,0},{5,1},{6,2},{7,3},{8,12},{9,13},{10,... | collective-permute-start | bytes 393224 | tf_op jit(solution)/shard_map/ppermute | solution.py:634
  17.9 0.0 copy-done
  17.9 0.0 copy-done.1
  17.9 0.0 copy-done.3
  17.9 0.0 copy-done.4
  17.9 0.0 copy-done.5
  17.9 1.4 %pick.1 = (f32[2,8,64,128]{3,2,1,0:T(8,128)}, f32[2,8,64,128]{3,2,1,0:T(8,128)S(1)}, f32[8,64,128]{2,1,0:T(8,128)S(1)}, f32[11,64,128]{2,1,0:T(8,128)S(1)}) custom-call(f32[4,64,128]{2,1,0:T(8,128)S(1)} %after.3.earlier.mine, f32[2,8,64,128]{3,2,1,0:T(8,128)S(1)} %copy-done.4, f32[2,8,64,128]{3,2,1,0:T(8,128)S(1)} %copy-done.5, ...), custom_call_target="tpu_custom_call" | custom-call | tf_op jit(solution)/shard_map/pick/pallas_call | solution.py:173
  19.3 0.1 collective-permute-start.2
  19.4 1.5 %collective-permute-start.9 = (f32[2,8,64,128]{3,2,1,0:T(8,128)}, f32[2,8,64,128]{3,2,1,0:T(8,128)S(1)}, u32[]{:S(2)}, u32[]{:S(2)}) collective-permute-start(f32[2,8,64,128]{3,2,1,0:T(8,128)} %get-tuple-element.41), channel_id=1, source_target_pairs={{0,2},{1,3},{2,0},{3,1},{4,6},{5,7},{6,4},{7,5},{8,10},{9,11},{10,... | collective-permute-start | bytes 1572872 | tf_op jit(solution)/shard_map/ppermute | solution.py:634
  20.8 0.1 collective-permute-done.4.other
  21.0 0.1 collective-permute-start.8
  21.1 0.4 collective-permute-start.3
  21.6 0.0 collective-permute-done.5.value
  21.6 0.7 after.4
  22.3 0.1 collective-permute-start.6
  22.4 0.0 collective-permute-done.2.mate0
  22.4 0.4 collective-permute-start.7
  23.5 0.0 collective-permute-done.3.mate1
  23.5 0.1 collective-permute-start.1
  23.6 0.0 collective-permute-done.8.speed_mate
  23.6 0.3 collective-permute-done.6.far0
  24.0 0.6 collective-permute-done.7.far1
  24.6 0.0 copy-done.7
  24.6 9.2 %forward_steps.1 = (f32[8,8,2,64,128]{4,3,2,1,0:T(8,128)S(1)}, f32[8,32,64,128]{3,2,1,0:T(8,128)S(1)}, f32[9,32,64,128]{3,2,1,0:T(8,128)S(1)}, f32[32,64,128]{2,1,0:T(8,128)S(1)}, f32[16,64,128]{2,1,0:T(8,128)S(1)}) custom-call(s32[1]{0:T(128)} %bitcast.3.start, s32[2]{0:T(128)S(1)} %copy-done.7, f32[8,64,128]{2,1,0:T(8,128)S(1)} %get-tuple-element.34.own0, ...), custom_call_target="tpu_custom_call" | custom-call | flops 1000 | bytes 1000 | tf_op jit(solution)/shard_map/forward_steps/pallas_call | solution.py:690
  33.8 0.1 collective-permute-done.9.value
  34.0 0.1 collective-permute-start.10
  34.0 1.0 %inject.1 = f32[8,32,64,128]{3,2,1,0:T(8,128)S(1)} custom-call(f32[9,32,64,128]{3,2,1,0:T(8,128)S(1)} %get-tuple-element.43.held, f32[8,32,64,128]{3,2,1,0:T(8,128)S(1)} %get-tuple-element.44.history), custom_call_target="tpu_custom_call" | custom-call | tf_op jit(solution)/shard_map/inject/pallas_call | solution.py:714
  35.0 0.0 collective-permute-done.1.mate
  35.0 0.9 %collective-permute-done.10.far = f32[2,8,64,128]{3,2,1,0:T(8,128)S(1)} collective-permute-done((f32[2,8,64,128]{3,2,1,0:T(8,128)S(1)}, f32[2,8,64,128]{3,2,1,0:T(8,128)S(1)}, u32[]{:S(2)}, u32[]{:S(2)}) %collective-permute-start.10) | collective-permute-done | bytes 524320 | tf_op jit(solution)/shard_map/ppermute | solution.py:634
  35.9 7.0 %adjoint_steps.1 = (f32[4,64,128]{2,1,0:T(8,128)S(1)}, f32[4,64,128]{2,1,0:T(8,128)S(1)}, f32[4,64,128]{2,1,0:T(8,128)S(1)}, f32[4,64,128]{2,1,0:T(8,128)S(1)}) custom-call(f32[2,8,64,128]{3,2,1,0:T(8,128)S(1)} %get-tuple-element.33.own, f32[2,8,64,128]{3,2,1,0:T(8,128)S(1)} %collective-permute-done.1.mate, f32[2,8,64,128]{3,2,1,0:T(8,128)S(1)} %after.5.over, ...), custom_call_target="tpu_custom_call" | custom-call | flops 62914560 | bytes 33554432 | tf_op jit(solution)/shard_map/adjoint_steps/pallas_call | solution.py:724
  43.0 2.7 %collective-permute-start.11 = (f32[4,64,128]{2,1,0:T(8,128)S(1)}, f32[4,64,128]{2,1,0:T(8,128)S(1)}, u32[]{:S(2)}, u32[]{:S(2)}) collective-permute-start(f32[4,64,128]{2,1,0:T(8,128)S(1)} %get-tuple-element.47), channel_id=1, source_target_pairs={{0,6},{1,7},{2,4},{3,5},{4,2},{5,3},{6,0},{7,1},{8,14},{9,15},{10,... | collective-permute-start | bytes 393224 | tf_op jit(solution)/shard_map/ppermute | solution.py:634
  45.7 0.5 collective-permute-start.12
  46.2 0.3 collective-permute-start.13
  46.5 3.1 %collective-permute-done.11.by_xy = f32[4,64,128]{2,1,0:T(8,128)S(1)} collective-permute-done((f32[4,64,128]{2,1,0:T(8,128)S(1)}, f32[4,64,128]{2,1,0:T(8,128)S(1)}, u32[]{:S(2)}, u32[]{:S(2)}) %collective-permute-start.11) | collective-permute-done | bytes 131104 | tf_op jit(solution)/shard_map/ppermute | solution.py:634
  49.6 2.7 %collective-permute-done.12.by_y = f32[4,64,128]{2,1,0:T(8,128)S(1)} collective-permute-done((f32[4,64,128]{2,1,0:T(8,128)S(1)}, f32[4,64,128]{2,1,0:T(8,128)S(1)}, u32[]{:S(2)}, u32[]{:S(2)}) %collective-permute-start.12) | collective-permute-done | bytes 131104 | tf_op jit(solution)/shard_map/ppermute | solution.py:634
  52.3 0.4 collective-permute-done.13.by_x
  52.7 1.7 %collective-permute-start.14 = (f32[2,64,128]{2,1,0:T(8,128)S(1)}, f32[2,64,128]{2,1,0:T(8,128)S(1)}, u32[]{:S(2)}, u32[]{:S(2)}) collective-permute-start(f32[2,64,128]{2,1,0:T(8,128)S(1)} %get-tuple-element.51), channel_id=1, source_target_pairs={{0,8},{1,9},{2,10},{3,11},{4,12},{5,13},{6,14},{7,15},{8,0},{9,1},... | collective-permute-start | bytes 196616 | tf_op jit(solution)/shard_map/ppermute | solution.py:634
  54.4 2.7 %collective-permute-done.14.other = f32[2,64,128]{2,1,0:T(8,128)S(1)} collective-permute-done((f32[2,64,128]{2,1,0:T(8,128)S(1)}, f32[2,64,128]{2,1,0:T(8,128)S(1)}, u32[]{:S(2)}, u32[]{:S(2)}) %collective-permute-start.14) | collective-permute-done | bytes 65568 | tf_op jit(solution)/shard_map/ppermute | solution.py:634
  57.1 2.7 %collective-permute-start.15 = (f32[2,64,128]{2,1,0:T(8,128)S(1)}, f32[2,64,128]{2,1,0:T(8,128)S(1)}, u32[]{:S(2)}, u32[]{:S(2)}) collective-permute-start(f32[2,64,128]{2,1,0:T(8,128)S(1)} %add_kernel.1.mine), channel_id=1, source_target_pairs={{0,16},{1,17},{2,18},{3,19},{4,20},{5,21},{6,22},{7,23},{8,24},{9,... | collective-permute-start | bytes 196616 | tf_op jit(solution)/shard_map/ppermute | solution.py:634
  59.7 2.6 %collective-permute-done.15.other = f32[2,64,128]{2,1,0:T(8,128)S(1)} collective-permute-done((f32[2,64,128]{2,1,0:T(8,128)S(1)}, f32[2,64,128]{2,1,0:T(8,128)S(1)}, u32[]{:S(2)}, u32[]{:S(2)}) %collective-permute-start.15) | collective-permute-done | bytes 65568 | tf_op jit(solution)/shard_map/ppermute | solution.py:634
  62.3 0.0 copy-done.2
  62.3 0.1 sums_kernel.1
  62.4 1.6 %collective-permute-start.16 = (f32[136,128]{1,0:T(8,128)S(1)}, f32[136,128]{1,0:T(8,128)S(1)}, u32[]{:S(2)}, u32[]{:S(2)}) collective-permute-start(f32[136,128]{1,0:T(8,128)S(1)} %get-tuple-element.52.mine), channel_id=1, source_target_pairs={{0,8},{1,9},{2,10},{3,11},{4,12},{5,13},{6,14},{7,15},{8,0},{9,1},... | collective-permute-start | bytes 208904 | tf_op jit(solution)/shard_map/ppermute | solution.py:634
  64.0 0.0 collective-permute-start.17
  64.0 0.5 collective-permute-start.18
  64.6 0.6 collective-permute-done.17.s1
  65.2 1.9 %collective-permute-done.18.s2 = f32[8,128]{1,0:T(8,128)S(1)} collective-permute-done((f32[8,128]{1,0:T(8,128)S(1)}, f32[8,128]{1,0:T(8,128)S(1)}, u32[]{:S(2)}, u32[]{:S(2)}) %collective-permute-start.18) | collective-permute-done | bytes 4128 | tf_op jit(solution)/shard_map/ppermute | solution.py:634
  67.1 0.0 collective-permute-done.16.other
  67.1 1.5 %collective-permute-start.19 = (f32[264,128]{1,0:T(8,128)S(1)}, f32[264,128]{1,0:T(8,128)S(1)}, u32[]{:S(2)}, u32[]{:S(2)}) collective-permute-start(f32[264,128]{1,0:T(8,128)S(1)} %get-tuple-element.54.mine), channel_id=1, source_target_pairs={{0,4},{1,5},{2,6},{3,7},{4,0},{5,1},{6,2},{7,3},{8,12},{9,13},{10,... | collective-permute-start | bytes 405512 | tf_op jit(solution)/shard_map/ppermute | solution.py:634
  68.6 0.8 %collective-permute-start.20 = (f32[8,128]{1,0:T(8,128)S(1)}, f32[8,128]{1,0:T(8,128)S(1)}, u32[]{:S(2)}, u32[]{:S(2)}) collective-permute-start(f32[8,128]{1,0:T(8,128)S(1)} %get-tuple-element.55.s0), channel_id=1, source_target_pairs={{0,2},{1,3},{2,0},{3,1},{4,6},{5,7},{6,4},{7,5},{8,10},{9,11},{10,... | collective-permute-start | bytes 12296 | tf_op jit(solution)/shard_map/ppermute | solution.py:634
  69.4 1.3 %collective-permute-start.21 = (f32[8,128]{1,0:T(8,128)S(1)}, f32[8,128]{1,0:T(8,128)S(1)}, u32[]{:S(2)}, u32[]{:S(2)}) collective-permute-start(f32[8,128]{1,0:T(8,128)S(1)} %get-tuple-element.55.s0), channel_id=1, source_target_pairs={{0,6},{1,7},{2,4},{3,5},{4,2},{5,3},{6,0},{7,1},{8,14},{9,15},{10,... | collective-permute-start | bytes 12296 | tf_op jit(solution)/shard_map/ppermute | solution.py:634
  70.6 1.5 %collective-permute-done.20.s1 = f32[8,128]{1,0:T(8,128)S(1)} collective-permute-done((f32[8,128]{1,0:T(8,128)S(1)}, f32[8,128]{1,0:T(8,128)S(1)}, u32[]{:S(2)}, u32[]{:S(2)}) %collective-permute-start.20) | collective-permute-done | bytes 4128 | tf_op jit(solution)/shard_map/ppermute | solution.py:634
  72.2 1.7 %collective-permute-done.21.s2 = f32[8,128]{1,0:T(8,128)S(1)} collective-permute-done((f32[8,128]{1,0:T(8,128)S(1)}, f32[8,128]{1,0:T(8,128)S(1)}, u32[]{:S(2)}, u32[]{:S(2)}) %collective-permute-start.21) | collective-permute-done | bytes 4128 | tf_op jit(solution)/shard_map/ppermute | solution.py:634
  73.9 0.0 collective-permute-done.19.other
  73.9 0.8 %finish.1 = (f32[8,64,128]{2,1,0:T(8,128)}, f32[1]{0:T(128)}) custom-call(f32[264,128]{1,0:T(8,128)S(1)} %get-tuple-element.54.mine, f32[264,128]{1,0:T(8,128)S(1)} %collective-permute-done.19.other, f32[8,64,128]{2,1,0:T(8,128)S(1)} %copy-done.2, f32[8,128]{1,0:T(8,128)S(1)} %get-tuple-element.55.s0, f32[8,128]{1,0:T(8,128)S(1)} %collective-permute-done.20.s1, ...), custom_call_target="tpu_custom_call" | custom-call | tf_op jit(solution)/shard_map/finish/pallas_call | solution.py:746
  (11 shorter events, 0.1 us)
Async XLA Ops:
  2.8 12.4 %collective-permute-start = (f32[4,64,128]{2,1,0:T(8,128)}, f32[4,64,128]{2,1,0:T(8,128)S(1)}, u32[]{:S(2)}, u32[]{:S(2)}) collective-permute-start(f32[4,64,128]{2,1,0:T(8,128)} %get-tuple-element.31), channel_id=1, source_target_pairs={{0,2},{1,3},{2,0},{3,1},{4,6},{5,7},{6,4},{7,5},{8,10},{9,11},{10,... | collective-permute-start | bytes 393224 | tf_op jit(solution)/shard_map/ppermute | solution.py:634
  5.8 12.1 %copy-start = (f32[2,8,64,128]{3,2,1,0:T(8,128)S(1)}, f32[2,8,64,128]{3,2,1,0:T(8,128)}, u32[]{:S(2)}) copy-start(f32[2,8,64,128]{3,2,1,0:T(8,128)} %fwd_prev.1) | copy-start | bytes 1572868
  5.8 12.1 %copy-start.1 = (f32[2,8,64,128]{3,2,1,0:T(8,128)S(1)}, f32[2,8,64,128]{3,2,1,0:T(8,128)}, u32[]{:S(2)}) copy-start(f32[2,8,64,128]{3,2,1,0:T(8,128)} %fwd_cur.1) | copy-start | bytes 1572868
  5.8 12.1 %copy-start.3 = (f32[8,64,128]{2,1,0:T(8,128)S(1)}, f32[8,64,128]{2,1,0:T(8,128)}, u32[]{:S(2)}) copy-start(f32[8,64,128]{2,1,0:T(8,128)} %get-tuple-element.32.speed.own) | copy-start | bytes 786436
  5.8 12.1 %copy-start.4 = (f32[2,8,64,128]{3,2,1,0:T(8,128)S(1)}, f32[2,8,64,128]{3,2,1,0:T(8,128)}, u32[]{:S(2)}) copy-start(f32[2,8,64,128]{3,2,1,0:T(8,128)} %adj_next.1) | copy-start | bytes 1572868
  5.8 12.1 %copy-start.5 = (f32[2,8,64,128]{3,2,1,0:T(8,128)S(1)}, f32[2,8,64,128]{3,2,1,0:T(8,128)}, u32[]{:S(2)}) copy-start(f32[2,8,64,128]{3,2,1,0:T(8,128)} %adj_cur.1) | copy-start | bytes 1572868
  5.8 18.8 %copy-start.7 = (s32[2]{0:T(128)S(1)}, s32[2]{0:T(128)}, u32[]{:S(2)}) copy-start(s32[2]{0:T(128)} %sources.1) | copy-start | bytes 28
  5.8 15.8 %collective-permute-start.5 = (f32[2,8,64,128]{3,2,1,0:T(8,128)}, f32[2,8,64,128]{3,2,1,0:T(8,128)S(1)}, u32[]{:S(2)}, u32[]{:S(2)}) collective-permute-start(f32[2,8,64,128]{3,2,1,0:T(8,128)} %get-tuple-element.36), channel_id=1, source_target_pairs={{0,2},{1,3},{2,0},{3,1},{4,6},{5,7},{6,4},{7,5},{8,10},{9,11},{10,... | collective-permute-start | bytes 1572872 | tf_op jit(solution)/shard_map/ppermute | solution.py:634
  15.2 0.7 copy-start.6
  15.9 5.0 %collective-permute-start.4 = (f32[4,64,128]{2,1,0:T(8,128)S(1)}, f32[4,64,128]{2,1,0:T(8,128)S(1)}, u32[]{:S(2)}, u32[]{:S(2)}) collective-permute-start(f32[4,64,128]{2,1,0:T(8,128)S(1)} %after.3.earlier.mine), channel_id=1, source_target_pairs={{0,4},{1,5},{2,6},{3,7},{4,0},{5,1},{6,2},{7,3},{8,12},{9,13},{10,... | collective-permute-start | bytes 393224 | tf_op jit(solution)/shard_map/ppermute | solution.py:634
  19.3 3.1 %collective-permute-start.2 = (f32[8,64,128]{2,1,0:T(8,128)S(1)}, f32[8,64,128]{2,1,0:T(8,128)S(1)}, u32[]{:S(2)}, u32[]{:S(2)}) collective-permute-start(f32[8,64,128]{2,1,0:T(8,128)S(1)} %get-tuple-element.34.own0), channel_id=1, source_target_pairs={{0,1},{1,0},{2,3},{3,2},{4,5},{5,4},{6,7},{7,6},{8,9},{9,8},{10,11... | collective-permute-start | bytes 786440 | tf_op jit(solution)/shard_map/ppermute | solution.py:634
  19.4 14.6 %collective-permute-start.9 = (f32[2,8,64,128]{3,2,1,0:T(8,128)}, f32[2,8,64,128]{3,2,1,0:T(8,128)S(1)}, u32[]{:S(2)}, u32[]{:S(2)}) collective-permute-start(f32[2,8,64,128]{3,2,1,0:T(8,128)} %get-tuple-element.41), channel_id=1, source_target_pairs={{0,2},{1,3},{2,0},{3,1},{4,6},{5,7},{6,4},{7,5},{8,10},{9,11},{10,... | collective-permute-start | bytes 1572872 | tf_op jit(solution)/shard_map/ppermute | solution.py:634
  21.0 2.6 %collective-permute-start.8 = (f32[13,64,128]{2,1,0:T(8,128)S(1)}, f32[13,64,128]{2,1,0:T(8,128)S(1)}, u32[]{:S(2)}, u32[]{:S(2)}) collective-permute-start(f32[13,64,128]{2,1,0:T(8,128)S(1)} %arrange_kernel.1.earlier.speed), channel_id=1, source_target_pairs={{0,1},{1,0},{2,3},{3,2},{4,5},{5,4},{6,7},{7,6},{8,9},{9,8},{10,11... | collective-permute-start | bytes 1277960 | tf_op jit(solution)/shard_map/ppermute | solution.py:634
  21.1 2.3 %collective-permute-start.3 = (f32[11,64,128]{2,1,0:T(8,128)S(1)}, f32[11,64,128]{2,1,0:T(8,128)S(1)}, u32[]{:S(2)}, u32[]{:S(2)}) collective-permute-start(f32[11,64,128]{2,1,0:T(8,128)S(1)} %get-tuple-element.35.own1), channel_id=1, source_target_pairs={{0,1},{1,0},{2,3},{3,2},{4,5},{5,4},{6,7},{7,6},{8,9},{9,8},{10,11... | collective-permute-start | bytes 1081352 | tf_op jit(solution)/shard_map/ppermute | solution.py:634
  22.3 1.7 %collective-permute-start.6 = (f32[8,64,128]{2,1,0:T(8,128)S(1)}, f32[8,64,128]{2,1,0:T(8,128)}, u32[]{:S(2)}, u32[]{:S(2)}) collective-permute-start(f32[8,64,128]{2,1,0:T(8,128)S(1)} %get-tuple-element.37.over0), channel_id=1, source_target_pairs={{0,1},{1,0},{2,3},{3,2},{4,5},{5,4},{6,7},{7,6},{8,9},{9,8},{10,11... | collective-permute-start | bytes 786440 | tf_op jit(solution)/shard_map/ppermute | solution.py:634
  22.4 2.2 %collective-permute-start.7 = (f32[8,64,128]{2,1,0:T(8,128)}, f32[8,64,128]{2,1,0:T(8,128)}, u32[]{:S(2)}, u32[]{:S(2)}) collective-permute-start(f32[8,64,128]{2,1,0:T(8,128)} %get-tuple-element.38.over1), channel_id=1, source_target_pairs={{0,1},{1,0},{2,3},{3,2},{4,5},{5,4},{6,7},{7,6},{8,9},{9,8},{10,11... | collective-permute-start | bytes 786440 | tf_op jit(solution)/shard_map/ppermute | solution.py:634
  23.5 11.6 %collective-permute-start.1 = (f32[2,8,64,128]{3,2,1,0:T(8,128)S(1)}, f32[2,8,64,128]{3,2,1,0:T(8,128)S(1)}, u32[]{:S(2)}, u32[]{:S(2)}) collective-permute-start(f32[2,8,64,128]{3,2,1,0:T(8,128)S(1)} %get-tuple-element.33.own), channel_id=1, source_target_pairs={{0,1},{1,0},{2,3},{3,2},{4,5},{5,4},{6,7},{7,6},{8,9},{9,8},{10,11... | collective-permute-start | bytes 1572872 | tf_op jit(solution)/shard_map/ppermute | solution.py:634
  34.0 2.0 %collective-permute-start.10 = (f32[2,8,64,128]{3,2,1,0:T(8,128)S(1)}, f32[2,8,64,128]{3,2,1,0:T(8,128)S(1)}, u32[]{:S(2)}, u32[]{:S(2)}) collective-permute-start(f32[2,8,64,128]{3,2,1,0:T(8,128)S(1)} %after.5.over), channel_id=1, source_target_pairs={{0,1},{1,0},{2,3},{3,2},{4,5},{5,4},{6,7},{7,6},{8,9},{9,8},{10,11... | collective-permute-start | bytes 1572872 | tf_op jit(solution)/shard_map/ppermute | solution.py:634
  35.9 26.4 %copy-start.2 = (f32[8,64,128]{2,1,0:T(8,128)S(1)}, f32[8,64,128]{2,1,0:T(8,128)}, u32[]{:S(2)}) copy-start(f32[8,64,128]{2,1,0:T(8,128)} %momentum.3) | copy-start | bytes 786436
  43.0 6.6 %collective-permute-start.11 = (f32[4,64,128]{2,1,0:T(8,128)S(1)}, f32[4,64,128]{2,1,0:T(8,128)S(1)}, u32[]{:S(2)}, u32[]{:S(2)}) collective-permute-start(f32[4,64,128]{2,1,0:T(8,128)S(1)} %get-tuple-element.47), channel_id=1, source_target_pairs={{0,6},{1,7},{2,4},{3,5},{4,2},{5,3},{6,0},{7,1},{8,14},{9,15},{10,... | collective-permute-start | bytes 393224 | tf_op jit(solution)/shard_map/ppermute | solution.py:634
  45.7 6.6 %collective-permute-start.12 = (f32[4,64,128]{2,1,0:T(8,128)S(1)}, f32[4,64,128]{2,1,0:T(8,128)S(1)}, u32[]{:S(2)}, u32[]{:S(2)}) collective-permute-start(f32[4,64,128]{2,1,0:T(8,128)S(1)} %get-tuple-element.48), channel_id=1, source_target_pairs={{0,4},{1,5},{2,6},{3,7},{4,0},{5,1},{6,2},{7,3},{8,12},{9,13},{10,... | collective-permute-start | bytes 393224 | tf_op jit(solution)/shard_map/ppermute | solution.py:634
  46.2 6.5 %collective-permute-start.13 = (f32[4,64,128]{2,1,0:T(8,128)S(1)}, f32[4,64,128]{2,1,0:T(8,128)S(1)}, u32[]{:S(2)}, u32[]{:S(2)}) collective-permute-start(f32[4,64,128]{2,1,0:T(8,128)S(1)} %get-tuple-element.49), channel_id=1, source_target_pairs={{0,2},{1,3},{2,0},{3,1},{4,6},{5,7},{6,4},{7,5},{8,10},{9,11},{10,... | collective-permute-start | bytes 393224 | tf_op jit(solution)/shard_map/ppermute | solution.py:634
  52.7 4.3 %collective-permute-start.14 = (f32[2,64,128]{2,1,0:T(8,128)S(1)}, f32[2,64,128]{2,1,0:T(8,128)S(1)}, u32[]{:S(2)}, u32[]{:S(2)}) collective-permute-start(f32[2,64,128]{2,1,0:T(8,128)S(1)} %get-tuple-element.51), channel_id=1, source_target_pairs={{0,8},{1,9},{2,10},{3,11},{4,12},{5,13},{6,14},{7,15},{8,0},{9,1},... | collective-permute-start | bytes 196616 | tf_op jit(solution)/shard_map/ppermute | solution.py:634
  57.1 5.2 %collective-permute-start.15 = (f32[2,64,128]{2,1,0:T(8,128)S(1)}, f32[2,64,128]{2,1,0:T(8,128)S(1)}, u32[]{:S(2)}, u32[]{:S(2)}) collective-permute-start(f32[2,64,128]{2,1,0:T(8,128)S(1)} %add_kernel.1.mine), channel_id=1, source_target_pairs={{0,16},{1,17},{2,18},{3,19},{4,20},{5,21},{6,22},{7,23},{8,24},{9,... | collective-permute-start | bytes 196616 | tf_op jit(solution)/shard_map/ppermute | solution.py:634
  62.4 4.7 %collective-permute-start.16 = (f32[136,128]{1,0:T(8,128)S(1)}, f32[136,128]{1,0:T(8,128)S(1)}, u32[]{:S(2)}, u32[]{:S(2)}) collective-permute-start(f32[136,128]{1,0:T(8,128)S(1)} %get-tuple-element.52.mine), channel_id=1, source_target_pairs={{0,8},{1,9},{2,10},{3,11},{4,12},{5,13},{6,14},{7,15},{8,0},{9,1},... | collective-permute-start | bytes 208904 | tf_op jit(solution)/shard_map/ppermute | solution.py:634
  64.0 1.2 %collective-permute-start.17 = (f32[8,128]{1,0:T(8,128)S(1)}, f32[8,128]{1,0:T(8,128)S(1)}, u32[]{:S(2)}, u32[]{:S(2)}) collective-permute-start(f32[8,128]{1,0:T(8,128)S(1)} %get-tuple-element.53.s0), channel_id=1, source_target_pairs={{0,1},{1,0},{2,3},{3,2},{4,5},{5,4},{6,7},{7,6},{8,9},{9,8},{10,11... | collective-permute-start | bytes 12296 | tf_op jit(solution)/shard_map/ppermute | solution.py:634
  64.0 3.0 %collective-permute-start.18 = (f32[8,128]{1,0:T(8,128)S(1)}, f32[8,128]{1,0:T(8,128)S(1)}, u32[]{:S(2)}, u32[]{:S(2)}) collective-permute-start(f32[8,128]{1,0:T(8,128)S(1)} %get-tuple-element.53.s0), channel_id=1, source_target_pairs={{0,9},{1,8},{2,11},{3,10},{4,13},{5,12},{6,15},{7,14},{8,1},{9,0},... | collective-permute-start | bytes 12296 | tf_op jit(solution)/shard_map/ppermute | solution.py:634
  67.1 6.8 %collective-permute-start.19 = (f32[264,128]{1,0:T(8,128)S(1)}, f32[264,128]{1,0:T(8,128)S(1)}, u32[]{:S(2)}, u32[]{:S(2)}) collective-permute-start(f32[264,128]{1,0:T(8,128)S(1)} %get-tuple-element.54.mine), channel_id=1, source_target_pairs={{0,4},{1,5},{2,6},{3,7},{4,0},{5,1},{6,2},{7,3},{8,12},{9,13},{10,... | collective-permute-start | bytes 405512 | tf_op jit(solution)/shard_map/ppermute | solution.py:634
  68.6 3.6 %collective-permute-start.20 = (f32[8,128]{1,0:T(8,128)S(1)}, f32[8,128]{1,0:T(8,128)S(1)}, u32[]{:S(2)}, u32[]{:S(2)}) collective-permute-start(f32[8,128]{1,0:T(8,128)S(1)} %get-tuple-element.55.s0), channel_id=1, source_target_pairs={{0,2},{1,3},{2,0},{3,1},{4,6},{5,7},{6,4},{7,5},{8,10},{9,11},{10,... | collective-permute-start | bytes 12296 | tf_op jit(solution)/shard_map/ppermute | solution.py:634
  69.4 4.5 %collective-permute-start.21 = (f32[8,128]{1,0:T(8,128)S(1)}, f32[8,128]{1,0:T(8,128)S(1)}, u32[]{:S(2)}, u32[]{:S(2)}) collective-permute-start(f32[8,128]{1,0:T(8,128)S(1)} %get-tuple-element.55.s0), channel_id=1, source_target_pairs={{0,6},{1,7},{2,4},{3,5},{4,2},{5,3},{6,0},{7,1},{8,14},{9,15},{10,... | collective-permute-start | bytes 12296 | tf_op jit(solution)/shard_map/ppermute | solution.py:634
